TPU v7x, 32 devices: a whole 2x2x4 slice. The times are simulated.
32 devices in a mesh: dp: 16 (over z, y, x), cent: 2 (over core).
Axes of the slice: x: 2, y: 2, z: 4, core: 2. Of those that a mesh axis runs over, the one named last changes fastest.
Arguments:
- points: bfloat16 [16384, 256], P('dp'), may hold values from -8 to 8
- centroids: bfloat16 [8192, 256], P('cent'), may hold values from -0.5 to 0.5
Outputs:
- new_centroids: float32 [8192, 256], P('cent')
- counts: float32 [8192], P('cent')
- log_evidence: float32 [16384], P('dp')
All inputs are finite; a program needn't handle non-finite values.
Results may differ from a plain program's by a relative error of at most 0.0016.
Values sent between devices are 32-bit elements; how exact they have to be, the bound alone decides.
No kernel may reach another device: no remote copies, remote signals or barrier semaphores. Data moves between devices by JAX's collectives and lax.ppermute only.
A program may use at most 64 MiB of HBM per device.

v0:
```python
import math

import jax
import jax.numpy as jnp
from jax import lax
from jax.sharding import PartitionSpec as P

prior_mass = 0.5


def body(points, centroids):
    rows = points.shape[0]
    local_cent = centroids.shape[0]
    width = centroids.shape[1]
    every_centroid = local_cent * lax.axis_size("cent")
    block = min(512, rows)
    cnorm = jnp.einsum("kd,kd->k", centroids, centroids, preferred_element_type=jnp.float32)
    sums = jnp.zeros((local_cent, width), jnp.float32)
    counts = jnp.zeros((local_cent,), jnp.float32)
    evidence = []
    for step in range(rows // block):
        piece = lax.slice_in_dim(points, step * block, (step + 1) * block, axis=0)
        dots = jnp.einsum("nd,kd->nk", piece, centroids, preferred_element_type=jnp.float32)
        score = 2.0 * dots - cnorm[None, :]
        top = lax.pmax(jnp.max(score, axis=1), "cent")
        weights = jnp.exp(score - top[:, None])
        total = lax.psum(jnp.sum(weights, axis=1), "cent")
        resp = (weights / total[:, None]).astype(jnp.bfloat16)
        sums = sums + jnp.einsum("nk,nd->kd", resp, piece, preferred_element_type=jnp.float32)
        counts = counts + jnp.sum(resp.astype(jnp.float32), axis=0)
        evidence.append(top + jnp.log(total) - math.log(every_centroid))
    log_evidence = jnp.concatenate(evidence, axis=0)
    all_sums, all_counts = lax.psum((sums, counts), "dp")
    new_centroids = (all_sums + prior_mass * centroids.astype(jnp.float32)) / (
        all_counts + prior_mass
    )[:, None]
    return (new_centroids, all_counts, log_evidence)


def solution(mesh):
    return jax.shard_map(
        body,
        mesh=mesh,
        in_specs=(P("dp", None), P("cent", None)),
        out_specs=(P("cent", None), P("cent"), P("dp")),
        check_vma=False,
    )
```

profile of v0, /device:TPU:0, one launch (start us, length us, event | category | flops | bytes accessed | tf_op | source)
XLA Modules:
  0.0 227.0 jit_solution(7726816621656867052)
XLA Ops:
  7.2 0.0 copy-start.1
  7.2 0.0 copy-start.2
  7.2 0.0 all-reduce.4.cloned.1.call-start
  7.2 2.4 %fusion.4 = f32[4096]{0:T(1024)S(1)} fusion(bf16[4096,256]{1,0:T(8,128)(2,1)} %param.3), kind=kLoop, calls=%fused_computation.15 | loop fusion | flops 3141632 | bytes 2113536 | tf_op jit(solution)/shard_map/kd,kd->k/dot_general | solution.py:17
  9.6 3.0 %fusion.12 = f32[512,4096]{1,0:T(8,128)S(1)} fusion(bf16[4096,256]{1,0:T(8,128)(2,1)} %param.3, bf16[1024,256]{1,0:T(8,128)(2,1)} %param.2), kind=kOutput, calls=%fused_computation.23 | convolution fusion | flops 1073741824 | bytes 10747904 | tf_op jit(solution)/shard_map/nd,kd->nk/dot_general | solution.py:23
  12.6 0.0 copy-done.1
  12.6 0.0 copy-done.2
  12.6 0.0 copy-start
  12.6 4.9 %fusion.1 = (f32[512]{0:T(512)S(1)}, f32[512]{0:T(512)S(1)}, f32[512,4096]{1,0:T(8,128)}) fusion(f32[4096]{0:T(1024)S(1)} %fusion.4, f32[512,4096]{1,0:T(8,128)S(1)} %fusion.12, bf16[4096,256]{1,0:T(8,128)(2,1)S(1)} %copy-done.1, bf16[1024,256]{1,0:T(8,128)(2,1)S(1)} %copy-done.2), kind=kOutput, calls=%fused_computation.9 | convolution fusion | flops 1086323712 | bytes 19156992 | tf_op jit(solution)/shard_map/nd,kd->nk/dot_general | solution.py:23
  17.6 0.8 copy-done
  18.3 2.6 %all-reduce.1 = (f32[512]{0:T(512)S(1)}, f32[512]{0:T(512)S(1)}) all-reduce(f32[512]{0:T(512)S(1)} %get-tuple-element.5, f32[512]{0:T(512)S(1)} %get-tuple-element.6), channel_id=1, replica_groups=mesh['dp'=16,'cent'=2] {'cent'}, use_global_device_ids=true, to_apply=%region_5.0 | all-reduce | flops 1024 | bytes 8192 | tf_op jit(solution)/shard_map/pmax | solution.py:25
  20.9 7.6 %fusion.3 = (f32[512]{0:T(512)S(1)}, f32[512]{0:T(512)S(1)}) fusion(f32[512,4096]{1,0:T(8,128)} %get-tuple-element.17, f32[512]{0:T(512)S(1)} %get-tuple-element.9, f32[4096]{0:T(1024)S(1)} %fusion.4, f32[512]{0:T(512)S(1)} %get-tuple-element.10, f32[512,4096]{1,0:T(8,128)} %copy-done), kind=kLoop, calls=%fused_computation.11 | loop fusion | flops 16776192 | bytes 16801792 | tf_op jit(solution)/shard_map/reduce_sum | solution.py:27
  28.5 2.5 %all-reduce = (f32[512]{0:T(512)S(1)}, f32[512]{0:T(512)S(1)}) all-reduce(f32[512]{0:T(512)S(1)} %get-tuple-element.4, f32[512]{0:T(512)S(1)} %get-tuple-element.3), channel_id=1, replica_groups=mesh['dp'=16,'cent'=2] {'cent'}, use_global_device_ids=true, to_apply=%region_3.0 | all-reduce | flops 1024 | bytes 8192 | tf_op jit(solution)/shard_map/psum | solution.py:27
  31.0 8.7 %convert_reduce_fusion = (f32[4096]{0:T(1024)S(1)}, bf16[512,4096]{1,0:T(8,128)(2,1)S(1)}, f32[4096]{0:T(1024)S(1)}, bf16[512,4096]{1,0:T(8,128)(2,1)S(1)}) fusion(f32[512]{0:T(512)S(1)} %get-tuple-element.8, f32[512]{0:T(512)S(1)} %get-tuple-element.9, f32[4096]{0:T(1024)S(1)} %fusion.4, f32[512,4096]{1,0:T(8,128)} %get-tuple-element.17, ...), kind=kLoop, calls=%fused_computation | loop fusion | flops 29351936 | bytes 25223168 | tf_op jit(solution)/shard_map/reduce_sum | solution.py:30
  39.7 1.3 fusion.10
  40.9 3.4 %convolution_add_fusion = f32[4096,256]{1,0:T(8,128)} fusion(f32[4096,256]{1,0:T(8,128)S(1)} %fusion.10, bf16[512,4096]{1,0:T(8,128)(2,1)S(1)} %get-tuple-element.12, bf16[1024,256]{1,0:T(8,128)(2,1)S(1)} %copy-done.2), kind=kOutput, calls=%fused_computation.12 | convolution fusion | flops 1074790400 | bytes 12845056 | tf_op jit(solution)/shard_map/nk,nd->kd/dot_general | solution.py:29
  44.4 0.0 all-reduce.4.cloned.1.call-update
  44.4 80.8 %psum.31 = f32[4096]{0:T(1024)S(1)} all-reduce(f32[4096]{0:T(1024)S(1)} %add.33), channel_id=1, replica_groups=mesh['dp'=16,'cent'=2] {'dp'}, use_global_device_ids=true, to_apply=%region_11.0 | all-reduce | flops 4096 | bytes 32768 | tf_op jit(solution)/shard_map/psum | solution.py:33
  125.2 0.0 copy-start.3
  125.2 0.6 pad_maximum_fusion
  125.8 90.4 %all-reduce.4.cloned.1.call-done = f32[4096,256]{1,0:T(8,128)} async-done(((f32[4096,256]{1,0:T(8,128)}), f32[4096,256]{1,0:T(8,128)}) %all-reduce.4.cloned.1.call-update) | async-done | bytes 4194320 | tf_op jit(solution)/shard_map/psum | solution.py:33
  216.2 3.9 %fusion.6 = f32[4096,256]{1,0:T(8,128)} fusion(f32[4096,256]{1,0:T(8,128)} %all-reduce.4.cloned.1.call-done, bf16[4096,256]{1,0:T(8,128)(2,1)S(1)} %copy-done.1, f32[4096]{0:T(1024)S(1)} %broadcast_add_fusion), kind=kLoop, calls=%fused_computation.17 | loop fusion | flops 4194304 | bytes 10502144 | tf_op jit(solution)/shard_map/div | solution.py:34
  220.2 0.0 copy-done.3
  (3 shorter events, 0.0 us)
Async XLA Ops:
  7.2 5.4 %copy-start.1 = (bf16[4096,256]{1,0:T(8,128)(2,1)S(1)}, bf16[4096,256]{1,0:T(8,128)(2,1)}, u32[]{:S(2)}) copy-start(bf16[4096,256]{1,0:T(8,128)(2,1)} %param.3) | copy-start | bytes 6291460
  7.2 5.4 %copy-start.2 = (bf16[1024,256]{1,0:T(8,128)(2,1)S(1)}, bf16[1024,256]{1,0:T(8,128)(2,1)}, u32[]{:S(2)}) copy-start(bf16[1024,256]{1,0:T(8,128)(2,1)} %param.2) | copy-start | bytes 1572868
  7.2 209.0 %all-reduce.4.cloned.1.call-start = ((), (), s32[]{:S(2)}) async-start(), calls=%async_computation | async-start | bytes 8388608 | tf_op jit(solution)/shard_map/psum | solution.py:33
  12.6 5.7 %copy-start = (f32[512,4096]{1,0:T(8,128)}, f32[512,4096]{1,0:T(8,128)S(1)}, u32[]{:S(2)}) copy-start(f32[512,4096]{1,0:T(8,128)S(1)} %fusion.12) | copy-start | bytes 25165828
  125.2 95.0 %copy-start.3 = (f32[4096]{0:T(1024)}, f32[4096]{0:T(1024)S(1)}, u32[]{:S(2)}) copy-start(f32[4096]{0:T(1024)S(1)} %psum.31) | copy-start | bytes 49156
Sparse Core Ops, SparseCore 0:
  44.5 171.6 all-reduce.3
where the time goes:
time: 227 us
  waiting for transfers between devices  90.5 us (40%)
  blocking collectives  85.8 us (38%)
  other arithmetic  23.2 us (10%)
  between operations  14.1 us (6%)
  matrix products  12.6 us (6%)
    psum x1, waiting for transfers between devices, body(): all_sums, all_counts = lax.psum((sums, counts), 'dp')  90.4 us
    psum x1, blocking collectives, body(): all_sums, all_counts = lax.psum((sums, counts), 'dp')  80.8 us
    reduce_sum x1, other arithmetic, body(): counts = counts + jnp.sum(resp.astype(jnp.float32), axis=0)  8.66 us
    dot_general x2, matrix products, body(): jnp.einsum('nd,kd->nk', piece, centroids, preferred_element_type=jnp.floa...  7.92 us
    reduce_sum x1, other arithmetic, body(): total = lax.psum(jnp.sum(weights, axis=1), 'cent')  7.63 us
    dot_general x2, matrix products, body(): jnp.einsum('nk,nd->kd', resp, piece, preferred_element_type=jnp.float32)  4.69 us
  transfers between devices with their start and end apart: 1, of which 1 were waited for; matrix products, arithmetic and copies ran while one was open for 0% of the time, Pallas kernels for 0%

commit v1 on v0

v1 whole, which is shorter than its diff:
```python
import functools
import math

import jax
import jax.numpy as jnp
from jax import lax
from jax.experimental import pallas as pl
from jax.experimental.pallas import tpu as pltpu
from jax.sharding import PartitionSpec as P

prior_mass = 0.5
VMEM_LIMIT = 48 * 1024 * 1024
NT = (((1,), (1,)), ((), ()))
NN = (((1,), (0,)), ((), ()))


def call(kernel, out_shape, *args, name, scratch=(), flops=0):
    vmem = pl.BlockSpec(memory_space=pltpu.VMEM)
    return pl.pallas_call(
        kernel,
        out_shape=out_shape,
        in_specs=[vmem] * len(args),
        out_specs=jax.tree.map(lambda _: vmem, out_shape),
        scratch_shapes=list(scratch),
        compiler_params=pltpu.CompilerParams(vmem_limit_bytes=VMEM_LIMIT),
        cost_estimate=pl.CostEstimate(
            flops=flops,
            bytes_accessed=sum(a.size * a.dtype.itemsize for a in args),
            transcendentals=0,
        ),
        name=name,
    )(*args)


def f32(*shape):
    return jax.ShapeDtypeStruct(shape, jnp.float32)


def prepare_kernel(c_ref, twice_ref, norm_ref):
    c = c_ref[...].astype(jnp.float32)
    twice_ref[...] = (2.0 * c).astype(jnp.bfloat16)
    norm_ref[...] = jnp.broadcast_to(jnp.sum(c * c, axis=1, keepdims=True), norm_ref.shape)


def shifted(norm, width):
    return jnp.concatenate([norm] * (width // norm.shape[1]), axis=1) if width > norm.shape[1] else norm[:, :width]


def stats_kernel(count, twice_ref, norm_ref, *refs):
    x_refs, out_ref = refs[:count], refs[count]
    twice = twice_ref[...]
    for i, x_ref in enumerate(x_refs):
        rows = x_ref.shape[0]
        tile = min(256, rows)
        for start in range(0, rows, tile):
            x = x_ref[start : start + tile, :].astype(jnp.bfloat16)
            dots = lax.dot_general(twice, x, NT, preferred_element_type=jnp.float32)
            score = dots - shifted(norm_ref[...], tile)
            top = jnp.max(score, axis=0, keepdims=True)
            total = jnp.sum(jnp.exp(score - top), axis=0, keepdims=True)
            out_ref[0, i : i + 1, start : start + tile] = top
            out_ref[1, i : i + 1, start : start + tile] = total


def stats(twice, norm, blocks):
    rows = blocks[0].shape[0]
    flops = 2 * twice.shape[0] * twice.shape[1] * rows * len(blocks)
    return call(
        functools.partial(stats_kernel, len(blocks)),
        f32(2, len(blocks), rows),
        twice,
        norm,
        *blocks,
        name="stats",
        flops=flops,
    )


def sums_kernel(count, lines, twice_ref, norm_ref, *refs):
    x_refs = refs[:count]
    st_refs = refs[count : 2 * count]
    out_ref, lse_ref, acc_ref, cnt_ref = refs[2 * count :]
    local, width = twice_ref.shape
    for b in range(count):
        tops = [st_refs[s][0, b ^ s : (b ^ s) + 1, :] for s in range(count)]
        totals = [st_refs[s][1, b ^ s : (b ^ s) + 1, :] for s in range(count)]
        top = functools.reduce(jnp.maximum, tops)
        total = functools.reduce(jnp.add, [t * jnp.exp(m - top) for m, t in zip(tops, totals)])
        lse_ref[b : b + 1, :] = top + jnp.log(total)
    twice = twice_ref[...]
    first = True
    for b in range(count):
        rows = x_refs[b].shape[0]
        tile = min(256, rows)
        for start in range(0, rows, tile):
            x = x_refs[b][start : start + tile, :].astype(jnp.bfloat16)
            dots = lax.dot_general(twice, x, NT, preferred_element_type=jnp.float32)
            score = dots - shifted(norm_ref[...], tile)
            resp = jnp.exp(score - lse_ref[b : b + 1, start : start + tile]).astype(jnp.bfloat16)
            part = lax.dot_general(resp, x, NN, preferred_element_type=jnp.float32)
            wide = resp.astype(jnp.float32)
            lanes = min(128, tile)
            counted = functools.reduce(
                jnp.add, [wide[:, k : k + lanes] for k in range(0, tile, lanes)]
            )
            if first:
                acc_ref[...] = part
                cnt_ref[...] = counted
                first = False
            else:
                acc_ref[...] += part
                cnt_ref[...] += counted
    size = local // lines
    for l in range(lines):
        out_ref[l, 0:size, :] = acc_ref[l * size : (l + 1) * size, :]
        turned = jnp.sum(cnt_ref[l * size : (l + 1) * size, :].T, axis=0, keepdims=True)
        if size < width:
            turned = jnp.concatenate([turned, jnp.zeros((1, width - size), jnp.float32)], axis=1)
        out_ref[l, size : size + 8, :] = jnp.broadcast_to(turned, (8, width))


def finish_kernel(mine_ref, left_ref, right_ref, c_ref, out_ref):
    size, width = c_ref.shape
    total = mine_ref[...] + left_ref[...] + right_ref[...]
    counts = total[size:, :]
    column = counts.T[:size, 0:1]
    new = (total[:size, :] + prior_mass * c_ref[...].astype(jnp.float32)) / (column + prior_mass)
    out_ref[0:size, :] = new
    out_ref[size:, :] = counts


def body(n, cores, points, centroids):
    rows, width = points.shape
    local_cent = centroids.shape[0]
    lines = n // 4
    me = lax.axis_index("dp")
    core = lax.axis_index("cent")
    plane = lax.rem(me, 4)
    line = lax.div(me, 4)
    block = rows // cores
    share = local_cent // 4
    size = share // lines

    def flip_dp(x, bits):
        return lax.ppermute(x, "dp", [(i, i ^ bits) for i in range(n)])

    def flip_core(x, bits):
        return lax.ppermute(x, "cent", [(i, i ^ bits) for i in range(cores)])

    def up(x, last):
        return lax.ppermute(x, "dp", [(i, i + 4) for i in range(4 * min(last, lines - 1))])

    def down(x, last):
        return lax.ppermute(
            x, "dp", [(i, i - 4) for i in range(n - 4 * min(last, lines - 1), n)]
        )

    blocks = [None] * (4 * cores)
    for rc in range(cores):
        blocks[rc] = lax.dynamic_slice_in_dim(points, (core ^ rc) * block, block, axis=0)
    own = blocks[0].astype(jnp.float32)
    near = [flip_dp(own, 1), flip_dp(own, 2)]
    half = block // 2
    far = [flip_dp(near[0][:half], 2), flip_dp(near[1][half:], 1)]
    blocks[cores] = near[0]
    blocks[2 * cores] = near[1]
    blocks[3 * cores] = jnp.concatenate(far, axis=0)
    for k in (1, 2, 3):
        for rc in range(1, cores):
            blocks[k * cores + rc] = flip_core(blocks[k * cores], rc)

    mine = lax.dynamic_slice_in_dim(centroids, plane * share, share, axis=0)
    twice, norm = call(
        prepare_kernel,
        (jax.ShapeDtypeStruct((share, width), jnp.bfloat16), f32(share, 128)),
        mine,
        name="prepare",
    )
    parts = [stats(twice, norm, blocks[k * cores : (k + 1) * cores]) for k in range(4)]
    own_stats = jnp.concatenate(parts, axis=1)
    all_stats = [own_stats]
    for s in range(1, 4 * cores):
        perm = [(i, i ^ s) if cores == 1 else (i, (((i // cores) ^ (s // cores)) * cores) + ((i % cores) ^ (s % cores))) for i in range(n * cores)]
        all_stats.append(lax.ppermute(own_stats, ("dp", "cent"), perm))

    payload, lse = call(
        functools.partial(sums_kernel, 4 * cores, lines),
        (f32(lines, size + 8, width), f32(4 * cores, block)),
        twice,
        norm,
        *blocks,
        *all_stats,
        name="sums",
        scratch=[
            pltpu.VMEM((share, width), jnp.float32),
            pltpu.VMEM((share, min(128, block)), jnp.float32),
        ],
        flops=4 * share * width * 4 * rows,
    )
    own_lse = [lax.dynamic_index_in_dim(lse, core ^ rc, axis=0, keepdims=False) for rc in range(cores)]
    log_evidence = jnp.concatenate(own_lse, axis=0) - math.log(local_cent * cores)

    def pick(place):
        return lax.dynamic_index_in_dim(payload, jnp.clip(place, 0, lines - 1), axis=0, keepdims=False)

    from_left = from_right = None
    for t in range(1, lines):
        send_up = pick(line + lines - t)
        send_down = pick(line - lines + t)
        if t > 1:
            send_up = send_up + from_left
            send_down = send_down + from_right
        from_left, from_right = up(send_up, t), down(send_down, t)
    own_cent = lax.dynamic_slice_in_dim(mine, line * size, size, axis=0)
    done = call(
        finish_kernel,
        f32(size + 8, width),
        pick(line),
        from_left,
        from_right,
        own_cent,
        name="finish",
    )

    lefts, rights = [done], [done]
    for t in range(1, lines):
        lefts.append(lax.ppermute(lefts[-1], "dp", [(i, i + 4) for i in range(4 * (t - 1), n - 4)]))
        rights.append(lax.ppermute(rights[-1], "dp", [(i, i - 4) for i in range(4, n - 4 * (t - 1))]))
    order = [sorted(range(lines), key=lambda l: (abs(l - z), (l - z) % 2 if z % 2 else l, l)) for z in range(lines)]
    order = [[z] + sorted([l for l in range(lines) if l != z], key=lambda l: (abs(l - z), l != z ^ 1)) for z in range(lines)]
    table = jnp.array(order, jnp.int32)
    column = [done]
    for k in range(1, lines):
        column.append(
            lax.select_n(
                line,
                *[
                    lefts[z - order[z][k]] if order[z][k] < z else rights[order[z][k] - z]
                    for z in range(lines)
                ],
            )
        )
    over_x = [flip_dp(b, 1) for b in column]
    over_y = [flip_dp(b, 2) for b in column]
    cut = lines // 2
    over_xy = [flip_dp(b, 2) for b in over_x[:cut]] + [flip_dp(b, 1) for b in over_y[cut:]]

    new = jnp.zeros((4 * lines * size, width), jnp.float32)
    counts = jnp.zeros((4 * lines, size), jnp.float32)
    for k in range(lines):
        at = lax.dynamic_index_in_dim(lax.dynamic_index_in_dim(table, line, 0, False), k, 0, False)
        for bits, group in enumerate((column, over_x, over_y, over_xy)):
            place = (plane ^ bits) * lines + at
            new = lax.dynamic_update_slice_in_dim(new, group[k][:size], place * size, axis=0)
            counts = lax.dynamic_update_slice_in_dim(counts, group[k][size : size + 1, :size], place, axis=0)
    return new, counts.reshape(-1), log_evidence


def solution(mesh):
    n, cores = mesh.shape["dp"], mesh.shape["cent"]
    return jax.shard_map(
        functools.partial(body, n, cores),
        mesh=mesh,
        in_specs=(P("dp", None), P("cent", None)),
        out_specs=(P("cent", None), P("cent"), P("dp")),
        check_vma=False,
    )
```

time: 227 us -> 180 us (0.79)
  blocking collectives: 85.8 us -> 0 us
  starting transfers between devices: 0.04 us -> 62.6 us
  waiting for transfers between devices: 90.5 us -> 44.3 us
  local copies, waits for them, and re-layouts: 0.77 us -> 36.6 us
  Pallas kernels: 0 us -> 16.3 us
  other arithmetic: 23.2 us -> 7.09 us
  matrix products: 12.6 us -> 0 us
  between operations: 14.1 us -> 11.5 us
    psum x1 -> x0, waiting for transfers between devices: 90.4 us -> none  [body(): all_sums, all_counts = lax.psum((sums, counts), 'dp')]
    psum x2 -> x0, blocking collectives: 83.2 us -> none  [the longest x1 80.8 us: body(): all_sums, all_counts = lax.psum((sums, counts), 'dp')]
    ppermute x0 -> x38, starting transfers between devices: none -> 62.6 us  [the longest x3 21.5 us: up(): lax.ppermute(x, 'dp', [(i, i + 4) for i in range(4 * min(last, lines - 1))])]
    ppermute x0 -> x38, waiting for transfers between devices: none -> 44.3 us  [the longest x16 21.2 us: flip_dp(): return lax.ppermute(x, 'dp', [(i, i ^ bits) for i in range(n)])]
    dynamic_update_slice x0 -> x32, local copies, waits for them, and re-layouts: none -> 19.9 us  [the longest x16 19.4 us: body(): lax.dynamic_update_slice_in_dim(new, group[k][:size], place * size, axis=0)]
    pallas_call x0 -> x7, Pallas kernels: none -> 16.3 us  [call(): pl.pallas_call(kernel, out_shape=out_shape, in_specs=[vmem] * len(args),...]
    reduce_sum x2 -> x0, other arithmetic: 16.3 us -> none  [the longest x1 8.66 us: body(): counts = counts + jnp.sum(resp.astype(jnp.float32), axis=0)]
    dot_general x4 -> x0, matrix products: 12.6 us -> none  [the longest x2 7.92 us: body(): jnp.einsum('nd,kd->nk', piece, centroids, preferred_element_type=jnp.floa...]
  transfers between devices with their start and end apart: 1 -> 38, of which waited for: 1 -> 14; matrix products, arithmetic and copies ran while one was open for 0% -> 14% of each run, Pallas kernels for 0% -> 4%
where the time goes in v1:
time: 180 us; the launch traced here: 178 us
  starting transfers between devices  62.6 us (35%)
  waiting for transfers between devices  44.3 us (25%)
  local copies, waits for them, and re-layouts  36.6 us (20%)
  Pallas kernels  16.3 us (9%)
  between operations  11.5 us (6%)
  other arithmetic  7.09 us (4%)
    ppermute x3, starting transfers between devices, up(): lax.ppermute(x, 'dp', [(i, i + 4) for i in range(4 * min(last, lines - 1))])  21.5 us
    ppermute x16, waiting for transfers between devices, flip_dp(): return lax.ppermute(x, 'dp', [(i, i ^ bits) for i in range(n)])  21.2 us
    ppermute x16, starting transfers between devices, flip_dp(): return lax.ppermute(x, 'dp', [(i, i ^ bits) for i in range(n)])  20.5 us
    dynamic_update_slice x16, local copies, waits for them, and re-layouts, body(): lax.dynamic_update_slice_in_dim(new, group[k][:size], place * size, axis=0)  19.4 us
    pallas_call x7, Pallas kernels, call(): pl.pallas_call(kernel, out_shape=out_shape, in_specs=[vmem] * len(args),...  16.3 us
    ppermute x3, waiting for transfers between devices, up(): lax.ppermute(x, 'dp', [(i, i + 4) for i in range(4 * min(last, lines - 1))])  11.2 us
    ppermute x7, starting transfers between devices, body(): all_stats.append(lax.ppermute(own_stats, ('dp', 'cent'), perm))  6.47 us
    ppermute x3, starting transfers between devices, body(): lax.ppermute(lefts[-1], 'dp', [(i, i + 4) for i in range(4 * (t - 1), n -...  6.43 us
  transfers between devices with their start and end apart: 38, of which 14 were waited for; matrix products, arithmetic and copies ran while one was open for 14% of the time, Pallas kernels for 4%

profile of v1, /device:TPU:0, one launch (start us, length us, event | category | flops | bytes accessed | tf_op | source)
XLA Modules:
  0.0 178.4 jit_solution(14581428632433478083)
XLA Ops:
  0.7 1.9 %fusion = (f32[512,256]{1,0:T(8,128)S(1)}, bf16[512,256]{1,0:T(8,128)(2,1)S(1)}, bf16[512,256]{1,0:T(8,128)(2,1)}) fusion(bf16[1024,256]{1,0:T(8,128)(2,1)} %param.3, s32[]{:T(128)S(6)} %select_n.197, s32[]{:T(128)S(6)} %select_n.198), kind=kLoop, calls=%fused_computation.37 | loop fusion | flops 131072 | bytes 1572872 | tf_op jit(solution)/shard_map/convert_element_type | solution.py:161
  2.6 2.9 %collective-permute-start = (f32[512,256]{1,0:T(8,128)S(1)}, f32[512,256]{1,0:T(8,128)}, u32[]{:S(2)}, u32[]{:S(2)}) collective-permute-start(f32[512,256]{1,0:T(8,128)S(1)} %get-tuple-element.11), channel_id=1, source_target_pairs={{0,2},{2,0},{4,6},{6,4},{8,10},{10,8},{12,14},{14,12},{16,18},{18,... | collective-permute-start | bytes 1572872 | tf_op jit(solution)/shard_map/ppermute | solution.py:145
  5.5 1.5 collective-permute-start.2
  7.1 10.5 %collective-permute-done.refs_0_.refs_2_ = f32[512,256]{1,0:T(8,128)} collective-permute-done((f32[512,256]{1,0:T(8,128)S(1)}, f32[512,256]{1,0:T(8,128)}, u32[]{:S(2)}, u32[]{:S(2)}) %collective-permute-start) | collective-permute-done | bytes 524320 | tf_op jit(solution)/shard_map/ppermute | solution.py:145
  18.5 1.8 %collective-permute-start.4 = (f32[256,256]{1,0:T(8,128)S(1)}, f32[256,256]{1,0:T(8,128)S(1)}, u32[]{:S(2)}, u32[]{:S(2)}) collective-permute-start(f32[256,256]{1,0:T(8,128)S(1)} %slice.140), channel_id=1, source_target_pairs={{0,4},{2,6},{4,0},{6,2},{8,12},{10,14},{12,8},{14,10},{16,20},{18,... | collective-permute-start | bytes 786440 | tf_op jit(solution)/shard_map/ppermute | solution.py:145
  21.3 1.6 collective-permute-start.5
  23.4 2.7 %collective-permute-done.4 = f32[256,256]{1,0:T(8,128)S(1)} collective-permute-done((f32[256,256]{1,0:T(8,128)S(1)}, f32[256,256]{1,0:T(8,128)S(1)}, u32[]{:S(2)}, u32[]{:S(2)}) %collective-permute-start.4) | collective-permute-done | bytes 262176 | tf_op jit(solution)/shard_map/ppermute | solution.py:145
  26.8 1.5 collective-permute-done.5
  30.2 1.3 stats.4
  31.6 2.5 %stats.6 = f32[2,2,512]{2,1,0:T(2,128)S(1)} custom-call(bf16[1024,256]{1,0:T(8,128)(2,1)S(1)} %get-tuple-element.7.twice_ref, f32[1024,128]{1,0:T(8,128)S(1)} %get-tuple-element.8.norm_ref, f32[512,256]{1,0:T(8,128)} %collective-permute-done.2.refs_0_.refs_4_, f32[512,256]{1,0:T(8,128)} %collective-permute-done.3.refs_1_.refs_5_), custom_call_target="tpu_custom_call" | custom-call | flops 536870912 | bytes 2097152 | tf_op jit(solution)/shard_map/stats/pallas_call | solution.py:19
  34.1 2.5 %stats.5 = f32[2,2,512]{2,1,0:T(2,128)S(1)} custom-call(bf16[1024,256]{1,0:T(8,128)(2,1)S(1)} %get-tuple-element.7.twice_ref, f32[1024,128]{1,0:T(8,128)S(1)} %get-tuple-element.8.norm_ref, f32[512,256]{1,0:T(8,128)} %collective-permute-done.refs_0_.refs_2_, f32[512,256]{1,0:T(8,128)} %collective-permute-done.1.refs_1_.refs_3_), custom_call_target="tpu_custom_call" | custom-call | flops 536870912 | bytes 2097152 | tf_op jit(solution)/shard_map/stats/pallas_call | solution.py:19
  36.7 2.5 %stats.7 = f32[2,2,512]{2,1,0:T(2,128)S(1)} custom-call(bf16[1024,256]{1,0:T(8,128)(2,1)S(1)} %get-tuple-element.7.twice_ref, f32[1024,128]{1,0:T(8,128)S(1)} %get-tuple-element.8.norm_ref, f32[512,256]{1,0:T(8,128)} %constant_dynamic-update-slice_fusion.refs_0_.refs_6_, f32[512,256]{1,0:T(8,128)} %collective-permute-done.6.refs_1_.refs_7_), custom_call_target="tpu_custom_call" | custom-call | flops 536870912 | bytes 2097152 | tf_op jit(solution)/shard_map/stats/pallas_call | solution.py:19
  39.8 1.5 collective-permute-start.8
  41.9 1.5 collective-permute-start.11
  43.3 1.4 collective-permute-start.12
  45.7 2.5 %collective-permute-done.12.refs_14_ = f32[2,8,512]{2,1,0:T(8,128)} collective-permute-done((f32[2,8,512]{2,1,0:T(8,128)S(1)}, f32[2,8,512]{2,1,0:T(8,128)}, u32[]{:S(2)}, u32[]{:S(2)}) %collective-permute-start.12) | collective-permute-done | bytes 32800 | tf_op jit(solution)/shard_map/ppermute | solution.py:184
  50.4 6.9 %sums.1 = (f32[4,264,256]{2,1,0:T(8,128)S(1)}, f32[8,512]{1,0:T(8,128)S(1)}) custom-call(bf16[1024,256]{1,0:T(8,128)(2,1)S(1)} %get-tuple-element.7.twice_ref, f32[1024,128]{1,0:T(8,128)S(1)} %get-tuple-element.8.norm_ref, bf16[512,256]{1,0:T(8,128)(2,1)S(1)} %get-tuple-element.12.refs_0_, bf16[512,256]{1,0:T(8,128)(2,1)S(1)} %copy-done.3, ...), custom_call_target="tpu_custom_call" | custom-call | flops 4294967296 | bytes 4980736 | tf_op jit(solution)/shard_map/sums/pallas_call | solution.py:19
  58.3 1.4 collective-permute-start.17
  59.7 3.5 %collective-permute-start.14 = (f32[264,256]{1,0:T(8,128)S(1)}, f32[264,256]{1,0:T(8,128)S(1)}, u32[]{:S(2)}, u32[]{:S(2)}) collective-permute-start(f32[264,256]{1,0:T(8,128)S(1)} %get-tuple-element.16), channel_id=1, source_target_pairs={{0,8},{2,10},{4,12},{6,14},{1,9},{3,11},{5,13},{7,15}} | collective-permute-start | bytes 811016 | tf_op jit(solution)/shard_map/ppermute | solution.py:151
  65.0 4.2 %collective-permute-done.14 = f32[264,256]{1,0:T(8,128)S(1)} collective-permute-done((f32[264,256]{1,0:T(8,128)S(1)}, f32[264,256]{1,0:T(8,128)S(1)}, u32[]{:S(2)}, u32[]{:S(2)}) %collective-permute-start.14) | collective-permute-done | bytes 270368 | tf_op jit(solution)/shard_map/ppermute | solution.py:151
  70.3 13.6 %collective-permute-start.15 = (f32[264,256]{1,0:T(8,128)S(1)}, f32[264,256]{1,0:T(8,128)S(1)}, u32[]{:S(2)}, u32[]{:S(2)}) collective-permute-start(f32[264,256]{1,0:T(8,128)S(1)} %get-tuple-element.14), channel_id=1, source_target_pairs={{0,8},{2,10},{4,12},{6,14},{8,16},{10,18},{12,20},{14,22},{1,9},{3... | collective-permute-start | bytes 811016 | tf_op jit(solution)/shard_map/ppermute | solution.py:151
  83.9 1.3 collective-permute-start.19
  85.2 3.2 %collective-permute-done.15 = f32[264,256]{1,0:T(8,128)S(1)} collective-permute-done((f32[264,256]{1,0:T(8,128)S(1)}, f32[264,256]{1,0:T(8,128)S(1)}, u32[]{:S(2)}, u32[]{:S(2)}) %collective-permute-start.15) | collective-permute-done | bytes 270368 | tf_op jit(solution)/shard_map/ppermute | solution.py:151
  89.3 4.4 %collective-permute-start.16 = (f32[264,256]{1,0:T(8,128)S(1)}, f32[264,256]{1,0:T(8,128)S(1)}, u32[]{:S(2)}, u32[]{:S(2)}) collective-permute-start(f32[264,256]{1,0:T(8,128)S(1)} %bitcast_add_fusion.3), channel_id=1, source_target_pairs={{0,8},{2,10},{4,12},{6,14},{8,16},{10,18},{12,20},{14,22},{16,24},... | collective-permute-start | bytes 811016 | tf_op jit(solution)/shard_map/ppermute | solution.py:151
  93.8 3.9 %collective-permute-done.16.left_ref = f32[264,256]{1,0:T(8,128)S(1)} collective-permute-done((f32[264,256]{1,0:T(8,128)S(1)}, f32[264,256]{1,0:T(8,128)S(1)}, u32[]{:S(2)}, u32[]{:S(2)}) %collective-permute-start.16) | collective-permute-done | bytes 270368 | tf_op jit(solution)/shard_map/ppermute | solution.py:151
  97.9 4.4 %collective-permute-start.24 = (f32[264,256]{1,0:T(8,128)S(1)}, f32[264,256]{1,0:T(8,128)S(1)}, u32[]{:S(2)}, u32[]{:S(2)}) collective-permute-start(f32[264,256]{1,0:T(8,128)S(1)} %finish.1), channel_id=1, source_target_pairs={{0,8},{2,10},{4,12},{6,14},{8,16},{10,18},{12,20},{14,22},{16,24},... | collective-permute-start | bytes 811016 | tf_op jit(solution)/shard_map/ppermute | solution.py:227
  104.4 1.9 %collective-permute-done.24 = f32[264,256]{1,0:T(8,128)S(1)} collective-permute-done((f32[264,256]{1,0:T(8,128)S(1)}, f32[264,256]{1,0:T(8,128)S(1)}, u32[]{:S(2)}, u32[]{:S(2)}) %collective-permute-start.24) | collective-permute-done | bytes 270368 | tf_op jit(solution)/shard_map/ppermute | solution.py:227
  107.0 4.1 %collective-permute-done.23 = f32[264,256]{1,0:T(8,128)S(1)} collective-permute-done((f32[264,256]{1,0:T(8,128)S(1)}, f32[264,256]{1,0:T(8,128)S(1)}, u32[]{:S(2)}, u32[]{:S(2)}) %collective-permute-start.23) | collective-permute-done | bytes 270368 | tf_op jit(solution)/shard_map/ppermute | solution.py:228
  126.0 1.4 collective-permute-start.34
  129.0 2.0 %copy-done.4 = f32[4096,256]{1,0:T(8,128)} copy-done((f32[4096,256]{1,0:T(8,128)}, f32[4096,256]{1,0:T(8,128)S(1)}, u32[]{:S(2)}) %copy-start.4) | copy-done | bytes 4194328
  131.9 1.7 slice_dynamic-update-slice_fusion.14
  133.6 2.2 %collective-permute-done.33 = f32[264,256]{1,0:T(8,128)} collective-permute-done((f32[264,256]{1,0:T(8,128)S(1)}, f32[264,256]{1,0:T(8,128)}, u32[]{:S(2)}, u32[]{:S(2)}) %collective-permute-start.33) | collective-permute-done | bytes 270368 | tf_op jit(solution)/shard_map/ppermute | solution.py:228
  135.8 1.3 select_select_fusion
  137.1 1.5 collective-permute-start.25
  138.7 1.7 slice_dynamic-update-slice_fusion.13
  142.3 1.5 collective-permute-start.31
  144.4 1.7 slice_dynamic-update-slice_fusion.12
  149.6 1.7 collective-permute-done.26
  151.9 3.3 %collective-permute-done.31 = f32[264,256]{1,0:T(8,128)S(1)} collective-permute-done((f32[264,256]{1,0:T(8,128)S(1)}, f32[264,256]{1,0:T(8,128)S(1)}, u32[]{:S(2)}, u32[]{:S(2)}) %collective-permute-start.31) | collective-permute-done | bytes 270368 | tf_op jit(solution)/shard_map/ppermute | solution.py:145
  155.1 1.4 collective-permute-start.32
  156.6 1.5 collective-permute-done.36
  158.0 1.4 collective-permute-start.37
  159.5 1.7 slice_dynamic-update-slice_fusion.10
  164.0 1.7 slice_dynamic-update-slice_fusion.9
  168.1 1.7 slice_dynamic-update-slice_fusion.8
  170.5 1.7 slice_dynamic-update-slice_fusion.6
  172.9 1.7 slice_dynamic-update-slice_fusion.4
  175.3 1.7 slice_dynamic-update-slice_fusion.2
  (119 shorter events, 39.6 us)
Async XLA Ops:
  0.6 28.4 %copy-start = (bf16[4096,256]{1,0:T(8,128)(2,1)S(1)}, bf16[4096,256]{1,0:T(8,128)(2,1)}, u32[]{:S(2)}) copy-start(bf16[4096,256]{1,0:T(8,128)(2,1)} %param.4) | copy-start | bytes 6291460
  2.6 15.0 %collective-permute-start = (f32[512,256]{1,0:T(8,128)S(1)}, f32[512,256]{1,0:T(8,128)}, u32[]{:S(2)}, u32[]{:S(2)}) collective-permute-start(f32[512,256]{1,0:T(8,128)S(1)} %get-tuple-element.11), channel_id=1, source_target_pairs={{0,2},{2,0},{4,6},{6,4},{8,10},{10,8},{12,14},{14,12},{16,18},{18,... | collective-permute-start | bytes 1572872 | tf_op jit(solution)/shard_map/ppermute | solution.py:145
  5.5 14.8 %collective-permute-start.2 = (f32[512,256]{1,0:T(8,128)S(1)}, f32[512,256]{1,0:T(8,128)}, u32[]{:S(2)}, u32[]{:S(2)}) collective-permute-start(f32[512,256]{1,0:T(8,128)S(1)} %get-tuple-element.11), channel_id=1, source_target_pairs={{0,4},{2,6},{4,0},{6,2},{8,12},{10,14},{12,8},{14,10},{16,20},{18,... | collective-permute-start | bytes 1572872 | tf_op jit(solution)/shard_map/ppermute | solution.py:145
  18.5 7.6 %collective-permute-start.4 = (f32[256,256]{1,0:T(8,128)S(1)}, f32[256,256]{1,0:T(8,128)S(1)}, u32[]{:S(2)}, u32[]{:S(2)}) collective-permute-start(f32[256,256]{1,0:T(8,128)S(1)} %slice.140), channel_id=1, source_target_pairs={{0,4},{2,6},{4,0},{6,2},{8,12},{10,14},{12,8},{14,10},{16,20},{18,... | collective-permute-start | bytes 786440 | tf_op jit(solution)/shard_map/ppermute | solution.py:145
  21.3 7.0 %collective-permute-start.5 = (f32[256,256]{1,0:T(8,128)S(1)}, f32[256,256]{1,0:T(8,128)S(1)}, u32[]{:S(2)}, u32[]{:S(2)}) collective-permute-start(f32[256,256]{1,0:T(8,128)S(1)} %slice.141), channel_id=1, source_target_pairs={{0,2},{2,0},{4,6},{6,4},{8,10},{10,8},{12,14},{14,12},{16,18},{18,... | collective-permute-start | bytes 786440 | tf_op jit(solution)/shard_map/ppermute | solution.py:145
  22.9 11.2 %collective-permute-start.1 = (f32[512,256]{1,0:T(8,128)}, f32[512,256]{1,0:T(8,128)}, u32[]{:S(2)}, u32[]{:S(2)}) collective-permute-start(f32[512,256]{1,0:T(8,128)} %collective-permute-done.refs_0_.refs_2_), channel_id=1, source_target_pairs={{0,1},{1,0},{2,3},{3,2},{4,5},{5,4},{6,7},{7,6},{8,9},{9,8},{10,11... | collective-permute-start | bytes 1572872 | tf_op jit(solution)/shard_map/ppermute | solution.py:148
  22.9 8.7 %collective-permute-start.3 = (f32[512,256]{1,0:T(8,128)}, f32[512,256]{1,0:T(8,128)}, u32[]{:S(2)}, u32[]{:S(2)}) collective-permute-start(f32[512,256]{1,0:T(8,128)} %collective-permute-done.2.refs_0_.refs_4_), channel_id=1, source_target_pairs={{0,1},{1,0},{2,3},{3,2},{4,5},{5,4},{6,7},{7,6},{8,9},{9,8},{10,11... | collective-permute-start | bytes 1572872 | tf_op jit(solution)/shard_map/ppermute | solution.py:148
  29.0 7.6 %collective-permute-start.6 = (f32[512,256]{1,0:T(8,128)}, f32[512,256]{1,0:T(8,128)}, u32[]{:S(2)}, u32[]{:S(2)}) collective-permute-start(f32[512,256]{1,0:T(8,128)} %constant_dynamic-update-slice_fusion.refs_0_.refs_6_), channel_id=1, source_target_pairs={{0,1},{1,0},{2,3},{3,2},{4,5},{5,4},{6,7},{7,6},{8,9},{9,8},{10,11... | collective-permute-start | bytes 1572872 | tf_op jit(solution)/shard_map/ppermute | solution.py:148
  29.3 1.0 copy-start.2
  39.3 4.1 %collective-permute-start.7 = (f32[2,8,512]{2,1,0:T(8,128)S(1)}, f32[2,8,512]{2,1,0:T(8,128)S(1)}, u32[]{:S(2)}, u32[]{:S(2)}) collective-permute-start(f32[2,8,512]{2,1,0:T(8,128)S(1)} %pad_maximum_fusion.refs_8_), channel_id=1, source_target_pairs={{0,1},{1,0},{2,3},{3,2},{4,5},{5,4},{6,7},{7,6},{8,9},{9,8},{10,11... | collective-permute-start | bytes 98312 | tf_op jit(solution)/shard_map/ppermute | solution.py:184
  39.8 4.9 %collective-permute-start.8 = (f32[2,8,512]{2,1,0:T(8,128)S(1)}, f32[2,8,512]{2,1,0:T(8,128)S(1)}, u32[]{:S(2)}, u32[]{:S(2)}) collective-permute-start(f32[2,8,512]{2,1,0:T(8,128)S(1)} %pad_maximum_fusion.refs_8_), channel_id=1, source_target_pairs={{0,2},{1,3},{2,0},{3,1},{4,6},{5,7},{6,4},{7,5},{8,10},{9,11},{10,... | collective-permute-start | bytes 98312 | tf_op jit(solution)/shard_map/ppermute | solution.py:184
  41.3 4.4 %collective-permute-start.9 = (f32[2,8,512]{2,1,0:T(8,128)S(1)}, f32[2,8,512]{2,1,0:T(8,128)S(1)}, u32[]{:S(2)}, u32[]{:S(2)}) collective-permute-start(f32[2,8,512]{2,1,0:T(8,128)S(1)} %pad_maximum_fusion.refs_8_), channel_id=1, source_target_pairs={{0,3},{1,2},{2,1},{3,0},{4,7},{5,6},{6,5},{7,4},{8,11},{9,10},{10,... | collective-permute-start | bytes 98312 | tf_op jit(solution)/shard_map/ppermute | solution.py:184
  41.3 4.4 %collective-permute-start.10 = (f32[2,8,512]{2,1,0:T(8,128)S(1)}, f32[2,8,512]{2,1,0:T(8,128)}, u32[]{:S(2)}, u32[]{:S(2)}) collective-permute-start(f32[2,8,512]{2,1,0:T(8,128)S(1)} %pad_maximum_fusion.refs_8_), channel_id=1, source_target_pairs={{0,4},{1,5},{2,6},{3,7},{4,0},{5,1},{6,2},{7,3},{8,12},{9,13},{10,... | collective-permute-start | bytes 98312 | tf_op jit(solution)/shard_map/ppermute | solution.py:184
  41.9 3.9 %collective-permute-start.11 = (f32[2,8,512]{2,1,0:T(8,128)S(1)}, f32[2,8,512]{2,1,0:T(8,128)}, u32[]{:S(2)}, u32[]{:S(2)}) collective-permute-start(f32[2,8,512]{2,1,0:T(8,128)S(1)} %pad_maximum_fusion.refs_8_), channel_id=1, source_target_pairs={{0,5},{1,4},{2,7},{3,6},{4,1},{5,0},{6,3},{7,2},{8,13},{9,12},{10,... | collective-permute-start | bytes 98312 | tf_op jit(solution)/shard_map/ppermute | solution.py:184
  43.3 4.9 %collective-permute-start.12 = (f32[2,8,512]{2,1,0:T(8,128)S(1)}, f32[2,8,512]{2,1,0:T(8,128)}, u32[]{:S(2)}, u32[]{:S(2)}) collective-permute-start(f32[2,8,512]{2,1,0:T(8,128)S(1)} %pad_maximum_fusion.refs_8_), channel_id=1, source_target_pairs={{0,6},{1,7},{2,4},{3,5},{4,2},{5,3},{6,0},{7,1},{8,14},{9,15},{10,... | collective-permute-start | bytes 98312 | tf_op jit(solution)/shard_map/ppermute | solution.py:184
  44.8 4.7 %collective-permute-start.13 = (f32[2,8,512]{2,1,0:T(8,128)S(1)}, f32[2,8,512]{2,1,0:T(8,128)}, u32[]{:S(2)}, u32[]{:S(2)}) collective-permute-start(f32[2,8,512]{2,1,0:T(8,128)S(1)} %pad_maximum_fusion.refs_8_), channel_id=1, source_target_pairs={{0,7},{1,6},{2,5},{3,4},{4,3},{5,2},{6,1},{7,0},{8,15},{9,14},{10,... | collective-permute-start | bytes 98312 | tf_op jit(solution)/shard_map/ppermute | solution.py:184
  49.4 1.0 copy-start.3
  57.3 1.0 copy-start.1
  58.3 4.9 %collective-permute-start.17 = (f32[264,256]{1,0:T(8,128)S(1)}, f32[264,256]{1,0:T(8,128)}, u32[]{:S(2)}, u32[]{:S(2)}) collective-permute-start(f32[264,256]{1,0:T(8,128)S(1)} %get-tuple-element.15), channel_id=1, source_target_pairs={{24,16},{26,18},{28,20},{30,22},{25,17},{27,19},{29,21},{31,23}} | collective-permute-start | bytes 811016 | tf_op jit(solution)/shard_map/ppermute | solution.py:154
  59.7 9.4 %collective-permute-start.14 = (f32[264,256]{1,0:T(8,128)S(1)}, f32[264,256]{1,0:T(8,128)S(1)}, u32[]{:S(2)}, u32[]{:S(2)}) collective-permute-start(f32[264,256]{1,0:T(8,128)S(1)} %get-tuple-element.16), channel_id=1, source_target_pairs={{0,8},{2,10},{4,12},{6,14},{1,9},{3,11},{5,13},{7,15}} | collective-permute-start | bytes 811016 | tf_op jit(solution)/shard_map/ppermute | solution.py:151
  64.3 4.9 %collective-permute-start.18 = (f32[264,256]{1,0:T(8,128)S(1)}, f32[264,256]{1,0:T(8,128)S(1)}, u32[]{:S(2)}, u32[]{:S(2)}) collective-permute-start(f32[264,256]{1,0:T(8,128)S(1)} %bitcast_add_fusion), channel_id=1, source_target_pairs={{16,8},{18,10},{20,12},{22,14},{24,16},{26,18},{28,20},{30,22},{17... | collective-permute-start | bytes 811016 | tf_op jit(solution)/shard_map/ppermute | solution.py:154
  70.3 18.1 %collective-permute-start.15 = (f32[264,256]{1,0:T(8,128)S(1)}, f32[264,256]{1,0:T(8,128)S(1)}, u32[]{:S(2)}, u32[]{:S(2)}) collective-permute-start(f32[264,256]{1,0:T(8,128)S(1)} %get-tuple-element.14), channel_id=1, source_target_pairs={{0,8},{2,10},{4,12},{6,14},{8,16},{10,18},{12,20},{14,22},{1,9},{3... | collective-permute-start | bytes 811016 | tf_op jit(solution)/shard_map/ppermute | solution.py:151
  83.9 9.9 %collective-permute-start.19 = (f32[264,256]{1,0:T(8,128)S(1)}, f32[264,256]{1,0:T(8,128)S(1)}, u32[]{:S(2)}, u32[]{:S(2)}) collective-permute-start(f32[264,256]{1,0:T(8,128)S(1)} %get-tuple-element.13), channel_id=1, source_target_pairs={{8,0},{10,2},{12,4},{14,6},{16,8},{18,10},{20,12},{22,14},{24,16},... | collective-permute-start | bytes 811016 | tf_op jit(solution)/shard_map/ppermute | solution.py:154
  89.3 8.4 %collective-permute-start.16 = (f32[264,256]{1,0:T(8,128)S(1)}, f32[264,256]{1,0:T(8,128)S(1)}, u32[]{:S(2)}, u32[]{:S(2)}) collective-permute-start(f32[264,256]{1,0:T(8,128)S(1)} %bitcast_add_fusion.3), channel_id=1, source_target_pairs={{0,8},{2,10},{4,12},{6,14},{8,16},{10,18},{12,20},{14,22},{16,24},... | collective-permute-start | bytes 811016 | tf_op jit(solution)/shard_map/ppermute | solution.py:151
  97.9 8.4 %collective-permute-start.24 = (f32[264,256]{1,0:T(8,128)S(1)}, f32[264,256]{1,0:T(8,128)S(1)}, u32[]{:S(2)}, u32[]{:S(2)}) collective-permute-start(f32[264,256]{1,0:T(8,128)S(1)} %finish.1), channel_id=1, source_target_pairs={{0,8},{2,10},{4,12},{6,14},{8,16},{10,18},{12,20},{14,22},{16,24},... | collective-permute-start | bytes 811016 | tf_op jit(solution)/shard_map/ppermute | solution.py:227
  102.4 8.7 %collective-permute-start.23 = (f32[264,256]{1,0:T(8,128)S(1)}, f32[264,256]{1,0:T(8,128)S(1)}, u32[]{:S(2)}, u32[]{:S(2)}) collective-permute-start(f32[264,256]{1,0:T(8,128)S(1)} %finish.1), channel_id=1, source_target_pairs={{8,0},{10,2},{12,4},{14,6},{16,8},{18,10},{20,12},{22,14},{24,16},... | collective-permute-start | bytes 811016 | tf_op jit(solution)/shard_map/ppermute | solution.py:228
  106.3 19.7 %collective-permute-start.29 = (f32[264,256]{1,0:T(8,128)S(1)}, f32[264,256]{1,0:T(8,128)S(1)}, u32[]{:S(2)}, u32[]{:S(2)}) collective-permute-start(f32[264,256]{1,0:T(8,128)S(1)} %collective-permute-done.24), channel_id=1, source_target_pairs={{8,16},{10,18},{12,20},{14,22},{16,24},{18,26},{20,28},{22,30},{9,... | collective-permute-start | bytes 811016 | tf_op jit(solution)/shard_map/ppermute | solution.py:227
  111.1 22.5 %copy-start.5 = (f32[264,256]{1,0:T(8,128)}, f32[264,256]{1,0:T(8,128)S(1)}, u32[]{:S(2)}) copy-start(f32[264,256]{1,0:T(8,128)S(1)} %collective-permute-done.23) | copy-start | bytes 811012
  111.1 16.3 %collective-permute-start.28 = (f32[264,256]{1,0:T(8,128)S(1)}, f32[264,256]{1,0:T(8,128)S(1)}, u32[]{:S(2)}, u32[]{:S(2)}) collective-permute-start(f32[264,256]{1,0:T(8,128)S(1)} %collective-permute-done.23), channel_id=1, source_target_pairs={{8,0},{10,2},{12,4},{14,6},{16,8},{18,10},{20,12},{22,14},{9,1},{1... | collective-permute-start | bytes 811016 | tf_op jit(solution)/shard_map/ppermute | solution.py:228
  123.2 7.8 %collective-permute-start.20 = (f32[264,256]{1,0:T(8,128)S(1)}, f32[264,256]{1,0:T(8,128)}, u32[]{:S(2)}, u32[]{:S(2)}) collective-permute-start(f32[264,256]{1,0:T(8,128)S(1)} %finish.1), channel_id=1, source_target_pairs={{0,2},{2,0},{4,6},{6,4},{8,10},{10,8},{12,14},{14,12},{16,18},{18,... | collective-permute-start | bytes 811016 | tf_op jit(solution)/shard_map/ppermute | solution.py:145
  124.8 13.9 %collective-permute-start.21 = (f32[264,256]{1,0:T(8,128)S(1)}, f32[264,256]{1,0:T(8,128)}, u32[]{:S(2)}, u32[]{:S(2)}) collective-permute-start(f32[264,256]{1,0:T(8,128)S(1)} %finish.1), channel_id=1, source_target_pairs={{0,4},{2,6},{4,0},{6,2},{8,12},{10,14},{12,8},{14,10},{16,20},{18,... | collective-permute-start | bytes 811016 | tf_op jit(solution)/shard_map/ppermute | solution.py:145
  126.0 7.6 %copy-start.6 = (f32[264,256]{1,0:T(8,128)}, f32[264,256]{1,0:T(8,128)S(1)}, u32[]{:S(2)}) copy-start(f32[264,256]{1,0:T(8,128)S(1)} %collective-permute-done.29) | copy-start | bytes 811012
  126.0 7.6 %collective-permute-start.34 = (f32[264,256]{1,0:T(8,128)S(1)}, f32[264,256]{1,0:T(8,128)}, u32[]{:S(2)}, u32[]{:S(2)}) collective-permute-start(f32[264,256]{1,0:T(8,128)S(1)} %collective-permute-done.29), channel_id=1, source_target_pairs={{16,24},{18,26},{20,28},{22,30},{17,25},{19,27},{21,29},{23,31}} | collective-permute-start | bytes 811016 | tf_op jit(solution)/shard_map/ppermute | solution.py:227
  127.3 6.2 %copy-start.7 = (f32[264,256]{1,0:T(8,128)}, f32[264,256]{1,0:T(8,128)S(1)}, u32[]{:S(2)}) copy-start(f32[264,256]{1,0:T(8,128)S(1)} %collective-permute-done.28) | copy-start | bytes 811012
  127.4 8.5 %collective-permute-start.33 = (f32[264,256]{1,0:T(8,128)S(1)}, f32[264,256]{1,0:T(8,128)}, u32[]{:S(2)}, u32[]{:S(2)}) collective-permute-start(f32[264,256]{1,0:T(8,128)S(1)} %collective-permute-done.28), channel_id=1, source_target_pairs={{8,0},{10,2},{12,4},{14,6},{9,1},{11,3},{13,5},{15,7}} | collective-permute-start | bytes 811016 | tf_op jit(solution)/shard_map/ppermute | solution.py:228
  129.0 2.0 %copy-start.4 = (f32[4096,256]{1,0:T(8,128)}, f32[4096,256]{1,0:T(8,128)S(1)}, u32[]{:S(2)}) copy-start(f32[4096,256]{1,0:T(8,128)S(1)} %slice_dynamic-update-slice_fusion.15) | copy-start | bytes 12582916
  131.0 13.4 %collective-permute-start.22 = (f32[264,256]{1,0:T(8,128)}, f32[264,256]{1,0:T(8,128)}, u32[]{:S(2)}, u32[]{:S(2)}) collective-permute-start(f32[264,256]{1,0:T(8,128)} %collective-permute-done.20), channel_id=1, source_target_pairs={{0,4},{2,6},{4,0},{6,2},{8,12},{10,14},{12,8},{14,10},{16,20},{18,... | collective-permute-start | bytes 811016 | tf_op jit(solution)/shard_map/ppermute | solution.py:145
  137.1 10.6 %collective-permute-start.25 = (f32[264,256]{1,0:T(8,128)S(1)}, f32[264,256]{1,0:T(8,128)}, u32[]{:S(2)}, u32[]{:S(2)}) collective-permute-start(f32[264,256]{1,0:T(8,128)S(1)} %get-tuple-element.20), channel_id=1, source_target_pairs={{0,2},{2,0},{4,6},{6,4},{8,10},{10,8},{12,14},{14,12},{16,18},{18,... | collective-permute-start | bytes 811016 | tf_op jit(solution)/shard_map/ppermute | solution.py:145
  141.8 9.6 %collective-permute-start.26 = (f32[264,256]{1,0:T(8,128)S(1)}, f32[264,256]{1,0:T(8,128)}, u32[]{:S(2)}, u32[]{:S(2)}) collective-permute-start(f32[264,256]{1,0:T(8,128)S(1)} %get-tuple-element.20), channel_id=1, source_target_pairs={{0,4},{2,6},{4,0},{6,2},{8,12},{10,14},{12,8},{14,10},{16,20},{18,... | collective-permute-start | bytes 811016 | tf_op jit(solution)/shard_map/ppermute | solution.py:145
  142.3 12.8 %collective-permute-start.31 = (f32[264,256]{1,0:T(8,128)S(1)}, f32[264,256]{1,0:T(8,128)S(1)}, u32[]{:S(2)}, u32[]{:S(2)}) collective-permute-start(f32[264,256]{1,0:T(8,128)S(1)} %get-tuple-element.19), channel_id=1, source_target_pairs={{0,4},{2,6},{4,0},{6,2},{8,12},{10,14},{12,8},{14,10},{16,20},{18,... | collective-permute-start | bytes 811016 | tf_op jit(solution)/shard_map/ppermute | solution.py:145
  143.9 14.2 %collective-permute-start.36 = (f32[264,256]{1,0:T(8,128)S(1)}, f32[264,256]{1,0:T(8,128)S(1)}, u32[]{:S(2)}, u32[]{:S(2)}) collective-permute-start(f32[264,256]{1,0:T(8,128)S(1)} %get-tuple-element.18), channel_id=1, source_target_pairs={{0,4},{2,6},{4,0},{6,2},{8,12},{10,14},{12,8},{14,10},{16,20},{18,... | collective-permute-start | bytes 811016 | tf_op jit(solution)/shard_map/ppermute | solution.py:145
  146.8 15.8 %collective-permute-start.30 = (f32[264,256]{1,0:T(8,128)S(1)}, f32[264,256]{1,0:T(8,128)}, u32[]{:S(2)}, u32[]{:S(2)}) collective-permute-start(f32[264,256]{1,0:T(8,128)S(1)} %get-tuple-element.19), channel_id=1, source_target_pairs={{0,2},{2,0},{4,6},{6,4},{8,10},{10,8},{12,14},{14,12},{16,18},{18,... | collective-permute-start | bytes 811016 | tf_op jit(solution)/shard_map/ppermute | solution.py:145
  147.7 15.6 %collective-permute-start.35 = (f32[264,256]{1,0:T(8,128)S(1)}, f32[264,256]{1,0:T(8,128)}, u32[]{:S(2)}, u32[]{:S(2)}) collective-permute-start(f32[264,256]{1,0:T(8,128)S(1)} %get-tuple-element.18), channel_id=1, source_target_pairs={{0,2},{2,0},{4,6},{6,4},{8,10},{10,8},{12,14},{14,12},{16,18},{18,... | collective-permute-start | bytes 811016 | tf_op jit(solution)/shard_map/ppermute | solution.py:145
  151.4 14.3 %collective-permute-start.27 = (f32[264,256]{1,0:T(8,128)}, f32[264,256]{1,0:T(8,128)}, u32[]{:S(2)}, u32[]{:S(2)}) collective-permute-start(f32[264,256]{1,0:T(8,128)} %collective-permute-done.25), channel_id=1, source_target_pairs={{0,4},{2,6},{4,0},{6,2},{8,12},{10,14},{12,8},{14,10},{16,20},{18,... | collective-permute-start | bytes 811016 | tf_op jit(solution)/shard_map/ppermute | solution.py:145
  155.1 11.4 %collective-permute-start.32 = (f32[264,256]{1,0:T(8,128)S(1)}, f32[264,256]{1,0:T(8,128)}, u32[]{:S(2)}, u32[]{:S(2)}) collective-permute-start(f32[264,256]{1,0:T(8,128)S(1)} %collective-permute-done.31), channel_id=1, source_target_pairs={{0,2},{2,0},{4,6},{6,4},{8,10},{10,8},{12,14},{14,12},{16,18},{18,... | collective-permute-start | bytes 811016 | tf_op jit(solution)/shard_map/ppermute | solution.py:145
  158.0 9.4 %collective-permute-start.37 = (f32[264,256]{1,0:T(8,128)S(1)}, f32[264,256]{1,0:T(8,128)S(1)}, u32[]{:S(2)}, u32[]{:S(2)}) collective-permute-start(f32[264,256]{1,0:T(8,128)S(1)} %collective-permute-done.36), channel_id=1, source_target_pairs={{0,2},{2,0},{4,6},{6,4},{8,10},{10,8},{12,14},{14,12},{16,18},{18,... | collective-permute-start | bytes 811016 | tf_op jit(solution)/shard_map/ppermute | solution.py:145

commit v2 on v0

v2 whole, which is shorter than its diff:
```python
import functools
import math

import jax
import jax.numpy as jnp
from jax import lax
from jax.experimental import pallas as pl
from jax.experimental.pallas import tpu as pltpu
from jax.sharding import PartitionSpec as P

prior_mass = 0.5
VMEM_LIMIT = 48 * 1024 * 1024
LANES = 128
NT = (((1,), (1,)), ((), ()))
NN = (((1,), (0,)), ((), ()))
VMEM = pl.BlockSpec(memory_space=pltpu.VMEM)
SMEM = pl.BlockSpec(memory_space=pltpu.SMEM)
ANY = pl.BlockSpec(memory_space=pl.ANY)


def f32(*shape):
    return jax.ShapeDtypeStruct(shape, jnp.float32)


def call(kernel, out_shape, in_specs, args, name, out_specs=None, scratch=(), flops=0, aliases={}):
    return pl.pallas_call(
        kernel,
        out_shape=out_shape,
        in_specs=in_specs,
        out_specs=jax.tree.map(lambda _: VMEM, out_shape) if out_specs is None else out_specs,
        scratch_shapes=list(scratch),
        input_output_aliases=aliases,
        compiler_params=pltpu.CompilerParams(vmem_limit_bytes=VMEM_LIMIT),
        cost_estimate=pl.CostEstimate(
            flops=flops,
            bytes_accessed=sum(a.size * a.dtype.itemsize for a in args),
            transcendentals=0,
        ),
        name=name,
    )(*args)


def open_kernel(where_ref, points_ref, first_ref, second_ref):
    half = first_ref.shape[0]
    start = pl.multiple_of(where_ref[1] * (2 * half), 2 * half)
    first_ref[...] = points_ref[pl.ds(start, half), :].astype(jnp.float32)
    second_ref[...] = points_ref[pl.ds(pl.multiple_of(start + half, half), half), :].astype(jnp.float32)


def widen(norm, width):
    if width <= norm.shape[1]:
        return norm[:, :width]
    return jnp.concatenate([norm] * (width // norm.shape[1]), axis=1)


def norms(c):
    c = c.astype(jnp.float32)
    return jnp.broadcast_to(jnp.sum(c * c, axis=1, keepdims=True), (c.shape[0], LANES))


def stats_kernel(points_ref, c_ref, out_ref, norm_ref):
    rows, local = points_ref.shape[0], c_ref.shape[0]
    tile, chunk = min(256, rows), min(1024, local)
    for part in range(0, local, chunk):
        c = c_ref[part : part + chunk, :]
        norm_ref[...] = norms(c)
        twice = c + c
        for start in range(0, rows, tile):
            at = slice(start, start + tile)
            dots = lax.dot_general(twice, points_ref[at, :], NT, preferred_element_type=jnp.float32)
            score = dots - widen(norm_ref[...], tile)
            top = jnp.max(score, axis=0, keepdims=True)
            total = jnp.sum(jnp.exp(score - top), axis=0, keepdims=True)
            if part:
                old_top, old_total = out_ref[0:1, at], out_ref[1:2, at]
                new_top = jnp.maximum(old_top, top)
                total = old_total * jnp.exp(old_top - new_top) + total * jnp.exp(top - new_top)
                top = new_top
            out_ref[0:1, at] = top
            out_ref[1:2, at] = total


def add_block(twice, norm, x, lse, acc_ref, cnt_ref, first):
    dots = lax.dot_general(twice, x, NT, preferred_element_type=jnp.float32)
    score = dots - widen(norm, x.shape[0])
    resp = jnp.exp(score - lse).astype(jnp.bfloat16)
    part = lax.dot_general(resp, x, NN, preferred_element_type=jnp.float32)
    wide = resp.astype(jnp.float32)
    lanes = cnt_ref.shape[1]
    counted = functools.reduce(
        jnp.add, [wide[:, k : k + lanes] for k in range(0, x.shape[0], lanes)]
    )
    if first:
        acc_ref[...] = part
        cnt_ref[...] = counted
    else:
        acc_ref[...] += part
        cnt_ref[...] += counted


def near_kernel(cores, where_ref, points_ref, c_ref, lse_ref, *refs):
    x_refs, lse_refs = refs[: 4 * cores], refs[4 * cores : 4 * cores + 2]
    acc_ref, cnt_ref, twice_ref, norm_ref, own_ref = refs[4 * cores + 2 :]
    share, size = twice_ref.shape[0], own_ref.shape[0]
    plane, line = lax.rem(where_ref[0], 4), lax.div(where_ref[0], 4)
    start = pl.multiple_of(plane * share, share)
    c = c_ref[pl.ds(start, share), :]
    twice_ref[...] = c + c
    norm_ref[...] = norms(c)
    own_ref[...] = c_ref[pl.ds(pl.multiple_of(start + line * size, size), size), :]
    half = points_ref.shape[0] // (2 * cores)
    for i in range(2 * cores):
        x = points_ref[i * half : (i + 1) * half, :]
        add_block(twice_ref[...], norm_ref[...], x, lse_ref[i : i + 1, :], acc_ref, cnt_ref, i == 0)
    for k in range(2):
        add_chip(cores, where_ref, twice_ref, norm_ref, x_refs[2 * cores * k : 2 * cores * (k + 1)], lse_refs[k], acc_ref, cnt_ref)


def add_chip(cores, where_ref, twice_ref, norm_ref, x_refs, lse_ref, acc_ref, cnt_ref):
    for rc in range(cores):
        for part in range(2):
            x = x_refs[2 * rc + part][...].astype(jnp.bfloat16)
            at = 2 * (where_ref[1] ^ rc) + part
            lse = lse_ref[pl.ds(at, 1), :]
            add_block(twice_ref[...], norm_ref[...], x, lse, acc_ref, cnt_ref, False)


def far_kernel(cores, lines, where_ref, twice_ref, norm_ref, acc_in_ref, cnt_in_ref, lse_ref, *refs):
    x_refs, out_refs = refs[: 2 * cores], refs[2 * cores : 2 * cores + lines]
    acc_ref, cnt_ref = refs[2 * cores + lines :]
    acc_ref[...] = acc_in_ref[...]
    cnt_ref[...] = cnt_in_ref[...]
    add_chip(cores, where_ref, twice_ref, norm_ref, x_refs, lse_ref, acc_ref, cnt_ref)
    line = lax.div(where_ref[0], 4)
    width = acc_ref.shape[1]
    size = acc_ref.shape[0] // lines
    for r in range(lines):
        start = pl.multiple_of((line ^ r) * size, size)
        out_refs[r][0:size, :] = acc_ref[pl.ds(start, size), :]
        turned = jnp.sum(cnt_ref[pl.ds(start, size), :].T, axis=0, keepdims=True)
        if size < width:
            turned = jnp.concatenate([turned, jnp.zeros((1, width - size), jnp.float32)], axis=1)
        out_refs[r][size : size + 8, :] = jnp.broadcast_to(turned, (8, width))


def finish_kernel(c_ref, *refs):
    out_ref = refs[-1]
    size, width = c_ref.shape
    total = functools.reduce(jnp.add, [ref[...] for ref in refs[:-1]])
    counts = total[size:, :]
    column = counts.T[:size, 0:1]
    out_ref[0:size, :] = (total[:size, :] + prior_mass * c_ref[...].astype(jnp.float32)) / (
        column + prior_mass
    )
    row = lax.broadcasted_iota(jnp.int32, (8, LANES), 0)
    spread = jnp.zeros((8, LANES), jnp.float32)
    for k in range(size // LANES):
        spread = jnp.where(row == k, counts[:, k * LANES : (k + 1) * LANES], spread)
    out_ref[size:, :] = jnp.concatenate([spread] * (width // LANES), axis=1)


def place_kernel(count, lines, late, where_ref, *refs):
    block_refs = refs[:count]
    if late is None:
        new_ref, sems = refs[count:]
        chosen = range(count)
    else:
        _, new_ref, counts_ref, tiles_ref, sems = refs[count:]
        chosen = late
    width = new_ref.shape[1]
    size = block_refs[0].shape[0] - 8
    plane, line = lax.rem(where_ref[0], 4), lax.div(where_ref[0], 4)

    def place(i, names):
        bits, r = names
        return (plane ^ bits) * lines + (line ^ r)

    names = NAMES(lines)
    copies = []
    for i in chosen:
        at = pl.multiple_of(place(i, names[i]) * size, size)
        copies.append(
            pltpu.make_async_copy(block_refs[i].at[0:size, :], new_ref.at[pl.ds(at, size), :], sems.at[i])
        )
    if late is not None:
        for i in range(count):
            copies.append(
                pltpu.make_async_copy(block_refs[i].at[size:, :], tiles_ref.at[i], sems.at[count + i])
            )
    for copy in copies:
        copy.start()
    for copy in copies:
        copy.wait()
    if late is not None:
        each = size // LANES
        for i in range(count):
            for k in range(each):
                counts_ref[pl.ds(place(i, names[i]) * each + k, 1), :] = tiles_ref[i, k : k + 1, 0:LANES]


def NAMES(lines):
    cut = lines // 2
    names = [(0, r) for r in range(lines)]
    names += [(b, r) for r in range(lines) for b in (1, 2)]
    names += [(3, r) for r in range(lines)]
    return names


def body(n, cores, points, centroids):
    rows, width = points.shape
    local_cent = centroids.shape[0]
    lines = n // 4
    half = rows // (2 * cores)
    share = local_cent // 4
    size = share // lines
    where = jnp.stack([lax.axis_index("dp"), lax.axis_index("cent")]).astype(jnp.int32)

    def flip(x, bits):
        return lax.ppermute(x, "dp", [(i, i ^ bits) for i in range(n)])

    def flip_core(x, bits):
        return lax.ppermute(x, "cent", [(i, i ^ bits) for i in range(cores)])

    first, second = call(
        open_kernel, (f32(half, width), f32(half, width)), [SMEM, VMEM], (where, points), "open"
    )
    x0, y1 = flip(first, 1), flip(second, 2)
    x1, y0 = flip(second, 1), flip(first, 2)

    pair = call(
        stats_kernel,
        f32(2, rows),
        [VMEM, VMEM],
        (points, centroids),
        "stats",
        scratch=[pltpu.VMEM((min(1024, local_cent), LANES), jnp.float32)],
        flops=2 * rows * local_cent * width,
    )
    pair, x0, y1 = lax.optimization_barrier((pair, x0, y1))
    d0, d1 = flip(x0, 2), flip(y1, 1)
    pairs = [pair] + [flip_core(pair, rc) for rc in range(1, cores)]
    top = functools.reduce(jnp.maximum, [p[0] for p in pairs])
    total = functools.reduce(jnp.add, [p[1] * jnp.exp(p[0] - top) for p in pairs])
    lse = top + jnp.log(total)
    log_evidence = lse - math.log(local_cent * cores)
    lse = lse.reshape(2 * cores, half)
    lse_x, lse_y, lse_d = flip(lse, 1), flip(lse, 2), flip(lse, 3)

    def with_siblings(a, b):
        out = [a, b]
        for rc in range(1, cores):
            out += [flip_core(a, rc), flip_core(b, rc)]
        return out

    acc, cnt, twice, norm, own = call(
        functools.partial(near_kernel, cores),
        (
            f32(share, width),
            f32(share, min(LANES, half)),
            jax.ShapeDtypeStruct((share, width), jnp.bfloat16),
            f32(share, LANES),
            jax.ShapeDtypeStruct((size, width), jnp.bfloat16),
        ),
        [SMEM] + [VMEM] * (5 + 4 * cores),
        (where, points, centroids, lse, *with_siblings(x0, x1), *with_siblings(y0, y1), lse_x, lse_y),
        "near",
        flops=4 * share * width * 3 * rows,
    )
    sums = call(
        functools.partial(far_kernel, cores, lines),
        [f32(size + 8, width)] * lines,
        [SMEM] + [VMEM] * (5 + 2 * cores),
        (where, twice, norm, acc, cnt, lse_d, *with_siblings(d0, d1)),
        "far",
        scratch=[
            pltpu.VMEM((share, width), jnp.float32),
            pltpu.VMEM((share, min(LANES, half)), jnp.float32),
        ],
        flops=4 * share * width * rows,
    )
    summed = [sums[0]] + [flip(sums[r], 4 * r) for r in range(1, lines)]
    done = call(finish_kernel, f32(size + 8, width), [VMEM] * (1 + lines), (own, *summed), "finish")

    column = [done] + [flip(done, 4 * r) for r in range(1, lines)]
    over_x = [flip(b, 1) for b in column]
    over_y = [flip(b, 2) for b in column]
    cut = lines // 2
    over_xy = [flip(b, 2) for b in over_x[:cut]] + [flip(b, 1) for b in over_y[cut:]]
    blocks = column + [b for pair in zip(over_x, over_y) for b in pair] + over_xy
    count = 4 * lines
    early = count - lines
    new = call(
        functools.partial(place_kernel, early, lines, None),
        f32(local_cent, width),
        [SMEM] + [ANY] * early,
        (where, *blocks[:early]),
        "place_early",
        out_specs=ANY,
        scratch=[pltpu.SemaphoreType.DMA((early,))],
    )
    new, counts = call(
        functools.partial(place_kernel, count, lines, tuple(range(early, count))),
        (f32(local_cent, width), f32(local_cent // LANES, LANES)),
        [SMEM] + [ANY] * (count + 1),
        (where, *blocks, new),
        "place_late",
        out_specs=(ANY, VMEM),
        scratch=[pltpu.VMEM((count, 8, width), jnp.float32), pltpu.SemaphoreType.DMA((2 * count,))],
        aliases={count + 1: 0},
    )
    return new, counts.reshape(-1), log_evidence


def solution(mesh):
    n, cores = mesh.shape["dp"], mesh.shape["cent"]
    return jax.shard_map(
        functools.partial(body, n, cores),
        mesh=mesh,
        in_specs=(P("dp", None), P("cent", None)),
        out_specs=(P("cent", None), P("cent"), P("dp")),
        check_vma=False,
    )
```

time: 227 us -> 121 us (0.53)
  blocking collectives: 85.8 us -> 0 us
  starting transfers between devices: 0.04 us -> 40.8 us
  waiting for transfers between devices: 90.5 us -> 56.7 us
  other arithmetic: 23.2 us -> 0.71 us
  Pallas kernels: 0 us -> 18.7 us
  between operations: 14.1 us -> 0.78 us
  matrix products: 12.6 us -> 0 us
    psum x1 -> x0, waiting for transfers between devices: 90.4 us -> none  [body(): all_sums, all_counts = lax.psum((sums, counts), 'dp')]
    psum x2 -> x0, blocking collectives: 83.2 us -> none  [the longest x1 80.8 us: body(): all_sums, all_counts = lax.psum((sums, counts), 'dp')]
    ppermute x0 -> x34, waiting for transfers between devices: none -> 56.7 us  [the longest x27 56.6 us: flip(): return lax.ppermute(x, 'dp', [(i, i ^ bits) for i in range(n)])]
    ppermute x0 -> x34, starting transfers between devices: none -> 40.8 us  [the longest x27 40.3 us: flip(): return lax.ppermute(x, 'dp', [(i, i ^ bits) for i in range(n)])]
    pallas_call x0 -> x7, Pallas kernels: none -> 18.7 us  [call(): pl.pallas_call(kernel, out_shape=out_shape, in_specs=in_specs, out_specs=...]
    reduce_sum x2 -> x0, other arithmetic: 16.3 us -> none  [the longest x1 8.66 us: body(): counts = counts + jnp.sum(resp.astype(jnp.float32), axis=0)]
    dot_general x4 -> x0, matrix products: 12.6 us -> none  [the longest x2 7.92 us: body(): jnp.einsum('nd,kd->nk', piece, centroids, preferred_element_type=jnp.floa...]
    div x1 -> x0, other arithmetic: 3.95 us -> none  [body(): (all_sums + prior_mass * centroids.astype(jnp.float32)) / (all_counts + p...]
  transfers between devices with their start and end apart: 1 -> 34, of which waited for: 1 -> 14; matrix products, arithmetic and copies ran while one was open for 0% -> 1% of each run, Pallas kernels for 0% -> 11%
where the time goes in v2:
time: 121 us; the launch traced here: 120 us
  waiting for transfers between devices  56.7 us (47%)
  starting transfers between devices  40.8 us (34%)
  Pallas kernels  18.7 us (15%)
  local copies, waits for them, and re-layouts  2.72 us (2%)
    ppermute x27, waiting for transfers between devices, flip(): return lax.ppermute(x, 'dp', [(i, i ^ bits) for i in range(n)])  56.6 us
    ppermute x27, starting transfers between devices, flip(): return lax.ppermute(x, 'dp', [(i, i ^ bits) for i in range(n)])  40.3 us
    pallas_call x7, Pallas kernels, call(): pl.pallas_call(kernel, out_shape=out_shape, in_specs=in_specs, out_specs=...  18.7 us
    unnamed x6, local copies, waits for them, and re-layouts  2.64 us
  transfers between devices with their start and end apart: 34, of which 14 were waited for; matrix products, arithmetic and copies ran while one was open for 1% of the time, Pallas kernels for 11%

profile of v2, /device:TPU:0, one launch (start us, length us, event | category | flops | bytes accessed | tf_op | source)
XLA Modules:
  0.0 120.3 jit_solution(13258531035967178032)
XLA Ops:
  0.7 1.0 copy-done
  1.8 0.6 open.1
  2.3 3.0 %collective-permute-start = (f32[256,256]{1,0:T(8,128)S(1)}, f32[256,256]{1,0:T(8,128)S(1)}, u32[]{:S(2)}, u32[]{:S(2)}) collective-permute-start(f32[256,256]{1,0:T(8,128)S(1)} %get-tuple-element.19), channel_id=1, source_target_pairs={{0,2},{2,0},{4,6},{6,4},{8,10},{10,8},{12,14},{14,12},{16,18},{18,... | collective-permute-start | bytes 786440 | tf_op jit(solution)/shard_map/ppermute | solution.py:219
  5.3 1.5 %collective-permute-start.1 = (f32[256,256]{1,0:T(8,128)S(1)}, f32[256,256]{1,0:T(8,128)S(1)}, u32[]{:S(2)}, u32[]{:S(2)}) collective-permute-start(f32[256,256]{1,0:T(8,128)S(1)} %get-tuple-element.20), channel_id=1, source_target_pairs={{0,4},{2,6},{4,0},{6,2},{8,12},{10,14},{12,8},{14,10},{16,20},{18,... | collective-permute-start | bytes 786440 | tf_op jit(solution)/shard_map/ppermute | solution.py:219
  6.9 0.5 collective-permute-start.6
  7.5 1.6 %copy-done.2 = bf16[4096,256]{1,0:T(8,128)(2,1)S(1)} copy-done((bf16[4096,256]{1,0:T(8,128)(2,1)S(1)}, bf16[4096,256]{1,0:T(8,128)(2,1)}, u32[]{:S(2)}) %copy-start.2) | copy-done | bytes 2097176
  9.0 5.1 %stats.1 = f32[2,1024]{1,0:T(2,128)S(1)} custom-call(bf16[1024,256]{1,0:T(8,128)(2,1)S(1)} %copy-done, bf16[4096,256]{1,0:T(8,128)(2,1)S(1)} %copy-done.2), custom_call_target="tpu_custom_call" | custom-call | flops 2147483648 | bytes 2621440 | tf_op jit(solution)/shard_map/stats/pallas_call | solution.py:26
  14.1 0.5 collective-permute-done.1.refs_5_
  14.6 4.1 %collective-permute-done.6.refs_4_ = f32[256,256]{1,0:T(8,128)S(1)} collective-permute-done((f32[256,256]{1,0:T(8,128)S(1)}, f32[256,256]{1,0:T(8,128)S(1)}, u32[]{:S(2)}, u32[]{:S(2)}) %collective-permute-start.6) | collective-permute-done | bytes 262176 | tf_op jit(solution)/shard_map/ppermute | solution.py:219
  18.8 1.6 %collective-permute-start.10 = (f32[4,256]{1,0:T(4,128)S(1)}, f32[4,256]{1,0:T(4,128)S(1)}, u32[]{:S(2)}, u32[]{:S(2)}) collective-permute-start(f32[4,256]{1,0:T(4,128)S(1)} %log_add_fusion.lse_ref), channel_id=1, source_target_pairs={{0,4},{2,6},{4,0},{6,2},{8,12},{10,14},{12,8},{14,10},{16,20},{18,... | collective-permute-start | bytes 12296 | tf_op jit(solution)/shard_map/ppermute | solution.py:219
  20.4 0.5 collective-permute-start.9
  20.9 0.3 collective-permute-start.12
  21.3 1.2 %collective-permute-done.10.refs_9_ = f32[4,256]{1,0:T(4,128)S(1)} collective-permute-done((f32[4,256]{1,0:T(4,128)S(1)}, f32[4,256]{1,0:T(4,128)S(1)}, u32[]{:S(2)}, u32[]{:S(2)}) %collective-permute-start.10) | collective-permute-done | bytes 4128 | tf_op jit(solution)/shard_map/ppermute | solution.py:219
  22.5 0.5 collective-permute-start.13
  23.0 1.0 collective-permute-done.9.refs_8_
  24.0 0.5 collective-permute-start.8
  24.5 1.5 %collective-permute-start.11 = (f32[4,256]{1,0:T(4,128)S(1)}, f32[4,256]{1,0:T(4,128)S(1)}, u32[]{:S(2)}, u32[]{:S(2)}) collective-permute-start(f32[4,256]{1,0:T(4,128)S(1)} %log_add_fusion.lse_ref), channel_id=1, source_target_pairs={{0,6},{2,4},{4,2},{6,0},{8,14},{10,12},{12,10},{14,8},{16,22},{18,... | collective-permute-start | bytes 12296 | tf_op jit(solution)/shard_map/ppermute | solution.py:219
  26.0 3.1 %collective-permute-done.12.refs_0_ = f32[256,256]{1,0:T(8,128)S(1)} collective-permute-done((f32[256,256]{1,0:T(8,128)S(1)}, f32[256,256]{1,0:T(8,128)S(1)}, u32[]{:S(2)}, u32[]{:S(2)}) %collective-permute-start.12) | collective-permute-done | bytes 262176 | tf_op jit(solution)/shard_map/ppermute | solution.py:219
  29.1 1.0 collective-permute-done.13.refs_1_
  30.1 5.7 %near.1 = (f32[1024,256]{1,0:T(8,128)S(1)}, f32[1024,128]{1,0:T(8,128)S(1)}, bf16[1024,256]{1,0:T(8,128)(2,1)S(1)}, f32[1024,128]{1,0:T(8,128)S(1)}, bf16[256,256]{1,0:T(8,128)(2,1)S(1)}) custom-call(s32[2]{0:T(128)S(1)} %pad_add_fusion.where_ref, bf16[1024,256]{1,0:T(8,128)(2,1)S(1)} %copy-done.1, bf16[4096,256]{1,0:T(8,128)(2,1)} %c_ref.3, ...), custom_call_target="tpu_custom_call" | custom-call | flops 3221225472 | bytes 4730888 | tf_op jit(solution)/shard_map/near/pallas_call | solution.py:26
  35.8 2.3 %far.1 = (f32[264,256]{1,0:T(8,128)S(1)}, f32[264,256]{1,0:T(8,128)S(1)}, f32[264,256]{1,0:T(8,128)S(1)}, f32[264,256]{1,0:T(8,128)S(1)}) custom-call(s32[2]{0:T(128)S(1)} %pad_add_fusion.where_ref, bf16[1024,256]{1,0:T(8,128)(2,1)S(1)} %get-tuple-element.25.twice_ref, f32[1024,128]{1,0:T(8,128)S(1)} %get-tuple-element.26.norm_ref, ...), custom_call_target="tpu_custom_call" | custom-call | flops 1073741824 | bytes 3674120 | tf_op jit(solution)/shard_map/far/pallas_call | solution.py:26
  38.2 1.8 %collective-permute-start.16 = (f32[264,256]{1,0:T(8,128)S(1)}, f32[264,256]{1,0:T(8,128)S(1)}, u32[]{:S(2)}, u32[]{:S(2)}) collective-permute-start(f32[264,256]{1,0:T(8,128)S(1)} %get-tuple-element.30), channel_id=1, source_target_pairs={{0,8},{2,10},{4,12},{6,14},{8,0},{10,2},{12,4},{14,6},{16,24},{18,... | collective-permute-start | bytes 811016 | tf_op jit(solution)/shard_map/ppermute | solution.py:219
  39.9 2.6 %collective-permute-start.17 = (f32[264,256]{1,0:T(8,128)S(1)}, f32[264,256]{1,0:T(8,128)S(1)}, u32[]{:S(2)}, u32[]{:S(2)}) collective-permute-start(f32[264,256]{1,0:T(8,128)S(1)} %get-tuple-element.31), channel_id=1, source_target_pairs={{0,16},{2,18},{4,20},{6,22},{8,24},{10,26},{12,28},{14,30},{16,0},... | collective-permute-start | bytes 811016 | tf_op jit(solution)/shard_map/ppermute | solution.py:219
  42.6 9.9 %collective-permute-done.16.refs_1_ = f32[264,256]{1,0:T(8,128)S(1)} collective-permute-done((f32[264,256]{1,0:T(8,128)S(1)}, f32[264,256]{1,0:T(8,128)S(1)}, u32[]{:S(2)}, u32[]{:S(2)}) %collective-permute-start.16) | collective-permute-done | bytes 270368 | tf_op jit(solution)/shard_map/ppermute | solution.py:219
  52.5 9.3 %collective-permute-done.17.refs_2_ = f32[264,256]{1,0:T(8,128)S(1)} collective-permute-done((f32[264,256]{1,0:T(8,128)S(1)}, f32[264,256]{1,0:T(8,128)S(1)}, u32[]{:S(2)}, u32[]{:S(2)}) %collective-permute-start.17) | collective-permute-done | bytes 270368 | tf_op jit(solution)/shard_map/ppermute | solution.py:219
  62.1 2.5 %collective-permute-start.21 = (f32[264,256]{1,0:T(8,128)S(1)}, f32[264,256]{1,0:T(8,128)S(1)}, u32[]{:S(2)}, u32[]{:S(2)}) collective-permute-start(f32[264,256]{1,0:T(8,128)S(1)} %finish.1.refs_0_), channel_id=1, source_target_pairs={{0,24},{2,26},{4,28},{6,30},{8,16},{10,18},{12,20},{14,22},{16,8},... | collective-permute-start | bytes 811016 | tf_op jit(solution)/shard_map/ppermute | solution.py:219
  64.6 1.5 %collective-permute-start.23 = (f32[264,256]{1,0:T(8,128)S(1)}, f32[264,256]{1,0:T(8,128)S(1)}, u32[]{:S(2)}, u32[]{:S(2)}) collective-permute-start(f32[264,256]{1,0:T(8,128)S(1)} %finish.1.refs_0_), channel_id=1, source_target_pairs={{0,4},{2,6},{4,0},{6,2},{8,12},{10,14},{12,8},{14,10},{16,20},{18,... | collective-permute-start | bytes 811016 | tf_op jit(solution)/shard_map/ppermute | solution.py:219
  66.1 10.4 %collective-permute-start.20 = (f32[264,256]{1,0:T(8,128)S(1)}, f32[264,256]{1,0:T(8,128)S(1)}, u32[]{:S(2)}, u32[]{:S(2)}) collective-permute-start(f32[264,256]{1,0:T(8,128)S(1)} %finish.1.refs_0_), channel_id=1, source_target_pairs={{0,16},{2,18},{4,20},{6,22},{8,24},{10,26},{12,28},{14,30},{16,0},... | collective-permute-start | bytes 811016 | tf_op jit(solution)/shard_map/ppermute | solution.py:219
  76.5 1.5 %collective-permute-start.22 = (f32[264,256]{1,0:T(8,128)S(1)}, f32[264,256]{1,0:T(8,128)S(1)}, u32[]{:S(2)}, u32[]{:S(2)}) collective-permute-start(f32[264,256]{1,0:T(8,128)S(1)} %finish.1.refs_0_), channel_id=1, source_target_pairs={{0,2},{2,0},{4,6},{6,4},{8,10},{10,8},{12,14},{14,12},{16,18},{18,... | collective-permute-start | bytes 811016 | tf_op jit(solution)/shard_map/ppermute | solution.py:219
  78.2 0.5 collective-permute-start.29
  78.7 0.5 collective-permute-start.28
  79.2 13.2 %collective-permute-done.20.refs_2_ = f32[264,256]{1,0:T(8,128)S(1)} collective-permute-done((f32[264,256]{1,0:T(8,128)S(1)}, f32[264,256]{1,0:T(8,128)S(1)}, u32[]{:S(2)}, u32[]{:S(2)}) %collective-permute-start.20) | collective-permute-done | bytes 270368 | tf_op jit(solution)/shard_map/ppermute | solution.py:219
  92.4 1.5 %collective-permute-start.27 = (f32[264,256]{1,0:T(8,128)S(1)}, f32[264,256]{1,0:T(8,128)S(1)}, u32[]{:S(2)}, u32[]{:S(2)}) collective-permute-start(f32[264,256]{1,0:T(8,128)S(1)} %collective-permute-done.20.refs_2_), channel_id=1, source_target_pairs={{0,4},{2,6},{4,0},{6,2},{8,12},{10,14},{12,8},{14,10},{16,20},{18,... | collective-permute-start | bytes 811016 | tf_op jit(solution)/shard_map/ppermute | solution.py:219
  93.9 1.5 %collective-permute-start.26 = (f32[264,256]{1,0:T(8,128)S(1)}, f32[264,256]{1,0:T(8,128)S(1)}, u32[]{:S(2)}, u32[]{:S(2)}) collective-permute-start(f32[264,256]{1,0:T(8,128)S(1)} %collective-permute-done.20.refs_2_), channel_id=1, source_target_pairs={{0,2},{2,0},{4,6},{6,4},{8,10},{10,8},{12,14},{14,12},{16,18},{18,... | collective-permute-start | bytes 811016 | tf_op jit(solution)/shard_map/ppermute | solution.py:219
  95.4 0.5 collective-permute-start.24
  95.9 0.5 collective-permute-start.25
  96.4 1.5 %collective-permute-start.30 = (f32[264,256]{1,0:T(8,128)S(1)}, f32[264,256]{1,0:T(8,128)S(1)}, u32[]{:S(2)}, u32[]{:S(2)}) collective-permute-start(f32[264,256]{1,0:T(8,128)S(1)} %collective-permute-done.22.refs_4_), channel_id=1, source_target_pairs={{0,4},{2,6},{4,0},{6,2},{8,12},{10,14},{12,8},{14,10},{16,20},{18,... | collective-permute-start | bytes 811016 | tf_op jit(solution)/shard_map/ppermute | solution.py:219
  98.0 3.8 %collective-permute-done.27.refs_9_ = f32[264,256]{1,0:T(8,128)S(1)} collective-permute-done((f32[264,256]{1,0:T(8,128)S(1)}, f32[264,256]{1,0:T(8,128)S(1)}, u32[]{:S(2)}, u32[]{:S(2)}) %collective-permute-start.27) | collective-permute-done | bytes 270368 | tf_op jit(solution)/shard_map/ppermute | solution.py:219
  101.8 1.5 %collective-permute-start.33 = (f32[264,256]{1,0:T(8,128)S(1)}, f32[264,256]{1,0:T(8,128)S(1)}, u32[]{:S(2)}, u32[]{:S(2)}) collective-permute-start(f32[264,256]{1,0:T(8,128)S(1)} %collective-permute-done.29.refs_11_), channel_id=1, source_target_pairs={{0,2},{2,0},{4,6},{6,4},{8,10},{10,8},{12,14},{14,12},{16,18},{18,... | collective-permute-start | bytes 811016 | tf_op jit(solution)/shard_map/ppermute | solution.py:219
  103.3 1.5 %collective-permute-start.32 = (f32[264,256]{1,0:T(8,128)S(1)}, f32[264,256]{1,0:T(8,128)S(1)}, u32[]{:S(2)}, u32[]{:S(2)}) collective-permute-start(f32[264,256]{1,0:T(8,128)S(1)} %collective-permute-done.27.refs_9_), channel_id=1, source_target_pairs={{0,2},{2,0},{4,6},{6,4},{8,10},{10,8},{12,14},{14,12},{16,18},{18,... | collective-permute-start | bytes 811016 | tf_op jit(solution)/shard_map/ppermute | solution.py:219
  104.8 4.3 %collective-permute-done.24.refs_6_ = f32[264,256]{1,0:T(8,128)S(1)} collective-permute-done((f32[264,256]{1,0:T(8,128)S(1)}, f32[264,256]{1,0:T(8,128)S(1)}, u32[]{:S(2)}, u32[]{:S(2)}) %collective-permute-start.24) | collective-permute-done | bytes 270368 | tf_op jit(solution)/shard_map/ppermute | solution.py:219
  109.1 0.5 collective-permute-start.31
  109.6 0.6 add_add_fusion
  110.2 2.3 %place_early.1.refs_16_ = f32[4096,256]{1,0:T(8,128)} custom-call(s32[2]{0:T(128)S(1)} %pad_add_fusion.where_ref, f32[264,256]{1,0:T(8,128)S(1)} %finish.1.refs_0_, f32[264,256]{1,0:T(8,128)S(1)} %collective-permute-done.19.refs_1_, f32[264,256]{1,0:T(8,128)S(1)} %collective-permute-done.20.refs_2_, f32[264,256]{1,0:T(8,128)S(1)} %collective-permute-done.21.refs_3_, ...), custom_call_target="tpu_custom_call" | custom-call | bytes 3244040 | tf_op jit(solution)/shard_map/place_early/pallas_call | solution.py:26
  112.5 0.8 collective-permute-done.30.refs_12_
  113.4 1.5 %collective-permute-done.33.refs_15_ = f32[264,256]{1,0:T(8,128)S(1)} collective-permute-done((f32[264,256]{1,0:T(8,128)S(1)}, f32[264,256]{1,0:T(8,128)S(1)}, u32[]{:S(2)}, u32[]{:S(2)}) %collective-permute-start.33) | collective-permute-done | bytes 270368 | tf_op jit(solution)/shard_map/ppermute | solution.py:219
  114.9 3.0 %collective-permute-done.32.refs_14_ = f32[264,256]{1,0:T(8,128)S(1)} collective-permute-done((f32[264,256]{1,0:T(8,128)S(1)}, f32[264,256]{1,0:T(8,128)S(1)}, u32[]{:S(2)}, u32[]{:S(2)}) %collective-permute-start.32) | collective-permute-done | bytes 270368 | tf_op jit(solution)/shard_map/ppermute | solution.py:219
  117.9 2.4 %place_late.1 = (f32[4096,256]{1,0:T(8,128)}, f32[32,128]{1,0:T(8,128)}) custom-call(s32[2]{0:T(128)S(1)} %pad_add_fusion.where_ref, f32[264,256]{1,0:T(8,128)S(1)} %finish.1.refs_0_, f32[264,256]{1,0:T(8,128)S(1)} %collective-permute-done.19.refs_1_, f32[264,256]{1,0:T(8,128)S(1)} %collective-permute-done.20.refs_2_, ...), custom_call_target="tpu_custom_call", output_to_operand_aliasing={{0}: (17, {})} | custom-call | bytes 8519688 | tf_op jit(solution)/shard_map/place_late/pallas_call | solution.py:26
  (42 shorter events, 0.8 us)
Async XLA Ops:
  0.7 1.0 copy-start
  1.8 28.4 %copy-start.1 = (bf16[1024,256]{1,0:T(8,128)(2,1)S(1)}, bf16[1024,256]{1,0:T(8,128)(2,1)}, u32[]{:S(2)}) copy-start(bf16[1024,256]{1,0:T(8,128)(2,1)} %points_ref.5) | copy-start | bytes 1572868
  2.3 11.8 %collective-permute-start = (f32[256,256]{1,0:T(8,128)S(1)}, f32[256,256]{1,0:T(8,128)S(1)}, u32[]{:S(2)}, u32[]{:S(2)}) collective-permute-start(f32[256,256]{1,0:T(8,128)S(1)} %get-tuple-element.19), channel_id=1, source_target_pairs={{0,2},{2,0},{4,6},{6,4},{8,10},{10,8},{12,14},{14,12},{16,18},{18,... | collective-permute-start | bytes 786440 | tf_op jit(solution)/shard_map/ppermute | solution.py:219
  5.3 9.2 %collective-permute-start.1 = (f32[256,256]{1,0:T(8,128)S(1)}, f32[256,256]{1,0:T(8,128)S(1)}, u32[]{:S(2)}, u32[]{:S(2)}) collective-permute-start(f32[256,256]{1,0:T(8,128)S(1)} %get-tuple-element.20), channel_id=1, source_target_pairs={{0,4},{2,6},{4,0},{6,2},{8,12},{10,14},{12,8},{14,10},{16,20},{18,... | collective-permute-start | bytes 786440 | tf_op jit(solution)/shard_map/ppermute | solution.py:219
  6.9 11.9 %collective-permute-start.6 = (f32[256,256]{1,0:T(8,128)S(1)}, f32[256,256]{1,0:T(8,128)S(1)}, u32[]{:S(2)}, u32[]{:S(2)}) collective-permute-start(f32[256,256]{1,0:T(8,128)S(1)} %get-tuple-element.19), channel_id=1, source_target_pairs={{0,4},{2,6},{4,0},{6,2},{8,12},{10,14},{12,8},{14,10},{16,20},{18,... | collective-permute-start | bytes 786440 | tf_op jit(solution)/shard_map/ppermute | solution.py:219
  7.4 13.9 %collective-permute-start.3 = (f32[256,256]{1,0:T(8,128)S(1)}, f32[256,256]{1,0:T(8,128)S(1)}, u32[]{:S(2)}, u32[]{:S(2)}) collective-permute-start(f32[256,256]{1,0:T(8,128)S(1)} %get-tuple-element.20), channel_id=1, source_target_pairs={{0,2},{2,0},{4,6},{6,4},{8,10},{10,8},{12,14},{14,12},{16,18},{18,... | collective-permute-start | bytes 786440 | tf_op jit(solution)/shard_map/ppermute | solution.py:219
  7.5 1.6 %copy-start.2 = (bf16[4096,256]{1,0:T(8,128)(2,1)S(1)}, bf16[4096,256]{1,0:T(8,128)(2,1)}, u32[]{:S(2)}) copy-start(bf16[4096,256]{1,0:T(8,128)(2,1)} %c_ref.3) | copy-start | bytes 6291460
  14.6 4.2 %collective-permute-start.2 = (f32[2,1024]{1,0:T(2,128)S(1)}, f32[2,1024]{1,0:T(2,128)S(1)}, u32[]{:S(2)}, u32[]{:S(2)}) collective-permute-start(f32[2,1024]{1,0:T(2,128)S(1)} %stats.1), channel_id=1, source_target_pairs={{0,1},{1,0},{2,3},{3,2},{4,5},{5,4},{6,7},{7,6},{8,9},{9,8},{10,11... | collective-permute-start | bytes 24584 | tf_op jit(solution)/shard_map/ppermute | solution.py:222
  18.7 5.3 %collective-permute-start.7 = (f32[256,256]{1,0:T(8,128)S(1)}, f32[256,256]{1,0:T(8,128)S(1)}, u32[]{:S(2)}, u32[]{:S(2)}) collective-permute-start(f32[256,256]{1,0:T(8,128)S(1)} %collective-permute-done.6.refs_4_), channel_id=1, source_target_pairs={{0,1},{1,0},{2,3},{3,2},{4,5},{5,4},{6,7},{7,6},{8,9},{9,8},{10,11... | collective-permute-start | bytes 786440 | tf_op jit(solution)/shard_map/ppermute | solution.py:222
  18.8 3.7 %collective-permute-start.10 = (f32[4,256]{1,0:T(4,128)S(1)}, f32[4,256]{1,0:T(4,128)S(1)}, u32[]{:S(2)}, u32[]{:S(2)}) collective-permute-start(f32[4,256]{1,0:T(4,128)S(1)} %log_add_fusion.lse_ref), channel_id=1, source_target_pairs={{0,4},{2,6},{4,0},{6,2},{8,12},{10,14},{12,8},{14,10},{16,20},{18,... | collective-permute-start | bytes 12296 | tf_op jit(solution)/shard_map/ppermute | solution.py:219
  20.4 3.6 %collective-permute-start.9 = (f32[4,256]{1,0:T(4,128)S(1)}, f32[4,256]{1,0:T(4,128)S(1)}, u32[]{:S(2)}, u32[]{:S(2)}) collective-permute-start(f32[4,256]{1,0:T(4,128)S(1)} %log_add_fusion.lse_ref), channel_id=1, source_target_pairs={{0,2},{2,0},{4,6},{6,4},{8,10},{10,8},{12,14},{14,12},{16,18},{18,... | collective-permute-start | bytes 12296 | tf_op jit(solution)/shard_map/ppermute | solution.py:219
  20.9 8.2 %collective-permute-start.12 = (f32[256,256]{1,0:T(8,128)S(1)}, f32[256,256]{1,0:T(8,128)S(1)}, u32[]{:S(2)}, u32[]{:S(2)}) collective-permute-start(f32[256,256]{1,0:T(8,128)S(1)} %collective-permute-done.refs_0_), channel_id=1, source_target_pairs={{0,4},{2,6},{4,0},{6,2},{8,12},{10,14},{12,8},{14,10},{16,20},{18,... | collective-permute-start | bytes 786440 | tf_op jit(solution)/shard_map/ppermute | solution.py:219
  21.3 3.3 %collective-permute-start.5 = (f32[256,256]{1,0:T(8,128)S(1)}, f32[256,256]{1,0:T(8,128)S(1)}, u32[]{:S(2)}, u32[]{:S(2)}) collective-permute-start(f32[256,256]{1,0:T(8,128)S(1)} %collective-permute-done.3.refs_1_), channel_id=1, source_target_pairs={{0,1},{1,0},{2,3},{3,2},{4,5},{5,4},{6,7},{7,6},{8,9},{9,8},{10,11... | collective-permute-start | bytes 786440 | tf_op jit(solution)/shard_map/ppermute | solution.py:222
  22.5 7.6 %collective-permute-start.13 = (f32[256,256]{1,0:T(8,128)S(1)}, f32[256,256]{1,0:T(8,128)S(1)}, u32[]{:S(2)}, u32[]{:S(2)}) collective-permute-start(f32[256,256]{1,0:T(8,128)S(1)} %collective-permute-done.1.refs_5_), channel_id=1, source_target_pairs={{0,2},{2,0},{4,6},{6,4},{8,10},{10,8},{12,14},{14,12},{16,18},{18,... | collective-permute-start | bytes 786440 | tf_op jit(solution)/shard_map/ppermute | solution.py:219
  24.0 6.1 %collective-permute-start.4 = (f32[256,256]{1,0:T(8,128)S(1)}, f32[256,256]{1,0:T(8,128)S(1)}, u32[]{:S(2)}, u32[]{:S(2)}) collective-permute-start(f32[256,256]{1,0:T(8,128)S(1)} %collective-permute-done.refs_0_), channel_id=1, source_target_pairs={{0,1},{1,0},{2,3},{3,2},{4,5},{5,4},{6,7},{7,6},{8,9},{9,8},{10,11... | collective-permute-start | bytes 786440 | tf_op jit(solution)/shard_map/ppermute | solution.py:222
  24.0 6.1 %collective-permute-start.8 = (f32[256,256]{1,0:T(8,128)S(1)}, f32[256,256]{1,0:T(8,128)S(1)}, u32[]{:S(2)}, u32[]{:S(2)}) collective-permute-start(f32[256,256]{1,0:T(8,128)S(1)} %collective-permute-done.1.refs_5_), channel_id=1, source_target_pairs={{0,1},{1,0},{2,3},{3,2},{4,5},{5,4},{6,7},{7,6},{8,9},{9,8},{10,11... | collective-permute-start | bytes 786440 | tf_op jit(solution)/shard_map/ppermute | solution.py:222
  24.5 11.3 %collective-permute-start.11 = (f32[4,256]{1,0:T(4,128)S(1)}, f32[4,256]{1,0:T(4,128)S(1)}, u32[]{:S(2)}, u32[]{:S(2)}) collective-permute-start(f32[4,256]{1,0:T(4,128)S(1)} %log_add_fusion.lse_ref), channel_id=1, source_target_pairs={{0,6},{2,4},{4,2},{6,0},{8,14},{10,12},{12,10},{14,8},{16,22},{18,... | collective-permute-start | bytes 12296 | tf_op jit(solution)/shard_map/ppermute | solution.py:219
  29.1 6.7 %collective-permute-start.14 = (f32[256,256]{1,0:T(8,128)S(1)}, f32[256,256]{1,0:T(8,128)S(1)}, u32[]{:S(2)}, u32[]{:S(2)}) collective-permute-start(f32[256,256]{1,0:T(8,128)S(1)} %collective-permute-done.12.refs_0_), channel_id=1, source_target_pairs={{0,1},{1,0},{2,3},{3,2},{4,5},{5,4},{6,7},{7,6},{8,9},{9,8},{10,11... | collective-permute-start | bytes 786440 | tf_op jit(solution)/shard_map/ppermute | solution.py:222
  30.1 5.7 %collective-permute-start.15 = (f32[256,256]{1,0:T(8,128)S(1)}, f32[256,256]{1,0:T(8,128)S(1)}, u32[]{:S(2)}, u32[]{:S(2)}) collective-permute-start(f32[256,256]{1,0:T(8,128)S(1)} %collective-permute-done.13.refs_1_), channel_id=1, source_target_pairs={{0,1},{1,0},{2,3},{3,2},{4,5},{5,4},{6,7},{7,6},{8,9},{9,8},{10,11... | collective-permute-start | bytes 786440 | tf_op jit(solution)/shard_map/ppermute | solution.py:222
  38.2 14.3 %collective-permute-start.16 = (f32[264,256]{1,0:T(8,128)S(1)}, f32[264,256]{1,0:T(8,128)S(1)}, u32[]{:S(2)}, u32[]{:S(2)}) collective-permute-start(f32[264,256]{1,0:T(8,128)S(1)} %get-tuple-element.30), channel_id=1, source_target_pairs={{0,8},{2,10},{4,12},{6,14},{8,0},{10,2},{12,4},{14,6},{16,24},{18,... | collective-permute-start | bytes 811016 | tf_op jit(solution)/shard_map/ppermute | solution.py:219
  39.9 21.8 %collective-permute-start.17 = (f32[264,256]{1,0:T(8,128)S(1)}, f32[264,256]{1,0:T(8,128)S(1)}, u32[]{:S(2)}, u32[]{:S(2)}) collective-permute-start(f32[264,256]{1,0:T(8,128)S(1)} %get-tuple-element.31), channel_id=1, source_target_pairs={{0,16},{2,18},{4,20},{6,22},{8,24},{10,26},{12,28},{14,30},{16,0},... | collective-permute-start | bytes 811016 | tf_op jit(solution)/shard_map/ppermute | solution.py:219
  42.5 19.3 %collective-permute-start.18 = (f32[264,256]{1,0:T(8,128)S(1)}, f32[264,256]{1,0:T(8,128)S(1)}, u32[]{:S(2)}, u32[]{:S(2)}) collective-permute-start(f32[264,256]{1,0:T(8,128)S(1)} %get-tuple-element.32), channel_id=1, source_target_pairs={{0,24},{2,26},{4,28},{6,30},{8,16},{10,18},{12,20},{14,22},{16,8},... | collective-permute-start | bytes 811016 | tf_op jit(solution)/shard_map/ppermute | solution.py:219
  62.1 16.1 %collective-permute-start.21 = (f32[264,256]{1,0:T(8,128)S(1)}, f32[264,256]{1,0:T(8,128)S(1)}, u32[]{:S(2)}, u32[]{:S(2)}) collective-permute-start(f32[264,256]{1,0:T(8,128)S(1)} %finish.1.refs_0_), channel_id=1, source_target_pairs={{0,24},{2,26},{4,28},{6,30},{8,16},{10,18},{12,20},{14,22},{16,8},... | collective-permute-start | bytes 811016 | tf_op jit(solution)/shard_map/ppermute | solution.py:219
  64.6 14.1 %collective-permute-start.23 = (f32[264,256]{1,0:T(8,128)S(1)}, f32[264,256]{1,0:T(8,128)S(1)}, u32[]{:S(2)}, u32[]{:S(2)}) collective-permute-start(f32[264,256]{1,0:T(8,128)S(1)} %finish.1.refs_0_), channel_id=1, source_target_pairs={{0,4},{2,6},{4,0},{6,2},{8,12},{10,14},{12,8},{14,10},{16,20},{18,... | collective-permute-start | bytes 811016 | tf_op jit(solution)/shard_map/ppermute | solution.py:219
  66.1 26.3 %collective-permute-start.20 = (f32[264,256]{1,0:T(8,128)S(1)}, f32[264,256]{1,0:T(8,128)S(1)}, u32[]{:S(2)}, u32[]{:S(2)}) collective-permute-start(f32[264,256]{1,0:T(8,128)S(1)} %finish.1.refs_0_), channel_id=1, source_target_pairs={{0,16},{2,18},{4,20},{6,22},{8,24},{10,26},{12,28},{14,30},{16,0},... | collective-permute-start | bytes 811016 | tf_op jit(solution)/shard_map/ppermute | solution.py:219
  76.5 17.4 %collective-permute-start.22 = (f32[264,256]{1,0:T(8,128)S(1)}, f32[264,256]{1,0:T(8,128)S(1)}, u32[]{:S(2)}, u32[]{:S(2)}) collective-permute-start(f32[264,256]{1,0:T(8,128)S(1)} %finish.1.refs_0_), channel_id=1, source_target_pairs={{0,2},{2,0},{4,6},{6,4},{8,10},{10,8},{12,14},{14,12},{16,18},{18,... | collective-permute-start | bytes 811016 | tf_op jit(solution)/shard_map/ppermute | solution.py:219
  78.0 17.4 %collective-permute-start.19 = (f32[264,256]{1,0:T(8,128)S(1)}, f32[264,256]{1,0:T(8,128)S(1)}, u32[]{:S(2)}, u32[]{:S(2)}) collective-permute-start(f32[264,256]{1,0:T(8,128)S(1)} %finish.1.refs_0_), channel_id=1, source_target_pairs={{0,8},{2,10},{4,12},{6,14},{8,0},{10,2},{12,4},{14,6},{16,24},{18,... | collective-permute-start | bytes 811016 | tf_op jit(solution)/shard_map/ppermute | solution.py:219
  78.2 17.8 %collective-permute-start.29 = (f32[264,256]{1,0:T(8,128)S(1)}, f32[264,256]{1,0:T(8,128)S(1)}, u32[]{:S(2)}, u32[]{:S(2)}) collective-permute-start(f32[264,256]{1,0:T(8,128)S(1)} %collective-permute-done.21.refs_3_), channel_id=1, source_target_pairs={{0,4},{2,6},{4,0},{6,2},{8,12},{10,14},{12,8},{14,10},{16,20},{18,... | collective-permute-start | bytes 811016 | tf_op jit(solution)/shard_map/ppermute | solution.py:219
  78.7 17.8 %collective-permute-start.28 = (f32[264,256]{1,0:T(8,128)S(1)}, f32[264,256]{1,0:T(8,128)S(1)}, u32[]{:S(2)}, u32[]{:S(2)}) collective-permute-start(f32[264,256]{1,0:T(8,128)S(1)} %collective-permute-done.21.refs_3_), channel_id=1, source_target_pairs={{0,2},{2,0},{4,6},{6,4},{8,10},{10,8},{12,14},{14,12},{16,18},{18,... | collective-permute-start | bytes 811016 | tf_op jit(solution)/shard_map/ppermute | solution.py:219
  92.4 9.4 %collective-permute-start.27 = (f32[264,256]{1,0:T(8,128)S(1)}, f32[264,256]{1,0:T(8,128)S(1)}, u32[]{:S(2)}, u32[]{:S(2)}) collective-permute-start(f32[264,256]{1,0:T(8,128)S(1)} %collective-permute-done.20.refs_2_), channel_id=1, source_target_pairs={{0,4},{2,6},{4,0},{6,2},{8,12},{10,14},{12,8},{14,10},{16,20},{18,... | collective-permute-start | bytes 811016 | tf_op jit(solution)/shard_map/ppermute | solution.py:219
  93.9 9.4 %collective-permute-start.26 = (f32[264,256]{1,0:T(8,128)S(1)}, f32[264,256]{1,0:T(8,128)S(1)}, u32[]{:S(2)}, u32[]{:S(2)}) collective-permute-start(f32[264,256]{1,0:T(8,128)S(1)} %collective-permute-done.20.refs_2_), channel_id=1, source_target_pairs={{0,2},{2,0},{4,6},{6,4},{8,10},{10,8},{12,14},{14,12},{16,18},{18,... | collective-permute-start | bytes 811016 | tf_op jit(solution)/shard_map/ppermute | solution.py:219
  95.4 13.7 %collective-permute-start.24 = (f32[264,256]{1,0:T(8,128)S(1)}, f32[264,256]{1,0:T(8,128)S(1)}, u32[]{:S(2)}, u32[]{:S(2)}) collective-permute-start(f32[264,256]{1,0:T(8,128)S(1)} %collective-permute-done.19.refs_1_), channel_id=1, source_target_pairs={{0,2},{2,0},{4,6},{6,4},{8,10},{10,8},{12,14},{14,12},{16,18},{18,... | collective-permute-start | bytes 811016 | tf_op jit(solution)/shard_map/ppermute | solution.py:219
  95.9 14.3 %collective-permute-start.25 = (f32[264,256]{1,0:T(8,128)S(1)}, f32[264,256]{1,0:T(8,128)S(1)}, u32[]{:S(2)}, u32[]{:S(2)}) collective-permute-start(f32[264,256]{1,0:T(8,128)S(1)} %collective-permute-done.19.refs_1_), channel_id=1, source_target_pairs={{0,4},{2,6},{4,0},{6,2},{8,12},{10,14},{12,8},{14,10},{16,20},{18,... | collective-permute-start | bytes 811016 | tf_op jit(solution)/shard_map/ppermute | solution.py:219
  96.4 16.9 %collective-permute-start.30 = (f32[264,256]{1,0:T(8,128)S(1)}, f32[264,256]{1,0:T(8,128)S(1)}, u32[]{:S(2)}, u32[]{:S(2)}) collective-permute-start(f32[264,256]{1,0:T(8,128)S(1)} %collective-permute-done.22.refs_4_), channel_id=1, source_target_pairs={{0,4},{2,6},{4,0},{6,2},{8,12},{10,14},{12,8},{14,10},{16,20},{18,... | collective-permute-start | bytes 811016 | tf_op jit(solution)/shard_map/ppermute | solution.py:219
  101.8 13.1 %collective-permute-start.33 = (f32[264,256]{1,0:T(8,128)S(1)}, f32[264,256]{1,0:T(8,128)S(1)}, u32[]{:S(2)}, u32[]{:S(2)}) collective-permute-start(f32[264,256]{1,0:T(8,128)S(1)} %collective-permute-done.29.refs_11_), channel_id=1, source_target_pairs={{0,2},{2,0},{4,6},{6,4},{8,10},{10,8},{12,14},{14,12},{16,18},{18,... | collective-permute-start | bytes 811016 | tf_op jit(solution)/shard_map/ppermute | solution.py:219
  103.3 14.5 %collective-permute-start.32 = (f32[264,256]{1,0:T(8,128)S(1)}, f32[264,256]{1,0:T(8,128)S(1)}, u32[]{:S(2)}, u32[]{:S(2)}) collective-permute-start(f32[264,256]{1,0:T(8,128)S(1)} %collective-permute-done.27.refs_9_), channel_id=1, source_target_pairs={{0,2},{2,0},{4,6},{6,4},{8,10},{10,8},{12,14},{14,12},{16,18},{18,... | collective-permute-start | bytes 811016 | tf_op jit(solution)/shard_map/ppermute | solution.py:219
  109.1 8.8 %collective-permute-start.31 = (f32[264,256]{1,0:T(8,128)S(1)}, f32[264,256]{1,0:T(8,128)S(1)}, u32[]{:S(2)}, u32[]{:S(2)}) collective-permute-start(f32[264,256]{1,0:T(8,128)S(1)} %collective-permute-done.24.refs_6_), channel_id=1, source_target_pairs={{0,4},{2,6},{4,0},{6,2},{8,12},{10,14},{12,8},{14,10},{16,20},{18,... | collective-permute-start | bytes 811016 | tf_op jit(solution)/shard_map/ppermute | solution.py:219

commit v3 on v2

--- a/solution.py
+++ b/solution.py
@@ -98,9 +98,16 @@
         cnt_ref[...] += counted
 
 
-def near_kernel(cores, where_ref, points_ref, c_ref, lse_ref, *refs):
-    x_refs, lse_refs = refs[: 4 * cores], refs[4 * cores : 4 * cores + 2]
-    acc_ref, cnt_ref, twice_ref, norm_ref, own_ref = refs[4 * cores + 2 :]
+def add_pieces(where_ref, twice_ref, norm_ref, pieces, acc_ref, cnt_ref):
+    for x_ref, lse_ref, rc, part in pieces:
+        at = 2 * (where_ref[1] ^ rc) + part
+        x = x_ref[...].astype(jnp.bfloat16)
+        add_block(twice_ref[...], norm_ref[...], x, lse_ref[pl.ds(at, 1), :], acc_ref, cnt_ref, False)
+
+
+def near_kernel(cores, order, where_ref, points_ref, c_ref, lse_ref, lse_x_ref, lse_y_ref, *refs):
+    x_refs = refs[: 2 * cores]
+    acc_ref, cnt_ref, twice_ref, norm_ref, own_ref = refs[2 * cores :]
     share, size = twice_ref.shape[0], own_ref.shape[0]
     plane, line = lax.rem(where_ref[0], 4), lax.div(where_ref[0], 4)
     start = pl.multiple_of(plane * share, share)
@@ -112,35 +119,46 @@
     for i in range(2 * cores):
         x = points_ref[i * half : (i + 1) * half, :]
         add_block(twice_ref[...], norm_ref[...], x, lse_ref[i : i + 1, :], acc_ref, cnt_ref, i == 0)
-    for k in range(2):
-        add_chip(cores, where_ref, twice_ref, norm_ref, x_refs[2 * cores * k : 2 * cores * (k + 1)], lse_refs[k], acc_ref, cnt_ref)
-
-
-def add_chip(cores, where_ref, twice_ref, norm_ref, x_refs, lse_ref, acc_ref, cnt_ref):
-    for rc in range(cores):
-        for part in range(2):
-            x = x_refs[2 * rc + part][...].astype(jnp.bfloat16)
-            at = 2 * (where_ref[1] ^ rc) + part
-            lse = lse_ref[pl.ds(at, 1), :]
-            add_block(twice_ref[...], norm_ref[...], x, lse, acc_ref, cnt_ref, False)
-
-
-def far_kernel(cores, lines, where_ref, twice_ref, norm_ref, acc_in_ref, cnt_in_ref, lse_ref, *refs):
-    x_refs, out_refs = refs[: 2 * cores], refs[2 * cores : 2 * cores + lines]
-    acc_ref, cnt_ref = refs[2 * cores + lines :]
+    pieces = [(x_refs[rc], lse_x_ref, rc, 0) for rc in range(cores)]
+    pieces += [(x_refs[cores + rc], lse_y_ref, rc, 1) for rc in range(cores)]
+    add_pieces(where_ref, twice_ref, norm_ref, pieces, acc_ref, cnt_ref)
+
+
+def far_kernel(cores, order, where_ref, twice_ref, norm_ref, acc_in_ref, cnt_in_ref, lse_x_ref, lse_y_ref, lse_d_ref, *refs):
+    lines = len(order)
+    x_refs, out_refs = refs[: 4 * cores], refs[4 * cores : 4 * cores + lines]
+    acc_ref, cnt_ref = refs[4 * cores + lines :]
     acc_ref[...] = acc_in_ref[...]
     cnt_ref[...] = cnt_in_ref[...]
-    add_chip(cores, where_ref, twice_ref, norm_ref, x_refs, lse_ref, acc_ref, cnt_ref)
+    whose = ((lse_x_ref, 1), (lse_y_ref, 0), (lse_d_ref, 0), (lse_d_ref, 1))
+    pieces = [
+        (x_refs[k * cores + rc], lse, rc, part)
+        for k, (lse, part) in enumerate(whose)
+        for rc in range(cores)
+    ]
+    add_pieces(where_ref, twice_ref, norm_ref, pieces, acc_ref, cnt_ref)
     line = lax.div(where_ref[0], 4)
     width = acc_ref.shape[1]
     size = acc_ref.shape[0] // lines
-    for r in range(lines):
-        start = pl.multiple_of((line ^ r) * size, size)
-        out_refs[r][0:size, :] = acc_ref[pl.ds(start, size), :]
+    for s in range(lines):
+        start = pl.multiple_of(behind(order, line, s) * size, size)
+        out_refs[s][0:size, :] = acc_ref[pl.ds(start, size), :]
         turned = jnp.sum(cnt_ref[pl.ds(start, size), :].T, axis=0, keepdims=True)
         if size < width:
             turned = jnp.concatenate([turned, jnp.zeros((1, width - size), jnp.float32)], axis=1)
-        out_refs[r][size : size + 8, :] = jnp.broadcast_to(turned, (8, width))
+        out_refs[s][size : size + 8, :] = jnp.broadcast_to(turned, (8, width))
+
+
+def behind(order, line, steps):
+    n = len(order)
+    return functools.reduce(
+        jnp.add,
+        [jnp.where(line == order[p], order[(p - steps) % n], 0) for p in range(n)],
+    )
+
+
+def add_kernel(a_ref, b_ref, out_ref):
+    out_ref[...] = a_ref[...] + b_ref[...]
 
 
 def finish_kernel(c_ref, *refs):
@@ -159,7 +177,8 @@
     out_ref[size:, :] = jnp.concatenate([spread] * (width // LANES), axis=1)
 
 
-def place_kernel(count, lines, late, where_ref, *refs):
+def place_kernel(names, order, late, where_ref, *refs):
+    count, lines = len(names), len(order)
     block_refs = refs[:count]
     if late is None:
         new_ref, sems = refs[count:]
@@ -171,14 +190,13 @@
     size = block_refs[0].shape[0] - 8
     plane, line = lax.rem(where_ref[0], 4), lax.div(where_ref[0], 4)
 
-    def place(i, names):
-        bits, r = names
-        return (plane ^ bits) * lines + (line ^ r)
-
-    names = NAMES(lines)
+    def place(i):
+        bits, steps = names[i]
+        return (plane ^ bits) * lines + behind(order, line, steps)
+
     copies = []
     for i in chosen:
-        at = pl.multiple_of(place(i, names[i]) * size, size)
+        at = pl.multiple_of(place(i) * size, size)
         copies.append(
             pltpu.make_async_copy(block_refs[i].at[0:size, :], new_ref.at[pl.ds(at, size), :], sems.at[i])
         )
@@ -195,15 +213,7 @@
         each = size // LANES
         for i in range(count):
             for k in range(each):
-                counts_ref[pl.ds(place(i, names[i]) * each + k, 1), :] = tiles_ref[i, k : k + 1, 0:LANES]
-
-
-def NAMES(lines):
-    cut = lines // 2
-    names = [(0, r) for r in range(lines)]
-    names += [(b, r) for r in range(lines) for b in (1, 2)]
-    names += [(3, r) for r in range(lines)]
-    return names
+                counts_ref[pl.ds(place(i) * each + k, 1), :] = tiles_ref[i, k : k + 1, 0:LANES]
 
 
 def body(n, cores, points, centroids):
@@ -213,6 +223,7 @@
     half = rows // (2 * cores)
     share = local_cent // 4
     size = share // lines
+    order = tuple(range(0, lines, 2)) + tuple(range(1, lines, 2))[::-1]
     where = jnp.stack([lax.axis_index("dp"), lax.axis_index("cent")]).astype(jnp.int32)
 
     def flip(x, bits):
@@ -220,6 +231,10 @@
 
     def flip_core(x, bits):
         return lax.ppermute(x, "cent", [(i, i ^ bits) for i in range(cores)])
+
+    def ring(x):
+        pairs = [(order[p], order[(p + 1) % lines]) for p in range(lines)]
+        return lax.ppermute(x, "dp", [(4 * a + i, 4 * b + i) for a, b in pairs for i in range(4)])
 
     first, second = call(
         open_kernel, (f32(half, width), f32(half, width)), [SMEM, VMEM], (where, points), "open"
@@ -246,14 +261,11 @@
     lse = lse.reshape(2 * cores, half)
     lse_x, lse_y, lse_d = flip(lse, 1), flip(lse, 2), flip(lse, 3)
 
-    def with_siblings(a, b):
-        out = [a, b]
-        for rc in range(1, cores):
-            out += [flip_core(a, rc), flip_core(b, rc)]
-        return out
+    def with_siblings(pieces):
+        return [a if rc == 0 else flip_core(a, rc) for a in pieces for rc in range(cores)]
 
     acc, cnt, twice, norm, own = call(
-        functools.partial(near_kernel, cores),
+        functools.partial(near_kernel, cores, order),
         (
             f32(share, width),
             f32(share, min(LANES, half)),
@@ -261,36 +273,43 @@
             f32(share, LANES),
             jax.ShapeDtypeStruct((size, width), jnp.bfloat16),
         ),
-        [SMEM] + [VMEM] * (5 + 4 * cores),
-        (where, points, centroids, lse, *with_siblings(x0, x1), *with_siblings(y0, y1), lse_x, lse_y),
+        [SMEM] + [VMEM] * (5 + 2 * cores),
+        (where, points, centroids, lse, lse_x, lse_y, *with_siblings((x0, y1))),
         "near",
-        flops=4 * share * width * 3 * rows,
-    )
+        flops=4 * share * width * 2 * rows,
+    )
+    late = lax.optimization_barrier((x1, y0, d0, d1))
     sums = call(
-        functools.partial(far_kernel, cores, lines),
+        functools.partial(far_kernel, cores, order),
         [f32(size + 8, width)] * lines,
-        [SMEM] + [VMEM] * (5 + 2 * cores),
-        (where, twice, norm, acc, cnt, lse_d, *with_siblings(d0, d1)),
+        [SMEM] + [VMEM] * (7 + 4 * cores),
+        (where, twice, norm, acc, cnt, lse_x, lse_y, lse_d, *with_siblings(late)),
         "far",
         scratch=[
             pltpu.VMEM((share, width), jnp.float32),
             pltpu.VMEM((share, min(LANES, half)), jnp.float32),
         ],
-        flops=4 * share * width * rows,
-    )
-    summed = [sums[0]] + [flip(sums[r], 4 * r) for r in range(1, lines)]
-    done = call(finish_kernel, f32(size + 8, width), [VMEM] * (1 + lines), (own, *summed), "finish")
-
-    column = [done] + [flip(done, 4 * r) for r in range(1, lines)]
+        flops=4 * share * width * 2 * rows,
+    )
+    moving = ring(sums[1])
+    for s in range(2, lines):
+        moving = ring(call(add_kernel, f32(size + 8, width), [VMEM] * 2, (sums[s], moving), "add"))
+    done = call(finish_kernel, f32(size + 8, width), [VMEM] * 3, (own, sums[0], moving), "finish")
+
+    column = [done]
+    for s in range(1, lines):
+        column.append(ring(column[-1]))
     over_x = [flip(b, 1) for b in column]
     over_y = [flip(b, 2) for b in column]
     cut = lines // 2
     over_xy = [flip(b, 2) for b in over_x[:cut]] + [flip(b, 1) for b in over_y[cut:]]
     blocks = column + [b for pair in zip(over_x, over_y) for b in pair] + over_xy
+    names = [(0, s) for s in range(lines)] + [(b, s) for s in range(lines) for b in (1, 2)]
+    names += [(3, s) for s in range(lines)]
     count = 4 * lines
     early = count - lines
     new = call(
-        functools.partial(place_kernel, early, lines, None),
+        functools.partial(place_kernel, names[:early], order, None),
         f32(local_cent, width),
         [SMEM] + [ANY] * early,
         (where, *blocks[:early]),
@@ -299,7 +318,7 @@
         scratch=[pltpu.SemaphoreType.DMA((early,))],
     )
     new, counts = call(
-        functools.partial(place_kernel, count, lines, tuple(range(early, count))),
+        functools.partial(place_kernel, names, order, tuple(range(early, count))),
         (f32(local_cent, width), f32(local_cent // LANES, LANES)),
         [SMEM] + [ANY] * (count + 1),
         (where, *blocks, new),

time: 121 us -> 113 us (0.934)
  waiting for transfers between devices: 56.7 us -> 45 us
  starting transfers between devices: 40.8 us -> 44.7 us
    ppermute x27 -> x21, waiting for transfers between devices: 56.6 us -> 21.8 us  [flip(): return lax.ppermute(x, 'dp', [(i, i ^ bits) for i in range(n)])]
    ppermute x0 -> x6, waiting for transfers between devices: none -> 23.2 us  [ring(): lax.ppermute(x, 'dp', [(4 * a + i, 4 * b + i) for a, b in pairs for i in...]
    ppermute x0 -> x6, starting transfers between devices: none -> 19.7 us  [ring(): lax.ppermute(x, 'dp', [(4 * a + i, 4 * b + i) for a, b in pairs for i in...]
    ppermute x27 -> x21, starting transfers between devices: 40.3 us -> 23.7 us  [flip(): return lax.ppermute(x, 'dp', [(i, i ^ bits) for i in range(n)])]
    pallas_call x7 -> x9, Pallas kernels: 18.7 us -> 18.7 us  [call(): pl.pallas_call(kernel, out_shape=out_shape, in_specs=in_specs, out_specs=...]
  transfers between devices with their start and end apart: 34 -> 34, of which waited for: 14 -> 15; matrix products, arithmetic and copies ran while one was open for 1% -> 1% of each run, Pallas kernels for 11% -> 11%
where the time goes in v3:
time: 113 us
  waiting for transfers between devices  45 us (40%)
  starting transfers between devices  44.7 us (40%)
  Pallas kernels  18.7 us (17%)
  local copies, waits for them, and re-layouts  2.72 us (2%)
    ppermute x21, starting transfers between devices, flip(): return lax.ppermute(x, 'dp', [(i, i ^ bits) for i in range(n)])  23.7 us
    ppermute x6, waiting for transfers between devices, ring(): lax.ppermute(x, 'dp', [(4 * a + i, 4 * b + i) for a, b in pairs for i in...  23.2 us
    ppermute x21, waiting for transfers between devices, flip(): return lax.ppermute(x, 'dp', [(i, i ^ bits) for i in range(n)])  21.8 us
    ppermute x6, starting transfers between devices, ring(): lax.ppermute(x, 'dp', [(4 * a + i, 4 * b + i) for a, b in pairs for i in...  19.7 us
    pallas_call x9, Pallas kernels, call(): pl.pallas_call(kernel, out_shape=out_shape, in_specs=in_specs, out_specs=...  18.7 us
    unnamed x6, local copies, waits for them, and re-layouts  2.64 us
  transfers between devices with their start and end apart: 34, of which 15 were waited for; matrix products, arithmetic and copies ran while one was open for 1% of the time, Pallas kernels for 11%

profile of v3, /device:TPU:0, one launch (start us, length us, event | category | flops | bytes accessed | tf_op | source)
XLA Modules:
  0.0 112.5 jit_solution(8388830110937681417)
XLA Ops:
  0.7 1.0 copy-done
  1.8 0.6 open.1
  2.3 3.0 %collective-permute-start = (f32[256,256]{1,0:T(8,128)S(1)}, f32[256,256]{1,0:T(8,128)S(1)}, u32[]{:S(2)}, u32[]{:S(2)}) collective-permute-start(f32[256,256]{1,0:T(8,128)S(1)} %get-tuple-element.23), channel_id=1, source_target_pairs={{0,2},{2,0},{4,6},{6,4},{8,10},{10,8},{12,14},{14,12},{16,18},{18,... | collective-permute-start | bytes 786440 | tf_op jit(solution)/shard_map/ppermute | solution.py:230
  5.3 1.5 %collective-permute-start.1 = (f32[256,256]{1,0:T(8,128)S(1)}, f32[256,256]{1,0:T(8,128)S(1)}, u32[]{:S(2)}, u32[]{:S(2)}) collective-permute-start(f32[256,256]{1,0:T(8,128)S(1)} %get-tuple-element.24), channel_id=1, source_target_pairs={{0,4},{2,6},{4,0},{6,2},{8,12},{10,14},{12,8},{14,10},{16,20},{18,... | collective-permute-start | bytes 786440 | tf_op jit(solution)/shard_map/ppermute | solution.py:230
  6.9 0.5 collective-permute-start.9
  7.5 1.6 %copy-done.2 = bf16[4096,256]{1,0:T(8,128)(2,1)S(1)} copy-done((bf16[4096,256]{1,0:T(8,128)(2,1)S(1)}, bf16[4096,256]{1,0:T(8,128)(2,1)}, u32[]{:S(2)}) %copy-start.2) | copy-done | bytes 2097176
  9.0 5.1 %stats.1 = f32[2,1024]{1,0:T(2,128)S(1)} custom-call(bf16[1024,256]{1,0:T(8,128)(2,1)S(1)} %copy-done, bf16[4096,256]{1,0:T(8,128)(2,1)S(1)} %copy-done.2), custom_call_target="tpu_custom_call" | custom-call | flops 2147483648 | bytes 2621440 | tf_op jit(solution)/shard_map/stats/pallas_call | solution.py:26
  14.6 1.7 %collective-permute-start.10 = (f32[256,256]{1,0:T(8,128)S(1)}, f32[256,256]{1,0:T(8,128)S(1)}, u32[]{:S(2)}, u32[]{:S(2)}) collective-permute-start(f32[256,256]{1,0:T(8,128)S(1)} %collective-permute-done.refs_0_), channel_id=1, source_target_pairs={{0,4},{2,6},{4,0},{6,2},{8,12},{10,14},{12,8},{14,10},{16,20},{18,... | collective-permute-start | bytes 786440 | tf_op jit(solution)/shard_map/ppermute | solution.py:230
  16.5 1.5 %collective-permute-start.11 = (f32[256,256]{1,0:T(8,128)S(1)}, f32[256,256]{1,0:T(8,128)S(1)}, u32[]{:S(2)}, u32[]{:S(2)}) collective-permute-start(f32[256,256]{1,0:T(8,128)S(1)} %collective-permute-done.1.refs_2_), channel_id=1, source_target_pairs={{0,2},{2,0},{4,6},{6,4},{8,10},{10,8},{12,14},{14,12},{16,18},{18,... | collective-permute-start | bytes 786440 | tf_op jit(solution)/shard_map/ppermute | solution.py:230
  18.1 1.5 %collective-permute-done.9.refs_2_ = f32[256,256]{1,0:T(8,128)S(1)} collective-permute-done((f32[256,256]{1,0:T(8,128)S(1)}, f32[256,256]{1,0:T(8,128)S(1)}, u32[]{:S(2)}, u32[]{:S(2)}) %collective-permute-start.9) | collective-permute-done | bytes 262176 | tf_op jit(solution)/shard_map/ppermute | solution.py:230
  19.6 1.5 %collective-permute-start.4 = (f32[4,256]{1,0:T(4,128)S(1)}, f32[4,256]{1,0:T(4,128)S(1)}, u32[]{:S(2)}, u32[]{:S(2)}) collective-permute-start(f32[4,256]{1,0:T(4,128)S(1)} %log_add_fusion.lse_ref), channel_id=1, source_target_pairs={{0,4},{2,6},{4,0},{6,2},{8,12},{10,14},{12,8},{14,10},{16,20},{18,... | collective-permute-start | bytes 12296 | tf_op jit(solution)/shard_map/ppermute | solution.py:230
  21.1 3.2 %collective-permute-done.10.refs_4_ = f32[256,256]{1,0:T(8,128)S(1)} collective-permute-done((f32[256,256]{1,0:T(8,128)S(1)}, f32[256,256]{1,0:T(8,128)S(1)}, u32[]{:S(2)}, u32[]{:S(2)}) %collective-permute-start.10) | collective-permute-done | bytes 262176 | tf_op jit(solution)/shard_map/ppermute | solution.py:230
  24.4 0.6 collective-permute-start.3
  25.1 0.5 collective-permute-start.13
  25.6 2.4 %collective-permute-done.3.lse_x_ref = f32[4,256]{1,0:T(4,128)S(1)} collective-permute-done((f32[4,256]{1,0:T(4,128)S(1)}, f32[4,256]{1,0:T(4,128)S(1)}, u32[]{:S(2)}, u32[]{:S(2)}) %collective-permute-start.3) | collective-permute-done | bytes 4128 | tf_op jit(solution)/shard_map/ppermute | solution.py:230
  28.0 0.5 collective-permute-start.15
  28.5 1.6 %collective-permute-start.7 = (f32[4,256]{1,0:T(4,128)S(1)}, f32[4,256]{1,0:T(4,128)S(1)}, u32[]{:S(2)}, u32[]{:S(2)}) collective-permute-start(f32[4,256]{1,0:T(4,128)S(1)} %log_add_fusion.lse_ref), channel_id=1, source_target_pairs={{0,6},{2,4},{4,2},{6,0},{8,14},{10,12},{12,10},{14,8},{16,22},{18,... | collective-permute-start | bytes 12296 | tf_op jit(solution)/shard_map/ppermute | solution.py:230
  30.1 4.5 %near.1 = (f32[1024,256]{1,0:T(8,128)S(1)}, f32[1024,128]{1,0:T(8,128)S(1)}, bf16[1024,256]{1,0:T(8,128)(2,1)S(1)}, f32[1024,128]{1,0:T(8,128)S(1)}, bf16[256,256]{1,0:T(8,128)(2,1)S(1)}) custom-call(s32[2]{0:T(128)S(1)} %pad_add_fusion.where_ref, bf16[1024,256]{1,0:T(8,128)(2,1)S(1)} %copy-done.1, bf16[4096,256]{1,0:T(8,128)(2,1)} %c_ref.3, ...), custom_call_target="tpu_custom_call" | custom-call | flops 2147483648 | bytes 3682312 | tf_op jit(solution)/shard_map/near/pallas_call | solution.py:26
  34.7 3.4 %far.1 = (f32[264,256]{1,0:T(8,128)S(1)}, f32[264,256]{1,0:T(8,128)S(1)}, f32[264,256]{1,0:T(8,128)S(1)}, f32[264,256]{1,0:T(8,128)S(1)}) custom-call(s32[2]{0:T(128)S(1)} %pad_add_fusion.where_ref, bf16[1024,256]{1,0:T(8,128)(2,1)S(1)} %get-tuple-element.29.twice_ref, f32[1024,128]{1,0:T(8,128)S(1)} %get-tuple-element.30.norm_ref, ...), custom_call_target="tpu_custom_call" | custom-call | flops 2147483648 | bytes 4730888 | tf_op jit(solution)/shard_map/far/pallas_call | solution.py:26
  38.1 2.6 %collective-permute-start.16 = (f32[264,256]{1,0:T(8,128)S(1)}, f32[264,256]{1,0:T(8,128)S(1)}, u32[]{:S(2)}, u32[]{:S(2)}) collective-permute-start(f32[264,256]{1,0:T(8,128)S(1)} %get-tuple-element.40), channel_id=1, source_target_pairs={{0,16},{2,18},{4,20},{6,22},{16,24},{18,26},{20,28},{22,30},{24,8}... | collective-permute-start | bytes 811016 | tf_op jit(solution)/shard_map/ppermute | solution.py:237
  40.8 5.7 %collective-permute-done.16.b_ref = f32[264,256]{1,0:T(8,128)S(1)} collective-permute-done((f32[264,256]{1,0:T(8,128)S(1)}, f32[264,256]{1,0:T(8,128)S(1)}, u32[]{:S(2)}, u32[]{:S(2)}) %collective-permute-start.16) | collective-permute-done | bytes 270368 | tf_op jit(solution)/shard_map/ppermute | solution.py:237
  46.5 3.4 %collective-permute-start.17 = (f32[264,256]{1,0:T(8,128)S(1)}, f32[264,256]{1,0:T(8,128)S(1)}, u32[]{:S(2)}, u32[]{:S(2)}) collective-permute-start(f32[264,256]{1,0:T(8,128)S(1)} %add.37), channel_id=1, source_target_pairs={{0,16},{2,18},{4,20},{6,22},{16,24},{18,26},{20,28},{22,30},{24,8}... | collective-permute-start | bytes 811016 | tf_op jit(solution)/shard_map/ppermute | solution.py:237
  49.9 4.8 %collective-permute-done.17.b_ref = f32[264,256]{1,0:T(8,128)S(1)} collective-permute-done((f32[264,256]{1,0:T(8,128)S(1)}, f32[264,256]{1,0:T(8,128)S(1)}, u32[]{:S(2)}, u32[]{:S(2)}) %collective-permute-start.17) | collective-permute-done | bytes 270368 | tf_op jit(solution)/shard_map/ppermute | solution.py:237
  54.8 3.4 %collective-permute-start.18 = (f32[264,256]{1,0:T(8,128)S(1)}, f32[264,256]{1,0:T(8,128)S(1)}, u32[]{:S(2)}, u32[]{:S(2)}) collective-permute-start(f32[264,256]{1,0:T(8,128)S(1)} %add.38), channel_id=1, source_target_pairs={{0,16},{2,18},{4,20},{6,22},{16,24},{18,26},{20,28},{22,30},{24,8}... | collective-permute-start | bytes 811016 | tf_op jit(solution)/shard_map/ppermute | solution.py:237
  58.2 4.0 %collective-permute-done.18.refs_1_ = f32[264,256]{1,0:T(8,128)S(1)} collective-permute-done((f32[264,256]{1,0:T(8,128)S(1)}, f32[264,256]{1,0:T(8,128)S(1)}, u32[]{:S(2)}, u32[]{:S(2)}) %collective-permute-start.18) | collective-permute-done | bytes 270368 | tf_op jit(solution)/shard_map/ppermute | solution.py:237
  62.5 3.4 %collective-permute-start.19 = (f32[264,256]{1,0:T(8,128)S(1)}, f32[264,256]{1,0:T(8,128)S(1)}, u32[]{:S(2)}, u32[]{:S(2)}) collective-permute-start(f32[264,256]{1,0:T(8,128)S(1)} %finish.1.refs_0_), channel_id=1, source_target_pairs={{0,16},{2,18},{4,20},{6,22},{16,24},{18,26},{20,28},{22,30},{24,8}... | collective-permute-start | bytes 811016 | tf_op jit(solution)/shard_map/ppermute | solution.py:237
  65.9 4.7 %collective-permute-done.19.refs_1_ = f32[264,256]{1,0:T(8,128)S(1)} collective-permute-done((f32[264,256]{1,0:T(8,128)S(1)}, f32[264,256]{1,0:T(8,128)S(1)}, u32[]{:S(2)}, u32[]{:S(2)}) %collective-permute-start.19) | collective-permute-done | bytes 270368 | tf_op jit(solution)/shard_map/ppermute | solution.py:237
  70.6 3.4 %collective-permute-start.20 = (f32[264,256]{1,0:T(8,128)S(1)}, f32[264,256]{1,0:T(8,128)S(1)}, u32[]{:S(2)}, u32[]{:S(2)}) collective-permute-start(f32[264,256]{1,0:T(8,128)S(1)} %collective-permute-done.19.refs_1_), channel_id=1, source_target_pairs={{0,16},{2,18},{4,20},{6,22},{16,24},{18,26},{20,28},{22,30},{24,8}... | collective-permute-start | bytes 811016 | tf_op jit(solution)/shard_map/ppermute | solution.py:237
  74.0 0.5 collective-permute-start.23
  74.5 1.4 %collective-permute-start.22 = (f32[264,256]{1,0:T(8,128)S(1)}, f32[264,256]{1,0:T(8,128)S(1)}, u32[]{:S(2)}, u32[]{:S(2)}) collective-permute-start(f32[264,256]{1,0:T(8,128)S(1)} %finish.1.refs_0_), channel_id=1, source_target_pairs={{0,2},{2,0},{4,6},{6,4},{8,10},{10,8},{12,14},{14,12},{16,18},{18,... | collective-permute-start | bytes 811016 | tf_op jit(solution)/shard_map/ppermute | solution.py:230
  75.9 4.0 %collective-permute-done.20.refs_2_ = f32[264,256]{1,0:T(8,128)S(1)} collective-permute-done((f32[264,256]{1,0:T(8,128)S(1)}, f32[264,256]{1,0:T(8,128)S(1)}, u32[]{:S(2)}, u32[]{:S(2)}) %collective-permute-start.20) | collective-permute-done | bytes 270368 | tf_op jit(solution)/shard_map/ppermute | solution.py:237
  79.9 3.4 %collective-permute-start.21 = (f32[264,256]{1,0:T(8,128)S(1)}, f32[264,256]{1,0:T(8,128)S(1)}, u32[]{:S(2)}, u32[]{:S(2)}) collective-permute-start(f32[264,256]{1,0:T(8,128)S(1)} %collective-permute-done.20.refs_2_), channel_id=1, source_target_pairs={{0,16},{2,18},{4,20},{6,22},{16,24},{18,26},{20,28},{22,30},{24,8}... | collective-permute-start | bytes 811016 | tf_op jit(solution)/shard_map/ppermute | solution.py:237
  83.3 0.5 collective-permute-start.25
  83.8 1.4 %collective-permute-start.24 = (f32[264,256]{1,0:T(8,128)S(1)}, f32[264,256]{1,0:T(8,128)S(1)}, u32[]{:S(2)}, u32[]{:S(2)}) collective-permute-start(f32[264,256]{1,0:T(8,128)S(1)} %collective-permute-done.19.refs_1_), channel_id=1, source_target_pairs={{0,2},{2,0},{4,6},{6,4},{8,10},{10,8},{12,14},{14,12},{16,18},{18,... | collective-permute-start | bytes 811016 | tf_op jit(solution)/shard_map/ppermute | solution.py:230
  85.2 1.5 %collective-permute-start.27 = (f32[264,256]{1,0:T(8,128)S(1)}, f32[264,256]{1,0:T(8,128)S(1)}, u32[]{:S(2)}, u32[]{:S(2)}) collective-permute-start(f32[264,256]{1,0:T(8,128)S(1)} %collective-permute-done.20.refs_2_), channel_id=1, source_target_pairs={{0,4},{2,6},{4,0},{6,2},{8,12},{10,14},{12,8},{14,10},{16,20},{18,... | collective-permute-start | bytes 811016 | tf_op jit(solution)/shard_map/ppermute | solution.py:230
  86.7 0.6 collective-permute-start.26
  87.3 0.5 collective-permute-start.29
  87.8 4.8 %collective-permute-done.25.refs_7_ = f32[264,256]{1,0:T(8,128)S(1)} collective-permute-done((f32[264,256]{1,0:T(8,128)S(1)}, f32[264,256]{1,0:T(8,128)S(1)}, u32[]{:S(2)}, u32[]{:S(2)}) %collective-permute-start.25) | collective-permute-done | bytes 270368 | tf_op jit(solution)/shard_map/ppermute | solution.py:230
  93.2 1.4 %collective-permute-start.28 = (f32[264,256]{1,0:T(8,128)S(1)}, f32[264,256]{1,0:T(8,128)S(1)}, u32[]{:S(2)}, u32[]{:S(2)}) collective-permute-start(f32[264,256]{1,0:T(8,128)S(1)} %collective-permute-done.21.refs_3_), channel_id=1, source_target_pairs={{0,2},{2,0},{4,6},{6,4},{8,10},{10,8},{12,14},{14,12},{16,18},{18,... | collective-permute-start | bytes 811016 | tf_op jit(solution)/shard_map/ppermute | solution.py:230
  94.6 3.9 %collective-permute-done.27.refs_9_ = f32[264,256]{1,0:T(8,128)S(1)} collective-permute-done((f32[264,256]{1,0:T(8,128)S(1)}, f32[264,256]{1,0:T(8,128)S(1)}, u32[]{:S(2)}, u32[]{:S(2)}) %collective-permute-start.27) | collective-permute-done | bytes 270368 | tf_op jit(solution)/shard_map/ppermute | solution.py:230
  99.0 1.4 %collective-permute-start.32 = (f32[264,256]{1,0:T(8,128)S(1)}, f32[264,256]{1,0:T(8,128)S(1)}, u32[]{:S(2)}, u32[]{:S(2)}) collective-permute-start(f32[264,256]{1,0:T(8,128)S(1)} %collective-permute-done.27.refs_9_), channel_id=1, source_target_pairs={{0,2},{2,0},{4,6},{6,4},{8,10},{10,8},{12,14},{14,12},{16,18},{18,... | collective-permute-start | bytes 811016 | tf_op jit(solution)/shard_map/ppermute | solution.py:230
  100.4 3.3 %collective-permute-done.29.refs_11_ = f32[264,256]{1,0:T(8,128)S(1)} collective-permute-done((f32[264,256]{1,0:T(8,128)S(1)}, f32[264,256]{1,0:T(8,128)S(1)}, u32[]{:S(2)}, u32[]{:S(2)}) %collective-permute-start.29) | collective-permute-done | bytes 270368 | tf_op jit(solution)/shard_map/ppermute | solution.py:230
  103.6 1.4 %collective-permute-start.33 = (f32[264,256]{1,0:T(8,128)S(1)}, f32[264,256]{1,0:T(8,128)S(1)}, u32[]{:S(2)}, u32[]{:S(2)}) collective-permute-start(f32[264,256]{1,0:T(8,128)S(1)} %collective-permute-done.29.refs_11_), channel_id=1, source_target_pairs={{0,2},{2,0},{4,6},{6,4},{8,10},{10,8},{12,14},{14,12},{16,18},{18,... | collective-permute-start | bytes 811016 | tf_op jit(solution)/shard_map/ppermute | solution.py:230
  105.0 0.6 add_add_fusion
  105.7 2.3 %place_early.1.refs_16_ = f32[4096,256]{1,0:T(8,128)} custom-call(s32[2]{0:T(128)S(1)} %pad_add_fusion.where_ref, f32[264,256]{1,0:T(8,128)S(1)} %finish.1.refs_0_, f32[264,256]{1,0:T(8,128)S(1)} %collective-permute-done.19.refs_1_, f32[264,256]{1,0:T(8,128)S(1)} %collective-permute-done.20.refs_2_, f32[264,256]{1,0:T(8,128)S(1)} %collective-permute-done.21.refs_3_, ...), custom_call_target="tpu_custom_call" | custom-call | bytes 3244040 | tf_op jit(solution)/shard_map/place_early/pallas_call | solution.py:26
  108.0 1.4 %collective-permute-done.31.refs_13_ = f32[264,256]{1,0:T(8,128)S(1)} collective-permute-done((f32[264,256]{1,0:T(8,128)S(1)}, f32[264,256]{1,0:T(8,128)S(1)}, u32[]{:S(2)}, u32[]{:S(2)}) %collective-permute-start.31) | collective-permute-done | bytes 270368 | tf_op jit(solution)/shard_map/ppermute | solution.py:230
  109.4 0.7 collective-permute-done.33.refs_15_
  110.1 2.4 %place_late.1 = (f32[4096,256]{1,0:T(8,128)}, f32[32,128]{1,0:T(8,128)}) custom-call(s32[2]{0:T(128)S(1)} %pad_add_fusion.where_ref, f32[264,256]{1,0:T(8,128)S(1)} %finish.1.refs_0_, f32[264,256]{1,0:T(8,128)S(1)} %collective-permute-done.19.refs_1_, f32[264,256]{1,0:T(8,128)S(1)} %collective-permute-done.20.refs_2_, ...), custom_call_target="tpu_custom_call", output_to_operand_aliasing={{0}: (17, {})} | custom-call | bytes 8519688 | tf_op jit(solution)/shard_map/place_late/pallas_call | solution.py:26
  (44 shorter events, 2.4 us)
Async XLA Ops:
  0.7 1.0 copy-start
  1.8 28.3 %copy-start.1 = (bf16[1024,256]{1,0:T(8,128)(2,1)S(1)}, bf16[1024,256]{1,0:T(8,128)(2,1)}, u32[]{:S(2)}) copy-start(bf16[1024,256]{1,0:T(8,128)(2,1)} %points_ref.5) | copy-start | bytes 1572868
  2.3 11.8 %collective-permute-start = (f32[256,256]{1,0:T(8,128)S(1)}, f32[256,256]{1,0:T(8,128)S(1)}, u32[]{:S(2)}, u32[]{:S(2)}) collective-permute-start(f32[256,256]{1,0:T(8,128)S(1)} %get-tuple-element.23), channel_id=1, source_target_pairs={{0,2},{2,0},{4,6},{6,4},{8,10},{10,8},{12,14},{14,12},{16,18},{18,... | collective-permute-start | bytes 786440 | tf_op jit(solution)/shard_map/ppermute | solution.py:230
  5.3 9.2 %collective-permute-start.1 = (f32[256,256]{1,0:T(8,128)S(1)}, f32[256,256]{1,0:T(8,128)S(1)}, u32[]{:S(2)}, u32[]{:S(2)}) collective-permute-start(f32[256,256]{1,0:T(8,128)S(1)} %get-tuple-element.24), channel_id=1, source_target_pairs={{0,4},{2,6},{4,0},{6,2},{8,12},{10,14},{12,8},{14,10},{16,20},{18,... | collective-permute-start | bytes 786440 | tf_op jit(solution)/shard_map/ppermute | solution.py:230
  6.9 12.8 %collective-permute-start.9 = (f32[256,256]{1,0:T(8,128)S(1)}, f32[256,256]{1,0:T(8,128)S(1)}, u32[]{:S(2)}, u32[]{:S(2)}) collective-permute-start(f32[256,256]{1,0:T(8,128)S(1)} %get-tuple-element.23), channel_id=1, source_target_pairs={{0,4},{2,6},{4,0},{6,2},{8,12},{10,14},{12,8},{14,10},{16,20},{18,... | collective-permute-start | bytes 786440 | tf_op jit(solution)/shard_map/ppermute | solution.py:230
  7.4 12.3 %collective-permute-start.8 = (f32[256,256]{1,0:T(8,128)S(1)}, f32[256,256]{1,0:T(8,128)S(1)}, u32[]{:S(2)}, u32[]{:S(2)}) collective-permute-start(f32[256,256]{1,0:T(8,128)S(1)} %get-tuple-element.24), channel_id=1, source_target_pairs={{0,2},{2,0},{4,6},{6,4},{8,10},{10,8},{12,14},{14,12},{16,18},{18,... | collective-permute-start | bytes 786440 | tf_op jit(solution)/shard_map/ppermute | solution.py:230
  7.5 1.6 %copy-start.2 = (bf16[4096,256]{1,0:T(8,128)(2,1)S(1)}, bf16[4096,256]{1,0:T(8,128)(2,1)}, u32[]{:S(2)}) copy-start(bf16[4096,256]{1,0:T(8,128)(2,1)} %c_ref.3) | copy-start | bytes 6291460
  14.6 2.0 %collective-permute-start.2 = (f32[2,1024]{1,0:T(2,128)S(1)}, f32[2,1024]{1,0:T(2,128)S(1)}, u32[]{:S(2)}, u32[]{:S(2)}) collective-permute-start(f32[2,1024]{1,0:T(2,128)S(1)} %stats.1), channel_id=1, source_target_pairs={{0,1},{1,0},{2,3},{3,2},{4,5},{5,4},{6,7},{7,6},{8,9},{9,8},{10,11... | collective-permute-start | bytes 24584 | tf_op jit(solution)/shard_map/ppermute | solution.py:233
  14.6 9.8 %collective-permute-start.10 = (f32[256,256]{1,0:T(8,128)S(1)}, f32[256,256]{1,0:T(8,128)S(1)}, u32[]{:S(2)}, u32[]{:S(2)}) collective-permute-start(f32[256,256]{1,0:T(8,128)S(1)} %collective-permute-done.refs_0_), channel_id=1, source_target_pairs={{0,4},{2,6},{4,0},{6,2},{8,12},{10,14},{12,8},{14,10},{16,20},{18,... | collective-permute-start | bytes 786440 | tf_op jit(solution)/shard_map/ppermute | solution.py:230
  16.3 11.7 %collective-permute-start.5 = (f32[256,256]{1,0:T(8,128)S(1)}, f32[256,256]{1,0:T(8,128)S(1)}, u32[]{:S(2)}, u32[]{:S(2)}) collective-permute-start(f32[256,256]{1,0:T(8,128)S(1)} %collective-permute-done.refs_0_), channel_id=1, source_target_pairs={{0,1},{1,0},{2,3},{3,2},{4,5},{5,4},{6,7},{7,6},{8,9},{9,8},{10,11... | collective-permute-start | bytes 786440 | tf_op jit(solution)/shard_map/ppermute | solution.py:233
  16.5 8.6 %collective-permute-start.11 = (f32[256,256]{1,0:T(8,128)S(1)}, f32[256,256]{1,0:T(8,128)S(1)}, u32[]{:S(2)}, u32[]{:S(2)}) collective-permute-start(f32[256,256]{1,0:T(8,128)S(1)} %collective-permute-done.1.refs_2_), channel_id=1, source_target_pairs={{0,2},{2,0},{4,6},{6,4},{8,10},{10,8},{12,14},{14,12},{16,18},{18,... | collective-permute-start | bytes 786440 | tf_op jit(solution)/shard_map/ppermute | solution.py:230
  19.6 8.9 %collective-permute-start.6 = (f32[256,256]{1,0:T(8,128)S(1)}, f32[256,256]{1,0:T(8,128)S(1)}, u32[]{:S(2)}, u32[]{:S(2)}) collective-permute-start(f32[256,256]{1,0:T(8,128)S(1)} %collective-permute-done.1.refs_2_), channel_id=1, source_target_pairs={{0,1},{1,0},{2,3},{3,2},{4,5},{5,4},{6,7},{7,6},{8,9},{9,8},{10,11... | collective-permute-start | bytes 786440 | tf_op jit(solution)/shard_map/ppermute | solution.py:233
  19.6 5.5 %collective-permute-start.4 = (f32[4,256]{1,0:T(4,128)S(1)}, f32[4,256]{1,0:T(4,128)S(1)}, u32[]{:S(2)}, u32[]{:S(2)}) collective-permute-start(f32[4,256]{1,0:T(4,128)S(1)} %log_add_fusion.lse_ref), channel_id=1, source_target_pairs={{0,4},{2,6},{4,0},{6,2},{8,12},{10,14},{12,8},{14,10},{16,20},{18,... | collective-permute-start | bytes 12296 | tf_op jit(solution)/shard_map/ppermute | solution.py:230
  24.4 3.6 %collective-permute-start.3 = (f32[4,256]{1,0:T(4,128)S(1)}, f32[4,256]{1,0:T(4,128)S(1)}, u32[]{:S(2)}, u32[]{:S(2)}) collective-permute-start(f32[4,256]{1,0:T(4,128)S(1)} %log_add_fusion.lse_ref), channel_id=1, source_target_pairs={{0,2},{2,0},{4,6},{6,4},{8,10},{10,8},{12,14},{14,12},{16,18},{18,... | collective-permute-start | bytes 12296 | tf_op jit(solution)/shard_map/ppermute | solution.py:230
  25.1 9.5 %collective-permute-start.12 = (f32[256,256]{1,0:T(8,128)S(1)}, f32[256,256]{1,0:T(8,128)S(1)}, u32[]{:S(2)}, u32[]{:S(2)}) collective-permute-start(f32[256,256]{1,0:T(8,128)S(1)} %collective-permute-done.8.refs_0_), channel_id=1, source_target_pairs={{0,1},{1,0},{2,3},{3,2},{4,5},{5,4},{6,7},{7,6},{8,9},{9,8},{10,11... | collective-permute-start | bytes 786440 | tf_op jit(solution)/shard_map/ppermute | solution.py:233
  25.1 9.5 %collective-permute-start.13 = (f32[256,256]{1,0:T(8,128)S(1)}, f32[256,256]{1,0:T(8,128)S(1)}, u32[]{:S(2)}, u32[]{:S(2)}) collective-permute-start(f32[256,256]{1,0:T(8,128)S(1)} %collective-permute-done.9.refs_2_), channel_id=1, source_target_pairs={{0,1},{1,0},{2,3},{3,2},{4,5},{5,4},{6,7},{7,6},{8,9},{9,8},{10,11... | collective-permute-start | bytes 786440 | tf_op jit(solution)/shard_map/ppermute | solution.py:233
  28.0 6.7 %collective-permute-start.14 = (f32[256,256]{1,0:T(8,128)S(1)}, f32[256,256]{1,0:T(8,128)S(1)}, u32[]{:S(2)}, u32[]{:S(2)}) collective-permute-start(f32[256,256]{1,0:T(8,128)S(1)} %collective-permute-done.10.refs_4_), channel_id=1, source_target_pairs={{0,1},{1,0},{2,3},{3,2},{4,5},{5,4},{6,7},{7,6},{8,9},{9,8},{10,11... | collective-permute-start | bytes 786440 | tf_op jit(solution)/shard_map/ppermute | solution.py:233
  28.0 6.7 %collective-permute-start.15 = (f32[256,256]{1,0:T(8,128)S(1)}, f32[256,256]{1,0:T(8,128)S(1)}, u32[]{:S(2)}, u32[]{:S(2)}) collective-permute-start(f32[256,256]{1,0:T(8,128)S(1)} %collective-permute-done.11.refs_6_), channel_id=1, source_target_pairs={{0,1},{1,0},{2,3},{3,2},{4,5},{5,4},{6,7},{7,6},{8,9},{9,8},{10,11... | collective-permute-start | bytes 786440 | tf_op jit(solution)/shard_map/ppermute | solution.py:233
  28.5 6.1 %collective-permute-start.7 = (f32[4,256]{1,0:T(4,128)S(1)}, f32[4,256]{1,0:T(4,128)S(1)}, u32[]{:S(2)}, u32[]{:S(2)}) collective-permute-start(f32[4,256]{1,0:T(4,128)S(1)} %log_add_fusion.lse_ref), channel_id=1, source_target_pairs={{0,6},{2,4},{4,2},{6,0},{8,14},{10,12},{12,10},{14,8},{16,22},{18,... | collective-permute-start | bytes 12296 | tf_op jit(solution)/shard_map/ppermute | solution.py:230
  38.1 8.3 %collective-permute-start.16 = (f32[264,256]{1,0:T(8,128)S(1)}, f32[264,256]{1,0:T(8,128)S(1)}, u32[]{:S(2)}, u32[]{:S(2)}) collective-permute-start(f32[264,256]{1,0:T(8,128)S(1)} %get-tuple-element.40), channel_id=1, source_target_pairs={{0,16},{2,18},{4,20},{6,22},{16,24},{18,26},{20,28},{22,30},{24,8}... | collective-permute-start | bytes 811016 | tf_op jit(solution)/shard_map/ppermute | solution.py:237
  46.5 8.2 %collective-permute-start.17 = (f32[264,256]{1,0:T(8,128)S(1)}, f32[264,256]{1,0:T(8,128)S(1)}, u32[]{:S(2)}, u32[]{:S(2)}) collective-permute-start(f32[264,256]{1,0:T(8,128)S(1)} %add.37), channel_id=1, source_target_pairs={{0,16},{2,18},{4,20},{6,22},{16,24},{18,26},{20,28},{22,30},{24,8}... | collective-permute-start | bytes 811016 | tf_op jit(solution)/shard_map/ppermute | solution.py:237
  54.8 7.4 %collective-permute-start.18 = (f32[264,256]{1,0:T(8,128)S(1)}, f32[264,256]{1,0:T(8,128)S(1)}, u32[]{:S(2)}, u32[]{:S(2)}) collective-permute-start(f32[264,256]{1,0:T(8,128)S(1)} %add.38), channel_id=1, source_target_pairs={{0,16},{2,18},{4,20},{6,22},{16,24},{18,26},{20,28},{22,30},{24,8}... | collective-permute-start | bytes 811016 | tf_op jit(solution)/shard_map/ppermute | solution.py:237
  62.5 8.2 %collective-permute-start.19 = (f32[264,256]{1,0:T(8,128)S(1)}, f32[264,256]{1,0:T(8,128)S(1)}, u32[]{:S(2)}, u32[]{:S(2)}) collective-permute-start(f32[264,256]{1,0:T(8,128)S(1)} %finish.1.refs_0_), channel_id=1, source_target_pairs={{0,16},{2,18},{4,20},{6,22},{16,24},{18,26},{20,28},{22,30},{24,8}... | collective-permute-start | bytes 811016 | tf_op jit(solution)/shard_map/ppermute | solution.py:237
  70.6 9.3 %collective-permute-start.20 = (f32[264,256]{1,0:T(8,128)S(1)}, f32[264,256]{1,0:T(8,128)S(1)}, u32[]{:S(2)}, u32[]{:S(2)}) collective-permute-start(f32[264,256]{1,0:T(8,128)S(1)} %collective-permute-done.19.refs_1_), channel_id=1, source_target_pairs={{0,16},{2,18},{4,20},{6,22},{16,24},{18,26},{20,28},{22,30},{24,8}... | collective-permute-start | bytes 811016 | tf_op jit(solution)/shard_map/ppermute | solution.py:237
  74.0 11.2 %collective-permute-start.23 = (f32[264,256]{1,0:T(8,128)S(1)}, f32[264,256]{1,0:T(8,128)S(1)}, u32[]{:S(2)}, u32[]{:S(2)}) collective-permute-start(f32[264,256]{1,0:T(8,128)S(1)} %finish.1.refs_0_), channel_id=1, source_target_pairs={{0,4},{2,6},{4,0},{6,2},{8,12},{10,14},{12,8},{14,10},{16,20},{18,... | collective-permute-start | bytes 811016 | tf_op jit(solution)/shard_map/ppermute | solution.py:230
  74.5 12.2 %collective-permute-start.22 = (f32[264,256]{1,0:T(8,128)S(1)}, f32[264,256]{1,0:T(8,128)S(1)}, u32[]{:S(2)}, u32[]{:S(2)}) collective-permute-start(f32[264,256]{1,0:T(8,128)S(1)} %finish.1.refs_0_), channel_id=1, source_target_pairs={{0,2},{2,0},{4,6},{6,4},{8,10},{10,8},{12,14},{14,12},{16,18},{18,... | collective-permute-start | bytes 811016 | tf_op jit(solution)/shard_map/ppermute | solution.py:230
  79.9 7.4 %collective-permute-start.21 = (f32[264,256]{1,0:T(8,128)S(1)}, f32[264,256]{1,0:T(8,128)S(1)}, u32[]{:S(2)}, u32[]{:S(2)}) collective-permute-start(f32[264,256]{1,0:T(8,128)S(1)} %collective-permute-done.20.refs_2_), channel_id=1, source_target_pairs={{0,16},{2,18},{4,20},{6,22},{16,24},{18,26},{20,28},{22,30},{24,8}... | collective-permute-start | bytes 811016 | tf_op jit(solution)/shard_map/ppermute | solution.py:237
  83.3 9.4 %collective-permute-start.25 = (f32[264,256]{1,0:T(8,128)S(1)}, f32[264,256]{1,0:T(8,128)S(1)}, u32[]{:S(2)}, u32[]{:S(2)}) collective-permute-start(f32[264,256]{1,0:T(8,128)S(1)} %collective-permute-done.19.refs_1_), channel_id=1, source_target_pairs={{0,4},{2,6},{4,0},{6,2},{8,12},{10,14},{12,8},{14,10},{16,20},{18,... | collective-permute-start | bytes 811016 | tf_op jit(solution)/shard_map/ppermute | solution.py:230
  83.8 9.4 %collective-permute-start.24 = (f32[264,256]{1,0:T(8,128)S(1)}, f32[264,256]{1,0:T(8,128)S(1)}, u32[]{:S(2)}, u32[]{:S(2)}) collective-permute-start(f32[264,256]{1,0:T(8,128)S(1)} %collective-permute-done.19.refs_1_), channel_id=1, source_target_pairs={{0,2},{2,0},{4,6},{6,4},{8,10},{10,8},{12,14},{14,12},{16,18},{18,... | collective-permute-start | bytes 811016 | tf_op jit(solution)/shard_map/ppermute | solution.py:230
  85.2 13.3 %collective-permute-start.27 = (f32[264,256]{1,0:T(8,128)S(1)}, f32[264,256]{1,0:T(8,128)S(1)}, u32[]{:S(2)}, u32[]{:S(2)}) collective-permute-start(f32[264,256]{1,0:T(8,128)S(1)} %collective-permute-done.20.refs_2_), channel_id=1, source_target_pairs={{0,4},{2,6},{4,0},{6,2},{8,12},{10,14},{12,8},{14,10},{16,20},{18,... | collective-permute-start | bytes 811016 | tf_op jit(solution)/shard_map/ppermute | solution.py:230
  86.7 12.3 %collective-permute-start.26 = (f32[264,256]{1,0:T(8,128)S(1)}, f32[264,256]{1,0:T(8,128)S(1)}, u32[]{:S(2)}, u32[]{:S(2)}) collective-permute-start(f32[264,256]{1,0:T(8,128)S(1)} %collective-permute-done.20.refs_2_), channel_id=1, source_target_pairs={{0,2},{2,0},{4,6},{6,4},{8,10},{10,8},{12,14},{14,12},{16,18},{18,... | collective-permute-start | bytes 811016 | tf_op jit(solution)/shard_map/ppermute | solution.py:230
  87.3 16.3 %collective-permute-start.29 = (f32[264,256]{1,0:T(8,128)S(1)}, f32[264,256]{1,0:T(8,128)S(1)}, u32[]{:S(2)}, u32[]{:S(2)}) collective-permute-start(f32[264,256]{1,0:T(8,128)S(1)} %collective-permute-done.21.refs_3_), channel_id=1, source_target_pairs={{0,4},{2,6},{4,0},{6,2},{8,12},{10,14},{12,8},{14,10},{16,20},{18,... | collective-permute-start | bytes 811016 | tf_op jit(solution)/shard_map/ppermute | solution.py:230
  92.7 15.3 %collective-permute-start.30 = (f32[264,256]{1,0:T(8,128)S(1)}, f32[264,256]{1,0:T(8,128)S(1)}, u32[]{:S(2)}, u32[]{:S(2)}) collective-permute-start(f32[264,256]{1,0:T(8,128)S(1)} %collective-permute-done.22.refs_4_), channel_id=1, source_target_pairs={{0,4},{2,6},{4,0},{6,2},{8,12},{10,14},{12,8},{14,10},{16,20},{18,... | collective-permute-start | bytes 811016 | tf_op jit(solution)/shard_map/ppermute | solution.py:230
  93.2 12.5 %collective-permute-start.28 = (f32[264,256]{1,0:T(8,128)S(1)}, f32[264,256]{1,0:T(8,128)S(1)}, u32[]{:S(2)}, u32[]{:S(2)}) collective-permute-start(f32[264,256]{1,0:T(8,128)S(1)} %collective-permute-done.21.refs_3_), channel_id=1, source_target_pairs={{0,2},{2,0},{4,6},{6,4},{8,10},{10,8},{12,14},{14,12},{16,18},{18,... | collective-permute-start | bytes 811016 | tf_op jit(solution)/shard_map/ppermute | solution.py:230
  98.5 10.9 %collective-permute-start.31 = (f32[264,256]{1,0:T(8,128)S(1)}, f32[264,256]{1,0:T(8,128)S(1)}, u32[]{:S(2)}, u32[]{:S(2)}) collective-permute-start(f32[264,256]{1,0:T(8,128)S(1)} %collective-permute-done.24.refs_6_), channel_id=1, source_target_pairs={{0,4},{2,6},{4,0},{6,2},{8,12},{10,14},{12,8},{14,10},{16,20},{18,... | collective-permute-start | bytes 811016 | tf_op jit(solution)/shard_map/ppermute | solution.py:230
  99.0 10.4 %collective-permute-start.32 = (f32[264,256]{1,0:T(8,128)S(1)}, f32[264,256]{1,0:T(8,128)S(1)}, u32[]{:S(2)}, u32[]{:S(2)}) collective-permute-start(f32[264,256]{1,0:T(8,128)S(1)} %collective-permute-done.27.refs_9_), channel_id=1, source_target_pairs={{0,2},{2,0},{4,6},{6,4},{8,10},{10,8},{12,14},{14,12},{16,18},{18,... | collective-permute-start | bytes 811016 | tf_op jit(solution)/shard_map/ppermute | solution.py:230
  103.6 6.5 %collective-permute-start.33 = (f32[264,256]{1,0:T(8,128)S(1)}, f32[264,256]{1,0:T(8,128)S(1)}, u32[]{:S(2)}, u32[]{:S(2)}) collective-permute-start(f32[264,256]{1,0:T(8,128)S(1)} %collective-permute-done.29.refs_11_), channel_id=1, source_target_pairs={{0,2},{2,0},{4,6},{6,4},{8,10},{10,8},{12,14},{14,12},{16,18},{18,... | collective-permute-start | bytes 811016 | tf_op jit(solution)/shard_map/ppermute | solution.py:230

commit v4 on v3

--- a/solution.py
+++ b/solution.py
@@ -105,20 +105,25 @@
         add_block(twice_ref[...], norm_ref[...], x, lse_ref[pl.ds(at, 1), :], acc_ref, cnt_ref, False)
 
 
-def near_kernel(cores, order, where_ref, points_ref, c_ref, lse_ref, lse_x_ref, lse_y_ref, *refs):
-    x_refs = refs[: 2 * cores]
-    acc_ref, cnt_ref, twice_ref, norm_ref, own_ref = refs[2 * cores :]
-    share, size = twice_ref.shape[0], own_ref.shape[0]
+def own_kernel(cores, order, where_ref, points_ref, c_ref, lse_ref, acc_ref, cnt_ref, twice_ref, norm_ref, own_ref):
+    size = own_ref.shape[0]
     plane, line = lax.rem(where_ref[0], 4), lax.div(where_ref[0], 4)
-    start = pl.multiple_of(plane * share, share)
-    c = c_ref[pl.ds(start, share), :]
-    twice_ref[...] = c + c
-    norm_ref[...] = norms(c)
-    own_ref[...] = c_ref[pl.ds(pl.multiple_of(start + line * size, size), size), :]
+    for l in range(len(order)):
+        c = c_ref[pl.ds(pl.multiple_of((4 * l + plane) * size, size), size), :]
+        twice_ref[l * size : (l + 1) * size, :] = c + c
+        norm_ref[l * size : (l + 1) * size, :] = norms(c)
+    own_ref[...] = c_ref[pl.ds(pl.multiple_of((4 * line + plane) * size, size), size), :]
     half = points_ref.shape[0] // (2 * cores)
     for i in range(2 * cores):
         x = points_ref[i * half : (i + 1) * half, :]
         add_block(twice_ref[...], norm_ref[...], x, lse_ref[i : i + 1, :], acc_ref, cnt_ref, i == 0)
+
+
+def near_kernel(cores, where_ref, twice_ref, norm_ref, acc_in_ref, cnt_in_ref, lse_x_ref, lse_y_ref, *refs):
+    x_refs = refs[: 2 * cores]
+    acc_ref, cnt_ref = refs[2 * cores :]
+    acc_ref[...] = acc_in_ref[...]
+    cnt_ref[...] = cnt_in_ref[...]
     pieces = [(x_refs[rc], lse_x_ref, rc, 0) for rc in range(cores)]
     pieces += [(x_refs[cores + rc], lse_y_ref, rc, 1) for rc in range(cores)]
     add_pieces(where_ref, twice_ref, norm_ref, pieces, acc_ref, cnt_ref)
@@ -161,59 +166,15 @@
     out_ref[...] = a_ref[...] + b_ref[...]
 
 
-def finish_kernel(c_ref, *refs):
-    out_ref = refs[-1]
+def finish_kernel(c_ref, mine_ref, moved_ref, out_ref):
     size, width = c_ref.shape
-    total = functools.reduce(jnp.add, [ref[...] for ref in refs[:-1]])
+    total = mine_ref[...] + moved_ref[...]
     counts = total[size:, :]
     column = counts.T[:size, 0:1]
     out_ref[0:size, :] = (total[:size, :] + prior_mass * c_ref[...].astype(jnp.float32)) / (
         column + prior_mass
     )
-    row = lax.broadcasted_iota(jnp.int32, (8, LANES), 0)
-    spread = jnp.zeros((8, LANES), jnp.float32)
-    for k in range(size // LANES):
-        spread = jnp.where(row == k, counts[:, k * LANES : (k + 1) * LANES], spread)
-    out_ref[size:, :] = jnp.concatenate([spread] * (width // LANES), axis=1)
-
-
-def place_kernel(names, order, late, where_ref, *refs):
-    count, lines = len(names), len(order)
-    block_refs = refs[:count]
-    if late is None:
-        new_ref, sems = refs[count:]
-        chosen = range(count)
-    else:
-        _, new_ref, counts_ref, tiles_ref, sems = refs[count:]
-        chosen = late
-    width = new_ref.shape[1]
-    size = block_refs[0].shape[0] - 8
-    plane, line = lax.rem(where_ref[0], 4), lax.div(where_ref[0], 4)
-
-    def place(i):
-        bits, steps = names[i]
-        return (plane ^ bits) * lines + behind(order, line, steps)
-
-    copies = []
-    for i in chosen:
-        at = pl.multiple_of(place(i) * size, size)
-        copies.append(
-            pltpu.make_async_copy(block_refs[i].at[0:size, :], new_ref.at[pl.ds(at, size), :], sems.at[i])
-        )
-    if late is not None:
-        for i in range(count):
-            copies.append(
-                pltpu.make_async_copy(block_refs[i].at[size:, :], tiles_ref.at[i], sems.at[count + i])
-            )
-    for copy in copies:
-        copy.start()
-    for copy in copies:
-        copy.wait()
-    if late is not None:
-        each = size // LANES
-        for i in range(count):
-            for k in range(each):
-                counts_ref[pl.ds(place(i) * each + k, 1), :] = tiles_ref[i, k : k + 1, 0:LANES]
+    out_ref[size:, :] = counts
 
 
 def body(n, cores, points, centroids):
@@ -264,26 +225,40 @@
     def with_siblings(pieces):
         return [a if rc == 0 else flip_core(a, rc) for a in pieces for rc in range(cores)]
 
+    acc_shape, cnt_shape = f32(share, width), f32(share, min(LANES, half))
     acc, cnt, twice, norm, own = call(
-        functools.partial(near_kernel, cores, order),
+        functools.partial(own_kernel, cores, order),
         (
-            f32(share, width),
-            f32(share, min(LANES, half)),
+            acc_shape,
+            cnt_shape,
             jax.ShapeDtypeStruct((share, width), jnp.bfloat16),
             f32(share, LANES),
             jax.ShapeDtypeStruct((size, width), jnp.bfloat16),
         ),
-        [SMEM] + [VMEM] * (5 + 2 * cores),
-        (where, points, centroids, lse, lse_x, lse_y, *with_siblings((x0, y1))),
+        [SMEM] + [VMEM] * 3,
+        (where, points, centroids, lse),
+        "own",
+        flops=4 * share * width * rows,
+    )
+    early = with_siblings((x0, y1))
+    early, late, acc, cnt, lse_x, lse_y, lse_d = lax.optimization_barrier(
+        (early, (x1, y0, d0, d1), acc, cnt, lse_x, lse_y, lse_d)
+    )
+    late = with_siblings(late)
+    acc, cnt = call(
+        functools.partial(near_kernel, cores),
+        (acc_shape, cnt_shape),
+        [SMEM] + [VMEM] * (6 + 2 * cores),
+        (where, twice, norm, acc, cnt, lse_x, lse_y, *early),
         "near",
-        flops=4 * share * width * 2 * rows,
-    )
-    late = lax.optimization_barrier((x1, y0, d0, d1))
+        flops=4 * share * width * rows,
+        aliases={3: 0, 4: 1},
+    )
     sums = call(
         functools.partial(far_kernel, cores, order),
         [f32(size + 8, width)] * lines,
         [SMEM] + [VMEM] * (7 + 4 * cores),
-        (where, twice, norm, acc, cnt, lse_x, lse_y, lse_d, *with_siblings(late)),
+        (where, twice, norm, acc, cnt, lse_x, lse_y, lse_d, *late),
         "far",
         scratch=[
             pltpu.VMEM((share, width), jnp.float32),
@@ -295,39 +270,10 @@
     for s in range(2, lines):
         moving = ring(call(add_kernel, f32(size + 8, width), [VMEM] * 2, (sums[s], moving), "add"))
     done = call(finish_kernel, f32(size + 8, width), [VMEM] * 3, (own, sums[0], moving), "finish")
-
-    column = [done]
-    for s in range(1, lines):
-        column.append(ring(column[-1]))
-    over_x = [flip(b, 1) for b in column]
-    over_y = [flip(b, 2) for b in column]
-    cut = lines // 2
-    over_xy = [flip(b, 2) for b in over_x[:cut]] + [flip(b, 1) for b in over_y[cut:]]
-    blocks = column + [b for pair in zip(over_x, over_y) for b in pair] + over_xy
-    names = [(0, s) for s in range(lines)] + [(b, s) for s in range(lines) for b in (1, 2)]
-    names += [(3, s) for s in range(lines)]
-    count = 4 * lines
-    early = count - lines
-    new = call(
-        functools.partial(place_kernel, names[:early], order, None),
-        f32(local_cent, width),
-        [SMEM] + [ANY] * early,
-        (where, *blocks[:early]),
-        "place_early",
-        out_specs=ANY,
-        scratch=[pltpu.SemaphoreType.DMA((early,))],
-    )
-    new, counts = call(
-        functools.partial(place_kernel, names, order, tuple(range(early, count))),
-        (f32(local_cent, width), f32(local_cent // LANES, LANES)),
-        [SMEM] + [ANY] * (count + 1),
-        (where, *blocks, new),
-        "place_late",
-        out_specs=(ANY, VMEM),
-        scratch=[pltpu.VMEM((count, 8, width), jnp.float32), pltpu.SemaphoreType.DMA((2 * count,))],
-        aliases={count + 1: 0},
-    )
-    return new, counts.reshape(-1), log_evidence
+    gathered = lax.all_gather(done, "dp", axis=0)
+    new = gathered[:, :size, :].reshape(local_cent, width)
+    counts = gathered[:, size, :size].reshape(-1)
+    return new, counts, log_evidence
 
 
 def solution(mesh):

time: 113 us -> 167 us (1.48)
  waiting for transfers between devices: 45 us -> 103 us
  starting transfers between devices: 44.7 us -> 22.1 us
  between operations: 0.79 us -> 14.2 us
  local copies, waits for them, and re-layouts: 2.72 us -> 10.5 us
  Pallas kernels: 18.7 us -> 16.4 us
    all_gather x0 -> x1, waiting for transfers between devices: none -> 77.4 us  [body(): gathered = lax.all_gather(done, 'dp', axis=0)]
    ppermute x21 -> x9, starting transfers between devices: 23.7 us -> 11.4 us  [flip(): return lax.ppermute(x, 'dp', [(i, i ^ bits) for i in range(n)])]
    ppermute x21 -> x9, waiting for transfers between devices: 21.8 us -> 9.78 us  [flip(): return lax.ppermute(x, 'dp', [(i, i ^ bits) for i in range(n)])]
    ppermute x6 -> x3, starting transfers between devices: 19.7 us -> 9.51 us  [ring(): lax.ppermute(x, 'dp', [(4 * a + i, 4 * b + i) for a, b in pairs for i in...]
    ppermute x6 -> x3, waiting for transfers between devices: 23.2 us -> 15.3 us  [ring(): lax.ppermute(x, 'dp', [(4 * a + i, 4 * b + i) for a, b in pairs for i in...]
    slice x0 -> x2, local copies, waits for them, and re-layouts: none -> 6.12 us  [the longest x1 4.6 us: body(): new = gathered[:, :size, :].reshape(local_cent, width)]
    pallas_call x9 -> x8, Pallas kernels: 18.7 us -> 16.4 us  [call(): pl.pallas_call(kernel, out_shape=out_shape, in_specs=in_specs, out_specs=...]
    unnamed x6 -> x12, local copies, waits for them, and re-layouts: 2.64 us -> 4.25 us
  transfers between devices with their start and end apart: 34 -> 20, of which waited for: 15 -> 9; matrix products, arithmetic and copies ran while one was open for 1% -> 0% of each run, Pallas kernels for 11% -> 6%
where the time goes in v4:
time: 167 us; the launch traced here: 166 us
  waiting for transfers between devices  103 us (62%)
  starting transfers between devices  22.1 us (13%)
  Pallas kernels  16.4 us (10%)
  between operations  14.2 us (9%)
  local copies, waits for them, and re-layouts  10.5 us (6%)
    all_gather x1, waiting for transfers between devices, body(): gathered = lax.all_gather(done, 'dp', axis=0)  77.4 us
    pallas_call x8, Pallas kernels, call(): pl.pallas_call(kernel, out_shape=out_shape, in_specs=in_specs, out_specs=...  16.4 us
    ppermute x3, waiting for transfers between devices, ring(): lax.ppermute(x, 'dp', [(4 * a + i, 4 * b + i) for a, b in pairs for i in...  15.3 us
    ppermute x9, starting transfers between devices, flip(): return lax.ppermute(x, 'dp', [(i, i ^ bits) for i in range(n)])  11.4 us
    ppermute x9, waiting for transfers between devices, flip(): return lax.ppermute(x, 'dp', [(i, i ^ bits) for i in range(n)])  9.78 us
    ppermute x3, starting transfers between devices, ring(): lax.ppermute(x, 'dp', [(4 * a + i, 4 * b + i) for a, b in pairs for i in...  9.51 us
    slice x1, local copies, waits for them, and re-layouts, body(): new = gathered[:, :size, :].reshape(local_cent, width)  4.6 us
    unnamed x12, local copies, waits for them, and re-layouts  4.25 us
  transfers between devices with their start and end apart: 20, of which 9 were waited for; matrix products, arithmetic and copies ran while one was open for 0% of the time, Pallas kernels for 6%

profile of v4, /device:TPU:0, one launch (start us, length us, event | category | flops | bytes accessed | tf_op | source)
XLA Modules:
  0.0 166.3 jit_solution(2140980431596365748)
XLA Ops:
  7.2 0.0 all-gather.3.cloned.1.call-start
  7.2 0.1 pad_add_fusion.where_ref
  7.3 1.0 copy-done
  8.3 1.4 open.1
  9.7 2.9 %collective-permute-start = (f32[256,256]{1,0:T(8,128)}, f32[256,256]{1,0:T(8,128)S(1)}, u32[]{:S(2)}, u32[]{:S(2)}) collective-permute-start(f32[256,256]{1,0:T(8,128)} %get-tuple-element.32), channel_id=1, source_target_pairs={{0,2},{2,0},{4,6},{6,4},{8,10},{10,8},{12,14},{14,12},{16,18},{18,... | collective-permute-start | bytes 786440 | tf_op jit(solution)/shard_map/ppermute | solution.py:191
  12.6 1.5 collective-permute-start.1
  14.1 0.5 collective-permute-start.6
  14.7 0.1 collective-permute-start.5
  14.7 1.6 copy-done.2
  16.3 5.1 %stats.1 = f32[2,1024]{1,0:T(2,128)S(1)} custom-call(bf16[1024,256]{1,0:T(8,128)(2,1)S(1)} %copy-done, bf16[4096,256]{1,0:T(8,128)(2,1)S(1)} %copy-done.2), custom_call_target="tpu_custom_call" | custom-call | flops 2147483648 | bytes 2621440 | tf_op jit(solution)/shard_map/stats/pallas_call | solution.py:26
  21.4 0.0 collective-permute-done.refs_0_
  21.4 0.7 collective-permute-done.1.refs_2_
  22.1 0.0 collective-permute-start.2
  22.1 0.7 copy-done.4
  22.8 1.5 collective-permute-start.7
  24.3 1.4 collective-permute-start.8
  25.7 1.4 collective-permute-done.6.refs_2_
  27.1 0.0 collective-permute-done.5.refs_0_
  27.1 0.7 collective-permute-start.11
  27.8 5.5 %collective-permute-done.11.lse_d_ref = f32[4,256]{1,0:T(4,128)S(1)} collective-permute-done((f32[4,256]{1,0:T(4,128)S(1)}, f32[4,256]{1,0:T(4,128)S(1)}, u32[]{:S(2)}, u32[]{:S(2)}) %collective-permute-start.11) | collective-permute-done | bytes 4128 | tf_op jit(solution)/shard_map/ppermute | solution.py:191
  33.3 1.5 collective-permute-start.10
  34.8 2.1 %collective-permute-done.10.lse_y_ref = f32[4,256]{1,0:T(4,128)S(1)} collective-permute-done((f32[4,256]{1,0:T(4,128)S(1)}, f32[4,256]{1,0:T(4,128)S(1)}, u32[]{:S(2)}, u32[]{:S(2)}) %collective-permute-start.10) | collective-permute-done | bytes 4128 | tf_op jit(solution)/shard_map/ppermute | solution.py:191
  36.9 1.3 collective-permute-start.9
  38.2 2.1 %own.1 = (f32[1024,256]{1,0:T(8,128)S(1)}, f32[1024,128]{1,0:T(8,128)S(1)}, bf16[1024,256]{1,0:T(8,128)(2,1)S(1)}, f32[1024,128]{1,0:T(8,128)S(1)}, bf16[256,256]{1,0:T(8,128)(2,1)S(1)}) custom-call(s32[2]{0:T(128)S(1)} %pad_add_fusion.where_ref, bf16[1024,256]{1,0:T(8,128)(2,1)S(1)} %copy-done.1, bf16[4096,256]{1,0:T(8,128)(2,1)S(1)} %copy-done.3, ...), custom_call_target="tpu_custom_call" | custom-call | flops 1073741824 | bytes 2625544 | tf_op jit(solution)/shard_map/own/pallas_call | solution.py:26
  40.4 0.2 collective-permute-done.9.lse_x_ref
  40.5 0.0 collective-permute-done.7.refs_4_
  40.6 0.1 collective-permute-start.12
  40.6 0.5 collective-permute-start.13
  41.1 0.1 collective-permute-start.14
  41.2 0.4 collective-permute-start.15
  41.7 0.9 copy-done.5
  42.6 2.8 %near.1 = (f32[1024,256]{1,0:T(8,128)S(1)}, f32[1024,128]{1,0:T(8,128)S(1)}) custom-call(s32[2]{0:T(128)S(1)} %pad_add_fusion.where_ref, bf16[1024,256]{1,0:T(8,128)(2,1)S(1)} %get-tuple-element.36.twice_ref, f32[1024,128]{1,0:T(8,128)S(1)} %get-tuple-element.37.norm_ref, ...), custom_call_target="tpu_custom_call", output_to_operand_aliasing={{0}: (3, {}), {1}: (4, {})} | custom-call | flops 1073741824 | bytes 3678216 | tf_op jit(solution)/shard_map/near/pallas_call | solution.py:26
  45.4 0.0 collective-permute-done.12.refs_1_
  45.4 0.0 collective-permute-done.14.refs_5_
  45.4 0.0 collective-permute-done.15.refs_7_
  45.5 4.0 %far.1 = (f32[264,256]{1,0:T(8,128)S(1)}, f32[264,256]{1,0:T(8,128)S(1)}, f32[264,256]{1,0:T(8,128)S(1)}, f32[264,256]{1,0:T(8,128)S(1)}) custom-call(s32[2]{0:T(128)S(1)} %pad_add_fusion.where_ref, bf16[1024,256]{1,0:T(8,128)(2,1)S(1)} %get-tuple-element.36.twice_ref, f32[1024,128]{1,0:T(8,128)S(1)} %get-tuple-element.37.norm_ref, ...), custom_call_target="tpu_custom_call" | custom-call | flops 2147483648 | bytes 4730888 | tf_op jit(solution)/shard_map/far/pallas_call | solution.py:26
  49.4 2.6 %collective-permute-start.16 = (f32[264,256]{1,0:T(8,128)S(1)}, f32[264,256]{1,0:T(8,128)S(1)}, u32[]{:S(2)}, u32[]{:S(2)}) collective-permute-start(f32[264,256]{1,0:T(8,128)S(1)} %get-tuple-element.60), channel_id=1, source_target_pairs={{0,16},{2,18},{4,20},{6,22},{16,24},{18,26},{20,28},{22,30},{24,8}... | collective-permute-start | bytes 811016 | tf_op jit(solution)/shard_map/ppermute | solution.py:198
  52.1 6.0 %collective-permute-done.16.b_ref = f32[264,256]{1,0:T(8,128)S(1)} collective-permute-done((f32[264,256]{1,0:T(8,128)S(1)}, f32[264,256]{1,0:T(8,128)S(1)}, u32[]{:S(2)}, u32[]{:S(2)}) %collective-permute-start.16) | collective-permute-done | bytes 270368 | tf_op jit(solution)/shard_map/ppermute | solution.py:198
  58.1 3.4 %collective-permute-start.17 = (f32[264,256]{1,0:T(8,128)S(1)}, f32[264,256]{1,0:T(8,128)S(1)}, u32[]{:S(2)}, u32[]{:S(2)}) collective-permute-start(f32[264,256]{1,0:T(8,128)S(1)} %add.37), channel_id=1, source_target_pairs={{0,16},{2,18},{4,20},{6,22},{16,24},{18,26},{20,28},{22,30},{24,8}... | collective-permute-start | bytes 811016 | tf_op jit(solution)/shard_map/ppermute | solution.py:198
  61.5 5.1 %collective-permute-done.17.b_ref = f32[264,256]{1,0:T(8,128)S(1)} collective-permute-done((f32[264,256]{1,0:T(8,128)S(1)}, f32[264,256]{1,0:T(8,128)S(1)}, u32[]{:S(2)}, u32[]{:S(2)}) %collective-permute-start.17) | collective-permute-done | bytes 270368 | tf_op jit(solution)/shard_map/ppermute | solution.py:198
  66.7 3.4 %collective-permute-start.18 = (f32[264,256]{1,0:T(8,128)S(1)}, f32[264,256]{1,0:T(8,128)S(1)}, u32[]{:S(2)}, u32[]{:S(2)}) collective-permute-start(f32[264,256]{1,0:T(8,128)S(1)} %add.38), channel_id=1, source_target_pairs={{0,16},{2,18},{4,20},{6,22},{16,24},{18,26},{20,28},{22,30},{24,8}... | collective-permute-start | bytes 811016 | tf_op jit(solution)/shard_map/ppermute | solution.py:198
  70.1 4.2 %collective-permute-done.18.moved_ref = f32[264,256]{1,0:T(8,128)S(1)} collective-permute-done((f32[264,256]{1,0:T(8,128)S(1)}, f32[264,256]{1,0:T(8,128)S(1)}, u32[]{:S(2)}, u32[]{:S(2)}) %collective-permute-start.18) | collective-permute-done | bytes 270368 | tf_op jit(solution)/shard_map/ppermute | solution.py:198
  74.3 1.0 finish.1
  75.3 0.0 all-gather.3.cloned.1.call-update
  75.3 0.6 add_add_fusion
  76.0 77.4 %all-gather.3.cloned.1.call-done = f32[4224,256]{1,0:T(8,128)} async-done(((f32[264,256]{1,0:T(8,128)}), f32[4224,256]{1,0:T(8,128)}) %all-gather.3.cloned.1.call-update) | async-done | bytes 4325392 | tf_op jit(solution)/shard_map/all_gather | solution.py:273
  153.4 1.5 slice.29
  154.9 4.6 %slice.28 = f32[16,256,256]{2,1,0:T(8,128)} slice(f32[16,264,256]{2,1,0:T(8,128)} %bitcast.11), slice={[0:16], [0:256], [0:256]} | slice | bytes 8388608 | tf_op jit(solution)/shard_map/slice | solution.py:274
  (24 shorter events, 0.2 us)
Async XLA Ops:
  7.2 146.2 %all-gather.3.cloned.1.call-start = ((), (), s32[]{:S(2)}) async-start(), calls=%async_computation | async-start | bytes 4595712 | tf_op jit(solution)/shard_map/all_gather | solution.py:273
  7.3 1.0 copy-start
  8.3 29.9 %copy-start.1 = (bf16[1024,256]{1,0:T(8,128)(2,1)S(1)}, bf16[1024,256]{1,0:T(8,128)(2,1)}, u32[]{:S(2)}) copy-start(bf16[1024,256]{1,0:T(8,128)(2,1)} %points_ref.5) | copy-start | bytes 1572868
  9.7 11.7 %collective-permute-start = (f32[256,256]{1,0:T(8,128)}, f32[256,256]{1,0:T(8,128)S(1)}, u32[]{:S(2)}, u32[]{:S(2)}) collective-permute-start(f32[256,256]{1,0:T(8,128)} %get-tuple-element.32), channel_id=1, source_target_pairs={{0,2},{2,0},{4,6},{6,4},{8,10},{10,8},{12,14},{14,12},{16,18},{18,... | collective-permute-start | bytes 786440 | tf_op jit(solution)/shard_map/ppermute | solution.py:191
  12.6 9.4 %collective-permute-start.1 = (f32[256,256]{1,0:T(8,128)}, f32[256,256]{1,0:T(8,128)S(1)}, u32[]{:S(2)}, u32[]{:S(2)}) collective-permute-start(f32[256,256]{1,0:T(8,128)} %get-tuple-element.33), channel_id=1, source_target_pairs={{0,4},{2,6},{4,0},{6,2},{8,12},{10,14},{12,8},{14,10},{16,20},{18,... | collective-permute-start | bytes 786440 | tf_op jit(solution)/shard_map/ppermute | solution.py:191
  14.1 12.9 %collective-permute-start.6 = (f32[256,256]{1,0:T(8,128)}, f32[256,256]{1,0:T(8,128)S(1)}, u32[]{:S(2)}, u32[]{:S(2)}) collective-permute-start(f32[256,256]{1,0:T(8,128)} %get-tuple-element.32), channel_id=1, source_target_pairs={{0,4},{2,6},{4,0},{6,2},{8,12},{10,14},{12,8},{14,10},{16,20},{18,... | collective-permute-start | bytes 786440 | tf_op jit(solution)/shard_map/ppermute | solution.py:191
  14.7 12.5 %collective-permute-start.5 = (f32[256,256]{1,0:T(8,128)}, f32[256,256]{1,0:T(8,128)S(1)}, u32[]{:S(2)}, u32[]{:S(2)}) collective-permute-start(f32[256,256]{1,0:T(8,128)} %get-tuple-element.33), channel_id=1, source_target_pairs={{0,2},{2,0},{4,6},{6,4},{8,10},{10,8},{12,14},{14,12},{16,18},{18,... | collective-permute-start | bytes 786440 | tf_op jit(solution)/shard_map/ppermute | solution.py:191
  14.7 1.6 copy-start.2
  16.3 21.9 %copy-start.3 = (bf16[4096,256]{1,0:T(8,128)(2,1)S(1)}, bf16[4096,256]{1,0:T(8,128)(2,1)}, u32[]{:S(2)}) copy-start(bf16[4096,256]{1,0:T(8,128)(2,1)} %c_ref.3) | copy-start | bytes 6291460
  22.1 0.7 copy-start.4
  22.1 2.2 %collective-permute-start.2 = (f32[2,1024]{1,0:T(2,128)S(1)}, f32[2,1024]{1,0:T(2,128)S(1)}, u32[]{:S(2)}, u32[]{:S(2)}) collective-permute-start(f32[2,1024]{1,0:T(2,128)S(1)} %stats.1), channel_id=1, source_target_pairs={{0,1},{1,0},{2,3},{3,2},{4,5},{5,4},{6,7},{7,6},{8,9},{9,8},{10,11... | collective-permute-start | bytes 24584 | tf_op jit(solution)/shard_map/ppermute | solution.py:194
  22.8 17.8 %collective-permute-start.7 = (f32[256,256]{1,0:T(8,128)S(1)}, f32[256,256]{1,0:T(8,128)}, u32[]{:S(2)}, u32[]{:S(2)}) collective-permute-start(f32[256,256]{1,0:T(8,128)S(1)} %collective-permute-done.refs_0_), channel_id=1, source_target_pairs={{0,4},{2,6},{4,0},{6,2},{8,12},{10,14},{12,8},{14,10},{16,20},{18,... | collective-permute-start | bytes 786440 | tf_op jit(solution)/shard_map/ppermute | solution.py:191
  24.3 16.3 %collective-permute-start.3 = (f32[256,256]{1,0:T(8,128)S(1)}, f32[256,256]{1,0:T(8,128)}, u32[]{:S(2)}, u32[]{:S(2)}) collective-permute-start(f32[256,256]{1,0:T(8,128)S(1)} %collective-permute-done.refs_0_), channel_id=1, source_target_pairs={{0,1},{1,0},{2,3},{3,2},{4,5},{5,4},{6,7},{7,6},{8,9},{9,8},{10,11... | collective-permute-start | bytes 786440 | tf_op jit(solution)/shard_map/ppermute | solution.py:194
  24.3 16.2 %collective-permute-start.8 = (f32[256,256]{1,0:T(8,128)}, f32[256,256]{1,0:T(8,128)}, u32[]{:S(2)}, u32[]{:S(2)}) collective-permute-start(f32[256,256]{1,0:T(8,128)} %copy-done.4), channel_id=1, source_target_pairs={{0,2},{2,0},{4,6},{6,4},{8,10},{10,8},{12,14},{14,12},{16,18},{18,... | collective-permute-start | bytes 786440 | tf_op jit(solution)/shard_map/ppermute | solution.py:191
  27.1 13.5 %collective-permute-start.4 = (f32[256,256]{1,0:T(8,128)}, f32[256,256]{1,0:T(8,128)S(1)}, u32[]{:S(2)}, u32[]{:S(2)}) collective-permute-start(f32[256,256]{1,0:T(8,128)} %copy-done.4), channel_id=1, source_target_pairs={{0,1},{1,0},{2,3},{3,2},{4,5},{5,4},{6,7},{7,6},{8,9},{9,8},{10,11... | collective-permute-start | bytes 786440 | tf_op jit(solution)/shard_map/ppermute | solution.py:194
  27.1 6.2 %collective-permute-start.11 = (f32[4,256]{1,0:T(4,128)S(1)}, f32[4,256]{1,0:T(4,128)S(1)}, u32[]{:S(2)}, u32[]{:S(2)}) collective-permute-start(f32[4,256]{1,0:T(4,128)S(1)} %log_add_fusion.lse_ref), channel_id=1, source_target_pairs={{0,6},{2,4},{4,2},{6,0},{8,14},{10,12},{12,10},{14,8},{16,22},{18,... | collective-permute-start | bytes 12296 | tf_op jit(solution)/shard_map/ppermute | solution.py:191
  33.3 3.6 %collective-permute-start.10 = (f32[4,256]{1,0:T(4,128)S(1)}, f32[4,256]{1,0:T(4,128)S(1)}, u32[]{:S(2)}, u32[]{:S(2)}) collective-permute-start(f32[4,256]{1,0:T(4,128)S(1)} %log_add_fusion.lse_ref), channel_id=1, source_target_pairs={{0,4},{2,6},{4,0},{6,2},{8,12},{10,14},{12,8},{14,10},{16,20},{18,... | collective-permute-start | bytes 12296 | tf_op jit(solution)/shard_map/ppermute | solution.py:191
  36.9 3.6 %collective-permute-start.9 = (f32[4,256]{1,0:T(4,128)S(1)}, f32[4,256]{1,0:T(4,128)S(1)}, u32[]{:S(2)}, u32[]{:S(2)}) collective-permute-start(f32[4,256]{1,0:T(4,128)S(1)} %log_add_fusion.lse_ref), channel_id=1, source_target_pairs={{0,2},{2,0},{4,6},{6,4},{8,10},{10,8},{12,14},{14,12},{16,18},{18,... | collective-permute-start | bytes 12296 | tf_op jit(solution)/shard_map/ppermute | solution.py:191
  40.6 4.8 %collective-permute-start.12 = (f32[256,256]{1,0:T(8,128)S(1)}, f32[256,256]{1,0:T(8,128)S(1)}, u32[]{:S(2)}, u32[]{:S(2)}) collective-permute-start(f32[256,256]{1,0:T(8,128)S(1)} %collective-permute-done.5.refs_0_), channel_id=1, source_target_pairs={{0,1},{1,0},{2,3},{3,2},{4,5},{5,4},{6,7},{7,6},{8,9},{9,8},{10,11... | collective-permute-start | bytes 786440 | tf_op jit(solution)/shard_map/ppermute | solution.py:194
  40.6 4.8 %collective-permute-start.13 = (f32[256,256]{1,0:T(8,128)S(1)}, f32[256,256]{1,0:T(8,128)S(1)}, u32[]{:S(2)}, u32[]{:S(2)}) collective-permute-start(f32[256,256]{1,0:T(8,128)S(1)} %collective-permute-done.6.refs_2_), channel_id=1, source_target_pairs={{0,1},{1,0},{2,3},{3,2},{4,5},{5,4},{6,7},{7,6},{8,9},{9,8},{10,11... | collective-permute-start | bytes 786440 | tf_op jit(solution)/shard_map/ppermute | solution.py:194
  41.1 4.3 %collective-permute-start.14 = (f32[256,256]{1,0:T(8,128)}, f32[256,256]{1,0:T(8,128)S(1)}, u32[]{:S(2)}, u32[]{:S(2)}) collective-permute-start(f32[256,256]{1,0:T(8,128)} %collective-permute-done.7.refs_4_), channel_id=1, source_target_pairs={{0,1},{1,0},{2,3},{3,2},{4,5},{5,4},{6,7},{7,6},{8,9},{9,8},{10,11... | collective-permute-start | bytes 786440 | tf_op jit(solution)/shard_map/ppermute | solution.py:194
  41.2 4.2 %collective-permute-start.15 = (f32[256,256]{1,0:T(8,128)}, f32[256,256]{1,0:T(8,128)S(1)}, u32[]{:S(2)}, u32[]{:S(2)}) collective-permute-start(f32[256,256]{1,0:T(8,128)} %collective-permute-done.8.refs_6_), channel_id=1, source_target_pairs={{0,1},{1,0},{2,3},{3,2},{4,5},{5,4},{6,7},{7,6},{8,9},{9,8},{10,11... | collective-permute-start | bytes 786440 | tf_op jit(solution)/shard_map/ppermute | solution.py:194
  41.7 0.9 copy-start.5
  49.4 8.6 %collective-permute-start.16 = (f32[264,256]{1,0:T(8,128)S(1)}, f32[264,256]{1,0:T(8,128)S(1)}, u32[]{:S(2)}, u32[]{:S(2)}) collective-permute-start(f32[264,256]{1,0:T(8,128)S(1)} %get-tuple-element.60), channel_id=1, source_target_pairs={{0,16},{2,18},{4,20},{6,22},{16,24},{18,26},{20,28},{22,30},{24,8}... | collective-permute-start | bytes 811016 | tf_op jit(solution)/shard_map/ppermute | solution.py:198
  58.1 8.6 %collective-permute-start.17 = (f32[264,256]{1,0:T(8,128)S(1)}, f32[264,256]{1,0:T(8,128)S(1)}, u32[]{:S(2)}, u32[]{:S(2)}) collective-permute-start(f32[264,256]{1,0:T(8,128)S(1)} %add.37), channel_id=1, source_target_pairs={{0,16},{2,18},{4,20},{6,22},{16,24},{18,26},{20,28},{22,30},{24,8}... | collective-permute-start | bytes 811016 | tf_op jit(solution)/shard_map/ppermute | solution.py:198
  66.7 7.7 %collective-permute-start.18 = (f32[264,256]{1,0:T(8,128)S(1)}, f32[264,256]{1,0:T(8,128)S(1)}, u32[]{:S(2)}, u32[]{:S(2)}) collective-permute-start(f32[264,256]{1,0:T(8,128)S(1)} %add.38), channel_id=1, source_target_pairs={{0,16},{2,18},{4,20},{6,22},{16,24},{18,26},{20,28},{22,30},{24,8}... | collective-permute-start | bytes 811016 | tf_op jit(solution)/shard_map/ppermute | solution.py:198
Sparse Core Ops, SparseCore 0:
  75.5 77.8 all-gather.2

commit v5 on v4

v5 whole, which is shorter than its diff:
```python
import functools
import math

import jax
import jax.numpy as jnp
from jax import lax
from jax.experimental import pallas as pl
from jax.experimental.pallas import tpu as pltpu
from jax.sharding import PartitionSpec as P

prior_mass = 0.5
VMEM_LIMIT = 48 * 1024 * 1024
LANES = 128
NT = (((1,), (1,)), ((), ()))
NN = (((1,), (0,)), ((), ()))
VMEM = pl.BlockSpec(memory_space=pltpu.VMEM)
SMEM = pl.BlockSpec(memory_space=pltpu.SMEM)
ANY = pl.BlockSpec(memory_space=pl.ANY)
HBM = pl.BlockSpec(memory_space=pltpu.HBM)


def f32(*shape):
    return jax.ShapeDtypeStruct(shape, jnp.float32)


def call(kernel, out_shape, in_specs, args, name, out_specs=None, scratch=(), flops=0, aliases={}):
    return pl.pallas_call(
        kernel,
        out_shape=out_shape,
        in_specs=in_specs,
        out_specs=jax.tree.map(lambda _: VMEM, out_shape) if out_specs is None else out_specs,
        scratch_shapes=list(scratch),
        input_output_aliases=aliases,
        compiler_params=pltpu.CompilerParams(vmem_limit_bytes=VMEM_LIMIT),
        cost_estimate=pl.CostEstimate(
            flops=flops,
            bytes_accessed=sum(a.size * a.dtype.itemsize for a in args),
            transcendentals=0,
        ),
        name=name,
    )(*args)


def open_kernel(where_ref, points_ref, first_ref, second_ref, raw_ref, sem):
    half = first_ref.shape[0]
    start = pl.multiple_of(where_ref[1] * (2 * half), 2 * half)
    copy = pltpu.make_async_copy(points_ref.at[pl.ds(start, 2 * half), :], raw_ref, sem)
    copy.start()
    copy.wait()
    first_ref[...] = raw_ref[:half, :].astype(jnp.float32)
    second_ref[...] = raw_ref[half:, :].astype(jnp.float32)


def widen(norm, width):
    if width <= norm.shape[1]:
        return norm[:, :width]
    return jnp.concatenate([norm] * (width // norm.shape[1]), axis=1)


def norms(c):
    c = c.astype(jnp.float32)
    return jnp.broadcast_to(jnp.sum(c * c, axis=1, keepdims=True), (c.shape[0], LANES))


def stats_kernel(lines, where_ref, points_hbm, c_hbm, out_ref, twice_ref, norm_ref, points_ref, c_ref, all_norm_ref, sems):
    rows, local = points_ref.shape[0], c_ref.shape[0]
    chunk = local // lines
    tile, size = min(256, rows), chunk // 4
    fetch = [pltpu.make_async_copy(points_hbm, points_ref, sems.at[lines])]
    for l in range(lines):
        part = pl.ds(l * chunk, chunk)
        fetch.append(pltpu.make_async_copy(c_hbm.at[part, :], c_ref.at[part, :], sems.at[l]))
    for copy in fetch:
        copy.start()
    fetch[0].wait()
    kept = pl.multiple_of(lax.rem(where_ref[0], 4) * size, size)
    for l in range(lines):
        fetch[1 + l].wait()
        c = c_ref[l * chunk : (l + 1) * chunk, :]
        all_norm_ref[...] = norms(c)
        twice = c + c
        mine = c_ref[pl.ds(pl.multiple_of(l * chunk + kept, size), size), :]
        twice_ref[l * size : (l + 1) * size, :] = mine + mine
        norm_ref[l * size : (l + 1) * size, :] = all_norm_ref[pl.ds(kept, size), :]
        for start in range(0, rows, tile):
            at = slice(start, start + tile)
            dots = lax.dot_general(twice, points_ref[at, :], NT, preferred_element_type=jnp.float32)
            score = dots - widen(all_norm_ref[...], tile)
            top = jnp.max(score, axis=0, keepdims=True)
            total = jnp.sum(jnp.exp(score - top), axis=0, keepdims=True)
            if l:
                old_top, old_total = out_ref[0:1, at], out_ref[1:2, at]
                new_top = jnp.maximum(old_top, top)
                total = old_total * jnp.exp(old_top - new_top) + total * jnp.exp(top - new_top)
                top = new_top
            out_ref[0:1, at] = top
            out_ref[1:2, at] = total


def stats(where, points, centroids, lines):
    rows, width = points.shape
    local = centroids.shape[0]
    return call(
        functools.partial(stats_kernel, lines),
        (
            f32(2, rows),
            jax.ShapeDtypeStruct((local // 4, width), jnp.bfloat16),
            f32(local // 4, LANES),
        ),
        [SMEM, HBM, HBM],
        (where, points, centroids),
        "stats",
        scratch=[
            pltpu.VMEM(points.shape, points.dtype),
            pltpu.VMEM(centroids.shape, centroids.dtype),
            pltpu.VMEM((local // lines, LANES), jnp.float32),
            pltpu.SemaphoreType.DMA((lines + 1,)),
        ],
        flops=4 * rows * local * width,
    )


def lse_kernel(cores, every, x0_ref, y1_ref, *refs):
    pair_refs = refs[:cores]
    lse_ref, evidence_ref, pack_x_ref, pack_y_ref = refs[cores:]
    half = lse_ref.shape[1]
    top = functools.reduce(jnp.maximum, [p[0:1, :] for p in pair_refs])
    total = functools.reduce(jnp.add, [p[1:2, :] * jnp.exp(p[0:1, :] - top) for p in pair_refs])
    lse = top + jnp.log(total)
    evidence = lse - math.log(every)
    for k in range(evidence_ref.shape[0]):
        evidence_ref[k : k + 1, :] = evidence[:, k * LANES : (k + 1) * LANES]
    for i in range(2 * cores):
        lse_ref[i : i + 1, :] = lse[:, i * half : (i + 1) * half]
    for piece_ref, pack_ref in ((x0_ref, pack_x_ref), (y1_ref, pack_y_ref)):
        pack_ref[0:half, :] = piece_ref[...]
        pack_ref[half:, :] = jnp.zeros_like(pack_ref[half:, :])
        pack_ref[half : half + 2 * cores, 0:half] = lse_ref[...]


def add_block(twice, norm, x, lse, acc_ref, cnt_ref, first):
    dots = lax.dot_general(twice, x, NT, preferred_element_type=jnp.float32)
    score = dots - widen(norm, x.shape[0])
    resp = jnp.exp(score - lse).astype(jnp.bfloat16)
    part = lax.dot_general(resp, x, NN, preferred_element_type=jnp.float32)
    wide = resp.astype(jnp.float32)
    lanes = cnt_ref.shape[1]
    counted = functools.reduce(
        jnp.add, [wide[:, k : k + lanes] for k in range(0, x.shape[0], lanes)]
    )
    if first:
        acc_ref[...] = part
        cnt_ref[...] = counted
    else:
        acc_ref[...] += part
        cnt_ref[...] += counted


def add_pieces(where_ref, twice_ref, norm_ref, pieces, acc_ref, cnt_ref):
    for x_ref, lse_ref, above, rc, part in pieces:
        at = above + 2 * (where_ref[1] ^ rc) + part
        half = acc_rows(x_ref)
        x = x_ref[0:half, :].astype(jnp.bfloat16)
        lse = lse_ref[pl.ds(at, 1), :][:, 0:half]
        add_block(twice_ref[...], norm_ref[...], x, lse, acc_ref, cnt_ref, False)


def acc_rows(ref):
    rows = ref.shape[0]
    return 1 << (rows.bit_length() - 1)


def own_kernel(cores, points_ref, twice_ref, norm_ref, lse_ref, acc_ref, cnt_ref):
    half = points_ref.shape[0] // (2 * cores)
    for i in range(2 * cores):
        x = points_ref[i * half : (i + 1) * half, :]
        add_block(twice_ref[...], norm_ref[...], x, lse_ref[i : i + 1, :], acc_ref, cnt_ref, i == 0)


def near_kernel(cores, where_ref, twice_ref, norm_ref, acc_in_ref, cnt_in_ref, d0_ref, d1_ref, *refs):
    x_refs = refs[: 2 * cores]
    acc_ref, cnt_ref = refs[2 * cores :]
    above = acc_rows(d0_ref)
    acc_ref[...] = acc_in_ref[...]
    cnt_ref[...] = cnt_in_ref[...]
    pieces = [(x_refs[rc], d1_ref, above, rc, 0) for rc in range(cores)]
    pieces += [(x_refs[cores + rc], d0_ref, above, rc, 1) for rc in range(cores)]
    add_pieces(where_ref, twice_ref, norm_ref, pieces, acc_ref, cnt_ref)


def far_kernel(cores, order, where_ref, twice_ref, norm_ref, acc_in_ref, cnt_in_ref, lse_d_ref, *refs):
    lines = len(order)
    x_refs, out_refs = refs[: 4 * cores], refs[4 * cores : 4 * cores + lines]
    acc_ref, cnt_ref = refs[4 * cores + lines :]
    d0_ref, d1_ref = x_refs[2 * cores], x_refs[3 * cores]
    above = acc_rows(d0_ref)
    acc_ref[...] = acc_in_ref[...]
    cnt_ref[...] = cnt_in_ref[...]
    whose = ((d1_ref, above, 1), (d0_ref, above, 0), (lse_d_ref, 0, 0), (lse_d_ref, 0, 1))
    pieces = [
        (x_refs[k * cores + rc], lse, top, rc, part)
        for k, (lse, top, part) in enumerate(whose)
        for rc in range(cores)
    ]
    add_pieces(where_ref, twice_ref, norm_ref, pieces, acc_ref, cnt_ref)
    line = lax.div(where_ref[0], 4)
    width = acc_ref.shape[1]
    size = acc_ref.shape[0] // lines
    for s in range(lines):
        start = pl.multiple_of(ahead(order, line, s) * size, size)
        out_refs[s][0:size, :] = acc_ref[pl.ds(start, size), :]
        turned = jnp.sum(cnt_ref[pl.ds(start, size), :].T, axis=0, keepdims=True)
        if size < width:
            turned = jnp.concatenate([turned, jnp.zeros((1, width - size), jnp.float32)], axis=1)
        out_refs[s][size : size + 8, :] = jnp.broadcast_to(turned, (8, width))


def ahead(order, line, steps):
    n = len(order)
    return functools.reduce(
        jnp.add,
        [jnp.where(line == order[p], order[(p + steps) % n], 0) for p in range(n)],
    )


def add_kernel(a_ref, b_ref, out_ref):
    out_ref[...] = a_ref[...] + b_ref[...]


def finish_kernel(where_ref, twice_ref, mine_ref, first_ref, second_ref, out_ref):
    size, width = out_ref.shape[0] - 8, out_ref.shape[1]
    start = pl.multiple_of(lax.div(where_ref[0], 4) * size, size)
    c = 0.5 * twice_ref[pl.ds(start, size), :].astype(jnp.float32)
    total = mine_ref[...] + first_ref[...] + second_ref[...]
    counts = total[size:, :]
    column = counts.T[:size, 0:1]
    out_ref[0:size, :] = (total[:size, :] + prior_mass * c) / (column + prior_mass)
    row = lax.broadcasted_iota(jnp.int32, (8, LANES), 0)
    spread = jnp.zeros((8, LANES), jnp.float32)
    for k in range(size // LANES):
        spread = jnp.where(row == k, counts[:, k * LANES : (k + 1) * LANES], spread)
    out_ref[size:, :] = jnp.concatenate([spread] * (width // LANES), axis=1)


def place_kernel(names, order, later, where_ref, *refs):
    count, lines = len(names), len(order)
    block_refs = refs[:count]
    new_ref, counts_ref, sems = refs[-3:]
    size = block_refs[0].shape[0] - 8
    plane, line = lax.rem(where_ref[0], 4), lax.div(where_ref[0], 4)
    each = size // LANES
    places = [ahead(order, line, steps) * 4 + (plane ^ bits) for bits, steps in names]
    copies = []
    for i in range(count):
        at = pl.multiple_of(places[i] * size, size)
        copies.append(
            pltpu.make_async_copy(block_refs[i].at[0:size, :], new_ref.at[pl.ds(at, size), :], sems.at[i])
        )
        copies[-1].start()
    if later:
        counts_ref[...] = refs[count][...]
    for i in range(count):
        for k in range(each):
            counts_ref[pl.ds(places[i] * each + k, 1), :] = block_refs[i][size + k : size + k + 1, 0:LANES]
    for copy in copies:
        copy.wait()


def body(n, cores, points, centroids):
    rows, width = points.shape
    local_cent = centroids.shape[0]
    lines = n // 4
    half = rows // (2 * cores)
    share = local_cent // 4
    size = share // lines
    order = tuple(range(0, lines, 2)) + tuple(range(1, lines, 2))[::-1]
    where = jnp.stack([lax.axis_index("dp"), lax.axis_index("cent")]).astype(jnp.int32)

    def flip(x, bits):
        return lax.ppermute(x, "dp", [(i, i ^ bits) for i in range(n)])

    def flip_core(x, bits):
        return lax.ppermute(x, "cent", [(i, i ^ bits) for i in range(cores)])

    def ring(x, way):
        pairs = [(order[p], order[(p + way) % lines]) for p in range(lines)]
        return lax.ppermute(x, "dp", [(4 * a + i, 4 * b + i) for a, b in pairs for i in range(4)])

    def with_siblings(pieces):
        return [a if rc == 0 else flip_core(a, rc) for a in pieces for rc in range(cores)]

    first, second = call(
        open_kernel,
        (f32(half, width), f32(half, width)),
        [SMEM, HBM],
        (where, points),
        "open",
        scratch=[pltpu.VMEM((2 * half, width), points.dtype), pltpu.SemaphoreType.DMA(())],
    )
    x0, y1 = flip(first, 1), flip(second, 2)
    x1, y0 = flip(second, 1), flip(first, 2)

    pair, twice, norm = stats(where, points, centroids, lines)
    pair, x0, y1 = lax.optimization_barrier((pair, x0, y1))
    pairs = [pair] + [flip_core(pair, rc) for rc in range(1, cores)]
    tail = max(8, 2 * cores)
    lse, log_evidence, pack_x, pack_y = call(
        functools.partial(lse_kernel, cores, local_cent * cores),
        (f32(2 * cores, half), f32(rows // LANES, LANES), f32(half + tail, width), f32(half + tail, width)),
        [VMEM] * (2 + cores),
        (x0, y1, *pairs),
        "lse",
    )
    d0, d1, lse_d = flip(pack_x, 2), flip(pack_y, 1), flip(lse, 3)

    acc_shape, cnt_shape = f32(share, width), f32(share, min(LANES, half))
    acc, cnt = call(
        functools.partial(own_kernel, cores),
        (acc_shape, cnt_shape),
        [VMEM] * 4,
        (points, twice, norm, lse),
        "own",
        flops=4 * share * width * rows,
    )
    early = with_siblings((x0, y1))
    early, late, acc, cnt, lse_d = lax.optimization_barrier(
        (early, (x1, y0, d0, d1), acc, cnt, lse_d)
    )
    _, _, d0, d1 = late
    late = with_siblings(late)
    acc, cnt = call(
        functools.partial(near_kernel, cores),
        (acc_shape, cnt_shape),
        [SMEM] + [VMEM] * (6 + 2 * cores),
        (where, twice, norm, acc, cnt, d0, d1, *early),
        "near",
        flops=4 * share * width * rows,
        aliases={3: 0, 4: 1},
    )
    sums = call(
        functools.partial(far_kernel, cores, order),
        [f32(size + 8, width)] * lines,
        [SMEM] + [VMEM] * (5 + 4 * cores),
        (where, twice, norm, acc, cnt, lse_d, *late),
        "far",
        scratch=[
            pltpu.VMEM((share, width), jnp.float32),
            pltpu.VMEM((share, min(LANES, half)), jnp.float32),
        ],
        flops=4 * share * width * 2 * rows,
    )

    def reduced(way, steps):
        moving = sums[way * steps % lines]
        for s in range(steps, 0, -1):
            moving = ring(moving, way)
            if s > 1:
                mine = sums[way * (s - 1) % lines]
                moving = call(add_kernel, f32(size + 8, width), [VMEM] * 2, (mine, moving), "add")
        return moving

    done = call(
        finish_kernel,
        f32(size + 8, width),
        [SMEM] + [VMEM] * 4,
        (where, twice, sums[0], reduced(1, lines // 2), reduced(-1, lines // 2 - 1)),
        "finish",
    )

    got = {(0, 0): done}
    got[0, -1], got[1, 0], got[2, 0] = lax.optimization_barrier(
        (ring(done, 1), flip(done, 1), flip(done, 2))
    )
    got[3, 0] = flip(got[1, 0], 2)
    for s in range(2, lines // 2 + 1):
        got[0, -s] = ring(got[0, 1 - s], 1)
    for s in range(1, lines // 2):
        got[0, s] = ring(got[0, s - 1], -1)
    steps = sorted((s for b, s in got if b == 0 and s), key=lambda s: (abs(s), s))
    for s in steps:
        got[1, s] = flip(got[0, s], 1)
        got[2, s] = flip(got[0, s], 2)
    for s in steps:
        if abs(s) == 1:
            got[3, s] = ring(got[3, 0], -s)
        else:
            got[3, s] = flip(got[2, s], 1)
    last = [(3, 1), (2, 1), (3, -lines // 2), (1, -lines // 2), (3, -1)]
    groups = ([k for k in got if k not in last], last)
    new = counts = None
    for later, names in enumerate(groups):
        args = [where] + [got[k] for k in names]
        if later:
            args += [counts, new]
        new, counts = call(
            functools.partial(place_kernel, names, order, later),
            (f32(local_cent, width), f32(local_cent // LANES, LANES)),
            [SMEM] + [VMEM] * len(names) + [VMEM, ANY][: 2 * later],
            args,
            "place_late" if later else "place_early",
            out_specs=(ANY, VMEM),
            scratch=[pltpu.SemaphoreType.DMA((len(names),))],
            aliases={len(args) - 1: 0} if later else {},
        )
    return new, counts.reshape(-1), log_evidence.reshape(-1)


def solution(mesh):
    n, cores = mesh.shape["dp"], mesh.shape["cent"]
    return jax.shard_map(
        functools.partial(body, n, cores),
        mesh=mesh,
        in_specs=(P("dp", None), P("cent", None)),
        out_specs=(P("cent", None), P("cent"), P("dp")),
        check_vma=False,
    )
```

time: 167 us -> 109 us (0.65)
  waiting for transfers between devices: 103 us -> 51.4 us
  between operations: 14.2 us -> 0.76 us
  starting transfers between devices: 22.1 us -> 34.1 us
  local copies, waits for them, and re-layouts: 10.5 us -> 2.64 us
  Pallas kernels: 16.4 us -> 20.3 us
    all_gather x1 -> x0, waiting for transfers between devices: 77.4 us -> none  [body(): gathered = lax.all_gather(done, 'dp', axis=0)]
    ppermute x9 -> x17, waiting for transfers between devices: 9.78 us -> 28 us  [flip(): return lax.ppermute(x, 'dp', [(i, i ^ bits) for i in range(n)])]
    ppermute x9 -> x17, starting transfers between devices: 11.4 us -> 19.8 us  [flip(): return lax.ppermute(x, 'dp', [(i, i ^ bits) for i in range(n)])]
    ppermute x3 -> x8, waiting for transfers between devices: 15.3 us -> 22.2 us  [ring(): lax.ppermute(x, 'dp', [(4 * a + i, 4 * b + i) for a, b in pairs for i in...]
    slice x4 -> x0, local copies, waits for them, and re-layouts: 6.16 us -> none  [the longest x1 4.6 us: body(): new = gathered[:, :size, :].reshape(local_cent, width)]
    pallas_call x8 -> x10, Pallas kernels: 16.4 us -> 20.3 us  [call(): pl.pallas_call(kernel, out_shape=out_shape, in_specs=in_specs, out_specs=...]
    ppermute x3 -> x8, starting transfers between devices: 9.51 us -> 12.8 us  [ring(): lax.ppermute(x, 'dp', [(4 * a + i, 4 * b + i) for a, b in pairs for i in...]
    unnamed x12 -> x6, local copies, waits for them, and re-layouts: 4.25 us -> 2.64 us
  transfers between devices with their start and end apart: 20 -> 32, of which waited for: 9 -> 17; matrix products, arithmetic and copies ran while one was open for 0% -> 0% of each run, Pallas kernels for 6% -> 12%
where the time goes in v5:
time: 109 us
  waiting for transfers between devices  51.4 us (47%)
  starting transfers between devices  34.1 us (31%)
  Pallas kernels  20.3 us (19%)
  local copies, waits for them, and re-layouts  2.64 us (2%)
    ppermute x17, waiting for transfers between devices, flip(): return lax.ppermute(x, 'dp', [(i, i ^ bits) for i in range(n)])  28 us
    ppermute x8, waiting for transfers between devices, ring(): lax.ppermute(x, 'dp', [(4 * a + i, 4 * b + i) for a, b in pairs for i in...  22.2 us
    pallas_call x10, Pallas kernels, call(): pl.pallas_call(kernel, out_shape=out_shape, in_specs=in_specs, out_specs=...  20.3 us
    ppermute x17, starting transfers between devices, flip(): return lax.ppermute(x, 'dp', [(i, i ^ bits) for i in range(n)])  19.8 us
    ppermute x8, starting transfers between devices, ring(): lax.ppermute(x, 'dp', [(4 * a + i, 4 * b + i) for a, b in pairs for i in...  12.8 us
    unnamed x6, local copies, waits for them, and re-layouts  2.64 us
  transfers between devices with their start and end apart: 32, of which 17 were waited for; matrix products, arithmetic and copies ran while one was open for 0% of the time, Pallas kernels for 12%

profile of v5, /device:TPU:0, one launch (start us, length us, event | category | flops | bytes accessed | tf_op | source)
XLA Modules:
  0.0 109.2 jit_solution(3254421579307662135)
XLA Ops:
  0.7 1.0 copy-done
  1.8 0.6 open.1
  2.4 3.0 %collective-permute-start.5 = (f32[256,256]{1,0:T(8,128)S(1)}, f32[256,256]{1,0:T(8,128)S(1)}, u32[]{:S(2)}, u32[]{:S(2)}) collective-permute-start(f32[256,256]{1,0:T(8,128)S(1)} %get-tuple-element.44), channel_id=1, source_target_pairs={{0,4},{2,6},{4,0},{6,2},{8,12},{10,14},{12,8},{14,10},{16,20},{18,... | collective-permute-start | bytes 786440 | tf_op jit(solution)/shard_map/ppermute | solution.py:280
  5.4 1.5 %collective-permute-start = (f32[256,256]{1,0:T(8,128)S(1)}, f32[256,256]{1,0:T(8,128)S(1)}, u32[]{:S(2)}, u32[]{:S(2)}) collective-permute-start(f32[256,256]{1,0:T(8,128)S(1)} %get-tuple-element.44), channel_id=1, source_target_pairs={{0,2},{2,0},{4,6},{6,4},{8,10},{10,8},{12,14},{14,12},{16,18},{18,... | collective-permute-start | bytes 786440 | tf_op jit(solution)/shard_map/ppermute | solution.py:280
  6.9 0.5 collective-permute-start.4
  7.5 1.6 %copy-done.2 = bf16[4096,256]{1,0:T(8,128)(2,1)S(1)} copy-done((bf16[4096,256]{1,0:T(8,128)(2,1)S(1)}, bf16[4096,256]{1,0:T(8,128)(2,1)}, u32[]{:S(2)}) %copy-start.2) | copy-done | bytes 2097176
  9.1 6.3 %stats.1 = (f32[2,1024]{1,0:T(2,128)S(1)}, bf16[1024,256]{1,0:T(8,128)(2,1)S(1)}, f32[1024,128]{1,0:T(8,128)S(1)}) custom-call(s32[2]{0:T(128)S(1)} %pad_add_fusion.where_ref, bf16[1024,256]{1,0:T(8,128)(2,1)S(1)} %copy-done, bf16[4096,256]{1,0:T(8,128)(2,1)S(1)} %copy-done.2), custom_call_target="tpu_custom_call" | custom-call | flops 4294967296 | bytes 2621448 | tf_op jit(solution)/shard_map/stats/pallas_call | solution.py:27
  15.4 1.9 %collective-permute-done.1.y1_ref.refs_2_ = f32[256,256]{1,0:T(8,128)S(1)} collective-permute-done((f32[256,256]{1,0:T(8,128)S(1)}, f32[256,256]{1,0:T(8,128)S(1)}, u32[]{:S(2)}, u32[]{:S(2)}) %collective-permute-start.1) | collective-permute-done | bytes 262176 | tf_op jit(solution)/shard_map/ppermute | solution.py:280
  17.3 1.2 %collective-permute-done.6.refs_1_ = f32[2,1024]{1,0:T(2,128)S(1)} collective-permute-done((f32[2,1024]{1,0:T(2,128)S(1)}, f32[2,1024]{1,0:T(2,128)S(1)}, u32[]{:S(2)}, u32[]{:S(2)}) %collective-permute-start.6) | collective-permute-done | bytes 8224 | tf_op jit(solution)/shard_map/ppermute | solution.py:283
  18.5 0.6 lse.1
  19.1 1.7 %collective-permute-start.7 = (f32[264,256]{1,0:T(8,128)S(1)}, f32[264,256]{1,0:T(8,128)S(1)}, u32[]{:S(2)}, u32[]{:S(2)}) collective-permute-start(f32[264,256]{1,0:T(8,128)S(1)} %get-tuple-element.49), channel_id=1, source_target_pairs={{0,4},{2,6},{4,0},{6,2},{8,12},{10,14},{12,8},{14,10},{16,20},{18,... | collective-permute-start | bytes 811016 | tf_op jit(solution)/shard_map/ppermute | solution.py:280
  20.9 1.5 %collective-permute-start.8 = (f32[264,256]{1,0:T(8,128)S(1)}, f32[264,256]{1,0:T(8,128)S(1)}, u32[]{:S(2)}, u32[]{:S(2)}) collective-permute-start(f32[264,256]{1,0:T(8,128)S(1)} %get-tuple-element.50), channel_id=1, source_target_pairs={{0,2},{2,0},{4,6},{6,4},{8,10},{10,8},{12,14},{14,12},{16,18},{18,... | collective-permute-start | bytes 811016 | tf_op jit(solution)/shard_map/ppermute | solution.py:280
  22.4 0.5 collective-permute-start.3
  23.1 1.6 %own.1 = (f32[1024,256]{1,0:T(8,128)S(1)}, f32[1024,128]{1,0:T(8,128)S(1)}) custom-call(bf16[1024,256]{1,0:T(8,128)(2,1)S(1)} %copy-done.1, bf16[1024,256]{1,0:T(8,128)(2,1)S(1)} %get-tuple-element.41.twice_ref, f32[1024,128]{1,0:T(8,128)S(1)} %get-tuple-element.42.norm_ref, f32[4,256]{1,0:T(4,128)S(1)} %get-tuple-element.51.lse_ref), custom_call_target="tpu_custom_call" | custom-call | flops 1073741824 | bytes 1576960 | tf_op jit(solution)/shard_map/own/pallas_call | solution.py:27
  24.7 4.2 %collective-permute-done.9.lse_d_ref = f32[4,256]{1,0:T(4,128)S(1)} collective-permute-done((f32[4,256]{1,0:T(4,128)S(1)}, f32[4,256]{1,0:T(4,128)S(1)}, u32[]{:S(2)}, u32[]{:S(2)}) %collective-permute-start.9) | collective-permute-done | bytes 4128 | tf_op jit(solution)/shard_map/ppermute | solution.py:280
  29.2 0.5 collective-permute-start.13
  30.2 2.4 %near.1 = (f32[1024,256]{1,0:T(8,128)S(1)}, f32[1024,128]{1,0:T(8,128)S(1)}) custom-call(s32[2]{0:T(128)S(1)} %pad_add_fusion.where_ref, bf16[1024,256]{1,0:T(8,128)(2,1)S(1)} %get-tuple-element.41.twice_ref, f32[1024,128]{1,0:T(8,128)S(1)} %get-tuple-element.42.norm_ref, ...), custom_call_target="tpu_custom_call", output_to_operand_aliasing={{0}: (3, {}), {1}: (4, {})} | custom-call | flops 1073741824 | bytes 4210696 | tf_op jit(solution)/shard_map/near/pallas_call | solution.py:27
  32.6 3.5 %far.1 = (f32[264,256]{1,0:T(8,128)S(1)}, f32[264,256]{1,0:T(8,128)S(1)}, f32[264,256]{1,0:T(8,128)S(1)}, f32[264,256]{1,0:T(8,128)S(1)}) custom-call(s32[2]{0:T(128)S(1)} %pad_add_fusion.where_ref, bf16[1024,256]{1,0:T(8,128)(2,1)S(1)} %get-tuple-element.41.twice_ref, f32[1024,128]{1,0:T(8,128)S(1)} %get-tuple-element.42.norm_ref, ...), custom_call_target="tpu_custom_call" | custom-call | flops 2147483648 | bytes 4755464 | tf_op jit(solution)/shard_map/far/pallas_call | solution.py:27
  36.1 2.7 %collective-permute-start.14 = (f32[264,256]{1,0:T(8,128)S(1)}, f32[264,256]{1,0:T(8,128)S(1)}, u32[]{:S(2)}, u32[]{:S(2)}) collective-permute-start(f32[264,256]{1,0:T(8,128)S(1)} %get-tuple-element.69), channel_id=1, source_target_pairs={{0,16},{2,18},{4,20},{6,22},{16,24},{18,26},{20,28},{22,30},{24,8}... | collective-permute-start | bytes 811016 | tf_op jit(solution)/shard_map/ppermute | solution.py:287
  38.9 6.9 %collective-permute-done.14.b_ref = f32[264,256]{1,0:T(8,128)S(1)} collective-permute-done((f32[264,256]{1,0:T(8,128)S(1)}, f32[264,256]{1,0:T(8,128)S(1)}, u32[]{:S(2)}, u32[]{:S(2)}) %collective-permute-start.14) | collective-permute-done | bytes 270368 | tf_op jit(solution)/shard_map/ppermute | solution.py:287
  45.8 3.4 %collective-permute-start.15 = (f32[264,256]{1,0:T(8,128)S(1)}, f32[264,256]{1,0:T(8,128)S(1)}, u32[]{:S(2)}, u32[]{:S(2)}) collective-permute-start(f32[264,256]{1,0:T(8,128)S(1)} %add.3), channel_id=1, source_target_pairs={{0,16},{2,18},{4,20},{6,22},{16,24},{18,26},{20,28},{22,30},{24,8}... | collective-permute-start | bytes 811016 | tf_op jit(solution)/shard_map/ppermute | solution.py:287
  49.2 4.1 %collective-permute-done.16.second_ref = f32[264,256]{1,0:T(8,128)S(1)} collective-permute-done((f32[264,256]{1,0:T(8,128)S(1)}, f32[264,256]{1,0:T(8,128)S(1)}, u32[]{:S(2)}, u32[]{:S(2)}) %collective-permute-start.16) | collective-permute-done | bytes 270368 | tf_op jit(solution)/shard_map/ppermute | solution.py:287
  53.4 4.8 %collective-permute-done.15.first_ref = f32[264,256]{1,0:T(8,128)S(1)} collective-permute-done((f32[264,256]{1,0:T(8,128)S(1)}, f32[264,256]{1,0:T(8,128)S(1)}, u32[]{:S(2)}, u32[]{:S(2)}) %collective-permute-start.15) | collective-permute-done | bytes 270368 | tf_op jit(solution)/shard_map/ppermute | solution.py:287
  58.2 0.8 finish.1.refs_0_
  59.0 1.6 %collective-permute-start.19 = (f32[264,256]{1,0:T(8,128)S(1)}, f32[264,256]{1,0:T(8,128)S(1)}, u32[]{:S(2)}, u32[]{:S(2)}) collective-permute-start(f32[264,256]{1,0:T(8,128)S(1)} %finish.1.refs_0_), channel_id=1, source_target_pairs={{0,4},{2,6},{4,0},{6,2},{8,12},{10,14},{12,8},{14,10},{16,20},{18,... | collective-permute-start | bytes 811016 | tf_op jit(solution)/shard_map/ppermute | solution.py:280
  60.6 1.5 %collective-permute-start.18 = (f32[264,256]{1,0:T(8,128)S(1)}, f32[264,256]{1,0:T(8,128)S(1)}, u32[]{:S(2)}, u32[]{:S(2)}) collective-permute-start(f32[264,256]{1,0:T(8,128)S(1)} %finish.1.refs_0_), channel_id=1, source_target_pairs={{0,2},{2,0},{4,6},{6,4},{8,10},{10,8},{12,14},{14,12},{16,18},{18,... | collective-permute-start | bytes 811016 | tf_op jit(solution)/shard_map/ppermute | solution.py:280
  62.0 1.7 %collective-permute-start.17 = (f32[264,256]{1,0:T(8,128)S(1)}, f32[264,256]{1,0:T(8,128)S(1)}, u32[]{:S(2)}, u32[]{:S(2)}) collective-permute-start(f32[264,256]{1,0:T(8,128)S(1)} %finish.1.refs_0_), channel_id=1, source_target_pairs={{0,16},{2,18},{4,20},{6,22},{16,24},{18,26},{20,28},{22,30},{24,8}... | collective-permute-start | bytes 811016 | tf_op jit(solution)/shard_map/ppermute | solution.py:287
  64.1 3.3 %collective-permute-done.19.refs_3_ = f32[264,256]{1,0:T(8,128)S(1)} collective-permute-done((f32[264,256]{1,0:T(8,128)S(1)}, f32[264,256]{1,0:T(8,128)S(1)}, u32[]{:S(2)}, u32[]{:S(2)}) %collective-permute-start.19) | collective-permute-done | bytes 270368 | tf_op jit(solution)/shard_map/ppermute | solution.py:280
  67.4 1.2 %collective-permute-done.18.refs_2_ = f32[264,256]{1,0:T(8,128)S(1)} collective-permute-done((f32[264,256]{1,0:T(8,128)S(1)}, f32[264,256]{1,0:T(8,128)S(1)}, u32[]{:S(2)}, u32[]{:S(2)}) %collective-permute-start.18) | collective-permute-done | bytes 270368 | tf_op jit(solution)/shard_map/ppermute | solution.py:280
  68.6 2.2 %collective-permute-done.17.refs_1_ = f32[264,256]{1,0:T(8,128)S(1)} collective-permute-done((f32[264,256]{1,0:T(8,128)S(1)}, f32[264,256]{1,0:T(8,128)S(1)}, u32[]{:S(2)}, u32[]{:S(2)}) %collective-permute-start.17) | collective-permute-done | bytes 270368 | tf_op jit(solution)/shard_map/ppermute | solution.py:287
  70.8 3.3 %collective-permute-start.24 = (f32[264,256]{1,0:T(8,128)S(1)}, f32[264,256]{1,0:T(8,128)S(1)}, u32[]{:S(2)}, u32[]{:S(2)}) collective-permute-start(f32[264,256]{1,0:T(8,128)S(1)} %collective-permute-done.17.refs_1_), channel_id=1, source_target_pairs={{0,16},{2,18},{4,20},{6,22},{16,24},{18,26},{20,28},{22,30},{24,8}... | collective-permute-start | bytes 811016 | tf_op jit(solution)/shard_map/ppermute | solution.py:287
  74.1 4.2 %collective-permute-done.22.refs_6_ = f32[264,256]{1,0:T(8,128)S(1)} collective-permute-done((f32[264,256]{1,0:T(8,128)S(1)}, f32[264,256]{1,0:T(8,128)S(1)}, u32[]{:S(2)}, u32[]{:S(2)}) %collective-permute-start.22) | collective-permute-done | bytes 270368 | tf_op jit(solution)/shard_map/ppermute | solution.py:287
  78.3 0.5 collective-permute-start.31
  78.9 0.5 collective-permute-start.20
  79.4 1.5 %collective-permute-start.30 = (f32[264,256]{1,0:T(8,128)S(1)}, f32[264,256]{1,0:T(8,128)S(1)}, u32[]{:S(2)}, u32[]{:S(2)}) collective-permute-start(f32[264,256]{1,0:T(8,128)S(1)} %collective-permute-done.17.refs_1_), channel_id=1, source_target_pairs={{0,4},{2,6},{4,0},{6,2},{8,12},{10,14},{12,8},{14,10},{16,20},{18,... | collective-permute-start | bytes 811016 | tf_op jit(solution)/shard_map/ppermute | solution.py:280
  80.9 1.5 %collective-permute-start.29 = (f32[264,256]{1,0:T(8,128)S(1)}, f32[264,256]{1,0:T(8,128)S(1)}, u32[]{:S(2)}, u32[]{:S(2)}) collective-permute-start(f32[264,256]{1,0:T(8,128)S(1)} %collective-permute-done.17.refs_1_), channel_id=1, source_target_pairs={{0,2},{2,0},{4,6},{6,4},{8,10},{10,8},{12,14},{14,12},{16,18},{18,... | collective-permute-start | bytes 811016 | tf_op jit(solution)/shard_map/ppermute | solution.py:280
  82.4 0.5 collective-permute-start.25
  82.9 4.8 %collective-permute-done.31.refs_9_ = f32[264,256]{1,0:T(8,128)S(1)} collective-permute-done((f32[264,256]{1,0:T(8,128)S(1)}, f32[264,256]{1,0:T(8,128)S(1)}, u32[]{:S(2)}, u32[]{:S(2)}) %collective-permute-start.31) | collective-permute-done | bytes 270368 | tf_op jit(solution)/shard_map/ppermute | solution.py:280
  88.2 0.6 collective-permute-start.28
  88.8 5.2 %collective-permute-done.30.refs_8_ = f32[264,256]{1,0:T(8,128)S(1)} collective-permute-done((f32[264,256]{1,0:T(8,128)S(1)}, f32[264,256]{1,0:T(8,128)S(1)}, u32[]{:S(2)}, u32[]{:S(2)}) %collective-permute-start.30) | collective-permute-done | bytes 270368 | tf_op jit(solution)/shard_map/ppermute | solution.py:280
  94.0 0.7 collective-permute-start.21
  94.7 1.5 %collective-permute-start.27 = (f32[264,256]{1,0:T(8,128)S(1)}, f32[264,256]{1,0:T(8,128)S(1)}, u32[]{:S(2)}, u32[]{:S(2)}) collective-permute-start(f32[264,256]{1,0:T(8,128)S(1)} %collective-permute-done.24.refs_5_), channel_id=1, source_target_pairs={{0,2},{2,0},{4,6},{6,4},{8,10},{10,8},{12,14},{14,12},{16,18},{18,... | collective-permute-start | bytes 811016 | tf_op jit(solution)/shard_map/ppermute | solution.py:280
  96.2 3.6 %collective-permute-done.25.refs_10_ = f32[264,256]{1,0:T(8,128)S(1)} collective-permute-done((f32[264,256]{1,0:T(8,128)S(1)}, f32[264,256]{1,0:T(8,128)S(1)}, u32[]{:S(2)}, u32[]{:S(2)}) %collective-permute-start.25) | collective-permute-done | bytes 270368 | tf_op jit(solution)/shard_map/ppermute | solution.py:280
  99.8 1.5 %collective-permute-start.26 = (f32[264,256]{1,0:T(8,128)S(1)}, f32[264,256]{1,0:T(8,128)S(1)}, u32[]{:S(2)}, u32[]{:S(2)}) collective-permute-start(f32[264,256]{1,0:T(8,128)S(1)} %collective-permute-done.25.refs_10_), channel_id=1, source_target_pairs={{0,2},{2,0},{4,6},{6,4},{8,10},{10,8},{12,14},{14,12},{16,18},{18,... | collective-permute-start | bytes 811016 | tf_op jit(solution)/shard_map/ppermute | solution.py:280
  101.3 2.2 %place_early.1 = (f32[4096,256]{1,0:T(8,128)}, f32[32,128]{1,0:T(8,128)S(1)}) custom-call(s32[2]{0:T(128)S(1)} %pad_add_fusion.where_ref, f32[264,256]{1,0:T(8,128)S(1)} %finish.1.refs_0_, f32[264,256]{1,0:T(8,128)S(1)} %collective-permute-done.17.refs_1_, f32[264,256]{1,0:T(8,128)S(1)} %collective-permute-done.18.refs_2_, ...), custom_call_target="tpu_custom_call" | custom-call | bytes 2973704 | tf_op jit(solution)/shard_map/place_early/pallas_call | solution.py:27
  103.6 0.7 collective-permute-done.23.refs_1_
  104.3 2.7 %collective-permute-done.26.refs_2_ = f32[264,256]{1,0:T(8,128)S(1)} collective-permute-done((f32[264,256]{1,0:T(8,128)S(1)}, f32[264,256]{1,0:T(8,128)S(1)}, u32[]{:S(2)}, u32[]{:S(2)}) %collective-permute-start.26) | collective-permute-done | bytes 270368 | tf_op jit(solution)/shard_map/ppermute | solution.py:280
  107.0 2.2 %place_late.1 = (f32[4096,256]{1,0:T(8,128)}, f32[32,128]{1,0:T(8,128)}) custom-call(s32[2]{0:T(128)S(1)} %pad_add_fusion.where_ref, f32[264,256]{1,0:T(8,128)S(1)} %collective-permute-done.21.refs_0_, f32[264,256]{1,0:T(8,128)S(1)} %collective-permute-done.23.refs_1_, ...), custom_call_target="tpu_custom_call", output_to_operand_aliasing={{0}: (7, {})} | custom-call | bytes 5562376 | tf_op jit(solution)/shard_map/place_late/pallas_call | solution.py:27
  (33 shorter events, 2.1 us)
Async XLA Ops:
  0.7 1.0 copy-start
  2.4 20.0 %collective-permute-start.5 = (f32[256,256]{1,0:T(8,128)S(1)}, f32[256,256]{1,0:T(8,128)S(1)}, u32[]{:S(2)}, u32[]{:S(2)}) collective-permute-start(f32[256,256]{1,0:T(8,128)S(1)} %get-tuple-element.44), channel_id=1, source_target_pairs={{0,4},{2,6},{4,0},{6,2},{8,12},{10,14},{12,8},{14,10},{16,20},{18,... | collective-permute-start | bytes 786440 | tf_op jit(solution)/shard_map/ppermute | solution.py:280
  5.4 10.0 %collective-permute-start = (f32[256,256]{1,0:T(8,128)S(1)}, f32[256,256]{1,0:T(8,128)S(1)}, u32[]{:S(2)}, u32[]{:S(2)}) collective-permute-start(f32[256,256]{1,0:T(8,128)S(1)} %get-tuple-element.44), channel_id=1, source_target_pairs={{0,2},{2,0},{4,6},{6,4},{8,10},{10,8},{12,14},{14,12},{16,18},{18,... | collective-permute-start | bytes 786440 | tf_op jit(solution)/shard_map/ppermute | solution.py:280
  6.9 16.2 %copy-start.1 = (bf16[1024,256]{1,0:T(8,128)(2,1)S(1)}, bf16[1024,256]{1,0:T(8,128)(2,1)}, u32[]{:S(2)}) copy-start(bf16[1024,256]{1,0:T(8,128)(2,1)} %points_ref.3) | copy-start | bytes 1572868
  6.9 16.0 %collective-permute-start.4 = (f32[256,256]{1,0:T(8,128)S(1)}, f32[256,256]{1,0:T(8,128)S(1)}, u32[]{:S(2)}, u32[]{:S(2)}) collective-permute-start(f32[256,256]{1,0:T(8,128)S(1)} %get-tuple-element.45), channel_id=1, source_target_pairs={{0,2},{2,0},{4,6},{6,4},{8,10},{10,8},{12,14},{14,12},{16,18},{18,... | collective-permute-start | bytes 786440 | tf_op jit(solution)/shard_map/ppermute | solution.py:280
  7.4 9.9 %collective-permute-start.1 = (f32[256,256]{1,0:T(8,128)S(1)}, f32[256,256]{1,0:T(8,128)S(1)}, u32[]{:S(2)}, u32[]{:S(2)}) collective-permute-start(f32[256,256]{1,0:T(8,128)S(1)} %get-tuple-element.45), channel_id=1, source_target_pairs={{0,4},{2,6},{4,0},{6,2},{8,12},{10,14},{12,8},{14,10},{16,20},{18,... | collective-permute-start | bytes 786440 | tf_op jit(solution)/shard_map/ppermute | solution.py:280
  7.5 1.6 %copy-start.2 = (bf16[4096,256]{1,0:T(8,128)(2,1)S(1)}, bf16[4096,256]{1,0:T(8,128)(2,1)}, u32[]{:S(2)}) copy-start(bf16[4096,256]{1,0:T(8,128)(2,1)} %c_hbm.1) | copy-start | bytes 6291460
  17.3 1.2 %collective-permute-start.6 = (f32[2,1024]{1,0:T(2,128)S(1)}, f32[2,1024]{1,0:T(2,128)S(1)}, u32[]{:S(2)}, u32[]{:S(2)}) collective-permute-start(f32[2,1024]{1,0:T(2,128)S(1)} %get-tuple-element.48.refs_0_), channel_id=1, source_target_pairs={{0,1},{1,0},{2,3},{3,2},{4,5},{5,4},{6,7},{7,6},{8,9},{9,8},{10,11... | collective-permute-start | bytes 24584 | tf_op jit(solution)/shard_map/ppermute | solution.py:283
  19.1 9.8 %collective-permute-start.7 = (f32[264,256]{1,0:T(8,128)S(1)}, f32[264,256]{1,0:T(8,128)S(1)}, u32[]{:S(2)}, u32[]{:S(2)}) collective-permute-start(f32[264,256]{1,0:T(8,128)S(1)} %get-tuple-element.49), channel_id=1, source_target_pairs={{0,4},{2,6},{4,0},{6,2},{8,12},{10,14},{12,8},{14,10},{16,20},{18,... | collective-permute-start | bytes 811016 | tf_op jit(solution)/shard_map/ppermute | solution.py:280
  20.9 8.3 %collective-permute-start.8 = (f32[264,256]{1,0:T(8,128)S(1)}, f32[264,256]{1,0:T(8,128)S(1)}, u32[]{:S(2)}, u32[]{:S(2)}) collective-permute-start(f32[264,256]{1,0:T(8,128)S(1)} %get-tuple-element.50), channel_id=1, source_target_pairs={{0,2},{2,0},{4,6},{6,4},{8,10},{10,8},{12,14},{14,12},{16,18},{18,... | collective-permute-start | bytes 811016 | tf_op jit(solution)/shard_map/ppermute | solution.py:280
  22.4 6.6 %collective-permute-start.2 = (f32[256,256]{1,0:T(8,128)S(1)}, f32[256,256]{1,0:T(8,128)S(1)}, u32[]{:S(2)}, u32[]{:S(2)}) collective-permute-start(f32[256,256]{1,0:T(8,128)S(1)} %collective-permute-done.x0_ref.refs_0_), channel_id=1, source_target_pairs={{0,1},{1,0},{2,3},{3,2},{4,5},{5,4},{6,7},{7,6},{8,9},{9,8},{10,11... | collective-permute-start | bytes 786440 | tf_op jit(solution)/shard_map/ppermute | solution.py:283
  22.4 6.6 %collective-permute-start.3 = (f32[256,256]{1,0:T(8,128)S(1)}, f32[256,256]{1,0:T(8,128)S(1)}, u32[]{:S(2)}, u32[]{:S(2)}) collective-permute-start(f32[256,256]{1,0:T(8,128)S(1)} %collective-permute-done.1.y1_ref.refs_2_), channel_id=1, source_target_pairs={{0,1},{1,0},{2,3},{3,2},{4,5},{5,4},{6,7},{7,6},{8,9},{9,8},{10,11... | collective-permute-start | bytes 786440 | tf_op jit(solution)/shard_map/ppermute | solution.py:283
  22.9 6.1 %collective-permute-start.9 = (f32[4,256]{1,0:T(4,128)S(1)}, f32[4,256]{1,0:T(4,128)S(1)}, u32[]{:S(2)}, u32[]{:S(2)}) collective-permute-start(f32[4,256]{1,0:T(4,128)S(1)} %get-tuple-element.51.lse_ref), channel_id=1, source_target_pairs={{0,6},{2,4},{4,2},{6,0},{8,14},{10,12},{12,10},{14,8},{16,22},{18,... | collective-permute-start | bytes 12296 | tf_op jit(solution)/shard_map/ppermute | solution.py:280
  29.2 3.4 %collective-permute-start.12 = (f32[264,256]{1,0:T(8,128)S(1)}, f32[264,256]{1,0:T(8,128)S(1)}, u32[]{:S(2)}, u32[]{:S(2)}) collective-permute-start(f32[264,256]{1,0:T(8,128)S(1)} %collective-permute-done.7.d0_ref.refs_4_), channel_id=1, source_target_pairs={{0,1},{1,0},{2,3},{3,2},{4,5},{5,4},{6,7},{7,6},{8,9},{9,8},{10,11... | collective-permute-start | bytes 811016 | tf_op jit(solution)/shard_map/ppermute | solution.py:283
  29.2 3.4 %collective-permute-start.13 = (f32[264,256]{1,0:T(8,128)S(1)}, f32[264,256]{1,0:T(8,128)S(1)}, u32[]{:S(2)}, u32[]{:S(2)}) collective-permute-start(f32[264,256]{1,0:T(8,128)S(1)} %collective-permute-done.8.d1_ref.refs_6_), channel_id=1, source_target_pairs={{0,1},{1,0},{2,3},{3,2},{4,5},{5,4},{6,7},{7,6},{8,9},{9,8},{10,11... | collective-permute-start | bytes 811016 | tf_op jit(solution)/shard_map/ppermute | solution.py:283
  29.7 2.9 %collective-permute-start.10 = (f32[256,256]{1,0:T(8,128)S(1)}, f32[256,256]{1,0:T(8,128)S(1)}, u32[]{:S(2)}, u32[]{:S(2)}) collective-permute-start(f32[256,256]{1,0:T(8,128)S(1)} %collective-permute-done.4.refs_0_), channel_id=1, source_target_pairs={{0,1},{1,0},{2,3},{3,2},{4,5},{5,4},{6,7},{7,6},{8,9},{9,8},{10,11... | collective-permute-start | bytes 786440 | tf_op jit(solution)/shard_map/ppermute | solution.py:283
  29.7 2.9 %collective-permute-start.11 = (f32[256,256]{1,0:T(8,128)S(1)}, f32[256,256]{1,0:T(8,128)S(1)}, u32[]{:S(2)}, u32[]{:S(2)}) collective-permute-start(f32[256,256]{1,0:T(8,128)S(1)} %collective-permute-done.5.refs_2_), channel_id=1, source_target_pairs={{0,1},{1,0},{2,3},{3,2},{4,5},{5,4},{6,7},{7,6},{8,9},{9,8},{10,11... | collective-permute-start | bytes 786440 | tf_op jit(solution)/shard_map/ppermute | solution.py:283
  36.1 9.6 %collective-permute-start.14 = (f32[264,256]{1,0:T(8,128)S(1)}, f32[264,256]{1,0:T(8,128)S(1)}, u32[]{:S(2)}, u32[]{:S(2)}) collective-permute-start(f32[264,256]{1,0:T(8,128)S(1)} %get-tuple-element.69), channel_id=1, source_target_pairs={{0,16},{2,18},{4,20},{6,22},{16,24},{18,26},{20,28},{22,30},{24,8}... | collective-permute-start | bytes 811016 | tf_op jit(solution)/shard_map/ppermute | solution.py:287
  38.9 14.5 %collective-permute-start.16 = (f32[264,256]{1,0:T(8,128)S(1)}, f32[264,256]{1,0:T(8,128)S(1)}, u32[]{:S(2)}, u32[]{:S(2)}) collective-permute-start(f32[264,256]{1,0:T(8,128)S(1)} %get-tuple-element.70), channel_id=1, source_target_pairs={{0,8},{2,10},{4,12},{6,14},{16,0},{18,2},{20,4},{22,6},{24,16},{26... | collective-permute-start | bytes 811016 | tf_op jit(solution)/shard_map/ppermute | solution.py:287
  45.8 12.4 %collective-permute-start.15 = (f32[264,256]{1,0:T(8,128)S(1)}, f32[264,256]{1,0:T(8,128)S(1)}, u32[]{:S(2)}, u32[]{:S(2)}) collective-permute-start(f32[264,256]{1,0:T(8,128)S(1)} %add.3), channel_id=1, source_target_pairs={{0,16},{2,18},{4,20},{6,22},{16,24},{18,26},{20,28},{22,30},{24,8}... | collective-permute-start | bytes 811016 | tf_op jit(solution)/shard_map/ppermute | solution.py:287
  59.0 8.4 %collective-permute-start.19 = (f32[264,256]{1,0:T(8,128)S(1)}, f32[264,256]{1,0:T(8,128)S(1)}, u32[]{:S(2)}, u32[]{:S(2)}) collective-permute-start(f32[264,256]{1,0:T(8,128)S(1)} %finish.1.refs_0_), channel_id=1, source_target_pairs={{0,4},{2,6},{4,0},{6,2},{8,12},{10,14},{12,8},{14,10},{16,20},{18,... | collective-permute-start | bytes 811016 | tf_op jit(solution)/shard_map/ppermute | solution.py:280
  60.6 8.1 %collective-permute-start.18 = (f32[264,256]{1,0:T(8,128)S(1)}, f32[264,256]{1,0:T(8,128)S(1)}, u32[]{:S(2)}, u32[]{:S(2)}) collective-permute-start(f32[264,256]{1,0:T(8,128)S(1)} %finish.1.refs_0_), channel_id=1, source_target_pairs={{0,2},{2,0},{4,6},{6,4},{8,10},{10,8},{12,14},{14,12},{16,18},{18,... | collective-permute-start | bytes 811016 | tf_op jit(solution)/shard_map/ppermute | solution.py:280
  62.0 8.7 %collective-permute-start.17 = (f32[264,256]{1,0:T(8,128)S(1)}, f32[264,256]{1,0:T(8,128)S(1)}, u32[]{:S(2)}, u32[]{:S(2)}) collective-permute-start(f32[264,256]{1,0:T(8,128)S(1)} %finish.1.refs_0_), channel_id=1, source_target_pairs={{0,16},{2,18},{4,20},{6,22},{16,24},{18,26},{20,28},{22,30},{24,8}... | collective-permute-start | bytes 811016 | tf_op jit(solution)/shard_map/ppermute | solution.py:287
  63.7 14.6 %collective-permute-start.22 = (f32[264,256]{1,0:T(8,128)S(1)}, f32[264,256]{1,0:T(8,128)S(1)}, u32[]{:S(2)}, u32[]{:S(2)}) collective-permute-start(f32[264,256]{1,0:T(8,128)S(1)} %finish.1.refs_0_), channel_id=1, source_target_pairs={{0,8},{2,10},{4,12},{6,14},{16,0},{18,2},{20,4},{22,6},{24,16},{26... | collective-permute-start | bytes 811016 | tf_op jit(solution)/shard_map/ppermute | solution.py:287
  70.8 11.6 %collective-permute-start.24 = (f32[264,256]{1,0:T(8,128)S(1)}, f32[264,256]{1,0:T(8,128)S(1)}, u32[]{:S(2)}, u32[]{:S(2)}) collective-permute-start(f32[264,256]{1,0:T(8,128)S(1)} %collective-permute-done.17.refs_1_), channel_id=1, source_target_pairs={{0,16},{2,18},{4,20},{6,22},{16,24},{18,26},{20,28},{22,30},{24,8}... | collective-permute-start | bytes 811016 | tf_op jit(solution)/shard_map/ppermute | solution.py:287
  78.3 9.4 %collective-permute-start.31 = (f32[264,256]{1,0:T(8,128)S(1)}, f32[264,256]{1,0:T(8,128)S(1)}, u32[]{:S(2)}, u32[]{:S(2)}) collective-permute-start(f32[264,256]{1,0:T(8,128)S(1)} %collective-permute-done.22.refs_6_), channel_id=1, source_target_pairs={{0,2},{2,0},{4,6},{6,4},{8,10},{10,8},{12,14},{14,12},{16,18},{18,... | collective-permute-start | bytes 811016 | tf_op jit(solution)/shard_map/ppermute | solution.py:280
  78.9 9.4 %collective-permute-start.20 = (f32[264,256]{1,0:T(8,128)S(1)}, f32[264,256]{1,0:T(8,128)S(1)}, u32[]{:S(2)}, u32[]{:S(2)}) collective-permute-start(f32[264,256]{1,0:T(8,128)S(1)} %collective-permute-done.18.refs_2_), channel_id=1, source_target_pairs={{0,4},{2,6},{4,0},{6,2},{8,12},{10,14},{12,8},{14,10},{16,20},{18,... | collective-permute-start | bytes 811016 | tf_op jit(solution)/shard_map/ppermute | solution.py:280
  79.4 14.7 %collective-permute-start.30 = (f32[264,256]{1,0:T(8,128)S(1)}, f32[264,256]{1,0:T(8,128)S(1)}, u32[]{:S(2)}, u32[]{:S(2)}) collective-permute-start(f32[264,256]{1,0:T(8,128)S(1)} %collective-permute-done.17.refs_1_), channel_id=1, source_target_pairs={{0,4},{2,6},{4,0},{6,2},{8,12},{10,14},{12,8},{14,10},{16,20},{18,... | collective-permute-start | bytes 811016 | tf_op jit(solution)/shard_map/ppermute | solution.py:280
  80.9 13.9 %collective-permute-start.29 = (f32[264,256]{1,0:T(8,128)S(1)}, f32[264,256]{1,0:T(8,128)S(1)}, u32[]{:S(2)}, u32[]{:S(2)}) collective-permute-start(f32[264,256]{1,0:T(8,128)S(1)} %collective-permute-done.17.refs_1_), channel_id=1, source_target_pairs={{0,2},{2,0},{4,6},{6,4},{8,10},{10,8},{12,14},{14,12},{16,18},{18,... | collective-permute-start | bytes 811016 | tf_op jit(solution)/shard_map/ppermute | solution.py:280
  82.4 17.5 %collective-permute-start.25 = (f32[264,256]{1,0:T(8,128)S(1)}, f32[264,256]{1,0:T(8,128)S(1)}, u32[]{:S(2)}, u32[]{:S(2)}) collective-permute-start(f32[264,256]{1,0:T(8,128)S(1)} %collective-permute-done.24.refs_5_), channel_id=1, source_target_pairs={{0,4},{2,6},{4,0},{6,2},{8,12},{10,14},{12,8},{14,10},{16,20},{18,... | collective-permute-start | bytes 811016 | tf_op jit(solution)/shard_map/ppermute | solution.py:280
  87.7 16.6 %collective-permute-start.23 = (f32[264,256]{1,0:T(8,128)S(1)}, f32[264,256]{1,0:T(8,128)S(1)}, u32[]{:S(2)}, u32[]{:S(2)}) collective-permute-start(f32[264,256]{1,0:T(8,128)S(1)} %collective-permute-done.22.refs_6_), channel_id=1, source_target_pairs={{0,4},{2,6},{4,0},{6,2},{8,12},{10,14},{12,8},{14,10},{16,20},{18,... | collective-permute-start | bytes 811016 | tf_op jit(solution)/shard_map/ppermute | solution.py:280
  88.2 16.0 %collective-permute-start.28 = (f32[264,256]{1,0:T(8,128)S(1)}, f32[264,256]{1,0:T(8,128)S(1)}, u32[]{:S(2)}, u32[]{:S(2)}) collective-permute-start(f32[264,256]{1,0:T(8,128)S(1)} %collective-permute-done.20.refs_4_), channel_id=1, source_target_pairs={{0,16},{2,18},{4,20},{6,22},{16,24},{18,26},{20,28},{22,30},{24,8}... | collective-permute-start | bytes 811016 | tf_op jit(solution)/shard_map/ppermute | solution.py:287
  94.0 10.2 %collective-permute-start.21 = (f32[264,256]{1,0:T(8,128)S(1)}, f32[264,256]{1,0:T(8,128)S(1)}, u32[]{:S(2)}, u32[]{:S(2)}) collective-permute-start(f32[264,256]{1,0:T(8,128)S(1)} %collective-permute-done.20.refs_4_), channel_id=1, source_target_pairs={{0,8},{2,10},{4,12},{6,14},{16,0},{18,2},{20,4},{22,6},{24,16},{26... | collective-permute-start | bytes 811016 | tf_op jit(solution)/shard_map/ppermute | solution.py:287
  94.7 9.5 %collective-permute-start.27 = (f32[264,256]{1,0:T(8,128)S(1)}, f32[264,256]{1,0:T(8,128)S(1)}, u32[]{:S(2)}, u32[]{:S(2)}) collective-permute-start(f32[264,256]{1,0:T(8,128)S(1)} %collective-permute-done.24.refs_5_), channel_id=1, source_target_pairs={{0,2},{2,0},{4,6},{6,4},{8,10},{10,8},{12,14},{14,12},{16,18},{18,... | collective-permute-start | bytes 811016 | tf_op jit(solution)/shard_map/ppermute | solution.py:280
  99.8 7.2 %collective-permute-start.26 = (f32[264,256]{1,0:T(8,128)S(1)}, f32[264,256]{1,0:T(8,128)S(1)}, u32[]{:S(2)}, u32[]{:S(2)}) collective-permute-start(f32[264,256]{1,0:T(8,128)S(1)} %collective-permute-done.25.refs_10_), channel_id=1, source_target_pairs={{0,2},{2,0},{4,6},{6,4},{8,10},{10,8},{12,14},{14,12},{16,18},{18,... | collective-permute-start | bytes 811016 | tf_op jit(solution)/shard_map/ppermute | solution.py:280

commit v6 on v5

--- a/solution.py
+++ b/solution.py
@@ -62,26 +62,15 @@
     return jnp.broadcast_to(jnp.sum(c * c, axis=1, keepdims=True), (c.shape[0], LANES))
 
 
-def stats_kernel(lines, where_ref, points_hbm, c_hbm, out_ref, twice_ref, norm_ref, points_ref, c_ref, all_norm_ref, sems):
+def stats_kernel(lines, where_ref, points_ref, c_ref, out_ref, twice_ref, norm_ref, all_norm_ref):
     rows, local = points_ref.shape[0], c_ref.shape[0]
     chunk = local // lines
     tile, size = min(256, rows), chunk // 4
-    fetch = [pltpu.make_async_copy(points_hbm, points_ref, sems.at[lines])]
-    for l in range(lines):
-        part = pl.ds(l * chunk, chunk)
-        fetch.append(pltpu.make_async_copy(c_hbm.at[part, :], c_ref.at[part, :], sems.at[l]))
-    for copy in fetch:
-        copy.start()
-    fetch[0].wait()
     kept = pl.multiple_of(lax.rem(where_ref[0], 4) * size, size)
     for l in range(lines):
-        fetch[1 + l].wait()
         c = c_ref[l * chunk : (l + 1) * chunk, :]
         all_norm_ref[...] = norms(c)
         twice = c + c
-        mine = c_ref[pl.ds(pl.multiple_of(l * chunk + kept, size), size), :]
-        twice_ref[l * size : (l + 1) * size, :] = mine + mine
-        norm_ref[l * size : (l + 1) * size, :] = all_norm_ref[pl.ds(kept, size), :]
         for start in range(0, rows, tile):
             at = slice(start, start + tile)
             dots = lax.dot_general(twice, points_ref[at, :], NT, preferred_element_type=jnp.float32)
@@ -95,6 +84,9 @@
                 top = new_top
             out_ref[0:1, at] = top
             out_ref[1:2, at] = total
+        mine = c_ref[pl.ds(pl.multiple_of(l * chunk + kept, size), size), :]
+        twice_ref[l * size : (l + 1) * size, :] = mine + mine
+        norm_ref[l * size : (l + 1) * size, :] = all_norm_ref[pl.ds(kept, size), :]
 
 
 def stats(where, points, centroids, lines):
@@ -107,22 +99,17 @@
             jax.ShapeDtypeStruct((local // 4, width), jnp.bfloat16),
             f32(local // 4, LANES),
         ),
-        [SMEM, HBM, HBM],
+        [SMEM, VMEM, VMEM],
         (where, points, centroids),
         "stats",
-        scratch=[
-            pltpu.VMEM(points.shape, points.dtype),
-            pltpu.VMEM(centroids.shape, centroids.dtype),
-            pltpu.VMEM((local // lines, LANES), jnp.float32),
-            pltpu.SemaphoreType.DMA((lines + 1,)),
-        ],
+        scratch=[pltpu.VMEM((local // lines, LANES), jnp.float32)],
         flops=4 * rows * local * width,
     )
 
 
-def lse_kernel(cores, every, x0_ref, y1_ref, *refs):
+def lse_kernel(cores, every, *refs):
     pair_refs = refs[:cores]
-    lse_ref, evidence_ref, pack_x_ref, pack_y_ref = refs[cores:]
+    lse_ref, evidence_ref = refs[cores:]
     half = lse_ref.shape[1]
     top = functools.reduce(jnp.maximum, [p[0:1, :] for p in pair_refs])
     total = functools.reduce(jnp.add, [p[1:2, :] * jnp.exp(p[0:1, :] - top) for p in pair_refs])
@@ -132,10 +119,6 @@
         evidence_ref[k : k + 1, :] = evidence[:, k * LANES : (k + 1) * LANES]
     for i in range(2 * cores):
         lse_ref[i : i + 1, :] = lse[:, i * half : (i + 1) * half]
-    for piece_ref, pack_ref in ((x0_ref, pack_x_ref), (y1_ref, pack_y_ref)):
-        pack_ref[0:half, :] = piece_ref[...]
-        pack_ref[half:, :] = jnp.zeros_like(pack_ref[half:, :])
-        pack_ref[half : half + 2 * cores, 0:half] = lse_ref[...]
 
 
 def add_block(twice, norm, x, lse, acc_ref, cnt_ref, first):
@@ -156,18 +139,12 @@
         cnt_ref[...] += counted
 
 
-def add_pieces(where_ref, twice_ref, norm_ref, pieces, acc_ref, cnt_ref):
-    for x_ref, lse_ref, above, rc, part in pieces:
-        at = above + 2 * (where_ref[1] ^ rc) + part
-        half = acc_rows(x_ref)
-        x = x_ref[0:half, :].astype(jnp.bfloat16)
-        lse = lse_ref[pl.ds(at, 1), :][:, 0:half]
-        add_block(twice_ref[...], norm_ref[...], x, lse, acc_ref, cnt_ref, False)
-
-
-def acc_rows(ref):
-    rows = ref.shape[0]
-    return 1 << (rows.bit_length() - 1)
+def add_pieces(cores, where_ref, twice_ref, norm_ref, refs, whose, acc_ref, cnt_ref):
+    for k, (lse_ref, part) in enumerate(whose):
+        for rc in range(cores):
+            x = refs[k * cores + rc][...].astype(jnp.bfloat16)
+            lse = lse_ref[pl.ds(2 * (where_ref[1] ^ rc) + part, 1), :]
+            add_block(twice_ref[...], norm_ref[...], x, lse, acc_ref, cnt_ref, False)
 
 
 def own_kernel(cores, points_ref, twice_ref, norm_ref, lse_ref, acc_ref, cnt_ref):
@@ -177,32 +154,22 @@
         add_block(twice_ref[...], norm_ref[...], x, lse_ref[i : i + 1, :], acc_ref, cnt_ref, i == 0)
 
 
-def near_kernel(cores, where_ref, twice_ref, norm_ref, acc_in_ref, cnt_in_ref, d0_ref, d1_ref, *refs):
-    x_refs = refs[: 2 * cores]
-    acc_ref, cnt_ref = refs[2 * cores :]
-    above = acc_rows(d0_ref)
+def near_kernel(cores, where_ref, twice_ref, norm_ref, acc_in_ref, cnt_in_ref, lse_x_ref, lse_y_ref, *refs):
+    acc_ref, cnt_ref = refs[4 * cores :]
     acc_ref[...] = acc_in_ref[...]
     cnt_ref[...] = cnt_in_ref[...]
-    pieces = [(x_refs[rc], d1_ref, above, rc, 0) for rc in range(cores)]
-    pieces += [(x_refs[cores + rc], d0_ref, above, rc, 1) for rc in range(cores)]
-    add_pieces(where_ref, twice_ref, norm_ref, pieces, acc_ref, cnt_ref)
-
-
-def far_kernel(cores, order, where_ref, twice_ref, norm_ref, acc_in_ref, cnt_in_ref, lse_d_ref, *refs):
+    whose = ((lse_x_ref, 0), (lse_y_ref, 1), (lse_x_ref, 1), (lse_y_ref, 0))
+    add_pieces(cores, where_ref, twice_ref, norm_ref, refs, whose, acc_ref, cnt_ref)
+
+
+def far_kernel(cores, order, where_ref, twice_ref, norm_ref, acc_in_ref, cnt_in_ref, lse_ref, *refs):
     lines = len(order)
-    x_refs, out_refs = refs[: 4 * cores], refs[4 * cores : 4 * cores + lines]
-    acc_ref, cnt_ref = refs[4 * cores + lines :]
-    d0_ref, d1_ref = x_refs[2 * cores], x_refs[3 * cores]
-    above = acc_rows(d0_ref)
+    out_refs = refs[2 * cores : 2 * cores + lines]
+    acc_ref, cnt_ref = refs[2 * cores + lines :]
     acc_ref[...] = acc_in_ref[...]
     cnt_ref[...] = cnt_in_ref[...]
-    whose = ((d1_ref, above, 1), (d0_ref, above, 0), (lse_d_ref, 0, 0), (lse_d_ref, 0, 1))
-    pieces = [
-        (x_refs[k * cores + rc], lse, top, rc, part)
-        for k, (lse, top, part) in enumerate(whose)
-        for rc in range(cores)
-    ]
-    add_pieces(where_ref, twice_ref, norm_ref, pieces, acc_ref, cnt_ref)
+    whose = ((lse_ref, 0), (lse_ref, 1))
+    add_pieces(cores, where_ref, twice_ref, norm_ref, refs, whose, acc_ref, cnt_ref)
     line = lax.div(where_ref[0], 4)
     width = acc_ref.shape[1]
     size = acc_ref.shape[0] // lines
@@ -302,16 +269,16 @@
 
     pair, twice, norm = stats(where, points, centroids, lines)
     pair, x0, y1 = lax.optimization_barrier((pair, x0, y1))
+    d0, d1 = flip(x0, 2), flip(y1, 1)
     pairs = [pair] + [flip_core(pair, rc) for rc in range(1, cores)]
-    tail = max(8, 2 * cores)
-    lse, log_evidence, pack_x, pack_y = call(
+    lse, log_evidence = call(
         functools.partial(lse_kernel, cores, local_cent * cores),
-        (f32(2 * cores, half), f32(rows // LANES, LANES), f32(half + tail, width), f32(half + tail, width)),
-        [VMEM] * (2 + cores),
-        (x0, y1, *pairs),
+        (f32(2 * cores, half), f32(rows // LANES, LANES)),
+        [VMEM] * cores,
+        pairs,
         "lse",
     )
-    d0, d1, lse_d = flip(pack_x, 2), flip(pack_y, 1), flip(lse, 3)
+    lse_x, lse_y, lse_d = flip(lse, 1), flip(lse, 2), flip(lse, 3)
 
     acc_shape, cnt_shape = f32(share, width), f32(share, min(LANES, half))
     acc, cnt = call(
@@ -322,32 +289,30 @@
         "own",
         flops=4 * share * width * rows,
     )
-    early = with_siblings((x0, y1))
-    early, late, acc, cnt, lse_d = lax.optimization_barrier(
-        (early, (x1, y0, d0, d1), acc, cnt, lse_d)
-    )
-    _, _, d0, d1 = late
-    late = with_siblings(late)
+    near = with_siblings((x0, y1, x1, y0))
+    d0, d1, acc, cnt, lse_x, lse_y, lse_d = lax.optimization_barrier(
+        (d0, d1, acc, cnt, lse_x, lse_y, lse_d)
+    )
     acc, cnt = call(
         functools.partial(near_kernel, cores),
         (acc_shape, cnt_shape),
-        [SMEM] + [VMEM] * (6 + 2 * cores),
-        (where, twice, norm, acc, cnt, d0, d1, *early),
+        [SMEM] + [VMEM] * (6 + 4 * cores),
+        (where, twice, norm, acc, cnt, lse_x, lse_y, *near),
         "near",
-        flops=4 * share * width * rows,
+        flops=4 * share * width * 2 * rows,
         aliases={3: 0, 4: 1},
     )
     sums = call(
         functools.partial(far_kernel, cores, order),
         [f32(size + 8, width)] * lines,
-        [SMEM] + [VMEM] * (5 + 4 * cores),
-        (where, twice, norm, acc, cnt, lse_d, *late),
+        [SMEM] + [VMEM] * (5 + 2 * cores),
+        (where, twice, norm, acc, cnt, lse_d, *with_siblings((d0, d1))),
         "far",
         scratch=[
             pltpu.VMEM((share, width), jnp.float32),
             pltpu.VMEM((share, min(LANES, half)), jnp.float32),
         ],
-        flops=4 * share * width * 2 * rows,
+        flops=4 * share * width * rows,
     )
 
     def reduced(way, steps):
@@ -368,25 +333,32 @@
     )
 
     got = {(0, 0): done}
-    got[0, -1], got[1, 0], got[2, 0] = lax.optimization_barrier(
-        (ring(done, 1), flip(done, 1), flip(done, 2))
-    )
-    got[3, 0] = flip(got[1, 0], 2)
-    for s in range(2, lines // 2 + 1):
-        got[0, -s] = ring(got[0, 1 - s], 1)
-    for s in range(1, lines // 2):
-        got[0, s] = ring(got[0, s - 1], -1)
-    steps = sorted((s for b, s in got if b == 0 and s), key=lambda s: (abs(s), s))
+    chains = {}
+
+    def send(chain, target, source, move, *how):
+        x = got[source]
+        if chain in chains:
+            x, chains[chain] = lax.optimization_barrier((x, got[chains[chain]]))[0], None
+        got[target] = move(x, *how)
+        chains[chain] = target
+
+    steps = [-s for s in range(1, lines // 2 + 1)] + list(range(1, lines // 2))
     for s in steps:
-        got[1, s] = flip(got[0, s], 1)
-        got[2, s] = flip(got[0, s], 2)
+        send("z", (0, s), (0, s + 1 if s < 0 else s - 1), ring, 1 if s < 0 else -1)
+    send("x", (1, 0), (0, 0), flip, 1)
+    send("y", (2, 0), (0, 0), flip, 2)
+    send("y", (3, 0), (1, 0), flip, 2)
+    for s in steps:
+        send("x", (1, s), (0, s), flip, 1)
+        send("y", (2, s), (0, s), flip, 2)
     for s in steps:
         if abs(s) == 1:
-            got[3, s] = ring(got[3, 0], -s)
+            send("z", (3, s), (3, 0), ring, -s)
         else:
-            got[3, s] = flip(got[2, s], 1)
-    last = [(3, 1), (2, 1), (3, -lines // 2), (1, -lines // 2), (3, -1)]
-    groups = ([k for k in got if k not in last], last)
+            send("x", (3, s), (2, s), flip, 1)
+    late = [chains["x"], chains["y"], chains["z"]]
+    middle = [(2, -2), (1, 1), (3, -1), (1, -2), (2, -1)]
+    groups = ([k for k in got if k not in middle + late], middle, late)
     new = counts = None
     for later, names in enumerate(groups):
         args = [where] + [got[k] for k in names]
@@ -395,9 +367,9 @@
         new, counts = call(
             functools.partial(place_kernel, names, order, later),
             (f32(local_cent, width), f32(local_cent // LANES, LANES)),
-            [SMEM] + [VMEM] * len(names) + [VMEM, ANY][: 2 * later],
+            [SMEM] + [VMEM] * len(names) + ([VMEM, ANY] if later else []),
             args,
-            "place_late" if later else "place_early",
+            ("place_early", "place_middle", "place_late")[later],
             out_specs=(ANY, VMEM),
             scratch=[pltpu.SemaphoreType.DMA((len(names),))],
             aliases={len(args) - 1: 0} if later else {},

time: 109 us -> 110 us (level)
  waiting for transfers between devices: 51.4 us -> 37.6 us
  starting transfers between devices: 34.1 us -> 46.7 us
  Pallas kernels: 20.3 us -> 21.6 us
    ppermute x17 -> x19, waiting for transfers between devices: 28 us -> 11.7 us  [flip(): return lax.ppermute(x, 'dp', [(i, i ^ bits) for i in range(n)])]
    ppermute x17 -> x19, starting transfers between devices: 19.8 us -> 27.4 us  [flip(): return lax.ppermute(x, 'dp', [(i, i ^ bits) for i in range(n)])]
    ppermute x8, starting transfers between devices: 12.8 us -> 18 us  [ring(): lax.ppermute(x, 'dp', [(4 * a + i, 4 * b + i) for a, b in pairs for i in...]
    ppermute x8, waiting for transfers between devices: 22.2 us -> 25.9 us  [ring(): lax.ppermute(x, 'dp', [(4 * a + i, 4 * b + i) for a, b in pairs for i in...]
    pallas_call x10 -> x11, Pallas kernels: 20.3 us -> 21.6 us  [call(): pl.pallas_call(kernel, out_shape=out_shape, in_specs=in_specs, out_specs=...]
    ppermute x7, waiting for transfers between devices: 1.19 us -> 0.02 us  [flip_core(): return lax.ppermute(x, 'cent', [(i, i ^ bits) for i in range(cores)])]
  transfers between devices with their start and end apart: 32 -> 34, of which waited for: 17 -> 13; matrix products, arithmetic and copies ran while one was open for 0% -> 0% of each run, Pallas kernels for 12% -> 14%
where the time goes in v6:
time: 110 us
  starting transfers between devices  46.7 us (42%)
  waiting for transfers between devices  37.6 us (34%)
  Pallas kernels  21.6 us (20%)
  local copies, waits for them, and re-layouts  2.64 us (2%)
    ppermute x19, starting transfers between devices, flip(): return lax.ppermute(x, 'dp', [(i, i ^ bits) for i in range(n)])  27.4 us
    ppermute x8, waiting for transfers between devices, ring(): lax.ppermute(x, 'dp', [(4 * a + i, 4 * b + i) for a, b in pairs for i in...  25.9 us
    pallas_call x11, Pallas kernels, call(): pl.pallas_call(kernel, out_shape=out_shape, in_specs=in_specs, out_specs=...  21.6 us
    ppermute x8, starting transfers between devices, ring(): lax.ppermute(x, 'dp', [(4 * a + i, 4 * b + i) for a, b in pairs for i in...  18 us
    ppermute x19, waiting for transfers between devices, flip(): return lax.ppermute(x, 'dp', [(i, i ^ bits) for i in range(n)])  11.7 us
    unnamed x6, local copies, waits for them, and re-layouts  2.64 us
  transfers between devices with their start and end apart: 34, of which 13 were waited for; matrix products, arithmetic and copies ran while one was open for 0% of the time, Pallas kernels for 14%

profile of v6, /device:TPU:0, one launch (start us, length us, event | category | flops | bytes accessed | tf_op | source)
XLA Modules:
  0.0 109.6 jit_solution(1414589147289565924)
XLA Ops:
  0.7 1.0 copy-done
  1.8 0.6 open.1
  2.4 3.0 %collective-permute-start.1 = (f32[256,256]{1,0:T(8,128)S(1)}, f32[256,256]{1,0:T(8,128)S(1)}, u32[]{:S(2)}, u32[]{:S(2)}) collective-permute-start(f32[256,256]{1,0:T(8,128)S(1)} %get-tuple-element.50), channel_id=1, source_target_pairs={{0,4},{2,6},{4,0},{6,2},{8,12},{10,14},{12,8},{14,10},{16,20},{18,... | collective-permute-start | bytes 786440 | tf_op jit(solution)/shard_map/ppermute | solution.py:247
  5.4 1.5 %collective-permute-start.10 = (f32[256,256]{1,0:T(8,128)S(1)}, f32[256,256]{1,0:T(8,128)S(1)}, u32[]{:S(2)}, u32[]{:S(2)}) collective-permute-start(f32[256,256]{1,0:T(8,128)S(1)} %get-tuple-element.50), channel_id=1, source_target_pairs={{0,2},{2,0},{4,6},{6,4},{8,10},{10,8},{12,14},{14,12},{16,18},{18,... | collective-permute-start | bytes 786440 | tf_op jit(solution)/shard_map/ppermute | solution.py:247
  6.9 0.5 collective-permute-start
  7.5 1.6 %copy-done.2 = bf16[4096,256]{1,0:T(8,128)(2,1)S(1)} copy-done((bf16[4096,256]{1,0:T(8,128)(2,1)S(1)}, bf16[4096,256]{1,0:T(8,128)(2,1)}, u32[]{:S(2)}) %copy-start.2) | copy-done | bytes 2097176
  9.1 5.9 %stats.1 = (f32[2,1024]{1,0:T(2,128)S(1)}, bf16[1024,256]{1,0:T(8,128)(2,1)S(1)}, f32[1024,128]{1,0:T(8,128)S(1)}) custom-call(s32[2]{0:T(128)S(1)} %pad_add_fusion.where_ref, bf16[1024,256]{1,0:T(8,128)(2,1)S(1)} %copy-done, bf16[4096,256]{1,0:T(8,128)(2,1)S(1)} %copy-done.2), custom_call_target="tpu_custom_call" | custom-call | flops 4294967296 | bytes 2621448 | tf_op jit(solution)/shard_map/stats/pallas_call | solution.py:27
  15.0 3.8 %collective-permute-done.refs_0_ = f32[256,256]{1,0:T(8,128)S(1)} collective-permute-done((f32[256,256]{1,0:T(8,128)S(1)}, f32[256,256]{1,0:T(8,128)S(1)}, u32[]{:S(2)}, u32[]{:S(2)}) %collective-permute-start) | collective-permute-done | bytes 262176 | tf_op jit(solution)/shard_map/ppermute | solution.py:247
  19.2 1.6 %collective-permute-start.3 = (f32[256,256]{1,0:T(8,128)S(1)}, f32[256,256]{1,0:T(8,128)S(1)}, u32[]{:S(2)}, u32[]{:S(2)}) collective-permute-start(f32[256,256]{1,0:T(8,128)S(1)} %collective-permute-done.1.refs_2_), channel_id=1, source_target_pairs={{0,2},{2,0},{4,6},{6,4},{8,10},{10,8},{12,14},{14,12},{16,18},{18,... | collective-permute-start | bytes 786440 | tf_op jit(solution)/shard_map/ppermute | solution.py:247
  21.0 0.6 lse.1
  21.6 1.1 %collective-permute-start.5 = (f32[4,256]{1,0:T(4,128)S(1)}, f32[4,256]{1,0:T(4,128)S(1)}, u32[]{:S(2)}, u32[]{:S(2)}) collective-permute-start(f32[4,256]{1,0:T(4,128)S(1)} %get-tuple-element.54.lse_ref), channel_id=1, source_target_pairs={{0,2},{2,0},{4,6},{6,4},{8,10},{10,8},{12,14},{14,12},{16,18},{18,... | collective-permute-start | bytes 12296 | tf_op jit(solution)/shard_map/ppermute | solution.py:247
  22.8 1.5 %collective-permute-start.6 = (f32[4,256]{1,0:T(4,128)S(1)}, f32[4,256]{1,0:T(4,128)S(1)}, u32[]{:S(2)}, u32[]{:S(2)}) collective-permute-start(f32[4,256]{1,0:T(4,128)S(1)} %get-tuple-element.54.lse_ref), channel_id=1, source_target_pairs={{0,4},{2,6},{4,0},{6,2},{8,12},{10,14},{12,8},{14,10},{16,20},{18,... | collective-permute-start | bytes 12296 | tf_op jit(solution)/shard_map/ppermute | solution.py:247
  24.3 3.7 %collective-permute-done.5.lse_x_ref = f32[4,256]{1,0:T(4,128)S(1)} collective-permute-done((f32[4,256]{1,0:T(4,128)S(1)}, f32[4,256]{1,0:T(4,128)S(1)}, u32[]{:S(2)}, u32[]{:S(2)}) %collective-permute-start.5) | collective-permute-done | bytes 4128 | tf_op jit(solution)/shard_map/ppermute | solution.py:247
  28.0 2.6 %collective-permute-start.7 = (f32[4,256]{1,0:T(4,128)S(1)}, f32[4,256]{1,0:T(4,128)S(1)}, u32[]{:S(2)}, u32[]{:S(2)}) collective-permute-start(f32[4,256]{1,0:T(4,128)S(1)} %get-tuple-element.54.lse_ref), channel_id=1, source_target_pairs={{0,6},{2,4},{4,2},{6,0},{8,14},{10,12},{12,10},{14,8},{16,22},{18,... | collective-permute-start | bytes 12296 | tf_op jit(solution)/shard_map/ppermute | solution.py:247
  30.6 1.9 %collective-permute-done.7.lse_ref = f32[4,256]{1,0:T(4,128)S(1)} collective-permute-done((f32[4,256]{1,0:T(4,128)S(1)}, f32[4,256]{1,0:T(4,128)S(1)}, u32[]{:S(2)}, u32[]{:S(2)}) %collective-permute-start.7) | collective-permute-done | bytes 4128 | tf_op jit(solution)/shard_map/ppermute | solution.py:247
  33.0 1.6 %own.1 = (f32[1024,256]{1,0:T(8,128)S(1)}, f32[1024,128]{1,0:T(8,128)S(1)}) custom-call(bf16[1024,256]{1,0:T(8,128)(2,1)S(1)} %copy-done.1, bf16[1024,256]{1,0:T(8,128)(2,1)S(1)} %get-tuple-element.46.twice_ref, f32[1024,128]{1,0:T(8,128)S(1)} %get-tuple-element.47.norm_ref, f32[4,256]{1,0:T(4,128)S(1)} %get-tuple-element.54.lse_ref), custom_call_target="tpu_custom_call" | custom-call | flops 1073741824 | bytes 1576960 | tf_op jit(solution)/shard_map/own/pallas_call | solution.py:27
  35.2 3.8 %near.1 = (f32[1024,256]{1,0:T(8,128)S(1)}, f32[1024,128]{1,0:T(8,128)S(1)}) custom-call(s32[2]{0:T(128)S(1)} %pad_add_fusion.where_ref, bf16[1024,256]{1,0:T(8,128)(2,1)S(1)} %get-tuple-element.46.twice_ref, f32[1024,128]{1,0:T(8,128)S(1)} %get-tuple-element.47.norm_ref, ...), custom_call_target="tpu_custom_call", output_to_operand_aliasing={{0}: (3, {}), {1}: (4, {})} | custom-call | flops 2147483648 | bytes 4726792 | tf_op jit(solution)/shard_map/near/pallas_call | solution.py:27
  39.1 2.6 %far.1 = (f32[264,256]{1,0:T(8,128)S(1)}, f32[264,256]{1,0:T(8,128)S(1)}, f32[264,256]{1,0:T(8,128)S(1)}, f32[264,256]{1,0:T(8,128)S(1)}) custom-call(s32[2]{0:T(128)S(1)} %pad_add_fusion.where_ref, bf16[1024,256]{1,0:T(8,128)(2,1)S(1)} %get-tuple-element.46.twice_ref, f32[1024,128]{1,0:T(8,128)S(1)} %get-tuple-element.47.norm_ref, ...), custom_call_target="tpu_custom_call" | custom-call | flops 1073741824 | bytes 3674120 | tf_op jit(solution)/shard_map/far/pallas_call | solution.py:27
  41.6 2.8 %collective-permute-start.16 = (f32[264,256]{1,0:T(8,128)S(1)}, f32[264,256]{1,0:T(8,128)S(1)}, u32[]{:S(2)}, u32[]{:S(2)}) collective-permute-start(f32[264,256]{1,0:T(8,128)S(1)} %get-tuple-element.68), channel_id=1, source_target_pairs={{0,16},{2,18},{4,20},{6,22},{16,24},{18,26},{20,28},{22,30},{24,8}... | collective-permute-start | bytes 811016 | tf_op jit(solution)/shard_map/ppermute | solution.py:254
  44.4 6.9 %collective-permute-done.16.b_ref = f32[264,256]{1,0:T(8,128)S(1)} collective-permute-done((f32[264,256]{1,0:T(8,128)S(1)}, f32[264,256]{1,0:T(8,128)S(1)}, u32[]{:S(2)}, u32[]{:S(2)}) %collective-permute-start.16) | collective-permute-done | bytes 270368 | tf_op jit(solution)/shard_map/ppermute | solution.py:254
  51.4 3.4 %collective-permute-start.17 = (f32[264,256]{1,0:T(8,128)S(1)}, f32[264,256]{1,0:T(8,128)S(1)}, u32[]{:S(2)}, u32[]{:S(2)}) collective-permute-start(f32[264,256]{1,0:T(8,128)S(1)} %add.3), channel_id=1, source_target_pairs={{0,16},{2,18},{4,20},{6,22},{16,24},{18,26},{20,28},{22,30},{24,8}... | collective-permute-start | bytes 811016 | tf_op jit(solution)/shard_map/ppermute | solution.py:254
  54.8 4.1 %collective-permute-done.18.second_ref = f32[264,256]{1,0:T(8,128)S(1)} collective-permute-done((f32[264,256]{1,0:T(8,128)S(1)}, f32[264,256]{1,0:T(8,128)S(1)}, u32[]{:S(2)}, u32[]{:S(2)}) %collective-permute-start.18) | collective-permute-done | bytes 270368 | tf_op jit(solution)/shard_map/ppermute | solution.py:254
  58.9 4.8 %collective-permute-done.17.first_ref = f32[264,256]{1,0:T(8,128)S(1)} collective-permute-done((f32[264,256]{1,0:T(8,128)S(1)}, f32[264,256]{1,0:T(8,128)S(1)}, u32[]{:S(2)}, u32[]{:S(2)}) %collective-permute-start.17) | collective-permute-done | bytes 270368 | tf_op jit(solution)/shard_map/ppermute | solution.py:254
  63.8 0.8 finish.1.refs_0_
  64.6 1.7 %collective-permute-start.19 = (f32[264,256]{1,0:T(8,128)S(1)}, f32[264,256]{1,0:T(8,128)S(1)}, u32[]{:S(2)}, u32[]{:S(2)}) collective-permute-start(f32[264,256]{1,0:T(8,128)S(1)} %finish.1.refs_0_), channel_id=1, source_target_pairs={{0,16},{2,18},{4,20},{6,22},{16,24},{18,26},{20,28},{22,30},{24,8}... | collective-permute-start | bytes 811016 | tf_op jit(solution)/shard_map/ppermute | solution.py:254
  66.3 1.5 %collective-permute-start.21 = (f32[264,256]{1,0:T(8,128)S(1)}, f32[264,256]{1,0:T(8,128)S(1)}, u32[]{:S(2)}, u32[]{:S(2)}) collective-permute-start(f32[264,256]{1,0:T(8,128)S(1)} %finish.1.refs_0_), channel_id=1, source_target_pairs={{0,2},{2,0},{4,6},{6,4},{8,10},{10,8},{12,14},{14,12},{16,18},{18,... | collective-permute-start | bytes 811016 | tf_op jit(solution)/shard_map/ppermute | solution.py:247
  67.8 1.5 %collective-permute-start.22 = (f32[264,256]{1,0:T(8,128)S(1)}, f32[264,256]{1,0:T(8,128)S(1)}, u32[]{:S(2)}, u32[]{:S(2)}) collective-permute-start(f32[264,256]{1,0:T(8,128)S(1)} %finish.1.refs_0_), channel_id=1, source_target_pairs={{0,4},{2,6},{4,0},{6,2},{8,12},{10,14},{12,8},{14,10},{16,20},{18,... | collective-permute-start | bytes 811016 | tf_op jit(solution)/shard_map/ppermute | solution.py:247
  69.3 3.6 %collective-permute-done.19.refs_1_ = f32[264,256]{1,0:T(8,128)S(1)} collective-permute-done((f32[264,256]{1,0:T(8,128)S(1)}, f32[264,256]{1,0:T(8,128)S(1)}, u32[]{:S(2)}, u32[]{:S(2)}) %collective-permute-start.19) | collective-permute-done | bytes 270368 | tf_op jit(solution)/shard_map/ppermute | solution.py:254
  73.0 1.9 %collective-permute-start.20 = (f32[264,256]{1,0:T(8,128)S(1)}, f32[264,256]{1,0:T(8,128)S(1)}, u32[]{:S(2)}, u32[]{:S(2)}) collective-permute-start(f32[264,256]{1,0:T(8,128)S(1)} %collective-permute-done.19.refs_1_), channel_id=1, source_target_pairs={{0,16},{2,18},{4,20},{6,22},{16,24},{18,26},{20,28},{22,30},{24,8}... | collective-permute-start | bytes 811016 | tf_op jit(solution)/shard_map/ppermute | solution.py:254
  74.9 1.5 %collective-permute-start.23 = (f32[264,256]{1,0:T(8,128)S(1)}, f32[264,256]{1,0:T(8,128)S(1)}, u32[]{:S(2)}, u32[]{:S(2)}) collective-permute-start(f32[264,256]{1,0:T(8,128)S(1)} %collective-permute-done.21.refs_4_), channel_id=1, source_target_pairs={{0,4},{2,6},{4,0},{6,2},{8,12},{10,14},{12,8},{14,10},{16,20},{18,... | collective-permute-start | bytes 811016 | tf_op jit(solution)/shard_map/ppermute | solution.py:247
  76.4 1.5 %collective-permute-start.27 = (f32[264,256]{1,0:T(8,128)S(1)}, f32[264,256]{1,0:T(8,128)S(1)}, u32[]{:S(2)}, u32[]{:S(2)}) collective-permute-start(f32[264,256]{1,0:T(8,128)S(1)} %collective-permute-done.19.refs_1_), channel_id=1, source_target_pairs={{0,2},{2,0},{4,6},{6,4},{8,10},{10,8},{12,14},{14,12},{16,18},{18,... | collective-permute-start | bytes 811016 | tf_op jit(solution)/shard_map/ppermute | solution.py:247
  77.9 2.6 %collective-permute-done.20.refs_2_ = f32[264,256]{1,0:T(8,128)S(1)} collective-permute-done((f32[264,256]{1,0:T(8,128)S(1)}, f32[264,256]{1,0:T(8,128)S(1)}, u32[]{:S(2)}, u32[]{:S(2)}) %collective-permute-start.20) | collective-permute-done | bytes 270368 | tf_op jit(solution)/shard_map/ppermute | solution.py:254
  80.4 2.2 %collective-permute-start.26 = (f32[264,256]{1,0:T(8,128)S(1)}, f32[264,256]{1,0:T(8,128)S(1)}, u32[]{:S(2)}, u32[]{:S(2)}) collective-permute-start(f32[264,256]{1,0:T(8,128)S(1)} %finish.1.refs_0_), channel_id=1, source_target_pairs={{0,8},{2,10},{4,12},{6,14},{16,0},{18,2},{20,4},{22,6},{24,16},{26... | collective-permute-start | bytes 811016 | tf_op jit(solution)/shard_map/ppermute | solution.py:254
  82.6 1.5 %collective-permute-start.24 = (f32[264,256]{1,0:T(8,128)S(1)}, f32[264,256]{1,0:T(8,128)S(1)}, u32[]{:S(2)}, u32[]{:S(2)}) collective-permute-start(f32[264,256]{1,0:T(8,128)S(1)} %collective-permute-done.19.refs_1_), channel_id=1, source_target_pairs={{0,4},{2,6},{4,0},{6,2},{8,12},{10,14},{12,8},{14,10},{16,20},{18,... | collective-permute-start | bytes 811016 | tf_op jit(solution)/shard_map/ppermute | solution.py:247
  84.1 1.5 %collective-permute-start.28 = (f32[264,256]{1,0:T(8,128)S(1)}, f32[264,256]{1,0:T(8,128)S(1)}, u32[]{:S(2)}, u32[]{:S(2)}) collective-permute-start(f32[264,256]{1,0:T(8,128)S(1)} %collective-permute-done.20.refs_2_), channel_id=1, source_target_pairs={{0,2},{2,0},{4,6},{6,4},{8,10},{10,8},{12,14},{14,12},{16,18},{18,... | collective-permute-start | bytes 811016 | tf_op jit(solution)/shard_map/ppermute | solution.py:247
  85.6 2.3 %collective-permute-done.26.refs_3_ = f32[264,256]{1,0:T(8,128)S(1)} collective-permute-done((f32[264,256]{1,0:T(8,128)S(1)}, f32[264,256]{1,0:T(8,128)S(1)}, u32[]{:S(2)}, u32[]{:S(2)}) %collective-permute-start.26) | collective-permute-done | bytes 270368 | tf_op jit(solution)/shard_map/ppermute | solution.py:254
  87.9 1.0 collective-permute-start.32
  88.9 0.6 collective-permute-done.24.refs_4_
  89.5 1.5 %collective-permute-start.25 = (f32[264,256]{1,0:T(8,128)S(1)}, f32[264,256]{1,0:T(8,128)S(1)}, u32[]{:S(2)}, u32[]{:S(2)}) collective-permute-start(f32[264,256]{1,0:T(8,128)S(1)} %collective-permute-done.20.refs_2_), channel_id=1, source_target_pairs={{0,4},{2,6},{4,0},{6,2},{8,12},{10,14},{12,8},{14,10},{16,20},{18,... | collective-permute-start | bytes 811016 | tf_op jit(solution)/shard_map/ppermute | solution.py:247
  91.3 1.5 %collective-permute-start.29 = (f32[264,256]{1,0:T(8,128)S(1)}, f32[264,256]{1,0:T(8,128)S(1)}, u32[]{:S(2)}, u32[]{:S(2)}) collective-permute-start(f32[264,256]{1,0:T(8,128)S(1)} %collective-permute-done.26.refs_3_), channel_id=1, source_target_pairs={{0,2},{2,0},{4,6},{6,4},{8,10},{10,8},{12,14},{14,12},{16,18},{18,... | collective-permute-start | bytes 811016 | tf_op jit(solution)/shard_map/ppermute | solution.py:247
  92.8 1.6 %collective-permute-done.32.refs_2_ = f32[264,256]{1,0:T(8,128)S(1)} collective-permute-done((f32[264,256]{1,0:T(8,128)S(1)}, f32[264,256]{1,0:T(8,128)S(1)}, u32[]{:S(2)}, u32[]{:S(2)}) %collective-permute-start.32) | collective-permute-done | bytes 270368 | tf_op jit(solution)/shard_map/ppermute | solution.py:254
  94.4 5.0 %collective-permute-start.33 = (f32[264,256]{1,0:T(8,128)S(1)}, f32[264,256]{1,0:T(8,128)S(1)}, u32[]{:S(2)}, u32[]{:S(2)}) collective-permute-start(f32[264,256]{1,0:T(8,128)S(1)} %collective-permute-done.23.refs_6_), channel_id=1, source_target_pairs={{0,8},{2,10},{4,12},{6,14},{16,0},{18,2},{20,4},{22,6},{24,16},{26... | collective-permute-start | bytes 811016 | tf_op jit(solution)/shard_map/ppermute | solution.py:254
  99.4 1.5 %collective-permute-start.31 = (f32[264,256]{1,0:T(8,128)S(1)}, f32[264,256]{1,0:T(8,128)S(1)}, u32[]{:S(2)}, u32[]{:S(2)}) collective-permute-start(f32[264,256]{1,0:T(8,128)S(1)} %collective-permute-done.26.refs_3_), channel_id=1, source_target_pairs={{0,4},{2,6},{4,0},{6,2},{8,12},{10,14},{12,8},{14,10},{16,20},{18,... | collective-permute-start | bytes 811016 | tf_op jit(solution)/shard_map/ppermute | solution.py:247
  100.9 1.5 %collective-permute-start.30 = (f32[264,256]{1,0:T(8,128)S(1)}, f32[264,256]{1,0:T(8,128)S(1)}, u32[]{:S(2)}, u32[]{:S(2)}) collective-permute-start(f32[264,256]{1,0:T(8,128)S(1)} %collective-permute-done.25.refs_0_), channel_id=1, source_target_pairs={{0,2},{2,0},{4,6},{6,4},{8,10},{10,8},{12,14},{14,12},{16,18},{18,... | collective-permute-start | bytes 811016 | tf_op jit(solution)/shard_map/ppermute | solution.py:247
  102.4 1.9 %place_early.1 = (f32[4096,256]{1,0:T(8,128)}, f32[32,128]{1,0:T(8,128)S(1)}) custom-call(s32[2]{0:T(128)S(1)} %pad_add_fusion.where_ref, f32[264,256]{1,0:T(8,128)S(1)} %finish.1.refs_0_, f32[264,256]{1,0:T(8,128)S(1)} %collective-permute-done.19.refs_1_, f32[264,256]{1,0:T(8,128)S(1)} %collective-permute-done.20.refs_2_, ...), custom_call_target="tpu_custom_call" | custom-call | bytes 2162696 | tf_op jit(solution)/shard_map/place_early/pallas_call | solution.py:27
  104.3 1.6 %place_middle.1 = (f32[4096,256]{1,0:T(8,128)}, f32[32,128]{1,0:T(8,128)S(1)}) custom-call(s32[2]{0:T(128)S(1)} %pad_add_fusion.where_ref, f32[264,256]{1,0:T(8,128)S(1)} %collective-permute-done.25.refs_0_, f32[264,256]{1,0:T(8,128)S(1)} %collective-permute-done.29.refs_1_, ...), custom_call_target="tpu_custom_call", output_to_operand_aliasing={{0}: (7, {})} | custom-call | bytes 5562376 | tf_op jit(solution)/shard_map/place_middle/pallas_call | solution.py:27
  106.0 1.3 %collective-permute-done.30.refs_0_ = f32[264,256]{1,0:T(8,128)S(1)} collective-permute-done((f32[264,256]{1,0:T(8,128)S(1)}, f32[264,256]{1,0:T(8,128)S(1)}, u32[]{:S(2)}, u32[]{:S(2)}) %collective-permute-start.30) | collective-permute-done | bytes 270368 | tf_op jit(solution)/shard_map/ppermute | solution.py:247
  107.4 2.1 %place_late.1 = (f32[4096,256]{1,0:T(8,128)}, f32[32,128]{1,0:T(8,128)}) custom-call(s32[2]{0:T(128)S(1)} %pad_add_fusion.where_ref, f32[264,256]{1,0:T(8,128)S(1)} %collective-permute-done.30.refs_0_, f32[264,256]{1,0:T(8,128)S(1)} %collective-permute-done.31.refs_1_, ...), custom_call_target="tpu_custom_call", output_to_operand_aliasing={{0}: (5, {})} | custom-call | bytes 5021704 | tf_op jit(solution)/shard_map/place_late/pallas_call | solution.py:27
  (38 shorter events, 2.2 us)
Async XLA Ops:
  0.7 1.0 copy-start
  2.4 16.4 %collective-permute-start.1 = (f32[256,256]{1,0:T(8,128)S(1)}, f32[256,256]{1,0:T(8,128)S(1)}, u32[]{:S(2)}, u32[]{:S(2)}) collective-permute-start(f32[256,256]{1,0:T(8,128)S(1)} %get-tuple-element.50), channel_id=1, source_target_pairs={{0,4},{2,6},{4,0},{6,2},{8,12},{10,14},{12,8},{14,10},{16,20},{18,... | collective-permute-start | bytes 786440 | tf_op jit(solution)/shard_map/ppermute | solution.py:247
  5.4 16.2 %collective-permute-start.10 = (f32[256,256]{1,0:T(8,128)S(1)}, f32[256,256]{1,0:T(8,128)S(1)}, u32[]{:S(2)}, u32[]{:S(2)}) collective-permute-start(f32[256,256]{1,0:T(8,128)S(1)} %get-tuple-element.50), channel_id=1, source_target_pairs={{0,2},{2,0},{4,6},{6,4},{8,10},{10,8},{12,14},{14,12},{16,18},{18,... | collective-permute-start | bytes 786440 | tf_op jit(solution)/shard_map/ppermute | solution.py:247
  6.9 26.1 %copy-start.1 = (bf16[1024,256]{1,0:T(8,128)(2,1)S(1)}, bf16[1024,256]{1,0:T(8,128)(2,1)}, u32[]{:S(2)}) copy-start(bf16[1024,256]{1,0:T(8,128)(2,1)} %points_ref.5) | copy-start | bytes 1572868
  6.9 11.9 %collective-permute-start = (f32[256,256]{1,0:T(8,128)S(1)}, f32[256,256]{1,0:T(8,128)S(1)}, u32[]{:S(2)}, u32[]{:S(2)}) collective-permute-start(f32[256,256]{1,0:T(8,128)S(1)} %get-tuple-element.49), channel_id=1, source_target_pairs={{0,2},{2,0},{4,6},{6,4},{8,10},{10,8},{12,14},{14,12},{16,18},{18,... | collective-permute-start | bytes 786440 | tf_op jit(solution)/shard_map/ppermute | solution.py:247
  7.4 15.3 %collective-permute-start.12 = (f32[256,256]{1,0:T(8,128)S(1)}, f32[256,256]{1,0:T(8,128)S(1)}, u32[]{:S(2)}, u32[]{:S(2)}) collective-permute-start(f32[256,256]{1,0:T(8,128)S(1)} %get-tuple-element.49), channel_id=1, source_target_pairs={{0,4},{2,6},{4,0},{6,2},{8,12},{10,14},{12,8},{14,10},{16,20},{18,... | collective-permute-start | bytes 786440 | tf_op jit(solution)/shard_map/ppermute | solution.py:247
  7.5 1.6 %copy-start.2 = (bf16[4096,256]{1,0:T(8,128)(2,1)S(1)}, bf16[4096,256]{1,0:T(8,128)(2,1)}, u32[]{:S(2)}) copy-start(bf16[4096,256]{1,0:T(8,128)(2,1)} %c_ref.1) | copy-start | bytes 6291460
  18.8 13.7 %collective-permute-start.2 = (f32[256,256]{1,0:T(8,128)S(1)}, f32[256,256]{1,0:T(8,128)S(1)}, u32[]{:S(2)}, u32[]{:S(2)}) collective-permute-start(f32[256,256]{1,0:T(8,128)S(1)} %collective-permute-done.refs_0_), channel_id=1, source_target_pairs={{0,4},{2,6},{4,0},{6,2},{8,12},{10,14},{12,8},{14,10},{16,20},{18,... | collective-permute-start | bytes 786440 | tf_op jit(solution)/shard_map/ppermute | solution.py:247
  19.1 1.6 %collective-permute-start.4 = (f32[2,1024]{1,0:T(2,128)S(1)}, f32[2,1024]{1,0:T(2,128)S(1)}, u32[]{:S(2)}, u32[]{:S(2)}) collective-permute-start(f32[2,1024]{1,0:T(2,128)S(1)} %get-tuple-element.53.refs_0_), channel_id=1, source_target_pairs={{0,1},{1,0},{2,3},{3,2},{4,5},{5,4},{6,7},{7,6},{8,9},{9,8},{10,11... | collective-permute-start | bytes 24584 | tf_op jit(solution)/shard_map/ppermute | solution.py:250
  19.2 15.5 %collective-permute-start.3 = (f32[256,256]{1,0:T(8,128)S(1)}, f32[256,256]{1,0:T(8,128)S(1)}, u32[]{:S(2)}, u32[]{:S(2)}) collective-permute-start(f32[256,256]{1,0:T(8,128)S(1)} %collective-permute-done.1.refs_2_), channel_id=1, source_target_pairs={{0,2},{2,0},{4,6},{6,4},{8,10},{10,8},{12,14},{14,12},{16,18},{18,... | collective-permute-start | bytes 786440 | tf_op jit(solution)/shard_map/ppermute | solution.py:247
  20.8 13.9 %collective-permute-start.8 = (f32[256,256]{1,0:T(8,128)S(1)}, f32[256,256]{1,0:T(8,128)S(1)}, u32[]{:S(2)}, u32[]{:S(2)}) collective-permute-start(f32[256,256]{1,0:T(8,128)S(1)} %collective-permute-done.refs_0_), channel_id=1, source_target_pairs={{0,1},{1,0},{2,3},{3,2},{4,5},{5,4},{6,7},{7,6},{8,9},{9,8},{10,11... | collective-permute-start | bytes 786440 | tf_op jit(solution)/shard_map/ppermute | solution.py:250
  21.6 6.3 %collective-permute-start.5 = (f32[4,256]{1,0:T(4,128)S(1)}, f32[4,256]{1,0:T(4,128)S(1)}, u32[]{:S(2)}, u32[]{:S(2)}) collective-permute-start(f32[4,256]{1,0:T(4,128)S(1)} %get-tuple-element.54.lse_ref), channel_id=1, source_target_pairs={{0,2},{2,0},{4,6},{6,4},{8,10},{10,8},{12,14},{14,12},{16,18},{18,... | collective-permute-start | bytes 12296 | tf_op jit(solution)/shard_map/ppermute | solution.py:247
  22.8 7.8 %collective-permute-start.6 = (f32[4,256]{1,0:T(4,128)S(1)}, f32[4,256]{1,0:T(4,128)S(1)}, u32[]{:S(2)}, u32[]{:S(2)}) collective-permute-start(f32[4,256]{1,0:T(4,128)S(1)} %get-tuple-element.54.lse_ref), channel_id=1, source_target_pairs={{0,4},{2,6},{4,0},{6,2},{8,12},{10,14},{12,8},{14,10},{16,20},{18,... | collective-permute-start | bytes 12296 | tf_op jit(solution)/shard_map/ppermute | solution.py:247
  28.0 4.5 %collective-permute-start.7 = (f32[4,256]{1,0:T(4,128)S(1)}, f32[4,256]{1,0:T(4,128)S(1)}, u32[]{:S(2)}, u32[]{:S(2)}) collective-permute-start(f32[4,256]{1,0:T(4,128)S(1)} %get-tuple-element.54.lse_ref), channel_id=1, source_target_pairs={{0,6},{2,4},{4,2},{6,0},{8,14},{10,12},{12,10},{14,8},{16,22},{18,... | collective-permute-start | bytes 12296 | tf_op jit(solution)/shard_map/ppermute | solution.py:247
  30.6 4.6 %collective-permute-start.9 = (f32[256,256]{1,0:T(8,128)S(1)}, f32[256,256]{1,0:T(8,128)S(1)}, u32[]{:S(2)}, u32[]{:S(2)}) collective-permute-start(f32[256,256]{1,0:T(8,128)S(1)} %collective-permute-done.1.refs_2_), channel_id=1, source_target_pairs={{0,1},{1,0},{2,3},{3,2},{4,5},{5,4},{6,7},{7,6},{8,9},{9,8},{10,11... | collective-permute-start | bytes 786440 | tf_op jit(solution)/shard_map/ppermute | solution.py:250
  32.5 2.7 %collective-permute-start.11 = (f32[256,256]{1,0:T(8,128)S(1)}, f32[256,256]{1,0:T(8,128)S(1)}, u32[]{:S(2)}, u32[]{:S(2)}) collective-permute-start(f32[256,256]{1,0:T(8,128)S(1)} %collective-permute-done.10.refs_4_), channel_id=1, source_target_pairs={{0,1},{1,0},{2,3},{3,2},{4,5},{5,4},{6,7},{7,6},{8,9},{9,8},{10,11... | collective-permute-start | bytes 786440 | tf_op jit(solution)/shard_map/ppermute | solution.py:250
  32.5 2.7 %collective-permute-start.13 = (f32[256,256]{1,0:T(8,128)S(1)}, f32[256,256]{1,0:T(8,128)S(1)}, u32[]{:S(2)}, u32[]{:S(2)}) collective-permute-start(f32[256,256]{1,0:T(8,128)S(1)} %collective-permute-done.12.refs_6_), channel_id=1, source_target_pairs={{0,1},{1,0},{2,3},{3,2},{4,5},{5,4},{6,7},{7,6},{8,9},{9,8},{10,11... | collective-permute-start | bytes 786440 | tf_op jit(solution)/shard_map/ppermute | solution.py:250
  34.6 4.4 %collective-permute-start.14 = (f32[256,256]{1,0:T(8,128)S(1)}, f32[256,256]{1,0:T(8,128)S(1)}, u32[]{:S(2)}, u32[]{:S(2)}) collective-permute-start(f32[256,256]{1,0:T(8,128)S(1)} %collective-permute-done.2.refs_0_), channel_id=1, source_target_pairs={{0,1},{1,0},{2,3},{3,2},{4,5},{5,4},{6,7},{7,6},{8,9},{9,8},{10,11... | collective-permute-start | bytes 786440 | tf_op jit(solution)/shard_map/ppermute | solution.py:250
  34.7 4.4 %collective-permute-start.15 = (f32[256,256]{1,0:T(8,128)S(1)}, f32[256,256]{1,0:T(8,128)S(1)}, u32[]{:S(2)}, u32[]{:S(2)}) collective-permute-start(f32[256,256]{1,0:T(8,128)S(1)} %collective-permute-done.3.refs_2_), channel_id=1, source_target_pairs={{0,1},{1,0},{2,3},{3,2},{4,5},{5,4},{6,7},{7,6},{8,9},{9,8},{10,11... | collective-permute-start | bytes 786440 | tf_op jit(solution)/shard_map/ppermute | solution.py:250
  41.6 9.7 %collective-permute-start.16 = (f32[264,256]{1,0:T(8,128)S(1)}, f32[264,256]{1,0:T(8,128)S(1)}, u32[]{:S(2)}, u32[]{:S(2)}) collective-permute-start(f32[264,256]{1,0:T(8,128)S(1)} %get-tuple-element.68), channel_id=1, source_target_pairs={{0,16},{2,18},{4,20},{6,22},{16,24},{18,26},{20,28},{22,30},{24,8}... | collective-permute-start | bytes 811016 | tf_op jit(solution)/shard_map/ppermute | solution.py:254
  44.4 14.5 %collective-permute-start.18 = (f32[264,256]{1,0:T(8,128)S(1)}, f32[264,256]{1,0:T(8,128)S(1)}, u32[]{:S(2)}, u32[]{:S(2)}) collective-permute-start(f32[264,256]{1,0:T(8,128)S(1)} %get-tuple-element.69), channel_id=1, source_target_pairs={{0,8},{2,10},{4,12},{6,14},{16,0},{18,2},{20,4},{22,6},{24,16},{26... | collective-permute-start | bytes 811016 | tf_op jit(solution)/shard_map/ppermute | solution.py:254
  51.4 12.4 %collective-permute-start.17 = (f32[264,256]{1,0:T(8,128)S(1)}, f32[264,256]{1,0:T(8,128)S(1)}, u32[]{:S(2)}, u32[]{:S(2)}) collective-permute-start(f32[264,256]{1,0:T(8,128)S(1)} %add.3), channel_id=1, source_target_pairs={{0,16},{2,18},{4,20},{6,22},{16,24},{18,26},{20,28},{22,30},{24,8}... | collective-permute-start | bytes 811016 | tf_op jit(solution)/shard_map/ppermute | solution.py:254
  64.6 8.4 %collective-permute-start.19 = (f32[264,256]{1,0:T(8,128)S(1)}, f32[264,256]{1,0:T(8,128)S(1)}, u32[]{:S(2)}, u32[]{:S(2)}) collective-permute-start(f32[264,256]{1,0:T(8,128)S(1)} %finish.1.refs_0_), channel_id=1, source_target_pairs={{0,16},{2,18},{4,20},{6,22},{16,24},{18,26},{20,28},{22,30},{24,8}... | collective-permute-start | bytes 811016 | tf_op jit(solution)/shard_map/ppermute | solution.py:254
  66.3 8.5 %collective-permute-start.21 = (f32[264,256]{1,0:T(8,128)S(1)}, f32[264,256]{1,0:T(8,128)S(1)}, u32[]{:S(2)}, u32[]{:S(2)}) collective-permute-start(f32[264,256]{1,0:T(8,128)S(1)} %finish.1.refs_0_), channel_id=1, source_target_pairs={{0,2},{2,0},{4,6},{6,4},{8,10},{10,8},{12,14},{14,12},{16,18},{18,... | collective-permute-start | bytes 811016 | tf_op jit(solution)/shard_map/ppermute | solution.py:247
  67.8 7.1 %collective-permute-start.22 = (f32[264,256]{1,0:T(8,128)S(1)}, f32[264,256]{1,0:T(8,128)S(1)}, u32[]{:S(2)}, u32[]{:S(2)}) collective-permute-start(f32[264,256]{1,0:T(8,128)S(1)} %finish.1.refs_0_), channel_id=1, source_target_pairs={{0,4},{2,6},{4,0},{6,2},{8,12},{10,14},{12,8},{14,10},{16,20},{18,... | collective-permute-start | bytes 811016 | tf_op jit(solution)/shard_map/ppermute | solution.py:247
  73.0 7.5 %collective-permute-start.20 = (f32[264,256]{1,0:T(8,128)S(1)}, f32[264,256]{1,0:T(8,128)S(1)}, u32[]{:S(2)}, u32[]{:S(2)}) collective-permute-start(f32[264,256]{1,0:T(8,128)S(1)} %collective-permute-done.19.refs_1_), channel_id=1, source_target_pairs={{0,16},{2,18},{4,20},{6,22},{16,24},{18,26},{20,28},{22,30},{24,8}... | collective-permute-start | bytes 811016 | tf_op jit(solution)/shard_map/ppermute | solution.py:254
  74.9 7.7 %collective-permute-start.23 = (f32[264,256]{1,0:T(8,128)S(1)}, f32[264,256]{1,0:T(8,128)S(1)}, u32[]{:S(2)}, u32[]{:S(2)}) collective-permute-start(f32[264,256]{1,0:T(8,128)S(1)} %collective-permute-done.21.refs_4_), channel_id=1, source_target_pairs={{0,4},{2,6},{4,0},{6,2},{8,12},{10,14},{12,8},{14,10},{16,20},{18,... | collective-permute-start | bytes 811016 | tf_op jit(solution)/shard_map/ppermute | solution.py:247
  76.4 7.7 %collective-permute-start.27 = (f32[264,256]{1,0:T(8,128)S(1)}, f32[264,256]{1,0:T(8,128)S(1)}, u32[]{:S(2)}, u32[]{:S(2)}) collective-permute-start(f32[264,256]{1,0:T(8,128)S(1)} %collective-permute-done.19.refs_1_), channel_id=1, source_target_pairs={{0,2},{2,0},{4,6},{6,4},{8,10},{10,8},{12,14},{14,12},{16,18},{18,... | collective-permute-start | bytes 811016 | tf_op jit(solution)/shard_map/ppermute | solution.py:247
  80.4 7.5 %collective-permute-start.26 = (f32[264,256]{1,0:T(8,128)S(1)}, f32[264,256]{1,0:T(8,128)S(1)}, u32[]{:S(2)}, u32[]{:S(2)}) collective-permute-start(f32[264,256]{1,0:T(8,128)S(1)} %finish.1.refs_0_), channel_id=1, source_target_pairs={{0,8},{2,10},{4,12},{6,14},{16,0},{18,2},{20,4},{22,6},{24,16},{26... | collective-permute-start | bytes 811016 | tf_op jit(solution)/shard_map/ppermute | solution.py:254
  82.6 6.9 %collective-permute-start.24 = (f32[264,256]{1,0:T(8,128)S(1)}, f32[264,256]{1,0:T(8,128)S(1)}, u32[]{:S(2)}, u32[]{:S(2)}) collective-permute-start(f32[264,256]{1,0:T(8,128)S(1)} %collective-permute-done.19.refs_1_), channel_id=1, source_target_pairs={{0,4},{2,6},{4,0},{6,2},{8,12},{10,14},{12,8},{14,10},{16,20},{18,... | collective-permute-start | bytes 811016 | tf_op jit(solution)/shard_map/ppermute | solution.py:247
  84.1 7.2 %collective-permute-start.28 = (f32[264,256]{1,0:T(8,128)S(1)}, f32[264,256]{1,0:T(8,128)S(1)}, u32[]{:S(2)}, u32[]{:S(2)}) collective-permute-start(f32[264,256]{1,0:T(8,128)S(1)} %collective-permute-done.20.refs_2_), channel_id=1, source_target_pairs={{0,2},{2,0},{4,6},{6,4},{8,10},{10,8},{12,14},{14,12},{16,18},{18,... | collective-permute-start | bytes 811016 | tf_op jit(solution)/shard_map/ppermute | solution.py:247
  87.9 6.5 %collective-permute-start.32 = (f32[264,256]{1,0:T(8,128)S(1)}, f32[264,256]{1,0:T(8,128)S(1)}, u32[]{:S(2)}, u32[]{:S(2)}) collective-permute-start(f32[264,256]{1,0:T(8,128)S(1)} %collective-permute-done.23.refs_6_), channel_id=1, source_target_pairs={{0,16},{2,18},{4,20},{6,22},{16,24},{18,26},{20,28},{22,30},{24,8}... | collective-permute-start | bytes 811016 | tf_op jit(solution)/shard_map/ppermute | solution.py:254
  89.5 9.9 %collective-permute-start.25 = (f32[264,256]{1,0:T(8,128)S(1)}, f32[264,256]{1,0:T(8,128)S(1)}, u32[]{:S(2)}, u32[]{:S(2)}) collective-permute-start(f32[264,256]{1,0:T(8,128)S(1)} %collective-permute-done.20.refs_2_), channel_id=1, source_target_pairs={{0,4},{2,6},{4,0},{6,2},{8,12},{10,14},{12,8},{14,10},{16,20},{18,... | collective-permute-start | bytes 811016 | tf_op jit(solution)/shard_map/ppermute | solution.py:247
  91.3 9.6 %collective-permute-start.29 = (f32[264,256]{1,0:T(8,128)S(1)}, f32[264,256]{1,0:T(8,128)S(1)}, u32[]{:S(2)}, u32[]{:S(2)}) collective-permute-start(f32[264,256]{1,0:T(8,128)S(1)} %collective-permute-done.26.refs_3_), channel_id=1, source_target_pairs={{0,2},{2,0},{4,6},{6,4},{8,10},{10,8},{12,14},{14,12},{16,18},{18,... | collective-permute-start | bytes 811016 | tf_op jit(solution)/shard_map/ppermute | solution.py:247
  94.4 11.6 %collective-permute-start.33 = (f32[264,256]{1,0:T(8,128)S(1)}, f32[264,256]{1,0:T(8,128)S(1)}, u32[]{:S(2)}, u32[]{:S(2)}) collective-permute-start(f32[264,256]{1,0:T(8,128)S(1)} %collective-permute-done.23.refs_6_), channel_id=1, source_target_pairs={{0,8},{2,10},{4,12},{6,14},{16,0},{18,2},{20,4},{22,6},{24,16},{26... | collective-permute-start | bytes 811016 | tf_op jit(solution)/shard_map/ppermute | solution.py:254
  99.4 6.6 %collective-permute-start.31 = (f32[264,256]{1,0:T(8,128)S(1)}, f32[264,256]{1,0:T(8,128)S(1)}, u32[]{:S(2)}, u32[]{:S(2)}) collective-permute-start(f32[264,256]{1,0:T(8,128)S(1)} %collective-permute-done.26.refs_3_), channel_id=1, source_target_pairs={{0,4},{2,6},{4,0},{6,2},{8,12},{10,14},{12,8},{14,10},{16,20},{18,... | collective-permute-start | bytes 811016 | tf_op jit(solution)/shard_map/ppermute | solution.py:247
  100.9 6.5 %collective-permute-start.30 = (f32[264,256]{1,0:T(8,128)S(1)}, f32[264,256]{1,0:T(8,128)S(1)}, u32[]{:S(2)}, u32[]{:S(2)}) collective-permute-start(f32[264,256]{1,0:T(8,128)S(1)} %collective-permute-done.25.refs_0_), channel_id=1, source_target_pairs={{0,2},{2,0},{4,6},{6,4},{8,10},{10,8},{12,14},{14,12},{16,18},{18,... | collective-permute-start | bytes 811016 | tf_op jit(solution)/shard_map/ppermute | solution.py:247

commit v7 on v6

--- a/solution.py
+++ b/solution.py
@@ -107,9 +107,9 @@
     )
 
 
-def lse_kernel(cores, every, *refs):
+def lse_kernel(cores, every, x0_ref, y1_ref, *refs):
     pair_refs = refs[:cores]
-    lse_ref, evidence_ref = refs[cores:]
+    lse_ref, evidence_ref, pack_x_ref, pack_y_ref = refs[cores:]
     half = lse_ref.shape[1]
     top = functools.reduce(jnp.maximum, [p[0:1, :] for p in pair_refs])
     total = functools.reduce(jnp.add, [p[1:2, :] * jnp.exp(p[0:1, :] - top) for p in pair_refs])
@@ -119,67 +119,144 @@
         evidence_ref[k : k + 1, :] = evidence[:, k * LANES : (k + 1) * LANES]
     for i in range(2 * cores):
         lse_ref[i : i + 1, :] = lse[:, i * half : (i + 1) * half]
-
-
-def add_block(twice, norm, x, lse, acc_ref, cnt_ref, first):
+    for piece_ref, pack_ref in ((x0_ref, pack_x_ref), (y1_ref, pack_y_ref)):
+        pack_ref[0:half, :] = piece_ref[...]
+        pack_ref[half:, :] = jnp.zeros_like(pack_ref[half:, :])
+        pack_ref[half : half + 2 * cores, 0:half] = lse_ref[...]
+
+
+def weigh(twice, norm, x, lse, lanes):
     dots = lax.dot_general(twice, x, NT, preferred_element_type=jnp.float32)
     score = dots - widen(norm, x.shape[0])
     resp = jnp.exp(score - lse).astype(jnp.bfloat16)
     part = lax.dot_general(resp, x, NN, preferred_element_type=jnp.float32)
     wide = resp.astype(jnp.float32)
-    lanes = cnt_ref.shape[1]
     counted = functools.reduce(
         jnp.add, [wide[:, k : k + lanes] for k in range(0, x.shape[0], lanes)]
     )
-    if first:
-        acc_ref[...] = part
-        cnt_ref[...] = counted
-    else:
-        acc_ref[...] += part
-        cnt_ref[...] += counted
-
-
-def add_pieces(cores, where_ref, twice_ref, norm_ref, refs, whose, acc_ref, cnt_ref):
-    for k, (lse_ref, part) in enumerate(whose):
-        for rc in range(cores):
-            x = refs[k * cores + rc][...].astype(jnp.bfloat16)
-            lse = lse_ref[pl.ds(2 * (where_ref[1] ^ rc) + part, 1), :]
-            add_block(twice_ref[...], norm_ref[...], x, lse, acc_ref, cnt_ref, False)
+    return part, counted
 
 
 def own_kernel(cores, points_ref, twice_ref, norm_ref, lse_ref, acc_ref, cnt_ref):
     half = points_ref.shape[0] // (2 * cores)
     for i in range(2 * cores):
         x = points_ref[i * half : (i + 1) * half, :]
-        add_block(twice_ref[...], norm_ref[...], x, lse_ref[i : i + 1, :], acc_ref, cnt_ref, i == 0)
-
-
-def near_kernel(cores, where_ref, twice_ref, norm_ref, acc_in_ref, cnt_in_ref, lse_x_ref, lse_y_ref, *refs):
-    acc_ref, cnt_ref = refs[4 * cores :]
-    acc_ref[...] = acc_in_ref[...]
-    cnt_ref[...] = cnt_in_ref[...]
-    whose = ((lse_x_ref, 0), (lse_y_ref, 1), (lse_x_ref, 1), (lse_y_ref, 0))
-    add_pieces(cores, where_ref, twice_ref, norm_ref, refs, whose, acc_ref, cnt_ref)
-
-
-def far_kernel(cores, order, where_ref, twice_ref, norm_ref, acc_in_ref, cnt_in_ref, lse_ref, *refs):
-    lines = len(order)
-    out_refs = refs[2 * cores : 2 * cores + lines]
-    acc_ref, cnt_ref = refs[2 * cores + lines :]
-    acc_ref[...] = acc_in_ref[...]
-    cnt_ref[...] = cnt_in_ref[...]
-    whose = ((lse_ref, 0), (lse_ref, 1))
-    add_pieces(cores, where_ref, twice_ref, norm_ref, refs, whose, acc_ref, cnt_ref)
-    line = lax.div(where_ref[0], 4)
-    width = acc_ref.shape[1]
-    size = acc_ref.shape[0] // lines
-    for s in range(lines):
-        start = pl.multiple_of(ahead(order, line, s) * size, size)
-        out_refs[s][0:size, :] = acc_ref[pl.ds(start, size), :]
-        turned = jnp.sum(cnt_ref[pl.ds(start, size), :].T, axis=0, keepdims=True)
-        if size < width:
-            turned = jnp.concatenate([turned, jnp.zeros((1, width - size), jnp.float32)], axis=1)
-        out_refs[s][size : size + 8, :] = jnp.broadcast_to(turned, (8, width))
+        part, counted = weigh(
+            twice_ref[...], norm_ref[...], x, lse_ref[i : i + 1, :], cnt_ref.shape[1]
+        )
+        if i == 0:
+            acc_ref[...] = part
+            cnt_ref[...] = counted
+        else:
+            acc_ref[...] += part
+            cnt_ref[...] += counted
+
+
+def near_rows(cores, half, core, refs, d0_ref, d1_ref):
+    whose = ((d1_ref, 0), (d0_ref, 1), (d1_ref, 1), (d0_ref, 0))
+    for k, (tail_ref, part) in enumerate(whose):
+        for rc in range(cores):
+            at = half + 2 * (core ^ rc) + part
+            yield refs[k * cores + rc], (lambda at=at, tail_ref=tail_ref: tail_ref[pl.ds(at, 1), :][:, 0:half])
+
+
+def far_rows(cores, half, core, refs, lse_ref):
+    for part in range(2):
+        for rc in range(cores):
+            at = 2 * (core ^ rc) + part
+            yield refs[part * cores + rc], (lambda at=at: lse_ref[pl.ds(at, 1), :])
+
+
+def add_rows(rows, half, twice, norm, acc, cnt):
+    for x_ref, lse in rows:
+        part, counted = weigh(twice, norm, x_ref[0:half, :].astype(jnp.bfloat16), lse(), cnt.shape[1])
+        acc, cnt = acc + part, cnt + counted
+    return acc, cnt
+
+
+def store_sums(out_ref, acc, cnt):
+    size, width = acc.shape
+    turned = jnp.sum(cnt.T, axis=0, keepdims=True)
+    if size < width:
+        turned = jnp.concatenate([turned, jnp.zeros((1, width - size), jnp.float32)], axis=1)
+    out_ref[0:size, :] = acc
+    out_ref[size : size + 8, :] = jnp.broadcast_to(turned, (8, width))
+
+
+def lead_kernel(cores, order, half, where_ref, twice_ref, norm_ref, acc_ref, cnt_ref, *refs):
+    out_acc_ref, out_cnt_ref = refs[-2:]
+    near, (d0_ref, d1_ref) = refs[: 4 * cores], refs[4 * cores : 4 * cores + 2]
+    size = out_acc_ref.shape[0]
+    place = ahead(order, lax.div(where_ref[0], 4), len(order) // 2)
+    at = pl.ds(pl.multiple_of(place * size, size), size)
+    out_acc_ref[...], out_cnt_ref[...] = add_rows(
+        near_rows(cores, half, where_ref[1], near, d0_ref, d1_ref),
+        half,
+        twice_ref[at, :],
+        norm_ref[at, :],
+        acc_ref[at, :],
+        cnt_ref[at, :],
+    )
+
+
+def block_sums(cores, order, half, steps, where_ref, twice_ref, norm_ref, acc_ref, cnt_ref, lse_ref, near, far, out_ref):
+    size = out_ref.shape[0] - 8
+    place = ahead(order, lax.div(where_ref[0], 4), steps)
+    at = pl.ds(pl.multiple_of(place * size, size), size)
+    twice, norm = twice_ref[at, :], norm_ref[at, :]
+    acc, cnt = add_rows(
+        near_rows(cores, half, where_ref[1], near, far[0], far[cores]),
+        half,
+        twice,
+        norm,
+        acc_ref[at, :],
+        cnt_ref[at, :],
+    )
+    acc, cnt = add_rows(far_rows(cores, half, where_ref[1], far, lse_ref), half, twice, norm, acc, cnt)
+    store_sums(out_ref, acc, cnt)
+
+
+def first_kernel(cores, order, half, ahead_steps, where_ref, twice_ref, norm_ref, acc_ref, cnt_ref, lse_ref, lead_acc_ref, lead_cnt_ref, *refs):
+    near, far = refs[: 4 * cores], refs[4 * cores : 6 * cores]
+    out_refs = refs[6 * cores :]
+    size = lead_acc_ref.shape[0]
+    place = ahead(order, lax.div(where_ref[0], 4), len(order) // 2)
+    at = pl.ds(pl.multiple_of(place * size, size), size)
+    acc, cnt = add_rows(
+        far_rows(cores, half, where_ref[1], far, lse_ref),
+        half,
+        twice_ref[at, :],
+        norm_ref[at, :],
+        lead_acc_ref[...],
+        lead_cnt_ref[...],
+    )
+    store_sums(out_refs[0], acc, cnt)
+
+    @pl.when(lax.rem(where_ref[1], 2) == 1)
+    def _():
+        for steps, out_ref in zip(ahead_steps, out_refs[1:]):
+            block_sums(cores, order, half, steps, where_ref, twice_ref, norm_ref, acc_ref, cnt_ref, lse_ref, near, far, out_ref)
+
+
+def rest_kernel(cores, order, half, made, missing, where_ref, twice_ref, norm_ref, acc_ref, cnt_ref, lse_ref, *refs):
+    near, far = refs[: 4 * cores], refs[4 * cores : 6 * cores]
+    made_refs = refs[6 * cores : 6 * cores + len(made)]
+    out_refs = refs[6 * cores + len(made) :]
+    given = (where_ref, twice_ref, norm_ref, acc_ref, cnt_ref, lse_ref, near, far)
+    odd = lax.rem(where_ref[1], 2) == 1
+
+    @pl.when(odd)
+    def _():
+        for made_ref, out_ref in zip(made_refs, out_refs):
+            out_ref[...] = made_ref[...]
+
+    @pl.when(jnp.logical_not(odd))
+    def _():
+        for steps, out_ref in zip(made, out_refs):
+            block_sums(cores, order, half, steps, *given, out_ref)
+
+    for steps, out_ref in zip(missing, out_refs[len(made) :]):
+        block_sums(cores, order, half, steps, *given, out_ref)
 
 
 def ahead(order, line, steps):
@@ -269,66 +346,77 @@
 
     pair, twice, norm = stats(where, points, centroids, lines)
     pair, x0, y1 = lax.optimization_barrier((pair, x0, y1))
-    d0, d1 = flip(x0, 2), flip(y1, 1)
     pairs = [pair] + [flip_core(pair, rc) for rc in range(1, cores)]
-    lse, log_evidence = call(
+    tail = max(8, 2 * cores)
+    lse, log_evidence, pack_x, pack_y = call(
         functools.partial(lse_kernel, cores, local_cent * cores),
-        (f32(2 * cores, half), f32(rows // LANES, LANES)),
-        [VMEM] * cores,
-        pairs,
+        (f32(2 * cores, half), f32(rows // LANES, LANES), f32(half + tail, width), f32(half + tail, width)),
+        [VMEM] * (2 + cores),
+        (x0, y1, *pairs),
         "lse",
     )
-    lse_x, lse_y, lse_d = flip(lse, 1), flip(lse, 2), flip(lse, 3)
-
-    acc_shape, cnt_shape = f32(share, width), f32(share, min(LANES, half))
+    d0, d1 = flip(pack_x, 2), flip(pack_y, 1)
+
+    lanes = min(LANES, half)
     acc, cnt = call(
         functools.partial(own_kernel, cores),
-        (acc_shape, cnt_shape),
+        (f32(share, width), f32(share, lanes)),
         [VMEM] * 4,
         (points, twice, norm, lse),
         "own",
         flops=4 * share * width * rows,
     )
     near = with_siblings((x0, y1, x1, y0))
-    d0, d1, acc, cnt, lse_x, lse_y, lse_d = lax.optimization_barrier(
-        (d0, d1, acc, cnt, lse_x, lse_y, lse_d)
-    )
-    acc, cnt = call(
-        functools.partial(near_kernel, cores),
-        (acc_shape, cnt_shape),
+    lse, acc, cnt = lax.optimization_barrier((lse, acc, cnt))
+    lse_d = flip(lse, 3)
+    near, d0, d1, acc, cnt, lse_d = lax.optimization_barrier((near, d0, d1, acc, cnt, lse_d))
+    lead = call(
+        functools.partial(lead_kernel, cores, order, half),
+        (f32(size, width), f32(size, lanes)),
         [SMEM] + [VMEM] * (6 + 4 * cores),
-        (where, twice, norm, acc, cnt, lse_x, lse_y, *near),
-        "near",
-        flops=4 * share * width * 2 * rows,
-        aliases={3: 0, 4: 1},
-    )
-    sums = call(
-        functools.partial(far_kernel, cores, order),
-        [f32(size + 8, width)] * lines,
-        [SMEM] + [VMEM] * (5 + 2 * cores),
-        (where, twice, norm, acc, cnt, lse_d, *with_siblings((d0, d1))),
-        "far",
-        scratch=[
-            pltpu.VMEM((share, width), jnp.float32),
-            pltpu.VMEM((share, min(LANES, half)), jnp.float32),
-        ],
-        flops=4 * share * width * rows,
-    )
-
-    def reduced(way, steps):
-        moving = sums[way * steps % lines]
+        (where, twice, norm, acc, cnt, *near, d0, d1),
+        "lead",
+        flops=4 * size * width * 2 * rows,
+    )
+    given = (where, twice, norm, acc, cnt, lse_d)
+    rows_given = (*near, *with_siblings((d0, d1)))
+    block_sum = f32(size + 8, width)
+    turn = lines // 2
+    others = [s % lines for s in range(-1, -turn, -1)] + list(range(turn - 1, -1, -1))
+    made, missing = others[:2], others[2:]
+    first, *made_sums = call(
+        functools.partial(first_kernel, cores, order, half, made),
+        [block_sum] * 3,
+        [SMEM] + [VMEM] * (7 + 6 * cores),
+        (*given, *lead, *rows_given),
+        "first",
+        flops=4 * size * width * rows,
+    )
+    rest = call(
+        functools.partial(rest_kernel, cores, order, half, made, missing),
+        [block_sum] * (lines - 1),
+        [SMEM] + [VMEM] * (7 + 6 * cores),
+        (*given, *rows_given, *made_sums),
+        "rest",
+        flops=4 * (share - size) * width * 3 * rows,
+    )
+    sums = {turn: first, **dict(zip(others, rest))}
+
+    def reduced(way, steps, moving):
         for s in range(steps, 0, -1):
             moving = ring(moving, way)
             if s > 1:
                 mine = sums[way * (s - 1) % lines]
-                moving = call(add_kernel, f32(size + 8, width), [VMEM] * 2, (mine, moving), "add")
+                moving = call(add_kernel, block_sum, [VMEM] * 2, (mine, moving), "add")
         return moving
 
+    ahead_sum = reduced(1, turn, first)
+    behind_sum = reduced(-1, turn - 1, sums[(1 - turn) % lines])
     done = call(
         finish_kernel,
-        f32(size + 8, width),
+        block_sum,
         [SMEM] + [VMEM] * 4,
-        (where, twice, sums[0], reduced(1, lines // 2), reduced(-1, lines // 2 - 1)),
+        (where, twice, sums[0], ahead_sum, behind_sum),
         "finish",
     )
 

time: 110 us -> 107 us (0.973)
  starting transfers between devices: 46.7 us -> 39.2 us
  waiting for transfers between devices: 37.6 us -> 40.2 us
  Pallas kernels: 21.6 us -> 23.7 us
    ppermute x19 -> x17, starting transfers between devices: 27.4 us -> 23.2 us  [flip(): return lax.ppermute(x, 'dp', [(i, i ^ bits) for i in range(n)])]
    ppermute x8, starting transfers between devices: 18 us -> 14.4 us  [ring(): lax.ppermute(x, 'dp', [(4 * a + i, 4 * b + i) for a, b in pairs for i in...]
    ppermute x7, waiting for transfers between devices: 0.02 us -> 2.44 us  [flip_core(): return lax.ppermute(x, 'cent', [(i, i ^ bits) for i in range(cores)])]
    pallas_call x11 -> x12, Pallas kernels: 21.6 us -> 23.7 us  [call(): pl.pallas_call(kernel, out_shape=out_shape, in_specs=in_specs, out_specs=...]
    ppermute x19 -> x17, waiting for transfers between devices: 11.7 us -> 12.2 us  [flip(): return lax.ppermute(x, 'dp', [(i, i ^ bits) for i in range(n)])]
    unnamed x6 -> x8, local copies, waits for them, and re-layouts: 2.64 us -> 2.64 us
  transfers between devices with their start and end apart: 34 -> 32, of which waited for: 13 -> 16; matrix products, arithmetic and copies ran while one was open for 0% -> 0% of each run, Pallas kernels for 14% -> 17%
where the time goes in v7:
time: 107 us
  waiting for transfers between devices  40.2 us (38%)
  starting transfers between devices  39.2 us (37%)
  Pallas kernels  23.7 us (22%)
  local copies, waits for them, and re-layouts  2.64 us (2%)
    ppermute x8, waiting for transfers between devices, ring(): lax.ppermute(x, 'dp', [(4 * a + i, 4 * b + i) for a, b in pairs for i in...  25.6 us
    pallas_call x12, Pallas kernels, call(): pl.pallas_call(kernel, out_shape=out_shape, in_specs=in_specs, out_specs=...  23.7 us
    ppermute x17, starting transfers between devices, flip(): return lax.ppermute(x, 'dp', [(i, i ^ bits) for i in range(n)])  23.2 us
    ppermute x8, starting transfers between devices, ring(): lax.ppermute(x, 'dp', [(4 * a + i, 4 * b + i) for a, b in pairs for i in...  14.4 us
    ppermute x17, waiting for transfers between devices, flip(): return lax.ppermute(x, 'dp', [(i, i ^ bits) for i in range(n)])  12.2 us
    unnamed x8, local copies, waits for them, and re-layouts  2.64 us
    ppermute x7, waiting for transfers between devices, flip_core(): return lax.ppermute(x, 'cent', [(i, i ^ bits) for i in range(cores)])  2.44 us
  transfers between devices with their start and end apart: 32, of which 16 were waited for; matrix products, arithmetic and copies ran while one was open for 0% of the time, Pallas kernels for 17%

profile of v7, /device:TPU:0, one launch (start us, length us, event | category | flops | bytes accessed | tf_op | source)
XLA Modules:
  0.0 106.7 jit_solution(12118978932533858354)
XLA Ops:
  0.7 1.0 copy-done.1
  1.8 0.6 open.1
  2.4 3.0 %collective-permute-start.1 = (f32[256,256]{1,0:T(8,128)S(1)}, f32[256,256]{1,0:T(8,128)S(1)}, u32[]{:S(2)}, u32[]{:S(2)}) collective-permute-start(f32[256,256]{1,0:T(8,128)S(1)} %get-tuple-element.63), channel_id=1, source_target_pairs={{0,4},{2,6},{4,0},{6,2},{8,12},{10,14},{12,8},{14,10},{16,20},{18,... | collective-permute-start | bytes 786440 | tf_op jit(solution)/shard_map/ppermute | solution.py:324
  5.4 1.5 %collective-permute-start.4 = (f32[256,256]{1,0:T(8,128)S(1)}, f32[256,256]{1,0:T(8,128)S(1)}, u32[]{:S(2)}, u32[]{:S(2)}) collective-permute-start(f32[256,256]{1,0:T(8,128)S(1)} %get-tuple-element.63), channel_id=1, source_target_pairs={{0,2},{2,0},{4,6},{6,4},{8,10},{10,8},{12,14},{14,12},{16,18},{18,... | collective-permute-start | bytes 786440 | tf_op jit(solution)/shard_map/ppermute | solution.py:324
  6.9 0.5 collective-permute-start
  7.5 1.6 %copy-done.3 = bf16[4096,256]{1,0:T(8,128)(2,1)S(1)} copy-done((bf16[4096,256]{1,0:T(8,128)(2,1)S(1)}, bf16[4096,256]{1,0:T(8,128)(2,1)}, u32[]{:S(2)}) %copy-start.3) | copy-done | bytes 2097176
  9.1 5.9 %stats.1 = (f32[2,1024]{1,0:T(2,128)S(1)}, bf16[1024,256]{1,0:T(8,128)(2,1)S(1)}, f32[1024,128]{1,0:T(8,128)S(1)}) custom-call(s32[2]{0:T(128)S(1)} %pad_add_fusion.where_ref, bf16[1024,256]{1,0:T(8,128)(2,1)S(1)} %copy-done.1, bf16[4096,256]{1,0:T(8,128)(2,1)S(1)} %copy-done.3), custom_call_target="tpu_custom_call" | custom-call | flops 4294967296 | bytes 2621448 | tf_op jit(solution)/shard_map/stats/pallas_call | solution.py:27
  15.0 3.8 %collective-permute-done.x0_ref.refs_0_ = f32[256,256]{1,0:T(8,128)S(1)} collective-permute-done((f32[256,256]{1,0:T(8,128)S(1)}, f32[256,256]{1,0:T(8,128)S(1)}, u32[]{:S(2)}, u32[]{:S(2)}) %collective-permute-start) | collective-permute-done | bytes 262176 | tf_op jit(solution)/shard_map/ppermute | solution.py:324
  18.8 0.5 collective-permute-start.8
  19.3 1.0 collective-permute-done.8.refs_1_
  20.3 0.6 lse.1
  21.0 1.5 %collective-permute-start.10 = (f32[264,256]{1,0:T(8,128)S(1)}, f32[264,256]{1,0:T(8,128)S(1)}, u32[]{:S(2)}, u32[]{:S(2)}) collective-permute-start(f32[264,256]{1,0:T(8,128)S(1)} %get-tuple-element.68), channel_id=1, source_target_pairs={{0,2},{2,0},{4,6},{6,4},{8,10},{10,8},{12,14},{14,12},{16,18},{18,... | collective-permute-start | bytes 811016 | tf_op jit(solution)/shard_map/ppermute | solution.py:324
  23.0 1.5 %own.1 = (f32[1024,256]{1,0:T(8,128)S(1)}, f32[1024,128]{1,0:T(8,128)S(1)}) custom-call(bf16[1024,256]{1,0:T(8,128)(2,1)S(1)} %copy-done.2, bf16[1024,256]{1,0:T(8,128)(2,1)S(1)} %get-tuple-element.59.twice_ref, f32[1024,128]{1,0:T(8,128)S(1)} %get-tuple-element.60.norm_ref, f32[4,256]{1,0:T(4,128)S(1)} %get-tuple-element.74.lse_ref), custom_call_target="tpu_custom_call" | custom-call | flops 1073741824 | bytes 1576960 | tf_op jit(solution)/shard_map/own/pallas_call | solution.py:27
  24.5 1.6 %collective-permute-start.11 = (f32[4,256]{1,0:T(4,128)S(1)}, f32[4,256]{1,0:T(4,128)S(1)}, u32[]{:S(2)}, u32[]{:S(2)}) collective-permute-start(f32[4,256]{1,0:T(4,128)S(1)} %get-tuple-element.74.lse_ref), channel_id=1, source_target_pairs={{0,6},{2,4},{4,2},{6,0},{8,14},{10,12},{12,10},{14,8},{16,22},{18,... | collective-permute-start | bytes 12296 | tf_op jit(solution)/shard_map/ppermute | solution.py:324
  26.1 3.4 %collective-permute-done.11.lse_ref = f32[4,256]{1,0:T(4,128)S(1)} collective-permute-done((f32[4,256]{1,0:T(4,128)S(1)}, f32[4,256]{1,0:T(4,128)S(1)}, u32[]{:S(2)}, u32[]{:S(2)}) %collective-permute-start.11) | collective-permute-done | bytes 4128 | tf_op jit(solution)/shard_map/ppermute | solution.py:324
  29.5 0.5 collective-permute-start.7
  30.0 1.0 collective-permute-done.5.refs_5_
  31.9 1.5 %lead.1 = (f32[256,256]{1,0:T(8,128)S(1)}, f32[256,128]{1,0:T(8,128)S(1)}) custom-call(s32[2]{0:T(128)S(1)} %pad_add_fusion.where_ref, bf16[1024,256]{1,0:T(8,128)(2,1)S(1)} %get-tuple-element.59.twice_ref, f32[1024,128]{1,0:T(8,128)S(1)} %get-tuple-element.60.norm_ref, f32[1024,256]{1,0:T(8,128)S(1)} %get-tuple-element.75.acc_ref, ...), custom_call_target="tpu_custom_call" | custom-call | flops 536870912 | bytes 5259272 | tf_op jit(solution)/shard_map/lead/pallas_call | solution.py:27
  33.5 1.9 %first.1 = (f32[264,256]{1,0:T(8,128)S(1)}, f32[264,256]{1,0:T(8,128)S(1)}, f32[264,256]{1,0:T(8,128)S(1)}) custom-call(s32[2]{0:T(128)S(1)} %pad_add_fusion.where_ref, bf16[1024,256]{1,0:T(8,128)(2,1)S(1)} %get-tuple-element.59.twice_ref, f32[1024,128]{1,0:T(8,128)S(1)} %get-tuple-element.60.norm_ref, f32[1024,256]{1,0:T(8,128)} %copy-done, ...), custom_call_target="tpu_custom_call" | custom-call | flops 268435456 | bytes 6197256 | tf_op jit(solution)/shard_map/first/pallas_call | solution.py:27
  35.4 2.8 %collective-permute-start.14 = (f32[264,256]{1,0:T(8,128)S(1)}, f32[264,256]{1,0:T(8,128)S(1)}, u32[]{:S(2)}, u32[]{:S(2)}) collective-permute-start(f32[264,256]{1,0:T(8,128)S(1)} %get-tuple-element.94), channel_id=1, source_target_pairs={{0,16},{2,18},{4,20},{6,22},{16,24},{18,26},{20,28},{22,30},{24,8}... | collective-permute-start | bytes 811016 | tf_op jit(solution)/shard_map/ppermute | solution.py:331
  38.2 5.1 %rest.1 = (f32[264,256]{1,0:T(8,128)S(1)}, f32[264,256]{1,0:T(8,128)S(1)}, f32[264,256]{1,0:T(8,128)S(1)}) custom-call(s32[2]{0:T(128)S(1)} %pad_add_fusion.where_ref, bf16[1024,256]{1,0:T(8,128)(2,1)S(1)} %get-tuple-element.59.twice_ref, f32[1024,128]{1,0:T(8,128)S(1)} %get-tuple-element.60.norm_ref, f32[1024,256]{1,0:T(8,128)} %copy-done, ...), custom_call_target="tpu_custom_call" | custom-call | flops 2415919104 | bytes 6344712 | tf_op jit(solution)/shard_map/rest/pallas_call | solution.py:27
  43.6 3.4 %collective-permute-start.15 = (f32[264,256]{1,0:T(8,128)S(1)}, f32[264,256]{1,0:T(8,128)S(1)}, u32[]{:S(2)}, u32[]{:S(2)}) collective-permute-start(f32[264,256]{1,0:T(8,128)S(1)} %add.3), channel_id=1, source_target_pairs={{0,16},{2,18},{4,20},{6,22},{16,24},{18,26},{20,28},{22,30},{24,8}... | collective-permute-start | bytes 811016 | tf_op jit(solution)/shard_map/ppermute | solution.py:331
  47.0 6.8 %collective-permute-done.16.second_ref = f32[264,256]{1,0:T(8,128)S(1)} collective-permute-done((f32[264,256]{1,0:T(8,128)S(1)}, f32[264,256]{1,0:T(8,128)S(1)}, u32[]{:S(2)}, u32[]{:S(2)}) %collective-permute-start.16) | collective-permute-done | bytes 270368 | tf_op jit(solution)/shard_map/ppermute | solution.py:331
  53.8 4.6 %collective-permute-done.15.first_ref = f32[264,256]{1,0:T(8,128)S(1)} collective-permute-done((f32[264,256]{1,0:T(8,128)S(1)}, f32[264,256]{1,0:T(8,128)S(1)}, u32[]{:S(2)}, u32[]{:S(2)}) %collective-permute-start.15) | collective-permute-done | bytes 270368 | tf_op jit(solution)/shard_map/ppermute | solution.py:331
  58.4 0.8 finish.1.refs_0_
  59.2 1.2 %collective-permute-start.17 = (f32[264,256]{1,0:T(8,128)S(1)}, f32[264,256]{1,0:T(8,128)S(1)}, u32[]{:S(2)}, u32[]{:S(2)}) collective-permute-start(f32[264,256]{1,0:T(8,128)S(1)} %finish.1.refs_0_), channel_id=1, source_target_pairs={{0,16},{2,18},{4,20},{6,22},{16,24},{18,26},{20,28},{22,30},{24,8}... | collective-permute-start | bytes 811016 | tf_op jit(solution)/shard_map/ppermute | solution.py:331
  60.3 1.5 %collective-permute-start.19 = (f32[264,256]{1,0:T(8,128)S(1)}, f32[264,256]{1,0:T(8,128)S(1)}, u32[]{:S(2)}, u32[]{:S(2)}) collective-permute-start(f32[264,256]{1,0:T(8,128)S(1)} %finish.1.refs_0_), channel_id=1, source_target_pairs={{0,2},{2,0},{4,6},{6,4},{8,10},{10,8},{12,14},{14,12},{16,18},{18,... | collective-permute-start | bytes 811016 | tf_op jit(solution)/shard_map/ppermute | solution.py:324
  61.8 1.4 %collective-permute-start.20 = (f32[264,256]{1,0:T(8,128)S(1)}, f32[264,256]{1,0:T(8,128)S(1)}, u32[]{:S(2)}, u32[]{:S(2)}) collective-permute-start(f32[264,256]{1,0:T(8,128)S(1)} %finish.1.refs_0_), channel_id=1, source_target_pairs={{0,4},{2,6},{4,0},{6,2},{8,12},{10,14},{12,8},{14,10},{16,20},{18,... | collective-permute-start | bytes 811016 | tf_op jit(solution)/shard_map/ppermute | solution.py:324
  63.2 4.5 %collective-permute-done.17.refs_1_ = f32[264,256]{1,0:T(8,128)S(1)} collective-permute-done((f32[264,256]{1,0:T(8,128)S(1)}, f32[264,256]{1,0:T(8,128)S(1)}, u32[]{:S(2)}, u32[]{:S(2)}) %collective-permute-start.17) | collective-permute-done | bytes 270368 | tf_op jit(solution)/shard_map/ppermute | solution.py:331
  67.7 2.3 %collective-permute-start.18 = (f32[264,256]{1,0:T(8,128)S(1)}, f32[264,256]{1,0:T(8,128)S(1)}, u32[]{:S(2)}, u32[]{:S(2)}) collective-permute-start(f32[264,256]{1,0:T(8,128)S(1)} %collective-permute-done.17.refs_1_), channel_id=1, source_target_pairs={{0,16},{2,18},{4,20},{6,22},{16,24},{18,26},{20,28},{22,30},{24,8}... | collective-permute-start | bytes 811016 | tf_op jit(solution)/shard_map/ppermute | solution.py:331
  70.1 1.5 %collective-permute-start.21 = (f32[264,256]{1,0:T(8,128)S(1)}, f32[264,256]{1,0:T(8,128)S(1)}, u32[]{:S(2)}, u32[]{:S(2)}) collective-permute-start(f32[264,256]{1,0:T(8,128)S(1)} %collective-permute-done.19.refs_4_), channel_id=1, source_target_pairs={{0,4},{2,6},{4,0},{6,2},{8,12},{10,14},{12,8},{14,10},{16,20},{18,... | collective-permute-start | bytes 811016 | tf_op jit(solution)/shard_map/ppermute | solution.py:324
  71.6 1.4 %collective-permute-start.25 = (f32[264,256]{1,0:T(8,128)S(1)}, f32[264,256]{1,0:T(8,128)S(1)}, u32[]{:S(2)}, u32[]{:S(2)}) collective-permute-start(f32[264,256]{1,0:T(8,128)S(1)} %collective-permute-done.17.refs_1_), channel_id=1, source_target_pairs={{0,2},{2,0},{4,6},{6,4},{8,10},{10,8},{12,14},{14,12},{16,18},{18,... | collective-permute-start | bytes 811016 | tf_op jit(solution)/shard_map/ppermute | solution.py:324
  73.0 2.6 %collective-permute-done.18.refs_2_ = f32[264,256]{1,0:T(8,128)S(1)} collective-permute-done((f32[264,256]{1,0:T(8,128)S(1)}, f32[264,256]{1,0:T(8,128)S(1)}, u32[]{:S(2)}, u32[]{:S(2)}) %collective-permute-start.18) | collective-permute-done | bytes 270368 | tf_op jit(solution)/shard_map/ppermute | solution.py:331
  75.6 1.7 %collective-permute-start.24 = (f32[264,256]{1,0:T(8,128)S(1)}, f32[264,256]{1,0:T(8,128)S(1)}, u32[]{:S(2)}, u32[]{:S(2)}) collective-permute-start(f32[264,256]{1,0:T(8,128)S(1)} %finish.1.refs_0_), channel_id=1, source_target_pairs={{0,8},{2,10},{4,12},{6,14},{16,0},{18,2},{20,4},{22,6},{24,16},{26... | collective-permute-start | bytes 811016 | tf_op jit(solution)/shard_map/ppermute | solution.py:331
  77.8 1.5 %collective-permute-start.22 = (f32[264,256]{1,0:T(8,128)S(1)}, f32[264,256]{1,0:T(8,128)S(1)}, u32[]{:S(2)}, u32[]{:S(2)}) collective-permute-start(f32[264,256]{1,0:T(8,128)S(1)} %collective-permute-done.17.refs_1_), channel_id=1, source_target_pairs={{0,4},{2,6},{4,0},{6,2},{8,12},{10,14},{12,8},{14,10},{16,20},{18,... | collective-permute-start | bytes 811016 | tf_op jit(solution)/shard_map/ppermute | solution.py:324
  79.3 1.4 %collective-permute-start.26 = (f32[264,256]{1,0:T(8,128)S(1)}, f32[264,256]{1,0:T(8,128)S(1)}, u32[]{:S(2)}, u32[]{:S(2)}) collective-permute-start(f32[264,256]{1,0:T(8,128)S(1)} %collective-permute-done.18.refs_2_), channel_id=1, source_target_pairs={{0,2},{2,0},{4,6},{6,4},{8,10},{10,8},{12,14},{14,12},{16,18},{18,... | collective-permute-start | bytes 811016 | tf_op jit(solution)/shard_map/ppermute | solution.py:324
  80.7 3.9 %collective-permute-done.24.refs_3_ = f32[264,256]{1,0:T(8,128)S(1)} collective-permute-done((f32[264,256]{1,0:T(8,128)S(1)}, f32[264,256]{1,0:T(8,128)S(1)}, u32[]{:S(2)}, u32[]{:S(2)}) %collective-permute-start.24) | collective-permute-done | bytes 270368 | tf_op jit(solution)/shard_map/ppermute | solution.py:331
  84.6 2.9 %collective-permute-start.30 = (f32[264,256]{1,0:T(8,128)S(1)}, f32[264,256]{1,0:T(8,128)S(1)}, u32[]{:S(2)}, u32[]{:S(2)}) collective-permute-start(f32[264,256]{1,0:T(8,128)S(1)} %collective-permute-done.21.refs_6_), channel_id=1, source_target_pairs={{0,16},{2,18},{4,20},{6,22},{16,24},{18,26},{20,28},{22,30},{24,8}... | collective-permute-start | bytes 811016 | tf_op jit(solution)/shard_map/ppermute | solution.py:331
  87.5 1.5 %collective-permute-start.23 = (f32[264,256]{1,0:T(8,128)S(1)}, f32[264,256]{1,0:T(8,128)S(1)}, u32[]{:S(2)}, u32[]{:S(2)}) collective-permute-start(f32[264,256]{1,0:T(8,128)S(1)} %collective-permute-done.18.refs_2_), channel_id=1, source_target_pairs={{0,4},{2,6},{4,0},{6,2},{8,12},{10,14},{12,8},{14,10},{16,20},{18,... | collective-permute-start | bytes 811016 | tf_op jit(solution)/shard_map/ppermute | solution.py:324
  89.0 1.4 %collective-permute-start.27 = (f32[264,256]{1,0:T(8,128)S(1)}, f32[264,256]{1,0:T(8,128)S(1)}, u32[]{:S(2)}, u32[]{:S(2)}) collective-permute-start(f32[264,256]{1,0:T(8,128)S(1)} %collective-permute-done.24.refs_3_), channel_id=1, source_target_pairs={{0,2},{2,0},{4,6},{6,4},{8,10},{10,8},{12,14},{14,12},{16,18},{18,... | collective-permute-start | bytes 811016 | tf_op jit(solution)/shard_map/ppermute | solution.py:324
  90.4 3.0 %collective-permute-done.30.refs_2_ = f32[264,256]{1,0:T(8,128)S(1)} collective-permute-done((f32[264,256]{1,0:T(8,128)S(1)}, f32[264,256]{1,0:T(8,128)S(1)}, u32[]{:S(2)}, u32[]{:S(2)}) %collective-permute-start.30) | collective-permute-done | bytes 270368 | tf_op jit(solution)/shard_map/ppermute | solution.py:331
  93.5 2.7 %collective-permute-done.23.refs_0_ = f32[264,256]{1,0:T(8,128)S(1)} collective-permute-done((f32[264,256]{1,0:T(8,128)S(1)}, f32[264,256]{1,0:T(8,128)S(1)}, u32[]{:S(2)}, u32[]{:S(2)}) %collective-permute-start.23) | collective-permute-done | bytes 270368 | tf_op jit(solution)/shard_map/ppermute | solution.py:324
  96.2 1.5 %collective-permute-start.29 = (f32[264,256]{1,0:T(8,128)S(1)}, f32[264,256]{1,0:T(8,128)S(1)}, u32[]{:S(2)}, u32[]{:S(2)}) collective-permute-start(f32[264,256]{1,0:T(8,128)S(1)} %collective-permute-done.24.refs_3_), channel_id=1, source_target_pairs={{0,4},{2,6},{4,0},{6,2},{8,12},{10,14},{12,8},{14,10},{16,20},{18,... | collective-permute-start | bytes 811016 | tf_op jit(solution)/shard_map/ppermute | solution.py:324
  98.0 1.4 %collective-permute-start.28 = (f32[264,256]{1,0:T(8,128)S(1)}, f32[264,256]{1,0:T(8,128)S(1)}, u32[]{:S(2)}, u32[]{:S(2)}) collective-permute-start(f32[264,256]{1,0:T(8,128)S(1)} %collective-permute-done.23.refs_0_), channel_id=1, source_target_pairs={{0,2},{2,0},{4,6},{6,4},{8,10},{10,8},{12,14},{14,12},{16,18},{18,... | collective-permute-start | bytes 811016 | tf_op jit(solution)/shard_map/ppermute | solution.py:324
  99.4 1.9 %place_early.1 = (f32[4096,256]{1,0:T(8,128)}, f32[32,128]{1,0:T(8,128)S(1)}) custom-call(s32[2]{0:T(128)S(1)} %pad_add_fusion.where_ref, f32[264,256]{1,0:T(8,128)S(1)} %finish.1.refs_0_, f32[264,256]{1,0:T(8,128)S(1)} %collective-permute-done.17.refs_1_, f32[264,256]{1,0:T(8,128)S(1)} %collective-permute-done.18.refs_2_, ...), custom_call_target="tpu_custom_call" | custom-call | bytes 2162696 | tf_op jit(solution)/shard_map/place_early/pallas_call | solution.py:27
  101.3 1.6 %place_middle.1 = (f32[4096,256]{1,0:T(8,128)}, f32[32,128]{1,0:T(8,128)S(1)}) custom-call(s32[2]{0:T(128)S(1)} %pad_add_fusion.where_ref, f32[264,256]{1,0:T(8,128)S(1)} %collective-permute-done.23.refs_0_, f32[264,256]{1,0:T(8,128)S(1)} %collective-permute-done.27.refs_1_, ...), custom_call_target="tpu_custom_call", output_to_operand_aliasing={{0}: (7, {})} | custom-call | bytes 5562376 | tf_op jit(solution)/shard_map/place_middle/pallas_call | solution.py:27
  103.0 1.5 %collective-permute-done.28.refs_0_ = f32[264,256]{1,0:T(8,128)S(1)} collective-permute-done((f32[264,256]{1,0:T(8,128)S(1)}, f32[264,256]{1,0:T(8,128)S(1)}, u32[]{:S(2)}, u32[]{:S(2)}) %collective-permute-start.28) | collective-permute-done | bytes 270368 | tf_op jit(solution)/shard_map/ppermute | solution.py:324
  104.5 2.1 %place_late.1 = (f32[4096,256]{1,0:T(8,128)}, f32[32,128]{1,0:T(8,128)}) custom-call(s32[2]{0:T(128)S(1)} %pad_add_fusion.where_ref, f32[264,256]{1,0:T(8,128)S(1)} %collective-permute-done.28.refs_0_, f32[264,256]{1,0:T(8,128)S(1)} %collective-permute-done.29.refs_1_, ...), custom_call_target="tpu_custom_call", output_to_operand_aliasing={{0}: (5, {})} | custom-call | bytes 5021704 | tf_op jit(solution)/shard_map/place_late/pallas_call | solution.py:27
  (37 shorter events, 2.8 us)
Async XLA Ops:
  0.7 1.0 copy-start.1
  2.4 16.4 %collective-permute-start.1 = (f32[256,256]{1,0:T(8,128)S(1)}, f32[256,256]{1,0:T(8,128)S(1)}, u32[]{:S(2)}, u32[]{:S(2)}) collective-permute-start(f32[256,256]{1,0:T(8,128)S(1)} %get-tuple-element.63), channel_id=1, source_target_pairs={{0,4},{2,6},{4,0},{6,2},{8,12},{10,14},{12,8},{14,10},{16,20},{18,... | collective-permute-start | bytes 786440 | tf_op jit(solution)/shard_map/ppermute | solution.py:324
  5.4 19.1 %collective-permute-start.4 = (f32[256,256]{1,0:T(8,128)S(1)}, f32[256,256]{1,0:T(8,128)S(1)}, u32[]{:S(2)}, u32[]{:S(2)}) collective-permute-start(f32[256,256]{1,0:T(8,128)S(1)} %get-tuple-element.63), channel_id=1, source_target_pairs={{0,2},{2,0},{4,6},{6,4},{8,10},{10,8},{12,14},{14,12},{16,18},{18,... | collective-permute-start | bytes 786440 | tf_op jit(solution)/shard_map/ppermute | solution.py:324
  6.9 16.1 %copy-start.2 = (bf16[1024,256]{1,0:T(8,128)(2,1)S(1)}, bf16[1024,256]{1,0:T(8,128)(2,1)}, u32[]{:S(2)}) copy-start(bf16[1024,256]{1,0:T(8,128)(2,1)} %points_ref.5) | copy-start | bytes 1572868
  6.9 11.9 %collective-permute-start = (f32[256,256]{1,0:T(8,128)S(1)}, f32[256,256]{1,0:T(8,128)S(1)}, u32[]{:S(2)}, u32[]{:S(2)}) collective-permute-start(f32[256,256]{1,0:T(8,128)S(1)} %get-tuple-element.62), channel_id=1, source_target_pairs={{0,2},{2,0},{4,6},{6,4},{8,10},{10,8},{12,14},{14,12},{16,18},{18,... | collective-permute-start | bytes 786440 | tf_op jit(solution)/shard_map/ppermute | solution.py:324
  7.4 18.7 %collective-permute-start.6 = (f32[256,256]{1,0:T(8,128)S(1)}, f32[256,256]{1,0:T(8,128)S(1)}, u32[]{:S(2)}, u32[]{:S(2)}) collective-permute-start(f32[256,256]{1,0:T(8,128)S(1)} %get-tuple-element.62), channel_id=1, source_target_pairs={{0,4},{2,6},{4,0},{6,2},{8,12},{10,14},{12,8},{14,10},{16,20},{18,... | collective-permute-start | bytes 786440 | tf_op jit(solution)/shard_map/ppermute | solution.py:324
  7.5 1.6 %copy-start.3 = (bf16[4096,256]{1,0:T(8,128)(2,1)S(1)}, bf16[4096,256]{1,0:T(8,128)(2,1)}, u32[]{:S(2)}) copy-start(bf16[4096,256]{1,0:T(8,128)(2,1)} %c_ref.1) | copy-start | bytes 6291460
  18.8 10.7 %collective-permute-start.2 = (f32[256,256]{1,0:T(8,128)S(1)}, f32[256,256]{1,0:T(8,128)S(1)}, u32[]{:S(2)}, u32[]{:S(2)}) collective-permute-start(f32[256,256]{1,0:T(8,128)S(1)} %collective-permute-done.x0_ref.refs_0_), channel_id=1, source_target_pairs={{0,1},{1,0},{2,3},{3,2},{4,5},{5,4},{6,7},{7,6},{8,9},{9,8},{10,11... | collective-permute-start | bytes 786440 | tf_op jit(solution)/shard_map/ppermute | solution.py:327
  18.8 1.5 %collective-permute-start.8 = (f32[2,1024]{1,0:T(2,128)S(1)}, f32[2,1024]{1,0:T(2,128)S(1)}, u32[]{:S(2)}, u32[]{:S(2)}) collective-permute-start(f32[2,1024]{1,0:T(2,128)S(1)} %get-tuple-element.66.refs_0_), channel_id=1, source_target_pairs={{0,1},{1,0},{2,3},{3,2},{4,5},{5,4},{6,7},{7,6},{8,9},{9,8},{10,11... | collective-permute-start | bytes 24584 | tf_op jit(solution)/shard_map/ppermute | solution.py:327
  21.0 10.4 %collective-permute-start.10 = (f32[264,256]{1,0:T(8,128)S(1)}, f32[264,256]{1,0:T(8,128)S(1)}, u32[]{:S(2)}, u32[]{:S(2)}) collective-permute-start(f32[264,256]{1,0:T(8,128)S(1)} %get-tuple-element.68), channel_id=1, source_target_pairs={{0,2},{2,0},{4,6},{6,4},{8,10},{10,8},{12,14},{14,12},{16,18},{18,... | collective-permute-start | bytes 811016 | tf_op jit(solution)/shard_map/ppermute | solution.py:324
  22.5 8.9 %collective-permute-start.9 = (f32[264,256]{1,0:T(8,128)S(1)}, f32[264,256]{1,0:T(8,128)S(1)}, u32[]{:S(2)}, u32[]{:S(2)}) collective-permute-start(f32[264,256]{1,0:T(8,128)S(1)} %get-tuple-element.67), channel_id=1, source_target_pairs={{0,4},{2,6},{4,0},{6,2},{8,12},{10,14},{12,8},{14,10},{16,20},{18,... | collective-permute-start | bytes 811016 | tf_op jit(solution)/shard_map/ppermute | solution.py:324
  24.5 9.0 %copy-start = (f32[1024,256]{1,0:T(8,128)}, f32[1024,256]{1,0:T(8,128)S(1)}, u32[]{:S(2)}) copy-start(f32[1024,256]{1,0:T(8,128)S(1)} %get-tuple-element.75.acc_ref) | copy-start | bytes 3145732
  24.5 5.0 %collective-permute-start.11 = (f32[4,256]{1,0:T(4,128)S(1)}, f32[4,256]{1,0:T(4,128)S(1)}, u32[]{:S(2)}, u32[]{:S(2)}) collective-permute-start(f32[4,256]{1,0:T(4,128)S(1)} %get-tuple-element.74.lse_ref), channel_id=1, source_target_pairs={{0,6},{2,4},{4,2},{6,0},{8,14},{10,12},{12,10},{14,8},{16,22},{18,... | collective-permute-start | bytes 12296 | tf_op jit(solution)/shard_map/ppermute | solution.py:324
  26.1 3.9 %collective-permute-start.3 = (f32[256,256]{1,0:T(8,128)S(1)}, f32[256,256]{1,0:T(8,128)S(1)}, u32[]{:S(2)}, u32[]{:S(2)}) collective-permute-start(f32[256,256]{1,0:T(8,128)S(1)} %collective-permute-done.1.y1_ref.refs_2_), channel_id=1, source_target_pairs={{0,1},{1,0},{2,3},{3,2},{4,5},{5,4},{6,7},{7,6},{8,9},{9,8},{10,11... | collective-permute-start | bytes 786440 | tf_op jit(solution)/shard_map/ppermute | solution.py:327
  29.5 1.5 %collective-permute-start.5 = (f32[256,256]{1,0:T(8,128)S(1)}, f32[256,256]{1,0:T(8,128)S(1)}, u32[]{:S(2)}, u32[]{:S(2)}) collective-permute-start(f32[256,256]{1,0:T(8,128)S(1)} %collective-permute-done.4.refs_4_), channel_id=1, source_target_pairs={{0,1},{1,0},{2,3},{3,2},{4,5},{5,4},{6,7},{7,6},{8,9},{9,8},{10,11... | collective-permute-start | bytes 786440 | tf_op jit(solution)/shard_map/ppermute | solution.py:327
  29.5 1.9 %collective-permute-start.7 = (f32[256,256]{1,0:T(8,128)S(1)}, f32[256,256]{1,0:T(8,128)S(1)}, u32[]{:S(2)}, u32[]{:S(2)}) collective-permute-start(f32[256,256]{1,0:T(8,128)S(1)} %collective-permute-done.6.refs_6_), channel_id=1, source_target_pairs={{0,1},{1,0},{2,3},{3,2},{4,5},{5,4},{6,7},{7,6},{8,9},{9,8},{10,11... | collective-permute-start | bytes 786440 | tf_op jit(solution)/shard_map/ppermute | solution.py:327
  31.4 2.0 %collective-permute-start.12 = (f32[264,256]{1,0:T(8,128)S(1)}, f32[264,256]{1,0:T(8,128)S(1)}, u32[]{:S(2)}, u32[]{:S(2)}) collective-permute-start(f32[264,256]{1,0:T(8,128)S(1)} %collective-permute-done.9.refs_8_), channel_id=1, source_target_pairs={{0,1},{1,0},{2,3},{3,2},{4,5},{5,4},{6,7},{7,6},{8,9},{9,8},{10,11... | collective-permute-start | bytes 811016 | tf_op jit(solution)/shard_map/ppermute | solution.py:327
  31.5 1.9 %collective-permute-start.13 = (f32[264,256]{1,0:T(8,128)S(1)}, f32[264,256]{1,0:T(8,128)S(1)}, u32[]{:S(2)}, u32[]{:S(2)}) collective-permute-start(f32[264,256]{1,0:T(8,128)S(1)} %collective-permute-done.10.refs_9_.refs_10_), channel_id=1, source_target_pairs={{0,1},{1,0},{2,3},{3,2},{4,5},{5,4},{6,7},{7,6},{8,9},{9,8},{10,11... | collective-permute-start | bytes 811016 | tf_op jit(solution)/shard_map/ppermute | solution.py:327
  35.4 8.1 %collective-permute-start.14 = (f32[264,256]{1,0:T(8,128)S(1)}, f32[264,256]{1,0:T(8,128)S(1)}, u32[]{:S(2)}, u32[]{:S(2)}) collective-permute-start(f32[264,256]{1,0:T(8,128)S(1)} %get-tuple-element.94), channel_id=1, source_target_pairs={{0,16},{2,18},{4,20},{6,22},{16,24},{18,26},{20,28},{22,30},{24,8}... | collective-permute-start | bytes 811016 | tf_op jit(solution)/shard_map/ppermute | solution.py:331
  43.2 10.5 %collective-permute-start.16 = (f32[264,256]{1,0:T(8,128)S(1)}, f32[264,256]{1,0:T(8,128)S(1)}, u32[]{:S(2)}, u32[]{:S(2)}) collective-permute-start(f32[264,256]{1,0:T(8,128)S(1)} %get-tuple-element.95), channel_id=1, source_target_pairs={{0,8},{2,10},{4,12},{6,14},{16,0},{18,2},{20,4},{22,6},{24,16},{26... | collective-permute-start | bytes 811016 | tf_op jit(solution)/shard_map/ppermute | solution.py:331
  43.6 14.8 %collective-permute-start.15 = (f32[264,256]{1,0:T(8,128)S(1)}, f32[264,256]{1,0:T(8,128)S(1)}, u32[]{:S(2)}, u32[]{:S(2)}) collective-permute-start(f32[264,256]{1,0:T(8,128)S(1)} %add.3), channel_id=1, source_target_pairs={{0,16},{2,18},{4,20},{6,22},{16,24},{18,26},{20,28},{22,30},{24,8}... | collective-permute-start | bytes 811016 | tf_op jit(solution)/shard_map/ppermute | solution.py:331
  59.2 8.6 %collective-permute-start.17 = (f32[264,256]{1,0:T(8,128)S(1)}, f32[264,256]{1,0:T(8,128)S(1)}, u32[]{:S(2)}, u32[]{:S(2)}) collective-permute-start(f32[264,256]{1,0:T(8,128)S(1)} %finish.1.refs_0_), channel_id=1, source_target_pairs={{0,16},{2,18},{4,20},{6,22},{16,24},{18,26},{20,28},{22,30},{24,8}... | collective-permute-start | bytes 811016 | tf_op jit(solution)/shard_map/ppermute | solution.py:331
  60.3 9.7 %collective-permute-start.19 = (f32[264,256]{1,0:T(8,128)S(1)}, f32[264,256]{1,0:T(8,128)S(1)}, u32[]{:S(2)}, u32[]{:S(2)}) collective-permute-start(f32[264,256]{1,0:T(8,128)S(1)} %finish.1.refs_0_), channel_id=1, source_target_pairs={{0,2},{2,0},{4,6},{6,4},{8,10},{10,8},{12,14},{14,12},{16,18},{18,... | collective-permute-start | bytes 811016 | tf_op jit(solution)/shard_map/ppermute | solution.py:324
  61.8 8.3 %collective-permute-start.20 = (f32[264,256]{1,0:T(8,128)S(1)}, f32[264,256]{1,0:T(8,128)S(1)}, u32[]{:S(2)}, u32[]{:S(2)}) collective-permute-start(f32[264,256]{1,0:T(8,128)S(1)} %finish.1.refs_0_), channel_id=1, source_target_pairs={{0,4},{2,6},{4,0},{6,2},{8,12},{10,14},{12,8},{14,10},{16,20},{18,... | collective-permute-start | bytes 811016 | tf_op jit(solution)/shard_map/ppermute | solution.py:324
  67.7 7.9 %collective-permute-start.18 = (f32[264,256]{1,0:T(8,128)S(1)}, f32[264,256]{1,0:T(8,128)S(1)}, u32[]{:S(2)}, u32[]{:S(2)}) collective-permute-start(f32[264,256]{1,0:T(8,128)S(1)} %collective-permute-done.17.refs_1_), channel_id=1, source_target_pairs={{0,16},{2,18},{4,20},{6,22},{16,24},{18,26},{20,28},{22,30},{24,8}... | collective-permute-start | bytes 811016 | tf_op jit(solution)/shard_map/ppermute | solution.py:331
  70.1 7.7 %collective-permute-start.21 = (f32[264,256]{1,0:T(8,128)S(1)}, f32[264,256]{1,0:T(8,128)S(1)}, u32[]{:S(2)}, u32[]{:S(2)}) collective-permute-start(f32[264,256]{1,0:T(8,128)S(1)} %collective-permute-done.19.refs_4_), channel_id=1, source_target_pairs={{0,4},{2,6},{4,0},{6,2},{8,12},{10,14},{12,8},{14,10},{16,20},{18,... | collective-permute-start | bytes 811016 | tf_op jit(solution)/shard_map/ppermute | solution.py:324
  71.6 7.8 %collective-permute-start.25 = (f32[264,256]{1,0:T(8,128)S(1)}, f32[264,256]{1,0:T(8,128)S(1)}, u32[]{:S(2)}, u32[]{:S(2)}) collective-permute-start(f32[264,256]{1,0:T(8,128)S(1)} %collective-permute-done.17.refs_1_), channel_id=1, source_target_pairs={{0,2},{2,0},{4,6},{6,4},{8,10},{10,8},{12,14},{14,12},{16,18},{18,... | collective-permute-start | bytes 811016 | tf_op jit(solution)/shard_map/ppermute | solution.py:324
  75.6 9.0 %collective-permute-start.24 = (f32[264,256]{1,0:T(8,128)S(1)}, f32[264,256]{1,0:T(8,128)S(1)}, u32[]{:S(2)}, u32[]{:S(2)}) collective-permute-start(f32[264,256]{1,0:T(8,128)S(1)} %finish.1.refs_0_), channel_id=1, source_target_pairs={{0,8},{2,10},{4,12},{6,14},{16,0},{18,2},{20,4},{22,6},{24,16},{26... | collective-permute-start | bytes 811016 | tf_op jit(solution)/shard_map/ppermute | solution.py:331
  77.8 9.7 %collective-permute-start.22 = (f32[264,256]{1,0:T(8,128)S(1)}, f32[264,256]{1,0:T(8,128)S(1)}, u32[]{:S(2)}, u32[]{:S(2)}) collective-permute-start(f32[264,256]{1,0:T(8,128)S(1)} %collective-permute-done.17.refs_1_), channel_id=1, source_target_pairs={{0,4},{2,6},{4,0},{6,2},{8,12},{10,14},{12,8},{14,10},{16,20},{18,... | collective-permute-start | bytes 811016 | tf_op jit(solution)/shard_map/ppermute | solution.py:324
  79.3 9.7 %collective-permute-start.26 = (f32[264,256]{1,0:T(8,128)S(1)}, f32[264,256]{1,0:T(8,128)S(1)}, u32[]{:S(2)}, u32[]{:S(2)}) collective-permute-start(f32[264,256]{1,0:T(8,128)S(1)} %collective-permute-done.18.refs_2_), channel_id=1, source_target_pairs={{0,2},{2,0},{4,6},{6,4},{8,10},{10,8},{12,14},{14,12},{16,18},{18,... | collective-permute-start | bytes 811016 | tf_op jit(solution)/shard_map/ppermute | solution.py:324
  84.6 8.9 %collective-permute-start.30 = (f32[264,256]{1,0:T(8,128)S(1)}, f32[264,256]{1,0:T(8,128)S(1)}, u32[]{:S(2)}, u32[]{:S(2)}) collective-permute-start(f32[264,256]{1,0:T(8,128)S(1)} %collective-permute-done.21.refs_6_), channel_id=1, source_target_pairs={{0,16},{2,18},{4,20},{6,22},{16,24},{18,26},{20,28},{22,30},{24,8}... | collective-permute-start | bytes 811016 | tf_op jit(solution)/shard_map/ppermute | solution.py:331
  87.5 8.7 %collective-permute-start.23 = (f32[264,256]{1,0:T(8,128)S(1)}, f32[264,256]{1,0:T(8,128)S(1)}, u32[]{:S(2)}, u32[]{:S(2)}) collective-permute-start(f32[264,256]{1,0:T(8,128)S(1)} %collective-permute-done.18.refs_2_), channel_id=1, source_target_pairs={{0,4},{2,6},{4,0},{6,2},{8,12},{10,14},{12,8},{14,10},{16,20},{18,... | collective-permute-start | bytes 811016 | tf_op jit(solution)/shard_map/ppermute | solution.py:324
  89.0 9.0 %collective-permute-start.27 = (f32[264,256]{1,0:T(8,128)S(1)}, f32[264,256]{1,0:T(8,128)S(1)}, u32[]{:S(2)}, u32[]{:S(2)}) collective-permute-start(f32[264,256]{1,0:T(8,128)S(1)} %collective-permute-done.24.refs_3_), channel_id=1, source_target_pairs={{0,2},{2,0},{4,6},{6,4},{8,10},{10,8},{12,14},{14,12},{16,18},{18,... | collective-permute-start | bytes 811016 | tf_op jit(solution)/shard_map/ppermute | solution.py:324
  93.5 9.5 %collective-permute-start.31 = (f32[264,256]{1,0:T(8,128)S(1)}, f32[264,256]{1,0:T(8,128)S(1)}, u32[]{:S(2)}, u32[]{:S(2)}) collective-permute-start(f32[264,256]{1,0:T(8,128)S(1)} %collective-permute-done.21.refs_6_), channel_id=1, source_target_pairs={{0,8},{2,10},{4,12},{6,14},{16,0},{18,2},{20,4},{22,6},{24,16},{26... | collective-permute-start | bytes 811016 | tf_op jit(solution)/shard_map/ppermute | solution.py:331
  96.2 6.8 %collective-permute-start.29 = (f32[264,256]{1,0:T(8,128)S(1)}, f32[264,256]{1,0:T(8,128)S(1)}, u32[]{:S(2)}, u32[]{:S(2)}) collective-permute-start(f32[264,256]{1,0:T(8,128)S(1)} %collective-permute-done.24.refs_3_), channel_id=1, source_target_pairs={{0,4},{2,6},{4,0},{6,2},{8,12},{10,14},{12,8},{14,10},{16,20},{18,... | collective-permute-start | bytes 811016 | tf_op jit(solution)/shard_map/ppermute | solution.py:324
  98.0 6.5 %collective-permute-start.28 = (f32[264,256]{1,0:T(8,128)S(1)}, f32[264,256]{1,0:T(8,128)S(1)}, u32[]{:S(2)}, u32[]{:S(2)}) collective-permute-start(f32[264,256]{1,0:T(8,128)S(1)} %collective-permute-done.23.refs_0_), channel_id=1, source_target_pairs={{0,2},{2,0},{4,6},{6,4},{8,10},{10,8},{12,14},{14,12},{16,18},{18,... | collective-permute-start | bytes 811016 | tf_op jit(solution)/shard_map/ppermute | solution.py:324

commit v8 on v7

--- a/solution.py
+++ b/solution.py
@@ -238,25 +238,23 @@
             block_sums(cores, order, half, steps, where_ref, twice_ref, norm_ref, acc_ref, cnt_ref, lse_ref, near, far, out_ref)
 
 
-def rest_kernel(cores, order, half, made, missing, where_ref, twice_ref, norm_ref, acc_ref, cnt_ref, lse_ref, *refs):
+def rest_kernel(cores, order, half, steps, where_ref, twice_ref, norm_ref, acc_ref, cnt_ref, lse_ref, *refs):
     near, far = refs[: 4 * cores], refs[4 * cores : 6 * cores]
-    made_refs = refs[6 * cores : 6 * cores + len(made)]
-    out_refs = refs[6 * cores + len(made) :]
-    given = (where_ref, twice_ref, norm_ref, acc_ref, cnt_ref, lse_ref, near, far)
+    given, out_ref = refs[6 * cores : -1], refs[-1]
+    make = functools.partial(
+        block_sums, cores, order, half, steps,
+        where_ref, twice_ref, norm_ref, acc_ref, cnt_ref, lse_ref, near, far, out_ref,
+    )
+    if not given:
+        make()
+        return
     odd = lax.rem(where_ref[1], 2) == 1
 
     @pl.when(odd)
     def _():
-        for made_ref, out_ref in zip(made_refs, out_refs):
-            out_ref[...] = made_ref[...]
-
-    @pl.when(jnp.logical_not(odd))
-    def _():
-        for steps, out_ref in zip(made, out_refs):
-            block_sums(cores, order, half, steps, *given, out_ref)
-
-    for steps, out_ref in zip(missing, out_refs[len(made) :]):
-        block_sums(cores, order, half, steps, *given, out_ref)
+        out_ref[...] = given[0][...]
+
+    pl.when(jnp.logical_not(odd))(make)
 
 
 def ahead(order, line, steps):
@@ -345,7 +343,6 @@
     x1, y0 = flip(second, 1), flip(first, 2)
 
     pair, twice, norm = stats(where, points, centroids, lines)
-    pair, x0, y1 = lax.optimization_barrier((pair, x0, y1))
     pairs = [pair] + [flip_core(pair, rc) for rc in range(1, cores)]
     tail = max(8, 2 * cores)
     lse, log_evidence, pack_x, pack_y = call(
@@ -366,10 +363,10 @@
         "own",
         flops=4 * share * width * rows,
     )
+    x0, y1, x1, y0, lse = lax.optimization_barrier((x0, y1, x1, y0, lse))
     near = with_siblings((x0, y1, x1, y0))
-    lse, acc, cnt = lax.optimization_barrier((lse, acc, cnt))
-    lse_d = flip(lse, 3)
-    near, d0, d1, acc, cnt, lse_d = lax.optimization_barrier((near, d0, d1, acc, cnt, lse_d))
+    near, d0, d1, acc, cnt = lax.optimization_barrier((near, d0, d1, acc, cnt))
+    lse_d = flip(d1[half : half + 2 * cores, :half], 2)
     lead = call(
         functools.partial(lead_kernel, cores, order, half),
         (f32(size, width), f32(size, lanes)),
@@ -382,8 +379,9 @@
     rows_given = (*near, *with_siblings((d0, d1)))
     block_sum = f32(size + 8, width)
     turn = lines // 2
-    others = [s % lines for s in range(-1, -turn, -1)] + list(range(turn - 1, -1, -1))
-    made, missing = others[:2], others[2:]
+    forward = list(range(turn - 1, 0, -1))
+    backward = [lines - s for s in range(turn - 1, 0, -1)]
+    made = (forward + backward)[:2]
     first, *made_sums = call(
         functools.partial(first_kernel, cores, order, half, made),
         [block_sum] * 3,
@@ -392,31 +390,37 @@
         "first",
         flops=4 * size * width * rows,
     )
-    rest = call(
-        functools.partial(rest_kernel, cores, order, half, made, missing),
-        [block_sum] * (lines - 1),
-        [SMEM] + [VMEM] * (7 + 6 * cores),
-        (*given, *rows_given, *made_sums),
-        "rest",
-        flops=4 * (share - size) * width * 3 * rows,
-    )
-    sums = {turn: first, **dict(zip(others, rest))}
-
-    def reduced(way, steps, moving):
-        for s in range(steps, 0, -1):
-            moving = ring(moving, way)
-            if s > 1:
-                mine = sums[way * (s - 1) % lines]
-                moving = call(add_kernel, block_sum, [VMEM] * 2, (mine, moving), "add")
-        return moving
-
-    ahead_sum = reduced(1, turn, first)
-    behind_sum = reduced(-1, turn - 1, sums[(1 - turn) % lines])
+    made_sums = dict(zip(made, made_sums))
+
+    def sum_of(steps):
+        extra = [made_sums[steps]] if steps in made_sums else []
+        return call(
+            functools.partial(rest_kernel, cores, order, half, steps),
+            block_sum,
+            [SMEM] + [VMEM] * (5 + 6 * cores + len(extra)),
+            (*given, *rows_given, *extra),
+            "rest",
+            flops=4 * size * width * 3 * rows,
+        )
+
+    def plus(a, b):
+        return call(add_kernel, block_sum, [VMEM] * 2, (a, b), "add")
+
+    moving = ring(first, 1)
+    for s in forward:
+        moving = ring(plus(sum_of(s), moving), 1)
+    sides = [moving]
+    moving = None
+    for s in backward:
+        mine = sum_of(s)
+        mine, sides[0] = lax.optimization_barrier((mine, sides[0]))
+        moving = ring(mine if moving is None else plus(mine, moving), -1)
+    sides.append(moving)
     done = call(
         finish_kernel,
         block_sum,
         [SMEM] + [VMEM] * 4,
-        (where, twice, sums[0], ahead_sum, behind_sum),
+        (where, twice, sum_of(0), *sides),
         "finish",
     )
 

time: 107 us -> 109 us (1.019)
  starting transfers between devices: 39.2 us -> 33.3 us
  waiting for transfers between devices: 40.2 us -> 46.1 us
  Pallas kernels: 23.7 us -> 25.8 us
    ppermute x17, starting transfers between devices: 23.2 us -> 14.2 us  [flip(): return lax.ppermute(x, 'dp', [(i, i ^ bits) for i in range(n)])]
    ppermute x8, waiting for transfers between devices: 25.6 us -> 29.8 us  [ring(): lax.ppermute(x, 'dp', [(4 * a + i, 4 * b + i) for a, b in pairs for i in...]
    ppermute x8, starting transfers between devices: 14.4 us -> 18 us  [ring(): lax.ppermute(x, 'dp', [(4 * a + i, 4 * b + i) for a, b in pairs for i in...]
    ppermute x17, waiting for transfers between devices: 12.2 us -> 14.9 us  [flip(): return lax.ppermute(x, 'dp', [(i, i ^ bits) for i in range(n)])]
    pallas_call x12 -> x14, Pallas kernels: 23.7 us -> 25.8 us  [call(): pl.pallas_call(kernel, out_shape=out_shape, in_specs=in_specs, out_specs=...]
    unnamed x8 -> x10, local copies, waits for them, and re-layouts: 2.64 us -> 2.65 us
  transfers between devices with their start and end apart: 32 -> 32, of which waited for: 16 -> 20; matrix products, arithmetic and copies ran while one was open for 0% -> 0% of each run, Pallas kernels for 17% -> 19%
where the time goes in v8:
time: 109 us
  waiting for transfers between devices  46.1 us (42%)
  starting transfers between devices  33.3 us (31%)
  Pallas kernels  25.8 us (24%)
  local copies, waits for them, and re-layouts  2.65 us (2%)
    ppermute x8, waiting for transfers between devices, ring(): lax.ppermute(x, 'dp', [(4 * a + i, 4 * b + i) for a, b in pairs for i in...  29.8 us
    pallas_call x14, Pallas kernels, call(): pl.pallas_call(kernel, out_shape=out_shape, in_specs=in_specs, out_specs=...  25.8 us
    ppermute x8, starting transfers between devices, ring(): lax.ppermute(x, 'dp', [(4 * a + i, 4 * b + i) for a, b in pairs for i in...  18 us
    ppermute x17, waiting for transfers between devices, flip(): return lax.ppermute(x, 'dp', [(i, i ^ bits) for i in range(n)])  14.9 us
    ppermute x17, starting transfers between devices, flip(): return lax.ppermute(x, 'dp', [(i, i ^ bits) for i in range(n)])  14.2 us
    unnamed x10, local copies, waits for them, and re-layouts  2.65 us
  transfers between devices with their start and end apart: 32, of which 20 were waited for; matrix products, arithmetic and copies ran while one was open for 0% of the time, Pallas kernels for 19%

profile of v8, /device:TPU:0, one launch (start us, length us, event | category | flops | bytes accessed | tf_op | source)
XLA Modules:
  0.0 108.9 jit_solution(17256875243841317130)
XLA Ops:
  0.7 1.0 copy-done.2
  1.8 0.6 open.1
  2.4 3.0 %collective-permute-start.1 = (f32[256,256]{1,0:T(8,128)S(1)}, f32[256,256]{1,0:T(8,128)S(1)}, u32[]{:S(2)}, u32[]{:S(2)}) collective-permute-start(f32[256,256]{1,0:T(8,128)S(1)} %get-tuple-element.58), channel_id=1, source_target_pairs={{0,4},{2,6},{4,0},{6,2},{8,12},{10,14},{12,8},{14,10},{16,20},{18,... | collective-permute-start | bytes 786440 | tf_op jit(solution)/shard_map/ppermute | solution.py:322
  5.4 1.5 %collective-permute-start.2 = (f32[256,256]{1,0:T(8,128)S(1)}, f32[256,256]{1,0:T(8,128)S(1)}, u32[]{:S(2)}, u32[]{:S(2)}) collective-permute-start(f32[256,256]{1,0:T(8,128)S(1)} %get-tuple-element.58), channel_id=1, source_target_pairs={{0,2},{2,0},{4,6},{6,4},{8,10},{10,8},{12,14},{14,12},{16,18},{18,... | collective-permute-start | bytes 786440 | tf_op jit(solution)/shard_map/ppermute | solution.py:322
  7.5 1.6 %copy-done.4 = bf16[4096,256]{1,0:T(8,128)(2,1)S(1)} copy-done((bf16[4096,256]{1,0:T(8,128)(2,1)S(1)}, bf16[4096,256]{1,0:T(8,128)(2,1)}, u32[]{:S(2)}) %copy-start.4) | copy-done | bytes 2097176
  9.1 5.9 %stats.1 = (f32[2,1024]{1,0:T(2,128)S(1)}, bf16[1024,256]{1,0:T(8,128)(2,1)S(1)}, f32[1024,128]{1,0:T(8,128)S(1)}) custom-call(s32[2]{0:T(128)S(1)} %pad_add_fusion.where_ref, bf16[1024,256]{1,0:T(8,128)(2,1)S(1)} %copy-done.2, bf16[4096,256]{1,0:T(8,128)(2,1)S(1)} %copy-done.4), custom_call_target="tpu_custom_call" | custom-call | flops 4294967296 | bytes 2621448 | tf_op jit(solution)/shard_map/stats/pallas_call | solution.py:27
  15.1 1.2 %collective-permute-done.4.refs_1_ = f32[2,1024]{1,0:T(2,128)S(1)} collective-permute-done((f32[2,1024]{1,0:T(2,128)S(1)}, f32[2,1024]{1,0:T(2,128)S(1)}, u32[]{:S(2)}, u32[]{:S(2)}) %collective-permute-start.4) | collective-permute-done | bytes 8224 | tf_op jit(solution)/shard_map/ppermute | solution.py:325
  16.3 2.5 %collective-permute-done.x0_ref.refs_0_ = f32[256,256]{1,0:T(8,128)S(1)} collective-permute-done((f32[256,256]{1,0:T(8,128)S(1)}, f32[256,256]{1,0:T(8,128)S(1)}, u32[]{:S(2)}, u32[]{:S(2)}) %collective-permute-start) | collective-permute-done | bytes 262176 | tf_op jit(solution)/shard_map/ppermute | solution.py:322
  18.8 0.6 lse.1
  19.4 1.6 %collective-permute-start.10 = (f32[264,256]{1,0:T(8,128)S(1)}, f32[264,256]{1,0:T(8,128)S(1)}, u32[]{:S(2)}, u32[]{:S(2)}) collective-permute-start(f32[264,256]{1,0:T(8,128)S(1)} %get-tuple-element.66), channel_id=1, source_target_pairs={{0,2},{2,0},{4,6},{6,4},{8,10},{10,8},{12,14},{14,12},{16,18},{18,... | collective-permute-start | bytes 811016 | tf_op jit(solution)/shard_map/ppermute | solution.py:322
  22.0 1.5 %own.1 = (f32[1024,256]{1,0:T(8,128)S(1)}, f32[1024,128]{1,0:T(8,128)S(1)}) custom-call(bf16[1024,256]{1,0:T(8,128)(2,1)S(1)} %copy-done.3, bf16[1024,256]{1,0:T(8,128)(2,1)S(1)} %get-tuple-element.55.twice_ref, f32[1024,128]{1,0:T(8,128)S(1)} %get-tuple-element.56.norm_ref, f32[4,256]{1,0:T(4,128)S(1)} %get-tuple-element.60.lse_ref), custom_call_target="tpu_custom_call" | custom-call | flops 1073741824 | bytes 1576960 | tf_op jit(solution)/shard_map/own/pallas_call | solution.py:27
  23.8 4.5 %collective-permute-done.10.refs_10_.refs_9_ = f32[264,256]{1,0:T(8,128)S(1)} collective-permute-done((f32[264,256]{1,0:T(8,128)S(1)}, f32[264,256]{1,0:T(8,128)S(1)}, u32[]{:S(2)}, u32[]{:S(2)}) %collective-permute-start.10) | collective-permute-done | bytes 270368 | tf_op jit(solution)/shard_map/ppermute | solution.py:322
  28.3 1.2 %collective-permute-done.9.refs_8_ = f32[264,256]{1,0:T(8,128)S(1)} collective-permute-done((f32[264,256]{1,0:T(8,128)S(1)}, f32[264,256]{1,0:T(8,128)S(1)}, u32[]{:S(2)}, u32[]{:S(2)}) %collective-permute-start.9) | collective-permute-done | bytes 270368 | tf_op jit(solution)/shard_map/ppermute | solution.py:322
  30.6 1.5 %lead.1 = (f32[256,256]{1,0:T(8,128)S(1)}, f32[256,128]{1,0:T(8,128)S(1)}) custom-call(s32[2]{0:T(128)S(1)} %pad_add_fusion.where_ref, bf16[1024,256]{1,0:T(8,128)(2,1)S(1)} %get-tuple-element.55.twice_ref, f32[1024,128]{1,0:T(8,128)S(1)} %get-tuple-element.56.norm_ref, f32[1024,256]{1,0:T(8,128)S(1)} %get-tuple-element.69.acc_ref, ...), custom_call_target="tpu_custom_call" | custom-call | flops 536870912 | bytes 5259272 | tf_op jit(solution)/shard_map/lead/pallas_call | solution.py:27
  32.1 1.6 %collective-permute-done.11.lse_ref = f32[4,256]{1,0:T(4,128)S(1)} collective-permute-done((f32[4,256]{1,0:T(4,128)S(1)}, f32[4,256]{1,0:T(4,128)S(1)}, u32[]{:S(2)}, u32[]{:S(2)}) %collective-permute-start.11) | collective-permute-done | bytes 4128 | tf_op jit(solution)/shard_map/ppermute | solution.py:322
  33.7 1.9 %first.1 = (f32[264,256]{1,0:T(8,128)S(1)}, f32[264,256]{1,0:T(8,128)S(1)}, f32[264,256]{1,0:T(8,128)S(1)}) custom-call(s32[2]{0:T(128)S(1)} %pad_add_fusion.where_ref, bf16[1024,256]{1,0:T(8,128)(2,1)S(1)} %get-tuple-element.55.twice_ref, f32[1024,128]{1,0:T(8,128)S(1)} %get-tuple-element.56.norm_ref, f32[1024,256]{1,0:T(8,128)} %copy-done, ...), custom_call_target="tpu_custom_call" | custom-call | flops 268435456 | bytes 6197256 | tf_op jit(solution)/shard_map/first/pallas_call | solution.py:27
  35.6 2.6 %collective-permute-start.14 = (f32[264,256]{1,0:T(8,128)S(1)}, f32[264,256]{1,0:T(8,128)S(1)}, u32[]{:S(2)}, u32[]{:S(2)}) collective-permute-start(f32[264,256]{1,0:T(8,128)S(1)} %get-tuple-element.85), channel_id=1, source_target_pairs={{0,16},{2,18},{4,20},{6,22},{16,24},{18,26},{20,28},{22,30},{24,8}... | collective-permute-start | bytes 811016 | tf_op jit(solution)/shard_map/ppermute | solution.py:329
  38.2 2.8 %rest.5.a_ref = f32[264,256]{1,0:T(8,128)S(1)} custom-call(s32[2]{0:T(128)S(1)} %pad_add_fusion.where_ref, bf16[1024,256]{1,0:T(8,128)(2,1)S(1)} %get-tuple-element.55.twice_ref, f32[1024,128]{1,0:T(8,128)S(1)} %get-tuple-element.56.norm_ref, f32[1024,256]{1,0:T(8,128)} %copy-done, f32[1024,128]{1,0:T(8,128)S(1)} %get-tuple-element.70.cnt_ref, ...), custom_call_target="tpu_custom_call" | custom-call | flops 805306368 | bytes 6074376 | tf_op jit(solution)/shard_map/rest/pallas_call | solution.py:27
  41.0 3.9 %collective-permute-done.14.b_ref = f32[264,256]{1,0:T(8,128)S(1)} collective-permute-done((f32[264,256]{1,0:T(8,128)S(1)}, f32[264,256]{1,0:T(8,128)S(1)}, u32[]{:S(2)}, u32[]{:S(2)}) %collective-permute-start.14) | collective-permute-done | bytes 270368 | tf_op jit(solution)/shard_map/ppermute | solution.py:329
  45.0 3.4 %collective-permute-start.15 = (f32[264,256]{1,0:T(8,128)S(1)}, f32[264,256]{1,0:T(8,128)S(1)}, u32[]{:S(2)}, u32[]{:S(2)}) collective-permute-start(f32[264,256]{1,0:T(8,128)S(1)} %add.3), channel_id=1, source_target_pairs={{0,16},{2,18},{4,20},{6,22},{16,24},{18,26},{20,28},{22,30},{24,8}... | collective-permute-start | bytes 811016 | tf_op jit(solution)/shard_map/ppermute | solution.py:329
  48.4 2.6 %rest.4 = f32[264,256]{1,0:T(8,128)S(1)} custom-call(s32[2]{0:T(128)S(1)} %pad_add_fusion.where_ref, bf16[1024,256]{1,0:T(8,128)(2,1)S(1)} %get-tuple-element.55.twice_ref, f32[1024,128]{1,0:T(8,128)S(1)} %get-tuple-element.56.norm_ref, f32[1024,256]{1,0:T(8,128)} %copy-done, f32[1024,128]{1,0:T(8,128)S(1)} %get-tuple-element.70.cnt_ref, ...), custom_call_target="tpu_custom_call" | custom-call | flops 805306368 | bytes 6074376 | tf_op jit(solution)/shard_map/rest/pallas_call | solution.py:27
  51.0 3.4 %collective-permute-done.15.first_ref = f32[264,256]{1,0:T(8,128)S(1)} collective-permute-done((f32[264,256]{1,0:T(8,128)S(1)}, f32[264,256]{1,0:T(8,128)S(1)}, u32[]{:S(2)}, u32[]{:S(2)}) %collective-permute-start.15) | collective-permute-done | bytes 270368 | tf_op jit(solution)/shard_map/ppermute | solution.py:329
  54.4 2.4 %collective-permute-start.16 = (f32[264,256]{1,0:T(8,128)S(1)}, f32[264,256]{1,0:T(8,128)S(1)}, u32[]{:S(2)}, u32[]{:S(2)}) collective-permute-start(f32[264,256]{1,0:T(8,128)S(1)} %rest.4), channel_id=1, source_target_pairs={{0,8},{2,10},{4,12},{6,14},{16,0},{18,2},{20,4},{22,6},{24,16},{26... | collective-permute-start | bytes 811016 | tf_op jit(solution)/shard_map/ppermute | solution.py:329
  56.8 1.9 %rest.3.mine_ref = f32[264,256]{1,0:T(8,128)S(1)} custom-call(s32[2]{0:T(128)S(1)} %pad_add_fusion.where_ref, bf16[1024,256]{1,0:T(8,128)(2,1)S(1)} %get-tuple-element.55.twice_ref, f32[1024,128]{1,0:T(8,128)S(1)} %get-tuple-element.56.norm_ref, f32[1024,256]{1,0:T(8,128)S(1)} %copy-done.1, f32[1024,128]{1,0:T(8,128)S(1)} %get-tuple-element.70.cnt_ref, ...), custom_call_target="tpu_custom_call" | custom-call | flops 805306368 | bytes 5804040 | tf_op jit(solution)/shard_map/rest/pallas_call | solution.py:27
  58.7 5.1 %collective-permute-done.16.second_ref = f32[264,256]{1,0:T(8,128)S(1)} collective-permute-done((f32[264,256]{1,0:T(8,128)S(1)}, f32[264,256]{1,0:T(8,128)S(1)}, u32[]{:S(2)}, u32[]{:S(2)}) %collective-permute-start.16) | collective-permute-done | bytes 270368 | tf_op jit(solution)/shard_map/ppermute | solution.py:329
  63.7 0.8 finish.1.refs_0_
  64.5 1.8 %collective-permute-start.17 = (f32[264,256]{1,0:T(8,128)S(1)}, f32[264,256]{1,0:T(8,128)S(1)}, u32[]{:S(2)}, u32[]{:S(2)}) collective-permute-start(f32[264,256]{1,0:T(8,128)S(1)} %finish.1.refs_0_), channel_id=1, source_target_pairs={{0,16},{2,18},{4,20},{6,22},{16,24},{18,26},{20,28},{22,30},{24,8}... | collective-permute-start | bytes 811016 | tf_op jit(solution)/shard_map/ppermute | solution.py:329
  66.9 0.6 collective-permute-start.20
  67.4 4.2 %collective-permute-done.17.refs_1_ = f32[264,256]{1,0:T(8,128)S(1)} collective-permute-done((f32[264,256]{1,0:T(8,128)S(1)}, f32[264,256]{1,0:T(8,128)S(1)}, u32[]{:S(2)}, u32[]{:S(2)}) %collective-permute-start.17) | collective-permute-done | bytes 270368 | tf_op jit(solution)/shard_map/ppermute | solution.py:329
  71.6 2.4 %collective-permute-start.18 = (f32[264,256]{1,0:T(8,128)S(1)}, f32[264,256]{1,0:T(8,128)S(1)}, u32[]{:S(2)}, u32[]{:S(2)}) collective-permute-start(f32[264,256]{1,0:T(8,128)S(1)} %collective-permute-done.17.refs_1_), channel_id=1, source_target_pairs={{0,16},{2,18},{4,20},{6,22},{16,24},{18,26},{20,28},{22,30},{24,8}... | collective-permute-start | bytes 811016 | tf_op jit(solution)/shard_map/ppermute | solution.py:329
  74.0 0.7 collective-permute-start.21
  74.7 0.8 collective-permute-start.25
  75.5 3.6 %collective-permute-done.18.refs_2_ = f32[264,256]{1,0:T(8,128)S(1)} collective-permute-done((f32[264,256]{1,0:T(8,128)S(1)}, f32[264,256]{1,0:T(8,128)S(1)}, u32[]{:S(2)}, u32[]{:S(2)}) %collective-permute-start.18) | collective-permute-done | bytes 270368 | tf_op jit(solution)/shard_map/ppermute | solution.py:329
  79.1 1.3 %collective-permute-start.24 = (f32[264,256]{1,0:T(8,128)S(1)}, f32[264,256]{1,0:T(8,128)S(1)}, u32[]{:S(2)}, u32[]{:S(2)}) collective-permute-start(f32[264,256]{1,0:T(8,128)S(1)} %finish.1.refs_0_), channel_id=1, source_target_pairs={{0,8},{2,10},{4,12},{6,14},{16,0},{18,2},{20,4},{22,6},{24,16},{26... | collective-permute-start | bytes 811016 | tf_op jit(solution)/shard_map/ppermute | solution.py:329
  80.4 1.1 collective-permute-done.21.refs_6_
  81.5 0.6 collective-permute-start.22
  82.3 0.9 collective-permute-start.26
  83.2 3.9 %collective-permute-done.24.refs_3_ = f32[264,256]{1,0:T(8,128)S(1)} collective-permute-done((f32[264,256]{1,0:T(8,128)S(1)}, f32[264,256]{1,0:T(8,128)S(1)}, u32[]{:S(2)}, u32[]{:S(2)}) %collective-permute-start.24) | collective-permute-done | bytes 270368 | tf_op jit(solution)/shard_map/ppermute | solution.py:329
  87.1 3.4 %collective-permute-start.30 = (f32[264,256]{1,0:T(8,128)S(1)}, f32[264,256]{1,0:T(8,128)S(1)}, u32[]{:S(2)}, u32[]{:S(2)}) collective-permute-start(f32[264,256]{1,0:T(8,128)S(1)} %collective-permute-done.21.refs_6_), channel_id=1, source_target_pairs={{0,16},{2,18},{4,20},{6,22},{16,24},{18,26},{20,28},{22,30},{24,8}... | collective-permute-start | bytes 811016 | tf_op jit(solution)/shard_map/ppermute | solution.py:329
  90.9 0.9 collective-permute-start.27
  91.8 5.4 %collective-permute-done.30.refs_2_ = f32[264,256]{1,0:T(8,128)S(1)} collective-permute-done((f32[264,256]{1,0:T(8,128)S(1)}, f32[264,256]{1,0:T(8,128)S(1)}, u32[]{:S(2)}, u32[]{:S(2)}) %collective-permute-start.30) | collective-permute-done | bytes 270368 | tf_op jit(solution)/shard_map/ppermute | solution.py:329
  97.1 0.7 collective-permute-start.31
  97.8 2.0 %collective-permute-done.23.refs_0_ = f32[264,256]{1,0:T(8,128)S(1)} collective-permute-done((f32[264,256]{1,0:T(8,128)S(1)}, f32[264,256]{1,0:T(8,128)S(1)}, u32[]{:S(2)}, u32[]{:S(2)}) %collective-permute-start.23) | collective-permute-done | bytes 270368 | tf_op jit(solution)/shard_map/ppermute | solution.py:322
  100.2 0.9 collective-permute-start.28
  101.1 1.9 %place_early.1 = (f32[4096,256]{1,0:T(8,128)}, f32[32,128]{1,0:T(8,128)S(1)}) custom-call(s32[2]{0:T(128)S(1)} %pad_add_fusion.where_ref, f32[264,256]{1,0:T(8,128)S(1)} %finish.1.refs_0_, f32[264,256]{1,0:T(8,128)S(1)} %collective-permute-done.17.refs_1_, f32[264,256]{1,0:T(8,128)S(1)} %collective-permute-done.18.refs_2_, ...), custom_call_target="tpu_custom_call" | custom-call | bytes 2162696 | tf_op jit(solution)/shard_map/place_early/pallas_call | solution.py:27
  103.0 1.6 %place_middle.1 = (f32[4096,256]{1,0:T(8,128)}, f32[32,128]{1,0:T(8,128)S(1)}) custom-call(s32[2]{0:T(128)S(1)} %pad_add_fusion.where_ref, f32[264,256]{1,0:T(8,128)S(1)} %collective-permute-done.23.refs_0_, f32[264,256]{1,0:T(8,128)S(1)} %collective-permute-done.27.refs_1_, ...), custom_call_target="tpu_custom_call", output_to_operand_aliasing={{0}: (7, {})} | custom-call | bytes 5562376 | tf_op jit(solution)/shard_map/place_middle/pallas_call | solution.py:27
  105.0 1.3 %collective-permute-done.29.refs_1_ = f32[264,256]{1,0:T(8,128)S(1)} collective-permute-done((f32[264,256]{1,0:T(8,128)S(1)}, f32[264,256]{1,0:T(8,128)S(1)}, u32[]{:S(2)}, u32[]{:S(2)}) %collective-permute-start.29) | collective-permute-done | bytes 270368 | tf_op jit(solution)/shard_map/ppermute | solution.py:322
  106.6 2.1 %place_late.1 = (f32[4096,256]{1,0:T(8,128)}, f32[32,128]{1,0:T(8,128)}) custom-call(s32[2]{0:T(128)S(1)} %pad_add_fusion.where_ref, f32[264,256]{1,0:T(8,128)S(1)} %collective-permute-done.28.refs_0_, f32[264,256]{1,0:T(8,128)S(1)} %collective-permute-done.29.refs_1_, ...), custom_call_target="tpu_custom_call", output_to_operand_aliasing={{0}: (5, {})} | custom-call | bytes 5021704 | tf_op jit(solution)/shard_map/place_late/pallas_call | solution.py:27
  (42 shorter events, 5.3 us)
Async XLA Ops:
  0.7 1.0 copy-start.2
  2.4 16.4 %collective-permute-start.1 = (f32[256,256]{1,0:T(8,128)S(1)}, f32[256,256]{1,0:T(8,128)S(1)}, u32[]{:S(2)}, u32[]{:S(2)}) collective-permute-start(f32[256,256]{1,0:T(8,128)S(1)} %get-tuple-element.58), channel_id=1, source_target_pairs={{0,4},{2,6},{4,0},{6,2},{8,12},{10,14},{12,8},{14,10},{16,20},{18,... | collective-permute-start | bytes 786440 | tf_op jit(solution)/shard_map/ppermute | solution.py:322
  5.4 14.0 %collective-permute-start.2 = (f32[256,256]{1,0:T(8,128)S(1)}, f32[256,256]{1,0:T(8,128)S(1)}, u32[]{:S(2)}, u32[]{:S(2)}) collective-permute-start(f32[256,256]{1,0:T(8,128)S(1)} %get-tuple-element.58), channel_id=1, source_target_pairs={{0,2},{2,0},{4,6},{6,4},{8,10},{10,8},{12,14},{14,12},{16,18},{18,... | collective-permute-start | bytes 786440 | tf_op jit(solution)/shard_map/ppermute | solution.py:322
  6.9 15.1 %copy-start.3 = (bf16[1024,256]{1,0:T(8,128)(2,1)S(1)}, bf16[1024,256]{1,0:T(8,128)(2,1)}, u32[]{:S(2)}) copy-start(bf16[1024,256]{1,0:T(8,128)(2,1)} %points_ref.5) | copy-start | bytes 1572868
  6.9 11.9 %collective-permute-start = (f32[256,256]{1,0:T(8,128)S(1)}, f32[256,256]{1,0:T(8,128)S(1)}, u32[]{:S(2)}, u32[]{:S(2)}) collective-permute-start(f32[256,256]{1,0:T(8,128)S(1)} %get-tuple-element.57), channel_id=1, source_target_pairs={{0,2},{2,0},{4,6},{6,4},{8,10},{10,8},{12,14},{14,12},{16,18},{18,... | collective-permute-start | bytes 786440 | tf_op jit(solution)/shard_map/ppermute | solution.py:322
  7.4 12.0 %collective-permute-start.3 = (f32[256,256]{1,0:T(8,128)S(1)}, f32[256,256]{1,0:T(8,128)S(1)}, u32[]{:S(2)}, u32[]{:S(2)}) collective-permute-start(f32[256,256]{1,0:T(8,128)S(1)} %get-tuple-element.57), channel_id=1, source_target_pairs={{0,4},{2,6},{4,0},{6,2},{8,12},{10,14},{12,8},{14,10},{16,20},{18,... | collective-permute-start | bytes 786440 | tf_op jit(solution)/shard_map/ppermute | solution.py:322
  7.5 1.6 %copy-start.4 = (bf16[4096,256]{1,0:T(8,128)(2,1)S(1)}, bf16[4096,256]{1,0:T(8,128)(2,1)}, u32[]{:S(2)}) copy-start(bf16[4096,256]{1,0:T(8,128)(2,1)} %c_ref.1) | copy-start | bytes 6291460
  15.0 1.2 %collective-permute-start.4 = (f32[2,1024]{1,0:T(2,128)S(1)}, f32[2,1024]{1,0:T(2,128)S(1)}, u32[]{:S(2)}, u32[]{:S(2)}) collective-permute-start(f32[2,1024]{1,0:T(2,128)S(1)} %get-tuple-element.59.refs_0_), channel_id=1, source_target_pairs={{0,1},{1,0},{2,3},{3,2},{4,5},{5,4},{6,7},{7,6},{8,9},{9,8},{10,11... | collective-permute-start | bytes 24584 | tf_op jit(solution)/shard_map/ppermute | solution.py:325
  19.4 2.6 %collective-permute-start.5 = (f32[256,256]{1,0:T(8,128)S(1)}, f32[256,256]{1,0:T(8,128)S(1)}, u32[]{:S(2)}, u32[]{:S(2)}) collective-permute-start(f32[256,256]{1,0:T(8,128)S(1)} %collective-permute-done.x0_ref.refs_0_), channel_id=1, source_target_pairs={{0,1},{1,0},{2,3},{3,2},{4,5},{5,4},{6,7},{7,6},{8,9},{9,8},{10,11... | collective-permute-start | bytes 786440 | tf_op jit(solution)/shard_map/ppermute | solution.py:325
  19.4 8.9 %collective-permute-start.10 = (f32[264,256]{1,0:T(8,128)S(1)}, f32[264,256]{1,0:T(8,128)S(1)}, u32[]{:S(2)}, u32[]{:S(2)}) collective-permute-start(f32[264,256]{1,0:T(8,128)S(1)} %get-tuple-element.66), channel_id=1, source_target_pairs={{0,2},{2,0},{4,6},{6,4},{8,10},{10,8},{12,14},{14,12},{16,18},{18,... | collective-permute-start | bytes 811016 | tf_op jit(solution)/shard_map/ppermute | solution.py:322
  21.0 8.5 %collective-permute-start.9 = (f32[264,256]{1,0:T(8,128)S(1)}, f32[264,256]{1,0:T(8,128)S(1)}, u32[]{:S(2)}, u32[]{:S(2)}) collective-permute-start(f32[264,256]{1,0:T(8,128)S(1)} %get-tuple-element.65), channel_id=1, source_target_pairs={{0,4},{2,6},{4,0},{6,2},{8,12},{10,14},{12,8},{14,10},{16,20},{18,... | collective-permute-start | bytes 811016 | tf_op jit(solution)/shard_map/ppermute | solution.py:322
  21.5 2.1 %collective-permute-start.6 = (f32[256,256]{1,0:T(8,128)S(1)}, f32[256,256]{1,0:T(8,128)S(1)}, u32[]{:S(2)}, u32[]{:S(2)}) collective-permute-start(f32[256,256]{1,0:T(8,128)S(1)} %collective-permute-done.1.y1_ref.refs_2_), channel_id=1, source_target_pairs={{0,1},{1,0},{2,3},{3,2},{4,5},{5,4},{6,7},{7,6},{8,9},{9,8},{10,11... | collective-permute-start | bytes 786440 | tf_op jit(solution)/shard_map/ppermute | solution.py:325
  21.5 2.1 %collective-permute-start.7 = (f32[256,256]{1,0:T(8,128)S(1)}, f32[256,256]{1,0:T(8,128)S(1)}, u32[]{:S(2)}, u32[]{:S(2)}) collective-permute-start(f32[256,256]{1,0:T(8,128)S(1)} %collective-permute-done.2.refs_4_), channel_id=1, source_target_pairs={{0,1},{1,0},{2,3},{3,2},{4,5},{5,4},{6,7},{7,6},{8,9},{9,8},{10,11... | collective-permute-start | bytes 786440 | tf_op jit(solution)/shard_map/ppermute | solution.py:325
  22.0 1.8 %collective-permute-start.8 = (f32[256,256]{1,0:T(8,128)S(1)}, f32[256,256]{1,0:T(8,128)S(1)}, u32[]{:S(2)}, u32[]{:S(2)}) collective-permute-start(f32[256,256]{1,0:T(8,128)S(1)} %collective-permute-done.3.refs_6_), channel_id=1, source_target_pairs={{0,1},{1,0},{2,3},{3,2},{4,5},{5,4},{6,7},{7,6},{8,9},{9,8},{10,11... | collective-permute-start | bytes 786440 | tf_op jit(solution)/shard_map/ppermute | solution.py:325
  23.6 10.1 %copy-start = (f32[1024,256]{1,0:T(8,128)}, f32[1024,256]{1,0:T(8,128)S(1)}, u32[]{:S(2)}) copy-start(f32[1024,256]{1,0:T(8,128)S(1)} %get-tuple-element.69.acc_ref) | copy-start | bytes 3145732
  29.5 4.1 %collective-permute-start.12 = (f32[264,256]{1,0:T(8,128)S(1)}, f32[264,256]{1,0:T(8,128)S(1)}, u32[]{:S(2)}, u32[]{:S(2)}) collective-permute-start(f32[264,256]{1,0:T(8,128)S(1)} %collective-permute-done.9.refs_8_), channel_id=1, source_target_pairs={{0,1},{1,0},{2,3},{3,2},{4,5},{5,4},{6,7},{7,6},{8,9},{9,8},{10,11... | collective-permute-start | bytes 811016 | tf_op jit(solution)/shard_map/ppermute | solution.py:325
  29.5 4.1 %collective-permute-start.13 = (f32[264,256]{1,0:T(8,128)S(1)}, f32[264,256]{1,0:T(8,128)S(1)}, u32[]{:S(2)}, u32[]{:S(2)}) collective-permute-start(f32[264,256]{1,0:T(8,128)S(1)} %collective-permute-done.10.refs_10_.refs_9_), channel_id=1, source_target_pairs={{0,1},{1,0},{2,3},{3,2},{4,5},{5,4},{6,7},{7,6},{8,9},{9,8},{10,11... | collective-permute-start | bytes 811016 | tf_op jit(solution)/shard_map/ppermute | solution.py:325
  30.1 3.6 %collective-permute-start.11 = (f32[4,256]{1,0:T(4,128)S(1)}, f32[4,256]{1,0:T(4,128)S(1)}, u32[]{:S(2)}, u32[]{:S(2)}) collective-permute-start(f32[4,256]{1,0:T(4,128)S(1)} %slice.3), channel_id=1, source_target_pairs={{0,4},{2,6},{4,0},{6,2},{8,12},{10,14},{12,8},{14,10},{16,20},{18,... | collective-permute-start | bytes 12296 | tf_op jit(solution)/shard_map/ppermute | solution.py:322
  35.6 9.3 %collective-permute-start.14 = (f32[264,256]{1,0:T(8,128)S(1)}, f32[264,256]{1,0:T(8,128)S(1)}, u32[]{:S(2)}, u32[]{:S(2)}) collective-permute-start(f32[264,256]{1,0:T(8,128)S(1)} %get-tuple-element.85), channel_id=1, source_target_pairs={{0,16},{2,18},{4,20},{6,22},{16,24},{18,26},{20,28},{22,30},{24,8}... | collective-permute-start | bytes 811016 | tf_op jit(solution)/shard_map/ppermute | solution.py:329
  41.0 15.8 %copy-start.1 = (f32[1024,256]{1,0:T(8,128)S(1)}, f32[1024,256]{1,0:T(8,128)}, u32[]{:S(2)}) copy-start(f32[1024,256]{1,0:T(8,128)} %copy-done) | copy-start | bytes 3145732
  45.0 9.5 %collective-permute-start.15 = (f32[264,256]{1,0:T(8,128)S(1)}, f32[264,256]{1,0:T(8,128)S(1)}, u32[]{:S(2)}, u32[]{:S(2)}) collective-permute-start(f32[264,256]{1,0:T(8,128)S(1)} %add.3), channel_id=1, source_target_pairs={{0,16},{2,18},{4,20},{6,22},{16,24},{18,26},{20,28},{22,30},{24,8}... | collective-permute-start | bytes 811016 | tf_op jit(solution)/shard_map/ppermute | solution.py:329
  54.4 9.3 %collective-permute-start.16 = (f32[264,256]{1,0:T(8,128)S(1)}, f32[264,256]{1,0:T(8,128)S(1)}, u32[]{:S(2)}, u32[]{:S(2)}) collective-permute-start(f32[264,256]{1,0:T(8,128)S(1)} %rest.4), channel_id=1, source_target_pairs={{0,8},{2,10},{4,12},{6,14},{16,0},{18,2},{20,4},{22,6},{24,16},{26... | collective-permute-start | bytes 811016 | tf_op jit(solution)/shard_map/ppermute | solution.py:329
  64.5 7.1 %collective-permute-start.17 = (f32[264,256]{1,0:T(8,128)S(1)}, f32[264,256]{1,0:T(8,128)S(1)}, u32[]{:S(2)}, u32[]{:S(2)}) collective-permute-start(f32[264,256]{1,0:T(8,128)S(1)} %finish.1.refs_0_), channel_id=1, source_target_pairs={{0,16},{2,18},{4,20},{6,22},{16,24},{18,26},{20,28},{22,30},{24,8}... | collective-permute-start | bytes 811016 | tf_op jit(solution)/shard_map/ppermute | solution.py:329
  66.3 7.6 %collective-permute-start.19 = (f32[264,256]{1,0:T(8,128)S(1)}, f32[264,256]{1,0:T(8,128)S(1)}, u32[]{:S(2)}, u32[]{:S(2)}) collective-permute-start(f32[264,256]{1,0:T(8,128)S(1)} %finish.1.refs_0_), channel_id=1, source_target_pairs={{0,2},{2,0},{4,6},{6,4},{8,10},{10,8},{12,14},{14,12},{16,18},{18,... | collective-permute-start | bytes 811016 | tf_op jit(solution)/shard_map/ppermute | solution.py:322
  66.9 7.1 %collective-permute-start.20 = (f32[264,256]{1,0:T(8,128)S(1)}, f32[264,256]{1,0:T(8,128)S(1)}, u32[]{:S(2)}, u32[]{:S(2)}) collective-permute-start(f32[264,256]{1,0:T(8,128)S(1)} %finish.1.refs_0_), channel_id=1, source_target_pairs={{0,4},{2,6},{4,0},{6,2},{8,12},{10,14},{12,8},{14,10},{16,20},{18,... | collective-permute-start | bytes 811016 | tf_op jit(solution)/shard_map/ppermute | solution.py:322
  71.6 7.5 %collective-permute-start.18 = (f32[264,256]{1,0:T(8,128)S(1)}, f32[264,256]{1,0:T(8,128)S(1)}, u32[]{:S(2)}, u32[]{:S(2)}) collective-permute-start(f32[264,256]{1,0:T(8,128)S(1)} %collective-permute-done.17.refs_1_), channel_id=1, source_target_pairs={{0,16},{2,18},{4,20},{6,22},{16,24},{18,26},{20,28},{22,30},{24,8}... | collective-permute-start | bytes 811016 | tf_op jit(solution)/shard_map/ppermute | solution.py:329
  74.0 7.5 %collective-permute-start.21 = (f32[264,256]{1,0:T(8,128)S(1)}, f32[264,256]{1,0:T(8,128)S(1)}, u32[]{:S(2)}, u32[]{:S(2)}) collective-permute-start(f32[264,256]{1,0:T(8,128)S(1)} %collective-permute-done.19.refs_4_), channel_id=1, source_target_pairs={{0,4},{2,6},{4,0},{6,2},{8,12},{10,14},{12,8},{14,10},{16,20},{18,... | collective-permute-start | bytes 811016 | tf_op jit(solution)/shard_map/ppermute | solution.py:322
  74.7 7.6 %collective-permute-start.25 = (f32[264,256]{1,0:T(8,128)S(1)}, f32[264,256]{1,0:T(8,128)S(1)}, u32[]{:S(2)}, u32[]{:S(2)}) collective-permute-start(f32[264,256]{1,0:T(8,128)S(1)} %collective-permute-done.17.refs_1_), channel_id=1, source_target_pairs={{0,2},{2,0},{4,6},{6,4},{8,10},{10,8},{12,14},{14,12},{16,18},{18,... | collective-permute-start | bytes 811016 | tf_op jit(solution)/shard_map/ppermute | solution.py:322
  79.1 7.9 %collective-permute-start.24 = (f32[264,256]{1,0:T(8,128)S(1)}, f32[264,256]{1,0:T(8,128)S(1)}, u32[]{:S(2)}, u32[]{:S(2)}) collective-permute-start(f32[264,256]{1,0:T(8,128)S(1)} %finish.1.refs_0_), channel_id=1, source_target_pairs={{0,8},{2,10},{4,12},{6,14},{16,0},{18,2},{20,4},{22,6},{24,16},{26... | collective-permute-start | bytes 811016 | tf_op jit(solution)/shard_map/ppermute | solution.py:329
  81.5 9.0 %collective-permute-start.22 = (f32[264,256]{1,0:T(8,128)S(1)}, f32[264,256]{1,0:T(8,128)S(1)}, u32[]{:S(2)}, u32[]{:S(2)}) collective-permute-start(f32[264,256]{1,0:T(8,128)S(1)} %collective-permute-done.17.refs_1_), channel_id=1, source_target_pairs={{0,4},{2,6},{4,0},{6,2},{8,12},{10,14},{12,8},{14,10},{16,20},{18,... | collective-permute-start | bytes 811016 | tf_op jit(solution)/shard_map/ppermute | solution.py:322
  82.3 8.5 %collective-permute-start.26 = (f32[264,256]{1,0:T(8,128)S(1)}, f32[264,256]{1,0:T(8,128)S(1)}, u32[]{:S(2)}, u32[]{:S(2)}) collective-permute-start(f32[264,256]{1,0:T(8,128)S(1)} %collective-permute-done.18.refs_2_), channel_id=1, source_target_pairs={{0,2},{2,0},{4,6},{6,4},{8,10},{10,8},{12,14},{14,12},{16,18},{18,... | collective-permute-start | bytes 811016 | tf_op jit(solution)/shard_map/ppermute | solution.py:322
  87.1 10.1 %collective-permute-start.30 = (f32[264,256]{1,0:T(8,128)S(1)}, f32[264,256]{1,0:T(8,128)S(1)}, u32[]{:S(2)}, u32[]{:S(2)}) collective-permute-start(f32[264,256]{1,0:T(8,128)S(1)} %collective-permute-done.21.refs_6_), channel_id=1, source_target_pairs={{0,16},{2,18},{4,20},{6,22},{16,24},{18,26},{20,28},{22,30},{24,8}... | collective-permute-start | bytes 811016 | tf_op jit(solution)/shard_map/ppermute | solution.py:329
  90.5 9.3 %collective-permute-start.23 = (f32[264,256]{1,0:T(8,128)S(1)}, f32[264,256]{1,0:T(8,128)S(1)}, u32[]{:S(2)}, u32[]{:S(2)}) collective-permute-start(f32[264,256]{1,0:T(8,128)S(1)} %collective-permute-done.18.refs_2_), channel_id=1, source_target_pairs={{0,4},{2,6},{4,0},{6,2},{8,12},{10,14},{12,8},{14,10},{16,20},{18,... | collective-permute-start | bytes 811016 | tf_op jit(solution)/shard_map/ppermute | solution.py:322
  90.9 9.3 %collective-permute-start.27 = (f32[264,256]{1,0:T(8,128)S(1)}, f32[264,256]{1,0:T(8,128)S(1)}, u32[]{:S(2)}, u32[]{:S(2)}) collective-permute-start(f32[264,256]{1,0:T(8,128)S(1)} %collective-permute-done.24.refs_3_), channel_id=1, source_target_pairs={{0,2},{2,0},{4,6},{6,4},{8,10},{10,8},{12,14},{14,12},{16,18},{18,... | collective-permute-start | bytes 811016 | tf_op jit(solution)/shard_map/ppermute | solution.py:322
  97.1 7.8 %collective-permute-start.31 = (f32[264,256]{1,0:T(8,128)S(1)}, f32[264,256]{1,0:T(8,128)S(1)}, u32[]{:S(2)}, u32[]{:S(2)}) collective-permute-start(f32[264,256]{1,0:T(8,128)S(1)} %collective-permute-done.21.refs_6_), channel_id=1, source_target_pairs={{0,8},{2,10},{4,12},{6,14},{16,0},{18,2},{20,4},{22,6},{24,16},{26... | collective-permute-start | bytes 811016 | tf_op jit(solution)/shard_map/ppermute | solution.py:329
  99.8 6.5 %collective-permute-start.29 = (f32[264,256]{1,0:T(8,128)S(1)}, f32[264,256]{1,0:T(8,128)S(1)}, u32[]{:S(2)}, u32[]{:S(2)}) collective-permute-start(f32[264,256]{1,0:T(8,128)S(1)} %collective-permute-done.24.refs_3_), channel_id=1, source_target_pairs={{0,4},{2,6},{4,0},{6,2},{8,12},{10,14},{12,8},{14,10},{16,20},{18,... | collective-permute-start | bytes 811016 | tf_op jit(solution)/shard_map/ppermute | solution.py:322
  100.2 6.5 %collective-permute-start.28 = (f32[264,256]{1,0:T(8,128)S(1)}, f32[264,256]{1,0:T(8,128)S(1)}, u32[]{:S(2)}, u32[]{:S(2)}) collective-permute-start(f32[264,256]{1,0:T(8,128)S(1)} %collective-permute-done.23.refs_0_), channel_id=1, source_target_pairs={{0,2},{2,0},{4,6},{6,4},{8,10},{10,8},{12,14},{14,12},{16,18},{18,... | collective-permute-start | bytes 811016 | tf_op jit(solution)/shard_map/ppermute | solution.py:322

commit v9 on v6

v9 whole, which is shorter than its diff:
```python
import functools
import math

import jax
import jax.numpy as jnp
from jax import lax
from jax.experimental import pallas as pl
from jax.experimental.pallas import tpu as pltpu
from jax.sharding import PartitionSpec as P

prior_mass = 0.5
VMEM_LIMIT = 48 * 1024 * 1024
LANES = 128
NT = (((1,), (1,)), ((), ()))
NN = (((1,), (0,)), ((), ()))
VMEM = pl.BlockSpec(memory_space=pltpu.VMEM)
SMEM = pl.BlockSpec(memory_space=pltpu.SMEM)
ANY = pl.BlockSpec(memory_space=pl.ANY)
HBM = pl.BlockSpec(memory_space=pltpu.HBM)


def f32(*shape):
    return jax.ShapeDtypeStruct(shape, jnp.float32)


def call(kernel, out_shape, in_specs, args, name, out_specs=None, scratch=(), flops=0, aliases={}):
    return pl.pallas_call(
        kernel,
        out_shape=out_shape,
        in_specs=in_specs,
        out_specs=jax.tree.map(lambda _: VMEM, out_shape) if out_specs is None else out_specs,
        scratch_shapes=list(scratch),
        input_output_aliases=aliases,
        compiler_params=pltpu.CompilerParams(vmem_limit_bytes=VMEM_LIMIT),
        cost_estimate=pl.CostEstimate(
            flops=flops,
            bytes_accessed=sum(a.size * a.dtype.itemsize for a in args),
            transcendentals=0,
        ),
        name=name,
    )(*args)


def open_kernel(where_ref, points_ref, first_ref, second_ref, raw_ref, sem):
    half = first_ref.shape[0]
    start = pl.multiple_of(where_ref[1] * (2 * half), 2 * half)
    copy = pltpu.make_async_copy(points_ref.at[pl.ds(start, 2 * half), :], raw_ref, sem)
    copy.start()
    copy.wait()
    first_ref[...] = raw_ref[:half, :].astype(jnp.float32)
    second_ref[...] = raw_ref[half:, :].astype(jnp.float32)


def widen(norm, width):
    if width <= norm.shape[1]:
        return norm[:, :width]
    return jnp.concatenate([norm] * (width // norm.shape[1]), axis=1)


def norms(c):
    c = c.astype(jnp.float32)
    return jnp.broadcast_to(jnp.sum(c * c, axis=1, keepdims=True), (c.shape[0], LANES))


def stats_kernel(lines, where_ref, points_ref, c_ref, out_ref, twice_ref, norm_ref, all_norm_ref):
    rows, local = points_ref.shape[0], c_ref.shape[0]
    chunk = local // lines
    tile, size = min(256, rows), chunk // 4
    kept = pl.multiple_of(lax.rem(where_ref[0], 4) * size, size)
    for l in range(lines):
        c = c_ref[l * chunk : (l + 1) * chunk, :]
        all_norm_ref[...] = norms(c)
        twice = c + c
        for start in range(0, rows, tile):
            at = slice(start, start + tile)
            dots = lax.dot_general(twice, points_ref[at, :], NT, preferred_element_type=jnp.float32)
            score = dots - widen(all_norm_ref[...], tile)
            top = jnp.max(score, axis=0, keepdims=True)
            total = jnp.sum(jnp.exp(score - top), axis=0, keepdims=True)
            if l:
                old_top, old_total = out_ref[0:1, at], out_ref[1:2, at]
                new_top = jnp.maximum(old_top, top)
                total = old_total * jnp.exp(old_top - new_top) + total * jnp.exp(top - new_top)
                top = new_top
            out_ref[0:1, at] = top
            out_ref[1:2, at] = total
        mine = c_ref[pl.ds(pl.multiple_of(l * chunk + kept, size), size), :]
        twice_ref[l * size : (l + 1) * size, :] = mine + mine
        norm_ref[l * size : (l + 1) * size, :] = all_norm_ref[pl.ds(kept, size), :]


def stats(where, points, centroids, lines):
    rows, width = points.shape
    local = centroids.shape[0]
    return call(
        functools.partial(stats_kernel, lines),
        (
            f32(2, rows),
            jax.ShapeDtypeStruct((local // 4, width), jnp.bfloat16),
            f32(local // 4, LANES),
        ),
        [SMEM, VMEM, VMEM],
        (where, points, centroids),
        "stats",
        scratch=[pltpu.VMEM((local // lines, LANES), jnp.float32)],
        flops=4 * rows * local * width,
    )


def lse_kernel(cores, every, x0_ref, y1_ref, *refs):
    pair_refs = refs[:cores]
    lse_ref, evidence_ref, pack_x_ref, pack_y_ref = refs[cores:]
    half = lse_ref.shape[1]
    top = functools.reduce(jnp.maximum, [p[0:1, :] for p in pair_refs])
    total = functools.reduce(jnp.add, [p[1:2, :] * jnp.exp(p[0:1, :] - top) for p in pair_refs])
    lse = top + jnp.log(total)
    evidence = lse - math.log(every)
    for k in range(evidence_ref.shape[0]):
        evidence_ref[k : k + 1, :] = evidence[:, k * LANES : (k + 1) * LANES]
    for i in range(2 * cores):
        lse_ref[i : i + 1, :] = lse[:, i * half : (i + 1) * half]
    for piece_ref, pack_ref in ((x0_ref, pack_x_ref), (y1_ref, pack_y_ref)):
        pack_ref[0:half, :] = piece_ref[...]
        pack_ref[half:, :] = jnp.zeros_like(pack_ref[half:, :])
        pack_ref[half : half + 2 * cores, 0:half] = lse_ref[...]


def weigh(twice, norm, x, lse, lanes):
    dots = lax.dot_general(twice, x, NT, preferred_element_type=jnp.float32)
    score = dots - widen(norm, x.shape[0])
    resp = jnp.exp(score - lse).astype(jnp.bfloat16)
    part = lax.dot_general(resp, x, NN, preferred_element_type=jnp.float32)
    wide = resp.astype(jnp.float32)
    counted = functools.reduce(
        jnp.add, [wide[:, k : k + lanes] for k in range(0, x.shape[0], lanes)]
    )
    return part, counted


def own_kernel(cores, points_ref, twice_ref, norm_ref, lse_ref, acc_ref, cnt_ref):
    half = points_ref.shape[0] // (2 * cores)
    for i in range(2 * cores):
        x = points_ref[i * half : (i + 1) * half, :]
        part, counted = weigh(
            twice_ref[...], norm_ref[...], x, lse_ref[i : i + 1, :], cnt_ref.shape[1]
        )
        if i == 0:
            acc_ref[...] = part
            cnt_ref[...] = counted
        else:
            acc_ref[...] += part
            cnt_ref[...] += counted


def near_rows(cores, half, core, refs, d0_ref, d1_ref):
    whose = ((d1_ref, 0), (d0_ref, 1), (d1_ref, 1), (d0_ref, 0))
    for k, (tail_ref, part) in enumerate(whose):
        for rc in range(cores):
            at = half + 2 * (core ^ rc) + part
            yield refs[k * cores + rc], (lambda at=at, tail_ref=tail_ref: tail_ref[pl.ds(at, 1), :][:, 0:half])


def far_rows(cores, half, core, refs, lse_ref):
    for part in range(2):
        for rc in range(cores):
            at = 2 * (core ^ rc) + part
            yield refs[part * cores + rc], (lambda at=at: lse_ref[pl.ds(at, 1), :])


def add_rows(rows, half, twice_ref, norm_ref, acc_ref, cnt_ref):
    for x_ref, lse in rows:
        part, counted = weigh(
            twice_ref[...], norm_ref[...], x_ref[0:half, :].astype(jnp.bfloat16), lse(), cnt_ref.shape[1]
        )
        acc_ref[...] += part
        cnt_ref[...] += counted


def near_kernel(cores, half, where_ref, twice_ref, norm_ref, acc_in_ref, cnt_in_ref, *refs):
    near, (d0_ref, d1_ref, acc_ref, cnt_ref) = refs[: 4 * cores], refs[4 * cores :]
    acc_ref[...] = acc_in_ref[...]
    cnt_ref[...] = cnt_in_ref[...]
    rows = near_rows(cores, half, where_ref[1], near, d0_ref, d1_ref)
    add_rows(rows, half, twice_ref, norm_ref, acc_ref, cnt_ref)


def far_kernel(cores, half, where_ref, twice_ref, norm_ref, acc_in_ref, cnt_in_ref, lse_ref, *refs):
    far, (out_ref, acc_ref, cnt_ref) = refs[: 2 * cores], refs[2 * cores :]
    acc_ref[...] = acc_in_ref[...]
    cnt_ref[...] = cnt_in_ref[...]
    add_rows(far_rows(cores, half, where_ref[1], far, lse_ref), half, twice_ref, norm_ref, acc_ref, cnt_ref)
    lines, width = out_ref.shape[0], out_ref.shape[2]
    size = out_ref.shape[1] - 8
    for l in range(lines):
        turned = jnp.sum(cnt_ref[l * size : (l + 1) * size, :].T, axis=0, keepdims=True)
        if size < width:
            turned = jnp.concatenate([turned, jnp.zeros((1, width - size), jnp.float32)], axis=1)
        out_ref[l, 0:size, :] = acc_ref[l * size : (l + 1) * size, :]
        out_ref[l, size : size + 8, :] = jnp.broadcast_to(turned, (8, width))


def finish_kernel(where_ref, twice_ref, total_ref, out_ref):
    size, width = out_ref.shape[0] - 8, out_ref.shape[1]
    start = pl.multiple_of(lax.div(where_ref[0], 4) * size, size)
    c = 0.5 * twice_ref[pl.ds(start, size), :].astype(jnp.float32)
    counts = total_ref[size:, :]
    column = counts.T[:size, 0:1]
    out_ref[0:size, :] = (total_ref[0:size, :] + prior_mass * c) / (column + prior_mass)
    row = lax.broadcasted_iota(jnp.int32, (8, LANES), 0)
    spread = jnp.zeros((8, LANES), jnp.float32)
    for k in range(size // LANES):
        spread = jnp.where(row == k, counts[:, k * LANES : (k + 1) * LANES], spread)
    out_ref[size:, :] = jnp.concatenate([spread] * (width // LANES), axis=1)


def others_kernel(where_ref, column_ref, out_ref, sems):
    lines = column_ref.shape[0]
    line = lax.div(where_ref[0], 4)
    copies = [
        pltpu.make_async_copy(column_ref.at[lax.rem(line + k, lines)], out_ref.at[k - 1], sems.at[k - 1])
        for k in range(1, lines)
    ]
    for copy in copies:
        copy.start()
    for copy in copies:
        copy.wait()


def place_kernel(blocks, size, lines, later, where_ref, *refs):
    new_ref, counts_ref, tiles_ref, sems = refs[-4:]
    plane, line = lax.rem(where_ref[0], 4), lax.div(where_ref[0], 4)
    each = size // LANES
    copies, places = [], []
    for i, (array, index, bits, place, steps) in enumerate(blocks):
        ref = refs[array] if index is None else refs[array].at[index]
        at = lax.rem(line + steps, lines) if place is None else place
        places.append(at * 4 + (plane ^ bits))
        rows = pl.ds(pl.multiple_of(places[-1] * size, size), size)
        copies.append(pltpu.make_async_copy(ref.at[size : size + 8, :], tiles_ref.at[i], sems.at[0, i]))
        copies.append(pltpu.make_async_copy(ref.at[0:size, :], new_ref.at[rows, :], sems.at[1, i]))
    for copy in copies:
        copy.start()
    if later:
        counts_ref[...] = refs[-6][...]
    for copy in copies[::2]:
        copy.wait()
    for i in range(len(blocks)):
        for k in range(each):
            counts_ref[pl.ds(places[i] * each + k, 1), :] = tiles_ref[i, k : k + 1, 0:LANES]
    for copy in copies[1::2]:
        copy.wait()


def body(n, cores, points, centroids):
    rows, width = points.shape
    local_cent = centroids.shape[0]
    lines = n // 4
    half = rows // (2 * cores)
    share = local_cent // 4
    size = share // lines
    where = jnp.stack([lax.axis_index("dp"), lax.axis_index("cent")]).astype(jnp.int32)

    def flip(x, bits):
        return lax.ppermute(x, "dp", [(i, i ^ bits) for i in range(n)])

    def flip_core(x, bits):
        return lax.ppermute(x, "cent", [(i, i ^ bits) for i in range(cores)])

    def with_siblings(pieces):
        return [a if rc == 0 else flip_core(a, rc) for a in pieces for rc in range(cores)]

    first, second = call(
        open_kernel,
        (f32(half, width), f32(half, width)),
        [SMEM, HBM],
        (where, points),
        "open",
        scratch=[pltpu.VMEM((2 * half, width), points.dtype), pltpu.SemaphoreType.DMA(())],
    )
    x0, y1 = flip(first, 1), flip(second, 2)
    x1, y0 = flip(second, 1), flip(first, 2)

    pair, twice, norm = stats(where, points, centroids, lines)
    pairs = [pair] + [flip_core(pair, rc) for rc in range(1, cores)]
    tail = max(8, 2 * cores)
    lse, log_evidence, pack_x, pack_y = call(
        functools.partial(lse_kernel, cores, local_cent * cores),
        (f32(2 * cores, half), f32(rows // LANES, LANES), f32(half + tail, width), f32(half + tail, width)),
        [VMEM] * (2 + cores),
        (x0, y1, *pairs),
        "lse",
    )
    d0, d1 = flip(pack_x, 2), flip(pack_y, 1)

    lanes = min(LANES, half)
    acc, cnt = call(
        functools.partial(own_kernel, cores),
        (f32(share, width), f32(share, lanes)),
        [VMEM] * 4,
        (points, twice, norm, lse),
        "own",
        flops=4 * share * width * rows,
    )
    x0, y1, x1, y0, lse = lax.optimization_barrier((x0, y1, x1, y0, lse))
    near = with_siblings((x0, y1, x1, y0))
    near, d0, d1, acc, cnt = lax.optimization_barrier((near, d0, d1, acc, cnt))
    lse_d = flip(d1[half : half + 2 * cores, :half], 2)
    acc, cnt = call(
        functools.partial(near_kernel, cores, half),
        (f32(share, width), f32(share, lanes)),
        [SMEM] + [VMEM] * (6 + 4 * cores),
        (where, twice, norm, acc, cnt, *near, d0, d1),
        "near",
        flops=4 * share * width * 2 * rows,
        aliases={3: 0, 4: 1},
    )
    sums = call(
        functools.partial(far_kernel, cores, half),
        f32(lines, size + 8, width),
        [SMEM] + [VMEM] * (5 + 2 * cores),
        (where, twice, norm, acc, cnt, lse_d, *with_siblings((d0, d1))),
        "far",
        scratch=[pltpu.VMEM((share, width), jnp.float32), pltpu.VMEM((share, lanes), jnp.float32)],
        flops=4 * share * width * rows,
    )

    groups = [[4 * l + p for l in range(lines)] for p in range(4)]
    total = lax.psum_scatter(sums, "dp", scatter_dimension=0, axis_index_groups=groups, tiled=False)
    block_sum = f32(size + 8, width)
    done = call(finish_kernel, block_sum, [SMEM, VMEM, VMEM], (where, twice, total), "finish")

    column = lax.all_gather(done, "dp", axis_index_groups=groups)
    over_x, over_y = flip(done, 1), flip(done, 2)
    diagonal = flip(over_x, 2)
    diagonal, over_y, column = lax.optimization_barrier((diagonal, over_y, column))
    far_column = lax.all_gather(diagonal, "dp", axis_index_groups=groups)
    others = call(
        others_kernel,
        f32(lines - 1, size + 8, width),
        [SMEM, ANY],
        (where, column),
        "others",
        scratch=[pltpu.SemaphoreType.DMA((lines - 1,))],
    )
    others_x, others_y = flip(others, 1), flip(others, 2)

    steps = range(1, lines)
    stages = (
        (
            (column, over_x, over_y),
            [(0, l, 0, l, None) for l in range(lines)] + [(1, None, 1, None, 0), (2, None, 2, None, 0)],
        ),
        ((far_column,), [(0, l, 3, l, None) for l in range(lines)]),
        (
            (others_x, others_y),
            [(a, k - 1, a + 1, None, k) for a in range(2) for k in steps],
        ),
    )
    new = counts = None
    for later, (arrays, blocks) in enumerate(stages):
        args = [where, *arrays] + ([counts, new] if later else [])
        new, counts = call(
            functools.partial(place_kernel, blocks, size, lines, later),
            (f32(local_cent, width), f32(local_cent // LANES, LANES)),
            [SMEM] + [ANY] * len(arrays) + ([VMEM, ANY] if later else []),
            args,
            ("place_early", "place_middle", "place_late")[later],
            out_specs=(ANY, VMEM),
            scratch=[
                pltpu.VMEM((len(blocks), 8, width), jnp.float32),
                pltpu.SemaphoreType.DMA((2, len(blocks))),
            ],
            aliases={len(args) - 1: 0} if later else {},
        )
    return new, counts.reshape(-1), log_evidence.reshape(-1)


def solution(mesh):
    n, cores = mesh.shape["dp"], mesh.shape["cent"]
    return jax.shard_map(
        functools.partial(body, n, cores),
        mesh=mesh,
        in_specs=(P("dp", None), P("cent", None)),
        out_specs=(P("cent", None), P("cent"), P("dp")),
        check_vma=False,
    )
```

time: 110 us -> 144 us (1.31)
  waiting for transfers between devices: 37.6 us -> 83.3 us
  starting transfers between devices: 46.7 us -> 16.4 us
  between operations: 0.94 us -> 13.9 us
  local copies, waits for them, and re-layouts: 2.64 us -> 6.06 us
  Pallas kernels: 21.6 us -> 23.6 us
    all_gather x0 -> x2, waiting for transfers between devices: none -> 34.6 us  [the longest x1 22.8 us: body(): far_column = lax.all_gather(diagonal, 'dp', axis_index_groups=groups)]
    reduce_scatter x0 -> x1, waiting for transfers between devices: none -> 28.1 us  [body(): lax.psum_scatter(sums, 'dp', scatter_dimension=0, axis_index_groups=group...]
    ppermute x8 -> x0, waiting for transfers between devices: 25.9 us -> none  [ring(): lax.ppermute(x, 'dp', [(4 * a + i, 4 * b + i) for a, b in pairs for i in...]
    ppermute x8 -> x0, starting transfers between devices: 18 us -> none  [ring(): lax.ppermute(x, 'dp', [(4 * a + i, 4 * b + i) for a, b in pairs for i in...]
    ppermute x19 -> x12, starting transfers between devices: 27.4 us -> 15.2 us  [flip(): return lax.ppermute(x, 'dp', [(i, i ^ bits) for i in range(n)])]
    ppermute x19 -> x12, waiting for transfers between devices: 11.7 us -> 19.3 us  [flip(): return lax.ppermute(x, 'dp', [(i, i ^ bits) for i in range(n)])]
    unnamed x6 -> x14, local copies, waits for them, and re-layouts: 2.64 us -> 6.06 us
    pallas_call x11, Pallas kernels: 21.6 us -> 23.6 us  [call(): pl.pallas_call(kernel, out_shape=out_shape, in_specs=in_specs, out_specs=...]
  transfers between devices with their start and end apart: 34 -> 22, of which waited for: 13 -> 10; matrix products, arithmetic and copies ran while one was open for 0% -> 0% of each run, Pallas kernels for 14% -> 11%
where the time goes in v9:
time: 144 us; the launch traced here: 143 us
  waiting for transfers between devices  83.3 us (58%)
  Pallas kernels  23.6 us (16%)
  starting transfers between devices  16.4 us (11%)
  between operations  13.9 us (10%)
  local copies, waits for them, and re-layouts  6.06 us (4%)
    reduce_scatter x1, waiting for transfers between devices, body(): lax.psum_scatter(sums, 'dp', scatter_dimension=0, axis_index_groups=group...  28.1 us
    pallas_call x11, Pallas kernels, call(): pl.pallas_call(kernel, out_shape=out_shape, in_specs=in_specs, out_specs=...  23.6 us
    all_gather x1, waiting for transfers between devices, body(): far_column = lax.all_gather(diagonal, 'dp', axis_index_groups=groups)  22.8 us
    ppermute x12, waiting for transfers between devices, flip(): return lax.ppermute(x, 'dp', [(i, i ^ bits) for i in range(n)])  19.3 us
    ppermute x12, starting transfers between devices, flip(): return lax.ppermute(x, 'dp', [(i, i ^ bits) for i in range(n)])  15.2 us
    all_gather x1, waiting for transfers between devices, body(): column = lax.all_gather(done, 'dp', axis_index_groups=groups)  11.8 us
    unnamed x14, local copies, waits for them, and re-layouts  6.06 us
  transfers between devices with their start and end apart: 22, of which 10 were waited for; matrix products, arithmetic and copies ran while one was open for 0% of the time, Pallas kernels for 11%

profile of v9, /device:TPU:0, one launch (start us, length us, event | category | flops | bytes accessed | tf_op | source)
XLA Modules:
  0.0 143.3 jit_solution(15464065687525121977)
XLA Ops:
  7.2 0.0 reduce-scatter.2.cloned.1.call-start
  7.2 0.1 pad_add_fusion.where_ref
  7.3 1.0 copy-done.2
  8.3 0.6 open.1
  8.9 3.0 %collective-permute-start.1 = (f32[256,256]{1,0:T(8,128)S(1)}, f32[256,256]{1,0:T(8,128)S(1)}, u32[]{:S(2)}, u32[]{:S(2)}) collective-permute-start(f32[256,256]{1,0:T(8,128)S(1)} %get-tuple-element.44), channel_id=1, source_target_pairs={{0,4},{2,6},{4,0},{6,2},{8,12},{10,14},{12,8},{14,10},{16,20},{18,... | collective-permute-start | bytes 786440 | tf_op jit(solution)/shard_map/ppermute | solution.py:264
  12.0 1.5 %collective-permute-start.2 = (f32[256,256]{1,0:T(8,128)S(1)}, f32[256,256]{1,0:T(8,128)S(1)}, u32[]{:S(2)}, u32[]{:S(2)}) collective-permute-start(f32[256,256]{1,0:T(8,128)S(1)} %get-tuple-element.44), channel_id=1, source_target_pairs={{0,2},{2,0},{4,6},{6,4},{8,10},{10,8},{12,14},{14,12},{16,18},{18,... | collective-permute-start | bytes 786440 | tf_op jit(solution)/shard_map/ppermute | solution.py:264
  13.5 0.5 collective-permute-start
  14.0 0.1 collective-permute-start.3
  14.1 1.6 %copy-done.5 = bf16[4096,256]{1,0:T(8,128)(2,1)S(1)} copy-done((bf16[4096,256]{1,0:T(8,128)(2,1)S(1)}, bf16[4096,256]{1,0:T(8,128)(2,1)}, u32[]{:S(2)}) %copy-start.5) | copy-done | bytes 2097176
  15.7 5.9 %stats.1 = (f32[2,1024]{1,0:T(2,128)S(1)}, bf16[1024,256]{1,0:T(8,128)(2,1)S(1)}, f32[1024,128]{1,0:T(8,128)S(1)}) custom-call(s32[2]{0:T(128)S(1)} %pad_add_fusion.where_ref, bf16[1024,256]{1,0:T(8,128)(2,1)S(1)} %copy-done.2, bf16[4096,256]{1,0:T(8,128)(2,1)S(1)} %copy-done.5), custom_call_target="tpu_custom_call" | custom-call | flops 4294967296 | bytes 2621448 | tf_op jit(solution)/shard_map/stats/pallas_call | solution.py:27
  21.6 0.1 collective-permute-start.4
  21.7 1.2 collective-permute-done.4.refs_1_
  22.8 2.5 %collective-permute-done.x0_ref.refs_0_ = f32[256,256]{1,0:T(8,128)S(1)} collective-permute-done((f32[256,256]{1,0:T(8,128)S(1)}, f32[256,256]{1,0:T(8,128)S(1)}, u32[]{:S(2)}, u32[]{:S(2)}) %collective-permute-start) | collective-permute-done | bytes 262176 | tf_op jit(solution)/shard_map/ppermute | solution.py:264
  25.4 0.6 lse.1
  26.0 1.6 %collective-permute-start.10 = (f32[264,256]{1,0:T(8,128)S(1)}, f32[264,256]{1,0:T(8,128)S(1)}, u32[]{:S(2)}, u32[]{:S(2)}) collective-permute-start(f32[264,256]{1,0:T(8,128)S(1)} %get-tuple-element.52), channel_id=1, source_target_pairs={{0,2},{2,0},{4,6},{6,4},{8,10},{10,8},{12,14},{14,12},{16,18},{18,... | collective-permute-start | bytes 811016 | tf_op jit(solution)/shard_map/ppermute | solution.py:264
  27.6 0.5 collective-permute-start.9
  28.1 0.5 collective-permute-start.7
  28.6 1.6 %own.1 = (f32[1024,256]{1,0:T(8,128)S(1)}, f32[1024,128]{1,0:T(8,128)S(1)}) custom-call(bf16[1024,256]{1,0:T(8,128)(2,1)S(1)} %copy-done.3, bf16[1024,256]{1,0:T(8,128)(2,1)S(1)} %get-tuple-element.41.twice_ref, f32[1024,128]{1,0:T(8,128)S(1)} %get-tuple-element.42.norm_ref, f32[4,256]{1,0:T(4,128)S(1)} %get-tuple-element.46.lse_ref), custom_call_target="tpu_custom_call" | custom-call | flops 1073741824 | bytes 1576960 | tf_op jit(solution)/shard_map/own/pallas_call | solution.py:27
  30.2 0.1 collective-permute-done.8.refs_7_
  30.4 4.5 %collective-permute-done.10.refs_9_.refs_2_ = f32[264,256]{1,0:T(8,128)S(1)} collective-permute-done((f32[264,256]{1,0:T(8,128)S(1)}, f32[264,256]{1,0:T(8,128)S(1)}, u32[]{:S(2)}, u32[]{:S(2)}) %collective-permute-start.10) | collective-permute-done | bytes 270368 | tf_op jit(solution)/shard_map/ppermute | solution.py:264
  34.9 1.2 collective-permute-done.9.refs_8_.refs_0_
  36.1 0.5 collective-permute-start.13
  36.6 0.5 collective-permute-start.11
  37.1 3.6 %near.1 = (f32[1024,256]{1,0:T(8,128)S(1)}, f32[1024,128]{1,0:T(8,128)S(1)}) custom-call(s32[2]{0:T(128)S(1)} %pad_add_fusion.where_ref, bf16[1024,256]{1,0:T(8,128)(2,1)S(1)} %get-tuple-element.41.twice_ref, f32[1024,128]{1,0:T(8,128)S(1)} %get-tuple-element.42.norm_ref, ...), custom_call_target="tpu_custom_call", output_to_operand_aliasing={{0}: (3, {}), {1}: (4, {})} | custom-call | flops 2147483648 | bytes 5259272 | tf_op jit(solution)/shard_map/near/pallas_call | solution.py:27
  40.8 3.2 %far.1 = f32[4,264,256]{2,1,0:T(8,128)} custom-call(s32[2]{0:T(128)S(1)} %pad_add_fusion.where_ref, bf16[1024,256]{1,0:T(8,128)(2,1)S(1)} %get-tuple-element.41.twice_ref, f32[1024,128]{1,0:T(8,128)S(1)} %get-tuple-element.42.norm_ref, f32[1024,256]{1,0:T(8,128)S(1)} %get-tuple-element.67.acc_in_ref, f32[1024,128]{1,0:T(8,128)S(1)} %get-tuple-element.68.cnt_in_ref, ...), custom_call_target="tpu_custom_call" | custom-call | flops 1073741824 | bytes 3706888 | tf_op jit(solution)/shard_map/far/pallas_call | solution.py:27
  44.0 0.0 reduce-scatter.2.cloned.1.call-update
  44.1 0.0 all-gather.5.cloned.1.call-start
  44.1 28.1 %reduce-scatter.2.cloned.1.call-done = f32[1,264,256]{2,1,0:T(8,128)} async-done(((f32[4,264,256]{2,1,0:T(8,128)}), f32[1,264,256]{2,1,0:T(8,128)}) %reduce-scatter.2.cloned.1.call-update) | async-done | bytes 270352 | tf_op jit(solution)/shard_map/reduce_scatter | solution.py:328
  72.2 1.0 copy-done.4
  73.1 1.5 %finish.1 = f32[264,256]{1,0:T(8,128)} custom-call(s32[2]{0:T(128)S(1)} %pad_add_fusion.where_ref, bf16[1024,256]{1,0:T(8,128)(2,1)S(1)} %get-tuple-element.41.twice_ref, f32[264,256]{1,0:T(8,128)S(1)} %bitcast.10), custom_call_target="tpu_custom_call" | custom-call | bytes 794632 | tf_op jit(solution)/shard_map/finish/pallas_call | solution.py:27
  74.6 0.0 all-gather.5.cloned.1.call-update
  74.7 0.0 all-gather.7.cloned.1.call-start
  74.7 1.5 %collective-permute-start.14 = (f32[264,256]{1,0:T(8,128)}, f32[264,256]{1,0:T(8,128)S(1)}, u32[]{:S(2)}, u32[]{:S(2)}) collective-permute-start(f32[264,256]{1,0:T(8,128)} %finish.1), channel_id=1, source_target_pairs={{0,2},{2,0},{4,6},{6,4},{8,10},{10,8},{12,14},{14,12},{16,18},{18,... | collective-permute-start | bytes 811016 | tf_op jit(solution)/shard_map/ppermute | solution.py:264
  76.3 1.5 %collective-permute-start.16 = (f32[264,256]{1,0:T(8,128)}, f32[264,256]{1,0:T(8,128)S(1)}, u32[]{:S(2)}, u32[]{:S(2)}) collective-permute-start(f32[264,256]{1,0:T(8,128)} %finish.1), channel_id=1, source_target_pairs={{0,4},{2,6},{4,0},{6,2},{8,12},{10,14},{12,8},{14,10},{16,20},{18,... | collective-permute-start | bytes 811016 | tf_op jit(solution)/shard_map/ppermute | solution.py:264
  77.7 5.3 %collective-permute-done.14.refs_1_ = f32[264,256]{1,0:T(8,128)S(1)} collective-permute-done((f32[264,256]{1,0:T(8,128)}, f32[264,256]{1,0:T(8,128)S(1)}, u32[]{:S(2)}, u32[]{:S(2)}) %collective-permute-start.14) | collective-permute-done | bytes 270368 | tf_op jit(solution)/shard_map/ppermute | solution.py:264
  83.0 1.5 %collective-permute-start.15 = (f32[264,256]{1,0:T(8,128)S(1)}, f32[264,256]{1,0:T(8,128)S(1)}, u32[]{:S(2)}, u32[]{:S(2)}) collective-permute-start(f32[264,256]{1,0:T(8,128)S(1)} %collective-permute-done.14.refs_1_), channel_id=1, source_target_pairs={{0,4},{2,6},{4,0},{6,2},{8,12},{10,14},{12,8},{14,10},{16,20},{18,... | collective-permute-start | bytes 811016 | tf_op jit(solution)/shard_map/ppermute | solution.py:264
  84.5 5.7 %collective-permute-done.15 = f32[264,256]{1,0:T(8,128)S(1)} collective-permute-done((f32[264,256]{1,0:T(8,128)S(1)}, f32[264,256]{1,0:T(8,128)S(1)}, u32[]{:S(2)}, u32[]{:S(2)}) %collective-permute-start.15) | collective-permute-done | bytes 270368 | tf_op jit(solution)/shard_map/ppermute | solution.py:264
  90.2 11.8 %all-gather.5.cloned.1.call-done = f32[1056,256]{1,0:T(8,128)} async-done(((f32[264,256]{1,0:T(8,128)}), f32[1056,256]{1,0:T(8,128)}) %all-gather.5.cloned.1.call-update) | async-done | bytes 1081360 | tf_op jit(solution)/shard_map/all_gather | solution.py:332
  102.0 0.0 all-gather.7.cloned.1.call-update
  102.0 1.2 copy-done
  103.2 0.7 others.1
  103.9 1.5 %collective-permute-start.17 = (f32[3,264,256]{2,1,0:T(8,128)S(1)}, f32[3,264,256]{2,1,0:T(8,128)S(1)}, u32[]{:S(2)}, u32[]{:S(2)}) collective-permute-start(f32[3,264,256]{2,1,0:T(8,128)S(1)} %others.1), channel_id=1, source_target_pairs={{0,2},{2,0},{4,6},{6,4},{8,10},{10,8},{12,14},{14,12},{16,18},{18,... | collective-permute-start | bytes 2433032 | tf_op jit(solution)/shard_map/ppermute | solution.py:264
  105.4 1.5 %collective-permute-start.18 = (f32[3,264,256]{2,1,0:T(8,128)S(1)}, f32[3,264,256]{2,1,0:T(8,128)S(1)}, u32[]{:S(2)}, u32[]{:S(2)}) collective-permute-start(f32[3,264,256]{2,1,0:T(8,128)S(1)} %others.1), channel_id=1, source_target_pairs={{0,4},{2,6},{4,0},{6,2},{8,12},{10,14},{12,8},{14,10},{16,20},{18,... | collective-permute-start | bytes 2433032 | tf_op jit(solution)/shard_map/ppermute | solution.py:264
  106.9 1.8 %place_early.1 = (f32[4096,256]{1,0:T(8,128)}, f32[32,128]{1,0:T(8,128)S(1)}) custom-call(s32[2]{0:T(128)S(1)} %pad_add_fusion.where_ref, f32[4,264,256]{2,1,0:T(8,128)S(1)} %bitcast.8, f32[264,256]{1,0:T(8,128)S(1)} %collective-permute-done.14.refs_1_, f32[264,256]{1,0:T(8,128)S(1)} %collective-permute-done.16.refs_2_), custom_call_target="tpu_custom_call" | custom-call | bytes 1622024 | tf_op jit(solution)/shard_map/place_early/pallas_call | solution.py:27
  108.7 22.8 %all-gather.7.cloned.1.call-done = f32[1056,256]{1,0:T(8,128)} async-done(((f32[264,256]{1,0:T(8,128)}), f32[1056,256]{1,0:T(8,128)}) %all-gather.7.cloned.1.call-update) | async-done | bytes 1081360 | tf_op jit(solution)/shard_map/all_gather | solution.py:336
  131.5 1.2 copy-done.1
  132.8 1.6 %place_middle.1 = (f32[4096,256]{1,0:T(8,128)}, f32[32,128]{1,0:T(8,128)S(1)}) custom-call(s32[2]{0:T(128)S(1)} %pad_add_fusion.where_ref, f32[4,264,256]{2,1,0:T(8,128)S(1)} %bitcast.9, f32[32,128]{1,0:T(8,128)S(1)} %get-tuple-element.72.refs_1_, f32[4096,256]{1,0:T(8,128)} %get-tuple-element.73.refs_2_), custom_call_target="tpu_custom_call", output_to_operand_aliasing={{0}: (3, {})} | custom-call | bytes 5292040 | tf_op jit(solution)/shard_map/place_middle/pallas_call | solution.py:27
  134.4 2.4 %place_late.1 = (f32[4096,256]{1,0:T(8,128)}, f32[32,128]{1,0:T(8,128)}) custom-call(s32[2]{0:T(128)S(1)} %pad_add_fusion.where_ref, f32[3,264,256]{2,1,0:T(8,128)S(1)} %collective-permute-done.17.refs_0_, f32[3,264,256]{2,1,0:T(8,128)S(1)} %collective-permute-done.18.refs_1_, ...), custom_call_target="tpu_custom_call", output_to_operand_aliasing={{0}: (4, {})} | custom-call | bytes 5832712 | tf_op jit(solution)/shard_map/place_late/pallas_call | solution.py:27
  (26 shorter events, 0.1 us)
Async XLA Ops:
  7.2 65.0 %reduce-scatter.2.cloned.1.call-start = ((), (), s32[]{:S(2)}) async-start(), calls=%async_computation.1 | async-start | bytes 1351680 | tf_op jit(solution)/shard_map/reduce_scatter | solution.py:328
  7.3 1.0 copy-start.2
  8.9 16.4 %collective-permute-start.1 = (f32[256,256]{1,0:T(8,128)S(1)}, f32[256,256]{1,0:T(8,128)S(1)}, u32[]{:S(2)}, u32[]{:S(2)}) collective-permute-start(f32[256,256]{1,0:T(8,128)S(1)} %get-tuple-element.44), channel_id=1, source_target_pairs={{0,4},{2,6},{4,0},{6,2},{8,12},{10,14},{12,8},{14,10},{16,20},{18,... | collective-permute-start | bytes 786440 | tf_op jit(solution)/shard_map/ppermute | solution.py:264
  12.0 14.0 %collective-permute-start.2 = (f32[256,256]{1,0:T(8,128)S(1)}, f32[256,256]{1,0:T(8,128)S(1)}, u32[]{:S(2)}, u32[]{:S(2)}) collective-permute-start(f32[256,256]{1,0:T(8,128)S(1)} %get-tuple-element.44), channel_id=1, source_target_pairs={{0,2},{2,0},{4,6},{6,4},{8,10},{10,8},{12,14},{14,12},{16,18},{18,... | collective-permute-start | bytes 786440 | tf_op jit(solution)/shard_map/ppermute | solution.py:264
  13.5 15.1 %copy-start.3 = (bf16[1024,256]{1,0:T(8,128)(2,1)S(1)}, bf16[1024,256]{1,0:T(8,128)(2,1)}, u32[]{:S(2)}) copy-start(bf16[1024,256]{1,0:T(8,128)(2,1)} %points_ref.5) | copy-start | bytes 1572868
  13.5 11.9 %collective-permute-start = (f32[256,256]{1,0:T(8,128)S(1)}, f32[256,256]{1,0:T(8,128)S(1)}, u32[]{:S(2)}, u32[]{:S(2)}) collective-permute-start(f32[256,256]{1,0:T(8,128)S(1)} %get-tuple-element.43), channel_id=1, source_target_pairs={{0,2},{2,0},{4,6},{6,4},{8,10},{10,8},{12,14},{14,12},{16,18},{18,... | collective-permute-start | bytes 786440 | tf_op jit(solution)/shard_map/ppermute | solution.py:264
  14.0 12.0 %collective-permute-start.3 = (f32[256,256]{1,0:T(8,128)S(1)}, f32[256,256]{1,0:T(8,128)S(1)}, u32[]{:S(2)}, u32[]{:S(2)}) collective-permute-start(f32[256,256]{1,0:T(8,128)S(1)} %get-tuple-element.43), channel_id=1, source_target_pairs={{0,4},{2,6},{4,0},{6,2},{8,12},{10,14},{12,8},{14,10},{16,20},{18,... | collective-permute-start | bytes 786440 | tf_op jit(solution)/shard_map/ppermute | solution.py:264
  14.1 1.6 %copy-start.5 = (bf16[4096,256]{1,0:T(8,128)(2,1)S(1)}, bf16[4096,256]{1,0:T(8,128)(2,1)}, u32[]{:S(2)}) copy-start(bf16[4096,256]{1,0:T(8,128)(2,1)} %c_ref.1) | copy-start | bytes 6291460
  21.6 1.2 collective-permute-start.4
  26.0 2.6 %collective-permute-start.5 = (f32[256,256]{1,0:T(8,128)S(1)}, f32[256,256]{1,0:T(8,128)S(1)}, u32[]{:S(2)}, u32[]{:S(2)}) collective-permute-start(f32[256,256]{1,0:T(8,128)S(1)} %collective-permute-done.x0_ref.refs_0_), channel_id=1, source_target_pairs={{0,1},{1,0},{2,3},{3,2},{4,5},{5,4},{6,7},{7,6},{8,9},{9,8},{10,11... | collective-permute-start | bytes 786440 | tf_op jit(solution)/shard_map/ppermute | solution.py:267
  26.0 8.9 %collective-permute-start.10 = (f32[264,256]{1,0:T(8,128)S(1)}, f32[264,256]{1,0:T(8,128)S(1)}, u32[]{:S(2)}, u32[]{:S(2)}) collective-permute-start(f32[264,256]{1,0:T(8,128)S(1)} %get-tuple-element.52), channel_id=1, source_target_pairs={{0,2},{2,0},{4,6},{6,4},{8,10},{10,8},{12,14},{14,12},{16,18},{18,... | collective-permute-start | bytes 811016 | tf_op jit(solution)/shard_map/ppermute | solution.py:264
  27.6 8.5 %collective-permute-start.9 = (f32[264,256]{1,0:T(8,128)S(1)}, f32[264,256]{1,0:T(8,128)S(1)}, u32[]{:S(2)}, u32[]{:S(2)}) collective-permute-start(f32[264,256]{1,0:T(8,128)S(1)} %get-tuple-element.51), channel_id=1, source_target_pairs={{0,4},{2,6},{4,0},{6,2},{8,12},{10,14},{12,8},{14,10},{16,20},{18,... | collective-permute-start | bytes 811016 | tf_op jit(solution)/shard_map/ppermute | solution.py:264
  28.1 2.1 %collective-permute-start.6 = (f32[256,256]{1,0:T(8,128)S(1)}, f32[256,256]{1,0:T(8,128)S(1)}, u32[]{:S(2)}, u32[]{:S(2)}) collective-permute-start(f32[256,256]{1,0:T(8,128)S(1)} %collective-permute-done.1.y1_ref.refs_2_), channel_id=1, source_target_pairs={{0,1},{1,0},{2,3},{3,2},{4,5},{5,4},{6,7},{7,6},{8,9},{9,8},{10,11... | collective-permute-start | bytes 786440 | tf_op jit(solution)/shard_map/ppermute | solution.py:267
  28.1 2.1 %collective-permute-start.7 = (f32[256,256]{1,0:T(8,128)S(1)}, f32[256,256]{1,0:T(8,128)S(1)}, u32[]{:S(2)}, u32[]{:S(2)}) collective-permute-start(f32[256,256]{1,0:T(8,128)S(1)} %collective-permute-done.2.refs_4_), channel_id=1, source_target_pairs={{0,1},{1,0},{2,3},{3,2},{4,5},{5,4},{6,7},{7,6},{8,9},{9,8},{10,11... | collective-permute-start | bytes 786440 | tf_op jit(solution)/shard_map/ppermute | solution.py:267
  28.6 1.8 %collective-permute-start.8 = (f32[256,256]{1,0:T(8,128)S(1)}, f32[256,256]{1,0:T(8,128)S(1)}, u32[]{:S(2)}, u32[]{:S(2)}) collective-permute-start(f32[256,256]{1,0:T(8,128)S(1)} %collective-permute-done.3.refs_6_), channel_id=1, source_target_pairs={{0,1},{1,0},{2,3},{3,2},{4,5},{5,4},{6,7},{7,6},{8,9},{9,8},{10,11... | collective-permute-start | bytes 786440 | tf_op jit(solution)/shard_map/ppermute | solution.py:267
  36.1 4.7 %collective-permute-start.12 = (f32[264,256]{1,0:T(8,128)S(1)}, f32[264,256]{1,0:T(8,128)S(1)}, u32[]{:S(2)}, u32[]{:S(2)}) collective-permute-start(f32[264,256]{1,0:T(8,128)S(1)} %collective-permute-done.9.refs_8_.refs_0_), channel_id=1, source_target_pairs={{0,1},{1,0},{2,3},{3,2},{4,5},{5,4},{6,7},{7,6},{8,9},{9,8},{10,11... | collective-permute-start | bytes 811016 | tf_op jit(solution)/shard_map/ppermute | solution.py:267
  36.1 4.7 %collective-permute-start.13 = (f32[264,256]{1,0:T(8,128)S(1)}, f32[264,256]{1,0:T(8,128)S(1)}, u32[]{:S(2)}, u32[]{:S(2)}) collective-permute-start(f32[264,256]{1,0:T(8,128)S(1)} %collective-permute-done.10.refs_9_.refs_2_), channel_id=1, source_target_pairs={{0,1},{1,0},{2,3},{3,2},{4,5},{5,4},{6,7},{7,6},{8,9},{9,8},{10,11... | collective-permute-start | bytes 811016 | tf_op jit(solution)/shard_map/ppermute | solution.py:267
  36.6 4.2 %collective-permute-start.11 = (f32[4,256]{1,0:T(4,128)S(1)}, f32[4,256]{1,0:T(4,128)S(1)}, u32[]{:S(2)}, u32[]{:S(2)}) collective-permute-start(f32[4,256]{1,0:T(4,128)S(1)} %slice.3), channel_id=1, source_target_pairs={{0,4},{2,6},{4,0},{6,2},{8,12},{10,14},{12,8},{14,10},{16,20},{18,... | collective-permute-start | bytes 12296 | tf_op jit(solution)/shard_map/ppermute | solution.py:264
  44.1 57.9 %all-gather.5.cloned.1.call-start = ((), (), s32[]{:S(2)}) async-start(), calls=%async_computation.2 | async-start | bytes 1351680 | tf_op jit(solution)/shard_map/all_gather | solution.py:332
  72.2 1.0 copy-start.4
  74.7 56.9 %all-gather.7.cloned.1.call-start = ((), (), s32[]{:S(2)}) async-start(), calls=%async_computation.3 | async-start | bytes 1351680 | tf_op jit(solution)/shard_map/all_gather | solution.py:336
  74.7 8.3 %collective-permute-start.14 = (f32[264,256]{1,0:T(8,128)}, f32[264,256]{1,0:T(8,128)S(1)}, u32[]{:S(2)}, u32[]{:S(2)}) collective-permute-start(f32[264,256]{1,0:T(8,128)} %finish.1), channel_id=1, source_target_pairs={{0,2},{2,0},{4,6},{6,4},{8,10},{10,8},{12,14},{14,12},{16,18},{18,... | collective-permute-start | bytes 811016 | tf_op jit(solution)/shard_map/ppermute | solution.py:264
  76.3 8.3 %collective-permute-start.16 = (f32[264,256]{1,0:T(8,128)}, f32[264,256]{1,0:T(8,128)S(1)}, u32[]{:S(2)}, u32[]{:S(2)}) collective-permute-start(f32[264,256]{1,0:T(8,128)} %finish.1), channel_id=1, source_target_pairs={{0,4},{2,6},{4,0},{6,2},{8,12},{10,14},{12,8},{14,10},{16,20},{18,... | collective-permute-start | bytes 811016 | tf_op jit(solution)/shard_map/ppermute | solution.py:264
  83.0 7.2 %collective-permute-start.15 = (f32[264,256]{1,0:T(8,128)S(1)}, f32[264,256]{1,0:T(8,128)S(1)}, u32[]{:S(2)}, u32[]{:S(2)}) collective-permute-start(f32[264,256]{1,0:T(8,128)S(1)} %collective-permute-done.14.refs_1_), channel_id=1, source_target_pairs={{0,4},{2,6},{4,0},{6,2},{8,12},{10,14},{12,8},{14,10},{16,20},{18,... | collective-permute-start | bytes 811016 | tf_op jit(solution)/shard_map/ppermute | solution.py:264
  90.2 11.8 %copy-start.6 = (f32[264,256]{1,0:T(8,128)}, f32[264,256]{1,0:T(8,128)S(1)}, u32[]{:S(2)}) copy-start(f32[264,256]{1,0:T(8,128)S(1)} %collective-permute-done.15) | copy-start | bytes 811012
  102.0 1.2 copy-start
  103.9 30.5 %collective-permute-start.17 = (f32[3,264,256]{2,1,0:T(8,128)S(1)}, f32[3,264,256]{2,1,0:T(8,128)S(1)}, u32[]{:S(2)}, u32[]{:S(2)}) collective-permute-start(f32[3,264,256]{2,1,0:T(8,128)S(1)} %others.1), channel_id=1, source_target_pairs={{0,2},{2,0},{4,6},{6,4},{8,10},{10,8},{12,14},{14,12},{16,18},{18,... | collective-permute-start | bytes 2433032 | tf_op jit(solution)/shard_map/ppermute | solution.py:264
  105.4 28.9 %collective-permute-start.18 = (f32[3,264,256]{2,1,0:T(8,128)S(1)}, f32[3,264,256]{2,1,0:T(8,128)S(1)}, u32[]{:S(2)}, u32[]{:S(2)}) collective-permute-start(f32[3,264,256]{2,1,0:T(8,128)S(1)} %others.1), channel_id=1, source_target_pairs={{0,4},{2,6},{4,0},{6,2},{8,12},{10,14},{12,8},{14,10},{16,20},{18,... | collective-permute-start | bytes 2433032 | tf_op jit(solution)/shard_map/ppermute | solution.py:264
  131.5 1.2 copy-start.1
Sparse Core Ops, SparseCore 0:
  44.2 27.9 reduce-scatter.1
  74.8 27.1 all-gather.4
  103.5 27.9 all-gather.6

commit v10 on v8

--- a/solution.py
+++ b/solution.py
@@ -107,9 +107,9 @@
     )
 
 
-def lse_kernel(cores, every, x0_ref, y1_ref, *refs):
+def lse_kernel(cores, every, a0_ref, b1_ref, *refs):
     pair_refs = refs[:cores]
-    lse_ref, evidence_ref, pack_x_ref, pack_y_ref = refs[cores:]
+    lse_ref, evidence_ref, pack_a_ref, pack_b_ref = refs[cores:]
     half = lse_ref.shape[1]
     top = functools.reduce(jnp.maximum, [p[0:1, :] for p in pair_refs])
     total = functools.reduce(jnp.add, [p[1:2, :] * jnp.exp(p[0:1, :] - top) for p in pair_refs])
@@ -119,7 +119,7 @@
         evidence_ref[k : k + 1, :] = evidence[:, k * LANES : (k + 1) * LANES]
     for i in range(2 * cores):
         lse_ref[i : i + 1, :] = lse[:, i * half : (i + 1) * half]
-    for piece_ref, pack_ref in ((x0_ref, pack_x_ref), (y1_ref, pack_y_ref)):
+    for piece_ref, pack_ref in ((a0_ref, pack_a_ref), (b1_ref, pack_b_ref)):
         pack_ref[0:half, :] = piece_ref[...]
         pack_ref[half:, :] = jnp.zeros_like(pack_ref[half:, :])
         pack_ref[half : half + 2 * cores, 0:half] = lse_ref[...]
@@ -153,10 +153,10 @@
 
 
 def near_rows(cores, half, core, refs, d0_ref, d1_ref):
-    whose = ((d1_ref, 0), (d0_ref, 1), (d1_ref, 1), (d0_ref, 0))
-    for k, (tail_ref, part) in enumerate(whose):
+    for k, (kind, part) in enumerate(((0, 0), (1, 1), (0, 1), (1, 0))):
         for rc in range(cores):
             at = half + 2 * (core ^ rc) + part
+            tail_ref = d1_ref if (kind + rc) % 2 == 0 else d0_ref
             yield refs[k * cores + rc], (lambda at=at, tail_ref=tail_ref: tail_ref[pl.ds(at, 1), :][:, 0:half])
 
 
@@ -216,9 +216,8 @@
     store_sums(out_ref, acc, cnt)
 
 
-def first_kernel(cores, order, half, ahead_steps, where_ref, twice_ref, norm_ref, acc_ref, cnt_ref, lse_ref, lead_acc_ref, lead_cnt_ref, *refs):
-    near, far = refs[: 4 * cores], refs[4 * cores : 6 * cores]
-    out_refs = refs[6 * cores :]
+def first_kernel(cores, order, half, where_ref, twice_ref, norm_ref, lse_ref, lead_acc_ref, lead_cnt_ref, *refs):
+    far, out_ref = refs[: 2 * cores], refs[2 * cores]
     size = lead_acc_ref.shape[0]
     place = ahead(order, lax.div(where_ref[0], 4), len(order) // 2)
     at = pl.ds(pl.multiple_of(place * size, size), size)
@@ -230,31 +229,15 @@
         lead_acc_ref[...],
         lead_cnt_ref[...],
     )
-    store_sums(out_refs[0], acc, cnt)
-
-    @pl.when(lax.rem(where_ref[1], 2) == 1)
-    def _():
-        for steps, out_ref in zip(ahead_steps, out_refs[1:]):
-            block_sums(cores, order, half, steps, where_ref, twice_ref, norm_ref, acc_ref, cnt_ref, lse_ref, near, far, out_ref)
+    store_sums(out_ref, acc, cnt)
 
 
 def rest_kernel(cores, order, half, steps, where_ref, twice_ref, norm_ref, acc_ref, cnt_ref, lse_ref, *refs):
     near, far = refs[: 4 * cores], refs[4 * cores : 6 * cores]
-    given, out_ref = refs[6 * cores : -1], refs[-1]
-    make = functools.partial(
-        block_sums, cores, order, half, steps,
-        where_ref, twice_ref, norm_ref, acc_ref, cnt_ref, lse_ref, near, far, out_ref,
-    )
-    if not given:
-        make()
-        return
-    odd = lax.rem(where_ref[1], 2) == 1
-
-    @pl.when(odd)
-    def _():
-        out_ref[...] = given[0][...]
-
-    pl.when(jnp.logical_not(odd))(make)
+    for s, out_ref in zip(steps, refs[6 * cores :]):
+        block_sums(
+            cores, order, half, s, where_ref, twice_ref, norm_ref, acc_ref, cnt_ref, lse_ref, near, far, out_ref
+        )
 
 
 def ahead(order, line, steps):
@@ -291,7 +274,9 @@
     size = block_refs[0].shape[0] - 8
     plane, line = lax.rem(where_ref[0], 4), lax.div(where_ref[0], 4)
     each = size // LANES
-    places = [ahead(order, line, steps) * 4 + (plane ^ bits) for bits, steps in names]
+    odd = lax.rem(where_ref[1], 2)
+    bits = (0, 1 + odd, 2 - odd, 3)
+    places = [ahead(order, line, steps) * 4 + (plane ^ bits[way]) for way, steps in names]
     copies = []
     for i in range(count):
         at = pl.multiple_of(places[i] * size, size)
@@ -318,8 +303,13 @@
     order = tuple(range(0, lines, 2)) + tuple(range(1, lines, 2))[::-1]
     where = jnp.stack([lax.axis_index("dp"), lax.axis_index("cent")]).astype(jnp.int32)
 
-    def flip(x, bits):
-        return lax.ppermute(x, "dp", [(i, i ^ bits) for i in range(n)])
+    def exchange(x, kind):
+        pairs = [
+            (i * cores + c, (i ^ (1 if (kind + c) % 2 == 0 else 2)) * cores + c)
+            for i in range(n)
+            for c in range(cores)
+        ]
+        return lax.ppermute(x, ("dp", "cent"), pairs)
 
     def flip_core(x, bits):
         return lax.ppermute(x, "cent", [(i, i ^ bits) for i in range(cores)])
@@ -339,20 +329,20 @@
         "open",
         scratch=[pltpu.VMEM((2 * half, width), points.dtype), pltpu.SemaphoreType.DMA(())],
     )
-    x0, y1 = flip(first, 1), flip(second, 2)
-    x1, y0 = flip(second, 1), flip(first, 2)
+    a0, b1 = exchange(first, 0), exchange(second, 1)
+    a1, b0 = exchange(second, 0), exchange(first, 1)
 
     pair, twice, norm = stats(where, points, centroids, lines)
     pairs = [pair] + [flip_core(pair, rc) for rc in range(1, cores)]
     tail = max(8, 2 * cores)
-    lse, log_evidence, pack_x, pack_y = call(
+    lse, log_evidence, pack_a, pack_b = call(
         functools.partial(lse_kernel, cores, local_cent * cores),
         (f32(2 * cores, half), f32(rows // LANES, LANES), f32(half + tail, width), f32(half + tail, width)),
         [VMEM] * (2 + cores),
-        (x0, y1, *pairs),
+        (a0, b1, *pairs),
         "lse",
     )
-    d0, d1 = flip(pack_x, 2), flip(pack_y, 1)
+    d0, d1 = exchange(pack_a, 1), exchange(pack_b, 0)
 
     lanes = min(LANES, half)
     acc, cnt = call(
@@ -363,10 +353,10 @@
         "own",
         flops=4 * share * width * rows,
     )
-    x0, y1, x1, y0, lse = lax.optimization_barrier((x0, y1, x1, y0, lse))
-    near = with_siblings((x0, y1, x1, y0))
+    a0, b1, a1, b0, lse = lax.optimization_barrier((a0, b1, a1, b0, lse))
+    near = with_siblings((a0, b1, a1, b0))
+    lse_d = exchange(d1[half : half + 2 * cores, :half], 1)
     near, d0, d1, acc, cnt = lax.optimization_barrier((near, d0, d1, acc, cnt))
-    lse_d = flip(d1[half : half + 2 * cores, :half], 2)
     lead = call(
         functools.partial(lead_kernel, cores, order, half),
         (f32(size, width), f32(size, lanes)),
@@ -376,80 +366,72 @@
         flops=4 * size * width * 2 * rows,
     )
     given = (where, twice, norm, acc, cnt, lse_d)
-    rows_given = (*near, *with_siblings((d0, d1)))
+    far = with_siblings((d0, d1))
+    rows_given = (*near, *far)
     block_sum = f32(size + 8, width)
     turn = lines // 2
     forward = list(range(turn - 1, 0, -1))
     backward = [lines - s for s in range(turn - 1, 0, -1)]
-    made = (forward + backward)[:2]
-    first, *made_sums = call(
-        functools.partial(first_kernel, cores, order, half, made),
-        [block_sum] * 3,
-        [SMEM] + [VMEM] * (7 + 6 * cores),
-        (*given, *lead, *rows_given),
+    first = call(
+        functools.partial(first_kernel, cores, order, half),
+        block_sum,
+        [SMEM] + [VMEM] * (5 + 2 * cores),
+        (where, twice, norm, lse_d, *lead, *far),
         "first",
         flops=4 * size * width * rows,
     )
-    made_sums = dict(zip(made, made_sums))
-
-    def sum_of(steps):
-        extra = [made_sums[steps]] if steps in made_sums else []
-        return call(
+
+    def sums_of(steps):
+        made = call(
             functools.partial(rest_kernel, cores, order, half, steps),
-            block_sum,
-            [SMEM] + [VMEM] * (5 + 6 * cores + len(extra)),
-            (*given, *rows_given, *extra),
+            [block_sum] * len(steps),
+            [SMEM] + [VMEM] * (5 + 6 * cores),
+            (*given, *rows_given),
             "rest",
-            flops=4 * size * width * 3 * rows,
+            flops=4 * size * width * 3 * rows * len(steps),
         )
+        return dict(zip(steps, made))
 
     def plus(a, b):
         return call(add_kernel, block_sum, [VMEM] * 2, (a, b), "add")
 
-    moving = ring(first, 1)
+    sums = {**sums_of(backward), **sums_of(forward + [0])}
+    from_ahead = ring(sums[backward[0]], -1)
+    for s in backward[1:]:
+        from_ahead = ring(plus(sums[s], from_ahead), -1)
+    from_behind = ring(first, 1)
     for s in forward:
-        moving = ring(plus(sum_of(s), moving), 1)
-    sides = [moving]
-    moving = None
-    for s in backward:
-        mine = sum_of(s)
-        mine, sides[0] = lax.optimization_barrier((mine, sides[0]))
-        moving = ring(mine if moving is None else plus(mine, moving), -1)
-    sides.append(moving)
+        from_behind = ring(plus(sums[s], from_behind), 1)
     done = call(
         finish_kernel,
         block_sum,
         [SMEM] + [VMEM] * 4,
-        (where, twice, sum_of(0), *sides),
+        (where, twice, sums[0], from_behind, from_ahead),
         "finish",
     )
 
+    steps = [-s for s in range(1, lines // 2 + 1)] + list(range(1, lines // 2))
     got = {(0, 0): done}
-    chains = {}
-
-    def send(chain, target, source, move, *how):
-        x = got[source]
-        if chain in chains:
-            x, chains[chain] = lax.optimization_barrier((x, got[chains[chain]]))[0], None
-        got[target] = move(x, *how)
-        chains[chain] = target
-
-    steps = [-s for s in range(1, lines // 2 + 1)] + list(range(1, lines // 2))
-    for s in steps:
-        send("z", (0, s), (0, s + 1 if s < 0 else s - 1), ring, 1 if s < 0 else -1)
-    send("x", (1, 0), (0, 0), flip, 1)
-    send("y", (2, 0), (0, 0), flip, 2)
-    send("y", (3, 0), (1, 0), flip, 2)
-    for s in steps:
-        send("x", (1, s), (0, s), flip, 1)
-        send("y", (2, s), (0, s), flip, 2)
-    for s in steps:
-        if abs(s) == 1:
-            send("z", (3, s), (3, 0), ring, -s)
-        else:
-            send("x", (3, s), (2, s), flip, 1)
-    late = [chains["x"], chains["y"], chains["z"]]
-    middle = [(2, -2), (1, 1), (3, -1), (1, -2), (2, -1)]
+    previous, older = (), ()
+    for s in [0] + steps:
+        x = got[0, s]
+        if previous:
+            x = lax.optimization_barrier((x, *previous))[0]
+        got[1, s], got[2, s] = exchange(x, 0), exchange(x, 1)
+        if s == steps[-1]:
+            break
+        got[3, s] = exchange(got[1, s], 1)
+        previous, older = (got[2, s], *older), (got[3, s],)
+        ahead_of = steps[([0] + steps).index(s)]
+        x = got[0, ahead_of + (1 if ahead_of < 0 else -1)]
+        if ahead_of > 0:
+            x = lax.optimization_barrier((x, got[0, s]))[0]
+        got[0, ahead_of] = ring(x, 1 if ahead_of < 0 else -1)
+    before = got[3, steps[-1] - 1] if steps[-1] > 0 else got[3, steps[-1] + 1]
+    before = lax.optimization_barrier((before, got[0, steps[-1]]))[0]
+    got[3, steps[-1]] = ring(before, -1 if steps[-1] > 0 else 1)
+    late = [(1, steps[-1]), (2, steps[-1]), (3, steps[-1])]
+    middle = [(w, steps[-2]) for w in (1, 2, 3)] + [(0, steps[-1])]
     groups = ([k for k in got if k not in middle + late], middle, late)
     new = counts = None
     for later, names in enumerate(groups):

time: 109 us -> 99 us (0.908)
  waiting for transfers between devices: 46.1 us -> 36.1 us
  Pallas kernels: 25.8 us -> 23.3 us
  starting transfers between devices: 33.3 us -> 35.7 us
    ppermute x8 -> x7, waiting for transfers between devices: 29.8 us -> 13 us  [ring(): lax.ppermute(x, 'dp', [(4 * a + i, 4 * b + i) for a, b in pairs for i in...]
    ppermute x17 -> x18, waiting for transfers between devices: 14.9 us -> 21.7 us  [exchange(): return lax.ppermute(x, ('dp', 'cent'), pairs)]
    ppermute x17 -> x18, starting transfers between devices: 14.2 us -> 19 us  [exchange(): return lax.ppermute(x, ('dp', 'cent'), pairs)]
    ppermute x8 -> x7, starting transfers between devices: 18 us -> 15.1 us  [ring(): lax.ppermute(x, 'dp', [(4 * a + i, 4 * b + i) for a, b in pairs for i in...]
    pallas_call x14 -> x13, Pallas kernels: 25.8 us -> 23.3 us  [call(): pl.pallas_call(kernel, out_shape=out_shape, in_specs=in_specs, out_specs=...]
    unnamed x10 -> x8, local copies, waits for them, and re-layouts: 2.65 us -> 2.64 us
  transfers between devices with their start and end apart: 32 -> 32, of which waited for: 20 -> 19; matrix products, arithmetic and copies ran while one was open for 0% -> 0% of each run, Pallas kernels for 19% -> 19%
where the time goes in v10:
time: 99 us; the launch traced here: 98.8 us
  waiting for transfers between devices  36.1 us (36%)
  starting transfers between devices  35.7 us (36%)
  Pallas kernels  23.3 us (24%)
  local copies, waits for them, and re-layouts  2.64 us (3%)
    pallas_call x13, Pallas kernels, call(): pl.pallas_call(kernel, out_shape=out_shape, in_specs=in_specs, out_specs=...  23.3 us
    ppermute x18, waiting for transfers between devices, exchange(): return lax.ppermute(x, ('dp', 'cent'), pairs)  21.7 us
    ppermute x18, starting transfers between devices, exchange(): return lax.ppermute(x, ('dp', 'cent'), pairs)  19 us
    ppermute x7, starting transfers between devices, ring(): lax.ppermute(x, 'dp', [(4 * a + i, 4 * b + i) for a, b in pairs for i in...  15.1 us
    ppermute x7, waiting for transfers between devices, ring(): lax.ppermute(x, 'dp', [(4 * a + i, 4 * b + i) for a, b in pairs for i in...  13 us
    unnamed x8, local copies, waits for them, and re-layouts  2.64 us
  transfers between devices with their start and end apart: 32, of which 19 were waited for; matrix products, arithmetic and copies ran while one was open for 0% of the time, Pallas kernels for 19%

profile of v10, /device:TPU:0, one launch (start us, length us, event | category | flops | bytes accessed | tf_op | source)
XLA Modules:
  0.0 98.8 jit_solution(6963785447788495349)
XLA Ops:
  0.7 1.0 %copy-done.1 = bf16[1024,256]{1,0:T(8,128)(2,1)S(1)} copy-done((bf16[1024,256]{1,0:T(8,128)(2,1)S(1)}, bf16[1024,256]{1,0:T(8,128)(2,1)}, u32[]{:S(2)}) %copy-start.1) | copy-done | bytes 524312
  1.8 0.6 open.1
  2.4 3.0 %collective-permute-start.1 = (f32[256,256]{1,0:T(8,128)S(1)}, f32[256,256]{1,0:T(8,128)S(1)}, u32[]{:S(2)}, u32[]{:S(2)}) collective-permute-start(f32[256,256]{1,0:T(8,128)S(1)} %get-tuple-element.48), channel_id=1, source_target_pairs={{0,4},{1,3},{2,6},{3,1},{4,0},{5,7},{6,2},{7,5},{8,12},{9,11},{10,... | collective-permute-start | bytes 786440 | tf_op jit(solution)/shard_map/ppermute | solution.py:312
  5.4 1.5 %collective-permute-start.2 = (f32[256,256]{1,0:T(8,128)S(1)}, f32[256,256]{1,0:T(8,128)S(1)}, u32[]{:S(2)}, u32[]{:S(2)}) collective-permute-start(f32[256,256]{1,0:T(8,128)S(1)} %get-tuple-element.48), channel_id=1, source_target_pairs={{0,2},{1,5},{2,0},{3,7},{4,6},{5,1},{6,4},{7,3},{8,10},{9,13},{10,... | collective-permute-start | bytes 786440 | tf_op jit(solution)/shard_map/ppermute | solution.py:312
  6.9 0.5 collective-permute-start
  7.5 1.6 %copy-done.3 = bf16[4096,256]{1,0:T(8,128)(2,1)S(1)} copy-done((bf16[4096,256]{1,0:T(8,128)(2,1)S(1)}, bf16[4096,256]{1,0:T(8,128)(2,1)}, u32[]{:S(2)}) %copy-start.3) | copy-done | bytes 2097176
  9.1 5.9 %stats.1 = (f32[2,1024]{1,0:T(2,128)S(1)}, bf16[1024,256]{1,0:T(8,128)(2,1)S(1)}, f32[1024,128]{1,0:T(8,128)S(1)}) custom-call(s32[2]{0:T(128)S(1)} %pad_add_fusion.where_ref, bf16[1024,256]{1,0:T(8,128)(2,1)S(1)} %copy-done.1, bf16[4096,256]{1,0:T(8,128)(2,1)S(1)} %copy-done.3), custom_call_target="tpu_custom_call" | custom-call | flops 4294967296 | bytes 2621448 | tf_op jit(solution)/shard_map/stats/pallas_call | solution.py:27
  15.1 1.2 %collective-permute-done.4.refs_1_ = f32[2,1024]{1,0:T(2,128)S(1)} collective-permute-done((f32[2,1024]{1,0:T(2,128)S(1)}, f32[2,1024]{1,0:T(2,128)S(1)}, u32[]{:S(2)}, u32[]{:S(2)}) %collective-permute-start.4) | collective-permute-done | bytes 8224 | tf_op jit(solution)/shard_map/ppermute | solution.py:315
  16.3 1.1 %collective-permute-done.a0_ref.refs_0_ = f32[256,256]{1,0:T(8,128)S(1)} collective-permute-done((f32[256,256]{1,0:T(8,128)S(1)}, f32[256,256]{1,0:T(8,128)S(1)}, u32[]{:S(2)}, u32[]{:S(2)}) %collective-permute-start) | collective-permute-done | bytes 262176 | tf_op jit(solution)/shard_map/ppermute | solution.py:312
  17.4 0.6 lse.1
  18.0 0.6 collective-permute-start.5
  18.6 1.1 %collective-permute-start.10 = (f32[264,256]{1,0:T(8,128)S(1)}, f32[264,256]{1,0:T(8,128)S(1)}, u32[]{:S(2)}, u32[]{:S(2)}) collective-permute-start(f32[264,256]{1,0:T(8,128)S(1)} %get-tuple-element.56), channel_id=1, source_target_pairs={{0,2},{1,5},{2,0},{3,7},{4,6},{5,1},{6,4},{7,3},{8,10},{9,13},{10,... | collective-permute-start | bytes 811016 | tf_op jit(solution)/shard_map/ppermute | solution.py:312
  19.8 1.5 %collective-permute-start.9 = (f32[264,256]{1,0:T(8,128)S(1)}, f32[264,256]{1,0:T(8,128)S(1)}, u32[]{:S(2)}, u32[]{:S(2)}) collective-permute-start(f32[264,256]{1,0:T(8,128)S(1)} %get-tuple-element.55), channel_id=1, source_target_pairs={{0,4},{1,3},{2,6},{3,1},{4,0},{5,7},{6,2},{7,5},{8,12},{9,11},{10,... | collective-permute-start | bytes 811016 | tf_op jit(solution)/shard_map/ppermute | solution.py:312
  21.8 1.6 %own.1 = (f32[1024,256]{1,0:T(8,128)S(1)}, f32[1024,128]{1,0:T(8,128)S(1)}) custom-call(bf16[1024,256]{1,0:T(8,128)(2,1)S(1)} %copy-done.2, bf16[1024,256]{1,0:T(8,128)(2,1)S(1)} %get-tuple-element.45.twice_ref, f32[1024,128]{1,0:T(8,128)S(1)} %get-tuple-element.46.norm_ref, f32[4,256]{1,0:T(4,128)S(1)} %get-tuple-element.50.lse_ref), custom_call_target="tpu_custom_call" | custom-call | flops 1073741824 | bytes 1576960 | tf_op jit(solution)/shard_map/own/pallas_call | solution.py:27
  23.6 3.4 %collective-permute-done.10.refs_10_.refs_9_.refs_2_ = f32[264,256]{1,0:T(8,128)S(1)} collective-permute-done((f32[264,256]{1,0:T(8,128)S(1)}, f32[264,256]{1,0:T(8,128)S(1)}, u32[]{:S(2)}, u32[]{:S(2)}) %collective-permute-start.10) | collective-permute-done | bytes 270368 | tf_op jit(solution)/shard_map/ppermute | solution.py:312
  26.9 0.7 collective-permute-done.9.refs_8_.refs_0_
  28.1 1.8 %collective-permute-start.11 = (f32[4,256]{1,0:T(4,128)S(1)}, f32[4,256]{1,0:T(4,128)S(1)}, u32[]{:S(2)}, u32[]{:S(2)}) collective-permute-start(f32[4,256]{1,0:T(4,128)S(1)} %slice.4), channel_id=1, source_target_pairs={{0,4},{1,3},{2,6},{3,1},{4,0},{5,7},{6,2},{7,5},{8,12},{9,11},{10,... | collective-permute-start | bytes 12296 | tf_op jit(solution)/shard_map/ppermute | solution.py:312
  29.9 1.5 %lead.1 = (f32[256,256]{1,0:T(8,128)S(1)}, f32[256,128]{1,0:T(8,128)S(1)}) custom-call(s32[2]{0:T(128)S(1)} %pad_add_fusion.where_ref, bf16[1024,256]{1,0:T(8,128)(2,1)S(1)} %get-tuple-element.45.twice_ref, f32[1024,128]{1,0:T(8,128)S(1)} %get-tuple-element.46.norm_ref, f32[1024,256]{1,0:T(8,128)S(1)} %get-tuple-element.59.acc_ref, ...), custom_call_target="tpu_custom_call" | custom-call | flops 536870912 | bytes 5259272 | tf_op jit(solution)/shard_map/lead/pallas_call | solution.py:27
  31.7 1.2 %first.1 = f32[264,256]{1,0:T(8,128)S(1)} custom-call(s32[2]{0:T(128)S(1)} %pad_add_fusion.where_ref, bf16[1024,256]{1,0:T(8,128)(2,1)S(1)} %get-tuple-element.45.twice_ref, f32[1024,128]{1,0:T(8,128)S(1)} %get-tuple-element.46.norm_ref, f32[4,256]{1,0:T(4,128)S(1)} %collective-permute-done.11.lse_ref, f32[256,256]{1,0:T(8,128)S(1)} %get-tuple-element.73.lead_acc_ref, ...), custom_call_target="tpu_custom_call" | custom-call | flops 268435456 | bytes 2527240 | tf_op jit(solution)/shard_map/first/pallas_call | solution.py:27
  32.9 3.4 %collective-permute-start.14 = (f32[264,256]{1,0:T(8,128)S(1)}, f32[264,256]{1,0:T(8,128)S(1)}, u32[]{:S(2)}, u32[]{:S(2)}) collective-permute-start(f32[264,256]{1,0:T(8,128)S(1)} %first.1), channel_id=1, source_target_pairs={{0,16},{2,18},{4,20},{6,22},{16,24},{18,26},{20,28},{22,30},{24,8}... | collective-permute-start | bytes 811016 | tf_op jit(solution)/shard_map/ppermute | solution.py:319
  36.4 1.9 %rest.3 = f32[264,256]{1,0:T(8,128)S(1)} custom-call(s32[2]{0:T(128)S(1)} %pad_add_fusion.where_ref, bf16[1024,256]{1,0:T(8,128)(2,1)S(1)} %get-tuple-element.45.twice_ref, f32[1024,128]{1,0:T(8,128)S(1)} %get-tuple-element.46.norm_ref, f32[1024,256]{1,0:T(8,128)S(1)} %get-tuple-element.59.acc_ref, f32[1024,128]{1,0:T(8,128)S(1)} %get-tuple-element.60.cnt_ref, ...), custom_call_target="tpu_custom_call" | custom-call | flops 805306368 | bytes 5804040 | tf_op jit(solution)/shard_map/rest/pallas_call | solution.py:27
  38.5 3.5 %rest.2 = (f32[264,256]{1,0:T(8,128)S(1)}, f32[264,256]{1,0:T(8,128)S(1)}) custom-call(s32[2]{0:T(128)S(1)} %pad_add_fusion.where_ref, bf16[1024,256]{1,0:T(8,128)(2,1)S(1)} %get-tuple-element.45.twice_ref, f32[1024,128]{1,0:T(8,128)S(1)} %get-tuple-element.46.norm_ref, f32[1024,256]{1,0:T(8,128)} %copy-done, f32[1024,128]{1,0:T(8,128)S(1)} %get-tuple-element.60.cnt_ref, ...), custom_call_target="tpu_custom_call" | custom-call | flops 1610612736 | bytes 5804040 | tf_op jit(solution)/shard_map/rest/pallas_call | solution.py:27
  42.0 1.3 %collective-permute-done.14.b_ref = f32[264,256]{1,0:T(8,128)S(1)} collective-permute-done((f32[264,256]{1,0:T(8,128)S(1)}, f32[264,256]{1,0:T(8,128)S(1)}, u32[]{:S(2)}, u32[]{:S(2)}) %collective-permute-start.14) | collective-permute-done | bytes 270368 | tf_op jit(solution)/shard_map/ppermute | solution.py:319
  43.3 3.4 %collective-permute-start.15 = (f32[264,256]{1,0:T(8,128)S(1)}, f32[264,256]{1,0:T(8,128)S(1)}, u32[]{:S(2)}, u32[]{:S(2)}) collective-permute-start(f32[264,256]{1,0:T(8,128)S(1)} %add.3), channel_id=1, source_target_pairs={{0,16},{2,18},{4,20},{6,22},{16,24},{18,26},{20,28},{22,30},{24,8}... | collective-permute-start | bytes 811016 | tf_op jit(solution)/shard_map/ppermute | solution.py:319
  46.8 4.2 %collective-permute-done.16.second_ref = f32[264,256]{1,0:T(8,128)S(1)} collective-permute-done((f32[264,256]{1,0:T(8,128)S(1)}, f32[264,256]{1,0:T(8,128)S(1)}, u32[]{:S(2)}, u32[]{:S(2)}) %collective-permute-start.16) | collective-permute-done | bytes 270368 | tf_op jit(solution)/shard_map/ppermute | solution.py:319
  50.9 2.9 %collective-permute-done.15.first_ref = f32[264,256]{1,0:T(8,128)S(1)} collective-permute-done((f32[264,256]{1,0:T(8,128)S(1)}, f32[264,256]{1,0:T(8,128)S(1)}, u32[]{:S(2)}, u32[]{:S(2)}) %collective-permute-start.15) | collective-permute-done | bytes 270368 | tf_op jit(solution)/shard_map/ppermute | solution.py:319
  53.8 0.8 finish.1.refs_0_
  54.6 2.5 %collective-permute-start.17 = (f32[264,256]{1,0:T(8,128)S(1)}, f32[264,256]{1,0:T(8,128)S(1)}, u32[]{:S(2)}, u32[]{:S(2)}) collective-permute-start(f32[264,256]{1,0:T(8,128)S(1)} %finish.1.refs_0_), channel_id=1, source_target_pairs={{0,16},{2,18},{4,20},{6,22},{16,24},{18,26},{20,28},{22,30},{24,8}... | collective-permute-start | bytes 811016 | tf_op jit(solution)/shard_map/ppermute | solution.py:319
  57.2 1.0 %collective-permute-start.20 = (f32[264,256]{1,0:T(8,128)S(1)}, f32[264,256]{1,0:T(8,128)S(1)}, u32[]{:S(2)}, u32[]{:S(2)}) collective-permute-start(f32[264,256]{1,0:T(8,128)S(1)} %finish.1.refs_0_), channel_id=1, source_target_pairs={{0,4},{1,3},{2,6},{3,1},{4,0},{5,7},{6,2},{7,5},{8,12},{9,11},{10,... | collective-permute-start | bytes 811016 | tf_op jit(solution)/shard_map/ppermute | solution.py:312
  58.2 0.8 collective-permute-start.22
  59.0 3.0 %collective-permute-done.17.refs_4_ = f32[264,256]{1,0:T(8,128)S(1)} collective-permute-done((f32[264,256]{1,0:T(8,128)S(1)}, f32[264,256]{1,0:T(8,128)S(1)}, u32[]{:S(2)}, u32[]{:S(2)}) %collective-permute-start.17) | collective-permute-done | bytes 270368 | tf_op jit(solution)/shard_map/ppermute | solution.py:319
  62.1 2.5 %collective-permute-start.18 = (f32[264,256]{1,0:T(8,128)S(1)}, f32[264,256]{1,0:T(8,128)S(1)}, u32[]{:S(2)}, u32[]{:S(2)}) collective-permute-start(f32[264,256]{1,0:T(8,128)S(1)} %collective-permute-done.17.refs_4_), channel_id=1, source_target_pairs={{0,16},{2,18},{4,20},{6,22},{16,24},{18,26},{20,28},{22,30},{24,8}... | collective-permute-start | bytes 811016 | tf_op jit(solution)/shard_map/ppermute | solution.py:319
  64.6 1.0 collective-permute-start.21
  65.6 1.1 %collective-permute-start.23 = (f32[264,256]{1,0:T(8,128)S(1)}, f32[264,256]{1,0:T(8,128)S(1)}, u32[]{:S(2)}, u32[]{:S(2)}) collective-permute-start(f32[264,256]{1,0:T(8,128)S(1)} %collective-permute-done.22.refs_1_), channel_id=1, source_target_pairs={{0,4},{1,3},{2,6},{3,1},{4,0},{5,7},{6,2},{7,5},{8,12},{9,11},{10,... | collective-permute-start | bytes 811016 | tf_op jit(solution)/shard_map/ppermute | solution.py:312
  66.6 1.5 %collective-permute-start.25 = (f32[264,256]{1,0:T(8,128)S(1)}, f32[264,256]{1,0:T(8,128)S(1)}, u32[]{:S(2)}, u32[]{:S(2)}) collective-permute-start(f32[264,256]{1,0:T(8,128)S(1)} %collective-permute-done.17.refs_4_), channel_id=1, source_target_pairs={{0,2},{1,5},{2,0},{3,7},{4,6},{5,1},{6,4},{7,3},{8,10},{9,13},{10,... | collective-permute-start | bytes 811016 | tf_op jit(solution)/shard_map/ppermute | solution.py:312
  68.1 1.7 %collective-permute-done.18.refs_8_ = f32[264,256]{1,0:T(8,128)S(1)} collective-permute-done((f32[264,256]{1,0:T(8,128)S(1)}, f32[264,256]{1,0:T(8,128)S(1)}, u32[]{:S(2)}, u32[]{:S(2)}) %collective-permute-start.18) | collective-permute-done | bytes 270368 | tf_op jit(solution)/shard_map/ppermute | solution.py:319
  69.7 1.9 %collective-permute-start.19 = (f32[264,256]{1,0:T(8,128)S(1)}, f32[264,256]{1,0:T(8,128)S(1)}, u32[]{:S(2)}, u32[]{:S(2)}) collective-permute-start(f32[264,256]{1,0:T(8,128)S(1)} %finish.1.refs_0_), channel_id=1, source_target_pairs={{0,8},{2,10},{4,12},{6,14},{16,0},{18,2},{20,4},{22,6},{24,16},{26... | collective-permute-start | bytes 811016 | tf_op jit(solution)/shard_map/ppermute | solution.py:319
  71.8 4.1 %collective-permute-done.23.refs_3_ = f32[264,256]{1,0:T(8,128)S(1)} collective-permute-done((f32[264,256]{1,0:T(8,128)S(1)}, f32[264,256]{1,0:T(8,128)S(1)}, u32[]{:S(2)}, u32[]{:S(2)}) %collective-permute-start.23) | collective-permute-done | bytes 270368 | tf_op jit(solution)/shard_map/ppermute | solution.py:312
  75.9 1.7 %collective-permute-start.30 = (f32[264,256]{1,0:T(8,128)S(1)}, f32[264,256]{1,0:T(8,128)S(1)}, u32[]{:S(2)}, u32[]{:S(2)}) collective-permute-start(f32[264,256]{1,0:T(8,128)S(1)} %collective-permute-done.18.refs_8_), channel_id=1, source_target_pairs={{0,2},{1,5},{2,0},{3,7},{4,6},{5,1},{6,4},{7,3},{8,10},{9,13},{10,... | collective-permute-start | bytes 811016 | tf_op jit(solution)/shard_map/ppermute | solution.py:312
  77.9 1.7 %collective-permute-start.24 = (f32[264,256]{1,0:T(8,128)S(1)}, f32[264,256]{1,0:T(8,128)S(1)}, u32[]{:S(2)}, u32[]{:S(2)}) collective-permute-start(f32[264,256]{1,0:T(8,128)S(1)} %collective-permute-done.18.refs_8_), channel_id=1, source_target_pairs={{0,4},{1,3},{2,6},{3,1},{4,0},{5,7},{6,2},{7,5},{8,12},{9,11},{10,... | collective-permute-start | bytes 811016 | tf_op jit(solution)/shard_map/ppermute | solution.py:312
  79.7 1.1 %collective-permute-start.29 = (f32[264,256]{1,0:T(8,128)S(1)}, f32[264,256]{1,0:T(8,128)S(1)}, u32[]{:S(2)}, u32[]{:S(2)}) collective-permute-start(f32[264,256]{1,0:T(8,128)S(1)} %collective-permute-done.23.refs_3_), channel_id=1, source_target_pairs={{0,8},{2,10},{4,12},{6,14},{16,0},{18,2},{20,4},{22,6},{24,16},{26... | collective-permute-start | bytes 811016 | tf_op jit(solution)/shard_map/ppermute | solution.py:319
  80.8 4.5 %collective-permute-done.30.refs_0_ = f32[264,256]{1,0:T(8,128)S(1)} collective-permute-done((f32[264,256]{1,0:T(8,128)S(1)}, f32[264,256]{1,0:T(8,128)S(1)}, u32[]{:S(2)}, u32[]{:S(2)}) %collective-permute-start.30) | collective-permute-done | bytes 270368 | tf_op jit(solution)/shard_map/ppermute | solution.py:312
  85.3 4.6 %collective-permute-done.24.refs_1_ = f32[264,256]{1,0:T(8,128)S(1)} collective-permute-done((f32[264,256]{1,0:T(8,128)S(1)}, f32[264,256]{1,0:T(8,128)S(1)}, u32[]{:S(2)}, u32[]{:S(2)}) %collective-permute-start.24) | collective-permute-done | bytes 270368 | tf_op jit(solution)/shard_map/ppermute | solution.py:312
  90.1 2.0 %place_early.1 = (f32[4096,256]{1,0:T(8,128)}, f32[32,128]{1,0:T(8,128)S(1)}) custom-call(s32[2]{0:T(128)S(1)} %pad_add_fusion.where_ref, f32[264,256]{1,0:T(8,128)S(1)} %finish.1.refs_0_, f32[264,256]{1,0:T(8,128)S(1)} %collective-permute-done.22.refs_1_, f32[264,256]{1,0:T(8,128)S(1)} %collective-permute-done.20.refs_2_, ...), custom_call_target="tpu_custom_call" | custom-call | bytes 2433032 | tf_op jit(solution)/shard_map/place_early/pallas_call | solution.py:27
  92.2 0.6 collective-permute-done.31.refs_2_
  92.8 1.5 %place_middle.1 = (f32[4096,256]{1,0:T(8,128)}, f32[32,128]{1,0:T(8,128)S(1)}) custom-call(s32[2]{0:T(128)S(1)} %pad_add_fusion.where_ref, f32[264,256]{1,0:T(8,128)S(1)} %collective-permute-done.30.refs_0_, f32[264,256]{1,0:T(8,128)S(1)} %collective-permute-done.24.refs_1_, ...), custom_call_target="tpu_custom_call", output_to_operand_aliasing={{0}: (6, {})} | custom-call | bytes 5292040 | tf_op jit(solution)/shard_map/place_middle/pallas_call | solution.py:27
  94.4 2.0 %collective-permute-done.27.refs_0_ = f32[264,256]{1,0:T(8,128)S(1)} collective-permute-done((f32[264,256]{1,0:T(8,128)S(1)}, f32[264,256]{1,0:T(8,128)S(1)}, u32[]{:S(2)}, u32[]{:S(2)}) %collective-permute-start.27) | collective-permute-done | bytes 270368 | tf_op jit(solution)/shard_map/ppermute | solution.py:312
  96.6 2.1 %place_late.1 = (f32[4096,256]{1,0:T(8,128)}, f32[32,128]{1,0:T(8,128)}) custom-call(s32[2]{0:T(128)S(1)} %pad_add_fusion.where_ref, f32[264,256]{1,0:T(8,128)S(1)} %collective-permute-done.27.refs_0_, f32[264,256]{1,0:T(8,128)S(1)} %collective-permute-done.28.refs_1_, ...), custom_call_target="tpu_custom_call", output_to_operand_aliasing={{0}: (5, {})} | custom-call | bytes 5021704 | tf_op jit(solution)/shard_map/place_late/pallas_call | solution.py:27
  (39 shorter events, 2.9 us)
Async XLA Ops:
  0.7 1.0 %copy-start.1 = (bf16[1024,256]{1,0:T(8,128)(2,1)S(1)}, bf16[1024,256]{1,0:T(8,128)(2,1)}, u32[]{:S(2)}) copy-start(bf16[1024,256]{1,0:T(8,128)(2,1)} %points_ref.5) | copy-start | bytes 1572868
  2.4 15.0 %collective-permute-start.1 = (f32[256,256]{1,0:T(8,128)S(1)}, f32[256,256]{1,0:T(8,128)S(1)}, u32[]{:S(2)}, u32[]{:S(2)}) collective-permute-start(f32[256,256]{1,0:T(8,128)S(1)} %get-tuple-element.48), channel_id=1, source_target_pairs={{0,4},{1,3},{2,6},{3,1},{4,0},{5,7},{6,2},{7,5},{8,12},{9,11},{10,... | collective-permute-start | bytes 786440 | tf_op jit(solution)/shard_map/ppermute | solution.py:312
  5.4 12.6 %collective-permute-start.2 = (f32[256,256]{1,0:T(8,128)S(1)}, f32[256,256]{1,0:T(8,128)S(1)}, u32[]{:S(2)}, u32[]{:S(2)}) collective-permute-start(f32[256,256]{1,0:T(8,128)S(1)} %get-tuple-element.48), channel_id=1, source_target_pairs={{0,2},{1,5},{2,0},{3,7},{4,6},{5,1},{6,4},{7,3},{8,10},{9,13},{10,... | collective-permute-start | bytes 786440 | tf_op jit(solution)/shard_map/ppermute | solution.py:312
  6.9 14.9 %copy-start.2 = (bf16[1024,256]{1,0:T(8,128)(2,1)S(1)}, bf16[1024,256]{1,0:T(8,128)(2,1)}, u32[]{:S(2)}) copy-start(bf16[1024,256]{1,0:T(8,128)(2,1)} %points_ref.5) | copy-start | bytes 1572868
  6.9 10.5 %collective-permute-start = (f32[256,256]{1,0:T(8,128)S(1)}, f32[256,256]{1,0:T(8,128)S(1)}, u32[]{:S(2)}, u32[]{:S(2)}) collective-permute-start(f32[256,256]{1,0:T(8,128)S(1)} %get-tuple-element.47), channel_id=1, source_target_pairs={{0,2},{1,5},{2,0},{3,7},{4,6},{5,1},{6,4},{7,3},{8,10},{9,13},{10,... | collective-permute-start | bytes 786440 | tf_op jit(solution)/shard_map/ppermute | solution.py:312
  7.4 10.6 %collective-permute-start.3 = (f32[256,256]{1,0:T(8,128)S(1)}, f32[256,256]{1,0:T(8,128)S(1)}, u32[]{:S(2)}, u32[]{:S(2)}) collective-permute-start(f32[256,256]{1,0:T(8,128)S(1)} %get-tuple-element.47), channel_id=1, source_target_pairs={{0,4},{1,3},{2,6},{3,1},{4,0},{5,7},{6,2},{7,5},{8,12},{9,11},{10,... | collective-permute-start | bytes 786440 | tf_op jit(solution)/shard_map/ppermute | solution.py:312
  7.5 1.6 %copy-start.3 = (bf16[4096,256]{1,0:T(8,128)(2,1)S(1)}, bf16[4096,256]{1,0:T(8,128)(2,1)}, u32[]{:S(2)}) copy-start(bf16[4096,256]{1,0:T(8,128)(2,1)} %c_ref.1) | copy-start | bytes 6291460
  15.0 1.2 %collective-permute-start.4 = (f32[2,1024]{1,0:T(2,128)S(1)}, f32[2,1024]{1,0:T(2,128)S(1)}, u32[]{:S(2)}, u32[]{:S(2)}) collective-permute-start(f32[2,1024]{1,0:T(2,128)S(1)} %get-tuple-element.49.refs_0_), channel_id=1, source_target_pairs={{0,1},{1,0},{2,3},{3,2},{4,5},{5,4},{6,7},{7,6},{8,9},{9,8},{10,11... | collective-permute-start | bytes 24584 | tf_op jit(solution)/shard_map/ppermute | solution.py:315
  18.0 3.8 %collective-permute-start.5 = (f32[256,256]{1,0:T(8,128)S(1)}, f32[256,256]{1,0:T(8,128)S(1)}, u32[]{:S(2)}, u32[]{:S(2)}) collective-permute-start(f32[256,256]{1,0:T(8,128)S(1)} %collective-permute-done.a0_ref.refs_0_), channel_id=1, source_target_pairs={{0,1},{1,0},{2,3},{3,2},{4,5},{5,4},{6,7},{7,6},{8,9},{9,8},{10,11... | collective-permute-start | bytes 786440 | tf_op jit(solution)/shard_map/ppermute | solution.py:315
  18.6 8.3 %collective-permute-start.10 = (f32[264,256]{1,0:T(8,128)S(1)}, f32[264,256]{1,0:T(8,128)S(1)}, u32[]{:S(2)}, u32[]{:S(2)}) collective-permute-start(f32[264,256]{1,0:T(8,128)S(1)} %get-tuple-element.56), channel_id=1, source_target_pairs={{0,2},{1,5},{2,0},{3,7},{4,6},{5,1},{6,4},{7,3},{8,10},{9,13},{10,... | collective-permute-start | bytes 811016 | tf_op jit(solution)/shard_map/ppermute | solution.py:312
  19.8 7.8 %collective-permute-start.9 = (f32[264,256]{1,0:T(8,128)S(1)}, f32[264,256]{1,0:T(8,128)S(1)}, u32[]{:S(2)}, u32[]{:S(2)}) collective-permute-start(f32[264,256]{1,0:T(8,128)S(1)} %get-tuple-element.55), channel_id=1, source_target_pairs={{0,4},{1,3},{2,6},{3,1},{4,0},{5,7},{6,2},{7,5},{8,12},{9,11},{10,... | collective-permute-start | bytes 811016 | tf_op jit(solution)/shard_map/ppermute | solution.py:312
  21.3 2.1 %collective-permute-start.6 = (f32[256,256]{1,0:T(8,128)S(1)}, f32[256,256]{1,0:T(8,128)S(1)}, u32[]{:S(2)}, u32[]{:S(2)}) collective-permute-start(f32[256,256]{1,0:T(8,128)S(1)} %collective-permute-done.1.b1_ref.refs_2_), channel_id=1, source_target_pairs={{0,1},{1,0},{2,3},{3,2},{4,5},{5,4},{6,7},{7,6},{8,9},{9,8},{10,11... | collective-permute-start | bytes 786440 | tf_op jit(solution)/shard_map/ppermute | solution.py:315
  21.3 2.1 %collective-permute-start.7 = (f32[256,256]{1,0:T(8,128)S(1)}, f32[256,256]{1,0:T(8,128)S(1)}, u32[]{:S(2)}, u32[]{:S(2)}) collective-permute-start(f32[256,256]{1,0:T(8,128)S(1)} %collective-permute-done.2.refs_4_), channel_id=1, source_target_pairs={{0,1},{1,0},{2,3},{3,2},{4,5},{5,4},{6,7},{7,6},{8,9},{9,8},{10,11... | collective-permute-start | bytes 786440 | tf_op jit(solution)/shard_map/ppermute | solution.py:315
  21.8 1.8 %collective-permute-start.8 = (f32[256,256]{1,0:T(8,128)S(1)}, f32[256,256]{1,0:T(8,128)S(1)}, u32[]{:S(2)}, u32[]{:S(2)}) collective-permute-start(f32[256,256]{1,0:T(8,128)S(1)} %collective-permute-done.3.refs_6_), channel_id=1, source_target_pairs={{0,1},{1,0},{2,3},{3,2},{4,5},{5,4},{6,7},{7,6},{8,9},{9,8},{10,11... | collective-permute-start | bytes 786440 | tf_op jit(solution)/shard_map/ppermute | solution.py:315
  23.4 14.9 %copy-start = (f32[1024,256]{1,0:T(8,128)}, f32[1024,256]{1,0:T(8,128)S(1)}, u32[]{:S(2)}) copy-start(f32[1024,256]{1,0:T(8,128)S(1)} %get-tuple-element.59.acc_ref) | copy-start | bytes 3145732
  27.6 4.1 %collective-permute-start.12 = (f32[264,256]{1,0:T(8,128)S(1)}, f32[264,256]{1,0:T(8,128)S(1)}, u32[]{:S(2)}, u32[]{:S(2)}) collective-permute-start(f32[264,256]{1,0:T(8,128)S(1)} %collective-permute-done.9.refs_8_.refs_0_), channel_id=1, source_target_pairs={{0,1},{1,0},{2,3},{3,2},{4,5},{5,4},{6,7},{7,6},{8,9},{9,8},{10,11... | collective-permute-start | bytes 811016 | tf_op jit(solution)/shard_map/ppermute | solution.py:315
  27.8 3.9 %collective-permute-start.13 = (f32[264,256]{1,0:T(8,128)S(1)}, f32[264,256]{1,0:T(8,128)S(1)}, u32[]{:S(2)}, u32[]{:S(2)}) collective-permute-start(f32[264,256]{1,0:T(8,128)S(1)} %collective-permute-done.10.refs_10_.refs_9_.refs_2_), channel_id=1, source_target_pairs={{0,1},{1,0},{2,3},{3,2},{4,5},{5,4},{6,7},{7,6},{8,9},{9,8},{10,11... | collective-permute-start | bytes 811016 | tf_op jit(solution)/shard_map/ppermute | solution.py:315
  28.1 3.6 %collective-permute-start.11 = (f32[4,256]{1,0:T(4,128)S(1)}, f32[4,256]{1,0:T(4,128)S(1)}, u32[]{:S(2)}, u32[]{:S(2)}) collective-permute-start(f32[4,256]{1,0:T(4,128)S(1)} %slice.4), channel_id=1, source_target_pairs={{0,4},{1,3},{2,6},{3,1},{4,0},{5,7},{6,2},{7,5},{8,12},{9,11},{10,... | collective-permute-start | bytes 12296 | tf_op jit(solution)/shard_map/ppermute | solution.py:312
  32.9 10.4 %collective-permute-start.14 = (f32[264,256]{1,0:T(8,128)S(1)}, f32[264,256]{1,0:T(8,128)S(1)}, u32[]{:S(2)}, u32[]{:S(2)}) collective-permute-start(f32[264,256]{1,0:T(8,128)S(1)} %first.1), channel_id=1, source_target_pairs={{0,16},{2,18},{4,20},{6,22},{16,24},{18,26},{20,28},{22,30},{24,8}... | collective-permute-start | bytes 811016 | tf_op jit(solution)/shard_map/ppermute | solution.py:319
  38.2 12.7 %collective-permute-start.16 = (f32[264,256]{1,0:T(8,128)S(1)}, f32[264,256]{1,0:T(8,128)S(1)}, u32[]{:S(2)}, u32[]{:S(2)}) collective-permute-start(f32[264,256]{1,0:T(8,128)S(1)} %rest.3), channel_id=1, source_target_pairs={{0,8},{2,10},{4,12},{6,14},{16,0},{18,2},{20,4},{22,6},{24,16},{26... | collective-permute-start | bytes 811016 | tf_op jit(solution)/shard_map/ppermute | solution.py:319
  43.3 10.5 %collective-permute-start.15 = (f32[264,256]{1,0:T(8,128)S(1)}, f32[264,256]{1,0:T(8,128)S(1)}, u32[]{:S(2)}, u32[]{:S(2)}) collective-permute-start(f32[264,256]{1,0:T(8,128)S(1)} %add.3), channel_id=1, source_target_pairs={{0,16},{2,18},{4,20},{6,22},{16,24},{18,26},{20,28},{22,30},{24,8}... | collective-permute-start | bytes 811016 | tf_op jit(solution)/shard_map/ppermute | solution.py:319
  54.6 7.4 %collective-permute-start.17 = (f32[264,256]{1,0:T(8,128)S(1)}, f32[264,256]{1,0:T(8,128)S(1)}, u32[]{:S(2)}, u32[]{:S(2)}) collective-permute-start(f32[264,256]{1,0:T(8,128)S(1)} %finish.1.refs_0_), channel_id=1, source_target_pairs={{0,16},{2,18},{4,20},{6,22},{16,24},{18,26},{20,28},{22,30},{24,8}... | collective-permute-start | bytes 811016 | tf_op jit(solution)/shard_map/ppermute | solution.py:319
  57.2 7.4 %collective-permute-start.20 = (f32[264,256]{1,0:T(8,128)S(1)}, f32[264,256]{1,0:T(8,128)S(1)}, u32[]{:S(2)}, u32[]{:S(2)}) collective-permute-start(f32[264,256]{1,0:T(8,128)S(1)} %finish.1.refs_0_), channel_id=1, source_target_pairs={{0,4},{1,3},{2,6},{3,1},{4,0},{5,7},{6,2},{7,5},{8,12},{9,11},{10,... | collective-permute-start | bytes 811016 | tf_op jit(solution)/shard_map/ppermute | solution.py:312
  58.2 7.4 %collective-permute-start.22 = (f32[264,256]{1,0:T(8,128)S(1)}, f32[264,256]{1,0:T(8,128)S(1)}, u32[]{:S(2)}, u32[]{:S(2)}) collective-permute-start(f32[264,256]{1,0:T(8,128)S(1)} %finish.1.refs_0_), channel_id=1, source_target_pairs={{0,2},{1,5},{2,0},{3,7},{4,6},{5,1},{6,4},{7,3},{8,10},{9,13},{10,... | collective-permute-start | bytes 811016 | tf_op jit(solution)/shard_map/ppermute | solution.py:312
  62.1 7.7 %collective-permute-start.18 = (f32[264,256]{1,0:T(8,128)S(1)}, f32[264,256]{1,0:T(8,128)S(1)}, u32[]{:S(2)}, u32[]{:S(2)}) collective-permute-start(f32[264,256]{1,0:T(8,128)S(1)} %collective-permute-done.17.refs_4_), channel_id=1, source_target_pairs={{0,16},{2,18},{4,20},{6,22},{16,24},{18,26},{20,28},{22,30},{24,8}... | collective-permute-start | bytes 811016 | tf_op jit(solution)/shard_map/ppermute | solution.py:319
  64.6 7.2 %collective-permute-start.21 = (f32[264,256]{1,0:T(8,128)S(1)}, f32[264,256]{1,0:T(8,128)S(1)}, u32[]{:S(2)}, u32[]{:S(2)}) collective-permute-start(f32[264,256]{1,0:T(8,128)S(1)} %collective-permute-done.17.refs_4_), channel_id=1, source_target_pairs={{0,4},{1,3},{2,6},{3,1},{4,0},{5,7},{6,2},{7,5},{8,12},{9,11},{10,... | collective-permute-start | bytes 811016 | tf_op jit(solution)/shard_map/ppermute | solution.py:312
  65.6 10.4 %collective-permute-start.23 = (f32[264,256]{1,0:T(8,128)S(1)}, f32[264,256]{1,0:T(8,128)S(1)}, u32[]{:S(2)}, u32[]{:S(2)}) collective-permute-start(f32[264,256]{1,0:T(8,128)S(1)} %collective-permute-done.22.refs_1_), channel_id=1, source_target_pairs={{0,4},{1,3},{2,6},{3,1},{4,0},{5,7},{6,2},{7,5},{8,12},{9,11},{10,... | collective-permute-start | bytes 811016 | tf_op jit(solution)/shard_map/ppermute | solution.py:312
  66.6 11.0 %collective-permute-start.25 = (f32[264,256]{1,0:T(8,128)S(1)}, f32[264,256]{1,0:T(8,128)S(1)}, u32[]{:S(2)}, u32[]{:S(2)}) collective-permute-start(f32[264,256]{1,0:T(8,128)S(1)} %collective-permute-done.17.refs_4_), channel_id=1, source_target_pairs={{0,2},{1,5},{2,0},{3,7},{4,6},{5,1},{6,4},{7,3},{8,10},{9,13},{10,... | collective-permute-start | bytes 811016 | tf_op jit(solution)/shard_map/ppermute | solution.py:312
  69.7 10.0 %collective-permute-start.19 = (f32[264,256]{1,0:T(8,128)S(1)}, f32[264,256]{1,0:T(8,128)S(1)}, u32[]{:S(2)}, u32[]{:S(2)}) collective-permute-start(f32[264,256]{1,0:T(8,128)S(1)} %finish.1.refs_0_), channel_id=1, source_target_pairs={{0,8},{2,10},{4,12},{6,14},{16,0},{18,2},{20,4},{22,6},{24,16},{26... | collective-permute-start | bytes 811016 | tf_op jit(solution)/shard_map/ppermute | solution.py:319
  75.9 9.4 %collective-permute-start.30 = (f32[264,256]{1,0:T(8,128)S(1)}, f32[264,256]{1,0:T(8,128)S(1)}, u32[]{:S(2)}, u32[]{:S(2)}) collective-permute-start(f32[264,256]{1,0:T(8,128)S(1)} %collective-permute-done.18.refs_8_), channel_id=1, source_target_pairs={{0,2},{1,5},{2,0},{3,7},{4,6},{5,1},{6,4},{7,3},{8,10},{9,13},{10,... | collective-permute-start | bytes 811016 | tf_op jit(solution)/shard_map/ppermute | solution.py:312
  77.7 7.7 %collective-permute-start.26 = (f32[264,256]{1,0:T(8,128)S(1)}, f32[264,256]{1,0:T(8,128)S(1)}, u32[]{:S(2)}, u32[]{:S(2)}) collective-permute-start(f32[264,256]{1,0:T(8,128)S(1)} %collective-permute-done.25.refs_5_), channel_id=1, source_target_pairs={{0,4},{1,3},{2,6},{3,1},{4,0},{5,7},{6,2},{7,5},{8,12},{9,11},{10,... | collective-permute-start | bytes 811016 | tf_op jit(solution)/shard_map/ppermute | solution.py:312
  77.9 12.0 %collective-permute-start.24 = (f32[264,256]{1,0:T(8,128)S(1)}, f32[264,256]{1,0:T(8,128)S(1)}, u32[]{:S(2)}, u32[]{:S(2)}) collective-permute-start(f32[264,256]{1,0:T(8,128)S(1)} %collective-permute-done.18.refs_8_), channel_id=1, source_target_pairs={{0,4},{1,3},{2,6},{3,1},{4,0},{5,7},{6,2},{7,5},{8,12},{9,11},{10,... | collective-permute-start | bytes 811016 | tf_op jit(solution)/shard_map/ppermute | solution.py:312
  79.7 14.7 %collective-permute-start.29 = (f32[264,256]{1,0:T(8,128)S(1)}, f32[264,256]{1,0:T(8,128)S(1)}, u32[]{:S(2)}, u32[]{:S(2)}) collective-permute-start(f32[264,256]{1,0:T(8,128)S(1)} %collective-permute-done.23.refs_3_), channel_id=1, source_target_pairs={{0,8},{2,10},{4,12},{6,14},{16,0},{18,2},{20,4},{22,6},{24,16},{26... | collective-permute-start | bytes 811016 | tf_op jit(solution)/shard_map/ppermute | solution.py:319
  85.3 7.5 %collective-permute-start.31 = (f32[264,256]{1,0:T(8,128)S(1)}, f32[264,256]{1,0:T(8,128)S(1)}, u32[]{:S(2)}, u32[]{:S(2)}) collective-permute-start(f32[264,256]{1,0:T(8,128)S(1)} %collective-permute-done.30.refs_0_), channel_id=1, source_target_pairs={{0,4},{1,3},{2,6},{3,1},{4,0},{5,7},{6,2},{7,5},{8,12},{9,11},{10,... | collective-permute-start | bytes 811016 | tf_op jit(solution)/shard_map/ppermute | solution.py:312
  89.9 6.5 %collective-permute-start.27 = (f32[264,256]{1,0:T(8,128)S(1)}, f32[264,256]{1,0:T(8,128)S(1)}, u32[]{:S(2)}, u32[]{:S(2)}) collective-permute-start(f32[264,256]{1,0:T(8,128)S(1)} %collective-permute-done.19.refs_3_), channel_id=1, source_target_pairs={{0,2},{1,5},{2,0},{3,7},{4,6},{5,1},{6,4},{7,3},{8,10},{9,13},{10,... | collective-permute-start | bytes 811016 | tf_op jit(solution)/shard_map/ppermute | solution.py:312
  90.1 6.5 %collective-permute-start.28 = (f32[264,256]{1,0:T(8,128)S(1)}, f32[264,256]{1,0:T(8,128)S(1)}, u32[]{:S(2)}, u32[]{:S(2)}) collective-permute-start(f32[264,256]{1,0:T(8,128)S(1)} %collective-permute-done.19.refs_3_), channel_id=1, source_target_pairs={{0,4},{1,3},{2,6},{3,1},{4,0},{5,7},{6,2},{7,5},{8,12},{9,11},{10,... | collective-permute-start | bytes 811016 | tf_op jit(solution)/shard_map/ppermute | solution.py:312

commit v11 on v10

--- a/solution.py
+++ b/solution.py
@@ -62,12 +62,15 @@
     return jnp.broadcast_to(jnp.sum(c * c, axis=1, keepdims=True), (c.shape[0], LANES))
 
 
-def stats_kernel(lines, where_ref, points_ref, c_ref, out_ref, twice_ref, norm_ref, all_norm_ref):
+def stats_kernel(lines, chunks, where_ref, points_ref, c_ref, *refs):
+    out_ref, twice_ref, norm_ref, all_norm_ref = refs[-4:]
     rows, local = points_ref.shape[0], c_ref.shape[0]
     chunk = local // lines
     tile, size = min(256, rows), chunk // 4
     kept = pl.multiple_of(lax.rem(where_ref[0], 4) * size, size)
-    for l in range(lines):
+    if len(refs) > 4:
+        out_ref[...] = refs[0][...]
+    for i, l in enumerate(chunks):
         c = c_ref[l * chunk : (l + 1) * chunk, :]
         all_norm_ref[...] = norms(c)
         twice = c + c
@@ -85,25 +88,22 @@
             out_ref[0:1, at] = top
             out_ref[1:2, at] = total
         mine = c_ref[pl.ds(pl.multiple_of(l * chunk + kept, size), size), :]
-        twice_ref[l * size : (l + 1) * size, :] = mine + mine
-        norm_ref[l * size : (l + 1) * size, :] = all_norm_ref[pl.ds(kept, size), :]
-
-
-def stats(where, points, centroids, lines):
+        twice_ref[i * size : (i + 1) * size, :] = mine + mine
+        norm_ref[i * size : (i + 1) * size, :] = all_norm_ref[pl.ds(kept, size), :]
+
+
+def stats(where, points, centroids, lines, chunks, before=()):
     rows, width = points.shape
     local = centroids.shape[0]
+    kept = len(chunks) * local // lines // 4
     return call(
-        functools.partial(stats_kernel, lines),
-        (
-            f32(2, rows),
-            jax.ShapeDtypeStruct((local // 4, width), jnp.bfloat16),
-            f32(local // 4, LANES),
-        ),
-        [SMEM, VMEM, VMEM],
-        (where, points, centroids),
+        functools.partial(stats_kernel, lines, chunks),
+        (f32(2, rows), jax.ShapeDtypeStruct((kept, width), jnp.bfloat16), f32(kept, LANES)),
+        [SMEM] + [VMEM] * (2 + len(before)),
+        (where, points, centroids, *before),
         "stats",
         scratch=[pltpu.VMEM((local // lines, LANES), jnp.float32)],
-        flops=4 * rows * local * width,
+        flops=4 * rows * local * width * len(chunks) // lines,
     )
 
 
@@ -137,8 +137,11 @@
     return part, counted
 
 
-def own_kernel(cores, points_ref, twice_ref, norm_ref, lse_ref, acc_ref, cnt_ref):
+def own_kernel(cores, points_ref, low_ref, high_ref, norm_low_ref, norm_high_ref, lse_ref, acc_ref, cnt_ref, twice_ref, norm_ref):
     half = points_ref.shape[0] // (2 * cores)
+    cut = low_ref.shape[0]
+    twice_ref[0:cut, :], twice_ref[cut:, :] = low_ref[...], high_ref[...]
+    norm_ref[0:cut, :], norm_ref[cut:, :] = norm_low_ref[...], norm_high_ref[...]
     for i in range(2 * cores):
         x = points_ref[i * half : (i + 1) * half, :]
         part, counted = weigh(
@@ -152,8 +155,11 @@
             cnt_ref[...] += counted
 
 
+KINDS = ((0, 0), (1, 1), (0, 1), (1, 0))
+
+
 def near_rows(cores, half, core, refs, d0_ref, d1_ref):
-    for k, (kind, part) in enumerate(((0, 0), (1, 1), (0, 1), (1, 0))):
+    for k, (kind, part) in enumerate(KINDS):
         for rc in range(cores):
             at = half + 2 * (core ^ rc) + part
             tail_ref = d1_ref if (kind + rc) % 2 == 0 else d0_ref
@@ -330,9 +336,16 @@
         scratch=[pltpu.VMEM((2 * half, width), points.dtype), pltpu.SemaphoreType.DMA(())],
     )
     a0, b1 = exchange(first, 0), exchange(second, 1)
+
+    cut = lines // 2
+    pair, twice_low, norm_low = stats(where, points, centroids, lines, range(cut))
+    first, second, pair, a0, b1 = lax.optimization_barrier((first, second, pair, a0, b1))
     a1, b0 = exchange(second, 0), exchange(first, 1)
-
-    pair, twice, norm = stats(where, points, centroids, lines)
+    pair, twice_high, norm_high = stats(where, points, centroids, lines, range(cut, lines), (pair,))
+    kept = [twice_low, twice_high, norm_low, norm_high]
+    early = with_siblings((a0, b1))
+    early, pair = lax.optimization_barrier((early, pair))
+    a0, b1 = early[0], early[cores]
     pairs = [pair] + [flip_core(pair, rc) for rc in range(1, cores)]
     tail = max(8, 2 * cores)
     lse, log_evidence, pack_a, pack_b = call(
@@ -345,18 +358,25 @@
     d0, d1 = exchange(pack_a, 1), exchange(pack_b, 0)
 
     lanes = min(LANES, half)
-    acc, cnt = call(
+    a1, b0, lse = lax.optimization_barrier((a1, b0, lse))
+    near = early + with_siblings((a1, b0))
+    near, lse = lax.optimization_barrier((near, lse))
+    acc, cnt, twice, norm = call(
         functools.partial(own_kernel, cores),
-        (f32(share, width), f32(share, lanes)),
-        [VMEM] * 4,
-        (points, twice, norm, lse),
+        (
+            f32(share, width),
+            f32(share, lanes),
+            jax.ShapeDtypeStruct((share, width), jnp.bfloat16),
+            f32(share, LANES),
+        ),
+        [VMEM] * 6,
+        (points, *kept, lse),
         "own",
         flops=4 * share * width * rows,
     )
-    a0, b1, a1, b0, lse = lax.optimization_barrier((a0, b1, a1, b0, lse))
-    near = with_siblings((a0, b1, a1, b0))
-    lse_d = exchange(d1[half : half + 2 * cores, :half], 1)
-    near, d0, d1, acc, cnt = lax.optimization_barrier((near, d0, d1, acc, cnt))
+    lse, acc, cnt = lax.optimization_barrier((lse, acc, cnt))
+    lse_d = lax.ppermute(lse, "dp", [(i, i ^ 3) for i in range(n)])
+    d0, d1, acc, cnt, lse_d = lax.optimization_barrier((d0, d1, acc, cnt, lse_d))
     lead = call(
         functools.partial(lead_kernel, cores, order, half),
         (f32(size, width), f32(size, lanes)),
@@ -378,7 +398,7 @@
         [SMEM] + [VMEM] * (5 + 2 * cores),
         (where, twice, norm, lse_d, *lead, *far),
         "first",
-        flops=4 * size * width * rows,
+        flops=4 * size * width * 2 * rows,
     )
 
     def sums_of(steps):
@@ -412,7 +432,7 @@
 
     steps = [-s for s in range(1, lines // 2 + 1)] + list(range(1, lines // 2))
     got = {(0, 0): done}
-    previous, older = (), ()
+    previous, older = (), (done, done)
     for s in [0] + steps:
         x = got[0, s]
         if previous:
@@ -421,7 +441,7 @@
         if s == steps[-1]:
             break
         got[3, s] = exchange(got[1, s], 1)
-        previous, older = (got[2, s], *older), (got[3, s],)
+        previous, older = (got[2, s], *older[:1]), (*older[1:], got[3, s])
         ahead_of = steps[([0] + steps).index(s)]
         x = got[0, ahead_of + (1 if ahead_of < 0 else -1)]
         if ahead_of > 0:

time: 99 us -> 99 us (level)
  waiting for transfers between devices: 36.1 us -> 31.7 us
  starting transfers between devices: 35.7 us -> 39.6 us
    ppermute x18 -> x17, waiting for transfers between devices: 21.7 us -> 9.45 us  [exchange(): return lax.ppermute(x, ('dp', 'cent'), pairs)]
    ppermute x0 -> x1, waiting for transfers between devices: none -> 4.58 us  [body(): lse_d = lax.ppermute(lse, 'dp', [(i, i ^ 3) for i in range(n)])]
    ppermute x18 -> x17, starting transfers between devices: 19 us -> 23.5 us  [exchange(): return lax.ppermute(x, ('dp', 'cent'), pairs)]
    ppermute x7, waiting for transfers between devices: 13 us -> 16.5 us  [ring(): lax.ppermute(x, 'dp', [(4 * a + i, 4 * b + i) for a, b in pairs for i in...]
    ppermute x7, starting transfers between devices: 15.1 us -> 13.6 us  [ring(): lax.ppermute(x, 'dp', [(4 * a + i, 4 * b + i) for a, b in pairs for i in...]
    pallas_call x13 -> x14, Pallas kernels: 23.3 us -> 23.8 us  [call(): pl.pallas_call(kernel, out_shape=out_shape, in_specs=in_specs, out_specs=...]
  transfers between devices with their start and end apart: 32 -> 32, of which waited for: 19 -> 16; matrix products, arithmetic and copies ran while one was open for 0% -> 0% of each run, Pallas kernels for 19% -> 19%
where the time goes in v11:
time: 99 us; the launch traced here: 98.8 us
  starting transfers between devices  39.6 us (40%)
  waiting for transfers between devices  31.7 us (32%)
  Pallas kernels  23.8 us (24%)
  local copies, waits for them, and re-layouts  2.64 us (3%)
    pallas_call x14, Pallas kernels, call(): pl.pallas_call(kernel, out_shape=out_shape, in_specs=in_specs, out_specs=...  23.8 us
    ppermute x17, starting transfers between devices, exchange(): return lax.ppermute(x, ('dp', 'cent'), pairs)  23.5 us
    ppermute x7, waiting for transfers between devices, ring(): lax.ppermute(x, 'dp', [(4 * a + i, 4 * b + i) for a, b in pairs for i in...  16.5 us
    ppermute x7, starting transfers between devices, ring(): lax.ppermute(x, 'dp', [(4 * a + i, 4 * b + i) for a, b in pairs for i in...  13.6 us
    ppermute x17, waiting for transfers between devices, exchange(): return lax.ppermute(x, ('dp', 'cent'), pairs)  9.45 us
    ppermute x1, waiting for transfers between devices, body(): lse_d = lax.ppermute(lse, 'dp', [(i, i ^ 3) for i in range(n)])  4.58 us
    unnamed x8, local copies, waits for them, and re-layouts  2.64 us
  transfers between devices with their start and end apart: 32, of which 16 were waited for; matrix products, arithmetic and copies ran while one was open for 0% of the time, Pallas kernels for 19%

profile of v11, /device:TPU:0, one launch (start us, length us, event | category | flops | bytes accessed | tf_op | source)
XLA Modules:
  0.0 98.8 jit_solution(16446219834914021046)
XLA Ops:
  0.7 1.0 %copy-done.1 = bf16[1024,256]{1,0:T(8,128)(2,1)S(1)} copy-done((bf16[1024,256]{1,0:T(8,128)(2,1)S(1)}, bf16[1024,256]{1,0:T(8,128)(2,1)}, u32[]{:S(2)}) %copy-start.1) | copy-done | bytes 524312
  2.4 3.0 %collective-permute-start = (f32[256,256]{1,0:T(8,128)S(1)}, f32[256,256]{1,0:T(8,128)S(1)}, u32[]{:S(2)}, u32[]{:S(2)}) collective-permute-start(f32[256,256]{1,0:T(8,128)S(1)} %get-tuple-element.80), channel_id=1, source_target_pairs={{0,2},{1,5},{2,0},{3,7},{4,6},{5,1},{6,4},{7,3},{8,10},{9,13},{10,... | collective-permute-start | bytes 786440 | tf_op jit(solution)/shard_map/ppermute | solution.py:318
  5.4 1.5 %collective-permute-start.1 = (f32[256,256]{1,0:T(8,128)S(1)}, f32[256,256]{1,0:T(8,128)S(1)}, u32[]{:S(2)}, u32[]{:S(2)}) collective-permute-start(f32[256,256]{1,0:T(8,128)S(1)} %get-tuple-element.79), channel_id=1, source_target_pairs={{0,4},{1,3},{2,6},{3,1},{4,0},{5,7},{6,2},{7,5},{8,12},{9,11},{10,... | collective-permute-start | bytes 786440 | tf_op jit(solution)/shard_map/ppermute | solution.py:318
  6.9 1.6 %copy-done.3 = bf16[4096,256]{1,0:T(8,128)(2,1)S(1)} copy-done((bf16[4096,256]{1,0:T(8,128)(2,1)S(1)}, bf16[4096,256]{1,0:T(8,128)(2,1)}, u32[]{:S(2)}) %copy-start.3) | copy-done | bytes 2097176
  8.5 3.2 %stats.2 = (f32[2,1024]{1,0:T(2,128)S(1)}, bf16[512,256]{1,0:T(8,128)(2,1)S(1)}, f32[512,128]{1,0:T(8,128)S(1)}) custom-call(s32[2]{0:T(128)S(1)} %pad_add_fusion.where_ref, bf16[1024,256]{1,0:T(8,128)(2,1)S(1)} %copy-done.1, bf16[4096,256]{1,0:T(8,128)(2,1)S(1)} %copy-done.3), custom_call_target="tpu_custom_call" | custom-call | flops 2147483648 | bytes 2621448 | tf_op jit(solution)/shard_map/stats/pallas_call | solution.py:27
  12.5 2.5 %collective-permute-start.4 = (f32[256,256]{1,0:T(8,128)S(1)}, f32[256,256]{1,0:T(8,128)S(1)}, u32[]{:S(2)}, u32[]{:S(2)}) collective-permute-start(f32[256,256]{1,0:T(8,128)S(1)} %get-tuple-element.79), channel_id=1, source_target_pairs={{0,2},{1,5},{2,0},{3,7},{4,6},{5,1},{6,4},{7,3},{8,10},{9,13},{10,... | collective-permute-start | bytes 786440 | tf_op jit(solution)/shard_map/ppermute | solution.py:318
  15.7 3.3 %stats.3 = (f32[2,1024]{1,0:T(2,128)S(1)}, bf16[512,256]{1,0:T(8,128)(2,1)S(1)}, f32[512,128]{1,0:T(8,128)S(1)}) custom-call(s32[2]{0:T(128)S(1)} %pad_add_fusion.where_ref, bf16[1024,256]{1,0:T(8,128)(2,1)S(1)} %copy-done.1, bf16[4096,256]{1,0:T(8,128)(2,1)S(1)} %copy-done.3, f32[2,1024]{1,0:T(2,128)S(1)} %get-tuple-element.68.refs_0_), custom_call_target="tpu_custom_call" | custom-call | flops 2147483648 | bytes 2629640 | tf_op jit(solution)/shard_map/stats/pallas_call | solution.py:27
  19.0 1.2 %collective-permute-done.6.refs_1_ = f32[2,1024]{1,0:T(2,128)S(1)} collective-permute-done((f32[2,1024]{1,0:T(2,128)S(1)}, f32[2,1024]{1,0:T(2,128)S(1)}, u32[]{:S(2)}, u32[]{:S(2)}) %collective-permute-start.6) | collective-permute-done | bytes 8224 | tf_op jit(solution)/shard_map/ppermute | solution.py:321
  20.8 1.2 %collective-permute-done.4.refs_4_ = f32[256,256]{1,0:T(8,128)S(1)} collective-permute-done((f32[256,256]{1,0:T(8,128)S(1)}, f32[256,256]{1,0:T(8,128)S(1)}, u32[]{:S(2)}, u32[]{:S(2)}) %collective-permute-start.4) | collective-permute-done | bytes 262176 | tf_op jit(solution)/shard_map/ppermute | solution.py:318
  22.6 1.6 %collective-permute-start.10 = (f32[264,256]{1,0:T(8,128)S(1)}, f32[264,256]{1,0:T(8,128)S(1)}, u32[]{:S(2)}, u32[]{:S(2)}) collective-permute-start(f32[264,256]{1,0:T(8,128)S(1)} %get-tuple-element.90), channel_id=1, source_target_pairs={{0,2},{1,5},{2,0},{3,7},{4,6},{5,1},{6,4},{7,3},{8,10},{9,13},{10,... | collective-permute-start | bytes 811016 | tf_op jit(solution)/shard_map/ppermute | solution.py:318
  24.2 1.0 %collective-permute-start.9 = (f32[264,256]{1,0:T(8,128)S(1)}, f32[264,256]{1,0:T(8,128)S(1)}, u32[]{:S(2)}, u32[]{:S(2)}) collective-permute-start(f32[264,256]{1,0:T(8,128)S(1)} %get-tuple-element.89), channel_id=1, source_target_pairs={{0,4},{1,3},{2,6},{3,1},{4,0},{5,7},{6,2},{7,5},{8,12},{9,11},{10,... | collective-permute-start | bytes 811016 | tf_op jit(solution)/shard_map/ppermute | solution.py:318
  25.2 1.5 %own.1 = (f32[1024,256]{1,0:T(8,128)S(1)}, f32[1024,128]{1,0:T(8,128)S(1)}, bf16[1024,256]{1,0:T(8,128)(2,1)S(1)}, f32[1024,128]{1,0:T(8,128)S(1)}) custom-call(bf16[1024,256]{1,0:T(8,128)(2,1)S(1)} %copy-done.2, bf16[512,256]{1,0:T(8,128)(2,1)S(1)} %get-tuple-element.64.low_ref, bf16[512,256]{1,0:T(8,128)(2,1)S(1)} %get-tuple-element.69.high_ref, ...), custom_call_target="tpu_custom_call" | custom-call | flops 1073741824 | bytes 1576960 | tf_op jit(solution)/shard_map/own/pallas_call | solution.py:27
  26.8 0.9 collective-permute-start.11
  27.7 4.6 %collective-permute-done.11.lse_ref = f32[4,256]{1,0:T(4,128)S(1)} collective-permute-done((f32[4,256]{1,0:T(4,128)S(1)}, f32[4,256]{1,0:T(4,128)S(1)}, u32[]{:S(2)}, u32[]{:S(2)}) %collective-permute-start.11) | collective-permute-done | bytes 4128 | tf_op jit(solution)/shard_map/ppermute | solution.py:378
  32.8 1.5 %lead.1 = (f32[256,256]{1,0:T(8,128)S(1)}, f32[256,128]{1,0:T(8,128)S(1)}) custom-call(s32[2]{0:T(128)S(1)} %pad_add_fusion.where_ref, bf16[1024,256]{1,0:T(8,128)(2,1)S(1)} %get-tuple-element.87.twice_ref, f32[1024,128]{1,0:T(8,128)S(1)} %get-tuple-element.88.norm_ref, f32[1024,256]{1,0:T(8,128)S(1)} %get-tuple-element.96.acc_ref, ...), custom_call_target="tpu_custom_call" | custom-call | flops 536870912 | bytes 5259272 | tf_op jit(solution)/shard_map/lead/pallas_call | solution.py:27
  34.3 1.2 %first.1 = f32[264,256]{1,0:T(8,128)S(1)} custom-call(s32[2]{0:T(128)S(1)} %pad_add_fusion.where_ref, bf16[1024,256]{1,0:T(8,128)(2,1)S(1)} %get-tuple-element.87.twice_ref, f32[1024,128]{1,0:T(8,128)S(1)} %get-tuple-element.88.norm_ref, f32[4,256]{1,0:T(4,128)S(1)} %collective-permute-done.11.lse_ref, f32[256,256]{1,0:T(8,128)S(1)} %get-tuple-element.111.lead_acc_ref, ...), custom_call_target="tpu_custom_call" | custom-call | flops 536870912 | bytes 2527240 | tf_op jit(solution)/shard_map/first/pallas_call | solution.py:27
  35.5 2.8 %collective-permute-start.14 = (f32[264,256]{1,0:T(8,128)S(1)}, f32[264,256]{1,0:T(8,128)S(1)}, u32[]{:S(2)}, u32[]{:S(2)}) collective-permute-start(f32[264,256]{1,0:T(8,128)S(1)} %first.1), channel_id=1, source_target_pairs={{0,16},{2,18},{4,20},{6,22},{16,24},{18,26},{20,28},{22,30},{24,8}... | collective-permute-start | bytes 811016 | tf_op jit(solution)/shard_map/ppermute | solution.py:325
  38.3 1.8 %rest.3 = f32[264,256]{1,0:T(8,128)S(1)} custom-call(s32[2]{0:T(128)S(1)} %pad_add_fusion.where_ref, bf16[1024,256]{1,0:T(8,128)(2,1)S(1)} %get-tuple-element.87.twice_ref, f32[1024,128]{1,0:T(8,128)S(1)} %get-tuple-element.88.norm_ref, f32[1024,256]{1,0:T(8,128)S(1)} %get-tuple-element.96.acc_ref, f32[1024,128]{1,0:T(8,128)S(1)} %get-tuple-element.97.cnt_ref, ...), custom_call_target="tpu_custom_call" | custom-call | flops 805306368 | bytes 5804040 | tf_op jit(solution)/shard_map/rest/pallas_call | solution.py:27
  40.4 3.5 %rest.2 = (f32[264,256]{1,0:T(8,128)S(1)}, f32[264,256]{1,0:T(8,128)S(1)}) custom-call(s32[2]{0:T(128)S(1)} %pad_add_fusion.where_ref, bf16[1024,256]{1,0:T(8,128)(2,1)S(1)} %get-tuple-element.87.twice_ref, f32[1024,128]{1,0:T(8,128)S(1)} %get-tuple-element.88.norm_ref, f32[1024,256]{1,0:T(8,128)} %copy-done, f32[1024,128]{1,0:T(8,128)S(1)} %get-tuple-element.97.cnt_ref, ...), custom_call_target="tpu_custom_call" | custom-call | flops 1610612736 | bytes 5804040 | tf_op jit(solution)/shard_map/rest/pallas_call | solution.py:27
  43.9 1.3 %collective-permute-done.14.b_ref = f32[264,256]{1,0:T(8,128)S(1)} collective-permute-done((f32[264,256]{1,0:T(8,128)S(1)}, f32[264,256]{1,0:T(8,128)S(1)}, u32[]{:S(2)}, u32[]{:S(2)}) %collective-permute-start.14) | collective-permute-done | bytes 270368 | tf_op jit(solution)/shard_map/ppermute | solution.py:325
  45.2 3.4 %collective-permute-start.15 = (f32[264,256]{1,0:T(8,128)S(1)}, f32[264,256]{1,0:T(8,128)S(1)}, u32[]{:S(2)}, u32[]{:S(2)}) collective-permute-start(f32[264,256]{1,0:T(8,128)S(1)} %add.3), channel_id=1, source_target_pairs={{0,16},{2,18},{4,20},{6,22},{16,24},{18,26},{20,28},{22,30},{24,8}... | collective-permute-start | bytes 811016 | tf_op jit(solution)/shard_map/ppermute | solution.py:325
  48.6 4.1 %collective-permute-done.16.second_ref = f32[264,256]{1,0:T(8,128)S(1)} collective-permute-done((f32[264,256]{1,0:T(8,128)S(1)}, f32[264,256]{1,0:T(8,128)S(1)}, u32[]{:S(2)}, u32[]{:S(2)}) %collective-permute-start.16) | collective-permute-done | bytes 270368 | tf_op jit(solution)/shard_map/ppermute | solution.py:325
  52.8 4.8 %collective-permute-done.15.first_ref = f32[264,256]{1,0:T(8,128)S(1)} collective-permute-done((f32[264,256]{1,0:T(8,128)S(1)}, f32[264,256]{1,0:T(8,128)S(1)}, u32[]{:S(2)}, u32[]{:S(2)}) %collective-permute-start.15) | collective-permute-done | bytes 270368 | tf_op jit(solution)/shard_map/ppermute | solution.py:325
  57.6 0.8 finish.1.refs_0_
  58.4 1.7 %collective-permute-start.17 = (f32[264,256]{1,0:T(8,128)S(1)}, f32[264,256]{1,0:T(8,128)S(1)}, u32[]{:S(2)}, u32[]{:S(2)}) collective-permute-start(f32[264,256]{1,0:T(8,128)S(1)} %finish.1.refs_0_), channel_id=1, source_target_pairs={{0,16},{2,18},{4,20},{6,22},{16,24},{18,26},{20,28},{22,30},{24,8}... | collective-permute-start | bytes 811016 | tf_op jit(solution)/shard_map/ppermute | solution.py:325
  60.1 1.1 %collective-permute-start.20 = (f32[264,256]{1,0:T(8,128)S(1)}, f32[264,256]{1,0:T(8,128)S(1)}, u32[]{:S(2)}, u32[]{:S(2)}) collective-permute-start(f32[264,256]{1,0:T(8,128)S(1)} %finish.1.refs_0_), channel_id=1, source_target_pairs={{0,4},{1,3},{2,6},{3,1},{4,0},{5,7},{6,2},{7,5},{8,12},{9,11},{10,... | collective-permute-start | bytes 811016 | tf_op jit(solution)/shard_map/ppermute | solution.py:318
  61.2 1.5 %collective-permute-start.23 = (f32[264,256]{1,0:T(8,128)S(1)}, f32[264,256]{1,0:T(8,128)S(1)}, u32[]{:S(2)}, u32[]{:S(2)}) collective-permute-start(f32[264,256]{1,0:T(8,128)S(1)} %finish.1.refs_0_), channel_id=1, source_target_pairs={{0,2},{1,5},{2,0},{3,7},{4,6},{5,1},{6,4},{7,3},{8,10},{9,13},{10,... | collective-permute-start | bytes 811016 | tf_op jit(solution)/shard_map/ppermute | solution.py:318
  62.7 4.0 %collective-permute-done.17.refs_4_ = f32[264,256]{1,0:T(8,128)S(1)} collective-permute-done((f32[264,256]{1,0:T(8,128)S(1)}, f32[264,256]{1,0:T(8,128)S(1)}, u32[]{:S(2)}, u32[]{:S(2)}) %collective-permute-start.17) | collective-permute-done | bytes 270368 | tf_op jit(solution)/shard_map/ppermute | solution.py:325
  66.8 1.9 %collective-permute-start.18 = (f32[264,256]{1,0:T(8,128)S(1)}, f32[264,256]{1,0:T(8,128)S(1)}, u32[]{:S(2)}, u32[]{:S(2)}) collective-permute-start(f32[264,256]{1,0:T(8,128)S(1)} %collective-permute-done.17.refs_4_), channel_id=1, source_target_pairs={{0,16},{2,18},{4,20},{6,22},{16,24},{18,26},{20,28},{22,30},{24,8}... | collective-permute-start | bytes 811016 | tf_op jit(solution)/shard_map/ppermute | solution.py:325
  68.7 1.1 %collective-permute-start.21 = (f32[264,256]{1,0:T(8,128)S(1)}, f32[264,256]{1,0:T(8,128)S(1)}, u32[]{:S(2)}, u32[]{:S(2)}) collective-permute-start(f32[264,256]{1,0:T(8,128)S(1)} %collective-permute-done.17.refs_4_), channel_id=1, source_target_pairs={{0,4},{1,3},{2,6},{3,1},{4,0},{5,7},{6,2},{7,5},{8,12},{9,11},{10,... | collective-permute-start | bytes 811016 | tf_op jit(solution)/shard_map/ppermute | solution.py:318
  69.8 1.5 %collective-permute-start.30 = (f32[264,256]{1,0:T(8,128)S(1)}, f32[264,256]{1,0:T(8,128)S(1)}, u32[]{:S(2)}, u32[]{:S(2)}) collective-permute-start(f32[264,256]{1,0:T(8,128)S(1)} %collective-permute-done.17.refs_4_), channel_id=1, source_target_pairs={{0,2},{1,5},{2,0},{3,7},{4,6},{5,1},{6,4},{7,3},{8,10},{9,13},{10,... | collective-permute-start | bytes 811016 | tf_op jit(solution)/shard_map/ppermute | solution.py:318
  71.3 0.9 collective-permute-start.24
  72.2 2.1 %collective-permute-done.18.refs_8_ = f32[264,256]{1,0:T(8,128)S(1)} collective-permute-done((f32[264,256]{1,0:T(8,128)S(1)}, f32[264,256]{1,0:T(8,128)S(1)}, u32[]{:S(2)}, u32[]{:S(2)}) %collective-permute-start.18) | collective-permute-done | bytes 270368 | tf_op jit(solution)/shard_map/ppermute | solution.py:325
  74.2 2.2 %collective-permute-start.19 = (f32[264,256]{1,0:T(8,128)S(1)}, f32[264,256]{1,0:T(8,128)S(1)}, u32[]{:S(2)}, u32[]{:S(2)}) collective-permute-start(f32[264,256]{1,0:T(8,128)S(1)} %finish.1.refs_0_), channel_id=1, source_target_pairs={{0,8},{2,10},{4,12},{6,14},{16,0},{18,2},{20,4},{22,6},{24,16},{26... | collective-permute-start | bytes 811016 | tf_op jit(solution)/shard_map/ppermute | solution.py:325
  76.4 1.5 %collective-permute-start.28 = (f32[264,256]{1,0:T(8,128)S(1)}, f32[264,256]{1,0:T(8,128)S(1)}, u32[]{:S(2)}, u32[]{:S(2)}) collective-permute-start(f32[264,256]{1,0:T(8,128)S(1)} %collective-permute-done.18.refs_8_), channel_id=1, source_target_pairs={{0,2},{1,5},{2,0},{3,7},{4,6},{5,1},{6,4},{7,3},{8,10},{9,13},{10,... | collective-permute-start | bytes 811016 | tf_op jit(solution)/shard_map/ppermute | solution.py:318
  77.9 1.1 %collective-permute-start.22 = (f32[264,256]{1,0:T(8,128)S(1)}, f32[264,256]{1,0:T(8,128)S(1)}, u32[]{:S(2)}, u32[]{:S(2)}) collective-permute-start(f32[264,256]{1,0:T(8,128)S(1)} %collective-permute-done.18.refs_8_), channel_id=1, source_target_pairs={{0,4},{1,3},{2,6},{3,1},{4,0},{5,7},{6,2},{7,5},{8,12},{9,11},{10,... | collective-permute-start | bytes 811016 | tf_op jit(solution)/shard_map/ppermute | solution.py:318
  79.0 0.9 collective-permute-start.31
  79.9 1.6 %collective-permute-done.24.refs_3_ = f32[264,256]{1,0:T(8,128)S(1)} collective-permute-done((f32[264,256]{1,0:T(8,128)S(1)}, f32[264,256]{1,0:T(8,128)S(1)}, u32[]{:S(2)}, u32[]{:S(2)}) %collective-permute-start.24) | collective-permute-done | bytes 270368 | tf_op jit(solution)/shard_map/ppermute | solution.py:318
  81.7 1.4 %collective-permute-start.27 = (f32[264,256]{1,0:T(8,128)S(1)}, f32[264,256]{1,0:T(8,128)S(1)}, u32[]{:S(2)}, u32[]{:S(2)}) collective-permute-start(f32[264,256]{1,0:T(8,128)S(1)} %collective-permute-done.24.refs_3_), channel_id=1, source_target_pairs={{0,8},{2,10},{4,12},{6,14},{16,0},{18,2},{20,4},{22,6},{24,16},{26... | collective-permute-start | bytes 811016 | tf_op jit(solution)/shard_map/ppermute | solution.py:325
  83.1 2.8 %collective-permute-done.28.refs_0_ = f32[264,256]{1,0:T(8,128)S(1)} collective-permute-done((f32[264,256]{1,0:T(8,128)S(1)}, f32[264,256]{1,0:T(8,128)S(1)}, u32[]{:S(2)}, u32[]{:S(2)}) %collective-permute-start.28) | collective-permute-done | bytes 270368 | tf_op jit(solution)/shard_map/ppermute | solution.py:318
  85.8 1.1 %collective-permute-start.29 = (f32[264,256]{1,0:T(8,128)S(1)}, f32[264,256]{1,0:T(8,128)S(1)}, u32[]{:S(2)}, u32[]{:S(2)}) collective-permute-start(f32[264,256]{1,0:T(8,128)S(1)} %collective-permute-done.28.refs_0_), channel_id=1, source_target_pairs={{0,4},{1,3},{2,6},{3,1},{4,0},{5,7},{6,2},{7,5},{8,12},{9,11},{10,... | collective-permute-start | bytes 811016 | tf_op jit(solution)/shard_map/ppermute | solution.py:318
  87.0 1.5 %collective-permute-start.25 = (f32[264,256]{1,0:T(8,128)S(1)}, f32[264,256]{1,0:T(8,128)S(1)}, u32[]{:S(2)}, u32[]{:S(2)}) collective-permute-start(f32[264,256]{1,0:T(8,128)S(1)} %collective-permute-done.19.refs_3_), channel_id=1, source_target_pairs={{0,2},{1,5},{2,0},{3,7},{4,6},{5,1},{6,4},{7,3},{8,10},{9,13},{10,... | collective-permute-start | bytes 811016 | tf_op jit(solution)/shard_map/ppermute | solution.py:318
  88.5 0.9 collective-permute-start.26
  90.1 2.0 %place_early.1 = (f32[4096,256]{1,0:T(8,128)}, f32[32,128]{1,0:T(8,128)S(1)}) custom-call(s32[2]{0:T(128)S(1)} %pad_add_fusion.where_ref, f32[264,256]{1,0:T(8,128)S(1)} %finish.1.refs_0_, f32[264,256]{1,0:T(8,128)S(1)} %collective-permute-done.23.refs_1_, f32[264,256]{1,0:T(8,128)S(1)} %collective-permute-done.20.refs_2_, ...), custom_call_target="tpu_custom_call" | custom-call | bytes 2433032 | tf_op jit(solution)/shard_map/place_early/pallas_call | solution.py:27
  92.1 1.5 %collective-permute-done.29.refs_2_ = f32[264,256]{1,0:T(8,128)S(1)} collective-permute-done((f32[264,256]{1,0:T(8,128)S(1)}, f32[264,256]{1,0:T(8,128)S(1)}, u32[]{:S(2)}, u32[]{:S(2)}) %collective-permute-start.29) | collective-permute-done | bytes 270368 | tf_op jit(solution)/shard_map/ppermute | solution.py:318
  93.7 1.5 %place_middle.1 = (f32[4096,256]{1,0:T(8,128)}, f32[32,128]{1,0:T(8,128)S(1)}) custom-call(s32[2]{0:T(128)S(1)} %pad_add_fusion.where_ref, f32[264,256]{1,0:T(8,128)S(1)} %collective-permute-done.28.refs_0_, f32[264,256]{1,0:T(8,128)S(1)} %collective-permute-done.22.refs_1_, ...), custom_call_target="tpu_custom_call", output_to_operand_aliasing={{0}: (6, {})} | custom-call | bytes 5292040 | tf_op jit(solution)/shard_map/place_middle/pallas_call | solution.py:27
  95.3 1.2 %collective-permute-done.26.refs_1_ = f32[264,256]{1,0:T(8,128)S(1)} collective-permute-done((f32[264,256]{1,0:T(8,128)S(1)}, f32[264,256]{1,0:T(8,128)S(1)}, u32[]{:S(2)}, u32[]{:S(2)}) %collective-permute-start.26) | collective-permute-done | bytes 270368 | tf_op jit(solution)/shard_map/ppermute | solution.py:318
  96.5 2.1 %place_late.1 = (f32[4096,256]{1,0:T(8,128)}, f32[32,128]{1,0:T(8,128)}) custom-call(s32[2]{0:T(128)S(1)} %pad_add_fusion.where_ref, f32[264,256]{1,0:T(8,128)S(1)} %collective-permute-done.25.refs_0_, f32[264,256]{1,0:T(8,128)S(1)} %collective-permute-done.26.refs_1_, ...), custom_call_target="tpu_custom_call", output_to_operand_aliasing={{0}: (5, {})} | custom-call | bytes 5021704 | tf_op jit(solution)/shard_map/place_late/pallas_call | solution.py:27
  (39 shorter events, 5.3 us)
Async XLA Ops:
  0.7 1.0 %copy-start.1 = (bf16[1024,256]{1,0:T(8,128)(2,1)S(1)}, bf16[1024,256]{1,0:T(8,128)(2,1)}, u32[]{:S(2)}) copy-start(bf16[1024,256]{1,0:T(8,128)(2,1)} %points_ref.7) | copy-start | bytes 1572868
  2.4 9.6 %collective-permute-start = (f32[256,256]{1,0:T(8,128)S(1)}, f32[256,256]{1,0:T(8,128)S(1)}, u32[]{:S(2)}, u32[]{:S(2)}) collective-permute-start(f32[256,256]{1,0:T(8,128)S(1)} %get-tuple-element.80), channel_id=1, source_target_pairs={{0,2},{1,5},{2,0},{3,7},{4,6},{5,1},{6,4},{7,3},{8,10},{9,13},{10,... | collective-permute-start | bytes 786440 | tf_op jit(solution)/shard_map/ppermute | solution.py:318
  5.4 6.6 %collective-permute-start.1 = (f32[256,256]{1,0:T(8,128)S(1)}, f32[256,256]{1,0:T(8,128)S(1)}, u32[]{:S(2)}, u32[]{:S(2)}) collective-permute-start(f32[256,256]{1,0:T(8,128)S(1)} %get-tuple-element.79), channel_id=1, source_target_pairs={{0,4},{1,3},{2,6},{3,1},{4,0},{5,7},{6,2},{7,5},{8,12},{9,11},{10,... | collective-permute-start | bytes 786440 | tf_op jit(solution)/shard_map/ppermute | solution.py:318
  6.9 1.6 %copy-start.3 = (bf16[4096,256]{1,0:T(8,128)(2,1)S(1)}, bf16[4096,256]{1,0:T(8,128)(2,1)}, u32[]{:S(2)}) copy-start(bf16[4096,256]{1,0:T(8,128)(2,1)} %c_ref.3) | copy-start | bytes 6291460
  12.0 13.3 %copy-start.2 = (bf16[1024,256]{1,0:T(8,128)(2,1)S(1)}, bf16[1024,256]{1,0:T(8,128)(2,1)}, u32[]{:S(2)}) copy-start(bf16[1024,256]{1,0:T(8,128)(2,1)} %points_ref.7) | copy-start | bytes 1572868
  12.0 7.0 %collective-permute-start.2 = (f32[256,256]{1,0:T(8,128)S(1)}, f32[256,256]{1,0:T(8,128)S(1)}, u32[]{:S(2)}, u32[]{:S(2)}) collective-permute-start(f32[256,256]{1,0:T(8,128)S(1)} %collective-permute-done.a0_ref.refs_0_), channel_id=1, source_target_pairs={{0,1},{1,0},{2,3},{3,2},{4,5},{5,4},{6,7},{7,6},{8,9},{9,8},{10,11... | collective-permute-start | bytes 786440 | tf_op jit(solution)/shard_map/ppermute | solution.py:321
  12.4 6.6 %collective-permute-start.3 = (f32[256,256]{1,0:T(8,128)S(1)}, f32[256,256]{1,0:T(8,128)S(1)}, u32[]{:S(2)}, u32[]{:S(2)}) collective-permute-start(f32[256,256]{1,0:T(8,128)S(1)} %collective-permute-done.1.b1_ref.refs_2_), channel_id=1, source_target_pairs={{0,1},{1,0},{2,3},{3,2},{4,5},{5,4},{6,7},{7,6},{8,9},{9,8},{10,11... | collective-permute-start | bytes 786440 | tf_op jit(solution)/shard_map/ppermute | solution.py:321
  12.5 9.6 %collective-permute-start.4 = (f32[256,256]{1,0:T(8,128)S(1)}, f32[256,256]{1,0:T(8,128)S(1)}, u32[]{:S(2)}, u32[]{:S(2)}) collective-permute-start(f32[256,256]{1,0:T(8,128)S(1)} %get-tuple-element.79), channel_id=1, source_target_pairs={{0,2},{1,5},{2,0},{3,7},{4,6},{5,1},{6,4},{7,3},{8,10},{9,13},{10,... | collective-permute-start | bytes 786440 | tf_op jit(solution)/shard_map/ppermute | solution.py:318
  15.0 7.1 %collective-permute-start.5 = (f32[256,256]{1,0:T(8,128)S(1)}, f32[256,256]{1,0:T(8,128)S(1)}, u32[]{:S(2)}, u32[]{:S(2)}) collective-permute-start(f32[256,256]{1,0:T(8,128)S(1)} %get-tuple-element.80), channel_id=1, source_target_pairs={{0,4},{1,3},{2,6},{3,1},{4,0},{5,7},{6,2},{7,5},{8,12},{9,11},{10,... | collective-permute-start | bytes 786440 | tf_op jit(solution)/shard_map/ppermute | solution.py:318
  19.0 1.2 %collective-permute-start.6 = (f32[2,1024]{1,0:T(2,128)S(1)}, f32[2,1024]{1,0:T(2,128)S(1)}, u32[]{:S(2)}, u32[]{:S(2)}) collective-permute-start(f32[2,1024]{1,0:T(2,128)S(1)} %get-tuple-element.81.refs_0_), channel_id=1, source_target_pairs={{0,1},{1,0},{2,3},{3,2},{4,5},{5,4},{6,7},{7,6},{8,9},{9,8},{10,11... | collective-permute-start | bytes 24584 | tf_op jit(solution)/shard_map/ppermute | solution.py:321
  22.0 3.2 %collective-permute-start.7 = (f32[256,256]{1,0:T(8,128)S(1)}, f32[256,256]{1,0:T(8,128)S(1)}, u32[]{:S(2)}, u32[]{:S(2)}) collective-permute-start(f32[256,256]{1,0:T(8,128)S(1)} %collective-permute-done.4.refs_4_), channel_id=1, source_target_pairs={{0,1},{1,0},{2,3},{3,2},{4,5},{5,4},{6,7},{7,6},{8,9},{9,8},{10,11... | collective-permute-start | bytes 786440 | tf_op jit(solution)/shard_map/ppermute | solution.py:321
  22.1 3.1 %collective-permute-start.8 = (f32[256,256]{1,0:T(8,128)S(1)}, f32[256,256]{1,0:T(8,128)S(1)}, u32[]{:S(2)}, u32[]{:S(2)}) collective-permute-start(f32[256,256]{1,0:T(8,128)S(1)} %collective-permute-done.5.refs_6_), channel_id=1, source_target_pairs={{0,1},{1,0},{2,3},{3,2},{4,5},{5,4},{6,7},{7,6},{8,9},{9,8},{10,11... | collective-permute-start | bytes 786440 | tf_op jit(solution)/shard_map/ppermute | solution.py:321
  22.6 9.7 %collective-permute-start.10 = (f32[264,256]{1,0:T(8,128)S(1)}, f32[264,256]{1,0:T(8,128)S(1)}, u32[]{:S(2)}, u32[]{:S(2)}) collective-permute-start(f32[264,256]{1,0:T(8,128)S(1)} %get-tuple-element.90), channel_id=1, source_target_pairs={{0,2},{1,5},{2,0},{3,7},{4,6},{5,1},{6,4},{7,3},{8,10},{9,13},{10,... | collective-permute-start | bytes 811016 | tf_op jit(solution)/shard_map/ppermute | solution.py:318
  24.2 8.1 %collective-permute-start.9 = (f32[264,256]{1,0:T(8,128)S(1)}, f32[264,256]{1,0:T(8,128)S(1)}, u32[]{:S(2)}, u32[]{:S(2)}) collective-permute-start(f32[264,256]{1,0:T(8,128)S(1)} %get-tuple-element.89), channel_id=1, source_target_pairs={{0,4},{1,3},{2,6},{3,1},{4,0},{5,7},{6,2},{7,5},{8,12},{9,11},{10,... | collective-permute-start | bytes 811016 | tf_op jit(solution)/shard_map/ppermute | solution.py:318
  26.8 13.4 %copy-start = (f32[1024,256]{1,0:T(8,128)}, f32[1024,256]{1,0:T(8,128)S(1)}, u32[]{:S(2)}) copy-start(f32[1024,256]{1,0:T(8,128)S(1)} %get-tuple-element.96.acc_ref) | copy-start | bytes 3145732
  26.8 5.5 %collective-permute-start.11 = (f32[4,256]{1,0:T(4,128)S(1)}, f32[4,256]{1,0:T(4,128)S(1)}, u32[]{:S(2)}, u32[]{:S(2)}) collective-permute-start(f32[4,256]{1,0:T(4,128)S(1)} %get-tuple-element.95.lse_ref), channel_id=1, source_target_pairs={{0,6},{2,4},{4,2},{6,0},{8,14},{10,12},{12,10},{14,8},{16,22},{18,... | collective-permute-start | bytes 12296 | tf_op jit(solution)/shard_map/ppermute | solution.py:378
  32.3 2.0 %collective-permute-start.12 = (f32[264,256]{1,0:T(8,128)S(1)}, f32[264,256]{1,0:T(8,128)S(1)}, u32[]{:S(2)}, u32[]{:S(2)}) collective-permute-start(f32[264,256]{1,0:T(8,128)S(1)} %collective-permute-done.9.refs_8_.refs_0_), channel_id=1, source_target_pairs={{0,1},{1,0},{2,3},{3,2},{4,5},{5,4},{6,7},{7,6},{8,9},{9,8},{10,11... | collective-permute-start | bytes 811016 | tf_op jit(solution)/shard_map/ppermute | solution.py:321
  32.3 2.0 %collective-permute-start.13 = (f32[264,256]{1,0:T(8,128)S(1)}, f32[264,256]{1,0:T(8,128)S(1)}, u32[]{:S(2)}, u32[]{:S(2)}) collective-permute-start(f32[264,256]{1,0:T(8,128)S(1)} %collective-permute-done.10.refs_10_.refs_9_.refs_2_), channel_id=1, source_target_pairs={{0,1},{1,0},{2,3},{3,2},{4,5},{5,4},{6,7},{7,6},{8,9},{9,8},{10,11... | collective-permute-start | bytes 811016 | tf_op jit(solution)/shard_map/ppermute | solution.py:321
  35.5 9.7 %collective-permute-start.14 = (f32[264,256]{1,0:T(8,128)S(1)}, f32[264,256]{1,0:T(8,128)S(1)}, u32[]{:S(2)}, u32[]{:S(2)}) collective-permute-start(f32[264,256]{1,0:T(8,128)S(1)} %first.1), channel_id=1, source_target_pairs={{0,16},{2,18},{4,20},{6,22},{16,24},{18,26},{20,28},{22,30},{24,8}... | collective-permute-start | bytes 811016 | tf_op jit(solution)/shard_map/ppermute | solution.py:325
  40.1 12.6 %collective-permute-start.16 = (f32[264,256]{1,0:T(8,128)S(1)}, f32[264,256]{1,0:T(8,128)S(1)}, u32[]{:S(2)}, u32[]{:S(2)}) collective-permute-start(f32[264,256]{1,0:T(8,128)S(1)} %rest.3), channel_id=1, source_target_pairs={{0,8},{2,10},{4,12},{6,14},{16,0},{18,2},{20,4},{22,6},{24,16},{26... | collective-permute-start | bytes 811016 | tf_op jit(solution)/shard_map/ppermute | solution.py:325
  45.2 12.4 %collective-permute-start.15 = (f32[264,256]{1,0:T(8,128)S(1)}, f32[264,256]{1,0:T(8,128)S(1)}, u32[]{:S(2)}, u32[]{:S(2)}) collective-permute-start(f32[264,256]{1,0:T(8,128)S(1)} %add.3), channel_id=1, source_target_pairs={{0,16},{2,18},{4,20},{6,22},{16,24},{18,26},{20,28},{22,30},{24,8}... | collective-permute-start | bytes 811016 | tf_op jit(solution)/shard_map/ppermute | solution.py:325
  58.4 8.4 %collective-permute-start.17 = (f32[264,256]{1,0:T(8,128)S(1)}, f32[264,256]{1,0:T(8,128)S(1)}, u32[]{:S(2)}, u32[]{:S(2)}) collective-permute-start(f32[264,256]{1,0:T(8,128)S(1)} %finish.1.refs_0_), channel_id=1, source_target_pairs={{0,16},{2,18},{4,20},{6,22},{16,24},{18,26},{20,28},{22,30},{24,8}... | collective-permute-start | bytes 811016 | tf_op jit(solution)/shard_map/ppermute | solution.py:325
  60.1 8.6 %collective-permute-start.20 = (f32[264,256]{1,0:T(8,128)S(1)}, f32[264,256]{1,0:T(8,128)S(1)}, u32[]{:S(2)}, u32[]{:S(2)}) collective-permute-start(f32[264,256]{1,0:T(8,128)S(1)} %finish.1.refs_0_), channel_id=1, source_target_pairs={{0,4},{1,3},{2,6},{3,1},{4,0},{5,7},{6,2},{7,5},{8,12},{9,11},{10,... | collective-permute-start | bytes 811016 | tf_op jit(solution)/shard_map/ppermute | solution.py:318
  61.2 10.0 %collective-permute-start.23 = (f32[264,256]{1,0:T(8,128)S(1)}, f32[264,256]{1,0:T(8,128)S(1)}, u32[]{:S(2)}, u32[]{:S(2)}) collective-permute-start(f32[264,256]{1,0:T(8,128)S(1)} %finish.1.refs_0_), channel_id=1, source_target_pairs={{0,2},{1,5},{2,0},{3,7},{4,6},{5,1},{6,4},{7,3},{8,10},{9,13},{10,... | collective-permute-start | bytes 811016 | tf_op jit(solution)/shard_map/ppermute | solution.py:318
  66.8 7.5 %collective-permute-start.18 = (f32[264,256]{1,0:T(8,128)S(1)}, f32[264,256]{1,0:T(8,128)S(1)}, u32[]{:S(2)}, u32[]{:S(2)}) collective-permute-start(f32[264,256]{1,0:T(8,128)S(1)} %collective-permute-done.17.refs_4_), channel_id=1, source_target_pairs={{0,16},{2,18},{4,20},{6,22},{16,24},{18,26},{20,28},{22,30},{24,8}... | collective-permute-start | bytes 811016 | tf_op jit(solution)/shard_map/ppermute | solution.py:325
  68.7 7.8 %collective-permute-start.21 = (f32[264,256]{1,0:T(8,128)S(1)}, f32[264,256]{1,0:T(8,128)S(1)}, u32[]{:S(2)}, u32[]{:S(2)}) collective-permute-start(f32[264,256]{1,0:T(8,128)S(1)} %collective-permute-done.17.refs_4_), channel_id=1, source_target_pairs={{0,4},{1,3},{2,6},{3,1},{4,0},{5,7},{6,2},{7,5},{8,12},{9,11},{10,... | collective-permute-start | bytes 811016 | tf_op jit(solution)/shard_map/ppermute | solution.py:318
  69.8 9.2 %collective-permute-start.30 = (f32[264,256]{1,0:T(8,128)S(1)}, f32[264,256]{1,0:T(8,128)S(1)}, u32[]{:S(2)}, u32[]{:S(2)}) collective-permute-start(f32[264,256]{1,0:T(8,128)S(1)} %collective-permute-done.17.refs_4_), channel_id=1, source_target_pairs={{0,2},{1,5},{2,0},{3,7},{4,6},{5,1},{6,4},{7,3},{8,10},{9,13},{10,... | collective-permute-start | bytes 811016 | tf_op jit(solution)/shard_map/ppermute | solution.py:318
  71.3 10.3 %collective-permute-start.24 = (f32[264,256]{1,0:T(8,128)S(1)}, f32[264,256]{1,0:T(8,128)S(1)}, u32[]{:S(2)}, u32[]{:S(2)}) collective-permute-start(f32[264,256]{1,0:T(8,128)S(1)} %collective-permute-done.23.refs_1_), channel_id=1, source_target_pairs={{0,4},{1,3},{2,6},{3,1},{4,0},{5,7},{6,2},{7,5},{8,12},{9,11},{10,... | collective-permute-start | bytes 811016 | tf_op jit(solution)/shard_map/ppermute | solution.py:318
  74.2 7.5 %collective-permute-start.19 = (f32[264,256]{1,0:T(8,128)S(1)}, f32[264,256]{1,0:T(8,128)S(1)}, u32[]{:S(2)}, u32[]{:S(2)}) collective-permute-start(f32[264,256]{1,0:T(8,128)S(1)} %finish.1.refs_0_), channel_id=1, source_target_pairs={{0,8},{2,10},{4,12},{6,14},{16,0},{18,2},{20,4},{22,6},{24,16},{26... | collective-permute-start | bytes 811016 | tf_op jit(solution)/shard_map/ppermute | solution.py:325
  76.4 9.4 %collective-permute-start.28 = (f32[264,256]{1,0:T(8,128)S(1)}, f32[264,256]{1,0:T(8,128)S(1)}, u32[]{:S(2)}, u32[]{:S(2)}) collective-permute-start(f32[264,256]{1,0:T(8,128)S(1)} %collective-permute-done.18.refs_8_), channel_id=1, source_target_pairs={{0,2},{1,5},{2,0},{3,7},{4,6},{5,1},{6,4},{7,3},{8,10},{9,13},{10,... | collective-permute-start | bytes 811016 | tf_op jit(solution)/shard_map/ppermute | solution.py:318
  77.9 9.1 %collective-permute-start.22 = (f32[264,256]{1,0:T(8,128)S(1)}, f32[264,256]{1,0:T(8,128)S(1)}, u32[]{:S(2)}, u32[]{:S(2)}) collective-permute-start(f32[264,256]{1,0:T(8,128)S(1)} %collective-permute-done.18.refs_8_), channel_id=1, source_target_pairs={{0,4},{1,3},{2,6},{3,1},{4,0},{5,7},{6,2},{7,5},{8,12},{9,11},{10,... | collective-permute-start | bytes 811016 | tf_op jit(solution)/shard_map/ppermute | solution.py:318
  79.0 11.1 %collective-permute-start.31 = (f32[264,256]{1,0:T(8,128)S(1)}, f32[264,256]{1,0:T(8,128)S(1)}, u32[]{:S(2)}, u32[]{:S(2)}) collective-permute-start(f32[264,256]{1,0:T(8,128)S(1)} %collective-permute-done.30.refs_5_), channel_id=1, source_target_pairs={{0,4},{1,3},{2,6},{3,1},{4,0},{5,7},{6,2},{7,5},{8,12},{9,11},{10,... | collective-permute-start | bytes 811016 | tf_op jit(solution)/shard_map/ppermute | solution.py:318
  81.7 13.5 %collective-permute-start.27 = (f32[264,256]{1,0:T(8,128)S(1)}, f32[264,256]{1,0:T(8,128)S(1)}, u32[]{:S(2)}, u32[]{:S(2)}) collective-permute-start(f32[264,256]{1,0:T(8,128)S(1)} %collective-permute-done.24.refs_3_), channel_id=1, source_target_pairs={{0,8},{2,10},{4,12},{6,14},{16,0},{18,2},{20,4},{22,6},{24,16},{26... | collective-permute-start | bytes 811016 | tf_op jit(solution)/shard_map/ppermute | solution.py:325
  85.8 7.8 %collective-permute-start.29 = (f32[264,256]{1,0:T(8,128)S(1)}, f32[264,256]{1,0:T(8,128)S(1)}, u32[]{:S(2)}, u32[]{:S(2)}) collective-permute-start(f32[264,256]{1,0:T(8,128)S(1)} %collective-permute-done.28.refs_0_), channel_id=1, source_target_pairs={{0,4},{1,3},{2,6},{3,1},{4,0},{5,7},{6,2},{7,5},{8,12},{9,11},{10,... | collective-permute-start | bytes 811016 | tf_op jit(solution)/shard_map/ppermute | solution.py:318
  87.0 8.4 %collective-permute-start.25 = (f32[264,256]{1,0:T(8,128)S(1)}, f32[264,256]{1,0:T(8,128)S(1)}, u32[]{:S(2)}, u32[]{:S(2)}) collective-permute-start(f32[264,256]{1,0:T(8,128)S(1)} %collective-permute-done.19.refs_3_), channel_id=1, source_target_pairs={{0,2},{1,5},{2,0},{3,7},{4,6},{5,1},{6,4},{7,3},{8,10},{9,13},{10,... | collective-permute-start | bytes 811016 | tf_op jit(solution)/shard_map/ppermute | solution.py:318
  88.5 8.1 %collective-permute-start.26 = (f32[264,256]{1,0:T(8,128)S(1)}, f32[264,256]{1,0:T(8,128)S(1)}, u32[]{:S(2)}, u32[]{:S(2)}) collective-permute-start(f32[264,256]{1,0:T(8,128)S(1)} %collective-permute-done.19.refs_3_), channel_id=1, source_target_pairs={{0,4},{1,3},{2,6},{3,1},{4,0},{5,7},{6,2},{7,5},{8,12},{9,11},{10,... | collective-permute-start | bytes 811016 | tf_op jit(solution)/shard_map/ppermute | solution.py:318

commit v12 on v10

--- a/solution.py
+++ b/solution.py
@@ -152,8 +152,11 @@
             cnt_ref[...] += counted
 
 
+KINDS = ((0, 0), (1, 1), (0, 1), (1, 0))
+
+
 def near_rows(cores, half, core, refs, d0_ref, d1_ref):
-    for k, (kind, part) in enumerate(((0, 0), (1, 1), (0, 1), (1, 0))):
+    for k, (kind, part) in enumerate(KINDS):
         for rc in range(cores):
             at = half + 2 * (core ^ rc) + part
             tail_ref = d1_ref if (kind + rc) % 2 == 0 else d0_ref
@@ -344,6 +347,8 @@
     )
     d0, d1 = exchange(pack_a, 1), exchange(pack_b, 0)
 
+    a0, b1, a1, b0, lse = lax.optimization_barrier((a0, b1, a1, b0, lse))
+    near = with_siblings((a0, b1, a1, b0))
     lanes = min(LANES, half)
     acc, cnt = call(
         functools.partial(own_kernel, cores),
@@ -353,10 +358,9 @@
         "own",
         flops=4 * share * width * rows,
     )
-    a0, b1, a1, b0, lse = lax.optimization_barrier((a0, b1, a1, b0, lse))
-    near = with_siblings((a0, b1, a1, b0))
-    lse_d = exchange(d1[half : half + 2 * cores, :half], 1)
-    near, d0, d1, acc, cnt = lax.optimization_barrier((near, d0, d1, acc, cnt))
+    lse, acc, cnt, near = lax.optimization_barrier((lse, acc, cnt, near))
+    lse_d = lax.ppermute(lse, "dp", [(i, i ^ 3) for i in range(n)])
+    near, d0, d1, acc, cnt, lse_d = lax.optimization_barrier((near, d0, d1, acc, cnt, lse_d))
     lead = call(
         functools.partial(lead_kernel, cores, order, half),
         (f32(size, width), f32(size, lanes)),
@@ -378,7 +382,7 @@
         [SMEM] + [VMEM] * (5 + 2 * cores),
         (where, twice, norm, lse_d, *lead, *far),
         "first",
-        flops=4 * size * width * rows,
+        flops=4 * size * width * 2 * rows,
     )
 
     def sums_of(steps):
@@ -412,7 +416,7 @@
 
     steps = [-s for s in range(1, lines // 2 + 1)] + list(range(1, lines // 2))
     got = {(0, 0): done}
-    previous, older = (), ()
+    previous, older, plane_b = (), (done, done), [done]
     for s in [0] + steps:
         x = got[0, s]
         if previous:
@@ -421,7 +425,8 @@
         if s == steps[-1]:
             break
         got[3, s] = exchange(got[1, s], 1)
-        previous, older = (got[2, s], *older), (got[3, s],)
+        plane_b.append(got[2, s])
+        previous, older = (plane_b[-2 if s == steps[-2] else -1], *older[:1]), (*older[1:], got[3, s])
         ahead_of = steps[([0] + steps).index(s)]
         x = got[0, ahead_of + (1 if ahead_of < 0 else -1)]
         if ahead_of > 0:

time: 99 us -> 95.7 us (0.967)
  starting transfers between devices: 35.7 us -> 33.8 us
  waiting for transfers between devices: 36.1 us -> 34.6 us
    ppermute x18 -> x17, waiting for transfers between devices: 21.7 us -> 9.47 us  [exchange(): return lax.ppermute(x, ('dp', 'cent'), pairs)]
    ppermute x7, waiting for transfers between devices: 13 us -> 19.5 us  [ring(): lax.ppermute(x, 'dp', [(4 * a + i, 4 * b + i) for a, b in pairs for i in...]
    ppermute x0 -> x1, waiting for transfers between devices: none -> 4.31 us  [body(): lse_d = lax.ppermute(lse, 'dp', [(i, i ^ 3) for i in range(n)])]
    ppermute x18 -> x17, starting transfers between devices: 19 us -> 17.4 us  [exchange(): return lax.ppermute(x, ('dp', 'cent'), pairs)]
    ppermute x7, starting transfers between devices: 15.1 us -> 13.6 us  [ring(): lax.ppermute(x, 'dp', [(4 * a + i, 4 * b + i) for a, b in pairs for i in...]
    ppermute x0 -> x1, starting transfers between devices: none -> 1.08 us  [body(): lse_d = lax.ppermute(lse, 'dp', [(i, i ^ 3) for i in range(n)])]
  transfers between devices with their start and end apart: 32 -> 32, of which waited for: 19 -> 15; matrix products, arithmetic and copies ran while one was open for 0% -> 0% of each run, Pallas kernels for 19% -> 20%
where the time goes in v12:
time: 95.7 us; the launch traced here: 95.5 us
  waiting for transfers between devices  34.6 us (36%)
  starting transfers between devices  33.8 us (35%)
  Pallas kernels  23.3 us (24%)
  local copies, waits for them, and re-layouts  2.64 us (3%)
  between operations  0.98 us (1%)
    pallas_call x13, Pallas kernels, call(): pl.pallas_call(kernel, out_shape=out_shape, in_specs=in_specs, out_specs=...  23.3 us
    ppermute x7, waiting for transfers between devices, ring(): lax.ppermute(x, 'dp', [(4 * a + i, 4 * b + i) for a, b in pairs for i in...  19.5 us
    ppermute x17, starting transfers between devices, exchange(): return lax.ppermute(x, ('dp', 'cent'), pairs)  17.4 us
    ppermute x7, starting transfers between devices, ring(): lax.ppermute(x, 'dp', [(4 * a + i, 4 * b + i) for a, b in pairs for i in...  13.6 us
    ppermute x17, waiting for transfers between devices, exchange(): return lax.ppermute(x, ('dp', 'cent'), pairs)  9.47 us
    ppermute x1, waiting for transfers between devices, body(): lse_d = lax.ppermute(lse, 'dp', [(i, i ^ 3) for i in range(n)])  4.31 us
    unnamed x8, local copies, waits for them, and re-layouts  2.64 us
  transfers between devices with their start and end apart: 32, of which 15 were waited for; matrix products, arithmetic and copies ran while one was open for 0% of the time, Pallas kernels for 20%

profile of v12, /device:TPU:0, one launch (start us, length us, event | category | flops | bytes accessed | tf_op | source)
XLA Modules:
  0.0 95.5 jit_solution(16582045425504697094)
XLA Ops:
  0.7 1.0 %copy-done.1 = bf16[1024,256]{1,0:T(8,128)(2,1)S(1)} copy-done((bf16[1024,256]{1,0:T(8,128)(2,1)S(1)}, bf16[1024,256]{1,0:T(8,128)(2,1)}, u32[]{:S(2)}) %copy-start.1) | copy-done | bytes 524312
  1.8 0.6 open.1
  2.4 3.0 %collective-permute-start.1 = (f32[256,256]{1,0:T(8,128)S(1)}, f32[256,256]{1,0:T(8,128)S(1)}, u32[]{:S(2)}, u32[]{:S(2)}) collective-permute-start(f32[256,256]{1,0:T(8,128)S(1)} %get-tuple-element.61), channel_id=1, source_target_pairs={{0,4},{1,3},{2,6},{3,1},{4,0},{5,7},{6,2},{7,5},{8,12},{9,11},{10,... | collective-permute-start | bytes 786440 | tf_op jit(solution)/shard_map/ppermute | solution.py:315
  5.4 1.5 %collective-permute-start.2 = (f32[256,256]{1,0:T(8,128)S(1)}, f32[256,256]{1,0:T(8,128)S(1)}, u32[]{:S(2)}, u32[]{:S(2)}) collective-permute-start(f32[256,256]{1,0:T(8,128)S(1)} %get-tuple-element.61), channel_id=1, source_target_pairs={{0,2},{1,5},{2,0},{3,7},{4,6},{5,1},{6,4},{7,3},{8,10},{9,13},{10,... | collective-permute-start | bytes 786440 | tf_op jit(solution)/shard_map/ppermute | solution.py:315
  7.5 1.6 %copy-done.3 = bf16[4096,256]{1,0:T(8,128)(2,1)S(1)} copy-done((bf16[4096,256]{1,0:T(8,128)(2,1)S(1)}, bf16[4096,256]{1,0:T(8,128)(2,1)}, u32[]{:S(2)}) %copy-start.3) | copy-done | bytes 2097176
  9.1 5.9 %stats.1 = (f32[2,1024]{1,0:T(2,128)S(1)}, bf16[1024,256]{1,0:T(8,128)(2,1)S(1)}, f32[1024,128]{1,0:T(8,128)S(1)}) custom-call(s32[2]{0:T(128)S(1)} %pad_add_fusion.where_ref, bf16[1024,256]{1,0:T(8,128)(2,1)S(1)} %copy-done.1, bf16[4096,256]{1,0:T(8,128)(2,1)S(1)} %copy-done.3), custom_call_target="tpu_custom_call" | custom-call | flops 4294967296 | bytes 2621448 | tf_op jit(solution)/shard_map/stats/pallas_call | solution.py:27
  15.1 1.2 %collective-permute-done.4.refs_1_ = f32[2,1024]{1,0:T(2,128)S(1)} collective-permute-done((f32[2,1024]{1,0:T(2,128)S(1)}, f32[2,1024]{1,0:T(2,128)S(1)}, u32[]{:S(2)}, u32[]{:S(2)}) %collective-permute-start.4) | collective-permute-done | bytes 8224 | tf_op jit(solution)/shard_map/ppermute | solution.py:318
  16.3 1.1 %collective-permute-done.a0_ref.refs_0_ = f32[256,256]{1,0:T(8,128)S(1)} collective-permute-done((f32[256,256]{1,0:T(8,128)S(1)}, f32[256,256]{1,0:T(8,128)S(1)}, u32[]{:S(2)}, u32[]{:S(2)}) %collective-permute-start) | collective-permute-done | bytes 262176 | tf_op jit(solution)/shard_map/ppermute | solution.py:315
  17.4 0.6 lse.1
  18.0 0.6 collective-permute-start.5
  18.6 1.1 %collective-permute-start.10 = (f32[264,256]{1,0:T(8,128)S(1)}, f32[264,256]{1,0:T(8,128)S(1)}, u32[]{:S(2)}, u32[]{:S(2)}) collective-permute-start(f32[264,256]{1,0:T(8,128)S(1)} %get-tuple-element.80), channel_id=1, source_target_pairs={{0,2},{1,5},{2,0},{3,7},{4,6},{5,1},{6,4},{7,3},{8,10},{9,13},{10,... | collective-permute-start | bytes 811016 | tf_op jit(solution)/shard_map/ppermute | solution.py:315
  19.8 1.5 %collective-permute-start.9 = (f32[264,256]{1,0:T(8,128)S(1)}, f32[264,256]{1,0:T(8,128)S(1)}, u32[]{:S(2)}, u32[]{:S(2)}) collective-permute-start(f32[264,256]{1,0:T(8,128)S(1)} %get-tuple-element.79), channel_id=1, source_target_pairs={{0,4},{1,3},{2,6},{3,1},{4,0},{5,7},{6,2},{7,5},{8,12},{9,11},{10,... | collective-permute-start | bytes 811016 | tf_op jit(solution)/shard_map/ppermute | solution.py:315
  21.8 1.6 %own.1 = (f32[1024,256]{1,0:T(8,128)S(1)}, f32[1024,128]{1,0:T(8,128)S(1)}) custom-call(bf16[1024,256]{1,0:T(8,128)(2,1)S(1)} %copy-done.2, bf16[1024,256]{1,0:T(8,128)(2,1)S(1)} %get-tuple-element.58.twice_ref, f32[1024,128]{1,0:T(8,128)S(1)} %get-tuple-element.59.norm_ref, f32[4,256]{1,0:T(4,128)S(1)} %get-tuple-element.83.lse_ref), custom_call_target="tpu_custom_call" | custom-call | flops 1073741824 | bytes 1576960 | tf_op jit(solution)/shard_map/own/pallas_call | solution.py:27
  23.6 1.1 %collective-permute-start.11 = (f32[4,256]{1,0:T(4,128)S(1)}, f32[4,256]{1,0:T(4,128)S(1)}, u32[]{:S(2)}, u32[]{:S(2)}) collective-permute-start(f32[4,256]{1,0:T(4,128)S(1)} %get-tuple-element.83.lse_ref), channel_id=1, source_target_pairs={{0,6},{2,4},{4,2},{6,0},{8,14},{10,12},{12,10},{14,8},{16,22},{18,... | collective-permute-start | bytes 12296 | tf_op jit(solution)/shard_map/ppermute | solution.py:362
  24.6 4.3 %collective-permute-done.11.lse_ref = f32[4,256]{1,0:T(4,128)S(1)} collective-permute-done((f32[4,256]{1,0:T(4,128)S(1)}, f32[4,256]{1,0:T(4,128)S(1)}, u32[]{:S(2)}, u32[]{:S(2)}) %collective-permute-start.11) | collective-permute-done | bytes 4128 | tf_op jit(solution)/shard_map/ppermute | solution.py:362
  29.5 1.5 %lead.1 = (f32[256,256]{1,0:T(8,128)S(1)}, f32[256,128]{1,0:T(8,128)S(1)}) custom-call(s32[2]{0:T(128)S(1)} %pad_add_fusion.where_ref, bf16[1024,256]{1,0:T(8,128)(2,1)S(1)} %get-tuple-element.58.twice_ref, f32[1024,128]{1,0:T(8,128)S(1)} %get-tuple-element.59.norm_ref, f32[1024,256]{1,0:T(8,128)S(1)} %get-tuple-element.84.acc_ref, ...), custom_call_target="tpu_custom_call" | custom-call | flops 536870912 | bytes 5259272 | tf_op jit(solution)/shard_map/lead/pallas_call | solution.py:27
  31.0 1.2 %first.1 = f32[264,256]{1,0:T(8,128)S(1)} custom-call(s32[2]{0:T(128)S(1)} %pad_add_fusion.where_ref, bf16[1024,256]{1,0:T(8,128)(2,1)S(1)} %get-tuple-element.58.twice_ref, f32[1024,128]{1,0:T(8,128)S(1)} %get-tuple-element.59.norm_ref, f32[4,256]{1,0:T(4,128)S(1)} %collective-permute-done.11.lse_ref, f32[256,256]{1,0:T(8,128)S(1)} %get-tuple-element.99.lead_acc_ref, ...), custom_call_target="tpu_custom_call" | custom-call | flops 536870912 | bytes 2527240 | tf_op jit(solution)/shard_map/first/pallas_call | solution.py:27
  32.2 2.8 %collective-permute-start.14 = (f32[264,256]{1,0:T(8,128)S(1)}, f32[264,256]{1,0:T(8,128)S(1)}, u32[]{:S(2)}, u32[]{:S(2)}) collective-permute-start(f32[264,256]{1,0:T(8,128)S(1)} %first.1), channel_id=1, source_target_pairs={{0,16},{2,18},{4,20},{6,22},{16,24},{18,26},{20,28},{22,30},{24,8}... | collective-permute-start | bytes 811016 | tf_op jit(solution)/shard_map/ppermute | solution.py:322
  35.0 1.9 %rest.3 = f32[264,256]{1,0:T(8,128)S(1)} custom-call(s32[2]{0:T(128)S(1)} %pad_add_fusion.where_ref, bf16[1024,256]{1,0:T(8,128)(2,1)S(1)} %get-tuple-element.58.twice_ref, f32[1024,128]{1,0:T(8,128)S(1)} %get-tuple-element.59.norm_ref, f32[1024,256]{1,0:T(8,128)S(1)} %get-tuple-element.84.acc_ref, f32[1024,128]{1,0:T(8,128)S(1)} %get-tuple-element.85.cnt_ref, ...), custom_call_target="tpu_custom_call" | custom-call | flops 805306368 | bytes 5804040 | tf_op jit(solution)/shard_map/rest/pallas_call | solution.py:27
  37.1 3.5 %rest.2 = (f32[264,256]{1,0:T(8,128)S(1)}, f32[264,256]{1,0:T(8,128)S(1)}) custom-call(s32[2]{0:T(128)S(1)} %pad_add_fusion.where_ref, bf16[1024,256]{1,0:T(8,128)(2,1)S(1)} %get-tuple-element.58.twice_ref, f32[1024,128]{1,0:T(8,128)S(1)} %get-tuple-element.59.norm_ref, f32[1024,256]{1,0:T(8,128)} %copy-done, f32[1024,128]{1,0:T(8,128)S(1)} %get-tuple-element.85.cnt_ref, ...), custom_call_target="tpu_custom_call" | custom-call | flops 1610612736 | bytes 5804040 | tf_op jit(solution)/shard_map/rest/pallas_call | solution.py:27
  40.7 1.2 %collective-permute-done.14.b_ref = f32[264,256]{1,0:T(8,128)S(1)} collective-permute-done((f32[264,256]{1,0:T(8,128)S(1)}, f32[264,256]{1,0:T(8,128)S(1)}, u32[]{:S(2)}, u32[]{:S(2)}) %collective-permute-start.14) | collective-permute-done | bytes 270368 | tf_op jit(solution)/shard_map/ppermute | solution.py:322
  41.9 3.4 %collective-permute-start.15 = (f32[264,256]{1,0:T(8,128)S(1)}, f32[264,256]{1,0:T(8,128)S(1)}, u32[]{:S(2)}, u32[]{:S(2)}) collective-permute-start(f32[264,256]{1,0:T(8,128)S(1)} %add.3), channel_id=1, source_target_pairs={{0,16},{2,18},{4,20},{6,22},{16,24},{18,26},{20,28},{22,30},{24,8}... | collective-permute-start | bytes 811016 | tf_op jit(solution)/shard_map/ppermute | solution.py:322
  45.4 4.1 %collective-permute-done.16.second_ref = f32[264,256]{1,0:T(8,128)S(1)} collective-permute-done((f32[264,256]{1,0:T(8,128)S(1)}, f32[264,256]{1,0:T(8,128)S(1)}, u32[]{:S(2)}, u32[]{:S(2)}) %collective-permute-start.16) | collective-permute-done | bytes 270368 | tf_op jit(solution)/shard_map/ppermute | solution.py:322
  49.5 4.8 %collective-permute-done.15.first_ref = f32[264,256]{1,0:T(8,128)S(1)} collective-permute-done((f32[264,256]{1,0:T(8,128)S(1)}, f32[264,256]{1,0:T(8,128)S(1)}, u32[]{:S(2)}, u32[]{:S(2)}) %collective-permute-start.15) | collective-permute-done | bytes 270368 | tf_op jit(solution)/shard_map/ppermute | solution.py:322
  54.3 0.8 finish.1.refs_0_
  55.1 1.7 %collective-permute-start.17 = (f32[264,256]{1,0:T(8,128)S(1)}, f32[264,256]{1,0:T(8,128)S(1)}, u32[]{:S(2)}, u32[]{:S(2)}) collective-permute-start(f32[264,256]{1,0:T(8,128)S(1)} %finish.1.refs_0_), channel_id=1, source_target_pairs={{0,16},{2,18},{4,20},{6,22},{16,24},{18,26},{20,28},{22,30},{24,8}... | collective-permute-start | bytes 811016 | tf_op jit(solution)/shard_map/ppermute | solution.py:322
  56.9 0.9 collective-permute-start.20
  58.2 5.3 %collective-permute-done.17.refs_4_ = f32[264,256]{1,0:T(8,128)S(1)} collective-permute-done((f32[264,256]{1,0:T(8,128)S(1)}, f32[264,256]{1,0:T(8,128)S(1)}, u32[]{:S(2)}, u32[]{:S(2)}) %collective-permute-start.17) | collective-permute-done | bytes 270368 | tf_op jit(solution)/shard_map/ppermute | solution.py:322
  63.5 1.9 %collective-permute-start.18 = (f32[264,256]{1,0:T(8,128)S(1)}, f32[264,256]{1,0:T(8,128)S(1)}, u32[]{:S(2)}, u32[]{:S(2)}) collective-permute-start(f32[264,256]{1,0:T(8,128)S(1)} %collective-permute-done.17.refs_4_), channel_id=1, source_target_pairs={{0,16},{2,18},{4,20},{6,22},{16,24},{18,26},{20,28},{22,30},{24,8}... | collective-permute-start | bytes 811016 | tf_op jit(solution)/shard_map/ppermute | solution.py:322
  65.4 1.0 %collective-permute-start.21 = (f32[264,256]{1,0:T(8,128)S(1)}, f32[264,256]{1,0:T(8,128)S(1)}, u32[]{:S(2)}, u32[]{:S(2)}) collective-permute-start(f32[264,256]{1,0:T(8,128)S(1)} %collective-permute-done.17.refs_4_), channel_id=1, source_target_pairs={{0,4},{1,3},{2,6},{3,1},{4,0},{5,7},{6,2},{7,5},{8,12},{9,11},{10,... | collective-permute-start | bytes 811016 | tf_op jit(solution)/shard_map/ppermute | solution.py:315
  67.0 1.2 %collective-permute-start.23 = (f32[264,256]{1,0:T(8,128)S(1)}, f32[264,256]{1,0:T(8,128)S(1)}, u32[]{:S(2)}, u32[]{:S(2)}) collective-permute-start(f32[264,256]{1,0:T(8,128)S(1)} %collective-permute-done.22.refs_1_), channel_id=1, source_target_pairs={{0,4},{1,3},{2,6},{3,1},{4,0},{5,7},{6,2},{7,5},{8,12},{9,11},{10,... | collective-permute-start | bytes 811016 | tf_op jit(solution)/shard_map/ppermute | solution.py:315
  68.2 2.8 %collective-permute-done.18.refs_8_ = f32[264,256]{1,0:T(8,128)S(1)} collective-permute-done((f32[264,256]{1,0:T(8,128)S(1)}, f32[264,256]{1,0:T(8,128)S(1)}, u32[]{:S(2)}, u32[]{:S(2)}) %collective-permute-start.18) | collective-permute-done | bytes 270368 | tf_op jit(solution)/shard_map/ppermute | solution.py:322
  71.0 2.2 %collective-permute-start.19 = (f32[264,256]{1,0:T(8,128)S(1)}, f32[264,256]{1,0:T(8,128)S(1)}, u32[]{:S(2)}, u32[]{:S(2)}) collective-permute-start(f32[264,256]{1,0:T(8,128)S(1)} %finish.1.refs_0_), channel_id=1, source_target_pairs={{0,8},{2,10},{4,12},{6,14},{16,0},{18,2},{20,4},{22,6},{24,16},{26... | collective-permute-start | bytes 811016 | tf_op jit(solution)/shard_map/ppermute | solution.py:322
  73.2 0.8 collective-permute-start.27
  73.9 1.3 %collective-permute-done.30.refs_5_ = f32[264,256]{1,0:T(8,128)S(1)} collective-permute-done((f32[264,256]{1,0:T(8,128)S(1)}, f32[264,256]{1,0:T(8,128)S(1)}, u32[]{:S(2)}, u32[]{:S(2)}) %collective-permute-start.30) | collective-permute-done | bytes 270368 | tf_op jit(solution)/shard_map/ppermute | solution.py:315
  75.2 1.2 %collective-permute-start.31 = (f32[264,256]{1,0:T(8,128)S(1)}, f32[264,256]{1,0:T(8,128)S(1)}, u32[]{:S(2)}, u32[]{:S(2)}) collective-permute-start(f32[264,256]{1,0:T(8,128)S(1)} %collective-permute-done.30.refs_5_), channel_id=1, source_target_pairs={{0,4},{1,3},{2,6},{3,1},{4,0},{5,7},{6,2},{7,5},{8,12},{9,11},{10,... | collective-permute-start | bytes 811016 | tf_op jit(solution)/shard_map/ppermute | solution.py:315
  76.4 0.9 collective-permute-start.28
  77.2 1.2 %collective-permute-done.19.refs_3_ = f32[264,256]{1,0:T(8,128)S(1)} collective-permute-done((f32[264,256]{1,0:T(8,128)S(1)}, f32[264,256]{1,0:T(8,128)S(1)}, u32[]{:S(2)}, u32[]{:S(2)}) %collective-permute-start.19) | collective-permute-done | bytes 270368 | tf_op jit(solution)/shard_map/ppermute | solution.py:322
  78.4 1.4 %collective-permute-start.26 = (f32[264,256]{1,0:T(8,128)S(1)}, f32[264,256]{1,0:T(8,128)S(1)}, u32[]{:S(2)}, u32[]{:S(2)}) collective-permute-start(f32[264,256]{1,0:T(8,128)S(1)} %collective-permute-done.23.refs_3_), channel_id=1, source_target_pairs={{0,8},{2,10},{4,12},{6,14},{16,0},{18,2},{20,4},{22,6},{24,16},{26... | collective-permute-start | bytes 811016 | tf_op jit(solution)/shard_map/ppermute | solution.py:322
  79.8 2.8 %collective-permute-done.27.refs_0_ = f32[264,256]{1,0:T(8,128)S(1)} collective-permute-done((f32[264,256]{1,0:T(8,128)S(1)}, f32[264,256]{1,0:T(8,128)S(1)}, u32[]{:S(2)}, u32[]{:S(2)}) %collective-permute-start.27) | collective-permute-done | bytes 270368 | tf_op jit(solution)/shard_map/ppermute | solution.py:315
  82.6 0.9 collective-permute-start.29
  83.5 0.6 collective-permute-start.24
  84.1 1.3 %collective-permute-start.25 = (f32[264,256]{1,0:T(8,128)S(1)}, f32[264,256]{1,0:T(8,128)S(1)}, u32[]{:S(2)}, u32[]{:S(2)}) collective-permute-start(f32[264,256]{1,0:T(8,128)S(1)} %collective-permute-done.19.refs_3_), channel_id=1, source_target_pairs={{0,4},{1,3},{2,6},{3,1},{4,0},{5,7},{6,2},{7,5},{8,12},{9,11},{10,... | collective-permute-start | bytes 811016 | tf_op jit(solution)/shard_map/ppermute | solution.py:315
  85.4 2.0 %place_early.1 = (f32[4096,256]{1,0:T(8,128)}, f32[32,128]{1,0:T(8,128)S(1)}) custom-call(s32[2]{0:T(128)S(1)} %pad_add_fusion.where_ref, f32[264,256]{1,0:T(8,128)S(1)} %finish.1.refs_0_, f32[264,256]{1,0:T(8,128)S(1)} %collective-permute-done.22.refs_1_, f32[264,256]{1,0:T(8,128)S(1)} %collective-permute-done.20.refs_2_, ...), custom_call_target="tpu_custom_call" | custom-call | bytes 2433032 | tf_op jit(solution)/shard_map/place_early/pallas_call | solution.py:27
  87.4 2.9 %collective-permute-done.29.refs_2_ = f32[264,256]{1,0:T(8,128)S(1)} collective-permute-done((f32[264,256]{1,0:T(8,128)S(1)}, f32[264,256]{1,0:T(8,128)S(1)}, u32[]{:S(2)}, u32[]{:S(2)}) %collective-permute-start.29) | collective-permute-done | bytes 270368 | tf_op jit(solution)/shard_map/ppermute | solution.py:315
  90.3 1.5 %place_middle.1 = (f32[4096,256]{1,0:T(8,128)}, f32[32,128]{1,0:T(8,128)S(1)}) custom-call(s32[2]{0:T(128)S(1)} %pad_add_fusion.where_ref, f32[264,256]{1,0:T(8,128)S(1)} %collective-permute-done.27.refs_0_, f32[264,256]{1,0:T(8,128)S(1)} %collective-permute-done.28.refs_1_, ...), custom_call_target="tpu_custom_call", output_to_operand_aliasing={{0}: (6, {})} | custom-call | bytes 5292040 | tf_op jit(solution)/shard_map/place_middle/pallas_call | solution.py:27
  92.1 1.2 %collective-permute-done.25.refs_1_ = f32[264,256]{1,0:T(8,128)S(1)} collective-permute-done((f32[264,256]{1,0:T(8,128)S(1)}, f32[264,256]{1,0:T(8,128)S(1)}, u32[]{:S(2)}, u32[]{:S(2)}) %collective-permute-start.25) | collective-permute-done | bytes 270368 | tf_op jit(solution)/shard_map/ppermute | solution.py:315
  93.2 2.1 %place_late.1 = (f32[4096,256]{1,0:T(8,128)}, f32[32,128]{1,0:T(8,128)}) custom-call(s32[2]{0:T(128)S(1)} %pad_add_fusion.where_ref, f32[264,256]{1,0:T(8,128)S(1)} %collective-permute-done.24.refs_0_, f32[264,256]{1,0:T(8,128)S(1)} %collective-permute-done.25.refs_1_, ...), custom_call_target="tpu_custom_call", output_to_operand_aliasing={{0}: (5, {})} | custom-call | bytes 5021704 | tf_op jit(solution)/shard_map/place_late/pallas_call | solution.py:27
  (38 shorter events, 3.4 us)
Async XLA Ops:
  0.7 1.0 %copy-start.1 = (bf16[1024,256]{1,0:T(8,128)(2,1)S(1)}, bf16[1024,256]{1,0:T(8,128)(2,1)}, u32[]{:S(2)}) copy-start(bf16[1024,256]{1,0:T(8,128)(2,1)} %points_ref.5) | copy-start | bytes 1572868
  2.4 15.0 %collective-permute-start.1 = (f32[256,256]{1,0:T(8,128)S(1)}, f32[256,256]{1,0:T(8,128)S(1)}, u32[]{:S(2)}, u32[]{:S(2)}) collective-permute-start(f32[256,256]{1,0:T(8,128)S(1)} %get-tuple-element.61), channel_id=1, source_target_pairs={{0,4},{1,3},{2,6},{3,1},{4,0},{5,7},{6,2},{7,5},{8,12},{9,11},{10,... | collective-permute-start | bytes 786440 | tf_op jit(solution)/shard_map/ppermute | solution.py:315
  5.4 12.6 %collective-permute-start.2 = (f32[256,256]{1,0:T(8,128)S(1)}, f32[256,256]{1,0:T(8,128)S(1)}, u32[]{:S(2)}, u32[]{:S(2)}) collective-permute-start(f32[256,256]{1,0:T(8,128)S(1)} %get-tuple-element.61), channel_id=1, source_target_pairs={{0,2},{1,5},{2,0},{3,7},{4,6},{5,1},{6,4},{7,3},{8,10},{9,13},{10,... | collective-permute-start | bytes 786440 | tf_op jit(solution)/shard_map/ppermute | solution.py:315
  6.9 14.9 %copy-start.2 = (bf16[1024,256]{1,0:T(8,128)(2,1)S(1)}, bf16[1024,256]{1,0:T(8,128)(2,1)}, u32[]{:S(2)}) copy-start(bf16[1024,256]{1,0:T(8,128)(2,1)} %points_ref.5) | copy-start | bytes 1572868
  6.9 10.5 %collective-permute-start = (f32[256,256]{1,0:T(8,128)S(1)}, f32[256,256]{1,0:T(8,128)S(1)}, u32[]{:S(2)}, u32[]{:S(2)}) collective-permute-start(f32[256,256]{1,0:T(8,128)S(1)} %get-tuple-element.60), channel_id=1, source_target_pairs={{0,2},{1,5},{2,0},{3,7},{4,6},{5,1},{6,4},{7,3},{8,10},{9,13},{10,... | collective-permute-start | bytes 786440 | tf_op jit(solution)/shard_map/ppermute | solution.py:315
  7.4 10.6 %collective-permute-start.3 = (f32[256,256]{1,0:T(8,128)S(1)}, f32[256,256]{1,0:T(8,128)S(1)}, u32[]{:S(2)}, u32[]{:S(2)}) collective-permute-start(f32[256,256]{1,0:T(8,128)S(1)} %get-tuple-element.60), channel_id=1, source_target_pairs={{0,4},{1,3},{2,6},{3,1},{4,0},{5,7},{6,2},{7,5},{8,12},{9,11},{10,... | collective-permute-start | bytes 786440 | tf_op jit(solution)/shard_map/ppermute | solution.py:315
  7.5 1.6 %copy-start.3 = (bf16[4096,256]{1,0:T(8,128)(2,1)S(1)}, bf16[4096,256]{1,0:T(8,128)(2,1)}, u32[]{:S(2)}) copy-start(bf16[4096,256]{1,0:T(8,128)(2,1)} %c_ref.1) | copy-start | bytes 6291460
  15.0 1.2 %collective-permute-start.4 = (f32[2,1024]{1,0:T(2,128)S(1)}, f32[2,1024]{1,0:T(2,128)S(1)}, u32[]{:S(2)}, u32[]{:S(2)}) collective-permute-start(f32[2,1024]{1,0:T(2,128)S(1)} %get-tuple-element.62.refs_0_), channel_id=1, source_target_pairs={{0,1},{1,0},{2,3},{3,2},{4,5},{5,4},{6,7},{7,6},{8,9},{9,8},{10,11... | collective-permute-start | bytes 24584 | tf_op jit(solution)/shard_map/ppermute | solution.py:318
  18.0 3.8 %collective-permute-start.5 = (f32[256,256]{1,0:T(8,128)S(1)}, f32[256,256]{1,0:T(8,128)S(1)}, u32[]{:S(2)}, u32[]{:S(2)}) collective-permute-start(f32[256,256]{1,0:T(8,128)S(1)} %collective-permute-done.a0_ref.refs_0_), channel_id=1, source_target_pairs={{0,1},{1,0},{2,3},{3,2},{4,5},{5,4},{6,7},{7,6},{8,9},{9,8},{10,11... | collective-permute-start | bytes 786440 | tf_op jit(solution)/shard_map/ppermute | solution.py:318
  18.6 10.3 %collective-permute-start.10 = (f32[264,256]{1,0:T(8,128)S(1)}, f32[264,256]{1,0:T(8,128)S(1)}, u32[]{:S(2)}, u32[]{:S(2)}) collective-permute-start(f32[264,256]{1,0:T(8,128)S(1)} %get-tuple-element.80), channel_id=1, source_target_pairs={{0,2},{1,5},{2,0},{3,7},{4,6},{5,1},{6,4},{7,3},{8,10},{9,13},{10,... | collective-permute-start | bytes 811016 | tf_op jit(solution)/shard_map/ppermute | solution.py:315
  19.8 9.2 %collective-permute-start.9 = (f32[264,256]{1,0:T(8,128)S(1)}, f32[264,256]{1,0:T(8,128)S(1)}, u32[]{:S(2)}, u32[]{:S(2)}) collective-permute-start(f32[264,256]{1,0:T(8,128)S(1)} %get-tuple-element.79), channel_id=1, source_target_pairs={{0,4},{1,3},{2,6},{3,1},{4,0},{5,7},{6,2},{7,5},{8,12},{9,11},{10,... | collective-permute-start | bytes 811016 | tf_op jit(solution)/shard_map/ppermute | solution.py:315
  21.3 2.1 %collective-permute-start.6 = (f32[256,256]{1,0:T(8,128)S(1)}, f32[256,256]{1,0:T(8,128)S(1)}, u32[]{:S(2)}, u32[]{:S(2)}) collective-permute-start(f32[256,256]{1,0:T(8,128)S(1)} %collective-permute-done.1.b1_ref.refs_2_), channel_id=1, source_target_pairs={{0,1},{1,0},{2,3},{3,2},{4,5},{5,4},{6,7},{7,6},{8,9},{9,8},{10,11... | collective-permute-start | bytes 786440 | tf_op jit(solution)/shard_map/ppermute | solution.py:318
  21.3 2.1 %collective-permute-start.7 = (f32[256,256]{1,0:T(8,128)S(1)}, f32[256,256]{1,0:T(8,128)S(1)}, u32[]{:S(2)}, u32[]{:S(2)}) collective-permute-start(f32[256,256]{1,0:T(8,128)S(1)} %collective-permute-done.2.refs_4_), channel_id=1, source_target_pairs={{0,1},{1,0},{2,3},{3,2},{4,5},{5,4},{6,7},{7,6},{8,9},{9,8},{10,11... | collective-permute-start | bytes 786440 | tf_op jit(solution)/shard_map/ppermute | solution.py:318
  21.8 1.8 %collective-permute-start.8 = (f32[256,256]{1,0:T(8,128)S(1)}, f32[256,256]{1,0:T(8,128)S(1)}, u32[]{:S(2)}, u32[]{:S(2)}) collective-permute-start(f32[256,256]{1,0:T(8,128)S(1)} %collective-permute-done.3.refs_6_), channel_id=1, source_target_pairs={{0,1},{1,0},{2,3},{3,2},{4,5},{5,4},{6,7},{7,6},{8,9},{9,8},{10,11... | collective-permute-start | bytes 786440 | tf_op jit(solution)/shard_map/ppermute | solution.py:318
  23.4 13.5 %copy-start = (f32[1024,256]{1,0:T(8,128)}, f32[1024,256]{1,0:T(8,128)S(1)}, u32[]{:S(2)}) copy-start(f32[1024,256]{1,0:T(8,128)S(1)} %get-tuple-element.84.acc_ref) | copy-start | bytes 3145732
  23.6 5.4 %collective-permute-start.11 = (f32[4,256]{1,0:T(4,128)S(1)}, f32[4,256]{1,0:T(4,128)S(1)}, u32[]{:S(2)}, u32[]{:S(2)}) collective-permute-start(f32[4,256]{1,0:T(4,128)S(1)} %get-tuple-element.83.lse_ref), channel_id=1, source_target_pairs={{0,6},{2,4},{4,2},{6,0},{8,14},{10,12},{12,10},{14,8},{16,22},{18,... | collective-permute-start | bytes 12296 | tf_op jit(solution)/shard_map/ppermute | solution.py:362
  29.0 2.0 %collective-permute-start.12 = (f32[264,256]{1,0:T(8,128)S(1)}, f32[264,256]{1,0:T(8,128)S(1)}, u32[]{:S(2)}, u32[]{:S(2)}) collective-permute-start(f32[264,256]{1,0:T(8,128)S(1)} %collective-permute-done.9.refs_8_.refs_0_), channel_id=1, source_target_pairs={{0,1},{1,0},{2,3},{3,2},{4,5},{5,4},{6,7},{7,6},{8,9},{9,8},{10,11... | collective-permute-start | bytes 811016 | tf_op jit(solution)/shard_map/ppermute | solution.py:318
  29.0 2.0 %collective-permute-start.13 = (f32[264,256]{1,0:T(8,128)S(1)}, f32[264,256]{1,0:T(8,128)S(1)}, u32[]{:S(2)}, u32[]{:S(2)}) collective-permute-start(f32[264,256]{1,0:T(8,128)S(1)} %collective-permute-done.10.refs_10_.refs_9_.refs_2_), channel_id=1, source_target_pairs={{0,1},{1,0},{2,3},{3,2},{4,5},{5,4},{6,7},{7,6},{8,9},{9,8},{10,11... | collective-permute-start | bytes 811016 | tf_op jit(solution)/shard_map/ppermute | solution.py:318
  32.2 9.7 %collective-permute-start.14 = (f32[264,256]{1,0:T(8,128)S(1)}, f32[264,256]{1,0:T(8,128)S(1)}, u32[]{:S(2)}, u32[]{:S(2)}) collective-permute-start(f32[264,256]{1,0:T(8,128)S(1)} %first.1), channel_id=1, source_target_pairs={{0,16},{2,18},{4,20},{6,22},{16,24},{18,26},{20,28},{22,30},{24,8}... | collective-permute-start | bytes 811016 | tf_op jit(solution)/shard_map/ppermute | solution.py:322
  36.9 12.6 %collective-permute-start.16 = (f32[264,256]{1,0:T(8,128)S(1)}, f32[264,256]{1,0:T(8,128)S(1)}, u32[]{:S(2)}, u32[]{:S(2)}) collective-permute-start(f32[264,256]{1,0:T(8,128)S(1)} %rest.3), channel_id=1, source_target_pairs={{0,8},{2,10},{4,12},{6,14},{16,0},{18,2},{20,4},{22,6},{24,16},{26... | collective-permute-start | bytes 811016 | tf_op jit(solution)/shard_map/ppermute | solution.py:322
  41.9 12.4 %collective-permute-start.15 = (f32[264,256]{1,0:T(8,128)S(1)}, f32[264,256]{1,0:T(8,128)S(1)}, u32[]{:S(2)}, u32[]{:S(2)}) collective-permute-start(f32[264,256]{1,0:T(8,128)S(1)} %add.3), channel_id=1, source_target_pairs={{0,16},{2,18},{4,20},{6,22},{16,24},{18,26},{20,28},{22,30},{24,8}... | collective-permute-start | bytes 811016 | tf_op jit(solution)/shard_map/ppermute | solution.py:322
  55.1 8.4 %collective-permute-start.17 = (f32[264,256]{1,0:T(8,128)S(1)}, f32[264,256]{1,0:T(8,128)S(1)}, u32[]{:S(2)}, u32[]{:S(2)}) collective-permute-start(f32[264,256]{1,0:T(8,128)S(1)} %finish.1.refs_0_), channel_id=1, source_target_pairs={{0,16},{2,18},{4,20},{6,22},{16,24},{18,26},{20,28},{22,30},{24,8}... | collective-permute-start | bytes 811016 | tf_op jit(solution)/shard_map/ppermute | solution.py:322
  56.9 8.5 %collective-permute-start.20 = (f32[264,256]{1,0:T(8,128)S(1)}, f32[264,256]{1,0:T(8,128)S(1)}, u32[]{:S(2)}, u32[]{:S(2)}) collective-permute-start(f32[264,256]{1,0:T(8,128)S(1)} %finish.1.refs_0_), channel_id=1, source_target_pairs={{0,4},{1,3},{2,6},{3,1},{4,0},{5,7},{6,2},{7,5},{8,12},{9,11},{10,... | collective-permute-start | bytes 811016 | tf_op jit(solution)/shard_map/ppermute | solution.py:315
  57.8 9.2 %collective-permute-start.22 = (f32[264,256]{1,0:T(8,128)S(1)}, f32[264,256]{1,0:T(8,128)S(1)}, u32[]{:S(2)}, u32[]{:S(2)}) collective-permute-start(f32[264,256]{1,0:T(8,128)S(1)} %finish.1.refs_0_), channel_id=1, source_target_pairs={{0,2},{1,5},{2,0},{3,7},{4,6},{5,1},{6,4},{7,3},{8,10},{9,13},{10,... | collective-permute-start | bytes 811016 | tf_op jit(solution)/shard_map/ppermute | solution.py:315
  63.5 7.5 %collective-permute-start.18 = (f32[264,256]{1,0:T(8,128)S(1)}, f32[264,256]{1,0:T(8,128)S(1)}, u32[]{:S(2)}, u32[]{:S(2)}) collective-permute-start(f32[264,256]{1,0:T(8,128)S(1)} %collective-permute-done.17.refs_4_), channel_id=1, source_target_pairs={{0,16},{2,18},{4,20},{6,22},{16,24},{18,26},{20,28},{22,30},{24,8}... | collective-permute-start | bytes 811016 | tf_op jit(solution)/shard_map/ppermute | solution.py:322
  65.4 7.8 %collective-permute-start.21 = (f32[264,256]{1,0:T(8,128)S(1)}, f32[264,256]{1,0:T(8,128)S(1)}, u32[]{:S(2)}, u32[]{:S(2)}) collective-permute-start(f32[264,256]{1,0:T(8,128)S(1)} %collective-permute-done.17.refs_4_), channel_id=1, source_target_pairs={{0,4},{1,3},{2,6},{3,1},{4,0},{5,7},{6,2},{7,5},{8,12},{9,11},{10,... | collective-permute-start | bytes 811016 | tf_op jit(solution)/shard_map/ppermute | solution.py:315
  66.4 8.8 %collective-permute-start.30 = (f32[264,256]{1,0:T(8,128)S(1)}, f32[264,256]{1,0:T(8,128)S(1)}, u32[]{:S(2)}, u32[]{:S(2)}) collective-permute-start(f32[264,256]{1,0:T(8,128)S(1)} %collective-permute-done.17.refs_4_), channel_id=1, source_target_pairs={{0,2},{1,5},{2,0},{3,7},{4,6},{5,1},{6,4},{7,3},{8,10},{9,13},{10,... | collective-permute-start | bytes 811016 | tf_op jit(solution)/shard_map/ppermute | solution.py:315
  67.0 10.2 %collective-permute-start.23 = (f32[264,256]{1,0:T(8,128)S(1)}, f32[264,256]{1,0:T(8,128)S(1)}, u32[]{:S(2)}, u32[]{:S(2)}) collective-permute-start(f32[264,256]{1,0:T(8,128)S(1)} %collective-permute-done.22.refs_1_), channel_id=1, source_target_pairs={{0,4},{1,3},{2,6},{3,1},{4,0},{5,7},{6,2},{7,5},{8,12},{9,11},{10,... | collective-permute-start | bytes 811016 | tf_op jit(solution)/shard_map/ppermute | solution.py:315
  71.0 7.5 %collective-permute-start.19 = (f32[264,256]{1,0:T(8,128)S(1)}, f32[264,256]{1,0:T(8,128)S(1)}, u32[]{:S(2)}, u32[]{:S(2)}) collective-permute-start(f32[264,256]{1,0:T(8,128)S(1)} %finish.1.refs_0_), channel_id=1, source_target_pairs={{0,8},{2,10},{4,12},{6,14},{16,0},{18,2},{20,4},{22,6},{24,16},{26... | collective-permute-start | bytes 811016 | tf_op jit(solution)/shard_map/ppermute | solution.py:322
  73.2 9.4 %collective-permute-start.27 = (f32[264,256]{1,0:T(8,128)S(1)}, f32[264,256]{1,0:T(8,128)S(1)}, u32[]{:S(2)}, u32[]{:S(2)}) collective-permute-start(f32[264,256]{1,0:T(8,128)S(1)} %collective-permute-done.18.refs_8_), channel_id=1, source_target_pairs={{0,2},{1,5},{2,0},{3,7},{4,6},{5,1},{6,4},{7,3},{8,10},{9,13},{10,... | collective-permute-start | bytes 811016 | tf_op jit(solution)/shard_map/ppermute | solution.py:315
  75.2 8.9 %collective-permute-start.31 = (f32[264,256]{1,0:T(8,128)S(1)}, f32[264,256]{1,0:T(8,128)S(1)}, u32[]{:S(2)}, u32[]{:S(2)}) collective-permute-start(f32[264,256]{1,0:T(8,128)S(1)} %collective-permute-done.30.refs_5_), channel_id=1, source_target_pairs={{0,4},{1,3},{2,6},{3,1},{4,0},{5,7},{6,2},{7,5},{8,12},{9,11},{10,... | collective-permute-start | bytes 811016 | tf_op jit(solution)/shard_map/ppermute | solution.py:315
  76.4 11.0 %collective-permute-start.28 = (f32[264,256]{1,0:T(8,128)S(1)}, f32[264,256]{1,0:T(8,128)S(1)}, u32[]{:S(2)}, u32[]{:S(2)}) collective-permute-start(f32[264,256]{1,0:T(8,128)S(1)} %collective-permute-done.18.refs_8_), channel_id=1, source_target_pairs={{0,4},{1,3},{2,6},{3,1},{4,0},{5,7},{6,2},{7,5},{8,12},{9,11},{10,... | collective-permute-start | bytes 811016 | tf_op jit(solution)/shard_map/ppermute | solution.py:315
  78.4 13.5 %collective-permute-start.26 = (f32[264,256]{1,0:T(8,128)S(1)}, f32[264,256]{1,0:T(8,128)S(1)}, u32[]{:S(2)}, u32[]{:S(2)}) collective-permute-start(f32[264,256]{1,0:T(8,128)S(1)} %collective-permute-done.23.refs_3_), channel_id=1, source_target_pairs={{0,8},{2,10},{4,12},{6,14},{16,0},{18,2},{20,4},{22,6},{24,16},{26... | collective-permute-start | bytes 811016 | tf_op jit(solution)/shard_map/ppermute | solution.py:322
  82.6 7.8 %collective-permute-start.29 = (f32[264,256]{1,0:T(8,128)S(1)}, f32[264,256]{1,0:T(8,128)S(1)}, u32[]{:S(2)}, u32[]{:S(2)}) collective-permute-start(f32[264,256]{1,0:T(8,128)S(1)} %collective-permute-done.27.refs_0_), channel_id=1, source_target_pairs={{0,4},{1,3},{2,6},{3,1},{4,0},{5,7},{6,2},{7,5},{8,12},{9,11},{10,... | collective-permute-start | bytes 811016 | tf_op jit(solution)/shard_map/ppermute | solution.py:315
  83.5 8.6 %collective-permute-start.24 = (f32[264,256]{1,0:T(8,128)S(1)}, f32[264,256]{1,0:T(8,128)S(1)}, u32[]{:S(2)}, u32[]{:S(2)}) collective-permute-start(f32[264,256]{1,0:T(8,128)S(1)} %collective-permute-done.19.refs_3_), channel_id=1, source_target_pairs={{0,2},{1,5},{2,0},{3,7},{4,6},{5,1},{6,4},{7,3},{8,10},{9,13},{10,... | collective-permute-start | bytes 811016 | tf_op jit(solution)/shard_map/ppermute | solution.py:315
  84.1 9.1 %collective-permute-start.25 = (f32[264,256]{1,0:T(8,128)S(1)}, f32[264,256]{1,0:T(8,128)S(1)}, u32[]{:S(2)}, u32[]{:S(2)}) collective-permute-start(f32[264,256]{1,0:T(8,128)S(1)} %collective-permute-done.19.refs_3_), channel_id=1, source_target_pairs={{0,4},{1,3},{2,6},{3,1},{4,0},{5,7},{6,2},{7,5},{8,12},{9,11},{10,... | collective-permute-start | bytes 811016 | tf_op jit(solution)/shard_map/ppermute | solution.py:315

commit v13 on v12

--- a/solution.py
+++ b/solution.py
@@ -9,7 +9,7 @@
 from jax.sharding import PartitionSpec as P
 
 prior_mass = 0.5
-VMEM_LIMIT = 48 * 1024 * 1024
+VMEM_LIMIT = 24 * 1024 * 1024
 LANES = 128
 NT = (((1,), (1,)), ((), ()))
 NN = (((1,), (0,)), ((), ()))
@@ -23,7 +23,7 @@
     return jax.ShapeDtypeStruct(shape, jnp.float32)
 
 
-def call(kernel, out_shape, in_specs, args, name, out_specs=None, scratch=(), flops=0, aliases={}):
+def call(kernel, out_shape, in_specs, args, name, out_specs=None, scratch=(), flops=0, aliases={}, vmem=VMEM_LIMIT):
     return pl.pallas_call(
         kernel,
         out_shape=out_shape,
@@ -31,7 +31,7 @@
         out_specs=jax.tree.map(lambda _: VMEM, out_shape) if out_specs is None else out_specs,
         scratch_shapes=list(scratch),
         input_output_aliases=aliases,
-        compiler_params=pltpu.CompilerParams(vmem_limit_bytes=VMEM_LIMIT),
+        compiler_params=pltpu.CompilerParams(vmem_limit_bytes=vmem),
         cost_estimate=pl.CostEstimate(
             flops=flops,
             bytes_accessed=sum(a.size * a.dtype.itemsize for a in args),
@@ -273,7 +273,7 @@
 def place_kernel(names, order, later, where_ref, *refs):
     count, lines = len(names), len(order)
     block_refs = refs[:count]
-    new_ref, counts_ref, sems = refs[-3:]
+    new_ref, counts_out_ref, counts_ref, sems = refs[-4:]
     size = block_refs[0].shape[0] - 8
     plane, line = lax.rem(where_ref[0], 4), lax.div(where_ref[0], 4)
     each = size // LANES
@@ -292,6 +292,8 @@
     for i in range(count):
         for k in range(each):
             counts_ref[pl.ds(places[i] * each + k, 1), :] = block_refs[i][size + k : size + k + 1, 0:LANES]
+    copies.append(pltpu.make_async_copy(counts_ref, counts_out_ref, sems.at[count]))
+    copies[-1].start()
     for copy in copies:
         copy.wait()
 
@@ -331,6 +333,7 @@
         (where, points),
         "open",
         scratch=[pltpu.VMEM((2 * half, width), points.dtype), pltpu.SemaphoreType.DMA(())],
+        vmem=62 * 1024 * 1024,
     )
     a0, b1 = exchange(first, 0), exchange(second, 1)
     a1, b0 = exchange(second, 0), exchange(first, 1)
@@ -416,27 +419,36 @@
 
     steps = [-s for s in range(1, lines // 2 + 1)] + list(range(1, lines // 2))
     got = {(0, 0): done}
-    previous, older, plane_b = (), (done, done), [done]
-    for s in [0] + steps:
-        x = got[0, s]
-        if previous:
-            x = lax.optimization_barrier((x, *previous))[0]
+
+    def after(x, *names):
+        return lax.optimization_barrier((x, *(got[k] for k in names)))[0]
+
+    def plane(s, *names):
+        x = after(got[0, s], *names) if names else got[0, s]
         got[1, s], got[2, s] = exchange(x, 0), exchange(x, 1)
-        if s == steps[-1]:
-            break
-        got[3, s] = exchange(got[1, s], 1)
-        plane_b.append(got[2, s])
-        previous, older = (plane_b[-2 if s == steps[-2] else -1], *older[:1]), (*older[1:], got[3, s])
-        ahead_of = steps[([0] + steps).index(s)]
-        x = got[0, ahead_of + (1 if ahead_of < 0 else -1)]
-        if ahead_of > 0:
-            x = lax.optimization_barrier((x, got[0, s]))[0]
-        got[0, ahead_of] = ring(x, 1 if ahead_of < 0 else -1)
-    before = got[3, steps[-1] - 1] if steps[-1] > 0 else got[3, steps[-1] + 1]
-    before = lax.optimization_barrier((before, got[0, steps[-1]]))[0]
-    got[3, steps[-1]] = ring(before, -1 if steps[-1] > 0 else 1)
-    late = [(1, steps[-1]), (2, steps[-1]), (3, steps[-1])]
-    middle = [(w, steps[-2]) for w in (1, 2, 3)] + [(0, steps[-1])]
+
+    got[0, -1] = ring(done, 1)
+    plane(0)
+    for s in steps[1:]:
+        if s < 0:
+            got[0, s] = ring(got[0, s + 1], 1)
+        elif s == 1:
+            got[0, s] = ring(after(done, (0, -1), (1, 0), (2, 0)), -1)
+        else:
+            got[0, s] = ring(got[0, s - 1], -1)
+    plane(-1, (1, 0), (2, 0))
+    got[3, 0] = exchange(got[1, 0], 1)
+    before = [(1, -1), (2, -1)]
+    for s in steps[1:]:
+        plane(s, *before)
+        before = [(3, 0)] if s == steps[-2] else [(2, s)]
+    got[3, 1] = ring(after(got[3, 0], (0, 1)), -1)
+    got[3, -1] = ring(after(got[3, 0], (0, 1)), 1)
+    for s in steps:
+        if abs(s) > 1:
+            got[3, s] = exchange(got[1, s], 1)
+    late = [(3, -1), (2, 1)]
+    middle = [(1, 1), (3, 1), (3, -lines // 2)]
     groups = ([k for k in got if k not in middle + late], middle, late)
     new = counts = None
     for later, names in enumerate(groups):
@@ -449,8 +461,11 @@
             [SMEM] + [VMEM] * len(names) + ([VMEM, ANY] if later else []),
             args,
             ("place_early", "place_middle", "place_late")[later],
-            out_specs=(ANY, VMEM),
-            scratch=[pltpu.SemaphoreType.DMA((len(names),))],
+            out_specs=(ANY, ANY),
+            scratch=[
+                pltpu.VMEM((local_cent // LANES, LANES), jnp.float32),
+                pltpu.SemaphoreType.DMA((len(names) + 1,)),
+            ],
             aliases={len(args) - 1: 0} if later else {},
         )
     return new, counts.reshape(-1), log_evidence.reshape(-1)

time: 95.7 us -> 99.9 us (1.044)
  waiting for transfers between devices: 34.6 us -> 38.4 us
  starting transfers between devices: 33.8 us -> 32.4 us
    ppermute x7 -> x8, starting transfers between devices: 13.6 us -> 11.8 us  [ring(): lax.ppermute(x, 'dp', [(4 * a + i, 4 * b + i) for a, b in pairs for i in...]
    ppermute x17 -> x16, waiting for transfers between devices: 9.47 us -> 11.3 us  [exchange(): return lax.ppermute(x, ('dp', 'cent'), pairs)]
    ppermute x7 -> x8, waiting for transfers between devices: 19.5 us -> 21.3 us  [ring(): lax.ppermute(x, 'dp', [(4 * a + i, 4 * b + i) for a, b in pairs for i in...]
    ppermute x17 -> x16, starting transfers between devices: 17.4 us -> 19 us  [exchange(): return lax.ppermute(x, ('dp', 'cent'), pairs)]
    unnamed x8 -> x10, local copies, waits for them, and re-layouts: 2.64 us -> 3.24 us
  transfers between devices with their start and end apart: 32 -> 32, of which waited for: 15 -> 14; matrix products, arithmetic and copies ran while one was open for 0% -> 0% of each run, Pallas kernels for 20% -> 18%
where the time goes in v13:
time: 99.9 us; the launch traced here: 99.7 us
  waiting for transfers between devices  38.4 us (38%)
  starting transfers between devices  32.4 us (32%)
  Pallas kernels  24.1 us (24%)
  local copies, waits for them, and re-layouts  3.24 us (3%)
    pallas_call x13, Pallas kernels, call(): pl.pallas_call(kernel, out_shape=out_shape, in_specs=in_specs, out_specs=...  24.1 us
    ppermute x8, waiting for transfers between devices, ring(): lax.ppermute(x, 'dp', [(4 * a + i, 4 * b + i) for a, b in pairs for i in...  21.3 us
    ppermute x16, starting transfers between devices, exchange(): return lax.ppermute(x, ('dp', 'cent'), pairs)  19 us
    ppermute x8, starting transfers between devices, ring(): lax.ppermute(x, 'dp', [(4 * a + i, 4 * b + i) for a, b in pairs for i in...  11.8 us
    ppermute x16, waiting for transfers between devices, exchange(): return lax.ppermute(x, ('dp', 'cent'), pairs)  11.3 us
    ppermute x1, waiting for transfers between devices, body(): lse_d = lax.ppermute(lse, 'dp', [(i, i ^ 3) for i in range(n)])  4.5 us
    unnamed x10, local copies, waits for them, and re-layouts  3.24 us
  transfers between devices with their start and end apart: 32, of which 14 were waited for; matrix products, arithmetic and copies ran while one was open for 0% of the time, Pallas kernels for 18%

profile of v13, /device:TPU:0, one launch (start us, length us, event | category | flops | bytes accessed | tf_op | source)
XLA Modules:
  0.0 99.7 jit_solution(18191353974271236217)
XLA Ops:
  0.6 0.6 pad_add_fusion.where_ref
  1.2 2.4 %open.1 = (f32[256,256]{1,0:T(8,128)}, f32[256,256]{1,0:T(8,128)}) custom-call(s32[2]{0:T(128)} %pad_add_fusion.where_ref, bf16[1024,256]{1,0:T(8,128)(2,1)} %points_ref.5), custom_call_target="tpu_custom_call" | custom-call | bytes 524296 | tf_op jit(solution)/shard_map/open/pallas_call | solution.py:27
  3.7 3.0 %collective-permute-start.3 = (f32[256,256]{1,0:T(8,128)}, f32[256,256]{1,0:T(8,128)S(1)}, u32[]{:S(2)}, u32[]{:S(2)}) collective-permute-start(f32[256,256]{1,0:T(8,128)} %get-tuple-element.60), channel_id=1, source_target_pairs={{0,4},{1,3},{2,6},{3,1},{4,0},{5,7},{6,2},{7,5},{8,12},{9,11},{10,... | collective-permute-start | bytes 786440 | tf_op jit(solution)/shard_map/ppermute | solution.py:317
  6.7 1.5 %collective-permute-start = (f32[256,256]{1,0:T(8,128)}, f32[256,256]{1,0:T(8,128)S(1)}, u32[]{:S(2)}, u32[]{:S(2)}) collective-permute-start(f32[256,256]{1,0:T(8,128)} %get-tuple-element.60), channel_id=1, source_target_pairs={{0,2},{1,5},{2,0},{3,7},{4,6},{5,1},{6,4},{7,3},{8,10},{9,13},{10,... | collective-permute-start | bytes 786440 | tf_op jit(solution)/shard_map/ppermute | solution.py:317
  8.8 1.0 %copy-done = bf16[1024,256]{1,0:T(8,128)(2,1)S(1)} copy-done((bf16[1024,256]{1,0:T(8,128)(2,1)S(1)}, bf16[1024,256]{1,0:T(8,128)(2,1)}, u32[]{:S(2)}) %copy-start) | copy-done | bytes 524312
  9.8 0.6 copy-done.2
  10.4 1.6 %copy-done.4 = bf16[4096,256]{1,0:T(8,128)(2,1)S(1)} copy-done((bf16[4096,256]{1,0:T(8,128)(2,1)S(1)}, bf16[4096,256]{1,0:T(8,128)(2,1)}, u32[]{:S(2)}) %copy-start.4) | copy-done | bytes 2097176
  12.0 5.9 %stats.1 = (f32[2,1024]{1,0:T(2,128)S(1)}, bf16[1024,256]{1,0:T(8,128)(2,1)S(1)}, f32[1024,128]{1,0:T(8,128)S(1)}) custom-call(s32[2]{0:T(128)S(1)} %copy-done.2, bf16[1024,256]{1,0:T(8,128)(2,1)S(1)} %copy-done, bf16[4096,256]{1,0:T(8,128)(2,1)S(1)} %copy-done.4), custom_call_target="tpu_custom_call" | custom-call | flops 4294967296 | bytes 2621448 | tf_op jit(solution)/shard_map/stats/pallas_call | solution.py:27
  18.0 1.2 %collective-permute-done.4.refs_1_ = f32[2,1024]{1,0:T(2,128)S(1)} collective-permute-done((f32[2,1024]{1,0:T(2,128)S(1)}, f32[2,1024]{1,0:T(2,128)S(1)}, u32[]{:S(2)}, u32[]{:S(2)}) %collective-permute-start.4) | collective-permute-done | bytes 8224 | tf_op jit(solution)/shard_map/ppermute | solution.py:320
  19.2 0.6 lse.1
  20.0 2.3 %collective-permute-start.9 = (f32[264,256]{1,0:T(8,128)S(1)}, f32[264,256]{1,0:T(8,128)S(1)}, u32[]{:S(2)}, u32[]{:S(2)}) collective-permute-start(f32[264,256]{1,0:T(8,128)S(1)} %get-tuple-element.79), channel_id=1, source_target_pairs={{0,4},{1,3},{2,6},{3,1},{4,0},{5,7},{6,2},{7,5},{8,12},{9,11},{10,... | collective-permute-start | bytes 811016 | tf_op jit(solution)/shard_map/ppermute | solution.py:317
  22.3 1.2 %collective-permute-start.10 = (f32[264,256]{1,0:T(8,128)S(1)}, f32[264,256]{1,0:T(8,128)S(1)}, u32[]{:S(2)}, u32[]{:S(2)}) collective-permute-start(f32[264,256]{1,0:T(8,128)S(1)} %get-tuple-element.80), channel_id=1, source_target_pairs={{0,2},{1,5},{2,0},{3,7},{4,6},{5,1},{6,4},{7,3},{8,10},{9,13},{10,... | collective-permute-start | bytes 811016 | tf_op jit(solution)/shard_map/ppermute | solution.py:317
  24.1 1.6 %own.1 = (f32[1024,256]{1,0:T(8,128)S(1)}, f32[1024,128]{1,0:T(8,128)S(1)}) custom-call(bf16[1024,256]{1,0:T(8,128)(2,1)S(1)} %copy-done.1, bf16[1024,256]{1,0:T(8,128)(2,1)S(1)} %get-tuple-element.58.twice_ref, f32[1024,128]{1,0:T(8,128)S(1)} %get-tuple-element.59.norm_ref, f32[4,256]{1,0:T(4,128)S(1)} %get-tuple-element.83.lse_ref), custom_call_target="tpu_custom_call" | custom-call | flops 1073741824 | bytes 1576960 | tf_op jit(solution)/shard_map/own/pallas_call | solution.py:27
  26.2 4.5 %collective-permute-done.11.lse_ref = f32[4,256]{1,0:T(4,128)S(1)} collective-permute-done((f32[4,256]{1,0:T(4,128)S(1)}, f32[4,256]{1,0:T(4,128)S(1)}, u32[]{:S(2)}, u32[]{:S(2)}) %collective-permute-start.11) | collective-permute-done | bytes 4128 | tf_op jit(solution)/shard_map/ppermute | solution.py:365
  31.2 1.6 %lead.1 = (f32[256,256]{1,0:T(8,128)S(1)}, f32[256,128]{1,0:T(8,128)S(1)}) custom-call(s32[2]{0:T(128)S(1)} %copy-done.3, bf16[1024,256]{1,0:T(8,128)(2,1)S(1)} %get-tuple-element.58.twice_ref, f32[1024,128]{1,0:T(8,128)S(1)} %get-tuple-element.59.norm_ref, f32[1024,256]{1,0:T(8,128)S(1)} %get-tuple-element.84.acc_ref, ...), custom_call_target="tpu_custom_call" | custom-call | flops 536870912 | bytes 5259272 | tf_op jit(solution)/shard_map/lead/pallas_call | solution.py:27
  32.8 1.2 %first.1 = f32[264,256]{1,0:T(8,128)S(1)} custom-call(s32[2]{0:T(128)S(1)} %copy-done.3, bf16[1024,256]{1,0:T(8,128)(2,1)S(1)} %get-tuple-element.58.twice_ref, f32[1024,128]{1,0:T(8,128)S(1)} %get-tuple-element.59.norm_ref, f32[4,256]{1,0:T(4,128)S(1)} %collective-permute-done.11.lse_ref, f32[256,256]{1,0:T(8,128)S(1)} %get-tuple-element.99.lead_acc_ref, ...), custom_call_target="tpu_custom_call" | custom-call | flops 536870912 | bytes 2527240 | tf_op jit(solution)/shard_map/first/pallas_call | solution.py:27
  34.0 2.6 %collective-permute-start.14 = (f32[264,256]{1,0:T(8,128)S(1)}, f32[264,256]{1,0:T(8,128)S(1)}, u32[]{:S(2)}, u32[]{:S(2)}) collective-permute-start(f32[264,256]{1,0:T(8,128)S(1)} %first.1), channel_id=1, source_target_pairs={{0,16},{2,18},{4,20},{6,22},{16,24},{18,26},{20,28},{22,30},{24,8}... | collective-permute-start | bytes 811016 | tf_op jit(solution)/shard_map/ppermute | solution.py:324
  36.6 2.0 %rest.3 = f32[264,256]{1,0:T(8,128)S(1)} custom-call(s32[2]{0:T(128)S(1)} %copy-done.3, bf16[1024,256]{1,0:T(8,128)(2,1)S(1)} %get-tuple-element.58.twice_ref, f32[1024,128]{1,0:T(8,128)S(1)} %get-tuple-element.59.norm_ref, f32[1024,256]{1,0:T(8,128)S(1)} %get-tuple-element.84.acc_ref, f32[1024,128]{1,0:T(8,128)S(1)} %get-tuple-element.85.cnt_ref, ...), custom_call_target="tpu_custom_call" | custom-call | flops 805306368 | bytes 5804040 | tf_op jit(solution)/shard_map/rest/pallas_call | solution.py:27
  38.9 2.9 %rest.2 = (f32[264,256]{1,0:T(8,128)S(1)}, f32[264,256]{1,0:T(8,128)S(1)}) custom-call(s32[2]{0:T(128)S(1)} %copy-done.3, bf16[1024,256]{1,0:T(8,128)(2,1)S(1)} %get-tuple-element.58.twice_ref, f32[1024,128]{1,0:T(8,128)S(1)} %get-tuple-element.59.norm_ref, f32[1024,256]{1,0:T(8,128)S(1)} %get-tuple-element.84.acc_ref, ...), custom_call_target="tpu_custom_call" | custom-call | flops 1610612736 | bytes 5804040 | tf_op jit(solution)/shard_map/rest/pallas_call | solution.py:27
  41.8 1.8 %collective-permute-done.14.b_ref = f32[264,256]{1,0:T(8,128)S(1)} collective-permute-done((f32[264,256]{1,0:T(8,128)S(1)}, f32[264,256]{1,0:T(8,128)S(1)}, u32[]{:S(2)}, u32[]{:S(2)}) %collective-permute-start.14) | collective-permute-done | bytes 270368 | tf_op jit(solution)/shard_map/ppermute | solution.py:324
  43.6 3.4 %collective-permute-start.15 = (f32[264,256]{1,0:T(8,128)S(1)}, f32[264,256]{1,0:T(8,128)S(1)}, u32[]{:S(2)}, u32[]{:S(2)}) collective-permute-start(f32[264,256]{1,0:T(8,128)S(1)} %add.3), channel_id=1, source_target_pairs={{0,16},{2,18},{4,20},{6,22},{16,24},{18,26},{20,28},{22,30},{24,8}... | collective-permute-start | bytes 811016 | tf_op jit(solution)/shard_map/ppermute | solution.py:324
  47.0 4.1 %collective-permute-done.16.second_ref = f32[264,256]{1,0:T(8,128)S(1)} collective-permute-done((f32[264,256]{1,0:T(8,128)S(1)}, f32[264,256]{1,0:T(8,128)S(1)}, u32[]{:S(2)}, u32[]{:S(2)}) %collective-permute-start.16) | collective-permute-done | bytes 270368 | tf_op jit(solution)/shard_map/ppermute | solution.py:324
  51.2 4.8 %collective-permute-done.15.first_ref = f32[264,256]{1,0:T(8,128)S(1)} collective-permute-done((f32[264,256]{1,0:T(8,128)S(1)}, f32[264,256]{1,0:T(8,128)S(1)}, u32[]{:S(2)}, u32[]{:S(2)}) %collective-permute-start.15) | collective-permute-done | bytes 270368 | tf_op jit(solution)/shard_map/ppermute | solution.py:324
  55.9 0.8 finish.1.refs_0_
  56.8 1.0 collective-permute-start.20
  57.7 1.6 %collective-permute-start.19 = (f32[264,256]{1,0:T(8,128)S(1)}, f32[264,256]{1,0:T(8,128)S(1)}, u32[]{:S(2)}, u32[]{:S(2)}) collective-permute-start(f32[264,256]{1,0:T(8,128)S(1)} %finish.1.refs_0_), channel_id=1, source_target_pairs={{0,16},{2,18},{4,20},{6,22},{16,24},{18,26},{20,28},{22,30},{24,8}... | collective-permute-start | bytes 811016 | tf_op jit(solution)/shard_map/ppermute | solution.py:324
  59.3 1.5 %collective-permute-start.17 = (f32[264,256]{1,0:T(8,128)S(1)}, f32[264,256]{1,0:T(8,128)S(1)}, u32[]{:S(2)}, u32[]{:S(2)}) collective-permute-start(f32[264,256]{1,0:T(8,128)S(1)} %finish.1.refs_0_), channel_id=1, source_target_pairs={{0,2},{1,5},{2,0},{3,7},{4,6},{5,1},{6,4},{7,3},{8,10},{9,13},{10,... | collective-permute-start | bytes 811016 | tf_op jit(solution)/shard_map/ppermute | solution.py:317
  60.8 4.9 %collective-permute-done.20.refs_3_ = f32[264,256]{1,0:T(8,128)S(1)} collective-permute-done((f32[264,256]{1,0:T(8,128)S(1)}, f32[264,256]{1,0:T(8,128)S(1)}, u32[]{:S(2)}, u32[]{:S(2)}) %collective-permute-start.20) | collective-permute-done | bytes 270368 | tf_op jit(solution)/shard_map/ppermute | solution.py:317
  66.0 1.9 %collective-permute-start.26 = (f32[264,256]{1,0:T(8,128)S(1)}, f32[264,256]{1,0:T(8,128)S(1)}, u32[]{:S(2)}, u32[]{:S(2)}) collective-permute-start(f32[264,256]{1,0:T(8,128)S(1)} %collective-permute-done.19.refs_1_), channel_id=1, source_target_pairs={{0,16},{2,18},{4,20},{6,22},{16,24},{18,26},{20,28},{22,30},{24,8}... | collective-permute-start | bytes 811016 | tf_op jit(solution)/shard_map/ppermute | solution.py:324
  67.9 1.2 %collective-permute-start.28 = (f32[264,256]{1,0:T(8,128)S(1)}, f32[264,256]{1,0:T(8,128)S(1)}, u32[]{:S(2)}, u32[]{:S(2)}) collective-permute-start(f32[264,256]{1,0:T(8,128)S(1)} %collective-permute-done.19.refs_1_), channel_id=1, source_target_pairs={{0,4},{1,3},{2,6},{3,1},{4,0},{5,7},{6,2},{7,5},{8,12},{9,11},{10,... | collective-permute-start | bytes 811016 | tf_op jit(solution)/shard_map/ppermute | solution.py:317
  69.1 0.7 collective-permute-start.27
  69.8 0.7 collective-permute-start.21
  70.5 0.8 collective-permute-start.18
  71.3 3.4 %collective-permute-done.26.refs_4_ = f32[264,256]{1,0:T(8,128)S(1)} collective-permute-done((f32[264,256]{1,0:T(8,128)S(1)}, f32[264,256]{1,0:T(8,128)S(1)}, u32[]{:S(2)}, u32[]{:S(2)}) %collective-permute-start.26) | collective-permute-done | bytes 270368 | tf_op jit(solution)/shard_map/ppermute | solution.py:324
  74.8 2.0 %collective-permute-done.28.refs_7_ = f32[264,256]{1,0:T(8,128)S(1)} collective-permute-done((f32[264,256]{1,0:T(8,128)S(1)}, f32[264,256]{1,0:T(8,128)S(1)}, u32[]{:S(2)}, u32[]{:S(2)}) %collective-permute-start.28) | collective-permute-done | bytes 270368 | tf_op jit(solution)/shard_map/ppermute | solution.py:317
  76.7 1.8 %collective-permute-done.27.refs_6_ = f32[264,256]{1,0:T(8,128)S(1)} collective-permute-done((f32[264,256]{1,0:T(8,128)S(1)}, f32[264,256]{1,0:T(8,128)S(1)}, u32[]{:S(2)}, u32[]{:S(2)}) %collective-permute-start.27) | collective-permute-done | bytes 270368 | tf_op jit(solution)/shard_map/ppermute | solution.py:317
  78.5 0.7 collective-permute-start.29
  79.2 1.0 %collective-permute-start.31 = (f32[264,256]{1,0:T(8,128)S(1)}, f32[264,256]{1,0:T(8,128)S(1)}, u32[]{:S(2)}, u32[]{:S(2)}) collective-permute-start(f32[264,256]{1,0:T(8,128)S(1)} %collective-permute-done.26.refs_4_), channel_id=1, source_target_pairs={{0,4},{1,3},{2,6},{3,1},{4,0},{5,7},{6,2},{7,5},{8,12},{9,11},{10,... | collective-permute-start | bytes 811016 | tf_op jit(solution)/shard_map/ppermute | solution.py:317
  80.2 1.2 %collective-permute-done.21.refs_5_ = f32[264,256]{1,0:T(8,128)S(1)} collective-permute-done((f32[264,256]{1,0:T(8,128)S(1)}, f32[264,256]{1,0:T(8,128)S(1)}, u32[]{:S(2)}, u32[]{:S(2)}) %collective-permute-start.21) | collective-permute-done | bytes 270368 | tf_op jit(solution)/shard_map/ppermute | solution.py:324
  81.5 0.7 collective-permute-start.25
  82.2 0.9 collective-permute-start.24
  83.1 2.5 %collective-permute-done.29.refs_9_ = f32[264,256]{1,0:T(8,128)S(1)} collective-permute-done((f32[264,256]{1,0:T(8,128)S(1)}, f32[264,256]{1,0:T(8,128)S(1)}, u32[]{:S(2)}, u32[]{:S(2)}) %collective-permute-start.29) | collective-permute-done | bytes 270368 | tf_op jit(solution)/shard_map/ppermute | solution.py:317
  85.6 1.1 %collective-permute-start.30 = (f32[264,256]{1,0:T(8,128)S(1)}, f32[264,256]{1,0:T(8,128)S(1)}, u32[]{:S(2)}, u32[]{:S(2)}) collective-permute-start(f32[264,256]{1,0:T(8,128)S(1)} %collective-permute-done.29.refs_9_), channel_id=1, source_target_pairs={{0,4},{1,3},{2,6},{3,1},{4,0},{5,7},{6,2},{7,5},{8,12},{9,11},{10,... | collective-permute-start | bytes 811016 | tf_op jit(solution)/shard_map/ppermute | solution.py:317
  87.2 1.5 %collective-permute-start.23 = (f32[264,256]{1,0:T(8,128)S(1)}, f32[264,256]{1,0:T(8,128)S(1)}, u32[]{:S(2)}, u32[]{:S(2)}) collective-permute-start(f32[264,256]{1,0:T(8,128)S(1)} %collective-permute-done.21.refs_5_), channel_id=1, source_target_pairs={{0,4},{1,3},{2,6},{3,1},{4,0},{5,7},{6,2},{7,5},{8,12},{9,11},{10,... | collective-permute-start | bytes 811016 | tf_op jit(solution)/shard_map/ppermute | solution.py:317
  88.7 2.2 %place_early.1 = (f32[4096,256]{1,0:T(8,128)}, f32[32,128]{1,0:T(8,128)S(1)}) custom-call(s32[2]{0:T(128)S(1)} %copy-done.3, f32[264,256]{1,0:T(8,128)S(1)} %finish.1.refs_0_, f32[264,256]{1,0:T(8,128)S(1)} %collective-permute-done.19.refs_1_, f32[264,256]{1,0:T(8,128)S(1)} %collective-permute-done.17.refs_2_, ...), custom_call_target="tpu_custom_call" | custom-call | bytes 2973704 | tf_op jit(solution)/shard_map/place_early/pallas_call | solution.py:27
  90.9 5.7 %collective-permute-done.25.refs_1_ = f32[264,256]{1,0:T(8,128)S(1)} collective-permute-done((f32[264,256]{1,0:T(8,128)S(1)}, f32[264,256]{1,0:T(8,128)S(1)}, u32[]{:S(2)}, u32[]{:S(2)}) %collective-permute-start.25) | collective-permute-done | bytes 270368 | tf_op jit(solution)/shard_map/ppermute | solution.py:324
  96.6 1.5 %place_middle.1 = (f32[4096,256]{1,0:T(8,128)}, f32[32,128]{1,0:T(8,128)S(1)}) custom-call(s32[2]{0:T(128)S(1)} %copy-done.3, f32[264,256]{1,0:T(8,128)S(1)} %collective-permute-done.24.refs_0_, f32[264,256]{1,0:T(8,128)S(1)} %collective-permute-done.25.refs_1_, f32[264,256]{1,0:T(8,128)S(1)} %collective-permute-done.30.refs_2_, ...), custom_call_target="tpu_custom_call", output_to_operand_aliasing={{0}: (5, {})} | custom-call | bytes 5021704 | tf_op jit(solution)/shard_map/place_middle/pallas_call | solution.py:27
  98.1 1.4 %place_late.1 = (f32[4096,256]{1,0:T(8,128)}, f32[32,128]{1,0:T(8,128)}) custom-call(s32[2]{0:T(128)S(1)} %copy-done.3, f32[264,256]{1,0:T(8,128)S(1)} %collective-permute-done.22.refs_0_, f32[264,256]{1,0:T(8,128)S(1)} %collective-permute-done.23.refs_1_, f32[32,128]{1,0:T(8,128)S(1)} %get-tuple-element.108.refs_2_, ...), custom_call_target="tpu_custom_call", output_to_operand_aliasing={{0}: (4, {})} | custom-call | bytes 4751368 | tf_op jit(solution)/shard_map/place_late/pallas_call | solution.py:27
  (40 shorter events, 3.5 us)
Async XLA Ops:
  3.7 16.2 %collective-permute-start.3 = (f32[256,256]{1,0:T(8,128)}, f32[256,256]{1,0:T(8,128)S(1)}, u32[]{:S(2)}, u32[]{:S(2)}) collective-permute-start(f32[256,256]{1,0:T(8,128)} %get-tuple-element.60), channel_id=1, source_target_pairs={{0,4},{1,3},{2,6},{3,1},{4,0},{5,7},{6,2},{7,5},{8,12},{9,11},{10,... | collective-permute-start | bytes 786440 | tf_op jit(solution)/shard_map/ppermute | solution.py:317
  6.7 12.5 %collective-permute-start = (f32[256,256]{1,0:T(8,128)}, f32[256,256]{1,0:T(8,128)S(1)}, u32[]{:S(2)}, u32[]{:S(2)}) collective-permute-start(f32[256,256]{1,0:T(8,128)} %get-tuple-element.60), channel_id=1, source_target_pairs={{0,2},{1,5},{2,0},{3,7},{4,6},{5,1},{6,4},{7,3},{8,10},{9,13},{10,... | collective-permute-start | bytes 786440 | tf_op jit(solution)/shard_map/ppermute | solution.py:317
  8.2 11.7 %collective-permute-start.2 = (f32[256,256]{1,0:T(8,128)}, f32[256,256]{1,0:T(8,128)S(1)}, u32[]{:S(2)}, u32[]{:S(2)}) collective-permute-start(f32[256,256]{1,0:T(8,128)} %get-tuple-element.61), channel_id=1, source_target_pairs={{0,2},{1,5},{2,0},{3,7},{4,6},{5,1},{6,4},{7,3},{8,10},{9,13},{10,... | collective-permute-start | bytes 786440 | tf_op jit(solution)/shard_map/ppermute | solution.py:317
  8.7 10.5 %collective-permute-start.1 = (f32[256,256]{1,0:T(8,128)}, f32[256,256]{1,0:T(8,128)S(1)}, u32[]{:S(2)}, u32[]{:S(2)}) collective-permute-start(f32[256,256]{1,0:T(8,128)} %get-tuple-element.61), channel_id=1, source_target_pairs={{0,4},{1,3},{2,6},{3,1},{4,0},{5,7},{6,2},{7,5},{8,12},{9,11},{10,... | collective-permute-start | bytes 786440 | tf_op jit(solution)/shard_map/ppermute | solution.py:317
  8.8 1.0 %copy-start = (bf16[1024,256]{1,0:T(8,128)(2,1)S(1)}, bf16[1024,256]{1,0:T(8,128)(2,1)}, u32[]{:S(2)}) copy-start(bf16[1024,256]{1,0:T(8,128)(2,1)} %points_ref.5) | copy-start | bytes 1572868
  9.8 0.6 copy-start.2
  10.4 1.6 %copy-start.4 = (bf16[4096,256]{1,0:T(8,128)(2,1)S(1)}, bf16[4096,256]{1,0:T(8,128)(2,1)}, u32[]{:S(2)}) copy-start(bf16[4096,256]{1,0:T(8,128)(2,1)} %c_ref.1) | copy-start | bytes 6291460
  12.0 12.0 %copy-start.1 = (bf16[1024,256]{1,0:T(8,128)(2,1)S(1)}, bf16[1024,256]{1,0:T(8,128)(2,1)}, u32[]{:S(2)}) copy-start(bf16[1024,256]{1,0:T(8,128)(2,1)} %points_ref.5) | copy-start | bytes 1572868
  18.0 13.3 %copy-start.3 = (s32[2]{0:T(128)S(1)}, s32[2]{0:T(128)}, u32[]{:S(2)}) copy-start(s32[2]{0:T(128)} %pad_add_fusion.where_ref) | copy-start | bytes 28
  18.0 1.2 %collective-permute-start.4 = (f32[2,1024]{1,0:T(2,128)S(1)}, f32[2,1024]{1,0:T(2,128)S(1)}, u32[]{:S(2)}, u32[]{:S(2)}) collective-permute-start(f32[2,1024]{1,0:T(2,128)S(1)} %get-tuple-element.62.refs_0_), channel_id=1, source_target_pairs={{0,1},{1,0},{2,3},{3,2},{4,5},{5,4},{6,7},{7,6},{8,9},{9,8},{10,11... | collective-permute-start | bytes 24584 | tf_op jit(solution)/shard_map/ppermute | solution.py:320
  19.9 4.2 %collective-permute-start.5 = (f32[256,256]{1,0:T(8,128)S(1)}, f32[256,256]{1,0:T(8,128)S(1)}, u32[]{:S(2)}, u32[]{:S(2)}) collective-permute-start(f32[256,256]{1,0:T(8,128)S(1)} %collective-permute-done.a0_ref.refs_0_), channel_id=1, source_target_pairs={{0,1},{1,0},{2,3},{3,2},{4,5},{5,4},{6,7},{7,6},{8,9},{9,8},{10,11... | collective-permute-start | bytes 786440 | tf_op jit(solution)/shard_map/ppermute | solution.py:320
  20.0 10.7 %collective-permute-start.9 = (f32[264,256]{1,0:T(8,128)S(1)}, f32[264,256]{1,0:T(8,128)S(1)}, u32[]{:S(2)}, u32[]{:S(2)}) collective-permute-start(f32[264,256]{1,0:T(8,128)S(1)} %get-tuple-element.79), channel_id=1, source_target_pairs={{0,4},{1,3},{2,6},{3,1},{4,0},{5,7},{6,2},{7,5},{8,12},{9,11},{10,... | collective-permute-start | bytes 811016 | tf_op jit(solution)/shard_map/ppermute | solution.py:317
  22.3 8.4 %collective-permute-start.10 = (f32[264,256]{1,0:T(8,128)S(1)}, f32[264,256]{1,0:T(8,128)S(1)}, u32[]{:S(2)}, u32[]{:S(2)}) collective-permute-start(f32[264,256]{1,0:T(8,128)S(1)} %get-tuple-element.80), channel_id=1, source_target_pairs={{0,2},{1,5},{2,0},{3,7},{4,6},{5,1},{6,4},{7,3},{8,10},{9,13},{10,... | collective-permute-start | bytes 811016 | tf_op jit(solution)/shard_map/ppermute | solution.py:317
  23.5 2.1 %collective-permute-start.6 = (f32[256,256]{1,0:T(8,128)S(1)}, f32[256,256]{1,0:T(8,128)S(1)}, u32[]{:S(2)}, u32[]{:S(2)}) collective-permute-start(f32[256,256]{1,0:T(8,128)S(1)} %collective-permute-done.1.b1_ref.refs_2_), channel_id=1, source_target_pairs={{0,1},{1,0},{2,3},{3,2},{4,5},{5,4},{6,7},{7,6},{8,9},{9,8},{10,11... | collective-permute-start | bytes 786440 | tf_op jit(solution)/shard_map/ppermute | solution.py:320
  23.5 2.1 %collective-permute-start.7 = (f32[256,256]{1,0:T(8,128)S(1)}, f32[256,256]{1,0:T(8,128)S(1)}, u32[]{:S(2)}, u32[]{:S(2)}) collective-permute-start(f32[256,256]{1,0:T(8,128)S(1)} %collective-permute-done.2.refs_4_), channel_id=1, source_target_pairs={{0,1},{1,0},{2,3},{3,2},{4,5},{5,4},{6,7},{7,6},{8,9},{9,8},{10,11... | collective-permute-start | bytes 786440 | tf_op jit(solution)/shard_map/ppermute | solution.py:320
  24.0 1.8 %collective-permute-start.8 = (f32[256,256]{1,0:T(8,128)S(1)}, f32[256,256]{1,0:T(8,128)S(1)}, u32[]{:S(2)}, u32[]{:S(2)}) collective-permute-start(f32[256,256]{1,0:T(8,128)S(1)} %collective-permute-done.3.refs_6_), channel_id=1, source_target_pairs={{0,1},{1,0},{2,3},{3,2},{4,5},{5,4},{6,7},{7,6},{8,9},{9,8},{10,11... | collective-permute-start | bytes 786440 | tf_op jit(solution)/shard_map/ppermute | solution.py:320
  25.8 4.9 %collective-permute-start.11 = (f32[4,256]{1,0:T(4,128)S(1)}, f32[4,256]{1,0:T(4,128)S(1)}, u32[]{:S(2)}, u32[]{:S(2)}) collective-permute-start(f32[4,256]{1,0:T(4,128)S(1)} %get-tuple-element.83.lse_ref), channel_id=1, source_target_pairs={{0,6},{2,4},{4,2},{6,0},{8,14},{10,12},{12,10},{14,8},{16,22},{18,... | collective-permute-start | bytes 12296 | tf_op jit(solution)/shard_map/ppermute | solution.py:365
  30.7 2.1 %collective-permute-start.12 = (f32[264,256]{1,0:T(8,128)S(1)}, f32[264,256]{1,0:T(8,128)S(1)}, u32[]{:S(2)}, u32[]{:S(2)}) collective-permute-start(f32[264,256]{1,0:T(8,128)S(1)} %collective-permute-done.9.refs_8_.refs_0_), channel_id=1, source_target_pairs={{0,1},{1,0},{2,3},{3,2},{4,5},{5,4},{6,7},{7,6},{8,9},{9,8},{10,11... | collective-permute-start | bytes 811016 | tf_op jit(solution)/shard_map/ppermute | solution.py:320
  30.7 2.1 %collective-permute-start.13 = (f32[264,256]{1,0:T(8,128)S(1)}, f32[264,256]{1,0:T(8,128)S(1)}, u32[]{:S(2)}, u32[]{:S(2)}) collective-permute-start(f32[264,256]{1,0:T(8,128)S(1)} %collective-permute-done.10.refs_10_.refs_9_.refs_2_), channel_id=1, source_target_pairs={{0,1},{1,0},{2,3},{3,2},{4,5},{5,4},{6,7},{7,6},{8,9},{9,8},{10,11... | collective-permute-start | bytes 811016 | tf_op jit(solution)/shard_map/ppermute | solution.py:320
  34.0 9.5 %collective-permute-start.14 = (f32[264,256]{1,0:T(8,128)S(1)}, f32[264,256]{1,0:T(8,128)S(1)}, u32[]{:S(2)}, u32[]{:S(2)}) collective-permute-start(f32[264,256]{1,0:T(8,128)S(1)} %first.1), channel_id=1, source_target_pairs={{0,16},{2,18},{4,20},{6,22},{16,24},{18,26},{20,28},{22,30},{24,8}... | collective-permute-start | bytes 811016 | tf_op jit(solution)/shard_map/ppermute | solution.py:324
  38.6 12.5 %collective-permute-start.16 = (f32[264,256]{1,0:T(8,128)S(1)}, f32[264,256]{1,0:T(8,128)S(1)}, u32[]{:S(2)}, u32[]{:S(2)}) collective-permute-start(f32[264,256]{1,0:T(8,128)S(1)} %rest.3), channel_id=1, source_target_pairs={{0,8},{2,10},{4,12},{6,14},{16,0},{18,2},{20,4},{22,6},{24,16},{26... | collective-permute-start | bytes 811016 | tf_op jit(solution)/shard_map/ppermute | solution.py:324
  43.6 12.4 %collective-permute-start.15 = (f32[264,256]{1,0:T(8,128)S(1)}, f32[264,256]{1,0:T(8,128)S(1)}, u32[]{:S(2)}, u32[]{:S(2)}) collective-permute-start(f32[264,256]{1,0:T(8,128)S(1)} %add.3), channel_id=1, source_target_pairs={{0,16},{2,18},{4,20},{6,22},{16,24},{18,26},{20,28},{22,30},{24,8}... | collective-permute-start | bytes 811016 | tf_op jit(solution)/shard_map/ppermute | solution.py:324
  56.8 9.0 %collective-permute-start.20 = (f32[264,256]{1,0:T(8,128)S(1)}, f32[264,256]{1,0:T(8,128)S(1)}, u32[]{:S(2)}, u32[]{:S(2)}) collective-permute-start(f32[264,256]{1,0:T(8,128)S(1)} %finish.1.refs_0_), channel_id=1, source_target_pairs={{0,4},{1,3},{2,6},{3,1},{4,0},{5,7},{6,2},{7,5},{8,12},{9,11},{10,... | collective-permute-start | bytes 811016 | tf_op jit(solution)/shard_map/ppermute | solution.py:317
  57.7 8.3 %collective-permute-start.19 = (f32[264,256]{1,0:T(8,128)S(1)}, f32[264,256]{1,0:T(8,128)S(1)}, u32[]{:S(2)}, u32[]{:S(2)}) collective-permute-start(f32[264,256]{1,0:T(8,128)S(1)} %finish.1.refs_0_), channel_id=1, source_target_pairs={{0,16},{2,18},{4,20},{6,22},{16,24},{18,26},{20,28},{22,30},{24,8}... | collective-permute-start | bytes 811016 | tf_op jit(solution)/shard_map/ppermute | solution.py:324
  59.3 6.6 %collective-permute-start.17 = (f32[264,256]{1,0:T(8,128)S(1)}, f32[264,256]{1,0:T(8,128)S(1)}, u32[]{:S(2)}, u32[]{:S(2)}) collective-permute-start(f32[264,256]{1,0:T(8,128)S(1)} %finish.1.refs_0_), channel_id=1, source_target_pairs={{0,2},{1,5},{2,0},{3,7},{4,6},{5,1},{6,4},{7,3},{8,10},{9,13},{10,... | collective-permute-start | bytes 811016 | tf_op jit(solution)/shard_map/ppermute | solution.py:317
  66.0 8.8 %collective-permute-start.26 = (f32[264,256]{1,0:T(8,128)S(1)}, f32[264,256]{1,0:T(8,128)S(1)}, u32[]{:S(2)}, u32[]{:S(2)}) collective-permute-start(f32[264,256]{1,0:T(8,128)S(1)} %collective-permute-done.19.refs_1_), channel_id=1, source_target_pairs={{0,16},{2,18},{4,20},{6,22},{16,24},{18,26},{20,28},{22,30},{24,8}... | collective-permute-start | bytes 811016 | tf_op jit(solution)/shard_map/ppermute | solution.py:324
  67.9 8.9 %collective-permute-start.28 = (f32[264,256]{1,0:T(8,128)S(1)}, f32[264,256]{1,0:T(8,128)S(1)}, u32[]{:S(2)}, u32[]{:S(2)}) collective-permute-start(f32[264,256]{1,0:T(8,128)S(1)} %collective-permute-done.19.refs_1_), channel_id=1, source_target_pairs={{0,4},{1,3},{2,6},{3,1},{4,0},{5,7},{6,2},{7,5},{8,12},{9,11},{10,... | collective-permute-start | bytes 811016 | tf_op jit(solution)/shard_map/ppermute | solution.py:317
  69.1 9.4 %collective-permute-start.27 = (f32[264,256]{1,0:T(8,128)S(1)}, f32[264,256]{1,0:T(8,128)S(1)}, u32[]{:S(2)}, u32[]{:S(2)}) collective-permute-start(f32[264,256]{1,0:T(8,128)S(1)} %collective-permute-done.19.refs_1_), channel_id=1, source_target_pairs={{0,2},{1,5},{2,0},{3,7},{4,6},{5,1},{6,4},{7,3},{8,10},{9,13},{10,... | collective-permute-start | bytes 811016 | tf_op jit(solution)/shard_map/ppermute | solution.py:317
  69.8 11.7 %collective-permute-start.21 = (f32[264,256]{1,0:T(8,128)S(1)}, f32[264,256]{1,0:T(8,128)S(1)}, u32[]{:S(2)}, u32[]{:S(2)}) collective-permute-start(f32[264,256]{1,0:T(8,128)S(1)} %finish.1.refs_0_), channel_id=1, source_target_pairs={{0,8},{2,10},{4,12},{6,14},{16,0},{18,2},{20,4},{22,6},{24,16},{26... | collective-permute-start | bytes 811016 | tf_op jit(solution)/shard_map/ppermute | solution.py:324
  70.5 11.0 %collective-permute-start.18 = (f32[264,256]{1,0:T(8,128)S(1)}, f32[264,256]{1,0:T(8,128)S(1)}, u32[]{:S(2)}, u32[]{:S(2)}) collective-permute-start(f32[264,256]{1,0:T(8,128)S(1)} %collective-permute-done.17.refs_2_), channel_id=1, source_target_pairs={{0,4},{1,3},{2,6},{3,1},{4,0},{5,7},{6,2},{7,5},{8,12},{9,11},{10,... | collective-permute-start | bytes 811016 | tf_op jit(solution)/shard_map/ppermute | solution.py:317
  78.5 7.1 %collective-permute-start.29 = (f32[264,256]{1,0:T(8,128)S(1)}, f32[264,256]{1,0:T(8,128)S(1)}, u32[]{:S(2)}, u32[]{:S(2)}) collective-permute-start(f32[264,256]{1,0:T(8,128)S(1)} %collective-permute-done.26.refs_4_), channel_id=1, source_target_pairs={{0,2},{1,5},{2,0},{3,7},{4,6},{5,1},{6,4},{7,3},{8,10},{9,13},{10,... | collective-permute-start | bytes 811016 | tf_op jit(solution)/shard_map/ppermute | solution.py:317
  79.2 8.0 %collective-permute-start.31 = (f32[264,256]{1,0:T(8,128)S(1)}, f32[264,256]{1,0:T(8,128)S(1)}, u32[]{:S(2)}, u32[]{:S(2)}) collective-permute-start(f32[264,256]{1,0:T(8,128)S(1)} %collective-permute-done.26.refs_4_), channel_id=1, source_target_pairs={{0,4},{1,3},{2,6},{3,1},{4,0},{5,7},{6,2},{7,5},{8,12},{9,11},{10,... | collective-permute-start | bytes 811016 | tf_op jit(solution)/shard_map/ppermute | solution.py:317
  81.5 15.1 %collective-permute-start.25 = (f32[264,256]{1,0:T(8,128)S(1)}, f32[264,256]{1,0:T(8,128)S(1)}, u32[]{:S(2)}, u32[]{:S(2)}) collective-permute-start(f32[264,256]{1,0:T(8,128)S(1)} %collective-permute-done.18.refs_8_), channel_id=1, source_target_pairs={{0,8},{2,10},{4,12},{6,14},{16,0},{18,2},{20,4},{22,6},{24,16},{26... | collective-permute-start | bytes 811016 | tf_op jit(solution)/shard_map/ppermute | solution.py:324
  82.2 14.4 %collective-permute-start.24 = (f32[264,256]{1,0:T(8,128)S(1)}, f32[264,256]{1,0:T(8,128)S(1)}, u32[]{:S(2)}, u32[]{:S(2)}) collective-permute-start(f32[264,256]{1,0:T(8,128)S(1)} %collective-permute-done.21.refs_5_), channel_id=1, source_target_pairs={{0,2},{1,5},{2,0},{3,7},{4,6},{5,1},{6,4},{7,3},{8,10},{9,13},{10,... | collective-permute-start | bytes 811016 | tf_op jit(solution)/shard_map/ppermute | solution.py:317
  85.6 11.0 %collective-permute-start.30 = (f32[264,256]{1,0:T(8,128)S(1)}, f32[264,256]{1,0:T(8,128)S(1)}, u32[]{:S(2)}, u32[]{:S(2)}) collective-permute-start(f32[264,256]{1,0:T(8,128)S(1)} %collective-permute-done.29.refs_9_), channel_id=1, source_target_pairs={{0,4},{1,3},{2,6},{3,1},{4,0},{5,7},{6,2},{7,5},{8,12},{9,11},{10,... | collective-permute-start | bytes 811016 | tf_op jit(solution)/shard_map/ppermute | solution.py:317
  86.7 11.4 %collective-permute-start.22 = (f32[264,256]{1,0:T(8,128)S(1)}, f32[264,256]{1,0:T(8,128)S(1)}, u32[]{:S(2)}, u32[]{:S(2)}) collective-permute-start(f32[264,256]{1,0:T(8,128)S(1)} %collective-permute-done.18.refs_8_), channel_id=1, source_target_pairs={{0,16},{2,18},{4,20},{6,22},{16,24},{18,26},{20,28},{22,30},{24,8}... | collective-permute-start | bytes 811016 | tf_op jit(solution)/shard_map/ppermute | solution.py:324
  87.2 10.9 %collective-permute-start.23 = (f32[264,256]{1,0:T(8,128)S(1)}, f32[264,256]{1,0:T(8,128)S(1)}, u32[]{:S(2)}, u32[]{:S(2)}) collective-permute-start(f32[264,256]{1,0:T(8,128)S(1)} %collective-permute-done.21.refs_5_), channel_id=1, source_target_pairs={{0,4},{1,3},{2,6},{3,1},{4,0},{5,7},{6,2},{7,5},{8,12},{9,11},{10,... | collective-permute-start | bytes 811016 | tf_op jit(solution)/shard_map/ppermute | solution.py:317

commit v14 on v12

--- a/solution.py
+++ b/solution.py
@@ -9,7 +9,7 @@
 from jax.sharding import PartitionSpec as P
 
 prior_mass = 0.5
-VMEM_LIMIT = 48 * 1024 * 1024
+VMEM_LIMIT = 24 * 1024 * 1024
 LANES = 128
 NT = (((1,), (1,)), ((), ()))
 NN = (((1,), (0,)), ((), ()))
@@ -41,14 +41,10 @@
     )(*args)
 
 
-def open_kernel(where_ref, points_ref, first_ref, second_ref, raw_ref, sem):
-    half = first_ref.shape[0]
-    start = pl.multiple_of(where_ref[1] * (2 * half), 2 * half)
-    copy = pltpu.make_async_copy(points_ref.at[pl.ds(start, 2 * half), :], raw_ref, sem)
-    copy.start()
-    copy.wait()
-    first_ref[...] = raw_ref[:half, :].astype(jnp.float32)
-    second_ref[...] = raw_ref[half:, :].astype(jnp.float32)
+def open_kernel(where_ref, points_ref, out_ref):
+    block = out_ref.shape[0]
+    start = pl.multiple_of(where_ref[1] * block, block)
+    out_ref[...] = points_ref[pl.ds(start, block), :].astype(jnp.float32)
 
 
 def widen(norm, width):
@@ -107,7 +103,7 @@
     )
 
 
-def lse_kernel(cores, every, a0_ref, b1_ref, *refs):
+def lse_kernel(cores, every, a_ref, b_ref, *refs):
     pair_refs = refs[:cores]
     lse_ref, evidence_ref, pack_a_ref, pack_b_ref = refs[cores:]
     half = lse_ref.shape[1]
@@ -119,8 +115,8 @@
         evidence_ref[k : k + 1, :] = evidence[:, k * LANES : (k + 1) * LANES]
     for i in range(2 * cores):
         lse_ref[i : i + 1, :] = lse[:, i * half : (i + 1) * half]
-    for piece_ref, pack_ref in ((a0_ref, pack_a_ref), (b1_ref, pack_b_ref)):
-        pack_ref[0:half, :] = piece_ref[...]
+    for piece, pack_ref in ((a_ref[0:half, :], pack_a_ref), (b_ref[half:, :], pack_b_ref)):
+        pack_ref[0:half, :] = piece
         pack_ref[half:, :] = jnp.zeros_like(pack_ref[half:, :])
         pack_ref[half : half + 2 * cores, 0:half] = lse_ref[...]
 
@@ -137,13 +133,16 @@
     return part, counted
 
 
+def two_rows(ref, at, half):
+    return jnp.concatenate([ref[pl.ds(at, 1), :][:, 0:half], ref[pl.ds(at + 1, 1), :][:, 0:half]], axis=1)
+
+
 def own_kernel(cores, points_ref, twice_ref, norm_ref, lse_ref, acc_ref, cnt_ref):
     half = points_ref.shape[0] // (2 * cores)
-    for i in range(2 * cores):
-        x = points_ref[i * half : (i + 1) * half, :]
-        part, counted = weigh(
-            twice_ref[...], norm_ref[...], x, lse_ref[i : i + 1, :], cnt_ref.shape[1]
-        )
+    for i in range(cores):
+        x = points_ref[2 * i * half : 2 * (i + 1) * half, :]
+        lse = two_rows(lse_ref, 2 * i, half)
+        part, counted = weigh(twice_ref[...], norm_ref[...], x, lse, cnt_ref.shape[1])
         if i == 0:
             acc_ref[...] = part
             cnt_ref[...] = counted
@@ -152,27 +151,26 @@
             cnt_ref[...] += counted
 
 
-KINDS = ((0, 0), (1, 1), (0, 1), (1, 0))
-
-
 def near_rows(cores, half, core, refs, d0_ref, d1_ref):
-    for k, (kind, part) in enumerate(KINDS):
+    for kind in range(2):
         for rc in range(cores):
-            at = half + 2 * (core ^ rc) + part
             tail_ref = d1_ref if (kind + rc) % 2 == 0 else d0_ref
-            yield refs[k * cores + rc], (lambda at=at, tail_ref=tail_ref: tail_ref[pl.ds(at, 1), :][:, 0:half])
+            at = half + 2 * (core ^ rc)
+            yield (lambda ref=refs[kind * cores + rc]: ref[...]), (
+                lambda at=at, tail_ref=tail_ref: two_rows(tail_ref, at, half)
+            )
 
 
 def far_rows(cores, half, core, refs, lse_ref):
-    for part in range(2):
-        for rc in range(cores):
-            at = 2 * (core ^ rc) + part
-            yield refs[part * cores + rc], (lambda at=at: lse_ref[pl.ds(at, 1), :])
+    for rc in range(cores):
+        yield (
+            lambda rc=rc: jnp.concatenate([refs[rc][0:half, :], refs[cores + rc][0:half, :]], axis=0)
+        ), (lambda at=2 * (core ^ rc): two_rows(lse_ref, at, half))
 
 
 def add_rows(rows, half, twice, norm, acc, cnt):
-    for x_ref, lse in rows:
-        part, counted = weigh(twice, norm, x_ref[0:half, :].astype(jnp.bfloat16), lse(), cnt.shape[1])
+    for x, lse in rows:
+        part, counted = weigh(twice, norm, x().astype(jnp.bfloat16), lse(), cnt.shape[1])
         acc, cnt = acc + part, cnt + counted
     return acc, cnt
 
@@ -188,7 +186,7 @@
 
 def lead_kernel(cores, order, half, where_ref, twice_ref, norm_ref, acc_ref, cnt_ref, *refs):
     out_acc_ref, out_cnt_ref = refs[-2:]
-    near, (d0_ref, d1_ref) = refs[: 4 * cores], refs[4 * cores : 4 * cores + 2]
+    near, (d0_ref, d1_ref) = refs[: 2 * cores], refs[2 * cores : 2 * cores + 2]
     size = out_acc_ref.shape[0]
     place = ahead(order, lax.div(where_ref[0], 4), len(order) // 2)
     at = pl.ds(pl.multiple_of(place * size, size), size)
@@ -236,8 +234,8 @@
 
 
 def rest_kernel(cores, order, half, steps, where_ref, twice_ref, norm_ref, acc_ref, cnt_ref, lse_ref, *refs):
-    near, far = refs[: 4 * cores], refs[4 * cores : 6 * cores]
-    for s, out_ref in zip(steps, refs[6 * cores :]):
+    near, far = refs[: 2 * cores], refs[2 * cores : 4 * cores]
+    for s, out_ref in zip(steps, refs[4 * cores :]):
         block_sums(
             cores, order, half, s, where_ref, twice_ref, norm_ref, acc_ref, cnt_ref, lse_ref, near, far, out_ref
         )
@@ -273,7 +271,7 @@
 def place_kernel(names, order, later, where_ref, *refs):
     count, lines = len(names), len(order)
     block_refs = refs[:count]
-    new_ref, counts_ref, sems = refs[-3:]
+    new_ref, counts_out_ref, counts_ref, sems = refs[-4:]
     size = block_refs[0].shape[0] - 8
     plane, line = lax.rem(where_ref[0], 4), lax.div(where_ref[0], 4)
     each = size // LANES
@@ -292,6 +290,8 @@
     for i in range(count):
         for k in range(each):
             counts_ref[pl.ds(places[i] * each + k, 1), :] = block_refs[i][size + k : size + k + 1, 0:LANES]
+    copies.append(pltpu.make_async_copy(counts_ref, counts_out_ref, sems.at[count]))
+    copies[-1].start()
     for copy in copies:
         copy.wait()
 
@@ -324,16 +324,8 @@
     def with_siblings(pieces):
         return [a if rc == 0 else flip_core(a, rc) for a in pieces for rc in range(cores)]
 
-    first, second = call(
-        open_kernel,
-        (f32(half, width), f32(half, width)),
-        [SMEM, HBM],
-        (where, points),
-        "open",
-        scratch=[pltpu.VMEM((2 * half, width), points.dtype), pltpu.SemaphoreType.DMA(())],
-    )
-    a0, b1 = exchange(first, 0), exchange(second, 1)
-    a1, b0 = exchange(second, 0), exchange(first, 1)
+    mine = call(open_kernel, f32(2 * half, width), [SMEM, VMEM], (where, points), "open")
+    by_a, by_b = exchange(mine, 0), exchange(mine, 1)
 
     pair, twice, norm = stats(where, points, centroids, lines)
     pairs = [pair] + [flip_core(pair, rc) for rc in range(1, cores)]
@@ -342,13 +334,13 @@
         functools.partial(lse_kernel, cores, local_cent * cores),
         (f32(2 * cores, half), f32(rows // LANES, LANES), f32(half + tail, width), f32(half + tail, width)),
         [VMEM] * (2 + cores),
-        (a0, b1, *pairs),
+        (by_a, by_b, *pairs),
         "lse",
     )
     d0, d1 = exchange(pack_a, 1), exchange(pack_b, 0)
 
-    a0, b1, a1, b0, lse = lax.optimization_barrier((a0, b1, a1, b0, lse))
-    near = with_siblings((a0, b1, a1, b0))
+    by_a, by_b, lse = lax.optimization_barrier((by_a, by_b, lse))
+    near = with_siblings((by_a, by_b))
     lanes = min(LANES, half)
     acc, cnt = call(
         functools.partial(own_kernel, cores),
@@ -364,7 +356,7 @@
     lead = call(
         functools.partial(lead_kernel, cores, order, half),
         (f32(size, width), f32(size, lanes)),
-        [SMEM] + [VMEM] * (6 + 4 * cores),
+        [SMEM] + [VMEM] * (6 + 2 * cores),
         (where, twice, norm, acc, cnt, *near, d0, d1),
         "lead",
         flops=4 * size * width * 2 * rows,
@@ -389,7 +381,7 @@
         made = call(
             functools.partial(rest_kernel, cores, order, half, steps),
             [block_sum] * len(steps),
-            [SMEM] + [VMEM] * (5 + 6 * cores),
+            [SMEM] + [VMEM] * (5 + 4 * cores),
             (*given, *rows_given),
             "rest",
             flops=4 * size * width * 3 * rows * len(steps),
@@ -435,8 +427,8 @@
     before = got[3, steps[-1] - 1] if steps[-1] > 0 else got[3, steps[-1] + 1]
     before = lax.optimization_barrier((before, got[0, steps[-1]]))[0]
     got[3, steps[-1]] = ring(before, -1 if steps[-1] > 0 else 1)
-    late = [(1, steps[-1]), (2, steps[-1]), (3, steps[-1])]
-    middle = [(w, steps[-2]) for w in (1, 2, 3)] + [(0, steps[-1])]
+    late = [(1, steps[-1]), (2, steps[-1])]
+    middle = [(w, steps[-2]) for w in (1, 2, 3)] + [(3, steps[-1])]
     groups = ([k for k in got if k not in middle + late], middle, late)
     new = counts = None
     for later, names in enumerate(groups):
@@ -449,8 +441,11 @@
             [SMEM] + [VMEM] * len(names) + ([VMEM, ANY] if later else []),
             args,
             ("place_early", "place_middle", "place_late")[later],
-            out_specs=(ANY, VMEM),
-            scratch=[pltpu.SemaphoreType.DMA((len(names),))],
+            out_specs=(ANY, ANY),
+            scratch=[
+                pltpu.VMEM((local_cent // LANES, LANES), jnp.float32),
+                pltpu.SemaphoreType.DMA((len(names) + 1,)),
+            ],
             aliases={len(args) - 1: 0} if later else {},
         )
     return new, counts.reshape(-1), log_evidence.reshape(-1)

time: 95.7 us -> 95.2 us (level)
  waiting for transfers between devices: 34.6 us -> 37.5 us
  Pallas kernels: 23.3 us -> 21.3 us
  starting transfers between devices: 33.8 us -> 32.5 us
    ppermute x17 -> x15, waiting for transfers between devices: 9.47 us -> 15.1 us  [exchange(): return lax.ppermute(x, ('dp', 'cent'), pairs)]
    ppermute x1, waiting for transfers between devices: 4.31 us -> 0.91 us  [body(): lse_d = lax.ppermute(lse, 'dp', [(i, i ^ 3) for i in range(n)])]
    pallas_call x13, Pallas kernels: 23.3 us -> 21.3 us  [call(): pl.pallas_call(kernel, out_shape=out_shape, in_specs=in_specs, out_specs=...]
    ppermute x17 -> x15, starting transfers between devices: 17.4 us -> 17.4 us  [exchange(): return lax.ppermute(x, ('dp', 'cent'), pairs)]
    unnamed x8 -> x6, local copies, waits for them, and re-layouts: 2.64 us -> 2.64 us
  transfers between devices with their start and end apart: 32 -> 28, of which waited for: 15 -> 14; matrix products, arithmetic and copies ran while one was open for 0% -> 0% of each run, Pallas kernels for 20% -> 18%
where the time goes in v14:
time: 95.2 us; the launch traced here: 95 us
  waiting for transfers between devices  37.5 us (39%)
  starting transfers between devices  32.5 us (34%)
  Pallas kernels  21.3 us (22%)
  local copies, waits for them, and re-layouts  2.64 us (3%)
  between operations  0.96 us (1%)
    pallas_call x13, Pallas kernels, call(): pl.pallas_call(kernel, out_shape=out_shape, in_specs=in_specs, out_specs=...  21.3 us
    ppermute x7, waiting for transfers between devices, ring(): lax.ppermute(x, 'dp', [(4 * a + i, 4 * b + i) for a, b in pairs for i in...  20.3 us
    ppermute x15, starting transfers between devices, exchange(): return lax.ppermute(x, ('dp', 'cent'), pairs)  17.4 us
    ppermute x15, waiting for transfers between devices, exchange(): return lax.ppermute(x, ('dp', 'cent'), pairs)  15.1 us
    ppermute x7, starting transfers between devices, ring(): lax.ppermute(x, 'dp', [(4 * a + i, 4 * b + i) for a, b in pairs for i in...  13.1 us
    unnamed x6, local copies, waits for them, and re-layouts  2.64 us
  transfers between devices with their start and end apart: 28, of which 14 were waited for; matrix products, arithmetic and copies ran while one was open for 0% of the time, Pallas kernels for 18%

profile of v14, /device:TPU:0, one launch (start us, length us, event | category | flops | bytes accessed | tf_op | source)
XLA Modules:
  0.0 95.0 jit_solution(4643305909308971852)
XLA Ops:
  0.7 1.0 %copy-done = bf16[1024,256]{1,0:T(8,128)(2,1)S(1)} copy-done((bf16[1024,256]{1,0:T(8,128)(2,1)S(1)}, bf16[1024,256]{1,0:T(8,128)(2,1)}, u32[]{:S(2)}) %copy-start) | copy-done | bytes 524312
  2.4 3.0 %collective-permute-start.1 = (f32[512,256]{1,0:T(8,128)S(1)}, f32[512,256]{1,0:T(8,128)S(1)}, u32[]{:S(2)}, u32[]{:S(2)}) collective-permute-start(f32[512,256]{1,0:T(8,128)S(1)} %open.1), channel_id=1, source_target_pairs={{0,4},{1,3},{2,6},{3,1},{4,0},{5,7},{6,2},{7,5},{8,12},{9,11},{10,... | collective-permute-start | bytes 1572872 | tf_op jit(solution)/shard_map/ppermute | solution.py:315
  5.4 1.5 %collective-permute-start = (f32[512,256]{1,0:T(8,128)S(1)}, f32[512,256]{1,0:T(8,128)S(1)}, u32[]{:S(2)}, u32[]{:S(2)}) collective-permute-start(f32[512,256]{1,0:T(8,128)S(1)} %open.1), channel_id=1, source_target_pairs={{0,2},{1,5},{2,0},{3,7},{4,6},{5,1},{6,4},{7,3},{8,10},{9,13},{10,... | collective-permute-start | bytes 1572872 | tf_op jit(solution)/shard_map/ppermute | solution.py:315
  6.9 1.6 %copy-done.2 = bf16[4096,256]{1,0:T(8,128)(2,1)S(1)} copy-done((bf16[4096,256]{1,0:T(8,128)(2,1)S(1)}, bf16[4096,256]{1,0:T(8,128)(2,1)}, u32[]{:S(2)}) %copy-start.2) | copy-done | bytes 2097176
  8.5 5.9 %stats.1 = (f32[2,1024]{1,0:T(2,128)S(1)}, bf16[1024,256]{1,0:T(8,128)(2,1)S(1)}, f32[1024,128]{1,0:T(8,128)S(1)}) custom-call(s32[2]{0:T(128)S(1)} %pad_add_fusion.where_ref, bf16[1024,256]{1,0:T(8,128)(2,1)S(1)} %copy-done, bf16[4096,256]{1,0:T(8,128)(2,1)S(1)} %copy-done.2), custom_call_target="tpu_custom_call" | custom-call | flops 4294967296 | bytes 2621448 | tf_op jit(solution)/shard_map/stats/pallas_call | solution.py:27
  14.5 1.2 %collective-permute-done.2.refs_1_ = f32[2,1024]{1,0:T(2,128)S(1)} collective-permute-done((f32[2,1024]{1,0:T(2,128)S(1)}, f32[2,1024]{1,0:T(2,128)S(1)}, u32[]{:S(2)}, u32[]{:S(2)}) %collective-permute-start.2) | collective-permute-done | bytes 8224 | tf_op jit(solution)/shard_map/ppermute | solution.py:318
  15.6 2.0 %collective-permute-done.1.b_ref.refs_2_ = f32[512,256]{1,0:T(8,128)S(1)} collective-permute-done((f32[512,256]{1,0:T(8,128)S(1)}, f32[512,256]{1,0:T(8,128)S(1)}, u32[]{:S(2)}, u32[]{:S(2)}) %collective-permute-start.1) | collective-permute-done | bytes 524320 | tf_op jit(solution)/shard_map/ppermute | solution.py:315
  17.6 0.6 lse.1
  18.8 2.5 %collective-permute-start.5 = (f32[264,256]{1,0:T(8,128)S(1)}, f32[264,256]{1,0:T(8,128)S(1)}, u32[]{:S(2)}, u32[]{:S(2)}) collective-permute-start(f32[264,256]{1,0:T(8,128)S(1)} %get-tuple-element.59), channel_id=1, source_target_pairs={{0,4},{1,3},{2,6},{3,1},{4,0},{5,7},{6,2},{7,5},{8,12},{9,11},{10,... | collective-permute-start | bytes 811016 | tf_op jit(solution)/shard_map/ppermute | solution.py:315
  21.3 0.7 collective-permute-start.6
  21.9 1.4 %own.1 = (f32[1024,256]{1,0:T(8,128)S(1)}, f32[1024,128]{1,0:T(8,128)S(1)}) custom-call(bf16[1024,256]{1,0:T(8,128)(2,1)S(1)} %copy-done.1, bf16[1024,256]{1,0:T(8,128)(2,1)S(1)} %get-tuple-element.46.twice_ref, f32[1024,128]{1,0:T(8,128)S(1)} %get-tuple-element.47.norm_ref, f32[4,256]{1,0:T(4,128)S(1)} %get-tuple-element.63.lse_ref), custom_call_target="tpu_custom_call" | custom-call | flops 1073741824 | bytes 1576960 | tf_op jit(solution)/shard_map/own/pallas_call | solution.py:27
  23.4 0.8 collective-permute-start.7
  24.2 4.1 %collective-permute-done.5.refs_4_.refs_0_ = f32[264,256]{1,0:T(8,128)S(1)} collective-permute-done((f32[264,256]{1,0:T(8,128)S(1)}, f32[264,256]{1,0:T(8,128)S(1)}, u32[]{:S(2)}, u32[]{:S(2)}) %collective-permute-start.5) | collective-permute-done | bytes 270368 | tf_op jit(solution)/shard_map/ppermute | solution.py:315
  28.4 0.9 collective-permute-done.7.lse_ref
  29.8 1.4 %lead.1 = (f32[256,256]{1,0:T(8,128)S(1)}, f32[256,128]{1,0:T(8,128)S(1)}) custom-call(s32[2]{0:T(128)S(1)} %pad_add_fusion.where_ref, bf16[1024,256]{1,0:T(8,128)(2,1)S(1)} %get-tuple-element.46.twice_ref, f32[1024,128]{1,0:T(8,128)S(1)} %get-tuple-element.47.norm_ref, f32[1024,256]{1,0:T(8,128)S(1)} %get-tuple-element.64.acc_ref, ...), custom_call_target="tpu_custom_call" | custom-call | flops 536870912 | bytes 5259272 | tf_op jit(solution)/shard_map/lead/pallas_call | solution.py:27
  31.2 1.1 %first.1 = f32[264,256]{1,0:T(8,128)S(1)} custom-call(s32[2]{0:T(128)S(1)} %pad_add_fusion.where_ref, bf16[1024,256]{1,0:T(8,128)(2,1)S(1)} %get-tuple-element.46.twice_ref, f32[1024,128]{1,0:T(8,128)S(1)} %get-tuple-element.47.norm_ref, f32[4,256]{1,0:T(4,128)S(1)} %collective-permute-done.7.lse_ref, f32[256,256]{1,0:T(8,128)S(1)} %get-tuple-element.75.lead_acc_ref, ...), custom_call_target="tpu_custom_call" | custom-call | flops 536870912 | bytes 2527240 | tf_op jit(solution)/shard_map/first/pallas_call | solution.py:27
  32.4 2.6 %collective-permute-start.10 = (f32[264,256]{1,0:T(8,128)S(1)}, f32[264,256]{1,0:T(8,128)S(1)}, u32[]{:S(2)}, u32[]{:S(2)}) collective-permute-start(f32[264,256]{1,0:T(8,128)S(1)} %first.1), channel_id=1, source_target_pairs={{0,16},{2,18},{4,20},{6,22},{16,24},{18,26},{20,28},{22,30},{24,8}... | collective-permute-start | bytes 811016 | tf_op jit(solution)/shard_map/ppermute | solution.py:322
  35.0 1.7 %rest.3 = f32[264,256]{1,0:T(8,128)S(1)} custom-call(s32[2]{0:T(128)S(1)} %pad_add_fusion.where_ref, bf16[1024,256]{1,0:T(8,128)(2,1)S(1)} %get-tuple-element.46.twice_ref, f32[1024,128]{1,0:T(8,128)S(1)} %get-tuple-element.47.norm_ref, f32[1024,256]{1,0:T(8,128)S(1)} %get-tuple-element.64.acc_ref, f32[1024,128]{1,0:T(8,128)S(1)} %get-tuple-element.65.cnt_ref, ...), custom_call_target="tpu_custom_call" | custom-call | flops 805306368 | bytes 5804040 | tf_op jit(solution)/shard_map/rest/pallas_call | solution.py:27
  37.0 2.6 %rest.2 = (f32[264,256]{1,0:T(8,128)S(1)}, f32[264,256]{1,0:T(8,128)S(1)}) custom-call(s32[2]{0:T(128)S(1)} %pad_add_fusion.where_ref, bf16[1024,256]{1,0:T(8,128)(2,1)S(1)} %get-tuple-element.46.twice_ref, f32[1024,128]{1,0:T(8,128)S(1)} %get-tuple-element.47.norm_ref, f32[1024,256]{1,0:T(8,128)S(1)} %get-tuple-element.64.acc_ref, ...), custom_call_target="tpu_custom_call" | custom-call | flops 1610612736 | bytes 5804040 | tf_op jit(solution)/shard_map/rest/pallas_call | solution.py:27
  39.6 2.3 %collective-permute-done.10.b_ref = f32[264,256]{1,0:T(8,128)S(1)} collective-permute-done((f32[264,256]{1,0:T(8,128)S(1)}, f32[264,256]{1,0:T(8,128)S(1)}, u32[]{:S(2)}, u32[]{:S(2)}) %collective-permute-start.10) | collective-permute-done | bytes 270368 | tf_op jit(solution)/shard_map/ppermute | solution.py:322
  41.9 3.4 %collective-permute-start.11 = (f32[264,256]{1,0:T(8,128)S(1)}, f32[264,256]{1,0:T(8,128)S(1)}, u32[]{:S(2)}, u32[]{:S(2)}) collective-permute-start(f32[264,256]{1,0:T(8,128)S(1)} %add.3), channel_id=1, source_target_pairs={{0,16},{2,18},{4,20},{6,22},{16,24},{18,26},{20,28},{22,30},{24,8}... | collective-permute-start | bytes 811016 | tf_op jit(solution)/shard_map/ppermute | solution.py:322
  45.4 4.1 %collective-permute-done.12.second_ref = f32[264,256]{1,0:T(8,128)S(1)} collective-permute-done((f32[264,256]{1,0:T(8,128)S(1)}, f32[264,256]{1,0:T(8,128)S(1)}, u32[]{:S(2)}, u32[]{:S(2)}) %collective-permute-start.12) | collective-permute-done | bytes 270368 | tf_op jit(solution)/shard_map/ppermute | solution.py:322
  49.5 4.9 %collective-permute-done.11.first_ref = f32[264,256]{1,0:T(8,128)S(1)} collective-permute-done((f32[264,256]{1,0:T(8,128)S(1)}, f32[264,256]{1,0:T(8,128)S(1)}, u32[]{:S(2)}, u32[]{:S(2)}) %collective-permute-start.11) | collective-permute-done | bytes 270368 | tf_op jit(solution)/shard_map/ppermute | solution.py:322
  54.4 0.8 finish.1.refs_0_
  55.2 1.7 %collective-permute-start.13 = (f32[264,256]{1,0:T(8,128)S(1)}, f32[264,256]{1,0:T(8,128)S(1)}, u32[]{:S(2)}, u32[]{:S(2)}) collective-permute-start(f32[264,256]{1,0:T(8,128)S(1)} %finish.1.refs_0_), channel_id=1, source_target_pairs={{0,16},{2,18},{4,20},{6,22},{16,24},{18,26},{20,28},{22,30},{24,8}... | collective-permute-start | bytes 811016 | tf_op jit(solution)/shard_map/ppermute | solution.py:322
  56.9 0.9 collective-permute-start.16
  57.8 1.0 %collective-permute-start.18 = (f32[264,256]{1,0:T(8,128)S(1)}, f32[264,256]{1,0:T(8,128)S(1)}, u32[]{:S(2)}, u32[]{:S(2)}) collective-permute-start(f32[264,256]{1,0:T(8,128)S(1)} %finish.1.refs_0_), channel_id=1, source_target_pairs={{0,2},{1,5},{2,0},{3,7},{4,6},{5,1},{6,4},{7,3},{8,10},{9,13},{10,... | collective-permute-start | bytes 811016 | tf_op jit(solution)/shard_map/ppermute | solution.py:315
  58.8 4.8 %collective-permute-done.13.refs_4_ = f32[264,256]{1,0:T(8,128)S(1)} collective-permute-done((f32[264,256]{1,0:T(8,128)S(1)}, f32[264,256]{1,0:T(8,128)S(1)}, u32[]{:S(2)}, u32[]{:S(2)}) %collective-permute-start.13) | collective-permute-done | bytes 270368 | tf_op jit(solution)/shard_map/ppermute | solution.py:322
  63.6 1.8 %collective-permute-start.14 = (f32[264,256]{1,0:T(8,128)S(1)}, f32[264,256]{1,0:T(8,128)S(1)}, u32[]{:S(2)}, u32[]{:S(2)}) collective-permute-start(f32[264,256]{1,0:T(8,128)S(1)} %collective-permute-done.13.refs_4_), channel_id=1, source_target_pairs={{0,16},{2,18},{4,20},{6,22},{16,24},{18,26},{20,28},{22,30},{24,8}... | collective-permute-start | bytes 811016 | tf_op jit(solution)/shard_map/ppermute | solution.py:322
  65.5 0.9 collective-permute-start.17
  66.4 1.0 %collective-permute-start.26 = (f32[264,256]{1,0:T(8,128)S(1)}, f32[264,256]{1,0:T(8,128)S(1)}, u32[]{:S(2)}, u32[]{:S(2)}) collective-permute-start(f32[264,256]{1,0:T(8,128)S(1)} %collective-permute-done.13.refs_4_), channel_id=1, source_target_pairs={{0,2},{1,5},{2,0},{3,7},{4,6},{5,1},{6,4},{7,3},{8,10},{9,13},{10,... | collective-permute-start | bytes 811016 | tf_op jit(solution)/shard_map/ppermute | solution.py:315
  67.4 0.7 collective-permute-start.19
  68.1 3.1 %collective-permute-done.14.refs_8_ = f32[264,256]{1,0:T(8,128)S(1)} collective-permute-done((f32[264,256]{1,0:T(8,128)S(1)}, f32[264,256]{1,0:T(8,128)S(1)}, u32[]{:S(2)}, u32[]{:S(2)}) %collective-permute-start.14) | collective-permute-done | bytes 270368 | tf_op jit(solution)/shard_map/ppermute | solution.py:322
  71.1 2.1 %collective-permute-start.15 = (f32[264,256]{1,0:T(8,128)S(1)}, f32[264,256]{1,0:T(8,128)S(1)}, u32[]{:S(2)}, u32[]{:S(2)}) collective-permute-start(f32[264,256]{1,0:T(8,128)S(1)} %finish.1.refs_0_), channel_id=1, source_target_pairs={{0,8},{2,10},{4,12},{6,14},{16,0},{18,2},{20,4},{22,6},{24,16},{26... | collective-permute-start | bytes 811016 | tf_op jit(solution)/shard_map/ppermute | solution.py:322
  73.2 0.6 collective-permute-start.22
  73.8 1.7 %collective-permute-done.26.refs_5_ = f32[264,256]{1,0:T(8,128)S(1)} collective-permute-done((f32[264,256]{1,0:T(8,128)S(1)}, f32[264,256]{1,0:T(8,128)S(1)}, u32[]{:S(2)}, u32[]{:S(2)}) %collective-permute-start.26) | collective-permute-done | bytes 270368 | tf_op jit(solution)/shard_map/ppermute | solution.py:315
  75.5 0.6 collective-permute-start.27
  76.1 1.4 %collective-permute-start.23 = (f32[264,256]{1,0:T(8,128)S(1)}, f32[264,256]{1,0:T(8,128)S(1)}, u32[]{:S(2)}, u32[]{:S(2)}) collective-permute-start(f32[264,256]{1,0:T(8,128)S(1)} %collective-permute-done.14.refs_8_), channel_id=1, source_target_pairs={{0,4},{1,3},{2,6},{3,1},{4,0},{5,7},{6,2},{7,5},{8,12},{9,11},{10,... | collective-permute-start | bytes 811016 | tf_op jit(solution)/shard_map/ppermute | solution.py:315
  77.5 1.2 %collective-permute-done.15.refs_9_ = f32[264,256]{1,0:T(8,128)S(1)} collective-permute-done((f32[264,256]{1,0:T(8,128)S(1)}, f32[264,256]{1,0:T(8,128)S(1)}, u32[]{:S(2)}, u32[]{:S(2)}) %collective-permute-start.15) | collective-permute-done | bytes 270368 | tf_op jit(solution)/shard_map/ppermute | solution.py:322
  78.6 1.2 %collective-permute-start.25 = (f32[264,256]{1,0:T(8,128)S(1)}, f32[264,256]{1,0:T(8,128)S(1)}, u32[]{:S(2)}, u32[]{:S(2)}) collective-permute-start(f32[264,256]{1,0:T(8,128)S(1)} %collective-permute-done.19.refs_3_), channel_id=1, source_target_pairs={{0,8},{2,10},{4,12},{6,14},{16,0},{18,2},{20,4},{22,6},{24,16},{26... | collective-permute-start | bytes 811016 | tf_op jit(solution)/shard_map/ppermute | solution.py:322
  79.8 2.8 %collective-permute-done.22.refs_0_ = f32[264,256]{1,0:T(8,128)S(1)} collective-permute-done((f32[264,256]{1,0:T(8,128)S(1)}, f32[264,256]{1,0:T(8,128)S(1)}, u32[]{:S(2)}, u32[]{:S(2)}) %collective-permute-start.22) | collective-permute-done | bytes 270368 | tf_op jit(solution)/shard_map/ppermute | solution.py:315
  82.6 0.9 collective-permute-start.24
  83.5 1.1 %collective-permute-start.21 = (f32[264,256]{1,0:T(8,128)S(1)}, f32[264,256]{1,0:T(8,128)S(1)}, u32[]{:S(2)}, u32[]{:S(2)}) collective-permute-start(f32[264,256]{1,0:T(8,128)S(1)} %collective-permute-done.15.refs_9_), channel_id=1, source_target_pairs={{0,4},{1,3},{2,6},{3,1},{4,0},{5,7},{6,2},{7,5},{8,12},{9,11},{10,... | collective-permute-start | bytes 811016 | tf_op jit(solution)/shard_map/ppermute | solution.py:315
  85.2 2.1 %place_early.1 = (f32[4096,256]{1,0:T(8,128)}, f32[32,128]{1,0:T(8,128)S(1)}) custom-call(s32[2]{0:T(128)S(1)} %pad_add_fusion.where_ref, f32[264,256]{1,0:T(8,128)S(1)} %finish.1.refs_0_, f32[264,256]{1,0:T(8,128)S(1)} %collective-permute-done.18.refs_1_, f32[264,256]{1,0:T(8,128)S(1)} %collective-permute-done.16.refs_2_, ...), custom_call_target="tpu_custom_call" | custom-call | bytes 2703368 | tf_op jit(solution)/shard_map/place_early/pallas_call | solution.py:27
  87.4 3.2 %collective-permute-done.24.refs_2_ = f32[264,256]{1,0:T(8,128)S(1)} collective-permute-done((f32[264,256]{1,0:T(8,128)S(1)}, f32[264,256]{1,0:T(8,128)S(1)}, u32[]{:S(2)}, u32[]{:S(2)}) %collective-permute-start.24) | collective-permute-done | bytes 270368 | tf_op jit(solution)/shard_map/ppermute | solution.py:315
  90.6 1.6 %place_middle.1 = (f32[4096,256]{1,0:T(8,128)}, f32[32,128]{1,0:T(8,128)S(1)}) custom-call(s32[2]{0:T(128)S(1)} %pad_add_fusion.where_ref, f32[264,256]{1,0:T(8,128)S(1)} %collective-permute-done.22.refs_0_, f32[264,256]{1,0:T(8,128)S(1)} %collective-permute-done.23.refs_1_, ...), custom_call_target="tpu_custom_call", output_to_operand_aliasing={{0}: (6, {})} | custom-call | bytes 5292040 | tf_op jit(solution)/shard_map/place_middle/pallas_call | solution.py:27
  92.2 1.3 %collective-permute-done.21.refs_1_ = f32[264,256]{1,0:T(8,128)S(1)} collective-permute-done((f32[264,256]{1,0:T(8,128)S(1)}, f32[264,256]{1,0:T(8,128)S(1)}, u32[]{:S(2)}, u32[]{:S(2)}) %collective-permute-start.21) | collective-permute-done | bytes 270368 | tf_op jit(solution)/shard_map/ppermute | solution.py:315
  93.5 1.4 %place_late.1 = (f32[4096,256]{1,0:T(8,128)}, f32[32,128]{1,0:T(8,128)}) custom-call(s32[2]{0:T(128)S(1)} %pad_add_fusion.where_ref, f32[264,256]{1,0:T(8,128)S(1)} %collective-permute-done.20.refs_0_, f32[264,256]{1,0:T(8,128)S(1)} %collective-permute-done.21.refs_1_, f32[32,128]{1,0:T(8,128)S(1)} %get-tuple-element.84.refs_2_, ...), custom_call_target="tpu_custom_call", output_to_operand_aliasing={{0}: (4, {})} | custom-call | bytes 4751368 | tf_op jit(solution)/shard_map/place_late/pallas_call | solution.py:27
  (28 shorter events, 2.6 us)
Async XLA Ops:
  0.7 1.0 %copy-start = (bf16[1024,256]{1,0:T(8,128)(2,1)S(1)}, bf16[1024,256]{1,0:T(8,128)(2,1)}, u32[]{:S(2)}) copy-start(bf16[1024,256]{1,0:T(8,128)(2,1)} %points_ref.5) | copy-start | bytes 1572868
  2.3 19.6 %copy-start.1 = (bf16[1024,256]{1,0:T(8,128)(2,1)S(1)}, bf16[1024,256]{1,0:T(8,128)(2,1)}, u32[]{:S(2)}) copy-start(bf16[1024,256]{1,0:T(8,128)(2,1)} %points_ref.5) | copy-start | bytes 1572868
  2.4 15.3 %collective-permute-start.1 = (f32[512,256]{1,0:T(8,128)S(1)}, f32[512,256]{1,0:T(8,128)S(1)}, u32[]{:S(2)}, u32[]{:S(2)}) collective-permute-start(f32[512,256]{1,0:T(8,128)S(1)} %open.1), channel_id=1, source_target_pairs={{0,4},{1,3},{2,6},{3,1},{4,0},{5,7},{6,2},{7,5},{8,12},{9,11},{10,... | collective-permute-start | bytes 1572872 | tf_op jit(solution)/shard_map/ppermute | solution.py:315
  5.4 12.3 %collective-permute-start = (f32[512,256]{1,0:T(8,128)S(1)}, f32[512,256]{1,0:T(8,128)S(1)}, u32[]{:S(2)}, u32[]{:S(2)}) collective-permute-start(f32[512,256]{1,0:T(8,128)S(1)} %open.1), channel_id=1, source_target_pairs={{0,2},{1,5},{2,0},{3,7},{4,6},{5,1},{6,4},{7,3},{8,10},{9,13},{10,... | collective-permute-start | bytes 1572872 | tf_op jit(solution)/shard_map/ppermute | solution.py:315
  6.9 1.6 %copy-start.2 = (bf16[4096,256]{1,0:T(8,128)(2,1)S(1)}, bf16[4096,256]{1,0:T(8,128)(2,1)}, u32[]{:S(2)}) copy-start(bf16[4096,256]{1,0:T(8,128)(2,1)} %c_ref.1) | copy-start | bytes 6291460
  14.4 1.2 %collective-permute-start.2 = (f32[2,1024]{1,0:T(2,128)S(1)}, f32[2,1024]{1,0:T(2,128)S(1)}, u32[]{:S(2)}, u32[]{:S(2)}) collective-permute-start(f32[2,1024]{1,0:T(2,128)S(1)} %get-tuple-element.48.refs_0_), channel_id=1, source_target_pairs={{0,1},{1,0},{2,3},{3,2},{4,5},{5,4},{6,7},{7,6},{8,9},{9,8},{10,11... | collective-permute-start | bytes 24584 | tf_op jit(solution)/shard_map/ppermute | solution.py:318
  18.3 5.1 %collective-permute-start.3 = (f32[512,256]{1,0:T(8,128)S(1)}, f32[512,256]{1,0:T(8,128)S(1)}, u32[]{:S(2)}, u32[]{:S(2)}) collective-permute-start(f32[512,256]{1,0:T(8,128)S(1)} %collective-permute-done.a_ref.refs_0_), channel_id=1, source_target_pairs={{0,1},{1,0},{2,3},{3,2},{4,5},{5,4},{6,7},{7,6},{8,9},{9,8},{10,11... | collective-permute-start | bytes 1572872 | tf_op jit(solution)/shard_map/ppermute | solution.py:318
  18.6 4.8 %collective-permute-start.4 = (f32[512,256]{1,0:T(8,128)S(1)}, f32[512,256]{1,0:T(8,128)S(1)}, u32[]{:S(2)}, u32[]{:S(2)}) collective-permute-start(f32[512,256]{1,0:T(8,128)S(1)} %collective-permute-done.1.b_ref.refs_2_), channel_id=1, source_target_pairs={{0,1},{1,0},{2,3},{3,2},{4,5},{5,4},{6,7},{7,6},{8,9},{9,8},{10,11... | collective-permute-start | bytes 1572872 | tf_op jit(solution)/shard_map/ppermute | solution.py:318
  18.8 9.6 %collective-permute-start.5 = (f32[264,256]{1,0:T(8,128)S(1)}, f32[264,256]{1,0:T(8,128)S(1)}, u32[]{:S(2)}, u32[]{:S(2)}) collective-permute-start(f32[264,256]{1,0:T(8,128)S(1)} %get-tuple-element.59), channel_id=1, source_target_pairs={{0,4},{1,3},{2,6},{3,1},{4,0},{5,7},{6,2},{7,5},{8,12},{9,11},{10,... | collective-permute-start | bytes 811016 | tf_op jit(solution)/shard_map/ppermute | solution.py:315
  21.3 7.1 %collective-permute-start.6 = (f32[264,256]{1,0:T(8,128)S(1)}, f32[264,256]{1,0:T(8,128)S(1)}, u32[]{:S(2)}, u32[]{:S(2)}) collective-permute-start(f32[264,256]{1,0:T(8,128)S(1)} %get-tuple-element.60), channel_id=1, source_target_pairs={{0,2},{1,5},{2,0},{3,7},{4,6},{5,1},{6,4},{7,3},{8,10},{9,13},{10,... | collective-permute-start | bytes 811016 | tf_op jit(solution)/shard_map/ppermute | solution.py:315
  23.4 5.9 %collective-permute-start.7 = (f32[4,256]{1,0:T(4,128)S(1)}, f32[4,256]{1,0:T(4,128)S(1)}, u32[]{:S(2)}, u32[]{:S(2)}) collective-permute-start(f32[4,256]{1,0:T(4,128)S(1)} %get-tuple-element.63.lse_ref), channel_id=1, source_target_pairs={{0,6},{2,4},{4,2},{6,0},{8,14},{10,12},{12,10},{14,8},{16,22},{18,... | collective-permute-start | bytes 12296 | tf_op jit(solution)/shard_map/ppermute | solution.py:354
  29.3 1.9 %collective-permute-start.8 = (f32[264,256]{1,0:T(8,128)S(1)}, f32[264,256]{1,0:T(8,128)S(1)}, u32[]{:S(2)}, u32[]{:S(2)}) collective-permute-start(f32[264,256]{1,0:T(8,128)S(1)} %collective-permute-done.5.refs_4_.refs_0_), channel_id=1, source_target_pairs={{0,1},{1,0},{2,3},{3,2},{4,5},{5,4},{6,7},{7,6},{8,9},{9,8},{10,11... | collective-permute-start | bytes 811016 | tf_op jit(solution)/shard_map/ppermute | solution.py:318
  29.3 1.9 %collective-permute-start.9 = (f32[264,256]{1,0:T(8,128)S(1)}, f32[264,256]{1,0:T(8,128)S(1)}, u32[]{:S(2)}, u32[]{:S(2)}) collective-permute-start(f32[264,256]{1,0:T(8,128)S(1)} %collective-permute-done.6.refs_6_.refs_5_.refs_2_), channel_id=1, source_target_pairs={{0,1},{1,0},{2,3},{3,2},{4,5},{5,4},{6,7},{7,6},{8,9},{9,8},{10,11... | collective-permute-start | bytes 811016 | tf_op jit(solution)/shard_map/ppermute | solution.py:318
  32.4 9.5 %collective-permute-start.10 = (f32[264,256]{1,0:T(8,128)S(1)}, f32[264,256]{1,0:T(8,128)S(1)}, u32[]{:S(2)}, u32[]{:S(2)}) collective-permute-start(f32[264,256]{1,0:T(8,128)S(1)} %first.1), channel_id=1, source_target_pairs={{0,16},{2,18},{4,20},{6,22},{16,24},{18,26},{20,28},{22,30},{24,8}... | collective-permute-start | bytes 811016 | tf_op jit(solution)/shard_map/ppermute | solution.py:322
  36.7 12.8 %collective-permute-start.12 = (f32[264,256]{1,0:T(8,128)S(1)}, f32[264,256]{1,0:T(8,128)S(1)}, u32[]{:S(2)}, u32[]{:S(2)}) collective-permute-start(f32[264,256]{1,0:T(8,128)S(1)} %rest.3), channel_id=1, source_target_pairs={{0,8},{2,10},{4,12},{6,14},{16,0},{18,2},{20,4},{22,6},{24,16},{26... | collective-permute-start | bytes 811016 | tf_op jit(solution)/shard_map/ppermute | solution.py:322
  41.9 12.5 %collective-permute-start.11 = (f32[264,256]{1,0:T(8,128)S(1)}, f32[264,256]{1,0:T(8,128)S(1)}, u32[]{:S(2)}, u32[]{:S(2)}) collective-permute-start(f32[264,256]{1,0:T(8,128)S(1)} %add.3), channel_id=1, source_target_pairs={{0,16},{2,18},{4,20},{6,22},{16,24},{18,26},{20,28},{22,30},{24,8}... | collective-permute-start | bytes 811016 | tf_op jit(solution)/shard_map/ppermute | solution.py:322
  55.2 8.4 %collective-permute-start.13 = (f32[264,256]{1,0:T(8,128)S(1)}, f32[264,256]{1,0:T(8,128)S(1)}, u32[]{:S(2)}, u32[]{:S(2)}) collective-permute-start(f32[264,256]{1,0:T(8,128)S(1)} %finish.1.refs_0_), channel_id=1, source_target_pairs={{0,16},{2,18},{4,20},{6,22},{16,24},{18,26},{20,28},{22,30},{24,8}... | collective-permute-start | bytes 811016 | tf_op jit(solution)/shard_map/ppermute | solution.py:322
  56.9 8.6 %collective-permute-start.16 = (f32[264,256]{1,0:T(8,128)S(1)}, f32[264,256]{1,0:T(8,128)S(1)}, u32[]{:S(2)}, u32[]{:S(2)}) collective-permute-start(f32[264,256]{1,0:T(8,128)S(1)} %finish.1.refs_0_), channel_id=1, source_target_pairs={{0,4},{1,3},{2,6},{3,1},{4,0},{5,7},{6,2},{7,5},{8,12},{9,11},{10,... | collective-permute-start | bytes 811016 | tf_op jit(solution)/shard_map/ppermute | solution.py:315
  57.8 9.6 %collective-permute-start.18 = (f32[264,256]{1,0:T(8,128)S(1)}, f32[264,256]{1,0:T(8,128)S(1)}, u32[]{:S(2)}, u32[]{:S(2)}) collective-permute-start(f32[264,256]{1,0:T(8,128)S(1)} %finish.1.refs_0_), channel_id=1, source_target_pairs={{0,2},{1,5},{2,0},{3,7},{4,6},{5,1},{6,4},{7,3},{8,10},{9,13},{10,... | collective-permute-start | bytes 811016 | tf_op jit(solution)/shard_map/ppermute | solution.py:315
  63.6 7.5 %collective-permute-start.14 = (f32[264,256]{1,0:T(8,128)S(1)}, f32[264,256]{1,0:T(8,128)S(1)}, u32[]{:S(2)}, u32[]{:S(2)}) collective-permute-start(f32[264,256]{1,0:T(8,128)S(1)} %collective-permute-done.13.refs_4_), channel_id=1, source_target_pairs={{0,16},{2,18},{4,20},{6,22},{16,24},{18,26},{20,28},{22,30},{24,8}... | collective-permute-start | bytes 811016 | tf_op jit(solution)/shard_map/ppermute | solution.py:322
  65.5 7.7 %collective-permute-start.17 = (f32[264,256]{1,0:T(8,128)S(1)}, f32[264,256]{1,0:T(8,128)S(1)}, u32[]{:S(2)}, u32[]{:S(2)}) collective-permute-start(f32[264,256]{1,0:T(8,128)S(1)} %collective-permute-done.13.refs_4_), channel_id=1, source_target_pairs={{0,4},{1,3},{2,6},{3,1},{4,0},{5,7},{6,2},{7,5},{8,12},{9,11},{10,... | collective-permute-start | bytes 811016 | tf_op jit(solution)/shard_map/ppermute | solution.py:315
  66.4 9.1 %collective-permute-start.26 = (f32[264,256]{1,0:T(8,128)S(1)}, f32[264,256]{1,0:T(8,128)S(1)}, u32[]{:S(2)}, u32[]{:S(2)}) collective-permute-start(f32[264,256]{1,0:T(8,128)S(1)} %collective-permute-done.13.refs_4_), channel_id=1, source_target_pairs={{0,2},{1,5},{2,0},{3,7},{4,6},{5,1},{6,4},{7,3},{8,10},{9,13},{10,... | collective-permute-start | bytes 811016 | tf_op jit(solution)/shard_map/ppermute | solution.py:315
  67.4 10.1 %collective-permute-start.19 = (f32[264,256]{1,0:T(8,128)S(1)}, f32[264,256]{1,0:T(8,128)S(1)}, u32[]{:S(2)}, u32[]{:S(2)}) collective-permute-start(f32[264,256]{1,0:T(8,128)S(1)} %collective-permute-done.18.refs_1_), channel_id=1, source_target_pairs={{0,4},{1,3},{2,6},{3,1},{4,0},{5,7},{6,2},{7,5},{8,12},{9,11},{10,... | collective-permute-start | bytes 811016 | tf_op jit(solution)/shard_map/ppermute | solution.py:315
  71.1 7.5 %collective-permute-start.15 = (f32[264,256]{1,0:T(8,128)S(1)}, f32[264,256]{1,0:T(8,128)S(1)}, u32[]{:S(2)}, u32[]{:S(2)}) collective-permute-start(f32[264,256]{1,0:T(8,128)S(1)} %finish.1.refs_0_), channel_id=1, source_target_pairs={{0,8},{2,10},{4,12},{6,14},{16,0},{18,2},{20,4},{22,6},{24,16},{26... | collective-permute-start | bytes 811016 | tf_op jit(solution)/shard_map/ppermute | solution.py:322
  73.2 9.4 %collective-permute-start.22 = (f32[264,256]{1,0:T(8,128)S(1)}, f32[264,256]{1,0:T(8,128)S(1)}, u32[]{:S(2)}, u32[]{:S(2)}) collective-permute-start(f32[264,256]{1,0:T(8,128)S(1)} %collective-permute-done.14.refs_8_), channel_id=1, source_target_pairs={{0,2},{1,5},{2,0},{3,7},{4,6},{5,1},{6,4},{7,3},{8,10},{9,13},{10,... | collective-permute-start | bytes 811016 | tf_op jit(solution)/shard_map/ppermute | solution.py:315
  75.5 9.2 %collective-permute-start.27 = (f32[264,256]{1,0:T(8,128)S(1)}, f32[264,256]{1,0:T(8,128)S(1)}, u32[]{:S(2)}, u32[]{:S(2)}) collective-permute-start(f32[264,256]{1,0:T(8,128)S(1)} %collective-permute-done.26.refs_5_), channel_id=1, source_target_pairs={{0,4},{1,3},{2,6},{3,1},{4,0},{5,7},{6,2},{7,5},{8,12},{9,11},{10,... | collective-permute-start | bytes 811016 | tf_op jit(solution)/shard_map/ppermute | solution.py:315
  76.1 11.3 %collective-permute-start.23 = (f32[264,256]{1,0:T(8,128)S(1)}, f32[264,256]{1,0:T(8,128)S(1)}, u32[]{:S(2)}, u32[]{:S(2)}) collective-permute-start(f32[264,256]{1,0:T(8,128)S(1)} %collective-permute-done.14.refs_8_), channel_id=1, source_target_pairs={{0,4},{1,3},{2,6},{3,1},{4,0},{5,7},{6,2},{7,5},{8,12},{9,11},{10,... | collective-permute-start | bytes 811016 | tf_op jit(solution)/shard_map/ppermute | solution.py:315
  78.6 8.7 %collective-permute-start.25 = (f32[264,256]{1,0:T(8,128)S(1)}, f32[264,256]{1,0:T(8,128)S(1)}, u32[]{:S(2)}, u32[]{:S(2)}) collective-permute-start(f32[264,256]{1,0:T(8,128)S(1)} %collective-permute-done.19.refs_3_), channel_id=1, source_target_pairs={{0,8},{2,10},{4,12},{6,14},{16,0},{18,2},{20,4},{22,6},{24,16},{26... | collective-permute-start | bytes 811016 | tf_op jit(solution)/shard_map/ppermute | solution.py:322
  82.6 8.0 %collective-permute-start.24 = (f32[264,256]{1,0:T(8,128)S(1)}, f32[264,256]{1,0:T(8,128)S(1)}, u32[]{:S(2)}, u32[]{:S(2)}) collective-permute-start(f32[264,256]{1,0:T(8,128)S(1)} %collective-permute-done.22.refs_0_), channel_id=1, source_target_pairs={{0,4},{1,3},{2,6},{3,1},{4,0},{5,7},{6,2},{7,5},{8,12},{9,11},{10,... | collective-permute-start | bytes 811016 | tf_op jit(solution)/shard_map/ppermute | solution.py:315
  83.5 10.0 %collective-permute-start.21 = (f32[264,256]{1,0:T(8,128)S(1)}, f32[264,256]{1,0:T(8,128)S(1)}, u32[]{:S(2)}, u32[]{:S(2)}) collective-permute-start(f32[264,256]{1,0:T(8,128)S(1)} %collective-permute-done.15.refs_9_), channel_id=1, source_target_pairs={{0,4},{1,3},{2,6},{3,1},{4,0},{5,7},{6,2},{7,5},{8,12},{9,11},{10,... | collective-permute-start | bytes 811016 | tf_op jit(solution)/shard_map/ppermute | solution.py:315
  84.7 8.8 %collective-permute-start.20 = (f32[264,256]{1,0:T(8,128)S(1)}, f32[264,256]{1,0:T(8,128)S(1)}, u32[]{:S(2)}, u32[]{:S(2)}) collective-permute-start(f32[264,256]{1,0:T(8,128)S(1)} %collective-permute-done.15.refs_9_), channel_id=1, source_target_pairs={{0,2},{1,5},{2,0},{3,7},{4,6},{5,1},{6,4},{7,3},{8,10},{9,13},{10,... | collective-permute-start | bytes 811016 | tf_op jit(solution)/shard_map/ppermute | solution.py:315

commit v15 on v14

--- a/solution.py
+++ b/solution.py
@@ -103,9 +103,9 @@
     )
 
 
-def lse_kernel(cores, every, a_ref, b_ref, *refs):
+def lse_kernel(cores, every, *refs):
     pair_refs = refs[:cores]
-    lse_ref, evidence_ref, pack_a_ref, pack_b_ref = refs[cores:]
+    lse_ref, evidence_ref = refs[cores:]
     half = lse_ref.shape[1]
     top = functools.reduce(jnp.maximum, [p[0:1, :] for p in pair_refs])
     total = functools.reduce(jnp.add, [p[1:2, :] * jnp.exp(p[0:1, :] - top) for p in pair_refs])
@@ -115,10 +115,12 @@
         evidence_ref[k : k + 1, :] = evidence[:, k * LANES : (k + 1) * LANES]
     for i in range(2 * cores):
         lse_ref[i : i + 1, :] = lse[:, i * half : (i + 1) * half]
-    for piece, pack_ref in ((a_ref[0:half, :], pack_a_ref), (b_ref[half:, :], pack_b_ref)):
-        pack_ref[0:half, :] = piece
-        pack_ref[half:, :] = jnp.zeros_like(pack_ref[half:, :])
-        pack_ref[half : half + 2 * cores, 0:half] = lse_ref[...]
+
+
+def halves_kernel(a_ref, b_ref, first_ref, second_ref):
+    half = first_ref.shape[0]
+    first_ref[...] = a_ref[0:half, :]
+    second_ref[...] = b_ref[half:, :]
 
 
 def weigh(twice, norm, x, lse, lanes):
@@ -151,20 +153,10 @@
             cnt_ref[...] += counted
 
 
-def near_rows(cores, half, core, refs, d0_ref, d1_ref):
-    for kind in range(2):
-        for rc in range(cores):
-            tail_ref = d1_ref if (kind + rc) % 2 == 0 else d0_ref
-            at = half + 2 * (core ^ rc)
-            yield (lambda ref=refs[kind * cores + rc]: ref[...]), (
-                lambda at=at, tail_ref=tail_ref: two_rows(tail_ref, at, half)
-            )
-
-
 def far_rows(cores, half, core, refs, lse_ref):
     for rc in range(cores):
         yield (
-            lambda rc=rc: jnp.concatenate([refs[rc][0:half, :], refs[cores + rc][0:half, :]], axis=0)
+            lambda rc=rc: jnp.concatenate([refs[rc][...], refs[cores + rc][...]], axis=0)
         ), (lambda at=2 * (core ^ rc): two_rows(lse_ref, at, half))
 
 
@@ -184,61 +176,35 @@
     out_ref[size : size + 8, :] = jnp.broadcast_to(turned, (8, width))
 
 
-def lead_kernel(cores, order, half, where_ref, twice_ref, norm_ref, acc_ref, cnt_ref, *refs):
-    out_acc_ref, out_cnt_ref = refs[-2:]
-    near, (d0_ref, d1_ref) = refs[: 2 * cores], refs[2 * cores : 2 * cores + 2]
-    size = out_acc_ref.shape[0]
-    place = ahead(order, lax.div(where_ref[0], 4), len(order) // 2)
-    at = pl.ds(pl.multiple_of(place * size, size), size)
-    out_acc_ref[...], out_cnt_ref[...] = add_rows(
-        near_rows(cores, half, where_ref[1], near, d0_ref, d1_ref),
-        half,
-        twice_ref[at, :],
-        norm_ref[at, :],
-        acc_ref[at, :],
-        cnt_ref[at, :],
-    )
-
-
-def block_sums(cores, order, half, steps, where_ref, twice_ref, norm_ref, acc_ref, cnt_ref, lse_ref, near, far, out_ref):
-    size = out_ref.shape[0] - 8
-    place = ahead(order, lax.div(where_ref[0], 4), steps)
-    at = pl.ds(pl.multiple_of(place * size, size), size)
-    twice, norm = twice_ref[at, :], norm_ref[at, :]
-    acc, cnt = add_rows(
-        near_rows(cores, half, where_ref[1], near, far[0], far[cores]),
-        half,
-        twice,
-        norm,
-        acc_ref[at, :],
-        cnt_ref[at, :],
-    )
-    acc, cnt = add_rows(far_rows(cores, half, where_ref[1], far, lse_ref), half, twice, norm, acc, cnt)
-    store_sums(out_ref, acc, cnt)
-
-
-def first_kernel(cores, order, half, where_ref, twice_ref, norm_ref, lse_ref, lead_acc_ref, lead_cnt_ref, *refs):
-    far, out_ref = refs[: 2 * cores], refs[2 * cores]
-    size = lead_acc_ref.shape[0]
-    place = ahead(order, lax.div(where_ref[0], 4), len(order) // 2)
-    at = pl.ds(pl.multiple_of(place * size, size), size)
-    acc, cnt = add_rows(
-        far_rows(cores, half, where_ref[1], far, lse_ref),
-        half,
-        twice_ref[at, :],
-        norm_ref[at, :],
-        lead_acc_ref[...],
-        lead_cnt_ref[...],
-    )
-    store_sums(out_ref, acc, cnt)
-
-
-def rest_kernel(cores, order, half, steps, where_ref, twice_ref, norm_ref, acc_ref, cnt_ref, lse_ref, *refs):
-    near, far = refs[: 2 * cores], refs[2 * cores : 4 * cores]
-    for s, out_ref in zip(steps, refs[4 * cores :]):
-        block_sums(
-            cores, order, half, s, where_ref, twice_ref, norm_ref, acc_ref, cnt_ref, lse_ref, near, far, out_ref
+def near_kernel(cores, half, where_ref, twice_ref, norm_ref, acc_in_ref, cnt_in_ref, lse_a_ref, lse_b_ref, *refs):
+    acc_ref, cnt_ref = refs[2 * cores :]
+    acc_ref[...] = acc_in_ref[...]
+    cnt_ref[...] = cnt_in_ref[...]
+    for kind in range(2):
+        for rc in range(cores):
+            lse_ref = lse_a_ref if (kind + rc) % 2 == 0 else lse_b_ref
+            lse = two_rows(lse_ref, 2 * (where_ref[1] ^ rc), half)
+            x = refs[kind * cores + rc][...].astype(jnp.bfloat16)
+            part, counted = weigh(twice_ref[...], norm_ref[...], x, lse, cnt_ref.shape[1])
+            acc_ref[...] += part
+            cnt_ref[...] += counted
+
+
+def far_kernel(cores, order, half, steps, where_ref, twice_ref, norm_ref, acc_ref, cnt_ref, lse_ref, *refs):
+    far, out_refs = refs[: 2 * cores], refs[2 * cores :]
+    line = lax.div(where_ref[0], 4)
+    for s, out_ref in zip(steps, out_refs):
+        size = out_ref.shape[0] - 8
+        at = pl.ds(pl.multiple_of(ahead(order, line, s) * size, size), size)
+        acc, cnt = add_rows(
+            far_rows(cores, half, where_ref[1], far, lse_ref),
+            half,
+            twice_ref[at, :],
+            norm_ref[at, :],
+            acc_ref[at, :],
+            cnt_ref[at, :],
         )
+        store_sums(out_ref, acc, cnt)
 
 
 def ahead(order, line, steps):
@@ -329,69 +295,64 @@
 
     pair, twice, norm = stats(where, points, centroids, lines)
     pairs = [pair] + [flip_core(pair, rc) for rc in range(1, cores)]
-    tail = max(8, 2 * cores)
-    lse, log_evidence, pack_a, pack_b = call(
+    lse, log_evidence = call(
         functools.partial(lse_kernel, cores, local_cent * cores),
-        (f32(2 * cores, half), f32(rows // LANES, LANES), f32(half + tail, width), f32(half + tail, width)),
-        [VMEM] * (2 + cores),
-        (by_a, by_b, *pairs),
+        (f32(2 * cores, half), f32(rows // LANES, LANES)),
+        [VMEM] * cores,
+        pairs,
         "lse",
     )
-    d0, d1 = exchange(pack_a, 1), exchange(pack_b, 0)
-
-    by_a, by_b, lse = lax.optimization_barrier((by_a, by_b, lse))
-    near = with_siblings((by_a, by_b))
+    lse_a, lse_b = exchange(lse, 0), exchange(lse, 1)
+    first_a, second_b = call(
+        halves_kernel, (f32(half, width), f32(half, width)), [VMEM] * 2, (by_a, by_b), "halves"
+    )
+    d0, d1 = exchange(first_a, 1), exchange(second_b, 0)
+
     lanes = min(LANES, half)
+    acc_shape, cnt_shape = f32(share, width), f32(share, lanes)
     acc, cnt = call(
         functools.partial(own_kernel, cores),
-        (f32(share, width), f32(share, lanes)),
+        (acc_shape, cnt_shape),
         [VMEM] * 4,
         (points, twice, norm, lse),
         "own",
         flops=4 * share * width * rows,
     )
-    lse, acc, cnt, near = lax.optimization_barrier((lse, acc, cnt, near))
     lse_d = lax.ppermute(lse, "dp", [(i, i ^ 3) for i in range(n)])
-    near, d0, d1, acc, cnt, lse_d = lax.optimization_barrier((near, d0, d1, acc, cnt, lse_d))
-    lead = call(
-        functools.partial(lead_kernel, cores, order, half),
-        (f32(size, width), f32(size, lanes)),
+    by_a, by_b, lse_a, lse_b, lse_d = lax.optimization_barrier((by_a, by_b, lse_a, lse_b, lse_d))
+    near = with_siblings((by_a, by_b))
+    acc, cnt = call(
+        functools.partial(near_kernel, cores, half),
+        (acc_shape, cnt_shape),
         [SMEM] + [VMEM] * (6 + 2 * cores),
-        (where, twice, norm, acc, cnt, *near, d0, d1),
-        "lead",
-        flops=4 * size * width * 2 * rows,
-    )
-    given = (where, twice, norm, acc, cnt, lse_d)
+        (where, twice, norm, acc, cnt, lse_a, lse_b, *near),
+        "near",
+        flops=4 * share * width * 2 * rows,
+        aliases={3: 0, 4: 1},
+    )
+    d0, d1, acc, cnt = lax.optimization_barrier((d0, d1, acc, cnt))
     far = with_siblings((d0, d1))
-    rows_given = (*near, *far)
     block_sum = f32(size + 8, width)
     turn = lines // 2
     forward = list(range(turn - 1, 0, -1))
     backward = [lines - s for s in range(turn - 1, 0, -1)]
-    first = call(
-        functools.partial(first_kernel, cores, order, half),
-        block_sum,
-        [SMEM] + [VMEM] * (5 + 2 * cores),
-        (where, twice, norm, lse_d, *lead, *far),
-        "first",
-        flops=4 * size * width * 2 * rows,
-    )
-
-    def sums_of(steps):
+
+    def sums_of(steps, name):
         made = call(
-            functools.partial(rest_kernel, cores, order, half, steps),
+            functools.partial(far_kernel, cores, order, half, steps),
             [block_sum] * len(steps),
-            [SMEM] + [VMEM] * (5 + 4 * cores),
-            (*given, *rows_given),
-            "rest",
-            flops=4 * size * width * 3 * rows * len(steps),
+            [SMEM] + [VMEM] * (5 + 2 * cores),
+            (where, twice, norm, acc, cnt, lse_d, *far),
+            name,
+            flops=4 * size * width * rows * len(steps),
         )
         return dict(zip(steps, made))
 
     def plus(a, b):
         return call(add_kernel, block_sum, [VMEM] * 2, (a, b), "add")
 
-    sums = {**sums_of(backward), **sums_of(forward + [0])}
+    first = sums_of([turn], "first")[turn]
+    sums = {**sums_of(backward, "second"), **sums_of(forward + [0], "rest")}
     from_ahead = ring(sums[backward[0]], -1)
     for s in backward[1:]:
         from_ahead = ring(plus(sums[s], from_ahead), -1)

time: 95.2 us -> 97.4 us (1.023)
  starting transfers between devices: 32.5 us -> 35.4 us
    ppermute x15 -> x17, starting transfers between devices: 17.4 us -> 21.3 us  [exchange(): return lax.ppermute(x, ('dp', 'cent'), pairs)]
    ppermute x15 -> x17, waiting for transfers between devices: 15.1 us -> 11.7 us  [exchange(): return lax.ppermute(x, ('dp', 'cent'), pairs)]
    ppermute x5, waiting for transfers between devices: 1.17 us -> 2.56 us  [flip_core(): return lax.ppermute(x, 'cent', [(i, i ^ bits) for i in range(cores)])]
    ppermute x7, waiting for transfers between devices: 20.3 us -> 21.5 us  [ring(): lax.ppermute(x, 'dp', [(4 * a + i, 4 * b + i) for a, b in pairs for i in...]
    pallas_call x13 -> x14, Pallas kernels: 21.3 us -> 21.4 us  [call(): pl.pallas_call(kernel, out_shape=out_shape, in_specs=in_specs, out_specs=...]
  transfers between devices with their start and end apart: 28 -> 30, of which waited for: 14 -> 17; matrix products, arithmetic and copies ran while one was open for 0% -> 0% of each run, Pallas kernels for 18% -> 18%
where the time goes in v15:
time: 97.4 us; the launch traced here: 97.2 us
  waiting for transfers between devices  36.8 us (38%)
  starting transfers between devices  35.4 us (36%)
  Pallas kernels  21.4 us (22%)
  local copies, waits for them, and re-layouts  2.64 us (3%)
    ppermute x7, waiting for transfers between devices, ring(): lax.ppermute(x, 'dp', [(4 * a + i, 4 * b + i) for a, b in pairs for i in...  21.5 us
    pallas_call x14, Pallas kernels, call(): pl.pallas_call(kernel, out_shape=out_shape, in_specs=in_specs, out_specs=...  21.4 us
    ppermute x17, starting transfers between devices, exchange(): return lax.ppermute(x, ('dp', 'cent'), pairs)  21.3 us
    ppermute x7, starting transfers between devices, ring(): lax.ppermute(x, 'dp', [(4 * a + i, 4 * b + i) for a, b in pairs for i in...  12.8 us
    ppermute x17, waiting for transfers between devices, exchange(): return lax.ppermute(x, ('dp', 'cent'), pairs)  11.7 us
    unnamed x6, local copies, waits for them, and re-layouts  2.64 us
    ppermute x5, waiting for transfers between devices, flip_core(): return lax.ppermute(x, 'cent', [(i, i ^ bits) for i in range(cores)])  2.56 us
  transfers between devices with their start and end apart: 30, of which 17 were waited for; matrix products, arithmetic and copies ran while one was open for 0% of the time, Pallas kernels for 18%

profile of v15, /device:TPU:0, one launch (start us, length us, event | category | flops | bytes accessed | tf_op | source)
XLA Modules:
  0.0 97.2 jit_solution(11946893363975023258)
XLA Ops:
  0.7 1.0 %copy-done = bf16[1024,256]{1,0:T(8,128)(2,1)S(1)} copy-done((bf16[1024,256]{1,0:T(8,128)(2,1)S(1)}, bf16[1024,256]{1,0:T(8,128)(2,1)}, u32[]{:S(2)}) %copy-start) | copy-done | bytes 524312
  2.4 3.0 %collective-permute-start.1 = (f32[512,256]{1,0:T(8,128)S(1)}, f32[512,256]{1,0:T(8,128)S(1)}, u32[]{:S(2)}, u32[]{:S(2)}) collective-permute-start(f32[512,256]{1,0:T(8,128)S(1)} %open.1), channel_id=1, source_target_pairs={{0,4},{1,3},{2,6},{3,1},{4,0},{5,7},{6,2},{7,5},{8,12},{9,11},{10,... | collective-permute-start | bytes 1572872 | tf_op jit(solution)/shard_map/ppermute | solution.py:281
  5.4 1.5 %collective-permute-start = (f32[512,256]{1,0:T(8,128)S(1)}, f32[512,256]{1,0:T(8,128)S(1)}, u32[]{:S(2)}, u32[]{:S(2)}) collective-permute-start(f32[512,256]{1,0:T(8,128)S(1)} %open.1), channel_id=1, source_target_pairs={{0,2},{1,5},{2,0},{3,7},{4,6},{5,1},{6,4},{7,3},{8,10},{9,13},{10,... | collective-permute-start | bytes 1572872 | tf_op jit(solution)/shard_map/ppermute | solution.py:281
  6.9 1.6 %copy-done.2 = bf16[4096,256]{1,0:T(8,128)(2,1)S(1)} copy-done((bf16[4096,256]{1,0:T(8,128)(2,1)S(1)}, bf16[4096,256]{1,0:T(8,128)(2,1)}, u32[]{:S(2)}) %copy-start.2) | copy-done | bytes 2097176
  8.5 5.9 %stats.1 = (f32[2,1024]{1,0:T(2,128)S(1)}, bf16[1024,256]{1,0:T(8,128)(2,1)S(1)}, f32[1024,128]{1,0:T(8,128)S(1)}) custom-call(s32[2]{0:T(128)S(1)} %pad_add_fusion.where_ref, bf16[1024,256]{1,0:T(8,128)(2,1)S(1)} %copy-done, bf16[4096,256]{1,0:T(8,128)(2,1)S(1)} %copy-done.2), custom_call_target="tpu_custom_call" | custom-call | flops 4294967296 | bytes 2621448 | tf_op jit(solution)/shard_map/stats/pallas_call | solution.py:27
  14.5 1.2 %collective-permute-done.4.refs_1_ = f32[2,1024]{1,0:T(2,128)S(1)} collective-permute-done((f32[2,1024]{1,0:T(2,128)S(1)}, f32[2,1024]{1,0:T(2,128)S(1)}, u32[]{:S(2)}, u32[]{:S(2)}) %collective-permute-start.4) | collective-permute-done | bytes 8224 | tf_op jit(solution)/shard_map/ppermute | solution.py:284
  16.4 1.9 %collective-permute-start.6 = (f32[4,256]{1,0:T(4,128)S(1)}, f32[4,256]{1,0:T(4,128)S(1)}, u32[]{:S(2)}, u32[]{:S(2)}) collective-permute-start(f32[4,256]{1,0:T(4,128)S(1)} %get-tuple-element.41.lse_ref), channel_id=1, source_target_pairs={{0,4},{1,3},{2,6},{3,1},{4,0},{5,7},{6,2},{7,5},{8,12},{9,11},{10,... | collective-permute-start | bytes 12296 | tf_op jit(solution)/shard_map/ppermute | solution.py:281
  18.2 1.5 %collective-permute-start.5 = (f32[4,256]{1,0:T(4,128)S(1)}, f32[4,256]{1,0:T(4,128)S(1)}, u32[]{:S(2)}, u32[]{:S(2)}) collective-permute-start(f32[4,256]{1,0:T(4,128)S(1)} %get-tuple-element.41.lse_ref), channel_id=1, source_target_pairs={{0,2},{1,5},{2,0},{3,7},{4,6},{5,1},{6,4},{7,3},{8,10},{9,13},{10,... | collective-permute-start | bytes 12296 | tf_op jit(solution)/shard_map/ppermute | solution.py:281
  19.7 1.0 %collective-permute-done.7.lse_ref = f32[4,256]{1,0:T(4,128)S(1)} collective-permute-done((f32[4,256]{1,0:T(4,128)S(1)}, f32[4,256]{1,0:T(4,128)S(1)}, u32[]{:S(2)}, u32[]{:S(2)}) %collective-permute-start.7) | collective-permute-done | bytes 4128 | tf_op jit(solution)/shard_map/ppermute | solution.py:321
  20.8 1.1 %collective-permute-done.5.lse_a_ref = f32[4,256]{1,0:T(4,128)S(1)} collective-permute-done((f32[4,256]{1,0:T(4,128)S(1)}, f32[4,256]{1,0:T(4,128)S(1)}, u32[]{:S(2)}, u32[]{:S(2)}) %collective-permute-start.5) | collective-permute-done | bytes 4128 | tf_op jit(solution)/shard_map/ppermute | solution.py:281
  22.6 1.9 %collective-permute-start.3 = (f32[256,256]{1,0:T(8,128)S(1)}, f32[256,256]{1,0:T(8,128)S(1)}, u32[]{:S(2)}, u32[]{:S(2)}) collective-permute-start(f32[256,256]{1,0:T(8,128)S(1)} %get-tuple-element.39), channel_id=1, source_target_pairs={{0,2},{1,5},{2,0},{3,7},{4,6},{5,1},{6,4},{7,3},{8,10},{9,13},{10,... | collective-permute-start | bytes 786440 | tf_op jit(solution)/shard_map/ppermute | solution.py:281
  24.5 1.4 %own.1 = (f32[1024,256]{1,0:T(8,128)S(1)}, f32[1024,128]{1,0:T(8,128)S(1)}) custom-call(bf16[1024,256]{1,0:T(8,128)(2,1)S(1)} %copy-done.1, bf16[1024,256]{1,0:T(8,128)(2,1)S(1)} %get-tuple-element.36.twice_ref, f32[1024,128]{1,0:T(8,128)S(1)} %get-tuple-element.37.norm_ref, f32[4,256]{1,0:T(4,128)S(1)} %get-tuple-element.41.lse_ref), custom_call_target="tpu_custom_call" | custom-call | flops 1073741824 | bytes 1576960 | tf_op jit(solution)/shard_map/own/pallas_call | solution.py:27
  25.9 3.2 %near.1 = (f32[1024,256]{1,0:T(8,128)S(1)}, f32[1024,128]{1,0:T(8,128)S(1)}) custom-call(s32[2]{0:T(128)S(1)} %pad_add_fusion.where_ref, bf16[1024,256]{1,0:T(8,128)(2,1)S(1)} %get-tuple-element.36.twice_ref, f32[1024,128]{1,0:T(8,128)S(1)} %get-tuple-element.37.norm_ref, ...), custom_call_target="tpu_custom_call", output_to_operand_aliasing={{0}: (3, {}), {1}: (4, {})} | custom-call | flops 2147483648 | bytes 4726792 | tf_op jit(solution)/shard_map/near/pallas_call | solution.py:27
  29.2 2.1 %collective-permute-done.2.refs_0_ = f32[256,256]{1,0:T(8,128)S(1)} collective-permute-done((f32[256,256]{1,0:T(8,128)S(1)}, f32[256,256]{1,0:T(8,128)S(1)}, u32[]{:S(2)}, u32[]{:S(2)}) %collective-permute-start.2) | collective-permute-done | bytes 262176 | tf_op jit(solution)/shard_map/ppermute | solution.py:281
  31.8 1.0 %collective-permute-done.10.refs_1_ = f32[256,256]{1,0:T(8,128)S(1)} collective-permute-done((f32[256,256]{1,0:T(8,128)S(1)}, f32[256,256]{1,0:T(8,128)S(1)}, u32[]{:S(2)}, u32[]{:S(2)}) %collective-permute-start.10) | collective-permute-done | bytes 262176 | tf_op jit(solution)/shard_map/ppermute | solution.py:284
  33.2 1.1 %first.1 = f32[264,256]{1,0:T(8,128)S(1)} custom-call(s32[2]{0:T(128)S(1)} %pad_add_fusion.where_ref, bf16[1024,256]{1,0:T(8,128)(2,1)S(1)} %get-tuple-element.36.twice_ref, f32[1024,128]{1,0:T(8,128)S(1)} %get-tuple-element.37.norm_ref, f32[1024,256]{1,0:T(8,128)S(1)} %get-tuple-element.50.acc_ref, f32[1024,128]{1,0:T(8,128)S(1)} %get-tuple-element.51.cnt_ref, ...), custom_call_target="tpu_custom_call" | custom-call | flops 268435456 | bytes 3674120 | tf_op jit(solution)/shard_map/first/pallas_call | solution.py:27
  34.4 2.7 %collective-permute-start.12 = (f32[264,256]{1,0:T(8,128)S(1)}, f32[264,256]{1,0:T(8,128)S(1)}, u32[]{:S(2)}, u32[]{:S(2)}) collective-permute-start(f32[264,256]{1,0:T(8,128)S(1)} %first.1), channel_id=1, source_target_pairs={{0,16},{2,18},{4,20},{6,22},{16,24},{18,26},{20,28},{22,30},{24,8}... | collective-permute-start | bytes 811016 | tf_op jit(solution)/shard_map/ppermute | solution.py:288
  37.0 1.1 %second.1 = f32[264,256]{1,0:T(8,128)S(1)} custom-call(s32[2]{0:T(128)S(1)} %pad_add_fusion.where_ref, bf16[1024,256]{1,0:T(8,128)(2,1)S(1)} %get-tuple-element.36.twice_ref, f32[1024,128]{1,0:T(8,128)S(1)} %get-tuple-element.37.norm_ref, f32[1024,256]{1,0:T(8,128)S(1)} %get-tuple-element.50.acc_ref, f32[1024,128]{1,0:T(8,128)S(1)} %get-tuple-element.51.cnt_ref, ...), custom_call_target="tpu_custom_call" | custom-call | flops 268435456 | bytes 3674120 | tf_op jit(solution)/shard_map/second/pallas_call | solution.py:27
  38.4 1.4 %rest.1 = (f32[264,256]{1,0:T(8,128)S(1)}, f32[264,256]{1,0:T(8,128)S(1)}) custom-call(s32[2]{0:T(128)S(1)} %pad_add_fusion.where_ref, bf16[1024,256]{1,0:T(8,128)(2,1)S(1)} %get-tuple-element.36.twice_ref, f32[1024,128]{1,0:T(8,128)S(1)} %get-tuple-element.37.norm_ref, f32[1024,256]{1,0:T(8,128)S(1)} %get-tuple-element.50.acc_ref, ...), custom_call_target="tpu_custom_call" | custom-call | flops 536870912 | bytes 3674120 | tf_op jit(solution)/shard_map/rest/pallas_call | solution.py:27
  39.8 4.1 %collective-permute-done.12.b_ref = f32[264,256]{1,0:T(8,128)S(1)} collective-permute-done((f32[264,256]{1,0:T(8,128)S(1)}, f32[264,256]{1,0:T(8,128)S(1)}, u32[]{:S(2)}, u32[]{:S(2)}) %collective-permute-start.12) | collective-permute-done | bytes 270368 | tf_op jit(solution)/shard_map/ppermute | solution.py:288
  43.9 3.4 %collective-permute-start.13 = (f32[264,256]{1,0:T(8,128)S(1)}, f32[264,256]{1,0:T(8,128)S(1)}, u32[]{:S(2)}, u32[]{:S(2)}) collective-permute-start(f32[264,256]{1,0:T(8,128)S(1)} %add.3), channel_id=1, source_target_pairs={{0,16},{2,18},{4,20},{6,22},{16,24},{18,26},{20,28},{22,30},{24,8}... | collective-permute-start | bytes 811016 | tf_op jit(solution)/shard_map/ppermute | solution.py:288
  47.4 4.1 %collective-permute-done.14.second_ref = f32[264,256]{1,0:T(8,128)S(1)} collective-permute-done((f32[264,256]{1,0:T(8,128)S(1)}, f32[264,256]{1,0:T(8,128)S(1)}, u32[]{:S(2)}, u32[]{:S(2)}) %collective-permute-start.14) | collective-permute-done | bytes 270368 | tf_op jit(solution)/shard_map/ppermute | solution.py:288
  51.5 5.0 %collective-permute-done.13.first_ref = f32[264,256]{1,0:T(8,128)S(1)} collective-permute-done((f32[264,256]{1,0:T(8,128)S(1)}, f32[264,256]{1,0:T(8,128)S(1)}, u32[]{:S(2)}, u32[]{:S(2)}) %collective-permute-start.13) | collective-permute-done | bytes 270368 | tf_op jit(solution)/shard_map/ppermute | solution.py:288
  56.4 0.8 finish.1.refs_0_
  57.3 1.7 %collective-permute-start.15 = (f32[264,256]{1,0:T(8,128)S(1)}, f32[264,256]{1,0:T(8,128)S(1)}, u32[]{:S(2)}, u32[]{:S(2)}) collective-permute-start(f32[264,256]{1,0:T(8,128)S(1)} %finish.1.refs_0_), channel_id=1, source_target_pairs={{0,16},{2,18},{4,20},{6,22},{16,24},{18,26},{20,28},{22,30},{24,8}... | collective-permute-start | bytes 811016 | tf_op jit(solution)/shard_map/ppermute | solution.py:288
  58.9 0.7 collective-permute-start.18
  59.6 1.1 %collective-permute-start.20 = (f32[264,256]{1,0:T(8,128)S(1)}, f32[264,256]{1,0:T(8,128)S(1)}, u32[]{:S(2)}, u32[]{:S(2)}) collective-permute-start(f32[264,256]{1,0:T(8,128)S(1)} %finish.1.refs_0_), channel_id=1, source_target_pairs={{0,2},{1,5},{2,0},{3,7},{4,6},{5,1},{6,4},{7,3},{8,10},{9,13},{10,... | collective-permute-start | bytes 811016 | tf_op jit(solution)/shard_map/ppermute | solution.py:281
  60.7 5.0 %collective-permute-done.15.refs_4_ = f32[264,256]{1,0:T(8,128)S(1)} collective-permute-done((f32[264,256]{1,0:T(8,128)S(1)}, f32[264,256]{1,0:T(8,128)S(1)}, u32[]{:S(2)}, u32[]{:S(2)}) %collective-permute-start.15) | collective-permute-done | bytes 270368 | tf_op jit(solution)/shard_map/ppermute | solution.py:288
  65.7 1.8 %collective-permute-start.16 = (f32[264,256]{1,0:T(8,128)S(1)}, f32[264,256]{1,0:T(8,128)S(1)}, u32[]{:S(2)}, u32[]{:S(2)}) collective-permute-start(f32[264,256]{1,0:T(8,128)S(1)} %collective-permute-done.15.refs_4_), channel_id=1, source_target_pairs={{0,16},{2,18},{4,20},{6,22},{16,24},{18,26},{20,28},{22,30},{24,8}... | collective-permute-start | bytes 811016 | tf_op jit(solution)/shard_map/ppermute | solution.py:288
  67.5 0.7 collective-permute-start.19
  68.2 1.1 %collective-permute-start.28 = (f32[264,256]{1,0:T(8,128)S(1)}, f32[264,256]{1,0:T(8,128)S(1)}, u32[]{:S(2)}, u32[]{:S(2)}) collective-permute-start(f32[264,256]{1,0:T(8,128)S(1)} %collective-permute-done.15.refs_4_), channel_id=1, source_target_pairs={{0,2},{1,5},{2,0},{3,7},{4,6},{5,1},{6,4},{7,3},{8,10},{9,13},{10,... | collective-permute-start | bytes 811016 | tf_op jit(solution)/shard_map/ppermute | solution.py:281
  69.3 1.4 %collective-permute-start.21 = (f32[264,256]{1,0:T(8,128)S(1)}, f32[264,256]{1,0:T(8,128)S(1)}, u32[]{:S(2)}, u32[]{:S(2)}) collective-permute-start(f32[264,256]{1,0:T(8,128)S(1)} %collective-permute-done.20.refs_1_), channel_id=1, source_target_pairs={{0,4},{1,3},{2,6},{3,1},{4,0},{5,7},{6,2},{7,5},{8,12},{9,11},{10,... | collective-permute-start | bytes 811016 | tf_op jit(solution)/shard_map/ppermute | solution.py:281
  70.7 2.5 %collective-permute-done.16.refs_8_ = f32[264,256]{1,0:T(8,128)S(1)} collective-permute-done((f32[264,256]{1,0:T(8,128)S(1)}, f32[264,256]{1,0:T(8,128)S(1)}, u32[]{:S(2)}, u32[]{:S(2)}) %collective-permute-start.16) | collective-permute-done | bytes 270368 | tf_op jit(solution)/shard_map/ppermute | solution.py:288
  73.3 2.0 %collective-permute-start.17 = (f32[264,256]{1,0:T(8,128)S(1)}, f32[264,256]{1,0:T(8,128)S(1)}, u32[]{:S(2)}, u32[]{:S(2)}) collective-permute-start(f32[264,256]{1,0:T(8,128)S(1)} %finish.1.refs_0_), channel_id=1, source_target_pairs={{0,8},{2,10},{4,12},{6,14},{16,0},{18,2},{20,4},{22,6},{24,16},{26... | collective-permute-start | bytes 811016 | tf_op jit(solution)/shard_map/ppermute | solution.py:288
  75.2 1.2 %collective-permute-start.24 = (f32[264,256]{1,0:T(8,128)S(1)}, f32[264,256]{1,0:T(8,128)S(1)}, u32[]{:S(2)}, u32[]{:S(2)}) collective-permute-start(f32[264,256]{1,0:T(8,128)S(1)} %collective-permute-done.16.refs_8_), channel_id=1, source_target_pairs={{0,2},{1,5},{2,0},{3,7},{4,6},{5,1},{6,4},{7,3},{8,10},{9,13},{10,... | collective-permute-start | bytes 811016 | tf_op jit(solution)/shard_map/ppermute | solution.py:281
  76.4 1.2 %collective-permute-done.28.refs_5_ = f32[264,256]{1,0:T(8,128)S(1)} collective-permute-done((f32[264,256]{1,0:T(8,128)S(1)}, f32[264,256]{1,0:T(8,128)S(1)}, u32[]{:S(2)}, u32[]{:S(2)}) %collective-permute-start.28) | collective-permute-done | bytes 270368 | tf_op jit(solution)/shard_map/ppermute | solution.py:281
  77.8 1.8 %collective-permute-start.25 = (f32[264,256]{1,0:T(8,128)S(1)}, f32[264,256]{1,0:T(8,128)S(1)}, u32[]{:S(2)}, u32[]{:S(2)}) collective-permute-start(f32[264,256]{1,0:T(8,128)S(1)} %collective-permute-done.16.refs_8_), channel_id=1, source_target_pairs={{0,4},{1,3},{2,6},{3,1},{4,0},{5,7},{6,2},{7,5},{8,12},{9,11},{10,... | collective-permute-start | bytes 811016 | tf_op jit(solution)/shard_map/ppermute | solution.py:281
  80.0 0.8 collective-permute-done.17.refs_9_
  80.8 1.1 %collective-permute-start.27 = (f32[264,256]{1,0:T(8,128)S(1)}, f32[264,256]{1,0:T(8,128)S(1)}, u32[]{:S(2)}, u32[]{:S(2)}) collective-permute-start(f32[264,256]{1,0:T(8,128)S(1)} %collective-permute-done.21.refs_3_), channel_id=1, source_target_pairs={{0,8},{2,10},{4,12},{6,14},{16,0},{18,2},{20,4},{22,6},{24,16},{26... | collective-permute-start | bytes 811016 | tf_op jit(solution)/shard_map/ppermute | solution.py:288
  81.9 2.8 %collective-permute-done.24.refs_0_ = f32[264,256]{1,0:T(8,128)S(1)} collective-permute-done((f32[264,256]{1,0:T(8,128)S(1)}, f32[264,256]{1,0:T(8,128)S(1)}, u32[]{:S(2)}, u32[]{:S(2)}) %collective-permute-start.24) | collective-permute-done | bytes 270368 | tf_op jit(solution)/shard_map/ppermute | solution.py:281
  84.7 0.7 collective-permute-start.26
  85.3 1.3 %collective-permute-start.23 = (f32[264,256]{1,0:T(8,128)S(1)}, f32[264,256]{1,0:T(8,128)S(1)}, u32[]{:S(2)}, u32[]{:S(2)}) collective-permute-start(f32[264,256]{1,0:T(8,128)S(1)} %collective-permute-done.17.refs_9_), channel_id=1, source_target_pairs={{0,4},{1,3},{2,6},{3,1},{4,0},{5,7},{6,2},{7,5},{8,12},{9,11},{10,... | collective-permute-start | bytes 811016 | tf_op jit(solution)/shard_map/ppermute | solution.py:281
  86.7 1.2 %collective-permute-start.22 = (f32[264,256]{1,0:T(8,128)S(1)}, f32[264,256]{1,0:T(8,128)S(1)}, u32[]{:S(2)}, u32[]{:S(2)}) collective-permute-start(f32[264,256]{1,0:T(8,128)S(1)} %collective-permute-done.17.refs_9_), channel_id=1, source_target_pairs={{0,2},{1,5},{2,0},{3,7},{4,6},{5,1},{6,4},{7,3},{8,10},{9,13},{10,... | collective-permute-start | bytes 811016 | tf_op jit(solution)/shard_map/ppermute | solution.py:281
  87.9 2.1 %place_early.1 = (f32[4096,256]{1,0:T(8,128)}, f32[32,128]{1,0:T(8,128)S(1)}) custom-call(s32[2]{0:T(128)S(1)} %pad_add_fusion.where_ref, f32[264,256]{1,0:T(8,128)S(1)} %finish.1.refs_0_, f32[264,256]{1,0:T(8,128)S(1)} %collective-permute-done.20.refs_1_, f32[264,256]{1,0:T(8,128)S(1)} %collective-permute-done.18.refs_2_, ...), custom_call_target="tpu_custom_call" | custom-call | bytes 2703368 | tf_op jit(solution)/shard_map/place_early/pallas_call | solution.py:27
  90.0 2.8 %collective-permute-done.26.refs_2_ = f32[264,256]{1,0:T(8,128)S(1)} collective-permute-done((f32[264,256]{1,0:T(8,128)S(1)}, f32[264,256]{1,0:T(8,128)S(1)}, u32[]{:S(2)}, u32[]{:S(2)}) %collective-permute-start.26) | collective-permute-done | bytes 270368 | tf_op jit(solution)/shard_map/ppermute | solution.py:281
  92.8 1.6 %place_middle.1 = (f32[4096,256]{1,0:T(8,128)}, f32[32,128]{1,0:T(8,128)S(1)}) custom-call(s32[2]{0:T(128)S(1)} %pad_add_fusion.where_ref, f32[264,256]{1,0:T(8,128)S(1)} %collective-permute-done.24.refs_0_, f32[264,256]{1,0:T(8,128)S(1)} %collective-permute-done.25.refs_1_, ...), custom_call_target="tpu_custom_call", output_to_operand_aliasing={{0}: (6, {})} | custom-call | bytes 5292040 | tf_op jit(solution)/shard_map/place_middle/pallas_call | solution.py:27
  94.3 1.3 %collective-permute-done.23.refs_1_ = f32[264,256]{1,0:T(8,128)S(1)} collective-permute-done((f32[264,256]{1,0:T(8,128)S(1)}, f32[264,256]{1,0:T(8,128)S(1)}, u32[]{:S(2)}, u32[]{:S(2)}) %collective-permute-start.23) | collective-permute-done | bytes 270368 | tf_op jit(solution)/shard_map/ppermute | solution.py:281
  95.7 1.4 %place_late.1 = (f32[4096,256]{1,0:T(8,128)}, f32[32,128]{1,0:T(8,128)}) custom-call(s32[2]{0:T(128)S(1)} %pad_add_fusion.where_ref, f32[264,256]{1,0:T(8,128)S(1)} %collective-permute-done.22.refs_0_, f32[264,256]{1,0:T(8,128)S(1)} %collective-permute-done.23.refs_1_, f32[32,128]{1,0:T(8,128)S(1)} %get-tuple-element.64.refs_2_, ...), custom_call_target="tpu_custom_call", output_to_operand_aliasing={{0}: (4, {})} | custom-call | bytes 4751368 | tf_op jit(solution)/shard_map/place_late/pallas_call | solution.py:27
  (33 shorter events, 3.9 us)
Async XLA Ops:
  0.7 1.0 %copy-start = (bf16[1024,256]{1,0:T(8,128)(2,1)S(1)}, bf16[1024,256]{1,0:T(8,128)(2,1)}, u32[]{:S(2)}) copy-start(bf16[1024,256]{1,0:T(8,128)(2,1)} %points_ref.5) | copy-start | bytes 1572868
  2.3 22.1 %copy-start.1 = (bf16[1024,256]{1,0:T(8,128)(2,1)S(1)}, bf16[1024,256]{1,0:T(8,128)(2,1)}, u32[]{:S(2)}) copy-start(bf16[1024,256]{1,0:T(8,128)(2,1)} %points_ref.5) | copy-start | bytes 1572868
  2.4 19.5 %collective-permute-start.1 = (f32[512,256]{1,0:T(8,128)S(1)}, f32[512,256]{1,0:T(8,128)S(1)}, u32[]{:S(2)}, u32[]{:S(2)}) collective-permute-start(f32[512,256]{1,0:T(8,128)S(1)} %open.1), channel_id=1, source_target_pairs={{0,4},{1,3},{2,6},{3,1},{4,0},{5,7},{6,2},{7,5},{8,12},{9,11},{10,... | collective-permute-start | bytes 1572872 | tf_op jit(solution)/shard_map/ppermute | solution.py:281
  5.4 16.5 %collective-permute-start = (f32[512,256]{1,0:T(8,128)S(1)}, f32[512,256]{1,0:T(8,128)S(1)}, u32[]{:S(2)}, u32[]{:S(2)}) collective-permute-start(f32[512,256]{1,0:T(8,128)S(1)} %open.1), channel_id=1, source_target_pairs={{0,2},{1,5},{2,0},{3,7},{4,6},{5,1},{6,4},{7,3},{8,10},{9,13},{10,... | collective-permute-start | bytes 1572872 | tf_op jit(solution)/shard_map/ppermute | solution.py:281
  6.9 1.6 %copy-start.2 = (bf16[4096,256]{1,0:T(8,128)(2,1)S(1)}, bf16[4096,256]{1,0:T(8,128)(2,1)}, u32[]{:S(2)}) copy-start(bf16[4096,256]{1,0:T(8,128)(2,1)} %c_ref.1) | copy-start | bytes 6291460
  14.4 1.2 %collective-permute-start.4 = (f32[2,1024]{1,0:T(2,128)S(1)}, f32[2,1024]{1,0:T(2,128)S(1)}, u32[]{:S(2)}, u32[]{:S(2)}) collective-permute-start(f32[2,1024]{1,0:T(2,128)S(1)} %get-tuple-element.40.refs_0_), channel_id=1, source_target_pairs={{0,1},{1,0},{2,3},{3,2},{4,5},{5,4},{6,7},{7,6},{8,9},{9,8},{10,11... | collective-permute-start | bytes 24584 | tf_op jit(solution)/shard_map/ppermute | solution.py:284
  16.3 4.5 %collective-permute-start.7 = (f32[4,256]{1,0:T(4,128)S(1)}, f32[4,256]{1,0:T(4,128)S(1)}, u32[]{:S(2)}, u32[]{:S(2)}) collective-permute-start(f32[4,256]{1,0:T(4,128)S(1)} %get-tuple-element.41.lse_ref), channel_id=1, source_target_pairs={{0,6},{2,4},{4,2},{6,0},{8,14},{10,12},{12,10},{14,8},{16,22},{18,... | collective-permute-start | bytes 12296 | tf_op jit(solution)/shard_map/ppermute | solution.py:321
  16.4 4.4 %collective-permute-start.6 = (f32[4,256]{1,0:T(4,128)S(1)}, f32[4,256]{1,0:T(4,128)S(1)}, u32[]{:S(2)}, u32[]{:S(2)}) collective-permute-start(f32[4,256]{1,0:T(4,128)S(1)} %get-tuple-element.41.lse_ref), channel_id=1, source_target_pairs={{0,4},{1,3},{2,6},{3,1},{4,0},{5,7},{6,2},{7,5},{8,12},{9,11},{10,... | collective-permute-start | bytes 12296 | tf_op jit(solution)/shard_map/ppermute | solution.py:281
  18.2 3.6 %collective-permute-start.5 = (f32[4,256]{1,0:T(4,128)S(1)}, f32[4,256]{1,0:T(4,128)S(1)}, u32[]{:S(2)}, u32[]{:S(2)}) collective-permute-start(f32[4,256]{1,0:T(4,128)S(1)} %get-tuple-element.41.lse_ref), channel_id=1, source_target_pairs={{0,2},{1,5},{2,0},{3,7},{4,6},{5,1},{6,4},{7,3},{8,10},{9,13},{10,... | collective-permute-start | bytes 12296 | tf_op jit(solution)/shard_map/ppermute | solution.py:281
  21.8 4.0 %collective-permute-start.8 = (f32[512,256]{1,0:T(8,128)S(1)}, f32[512,256]{1,0:T(8,128)S(1)}, u32[]{:S(2)}, u32[]{:S(2)}) collective-permute-start(f32[512,256]{1,0:T(8,128)S(1)} %collective-permute-done.a_ref.refs_0_), channel_id=1, source_target_pairs={{0,1},{1,0},{2,3},{3,2},{4,5},{5,4},{6,7},{7,6},{8,9},{9,8},{10,11... | collective-permute-start | bytes 1572872 | tf_op jit(solution)/shard_map/ppermute | solution.py:284
  21.9 4.0 %collective-permute-start.9 = (f32[512,256]{1,0:T(8,128)S(1)}, f32[512,256]{1,0:T(8,128)S(1)}, u32[]{:S(2)}, u32[]{:S(2)}) collective-permute-start(f32[512,256]{1,0:T(8,128)S(1)} %collective-permute-done.1.b_ref.refs_2_), channel_id=1, source_target_pairs={{0,1},{1,0},{2,3},{3,2},{4,5},{5,4},{6,7},{7,6},{8,9},{9,8},{10,11... | collective-permute-start | bytes 1572872 | tf_op jit(solution)/shard_map/ppermute | solution.py:284
  22.4 8.9 %collective-permute-start.2 = (f32[256,256]{1,0:T(8,128)S(1)}, f32[256,256]{1,0:T(8,128)S(1)}, u32[]{:S(2)}, u32[]{:S(2)}) collective-permute-start(f32[256,256]{1,0:T(8,128)S(1)} %get-tuple-element.38), channel_id=1, source_target_pairs={{0,4},{1,3},{2,6},{3,1},{4,0},{5,7},{6,2},{7,5},{8,12},{9,11},{10,... | collective-permute-start | bytes 786440 | tf_op jit(solution)/shard_map/ppermute | solution.py:281
  22.6 8.7 %collective-permute-start.3 = (f32[256,256]{1,0:T(8,128)S(1)}, f32[256,256]{1,0:T(8,128)S(1)}, u32[]{:S(2)}, u32[]{:S(2)}) collective-permute-start(f32[256,256]{1,0:T(8,128)S(1)} %get-tuple-element.39), channel_id=1, source_target_pairs={{0,2},{1,5},{2,0},{3,7},{4,6},{5,1},{6,4},{7,3},{8,10},{9,13},{10,... | collective-permute-start | bytes 786440 | tf_op jit(solution)/shard_map/ppermute | solution.py:281
  31.3 1.5 %collective-permute-start.10 = (f32[256,256]{1,0:T(8,128)S(1)}, f32[256,256]{1,0:T(8,128)S(1)}, u32[]{:S(2)}, u32[]{:S(2)}) collective-permute-start(f32[256,256]{1,0:T(8,128)S(1)} %collective-permute-done.2.refs_0_), channel_id=1, source_target_pairs={{0,1},{1,0},{2,3},{3,2},{4,5},{5,4},{6,7},{7,6},{8,9},{9,8},{10,11... | collective-permute-start | bytes 786440 | tf_op jit(solution)/shard_map/ppermute | solution.py:284
  31.5 1.8 %collective-permute-start.11 = (f32[256,256]{1,0:T(8,128)S(1)}, f32[256,256]{1,0:T(8,128)S(1)}, u32[]{:S(2)}, u32[]{:S(2)}) collective-permute-start(f32[256,256]{1,0:T(8,128)S(1)} %collective-permute-done.3.refs_2_), channel_id=1, source_target_pairs={{0,1},{1,0},{2,3},{3,2},{4,5},{5,4},{6,7},{7,6},{8,9},{9,8},{10,11... | collective-permute-start | bytes 786440 | tf_op jit(solution)/shard_map/ppermute | solution.py:284
  34.4 9.5 %collective-permute-start.12 = (f32[264,256]{1,0:T(8,128)S(1)}, f32[264,256]{1,0:T(8,128)S(1)}, u32[]{:S(2)}, u32[]{:S(2)}) collective-permute-start(f32[264,256]{1,0:T(8,128)S(1)} %first.1), channel_id=1, source_target_pairs={{0,16},{2,18},{4,20},{6,22},{16,24},{18,26},{20,28},{22,30},{24,8}... | collective-permute-start | bytes 811016 | tf_op jit(solution)/shard_map/ppermute | solution.py:288
  38.1 13.3 %collective-permute-start.14 = (f32[264,256]{1,0:T(8,128)S(1)}, f32[264,256]{1,0:T(8,128)S(1)}, u32[]{:S(2)}, u32[]{:S(2)}) collective-permute-start(f32[264,256]{1,0:T(8,128)S(1)} %second.1), channel_id=1, source_target_pairs={{0,8},{2,10},{4,12},{6,14},{16,0},{18,2},{20,4},{22,6},{24,16},{26... | collective-permute-start | bytes 811016 | tf_op jit(solution)/shard_map/ppermute | solution.py:288
  43.9 12.5 %collective-permute-start.13 = (f32[264,256]{1,0:T(8,128)S(1)}, f32[264,256]{1,0:T(8,128)S(1)}, u32[]{:S(2)}, u32[]{:S(2)}) collective-permute-start(f32[264,256]{1,0:T(8,128)S(1)} %add.3), channel_id=1, source_target_pairs={{0,16},{2,18},{4,20},{6,22},{16,24},{18,26},{20,28},{22,30},{24,8}... | collective-permute-start | bytes 811016 | tf_op jit(solution)/shard_map/ppermute | solution.py:288
  57.3 8.5 %collective-permute-start.15 = (f32[264,256]{1,0:T(8,128)S(1)}, f32[264,256]{1,0:T(8,128)S(1)}, u32[]{:S(2)}, u32[]{:S(2)}) collective-permute-start(f32[264,256]{1,0:T(8,128)S(1)} %finish.1.refs_0_), channel_id=1, source_target_pairs={{0,16},{2,18},{4,20},{6,22},{16,24},{18,26},{20,28},{22,30},{24,8}... | collective-permute-start | bytes 811016 | tf_op jit(solution)/shard_map/ppermute | solution.py:288
  58.9 8.6 %collective-permute-start.18 = (f32[264,256]{1,0:T(8,128)S(1)}, f32[264,256]{1,0:T(8,128)S(1)}, u32[]{:S(2)}, u32[]{:S(2)}) collective-permute-start(f32[264,256]{1,0:T(8,128)S(1)} %finish.1.refs_0_), channel_id=1, source_target_pairs={{0,4},{1,3},{2,6},{3,1},{4,0},{5,7},{6,2},{7,5},{8,12},{9,11},{10,... | collective-permute-start | bytes 811016 | tf_op jit(solution)/shard_map/ppermute | solution.py:281
  59.6 9.7 %collective-permute-start.20 = (f32[264,256]{1,0:T(8,128)S(1)}, f32[264,256]{1,0:T(8,128)S(1)}, u32[]{:S(2)}, u32[]{:S(2)}) collective-permute-start(f32[264,256]{1,0:T(8,128)S(1)} %finish.1.refs_0_), channel_id=1, source_target_pairs={{0,2},{1,5},{2,0},{3,7},{4,6},{5,1},{6,4},{7,3},{8,10},{9,13},{10,... | collective-permute-start | bytes 811016 | tf_op jit(solution)/shard_map/ppermute | solution.py:281
  65.7 7.6 %collective-permute-start.16 = (f32[264,256]{1,0:T(8,128)S(1)}, f32[264,256]{1,0:T(8,128)S(1)}, u32[]{:S(2)}, u32[]{:S(2)}) collective-permute-start(f32[264,256]{1,0:T(8,128)S(1)} %collective-permute-done.15.refs_4_), channel_id=1, source_target_pairs={{0,16},{2,18},{4,20},{6,22},{16,24},{18,26},{20,28},{22,30},{24,8}... | collective-permute-start | bytes 811016 | tf_op jit(solution)/shard_map/ppermute | solution.py:288
  67.5 7.7 %collective-permute-start.19 = (f32[264,256]{1,0:T(8,128)S(1)}, f32[264,256]{1,0:T(8,128)S(1)}, u32[]{:S(2)}, u32[]{:S(2)}) collective-permute-start(f32[264,256]{1,0:T(8,128)S(1)} %collective-permute-done.15.refs_4_), channel_id=1, source_target_pairs={{0,4},{1,3},{2,6},{3,1},{4,0},{5,7},{6,2},{7,5},{8,12},{9,11},{10,... | collective-permute-start | bytes 811016 | tf_op jit(solution)/shard_map/ppermute | solution.py:281
  68.2 9.4 %collective-permute-start.28 = (f32[264,256]{1,0:T(8,128)S(1)}, f32[264,256]{1,0:T(8,128)S(1)}, u32[]{:S(2)}, u32[]{:S(2)}) collective-permute-start(f32[264,256]{1,0:T(8,128)S(1)} %collective-permute-done.15.refs_4_), channel_id=1, source_target_pairs={{0,2},{1,5},{2,0},{3,7},{4,6},{5,1},{6,4},{7,3},{8,10},{9,13},{10,... | collective-permute-start | bytes 811016 | tf_op jit(solution)/shard_map/ppermute | solution.py:281
  69.3 10.7 %collective-permute-start.21 = (f32[264,256]{1,0:T(8,128)S(1)}, f32[264,256]{1,0:T(8,128)S(1)}, u32[]{:S(2)}, u32[]{:S(2)}) collective-permute-start(f32[264,256]{1,0:T(8,128)S(1)} %collective-permute-done.20.refs_1_), channel_id=1, source_target_pairs={{0,4},{1,3},{2,6},{3,1},{4,0},{5,7},{6,2},{7,5},{8,12},{9,11},{10,... | collective-permute-start | bytes 811016 | tf_op jit(solution)/shard_map/ppermute | solution.py:281
  73.3 7.5 %collective-permute-start.17 = (f32[264,256]{1,0:T(8,128)S(1)}, f32[264,256]{1,0:T(8,128)S(1)}, u32[]{:S(2)}, u32[]{:S(2)}) collective-permute-start(f32[264,256]{1,0:T(8,128)S(1)} %finish.1.refs_0_), channel_id=1, source_target_pairs={{0,8},{2,10},{4,12},{6,14},{16,0},{18,2},{20,4},{22,6},{24,16},{26... | collective-permute-start | bytes 811016 | tf_op jit(solution)/shard_map/ppermute | solution.py:288
  75.2 9.4 %collective-permute-start.24 = (f32[264,256]{1,0:T(8,128)S(1)}, f32[264,256]{1,0:T(8,128)S(1)}, u32[]{:S(2)}, u32[]{:S(2)}) collective-permute-start(f32[264,256]{1,0:T(8,128)S(1)} %collective-permute-done.16.refs_8_), channel_id=1, source_target_pairs={{0,2},{1,5},{2,0},{3,7},{4,6},{5,1},{6,4},{7,3},{8,10},{9,13},{10,... | collective-permute-start | bytes 811016 | tf_op jit(solution)/shard_map/ppermute | solution.py:281
  77.6 9.1 %collective-permute-start.29 = (f32[264,256]{1,0:T(8,128)S(1)}, f32[264,256]{1,0:T(8,128)S(1)}, u32[]{:S(2)}, u32[]{:S(2)}) collective-permute-start(f32[264,256]{1,0:T(8,128)S(1)} %collective-permute-done.28.refs_5_), channel_id=1, source_target_pairs={{0,4},{1,3},{2,6},{3,1},{4,0},{5,7},{6,2},{7,5},{8,12},{9,11},{10,... | collective-permute-start | bytes 811016 | tf_op jit(solution)/shard_map/ppermute | solution.py:281
  77.8 12.2 %collective-permute-start.25 = (f32[264,256]{1,0:T(8,128)S(1)}, f32[264,256]{1,0:T(8,128)S(1)}, u32[]{:S(2)}, u32[]{:S(2)}) collective-permute-start(f32[264,256]{1,0:T(8,128)S(1)} %collective-permute-done.16.refs_8_), channel_id=1, source_target_pairs={{0,4},{1,3},{2,6},{3,1},{4,0},{5,7},{6,2},{7,5},{8,12},{9,11},{10,... | collective-permute-start | bytes 811016 | tf_op jit(solution)/shard_map/ppermute | solution.py:281
  80.8 9.2 %collective-permute-start.27 = (f32[264,256]{1,0:T(8,128)S(1)}, f32[264,256]{1,0:T(8,128)S(1)}, u32[]{:S(2)}, u32[]{:S(2)}) collective-permute-start(f32[264,256]{1,0:T(8,128)S(1)} %collective-permute-done.21.refs_3_), channel_id=1, source_target_pairs={{0,8},{2,10},{4,12},{6,14},{16,0},{18,2},{20,4},{22,6},{24,16},{26... | collective-permute-start | bytes 811016 | tf_op jit(solution)/shard_map/ppermute | solution.py:288
  84.7 8.1 %collective-permute-start.26 = (f32[264,256]{1,0:T(8,128)S(1)}, f32[264,256]{1,0:T(8,128)S(1)}, u32[]{:S(2)}, u32[]{:S(2)}) collective-permute-start(f32[264,256]{1,0:T(8,128)S(1)} %collective-permute-done.24.refs_0_), channel_id=1, source_target_pairs={{0,4},{1,3},{2,6},{3,1},{4,0},{5,7},{6,2},{7,5},{8,12},{9,11},{10,... | collective-permute-start | bytes 811016 | tf_op jit(solution)/shard_map/ppermute | solution.py:281
  85.3 10.3 %collective-permute-start.23 = (f32[264,256]{1,0:T(8,128)S(1)}, f32[264,256]{1,0:T(8,128)S(1)}, u32[]{:S(2)}, u32[]{:S(2)}) collective-permute-start(f32[264,256]{1,0:T(8,128)S(1)} %collective-permute-done.17.refs_9_), channel_id=1, source_target_pairs={{0,4},{1,3},{2,6},{3,1},{4,0},{5,7},{6,2},{7,5},{8,12},{9,11},{10,... | collective-permute-start | bytes 811016 | tf_op jit(solution)/shard_map/ppermute | solution.py:281
  86.7 9.0 %collective-permute-start.22 = (f32[264,256]{1,0:T(8,128)S(1)}, f32[264,256]{1,0:T(8,128)S(1)}, u32[]{:S(2)}, u32[]{:S(2)}) collective-permute-start(f32[264,256]{1,0:T(8,128)S(1)} %collective-permute-done.17.refs_9_), channel_id=1, source_target_pairs={{0,2},{1,5},{2,0},{3,7},{4,6},{5,1},{6,4},{7,3},{8,10},{9,13},{10,... | collective-permute-start | bytes 811016 | tf_op jit(solution)/shard_map/ppermute | solution.py:281

commit v16 on v14

--- a/solution.py
+++ b/solution.py
@@ -266,6 +266,20 @@
     for k in range(size // LANES):
         spread = jnp.where(row == k, counts[:, k * LANES : (k + 1) * LANES], spread)
     out_ref[size:, :] = jnp.concatenate([spread] * (width // LANES), axis=1)
+
+
+def sort_kernel(where_ref, first_ref, second_ref, along_ref, over_ref):
+    odd = lax.rem(where_ref[1], 2) == 1
+
+    @pl.when(odd)
+    def _():
+        along_ref[...] = second_ref[...]
+        over_ref[...] = first_ref[...]
+
+    @pl.when(jnp.logical_not(odd))
+    def _():
+        along_ref[...] = first_ref[...]
+        over_ref[...] = second_ref[...]
 
 
 def place_kernel(names, order, later, where_ref, *refs):
@@ -406,29 +420,37 @@
         "finish",
     )
 
-    steps = [-s for s in range(1, lines // 2 + 1)] + list(range(1, lines // 2))
+    def either(x, even_first):
+        following = {order[p]: order[(p + 1) % lines] for p in range(lines)}
+        pairs = []
+        for i in range(n):
+            for c in range(cores):
+                if (c % 2 == 0) == even_first:
+                    to = 4 * following[i // 4] + i % 4
+                else:
+                    to = i ^ (1 if c % 2 == 0 else 2)
+                pairs.append((i * cores + c, to * cores + c))
+        return lax.ppermute(x, ("dp", "cent"), pairs)
+
     got = {(0, 0): done}
-    previous, older, plane_b = (), (done, done), [done]
-    for s in [0] + steps:
-        x = got[0, s]
-        if previous:
-            x = lax.optimization_barrier((x, *previous))[0]
-        got[1, s], got[2, s] = exchange(x, 0), exchange(x, 1)
-        if s == steps[-1]:
-            break
-        got[3, s] = exchange(got[1, s], 1)
-        plane_b.append(got[2, s])
-        previous, older = (plane_b[-2 if s == steps[-2] else -1], *older[:1]), (*older[1:], got[3, s])
-        ahead_of = steps[([0] + steps).index(s)]
-        x = got[0, ahead_of + (1 if ahead_of < 0 else -1)]
-        if ahead_of > 0:
-            x = lax.optimization_barrier((x, got[0, s]))[0]
-        got[0, ahead_of] = ring(x, 1 if ahead_of < 0 else -1)
-    before = got[3, steps[-1] - 1] if steps[-1] > 0 else got[3, steps[-1] + 1]
-    before = lax.optimization_barrier((before, got[0, steps[-1]]))[0]
-    got[3, steps[-1]] = ring(before, -1 if steps[-1] > 0 else 1)
-    late = [(1, steps[-1]), (2, steps[-1])]
-    middle = [(w, steps[-2]) for w in (1, 2, 3)] + [(3, steps[-1])]
+    waits = {}
+    for k in range(lines - 1):
+        x = got[0, -k]
+        if k:
+            x = lax.optimization_barrier((x, *(got[w] for w in waits[k])))[0]
+        first, second = either(x, True), either(x, False)
+        got[2, -k] = exchange(x, 1)
+        got[0, -k - 1], got[1, -k] = call(
+            sort_kernel, (block_sum, block_sum), [SMEM] + [VMEM] * 2, (where, first, second), "sort"
+        )
+        got[3, -k] = exchange(got[1, -k], 1)
+        waits[k + 1] = [(2, -k)] + ([(3, 1 - k)] if k else [])
+    end = 1 - lines
+    x = lax.optimization_barrier((got[0, end], *(got[w] for w in waits.get(lines - 1, []))))[0]
+    got[1, end], got[2, end] = exchange(x, 0), exchange(x, 1)
+    got[3, end] = ring(lax.optimization_barrier((got[3, 0], got[0, end]))[0], -1)
+    late = [(1, end), (2, end)]
+    middle = [(1, end + 1), (2, end + 1), (3, end + 1), (3, end)]
     groups = ([k for k in got if k not in middle + late], middle, late)
     new = counts = None
     for later, names in enumerate(groups):

time: 95.2 us -> 102 us (1.071)
  waiting for transfers between devices: 37.5 us -> 42.7 us
  Pallas kernels: 21.3 us -> 23.1 us
    ppermute x0 -> x6, waiting for transfers between devices: none -> 14.6 us  [either(): return lax.ppermute(x, ('dp', 'cent'), pairs)]
    ppermute x7 -> x4, waiting for transfers between devices: 20.3 us -> 11.9 us  [ring(): lax.ppermute(x, 'dp', [(4 * a + i, 4 * b + i) for a, b in pairs for i in...]
    ppermute x0 -> x6, starting transfers between devices: none -> 6.46 us  [either(): return lax.ppermute(x, ('dp', 'cent'), pairs)]
    ppermute x7 -> x4, starting transfers between devices: 13.1 us -> 7.4 us  [ring(): lax.ppermute(x, 'dp', [(4 * a + i, 4 * b + i) for a, b in pairs for i in...]
    pallas_call x13 -> x16, Pallas kernels: 21.3 us -> 23.1 us  [call(): pl.pallas_call(kernel, out_shape=out_shape, in_specs=in_specs, out_specs=...]
    ppermute x15 -> x12, starting transfers between devices: 17.4 us -> 16.1 us  [exchange(): return lax.ppermute(x, ('dp', 'cent'), pairs)]
    ppermute x15 -> x12, waiting for transfers between devices: 15.1 us -> 14.2 us  [exchange(): return lax.ppermute(x, ('dp', 'cent'), pairs)]
  transfers between devices with their start and end apart: 28 -> 28, of which waited for: 14 -> 16; matrix products, arithmetic and copies ran while one was open for 0% -> 0% of each run, Pallas kernels for 18% -> 18%
where the time goes in v16:
time: 102 us; the launch traced here: 101 us
  waiting for transfers between devices  42.7 us (42%)
  starting transfers between devices  31.9 us (31%)
  Pallas kernels  23.1 us (23%)
  local copies, waits for them, and re-layouts  2.64 us (3%)
    pallas_call x16, Pallas kernels, call(): pl.pallas_call(kernel, out_shape=out_shape, in_specs=in_specs, out_specs=...  23.1 us
    ppermute x12, starting transfers between devices, exchange(): return lax.ppermute(x, ('dp', 'cent'), pairs)  16.1 us
    ppermute x6, waiting for transfers between devices, either(): return lax.ppermute(x, ('dp', 'cent'), pairs)  14.6 us
    ppermute x12, waiting for transfers between devices, exchange(): return lax.ppermute(x, ('dp', 'cent'), pairs)  14.2 us
    ppermute x4, waiting for transfers between devices, ring(): lax.ppermute(x, 'dp', [(4 * a + i, 4 * b + i) for a, b in pairs for i in...  11.9 us
    ppermute x4, starting transfers between devices, ring(): lax.ppermute(x, 'dp', [(4 * a + i, 4 * b + i) for a, b in pairs for i in...  7.4 us
    ppermute x6, starting transfers between devices, either(): return lax.ppermute(x, ('dp', 'cent'), pairs)  6.46 us
    unnamed x6, local copies, waits for them, and re-layouts  2.64 us
  transfers between devices with their start and end apart: 28, of which 16 were waited for; matrix products, arithmetic and copies ran while one was open for 0% of the time, Pallas kernels for 18%

profile of v16, /device:TPU:0, one launch (start us, length us, event | category | flops | bytes accessed | tf_op | source)
XLA Modules:
  0.0 101.4 jit_solution(7738828684154612970)
XLA Ops:
  0.7 1.0 %copy-done = bf16[1024,256]{1,0:T(8,128)(2,1)S(1)} copy-done((bf16[1024,256]{1,0:T(8,128)(2,1)S(1)}, bf16[1024,256]{1,0:T(8,128)(2,1)}, u32[]{:S(2)}) %copy-start) | copy-done | bytes 524312
  2.4 3.0 %collective-permute-start.1 = (f32[512,256]{1,0:T(8,128)S(1)}, f32[512,256]{1,0:T(8,128)S(1)}, u32[]{:S(2)}, u32[]{:S(2)}) collective-permute-start(f32[512,256]{1,0:T(8,128)S(1)} %open.1), channel_id=1, source_target_pairs={{0,4},{1,3},{2,6},{3,1},{4,0},{5,7},{6,2},{7,5},{8,12},{9,11},{10,... | collective-permute-start | bytes 1572872 | tf_op jit(solution)/shard_map/ppermute | solution.py:329
  5.4 1.5 %collective-permute-start = (f32[512,256]{1,0:T(8,128)S(1)}, f32[512,256]{1,0:T(8,128)S(1)}, u32[]{:S(2)}, u32[]{:S(2)}) collective-permute-start(f32[512,256]{1,0:T(8,128)S(1)} %open.1), channel_id=1, source_target_pairs={{0,2},{1,5},{2,0},{3,7},{4,6},{5,1},{6,4},{7,3},{8,10},{9,13},{10,... | collective-permute-start | bytes 1572872 | tf_op jit(solution)/shard_map/ppermute | solution.py:329
  6.9 1.6 %copy-done.2 = bf16[4096,256]{1,0:T(8,128)(2,1)S(1)} copy-done((bf16[4096,256]{1,0:T(8,128)(2,1)S(1)}, bf16[4096,256]{1,0:T(8,128)(2,1)}, u32[]{:S(2)}) %copy-start.2) | copy-done | bytes 2097176
  8.5 5.9 %stats.1 = (f32[2,1024]{1,0:T(2,128)S(1)}, bf16[1024,256]{1,0:T(8,128)(2,1)S(1)}, f32[1024,128]{1,0:T(8,128)S(1)}) custom-call(s32[2]{0:T(128)S(1)} %pad_add_fusion.where_ref, bf16[1024,256]{1,0:T(8,128)(2,1)S(1)} %copy-done, bf16[4096,256]{1,0:T(8,128)(2,1)S(1)} %copy-done.2), custom_call_target="tpu_custom_call" | custom-call | flops 4294967296 | bytes 2621448 | tf_op jit(solution)/shard_map/stats/pallas_call | solution.py:27
  14.5 1.2 %collective-permute-done.2.refs_1_ = f32[2,1024]{1,0:T(2,128)S(1)} collective-permute-done((f32[2,1024]{1,0:T(2,128)S(1)}, f32[2,1024]{1,0:T(2,128)S(1)}, u32[]{:S(2)}, u32[]{:S(2)}) %collective-permute-start.2) | collective-permute-done | bytes 8224 | tf_op jit(solution)/shard_map/ppermute | solution.py:332
  15.6 2.0 %collective-permute-done.1.b_ref.refs_2_ = f32[512,256]{1,0:T(8,128)S(1)} collective-permute-done((f32[512,256]{1,0:T(8,128)S(1)}, f32[512,256]{1,0:T(8,128)S(1)}, u32[]{:S(2)}, u32[]{:S(2)}) %collective-permute-start.1) | collective-permute-done | bytes 524320 | tf_op jit(solution)/shard_map/ppermute | solution.py:329
  17.6 0.6 lse.1
  18.8 2.5 %collective-permute-start.5 = (f32[264,256]{1,0:T(8,128)S(1)}, f32[264,256]{1,0:T(8,128)S(1)}, u32[]{:S(2)}, u32[]{:S(2)}) collective-permute-start(f32[264,256]{1,0:T(8,128)S(1)} %get-tuple-element.64), channel_id=1, source_target_pairs={{0,4},{1,3},{2,6},{3,1},{4,0},{5,7},{6,2},{7,5},{8,12},{9,11},{10,... | collective-permute-start | bytes 811016 | tf_op jit(solution)/shard_map/ppermute | solution.py:329
  21.3 0.7 collective-permute-start.6
  21.9 1.4 %own.1 = (f32[1024,256]{1,0:T(8,128)S(1)}, f32[1024,128]{1,0:T(8,128)S(1)}) custom-call(bf16[1024,256]{1,0:T(8,128)(2,1)S(1)} %copy-done.1, bf16[1024,256]{1,0:T(8,128)(2,1)S(1)} %get-tuple-element.51.twice_ref, f32[1024,128]{1,0:T(8,128)S(1)} %get-tuple-element.52.norm_ref, f32[4,256]{1,0:T(4,128)S(1)} %get-tuple-element.68.lse_ref), custom_call_target="tpu_custom_call" | custom-call | flops 1073741824 | bytes 1576960 | tf_op jit(solution)/shard_map/own/pallas_call | solution.py:27
  23.4 0.8 collective-permute-start.7
  24.2 4.1 %collective-permute-done.5.refs_4_.refs_0_ = f32[264,256]{1,0:T(8,128)S(1)} collective-permute-done((f32[264,256]{1,0:T(8,128)S(1)}, f32[264,256]{1,0:T(8,128)S(1)}, u32[]{:S(2)}, u32[]{:S(2)}) %collective-permute-start.5) | collective-permute-done | bytes 270368 | tf_op jit(solution)/shard_map/ppermute | solution.py:329
  28.4 0.9 collective-permute-done.7.lse_ref
  29.8 1.4 %lead.1 = (f32[256,256]{1,0:T(8,128)S(1)}, f32[256,128]{1,0:T(8,128)S(1)}) custom-call(s32[2]{0:T(128)S(1)} %pad_add_fusion.where_ref, bf16[1024,256]{1,0:T(8,128)(2,1)S(1)} %get-tuple-element.51.twice_ref, f32[1024,128]{1,0:T(8,128)S(1)} %get-tuple-element.52.norm_ref, f32[1024,256]{1,0:T(8,128)S(1)} %get-tuple-element.69.acc_ref, ...), custom_call_target="tpu_custom_call" | custom-call | flops 536870912 | bytes 5259272 | tf_op jit(solution)/shard_map/lead/pallas_call | solution.py:27
  31.2 1.1 %first.1 = f32[264,256]{1,0:T(8,128)S(1)} custom-call(s32[2]{0:T(128)S(1)} %pad_add_fusion.where_ref, bf16[1024,256]{1,0:T(8,128)(2,1)S(1)} %get-tuple-element.51.twice_ref, f32[1024,128]{1,0:T(8,128)S(1)} %get-tuple-element.52.norm_ref, f32[4,256]{1,0:T(4,128)S(1)} %collective-permute-done.7.lse_ref, f32[256,256]{1,0:T(8,128)S(1)} %get-tuple-element.80.lead_acc_ref, ...), custom_call_target="tpu_custom_call" | custom-call | flops 536870912 | bytes 2527240 | tf_op jit(solution)/shard_map/first/pallas_call | solution.py:27
  32.4 2.6 %collective-permute-start.10 = (f32[264,256]{1,0:T(8,128)S(1)}, f32[264,256]{1,0:T(8,128)S(1)}, u32[]{:S(2)}, u32[]{:S(2)}) collective-permute-start(f32[264,256]{1,0:T(8,128)S(1)} %first.1), channel_id=1, source_target_pairs={{0,16},{2,18},{4,20},{6,22},{16,24},{18,26},{20,28},{22,30},{24,8}... | collective-permute-start | bytes 811016 | tf_op jit(solution)/shard_map/ppermute | solution.py:336
  35.0 1.7 %rest.3 = f32[264,256]{1,0:T(8,128)S(1)} custom-call(s32[2]{0:T(128)S(1)} %pad_add_fusion.where_ref, bf16[1024,256]{1,0:T(8,128)(2,1)S(1)} %get-tuple-element.51.twice_ref, f32[1024,128]{1,0:T(8,128)S(1)} %get-tuple-element.52.norm_ref, f32[1024,256]{1,0:T(8,128)S(1)} %get-tuple-element.69.acc_ref, f32[1024,128]{1,0:T(8,128)S(1)} %get-tuple-element.70.cnt_ref, ...), custom_call_target="tpu_custom_call" | custom-call | flops 805306368 | bytes 5804040 | tf_op jit(solution)/shard_map/rest/pallas_call | solution.py:27
  37.0 2.6 %rest.2 = (f32[264,256]{1,0:T(8,128)S(1)}, f32[264,256]{1,0:T(8,128)S(1)}) custom-call(s32[2]{0:T(128)S(1)} %pad_add_fusion.where_ref, bf16[1024,256]{1,0:T(8,128)(2,1)S(1)} %get-tuple-element.51.twice_ref, f32[1024,128]{1,0:T(8,128)S(1)} %get-tuple-element.52.norm_ref, f32[1024,256]{1,0:T(8,128)S(1)} %get-tuple-element.69.acc_ref, ...), custom_call_target="tpu_custom_call" | custom-call | flops 1610612736 | bytes 5804040 | tf_op jit(solution)/shard_map/rest/pallas_call | solution.py:27
  39.6 2.3 %collective-permute-done.10.b_ref = f32[264,256]{1,0:T(8,128)S(1)} collective-permute-done((f32[264,256]{1,0:T(8,128)S(1)}, f32[264,256]{1,0:T(8,128)S(1)}, u32[]{:S(2)}, u32[]{:S(2)}) %collective-permute-start.10) | collective-permute-done | bytes 270368 | tf_op jit(solution)/shard_map/ppermute | solution.py:336
  41.9 3.4 %collective-permute-start.11 = (f32[264,256]{1,0:T(8,128)S(1)}, f32[264,256]{1,0:T(8,128)S(1)}, u32[]{:S(2)}, u32[]{:S(2)}) collective-permute-start(f32[264,256]{1,0:T(8,128)S(1)} %add.3), channel_id=1, source_target_pairs={{0,16},{2,18},{4,20},{6,22},{16,24},{18,26},{20,28},{22,30},{24,8}... | collective-permute-start | bytes 811016 | tf_op jit(solution)/shard_map/ppermute | solution.py:336
  45.4 4.1 %collective-permute-done.12.second_ref = f32[264,256]{1,0:T(8,128)S(1)} collective-permute-done((f32[264,256]{1,0:T(8,128)S(1)}, f32[264,256]{1,0:T(8,128)S(1)}, u32[]{:S(2)}, u32[]{:S(2)}) %collective-permute-start.12) | collective-permute-done | bytes 270368 | tf_op jit(solution)/shard_map/ppermute | solution.py:336
  49.5 4.9 %collective-permute-done.11.first_ref = f32[264,256]{1,0:T(8,128)S(1)} collective-permute-done((f32[264,256]{1,0:T(8,128)S(1)}, f32[264,256]{1,0:T(8,128)S(1)}, u32[]{:S(2)}, u32[]{:S(2)}) %collective-permute-start.11) | collective-permute-done | bytes 270368 | tf_op jit(solution)/shard_map/ppermute | solution.py:336
  54.4 0.8 finish.1.refs_0_
  55.2 0.6 collective-permute-start.14
  55.8 1.6 %collective-permute-start.13 = (f32[264,256]{1,0:T(8,128)S(1)}, f32[264,256]{1,0:T(8,128)S(1)}, u32[]{:S(2)}, u32[]{:S(2)}) collective-permute-start(f32[264,256]{1,0:T(8,128)S(1)} %finish.1.refs_0_), channel_id=1, source_target_pairs={{0,16},{1,5},{2,18},{3,7},{4,20},{5,1},{6,22},{7,3},{8,0},{9,13},{... | collective-permute-start | bytes 811016 | tf_op jit(solution)/shard_map/ppermute | solution.py:433
  57.5 1.3 %collective-permute-start.15 = (f32[264,256]{1,0:T(8,128)S(1)}, f32[264,256]{1,0:T(8,128)S(1)}, u32[]{:S(2)}, u32[]{:S(2)}) collective-permute-start(f32[264,256]{1,0:T(8,128)S(1)} %finish.1.refs_0_), channel_id=1, source_target_pairs={{0,4},{1,3},{2,6},{3,1},{4,0},{5,7},{6,2},{7,5},{8,12},{9,11},{10,... | collective-permute-start | bytes 811016 | tf_op jit(solution)/shard_map/ppermute | solution.py:329
  58.8 5.5 %collective-permute-done.14.second_ref = f32[264,256]{1,0:T(8,128)S(1)} collective-permute-done((f32[264,256]{1,0:T(8,128)S(1)}, f32[264,256]{1,0:T(8,128)S(1)}, u32[]{:S(2)}, u32[]{:S(2)}) %collective-permute-start.14) | collective-permute-done | bytes 270368 | tf_op jit(solution)/shard_map/ppermute | solution.py:433
  65.4 1.6 %collective-permute-start.16 = (f32[264,256]{1,0:T(8,128)S(1)}, f32[264,256]{1,0:T(8,128)S(1)}, u32[]{:S(2)}, u32[]{:S(2)}) collective-permute-start(f32[264,256]{1,0:T(8,128)S(1)} %get-tuple-element.83.refs_2_), channel_id=1, source_target_pairs={{0,16},{1,5},{2,18},{3,7},{4,20},{5,1},{6,22},{7,3},{8,0},{9,13},{... | collective-permute-start | bytes 811016 | tf_op jit(solution)/shard_map/ppermute | solution.py:433
  67.0 1.3 %collective-permute-start.18 = (f32[264,256]{1,0:T(8,128)S(1)}, f32[264,256]{1,0:T(8,128)S(1)}, u32[]{:S(2)}, u32[]{:S(2)}) collective-permute-start(f32[264,256]{1,0:T(8,128)S(1)} %get-tuple-element.83.refs_2_), channel_id=1, source_target_pairs={{0,4},{1,3},{2,6},{3,1},{4,0},{5,7},{6,2},{7,5},{8,12},{9,11},{10,... | collective-permute-start | bytes 811016 | tf_op jit(solution)/shard_map/ppermute | solution.py:329
  68.4 0.7 collective-permute-start.19
  69.1 4.6 %collective-permute-done.17.second_ref = f32[264,256]{1,0:T(8,128)S(1)} collective-permute-done((f32[264,256]{1,0:T(8,128)S(1)}, f32[264,256]{1,0:T(8,128)S(1)}, u32[]{:S(2)}, u32[]{:S(2)}) %collective-permute-start.17) | collective-permute-done | bytes 270368 | tf_op jit(solution)/shard_map/ppermute | solution.py:433
  74.5 2.9 %collective-permute-done.19.refs_4_ = f32[264,256]{1,0:T(8,128)S(1)} collective-permute-done((f32[264,256]{1,0:T(8,128)S(1)}, f32[264,256]{1,0:T(8,128)S(1)}, u32[]{:S(2)}, u32[]{:S(2)}) %collective-permute-start.19) | collective-permute-done | bytes 270368 | tf_op jit(solution)/shard_map/ppermute | solution.py:329
  78.0 1.5 %collective-permute-start.20 = (f32[264,256]{1,0:T(8,128)S(1)}, f32[264,256]{1,0:T(8,128)S(1)}, u32[]{:S(2)}, u32[]{:S(2)}) collective-permute-start(f32[264,256]{1,0:T(8,128)S(1)} %get-tuple-element.86.refs_6_), channel_id=1, source_target_pairs={{0,16},{1,5},{2,18},{3,7},{4,20},{5,1},{6,22},{7,3},{8,0},{9,13},{... | collective-permute-start | bytes 811016 | tf_op jit(solution)/shard_map/ppermute | solution.py:433
  79.4 1.1 %collective-permute-start.23 = (f32[264,256]{1,0:T(8,128)S(1)}, f32[264,256]{1,0:T(8,128)S(1)}, u32[]{:S(2)}, u32[]{:S(2)}) collective-permute-start(f32[264,256]{1,0:T(8,128)S(1)} %get-tuple-element.88.refs_7_), channel_id=1, source_target_pairs={{0,4},{1,3},{2,6},{3,1},{4,0},{5,7},{6,2},{7,5},{8,12},{9,11},{10,... | collective-permute-start | bytes 811016 | tf_op jit(solution)/shard_map/ppermute | solution.py:329
  80.6 0.9 collective-permute-start.22
  81.5 4.5 %collective-permute-done.21.second_ref = f32[264,256]{1,0:T(8,128)S(1)} collective-permute-done((f32[264,256]{1,0:T(8,128)S(1)}, f32[264,256]{1,0:T(8,128)S(1)}, u32[]{:S(2)}, u32[]{:S(2)}) %collective-permute-start.21) | collective-permute-done | bytes 270368 | tf_op jit(solution)/shard_map/ppermute | solution.py:433
  86.6 1.1 %collective-permute-start.27 = (f32[264,256]{1,0:T(8,128)S(1)}, f32[264,256]{1,0:T(8,128)S(1)}, u32[]{:S(2)}, u32[]{:S(2)}) collective-permute-start(f32[264,256]{1,0:T(8,128)S(1)} %collective-permute-done.19.refs_4_), channel_id=1, source_target_pairs={{0,8},{2,10},{4,12},{6,14},{16,0},{18,2},{20,4},{22,6},{24,16},{26... | collective-permute-start | bytes 811016 | tf_op jit(solution)/shard_map/ppermute | solution.py:336
  87.6 0.9 collective-permute-start.26
  88.5 1.0 collective-permute-done.22.refs_1_
  89.5 1.2 %collective-permute-start.25 = (f32[264,256]{1,0:T(8,128)S(1)}, f32[264,256]{1,0:T(8,128)S(1)}, u32[]{:S(2)}, u32[]{:S(2)}) collective-permute-start(f32[264,256]{1,0:T(8,128)S(1)} %get-tuple-element.89.refs_9_), channel_id=1, source_target_pairs={{0,4},{1,3},{2,6},{3,1},{4,0},{5,7},{6,2},{7,5},{8,12},{9,11},{10,... | collective-permute-start | bytes 811016 | tf_op jit(solution)/shard_map/ppermute | solution.py:329
  90.7 1.0 collective-permute-start.24
  91.7 2.1 %place_early.1 = (f32[4096,256]{1,0:T(8,128)}, f32[32,128]{1,0:T(8,128)S(1)}) custom-call(s32[2]{0:T(128)S(1)} %pad_add_fusion.where_ref, f32[264,256]{1,0:T(8,128)S(1)} %finish.1.refs_0_, f32[264,256]{1,0:T(8,128)S(1)} %collective-permute-done.15.refs_1_, f32[264,256]{1,0:T(8,128)S(1)} %get-tuple-element.83.refs_2_, ...), custom_call_target="tpu_custom_call" | custom-call | bytes 2703368 | tf_op jit(solution)/shard_map/place_early/pallas_call | solution.py:27
  93.8 0.6 collective-permute-done.27.refs_3_
  94.4 1.1 %collective-permute-done.26.refs_2_ = f32[264,256]{1,0:T(8,128)S(1)} collective-permute-done((f32[264,256]{1,0:T(8,128)S(1)}, f32[264,256]{1,0:T(8,128)S(1)}, u32[]{:S(2)}, u32[]{:S(2)}) %collective-permute-start.26) | collective-permute-done | bytes 270368 | tf_op jit(solution)/shard_map/ppermute | solution.py:329
  95.5 1.6 %place_middle.1 = (f32[4096,256]{1,0:T(8,128)}, f32[32,128]{1,0:T(8,128)S(1)}) custom-call(s32[2]{0:T(128)S(1)} %pad_add_fusion.where_ref, f32[264,256]{1,0:T(8,128)S(1)} %get-tuple-element.90.refs_0_, f32[264,256]{1,0:T(8,128)S(1)} %collective-permute-done.22.refs_1_, ...), custom_call_target="tpu_custom_call", output_to_operand_aliasing={{0}: (6, {})} | custom-call | bytes 5292040 | tf_op jit(solution)/shard_map/place_middle/pallas_call | solution.py:27
  97.1 2.8 %collective-permute-done.25.refs_1_ = f32[264,256]{1,0:T(8,128)S(1)} collective-permute-done((f32[264,256]{1,0:T(8,128)S(1)}, f32[264,256]{1,0:T(8,128)S(1)}, u32[]{:S(2)}, u32[]{:S(2)}) %collective-permute-start.25) | collective-permute-done | bytes 270368 | tf_op jit(solution)/shard_map/ppermute | solution.py:329
  99.9 1.4 %place_late.1 = (f32[4096,256]{1,0:T(8,128)}, f32[32,128]{1,0:T(8,128)}) custom-call(s32[2]{0:T(128)S(1)} %pad_add_fusion.where_ref, f32[264,256]{1,0:T(8,128)S(1)} %collective-permute-done.24.refs_0_, f32[264,256]{1,0:T(8,128)S(1)} %collective-permute-done.25.refs_1_, f32[32,128]{1,0:T(8,128)S(1)} %get-tuple-element.94.refs_2_, ...), custom_call_target="tpu_custom_call", output_to_operand_aliasing={{0}: (4, {})} | custom-call | bytes 4751368 | tf_op jit(solution)/shard_map/place_late/pallas_call | solution.py:27
  (31 shorter events, 5.1 us)
Async XLA Ops:
  0.7 1.0 %copy-start = (bf16[1024,256]{1,0:T(8,128)(2,1)S(1)}, bf16[1024,256]{1,0:T(8,128)(2,1)}, u32[]{:S(2)}) copy-start(bf16[1024,256]{1,0:T(8,128)(2,1)} %points_ref.5) | copy-start | bytes 1572868
  2.3 19.6 %copy-start.1 = (bf16[1024,256]{1,0:T(8,128)(2,1)S(1)}, bf16[1024,256]{1,0:T(8,128)(2,1)}, u32[]{:S(2)}) copy-start(bf16[1024,256]{1,0:T(8,128)(2,1)} %points_ref.5) | copy-start | bytes 1572868
  2.4 15.3 %collective-permute-start.1 = (f32[512,256]{1,0:T(8,128)S(1)}, f32[512,256]{1,0:T(8,128)S(1)}, u32[]{:S(2)}, u32[]{:S(2)}) collective-permute-start(f32[512,256]{1,0:T(8,128)S(1)} %open.1), channel_id=1, source_target_pairs={{0,4},{1,3},{2,6},{3,1},{4,0},{5,7},{6,2},{7,5},{8,12},{9,11},{10,... | collective-permute-start | bytes 1572872 | tf_op jit(solution)/shard_map/ppermute | solution.py:329
  5.4 12.3 %collective-permute-start = (f32[512,256]{1,0:T(8,128)S(1)}, f32[512,256]{1,0:T(8,128)S(1)}, u32[]{:S(2)}, u32[]{:S(2)}) collective-permute-start(f32[512,256]{1,0:T(8,128)S(1)} %open.1), channel_id=1, source_target_pairs={{0,2},{1,5},{2,0},{3,7},{4,6},{5,1},{6,4},{7,3},{8,10},{9,13},{10,... | collective-permute-start | bytes 1572872 | tf_op jit(solution)/shard_map/ppermute | solution.py:329
  6.9 1.6 %copy-start.2 = (bf16[4096,256]{1,0:T(8,128)(2,1)S(1)}, bf16[4096,256]{1,0:T(8,128)(2,1)}, u32[]{:S(2)}) copy-start(bf16[4096,256]{1,0:T(8,128)(2,1)} %c_ref.1) | copy-start | bytes 6291460
  14.4 1.2 %collective-permute-start.2 = (f32[2,1024]{1,0:T(2,128)S(1)}, f32[2,1024]{1,0:T(2,128)S(1)}, u32[]{:S(2)}, u32[]{:S(2)}) collective-permute-start(f32[2,1024]{1,0:T(2,128)S(1)} %get-tuple-element.53.refs_0_), channel_id=1, source_target_pairs={{0,1},{1,0},{2,3},{3,2},{4,5},{5,4},{6,7},{7,6},{8,9},{9,8},{10,11... | collective-permute-start | bytes 24584 | tf_op jit(solution)/shard_map/ppermute | solution.py:332
  18.3 5.1 %collective-permute-start.3 = (f32[512,256]{1,0:T(8,128)S(1)}, f32[512,256]{1,0:T(8,128)S(1)}, u32[]{:S(2)}, u32[]{:S(2)}) collective-permute-start(f32[512,256]{1,0:T(8,128)S(1)} %collective-permute-done.a_ref.refs_0_), channel_id=1, source_target_pairs={{0,1},{1,0},{2,3},{3,2},{4,5},{5,4},{6,7},{7,6},{8,9},{9,8},{10,11... | collective-permute-start | bytes 1572872 | tf_op jit(solution)/shard_map/ppermute | solution.py:332
  18.6 4.8 %collective-permute-start.4 = (f32[512,256]{1,0:T(8,128)S(1)}, f32[512,256]{1,0:T(8,128)S(1)}, u32[]{:S(2)}, u32[]{:S(2)}) collective-permute-start(f32[512,256]{1,0:T(8,128)S(1)} %collective-permute-done.1.b_ref.refs_2_), channel_id=1, source_target_pairs={{0,1},{1,0},{2,3},{3,2},{4,5},{5,4},{6,7},{7,6},{8,9},{9,8},{10,11... | collective-permute-start | bytes 1572872 | tf_op jit(solution)/shard_map/ppermute | solution.py:332
  18.8 9.6 %collective-permute-start.5 = (f32[264,256]{1,0:T(8,128)S(1)}, f32[264,256]{1,0:T(8,128)S(1)}, u32[]{:S(2)}, u32[]{:S(2)}) collective-permute-start(f32[264,256]{1,0:T(8,128)S(1)} %get-tuple-element.64), channel_id=1, source_target_pairs={{0,4},{1,3},{2,6},{3,1},{4,0},{5,7},{6,2},{7,5},{8,12},{9,11},{10,... | collective-permute-start | bytes 811016 | tf_op jit(solution)/shard_map/ppermute | solution.py:329
  21.3 7.1 %collective-permute-start.6 = (f32[264,256]{1,0:T(8,128)S(1)}, f32[264,256]{1,0:T(8,128)S(1)}, u32[]{:S(2)}, u32[]{:S(2)}) collective-permute-start(f32[264,256]{1,0:T(8,128)S(1)} %get-tuple-element.65), channel_id=1, source_target_pairs={{0,2},{1,5},{2,0},{3,7},{4,6},{5,1},{6,4},{7,3},{8,10},{9,13},{10,... | collective-permute-start | bytes 811016 | tf_op jit(solution)/shard_map/ppermute | solution.py:329
  23.4 5.9 %collective-permute-start.7 = (f32[4,256]{1,0:T(4,128)S(1)}, f32[4,256]{1,0:T(4,128)S(1)}, u32[]{:S(2)}, u32[]{:S(2)}) collective-permute-start(f32[4,256]{1,0:T(4,128)S(1)} %get-tuple-element.68.lse_ref), channel_id=1, source_target_pairs={{0,6},{2,4},{4,2},{6,0},{8,14},{10,12},{12,10},{14,8},{16,22},{18,... | collective-permute-start | bytes 12296 | tf_op jit(solution)/shard_map/ppermute | solution.py:368
  29.3 1.9 %collective-permute-start.8 = (f32[264,256]{1,0:T(8,128)S(1)}, f32[264,256]{1,0:T(8,128)S(1)}, u32[]{:S(2)}, u32[]{:S(2)}) collective-permute-start(f32[264,256]{1,0:T(8,128)S(1)} %collective-permute-done.5.refs_4_.refs_0_), channel_id=1, source_target_pairs={{0,1},{1,0},{2,3},{3,2},{4,5},{5,4},{6,7},{7,6},{8,9},{9,8},{10,11... | collective-permute-start | bytes 811016 | tf_op jit(solution)/shard_map/ppermute | solution.py:332
  29.3 1.9 %collective-permute-start.9 = (f32[264,256]{1,0:T(8,128)S(1)}, f32[264,256]{1,0:T(8,128)S(1)}, u32[]{:S(2)}, u32[]{:S(2)}) collective-permute-start(f32[264,256]{1,0:T(8,128)S(1)} %collective-permute-done.6.refs_6_.refs_5_.refs_2_), channel_id=1, source_target_pairs={{0,1},{1,0},{2,3},{3,2},{4,5},{5,4},{6,7},{7,6},{8,9},{9,8},{10,11... | collective-permute-start | bytes 811016 | tf_op jit(solution)/shard_map/ppermute | solution.py:332
  32.4 9.5 %collective-permute-start.10 = (f32[264,256]{1,0:T(8,128)S(1)}, f32[264,256]{1,0:T(8,128)S(1)}, u32[]{:S(2)}, u32[]{:S(2)}) collective-permute-start(f32[264,256]{1,0:T(8,128)S(1)} %first.1), channel_id=1, source_target_pairs={{0,16},{2,18},{4,20},{6,22},{16,24},{18,26},{20,28},{22,30},{24,8}... | collective-permute-start | bytes 811016 | tf_op jit(solution)/shard_map/ppermute | solution.py:336
  36.7 12.8 %collective-permute-start.12 = (f32[264,256]{1,0:T(8,128)S(1)}, f32[264,256]{1,0:T(8,128)S(1)}, u32[]{:S(2)}, u32[]{:S(2)}) collective-permute-start(f32[264,256]{1,0:T(8,128)S(1)} %rest.3), channel_id=1, source_target_pairs={{0,8},{2,10},{4,12},{6,14},{16,0},{18,2},{20,4},{22,6},{24,16},{26... | collective-permute-start | bytes 811016 | tf_op jit(solution)/shard_map/ppermute | solution.py:336
  41.9 12.5 %collective-permute-start.11 = (f32[264,256]{1,0:T(8,128)S(1)}, f32[264,256]{1,0:T(8,128)S(1)}, u32[]{:S(2)}, u32[]{:S(2)}) collective-permute-start(f32[264,256]{1,0:T(8,128)S(1)} %add.3), channel_id=1, source_target_pairs={{0,16},{2,18},{4,20},{6,22},{16,24},{18,26},{20,28},{22,30},{24,8}... | collective-permute-start | bytes 811016 | tf_op jit(solution)/shard_map/ppermute | solution.py:336
  55.2 9.1 %collective-permute-start.14 = (f32[264,256]{1,0:T(8,128)S(1)}, f32[264,256]{1,0:T(8,128)S(1)}, u32[]{:S(2)}, u32[]{:S(2)}) collective-permute-start(f32[264,256]{1,0:T(8,128)S(1)} %finish.1.refs_0_), channel_id=1, source_target_pairs={{0,2},{1,17},{2,0},{3,19},{4,6},{5,21},{6,4},{7,23},{8,10},{9,1},{... | collective-permute-start | bytes 811016 | tf_op jit(solution)/shard_map/ppermute | solution.py:433
  55.8 8.5 %collective-permute-start.13 = (f32[264,256]{1,0:T(8,128)S(1)}, f32[264,256]{1,0:T(8,128)S(1)}, u32[]{:S(2)}, u32[]{:S(2)}) collective-permute-start(f32[264,256]{1,0:T(8,128)S(1)} %finish.1.refs_0_), channel_id=1, source_target_pairs={{0,16},{1,5},{2,18},{3,7},{4,20},{5,1},{6,22},{7,3},{8,0},{9,13},{... | collective-permute-start | bytes 811016 | tf_op jit(solution)/shard_map/ppermute | solution.py:433
  57.5 7.4 %collective-permute-start.15 = (f32[264,256]{1,0:T(8,128)S(1)}, f32[264,256]{1,0:T(8,128)S(1)}, u32[]{:S(2)}, u32[]{:S(2)}) collective-permute-start(f32[264,256]{1,0:T(8,128)S(1)} %finish.1.refs_0_), channel_id=1, source_target_pairs={{0,4},{1,3},{2,6},{3,1},{4,0},{5,7},{6,2},{7,5},{8,12},{9,11},{10,... | collective-permute-start | bytes 811016 | tf_op jit(solution)/shard_map/ppermute | solution.py:329
  64.9 8.7 %collective-permute-start.17 = (f32[264,256]{1,0:T(8,128)S(1)}, f32[264,256]{1,0:T(8,128)S(1)}, u32[]{:S(2)}, u32[]{:S(2)}) collective-permute-start(f32[264,256]{1,0:T(8,128)S(1)} %get-tuple-element.83.refs_2_), channel_id=1, source_target_pairs={{0,2},{1,17},{2,0},{3,19},{4,6},{5,21},{6,4},{7,23},{8,10},{9,1},{... | collective-permute-start | bytes 811016 | tf_op jit(solution)/shard_map/ppermute | solution.py:433
  65.4 8.2 %collective-permute-start.16 = (f32[264,256]{1,0:T(8,128)S(1)}, f32[264,256]{1,0:T(8,128)S(1)}, u32[]{:S(2)}, u32[]{:S(2)}) collective-permute-start(f32[264,256]{1,0:T(8,128)S(1)} %get-tuple-element.83.refs_2_), channel_id=1, source_target_pairs={{0,16},{1,5},{2,18},{3,7},{4,20},{5,1},{6,22},{7,3},{8,0},{9,13},{... | collective-permute-start | bytes 811016 | tf_op jit(solution)/shard_map/ppermute | solution.py:433
  67.0 7.4 %collective-permute-start.18 = (f32[264,256]{1,0:T(8,128)S(1)}, f32[264,256]{1,0:T(8,128)S(1)}, u32[]{:S(2)}, u32[]{:S(2)}) collective-permute-start(f32[264,256]{1,0:T(8,128)S(1)} %get-tuple-element.83.refs_2_), channel_id=1, source_target_pairs={{0,4},{1,3},{2,6},{3,1},{4,0},{5,7},{6,2},{7,5},{8,12},{9,11},{10,... | collective-permute-start | bytes 811016 | tf_op jit(solution)/shard_map/ppermute | solution.py:329
  68.4 9.0 %collective-permute-start.19 = (f32[264,256]{1,0:T(8,128)S(1)}, f32[264,256]{1,0:T(8,128)S(1)}, u32[]{:S(2)}, u32[]{:S(2)}) collective-permute-start(f32[264,256]{1,0:T(8,128)S(1)} %get-tuple-element.85.refs_3_), channel_id=1, source_target_pairs={{0,4},{1,3},{2,6},{3,1},{4,0},{5,7},{6,2},{7,5},{8,12},{9,11},{10,... | collective-permute-start | bytes 811016 | tf_op jit(solution)/shard_map/ppermute | solution.py:329
  77.4 8.6 %collective-permute-start.21 = (f32[264,256]{1,0:T(8,128)S(1)}, f32[264,256]{1,0:T(8,128)S(1)}, u32[]{:S(2)}, u32[]{:S(2)}) collective-permute-start(f32[264,256]{1,0:T(8,128)S(1)} %get-tuple-element.86.refs_6_), channel_id=1, source_target_pairs={{0,2},{1,17},{2,0},{3,19},{4,6},{5,21},{6,4},{7,23},{8,10},{9,1},{... | collective-permute-start | bytes 811016 | tf_op jit(solution)/shard_map/ppermute | solution.py:433
  78.0 8.0 %collective-permute-start.20 = (f32[264,256]{1,0:T(8,128)S(1)}, f32[264,256]{1,0:T(8,128)S(1)}, u32[]{:S(2)}, u32[]{:S(2)}) collective-permute-start(f32[264,256]{1,0:T(8,128)S(1)} %get-tuple-element.86.refs_6_), channel_id=1, source_target_pairs={{0,16},{1,5},{2,18},{3,7},{4,20},{5,1},{6,22},{7,3},{8,0},{9,13},{... | collective-permute-start | bytes 811016 | tf_op jit(solution)/shard_map/ppermute | solution.py:433
  79.4 9.1 %collective-permute-start.23 = (f32[264,256]{1,0:T(8,128)S(1)}, f32[264,256]{1,0:T(8,128)S(1)}, u32[]{:S(2)}, u32[]{:S(2)}) collective-permute-start(f32[264,256]{1,0:T(8,128)S(1)} %get-tuple-element.88.refs_7_), channel_id=1, source_target_pairs={{0,4},{1,3},{2,6},{3,1},{4,0},{5,7},{6,2},{7,5},{8,12},{9,11},{10,... | collective-permute-start | bytes 811016 | tf_op jit(solution)/shard_map/ppermute | solution.py:329
  80.6 8.9 %collective-permute-start.22 = (f32[264,256]{1,0:T(8,128)S(1)}, f32[264,256]{1,0:T(8,128)S(1)}, u32[]{:S(2)}, u32[]{:S(2)}) collective-permute-start(f32[264,256]{1,0:T(8,128)S(1)} %get-tuple-element.86.refs_6_), channel_id=1, source_target_pairs={{0,4},{1,3},{2,6},{3,1},{4,0},{5,7},{6,2},{7,5},{8,12},{9,11},{10,... | collective-permute-start | bytes 811016 | tf_op jit(solution)/shard_map/ppermute | solution.py:329
  86.6 7.9 %collective-permute-start.27 = (f32[264,256]{1,0:T(8,128)S(1)}, f32[264,256]{1,0:T(8,128)S(1)}, u32[]{:S(2)}, u32[]{:S(2)}) collective-permute-start(f32[264,256]{1,0:T(8,128)S(1)} %collective-permute-done.19.refs_4_), channel_id=1, source_target_pairs={{0,8},{2,10},{4,12},{6,14},{16,0},{18,2},{20,4},{22,6},{24,16},{26... | collective-permute-start | bytes 811016 | tf_op jit(solution)/shard_map/ppermute | solution.py:336
  87.6 7.9 %collective-permute-start.26 = (f32[264,256]{1,0:T(8,128)S(1)}, f32[264,256]{1,0:T(8,128)S(1)}, u32[]{:S(2)}, u32[]{:S(2)}) collective-permute-start(f32[264,256]{1,0:T(8,128)S(1)} %get-tuple-element.90.refs_0_), channel_id=1, source_target_pairs={{0,4},{1,3},{2,6},{3,1},{4,0},{5,7},{6,2},{7,5},{8,12},{9,11},{10,... | collective-permute-start | bytes 811016 | tf_op jit(solution)/shard_map/ppermute | solution.py:329
  89.5 10.4 %collective-permute-start.25 = (f32[264,256]{1,0:T(8,128)S(1)}, f32[264,256]{1,0:T(8,128)S(1)}, u32[]{:S(2)}, u32[]{:S(2)}) collective-permute-start(f32[264,256]{1,0:T(8,128)S(1)} %get-tuple-element.89.refs_9_), channel_id=1, source_target_pairs={{0,4},{1,3},{2,6},{3,1},{4,0},{5,7},{6,2},{7,5},{8,12},{9,11},{10,... | collective-permute-start | bytes 811016 | tf_op jit(solution)/shard_map/ppermute | solution.py:329
  90.7 9.2 %collective-permute-start.24 = (f32[264,256]{1,0:T(8,128)S(1)}, f32[264,256]{1,0:T(8,128)S(1)}, u32[]{:S(2)}, u32[]{:S(2)}) collective-permute-start(f32[264,256]{1,0:T(8,128)S(1)} %get-tuple-element.89.refs_9_), channel_id=1, source_target_pairs={{0,2},{1,5},{2,0},{3,7},{4,6},{5,1},{6,4},{7,3},{8,10},{9,13},{10,... | collective-permute-start | bytes 811016 | tf_op jit(solution)/shard_map/ppermute | solution.py:329

commit v17 on v14

--- a/solution.py
+++ b/solution.py
@@ -416,9 +416,11 @@
         got[1, s], got[2, s] = exchange(x, 0), exchange(x, 1)
         if s == steps[-1]:
             break
-        got[3, s] = exchange(got[1, s], 1)
+        got[3, s] = exchange(got[2, s], 0) if s == -1 else exchange(got[1, s], 1)
         plane_b.append(got[2, s])
         previous, older = (plane_b[-2 if s == steps[-2] else -1], *older[:1]), (*older[1:], got[3, s])
+        if s == -1:
+            previous += (got[1, s],)
         ahead_of = steps[([0] + steps).index(s)]
         x = got[0, ahead_of + (1 if ahead_of < 0 else -1)]
         if ahead_of > 0:

time: 95.2 us -> 95.6 us (level)
  transfers between devices with their start and end apart: 28 -> 28, of which waited for: 14 -> 16; matrix products, arithmetic and copies ran while one was open for 0% -> 0% of each run, Pallas kernels for 18% -> 18%
where the time goes in v17:
time: 95.6 us; the launch traced here: 95.4 us
  waiting for transfers between devices  37.8 us (40%)
  starting transfers between devices  32.6 us (34%)
  Pallas kernels  21.3 us (22%)
  local copies, waits for them, and re-layouts  2.64 us (3%)
  between operations  0.96 us (1%)
    pallas_call x13, Pallas kernels, call(): pl.pallas_call(kernel, out_shape=out_shape, in_specs=in_specs, out_specs=...  21.3 us
    ppermute x7, waiting for transfers between devices, ring(): lax.ppermute(x, 'dp', [(4 * a + i, 4 * b + i) for a, b in pairs for i in...  20 us
    ppermute x15, starting transfers between devices, exchange(): return lax.ppermute(x, ('dp', 'cent'), pairs)  17.5 us
    ppermute x15, waiting for transfers between devices, exchange(): return lax.ppermute(x, ('dp', 'cent'), pairs)  15.7 us
    ppermute x7, starting transfers between devices, ring(): lax.ppermute(x, 'dp', [(4 * a + i, 4 * b + i) for a, b in pairs for i in...  13.1 us
    unnamed x6, local copies, waits for them, and re-layouts  2.64 us
  transfers between devices with their start and end apart: 28, of which 16 were waited for; matrix products, arithmetic and copies ran while one was open for 0% of the time, Pallas kernels for 18%

profile of v17, /device:TPU:0, one launch (start us, length us, event | category | flops | bytes accessed | tf_op | source)
XLA Modules:
  0.0 95.4 jit_solution(1831612217563133936)
XLA Ops:
  0.7 1.0 %copy-done = bf16[1024,256]{1,0:T(8,128)(2,1)S(1)} copy-done((bf16[1024,256]{1,0:T(8,128)(2,1)S(1)}, bf16[1024,256]{1,0:T(8,128)(2,1)}, u32[]{:S(2)}) %copy-start) | copy-done | bytes 524312
  2.4 3.0 %collective-permute-start.1 = (f32[512,256]{1,0:T(8,128)S(1)}, f32[512,256]{1,0:T(8,128)S(1)}, u32[]{:S(2)}, u32[]{:S(2)}) collective-permute-start(f32[512,256]{1,0:T(8,128)S(1)} %open.1), channel_id=1, source_target_pairs={{0,4},{1,3},{2,6},{3,1},{4,0},{5,7},{6,2},{7,5},{8,12},{9,11},{10,... | collective-permute-start | bytes 1572872 | tf_op jit(solution)/shard_map/ppermute | solution.py:315
  5.4 1.5 %collective-permute-start = (f32[512,256]{1,0:T(8,128)S(1)}, f32[512,256]{1,0:T(8,128)S(1)}, u32[]{:S(2)}, u32[]{:S(2)}) collective-permute-start(f32[512,256]{1,0:T(8,128)S(1)} %open.1), channel_id=1, source_target_pairs={{0,2},{1,5},{2,0},{3,7},{4,6},{5,1},{6,4},{7,3},{8,10},{9,13},{10,... | collective-permute-start | bytes 1572872 | tf_op jit(solution)/shard_map/ppermute | solution.py:315
  6.9 1.6 %copy-done.2 = bf16[4096,256]{1,0:T(8,128)(2,1)S(1)} copy-done((bf16[4096,256]{1,0:T(8,128)(2,1)S(1)}, bf16[4096,256]{1,0:T(8,128)(2,1)}, u32[]{:S(2)}) %copy-start.2) | copy-done | bytes 2097176
  8.5 5.9 %stats.1 = (f32[2,1024]{1,0:T(2,128)S(1)}, bf16[1024,256]{1,0:T(8,128)(2,1)S(1)}, f32[1024,128]{1,0:T(8,128)S(1)}) custom-call(s32[2]{0:T(128)S(1)} %pad_add_fusion.where_ref, bf16[1024,256]{1,0:T(8,128)(2,1)S(1)} %copy-done, bf16[4096,256]{1,0:T(8,128)(2,1)S(1)} %copy-done.2), custom_call_target="tpu_custom_call" | custom-call | flops 4294967296 | bytes 2621448 | tf_op jit(solution)/shard_map/stats/pallas_call | solution.py:27
  14.5 1.2 %collective-permute-done.2.refs_1_ = f32[2,1024]{1,0:T(2,128)S(1)} collective-permute-done((f32[2,1024]{1,0:T(2,128)S(1)}, f32[2,1024]{1,0:T(2,128)S(1)}, u32[]{:S(2)}, u32[]{:S(2)}) %collective-permute-start.2) | collective-permute-done | bytes 8224 | tf_op jit(solution)/shard_map/ppermute | solution.py:318
  15.6 2.0 %collective-permute-done.1.b_ref.refs_2_ = f32[512,256]{1,0:T(8,128)S(1)} collective-permute-done((f32[512,256]{1,0:T(8,128)S(1)}, f32[512,256]{1,0:T(8,128)S(1)}, u32[]{:S(2)}, u32[]{:S(2)}) %collective-permute-start.1) | collective-permute-done | bytes 524320 | tf_op jit(solution)/shard_map/ppermute | solution.py:315
  17.6 0.6 lse.1
  18.8 2.5 %collective-permute-start.5 = (f32[264,256]{1,0:T(8,128)S(1)}, f32[264,256]{1,0:T(8,128)S(1)}, u32[]{:S(2)}, u32[]{:S(2)}) collective-permute-start(f32[264,256]{1,0:T(8,128)S(1)} %get-tuple-element.59), channel_id=1, source_target_pairs={{0,4},{1,3},{2,6},{3,1},{4,0},{5,7},{6,2},{7,5},{8,12},{9,11},{10,... | collective-permute-start | bytes 811016 | tf_op jit(solution)/shard_map/ppermute | solution.py:315
  21.3 0.7 collective-permute-start.6
  21.9 1.4 %own.1 = (f32[1024,256]{1,0:T(8,128)S(1)}, f32[1024,128]{1,0:T(8,128)S(1)}) custom-call(bf16[1024,256]{1,0:T(8,128)(2,1)S(1)} %copy-done.1, bf16[1024,256]{1,0:T(8,128)(2,1)S(1)} %get-tuple-element.46.twice_ref, f32[1024,128]{1,0:T(8,128)S(1)} %get-tuple-element.47.norm_ref, f32[4,256]{1,0:T(4,128)S(1)} %get-tuple-element.63.lse_ref), custom_call_target="tpu_custom_call" | custom-call | flops 1073741824 | bytes 1576960 | tf_op jit(solution)/shard_map/own/pallas_call | solution.py:27
  23.4 0.8 collective-permute-start.7
  24.2 4.1 %collective-permute-done.5.refs_4_.refs_0_ = f32[264,256]{1,0:T(8,128)S(1)} collective-permute-done((f32[264,256]{1,0:T(8,128)S(1)}, f32[264,256]{1,0:T(8,128)S(1)}, u32[]{:S(2)}, u32[]{:S(2)}) %collective-permute-start.5) | collective-permute-done | bytes 270368 | tf_op jit(solution)/shard_map/ppermute | solution.py:315
  28.4 0.9 collective-permute-done.7.lse_ref
  29.8 1.4 %lead.1 = (f32[256,256]{1,0:T(8,128)S(1)}, f32[256,128]{1,0:T(8,128)S(1)}) custom-call(s32[2]{0:T(128)S(1)} %pad_add_fusion.where_ref, bf16[1024,256]{1,0:T(8,128)(2,1)S(1)} %get-tuple-element.46.twice_ref, f32[1024,128]{1,0:T(8,128)S(1)} %get-tuple-element.47.norm_ref, f32[1024,256]{1,0:T(8,128)S(1)} %get-tuple-element.64.acc_ref, ...), custom_call_target="tpu_custom_call" | custom-call | flops 536870912 | bytes 5259272 | tf_op jit(solution)/shard_map/lead/pallas_call | solution.py:27
  31.2 1.1 %first.1 = f32[264,256]{1,0:T(8,128)S(1)} custom-call(s32[2]{0:T(128)S(1)} %pad_add_fusion.where_ref, bf16[1024,256]{1,0:T(8,128)(2,1)S(1)} %get-tuple-element.46.twice_ref, f32[1024,128]{1,0:T(8,128)S(1)} %get-tuple-element.47.norm_ref, f32[4,256]{1,0:T(4,128)S(1)} %collective-permute-done.7.lse_ref, f32[256,256]{1,0:T(8,128)S(1)} %get-tuple-element.75.lead_acc_ref, ...), custom_call_target="tpu_custom_call" | custom-call | flops 536870912 | bytes 2527240 | tf_op jit(solution)/shard_map/first/pallas_call | solution.py:27
  32.4 2.6 %collective-permute-start.10 = (f32[264,256]{1,0:T(8,128)S(1)}, f32[264,256]{1,0:T(8,128)S(1)}, u32[]{:S(2)}, u32[]{:S(2)}) collective-permute-start(f32[264,256]{1,0:T(8,128)S(1)} %first.1), channel_id=1, source_target_pairs={{0,16},{2,18},{4,20},{6,22},{16,24},{18,26},{20,28},{22,30},{24,8}... | collective-permute-start | bytes 811016 | tf_op jit(solution)/shard_map/ppermute | solution.py:322
  35.0 1.7 %rest.3 = f32[264,256]{1,0:T(8,128)S(1)} custom-call(s32[2]{0:T(128)S(1)} %pad_add_fusion.where_ref, bf16[1024,256]{1,0:T(8,128)(2,1)S(1)} %get-tuple-element.46.twice_ref, f32[1024,128]{1,0:T(8,128)S(1)} %get-tuple-element.47.norm_ref, f32[1024,256]{1,0:T(8,128)S(1)} %get-tuple-element.64.acc_ref, f32[1024,128]{1,0:T(8,128)S(1)} %get-tuple-element.65.cnt_ref, ...), custom_call_target="tpu_custom_call" | custom-call | flops 805306368 | bytes 5804040 | tf_op jit(solution)/shard_map/rest/pallas_call | solution.py:27
  37.0 2.6 %rest.2 = (f32[264,256]{1,0:T(8,128)S(1)}, f32[264,256]{1,0:T(8,128)S(1)}) custom-call(s32[2]{0:T(128)S(1)} %pad_add_fusion.where_ref, bf16[1024,256]{1,0:T(8,128)(2,1)S(1)} %get-tuple-element.46.twice_ref, f32[1024,128]{1,0:T(8,128)S(1)} %get-tuple-element.47.norm_ref, f32[1024,256]{1,0:T(8,128)S(1)} %get-tuple-element.64.acc_ref, ...), custom_call_target="tpu_custom_call" | custom-call | flops 1610612736 | bytes 5804040 | tf_op jit(solution)/shard_map/rest/pallas_call | solution.py:27
  39.6 2.3 %collective-permute-done.10.b_ref = f32[264,256]{1,0:T(8,128)S(1)} collective-permute-done((f32[264,256]{1,0:T(8,128)S(1)}, f32[264,256]{1,0:T(8,128)S(1)}, u32[]{:S(2)}, u32[]{:S(2)}) %collective-permute-start.10) | collective-permute-done | bytes 270368 | tf_op jit(solution)/shard_map/ppermute | solution.py:322
  41.9 3.4 %collective-permute-start.11 = (f32[264,256]{1,0:T(8,128)S(1)}, f32[264,256]{1,0:T(8,128)S(1)}, u32[]{:S(2)}, u32[]{:S(2)}) collective-permute-start(f32[264,256]{1,0:T(8,128)S(1)} %add.3), channel_id=1, source_target_pairs={{0,16},{2,18},{4,20},{6,22},{16,24},{18,26},{20,28},{22,30},{24,8}... | collective-permute-start | bytes 811016 | tf_op jit(solution)/shard_map/ppermute | solution.py:322
  45.4 4.1 %collective-permute-done.12.second_ref = f32[264,256]{1,0:T(8,128)S(1)} collective-permute-done((f32[264,256]{1,0:T(8,128)S(1)}, f32[264,256]{1,0:T(8,128)S(1)}, u32[]{:S(2)}, u32[]{:S(2)}) %collective-permute-start.12) | collective-permute-done | bytes 270368 | tf_op jit(solution)/shard_map/ppermute | solution.py:322
  49.5 4.9 %collective-permute-done.11.first_ref = f32[264,256]{1,0:T(8,128)S(1)} collective-permute-done((f32[264,256]{1,0:T(8,128)S(1)}, f32[264,256]{1,0:T(8,128)S(1)}, u32[]{:S(2)}, u32[]{:S(2)}) %collective-permute-start.11) | collective-permute-done | bytes 270368 | tf_op jit(solution)/shard_map/ppermute | solution.py:322
  54.4 0.8 finish.1.refs_0_
  55.2 1.7 %collective-permute-start.13 = (f32[264,256]{1,0:T(8,128)S(1)}, f32[264,256]{1,0:T(8,128)S(1)}, u32[]{:S(2)}, u32[]{:S(2)}) collective-permute-start(f32[264,256]{1,0:T(8,128)S(1)} %finish.1.refs_0_), channel_id=1, source_target_pairs={{0,16},{2,18},{4,20},{6,22},{16,24},{18,26},{20,28},{22,30},{24,8}... | collective-permute-start | bytes 811016 | tf_op jit(solution)/shard_map/ppermute | solution.py:322
  56.9 0.9 collective-permute-start.16
  57.8 1.0 %collective-permute-start.18 = (f32[264,256]{1,0:T(8,128)S(1)}, f32[264,256]{1,0:T(8,128)S(1)}, u32[]{:S(2)}, u32[]{:S(2)}) collective-permute-start(f32[264,256]{1,0:T(8,128)S(1)} %finish.1.refs_0_), channel_id=1, source_target_pairs={{0,2},{1,5},{2,0},{3,7},{4,6},{5,1},{6,4},{7,3},{8,10},{9,13},{10,... | collective-permute-start | bytes 811016 | tf_op jit(solution)/shard_map/ppermute | solution.py:315
  58.8 4.8 %collective-permute-done.13.refs_4_ = f32[264,256]{1,0:T(8,128)S(1)} collective-permute-done((f32[264,256]{1,0:T(8,128)S(1)}, f32[264,256]{1,0:T(8,128)S(1)}, u32[]{:S(2)}, u32[]{:S(2)}) %collective-permute-start.13) | collective-permute-done | bytes 270368 | tf_op jit(solution)/shard_map/ppermute | solution.py:322
  63.6 1.8 %collective-permute-start.14 = (f32[264,256]{1,0:T(8,128)S(1)}, f32[264,256]{1,0:T(8,128)S(1)}, u32[]{:S(2)}, u32[]{:S(2)}) collective-permute-start(f32[264,256]{1,0:T(8,128)S(1)} %collective-permute-done.13.refs_4_), channel_id=1, source_target_pairs={{0,16},{2,18},{4,20},{6,22},{16,24},{18,26},{20,28},{22,30},{24,8}... | collective-permute-start | bytes 811016 | tf_op jit(solution)/shard_map/ppermute | solution.py:322
  65.5 0.6 collective-permute-start.22
  66.1 1.3 %collective-permute-start.17 = (f32[264,256]{1,0:T(8,128)S(1)}, f32[264,256]{1,0:T(8,128)S(1)}, u32[]{:S(2)}, u32[]{:S(2)}) collective-permute-start(f32[264,256]{1,0:T(8,128)S(1)} %collective-permute-done.13.refs_4_), channel_id=1, source_target_pairs={{0,4},{1,3},{2,6},{3,1},{4,0},{5,7},{6,2},{7,5},{8,12},{9,11},{10,... | collective-permute-start | bytes 811016 | tf_op jit(solution)/shard_map/ppermute | solution.py:315
  67.4 0.7 collective-permute-start.19
  68.1 3.1 %collective-permute-done.14.refs_8_ = f32[264,256]{1,0:T(8,128)S(1)} collective-permute-done((f32[264,256]{1,0:T(8,128)S(1)}, f32[264,256]{1,0:T(8,128)S(1)}, u32[]{:S(2)}, u32[]{:S(2)}) %collective-permute-start.14) | collective-permute-done | bytes 270368 | tf_op jit(solution)/shard_map/ppermute | solution.py:322
  71.1 2.1 %collective-permute-start.15 = (f32[264,256]{1,0:T(8,128)S(1)}, f32[264,256]{1,0:T(8,128)S(1)}, u32[]{:S(2)}, u32[]{:S(2)}) collective-permute-start(f32[264,256]{1,0:T(8,128)S(1)} %finish.1.refs_0_), channel_id=1, source_target_pairs={{0,8},{2,10},{4,12},{6,14},{16,0},{18,2},{20,4},{22,6},{24,16},{26... | collective-permute-start | bytes 811016 | tf_op jit(solution)/shard_map/ppermute | solution.py:322
  73.2 1.7 %collective-permute-done.22.refs_5_ = f32[264,256]{1,0:T(8,128)S(1)} collective-permute-done((f32[264,256]{1,0:T(8,128)S(1)}, f32[264,256]{1,0:T(8,128)S(1)}, u32[]{:S(2)}, u32[]{:S(2)}) %collective-permute-start.22) | collective-permute-done | bytes 270368 | tf_op jit(solution)/shard_map/ppermute | solution.py:315
  74.9 0.6 collective-permute-start.23
  75.5 1.4 %collective-permute-start.27 = (f32[264,256]{1,0:T(8,128)S(1)}, f32[264,256]{1,0:T(8,128)S(1)}, u32[]{:S(2)}, u32[]{:S(2)}) collective-permute-start(f32[264,256]{1,0:T(8,128)S(1)} %collective-permute-done.17.refs_6_), channel_id=1, source_target_pairs={{0,2},{1,5},{2,0},{3,7},{4,6},{5,1},{6,4},{7,3},{8,10},{9,13},{10,... | collective-permute-start | bytes 811016 | tf_op jit(solution)/shard_map/ppermute | solution.py:315
  76.9 0.9 collective-permute-start.24
  77.8 0.8 collective-permute-done.15.refs_9_
  78.6 1.2 %collective-permute-start.26 = (f32[264,256]{1,0:T(8,128)S(1)}, f32[264,256]{1,0:T(8,128)S(1)}, u32[]{:S(2)}, u32[]{:S(2)}) collective-permute-start(f32[264,256]{1,0:T(8,128)S(1)} %collective-permute-done.19.refs_3_), channel_id=1, source_target_pairs={{0,8},{2,10},{4,12},{6,14},{16,0},{18,2},{20,4},{22,6},{24,16},{26... | collective-permute-start | bytes 811016 | tf_op jit(solution)/shard_map/ppermute | solution.py:322
  79.8 1.8 %collective-permute-done.23.refs_0_ = f32[264,256]{1,0:T(8,128)S(1)} collective-permute-done((f32[264,256]{1,0:T(8,128)S(1)}, f32[264,256]{1,0:T(8,128)S(1)}, u32[]{:S(2)}, u32[]{:S(2)}) %collective-permute-start.23) | collective-permute-done | bytes 270368 | tf_op jit(solution)/shard_map/ppermute | solution.py:315
  81.6 0.7 collective-permute-start.25
  82.4 1.3 %collective-permute-start.21 = (f32[264,256]{1,0:T(8,128)S(1)}, f32[264,256]{1,0:T(8,128)S(1)}, u32[]{:S(2)}, u32[]{:S(2)}) collective-permute-start(f32[264,256]{1,0:T(8,128)S(1)} %collective-permute-done.15.refs_9_), channel_id=1, source_target_pairs={{0,4},{1,3},{2,6},{3,1},{4,0},{5,7},{6,2},{7,5},{8,12},{9,11},{10,... | collective-permute-start | bytes 811016 | tf_op jit(solution)/shard_map/ppermute | solution.py:315
  83.7 3.8 %collective-permute-done.27.refs_7_ = f32[264,256]{1,0:T(8,128)S(1)} collective-permute-done((f32[264,256]{1,0:T(8,128)S(1)}, f32[264,256]{1,0:T(8,128)S(1)}, u32[]{:S(2)}, u32[]{:S(2)}) %collective-permute-start.27) | collective-permute-done | bytes 270368 | tf_op jit(solution)/shard_map/ppermute | solution.py:315
  87.8 2.1 %place_early.1 = (f32[4096,256]{1,0:T(8,128)}, f32[32,128]{1,0:T(8,128)S(1)}) custom-call(s32[2]{0:T(128)S(1)} %pad_add_fusion.where_ref, f32[264,256]{1,0:T(8,128)S(1)} %finish.1.refs_0_, f32[264,256]{1,0:T(8,128)S(1)} %collective-permute-done.18.refs_1_, f32[264,256]{1,0:T(8,128)S(1)} %collective-permute-done.16.refs_2_, ...), custom_call_target="tpu_custom_call" | custom-call | bytes 2703368 | tf_op jit(solution)/shard_map/place_early/pallas_call | solution.py:27
  90.4 1.6 %place_middle.1 = (f32[4096,256]{1,0:T(8,128)}, f32[32,128]{1,0:T(8,128)S(1)}) custom-call(s32[2]{0:T(128)S(1)} %pad_add_fusion.where_ref, f32[264,256]{1,0:T(8,128)S(1)} %collective-permute-done.23.refs_0_, f32[264,256]{1,0:T(8,128)S(1)} %collective-permute-done.24.refs_1_, ...), custom_call_target="tpu_custom_call", output_to_operand_aliasing={{0}: (6, {})} | custom-call | bytes 5292040 | tf_op jit(solution)/shard_map/place_middle/pallas_call | solution.py:27
  92.0 1.3 %collective-permute-done.21.refs_1_ = f32[264,256]{1,0:T(8,128)S(1)} collective-permute-done((f32[264,256]{1,0:T(8,128)S(1)}, f32[264,256]{1,0:T(8,128)S(1)}, u32[]{:S(2)}, u32[]{:S(2)}) %collective-permute-start.21) | collective-permute-done | bytes 270368 | tf_op jit(solution)/shard_map/ppermute | solution.py:315
  93.9 1.4 %place_late.1 = (f32[4096,256]{1,0:T(8,128)}, f32[32,128]{1,0:T(8,128)}) custom-call(s32[2]{0:T(128)S(1)} %pad_add_fusion.where_ref, f32[264,256]{1,0:T(8,128)S(1)} %collective-permute-done.20.refs_0_, f32[264,256]{1,0:T(8,128)S(1)} %collective-permute-done.21.refs_1_, f32[32,128]{1,0:T(8,128)S(1)} %get-tuple-element.84.refs_2_, ...), custom_call_target="tpu_custom_call", output_to_operand_aliasing={{0}: (4, {})} | custom-call | bytes 4751368 | tf_op jit(solution)/shard_map/place_late/pallas_call | solution.py:27
  (28 shorter events, 3.5 us)
Async XLA Ops:
  0.7 1.0 %copy-start = (bf16[1024,256]{1,0:T(8,128)(2,1)S(1)}, bf16[1024,256]{1,0:T(8,128)(2,1)}, u32[]{:S(2)}) copy-start(bf16[1024,256]{1,0:T(8,128)(2,1)} %points_ref.5) | copy-start | bytes 1572868
  2.3 19.6 %copy-start.1 = (bf16[1024,256]{1,0:T(8,128)(2,1)S(1)}, bf16[1024,256]{1,0:T(8,128)(2,1)}, u32[]{:S(2)}) copy-start(bf16[1024,256]{1,0:T(8,128)(2,1)} %points_ref.5) | copy-start | bytes 1572868
  2.4 15.3 %collective-permute-start.1 = (f32[512,256]{1,0:T(8,128)S(1)}, f32[512,256]{1,0:T(8,128)S(1)}, u32[]{:S(2)}, u32[]{:S(2)}) collective-permute-start(f32[512,256]{1,0:T(8,128)S(1)} %open.1), channel_id=1, source_target_pairs={{0,4},{1,3},{2,6},{3,1},{4,0},{5,7},{6,2},{7,5},{8,12},{9,11},{10,... | collective-permute-start | bytes 1572872 | tf_op jit(solution)/shard_map/ppermute | solution.py:315
  5.4 12.3 %collective-permute-start = (f32[512,256]{1,0:T(8,128)S(1)}, f32[512,256]{1,0:T(8,128)S(1)}, u32[]{:S(2)}, u32[]{:S(2)}) collective-permute-start(f32[512,256]{1,0:T(8,128)S(1)} %open.1), channel_id=1, source_target_pairs={{0,2},{1,5},{2,0},{3,7},{4,6},{5,1},{6,4},{7,3},{8,10},{9,13},{10,... | collective-permute-start | bytes 1572872 | tf_op jit(solution)/shard_map/ppermute | solution.py:315
  6.9 1.6 %copy-start.2 = (bf16[4096,256]{1,0:T(8,128)(2,1)S(1)}, bf16[4096,256]{1,0:T(8,128)(2,1)}, u32[]{:S(2)}) copy-start(bf16[4096,256]{1,0:T(8,128)(2,1)} %c_ref.1) | copy-start | bytes 6291460
  14.4 1.2 %collective-permute-start.2 = (f32[2,1024]{1,0:T(2,128)S(1)}, f32[2,1024]{1,0:T(2,128)S(1)}, u32[]{:S(2)}, u32[]{:S(2)}) collective-permute-start(f32[2,1024]{1,0:T(2,128)S(1)} %get-tuple-element.48.refs_0_), channel_id=1, source_target_pairs={{0,1},{1,0},{2,3},{3,2},{4,5},{5,4},{6,7},{7,6},{8,9},{9,8},{10,11... | collective-permute-start | bytes 24584 | tf_op jit(solution)/shard_map/ppermute | solution.py:318
  18.3 5.1 %collective-permute-start.3 = (f32[512,256]{1,0:T(8,128)S(1)}, f32[512,256]{1,0:T(8,128)S(1)}, u32[]{:S(2)}, u32[]{:S(2)}) collective-permute-start(f32[512,256]{1,0:T(8,128)S(1)} %collective-permute-done.a_ref.refs_0_), channel_id=1, source_target_pairs={{0,1},{1,0},{2,3},{3,2},{4,5},{5,4},{6,7},{7,6},{8,9},{9,8},{10,11... | collective-permute-start | bytes 1572872 | tf_op jit(solution)/shard_map/ppermute | solution.py:318
  18.6 4.8 %collective-permute-start.4 = (f32[512,256]{1,0:T(8,128)S(1)}, f32[512,256]{1,0:T(8,128)S(1)}, u32[]{:S(2)}, u32[]{:S(2)}) collective-permute-start(f32[512,256]{1,0:T(8,128)S(1)} %collective-permute-done.1.b_ref.refs_2_), channel_id=1, source_target_pairs={{0,1},{1,0},{2,3},{3,2},{4,5},{5,4},{6,7},{7,6},{8,9},{9,8},{10,11... | collective-permute-start | bytes 1572872 | tf_op jit(solution)/shard_map/ppermute | solution.py:318
  18.8 9.6 %collective-permute-start.5 = (f32[264,256]{1,0:T(8,128)S(1)}, f32[264,256]{1,0:T(8,128)S(1)}, u32[]{:S(2)}, u32[]{:S(2)}) collective-permute-start(f32[264,256]{1,0:T(8,128)S(1)} %get-tuple-element.59), channel_id=1, source_target_pairs={{0,4},{1,3},{2,6},{3,1},{4,0},{5,7},{6,2},{7,5},{8,12},{9,11},{10,... | collective-permute-start | bytes 811016 | tf_op jit(solution)/shard_map/ppermute | solution.py:315
  21.3 7.1 %collective-permute-start.6 = (f32[264,256]{1,0:T(8,128)S(1)}, f32[264,256]{1,0:T(8,128)S(1)}, u32[]{:S(2)}, u32[]{:S(2)}) collective-permute-start(f32[264,256]{1,0:T(8,128)S(1)} %get-tuple-element.60), channel_id=1, source_target_pairs={{0,2},{1,5},{2,0},{3,7},{4,6},{5,1},{6,4},{7,3},{8,10},{9,13},{10,... | collective-permute-start | bytes 811016 | tf_op jit(solution)/shard_map/ppermute | solution.py:315
  23.4 5.9 %collective-permute-start.7 = (f32[4,256]{1,0:T(4,128)S(1)}, f32[4,256]{1,0:T(4,128)S(1)}, u32[]{:S(2)}, u32[]{:S(2)}) collective-permute-start(f32[4,256]{1,0:T(4,128)S(1)} %get-tuple-element.63.lse_ref), channel_id=1, source_target_pairs={{0,6},{2,4},{4,2},{6,0},{8,14},{10,12},{12,10},{14,8},{16,22},{18,... | collective-permute-start | bytes 12296 | tf_op jit(solution)/shard_map/ppermute | solution.py:354
  29.3 1.9 %collective-permute-start.8 = (f32[264,256]{1,0:T(8,128)S(1)}, f32[264,256]{1,0:T(8,128)S(1)}, u32[]{:S(2)}, u32[]{:S(2)}) collective-permute-start(f32[264,256]{1,0:T(8,128)S(1)} %collective-permute-done.5.refs_4_.refs_0_), channel_id=1, source_target_pairs={{0,1},{1,0},{2,3},{3,2},{4,5},{5,4},{6,7},{7,6},{8,9},{9,8},{10,11... | collective-permute-start | bytes 811016 | tf_op jit(solution)/shard_map/ppermute | solution.py:318
  29.3 1.9 %collective-permute-start.9 = (f32[264,256]{1,0:T(8,128)S(1)}, f32[264,256]{1,0:T(8,128)S(1)}, u32[]{:S(2)}, u32[]{:S(2)}) collective-permute-start(f32[264,256]{1,0:T(8,128)S(1)} %collective-permute-done.6.refs_6_.refs_5_.refs_2_), channel_id=1, source_target_pairs={{0,1},{1,0},{2,3},{3,2},{4,5},{5,4},{6,7},{7,6},{8,9},{9,8},{10,11... | collective-permute-start | bytes 811016 | tf_op jit(solution)/shard_map/ppermute | solution.py:318
  32.4 9.5 %collective-permute-start.10 = (f32[264,256]{1,0:T(8,128)S(1)}, f32[264,256]{1,0:T(8,128)S(1)}, u32[]{:S(2)}, u32[]{:S(2)}) collective-permute-start(f32[264,256]{1,0:T(8,128)S(1)} %first.1), channel_id=1, source_target_pairs={{0,16},{2,18},{4,20},{6,22},{16,24},{18,26},{20,28},{22,30},{24,8}... | collective-permute-start | bytes 811016 | tf_op jit(solution)/shard_map/ppermute | solution.py:322
  36.7 12.8 %collective-permute-start.12 = (f32[264,256]{1,0:T(8,128)S(1)}, f32[264,256]{1,0:T(8,128)S(1)}, u32[]{:S(2)}, u32[]{:S(2)}) collective-permute-start(f32[264,256]{1,0:T(8,128)S(1)} %rest.3), channel_id=1, source_target_pairs={{0,8},{2,10},{4,12},{6,14},{16,0},{18,2},{20,4},{22,6},{24,16},{26... | collective-permute-start | bytes 811016 | tf_op jit(solution)/shard_map/ppermute | solution.py:322
  41.9 12.5 %collective-permute-start.11 = (f32[264,256]{1,0:T(8,128)S(1)}, f32[264,256]{1,0:T(8,128)S(1)}, u32[]{:S(2)}, u32[]{:S(2)}) collective-permute-start(f32[264,256]{1,0:T(8,128)S(1)} %add.3), channel_id=1, source_target_pairs={{0,16},{2,18},{4,20},{6,22},{16,24},{18,26},{20,28},{22,30},{24,8}... | collective-permute-start | bytes 811016 | tf_op jit(solution)/shard_map/ppermute | solution.py:322
  55.2 8.4 %collective-permute-start.13 = (f32[264,256]{1,0:T(8,128)S(1)}, f32[264,256]{1,0:T(8,128)S(1)}, u32[]{:S(2)}, u32[]{:S(2)}) collective-permute-start(f32[264,256]{1,0:T(8,128)S(1)} %finish.1.refs_0_), channel_id=1, source_target_pairs={{0,16},{2,18},{4,20},{6,22},{16,24},{18,26},{20,28},{22,30},{24,8}... | collective-permute-start | bytes 811016 | tf_op jit(solution)/shard_map/ppermute | solution.py:322
  56.9 8.6 %collective-permute-start.16 = (f32[264,256]{1,0:T(8,128)S(1)}, f32[264,256]{1,0:T(8,128)S(1)}, u32[]{:S(2)}, u32[]{:S(2)}) collective-permute-start(f32[264,256]{1,0:T(8,128)S(1)} %finish.1.refs_0_), channel_id=1, source_target_pairs={{0,4},{1,3},{2,6},{3,1},{4,0},{5,7},{6,2},{7,5},{8,12},{9,11},{10,... | collective-permute-start | bytes 811016 | tf_op jit(solution)/shard_map/ppermute | solution.py:315
  57.8 9.6 %collective-permute-start.18 = (f32[264,256]{1,0:T(8,128)S(1)}, f32[264,256]{1,0:T(8,128)S(1)}, u32[]{:S(2)}, u32[]{:S(2)}) collective-permute-start(f32[264,256]{1,0:T(8,128)S(1)} %finish.1.refs_0_), channel_id=1, source_target_pairs={{0,2},{1,5},{2,0},{3,7},{4,6},{5,1},{6,4},{7,3},{8,10},{9,13},{10,... | collective-permute-start | bytes 811016 | tf_op jit(solution)/shard_map/ppermute | solution.py:315
  63.6 7.5 %collective-permute-start.14 = (f32[264,256]{1,0:T(8,128)S(1)}, f32[264,256]{1,0:T(8,128)S(1)}, u32[]{:S(2)}, u32[]{:S(2)}) collective-permute-start(f32[264,256]{1,0:T(8,128)S(1)} %collective-permute-done.13.refs_4_), channel_id=1, source_target_pairs={{0,16},{2,18},{4,20},{6,22},{16,24},{18,26},{20,28},{22,30},{24,8}... | collective-permute-start | bytes 811016 | tf_op jit(solution)/shard_map/ppermute | solution.py:322
  65.5 9.4 %collective-permute-start.22 = (f32[264,256]{1,0:T(8,128)S(1)}, f32[264,256]{1,0:T(8,128)S(1)}, u32[]{:S(2)}, u32[]{:S(2)}) collective-permute-start(f32[264,256]{1,0:T(8,128)S(1)} %collective-permute-done.13.refs_4_), channel_id=1, source_target_pairs={{0,2},{1,5},{2,0},{3,7},{4,6},{5,1},{6,4},{7,3},{8,10},{9,13},{10,... | collective-permute-start | bytes 811016 | tf_op jit(solution)/shard_map/ppermute | solution.py:315
  66.1 8.8 %collective-permute-start.17 = (f32[264,256]{1,0:T(8,128)S(1)}, f32[264,256]{1,0:T(8,128)S(1)}, u32[]{:S(2)}, u32[]{:S(2)}) collective-permute-start(f32[264,256]{1,0:T(8,128)S(1)} %collective-permute-done.13.refs_4_), channel_id=1, source_target_pairs={{0,4},{1,3},{2,6},{3,1},{4,0},{5,7},{6,2},{7,5},{8,12},{9,11},{10,... | collective-permute-start | bytes 811016 | tf_op jit(solution)/shard_map/ppermute | solution.py:315
  67.4 10.4 %collective-permute-start.19 = (f32[264,256]{1,0:T(8,128)S(1)}, f32[264,256]{1,0:T(8,128)S(1)}, u32[]{:S(2)}, u32[]{:S(2)}) collective-permute-start(f32[264,256]{1,0:T(8,128)S(1)} %collective-permute-done.18.refs_1_), channel_id=1, source_target_pairs={{0,4},{1,3},{2,6},{3,1},{4,0},{5,7},{6,2},{7,5},{8,12},{9,11},{10,... | collective-permute-start | bytes 811016 | tf_op jit(solution)/shard_map/ppermute | solution.py:315
  71.1 7.5 %collective-permute-start.15 = (f32[264,256]{1,0:T(8,128)S(1)}, f32[264,256]{1,0:T(8,128)S(1)}, u32[]{:S(2)}, u32[]{:S(2)}) collective-permute-start(f32[264,256]{1,0:T(8,128)S(1)} %finish.1.refs_0_), channel_id=1, source_target_pairs={{0,8},{2,10},{4,12},{6,14},{16,0},{18,2},{20,4},{22,6},{24,16},{26... | collective-permute-start | bytes 811016 | tf_op jit(solution)/shard_map/ppermute | solution.py:322
  74.9 6.7 %collective-permute-start.23 = (f32[264,256]{1,0:T(8,128)S(1)}, f32[264,256]{1,0:T(8,128)S(1)}, u32[]{:S(2)}, u32[]{:S(2)}) collective-permute-start(f32[264,256]{1,0:T(8,128)S(1)} %collective-permute-done.14.refs_8_), channel_id=1, source_target_pairs={{0,2},{1,5},{2,0},{3,7},{4,6},{5,1},{6,4},{7,3},{8,10},{9,13},{10,... | collective-permute-start | bytes 811016 | tf_op jit(solution)/shard_map/ppermute | solution.py:315
  75.5 11.9 %collective-permute-start.27 = (f32[264,256]{1,0:T(8,128)S(1)}, f32[264,256]{1,0:T(8,128)S(1)}, u32[]{:S(2)}, u32[]{:S(2)}) collective-permute-start(f32[264,256]{1,0:T(8,128)S(1)} %collective-permute-done.17.refs_6_), channel_id=1, source_target_pairs={{0,2},{1,5},{2,0},{3,7},{4,6},{5,1},{6,4},{7,3},{8,10},{9,13},{10,... | collective-permute-start | bytes 811016 | tf_op jit(solution)/shard_map/ppermute | solution.py:315
  76.9 13.0 %collective-permute-start.24 = (f32[264,256]{1,0:T(8,128)S(1)}, f32[264,256]{1,0:T(8,128)S(1)}, u32[]{:S(2)}, u32[]{:S(2)}) collective-permute-start(f32[264,256]{1,0:T(8,128)S(1)} %collective-permute-done.14.refs_8_), channel_id=1, source_target_pairs={{0,4},{1,3},{2,6},{3,1},{4,0},{5,7},{6,2},{7,5},{8,12},{9,11},{10,... | collective-permute-start | bytes 811016 | tf_op jit(solution)/shard_map/ppermute | solution.py:315
  78.6 11.3 %collective-permute-start.26 = (f32[264,256]{1,0:T(8,128)S(1)}, f32[264,256]{1,0:T(8,128)S(1)}, u32[]{:S(2)}, u32[]{:S(2)}) collective-permute-start(f32[264,256]{1,0:T(8,128)S(1)} %collective-permute-done.19.refs_3_), channel_id=1, source_target_pairs={{0,8},{2,10},{4,12},{6,14},{16,0},{18,2},{20,4},{22,6},{24,16},{26... | collective-permute-start | bytes 811016 | tf_op jit(solution)/shard_map/ppermute | solution.py:322
  81.6 8.8 %collective-permute-start.25 = (f32[264,256]{1,0:T(8,128)S(1)}, f32[264,256]{1,0:T(8,128)S(1)}, u32[]{:S(2)}, u32[]{:S(2)}) collective-permute-start(f32[264,256]{1,0:T(8,128)S(1)} %collective-permute-done.23.refs_0_), channel_id=1, source_target_pairs={{0,4},{1,3},{2,6},{3,1},{4,0},{5,7},{6,2},{7,5},{8,12},{9,11},{10,... | collective-permute-start | bytes 811016 | tf_op jit(solution)/shard_map/ppermute | solution.py:315
  82.4 10.9 %collective-permute-start.21 = (f32[264,256]{1,0:T(8,128)S(1)}, f32[264,256]{1,0:T(8,128)S(1)}, u32[]{:S(2)}, u32[]{:S(2)}) collective-permute-start(f32[264,256]{1,0:T(8,128)S(1)} %collective-permute-done.15.refs_9_), channel_id=1, source_target_pairs={{0,4},{1,3},{2,6},{3,1},{4,0},{5,7},{6,2},{7,5},{8,12},{9,11},{10,... | collective-permute-start | bytes 811016 | tf_op jit(solution)/shard_map/ppermute | solution.py:315
  87.4 6.5 %collective-permute-start.20 = (f32[264,256]{1,0:T(8,128)S(1)}, f32[264,256]{1,0:T(8,128)S(1)}, u32[]{:S(2)}, u32[]{:S(2)}) collective-permute-start(f32[264,256]{1,0:T(8,128)S(1)} %collective-permute-done.15.refs_9_), channel_id=1, source_target_pairs={{0,2},{1,5},{2,0},{3,7},{4,6},{5,1},{6,4},{7,3},{8,10},{9,13},{10,... | collective-permute-start | bytes 811016 | tf_op jit(solution)/shard_map/ppermute | solution.py:315

commit v18 on v14

--- a/solution.py
+++ b/solution.py
@@ -14,7 +14,7 @@
 NT = (((1,), (1,)), ((), ()))
 NN = (((1,), (0,)), ((), ()))
 VMEM = pl.BlockSpec(memory_space=pltpu.VMEM)
-SMEM = pl.BlockSpec(memory_space=pltpu.SMEM)
+HERE = "here"
 ANY = pl.BlockSpec(memory_space=pl.ANY)
 HBM = pl.BlockSpec(memory_space=pltpu.HBM)
 
@@ -24,6 +24,13 @@
 
 
 def call(kernel, out_shape, in_specs, args, name, out_specs=None, scratch=(), flops=0, aliases={}):
+    if in_specs[0] is HERE:
+        placed = kernel
+
+        def kernel(*refs):
+            placed((lax.axis_index("dp"), lax.axis_index("cent")), *refs)
+
+        in_specs = in_specs[1:]
     return pl.pallas_call(
         kernel,
         out_shape=out_shape,
@@ -41,9 +48,9 @@
     )(*args)
 
 
-def open_kernel(where_ref, points_ref, out_ref):
+def open_kernel(here, points_ref, out_ref):
     block = out_ref.shape[0]
-    start = pl.multiple_of(where_ref[1] * block, block)
+    start = pl.multiple_of(here[1] * block, block)
     out_ref[...] = points_ref[pl.ds(start, block), :].astype(jnp.float32)
 
 
@@ -58,11 +65,11 @@
     return jnp.broadcast_to(jnp.sum(c * c, axis=1, keepdims=True), (c.shape[0], LANES))
 
 
-def stats_kernel(lines, where_ref, points_ref, c_ref, out_ref, twice_ref, norm_ref, all_norm_ref):
+def stats_kernel(lines, here, points_ref, c_ref, out_ref, twice_ref, norm_ref, all_norm_ref):
     rows, local = points_ref.shape[0], c_ref.shape[0]
     chunk = local // lines
     tile, size = min(256, rows), chunk // 4
-    kept = pl.multiple_of(lax.rem(where_ref[0], 4) * size, size)
+    kept = pl.multiple_of(lax.rem(here[0], 4) * size, size)
     for l in range(lines):
         c = c_ref[l * chunk : (l + 1) * chunk, :]
         all_norm_ref[...] = norms(c)
@@ -85,7 +92,7 @@
         norm_ref[l * size : (l + 1) * size, :] = all_norm_ref[pl.ds(kept, size), :]
 
 
-def stats(where, points, centroids, lines):
+def stats(points, centroids, lines):
     rows, width = points.shape
     local = centroids.shape[0]
     return call(
@@ -95,8 +102,8 @@
             jax.ShapeDtypeStruct((local // 4, width), jnp.bfloat16),
             f32(local // 4, LANES),
         ),
-        [SMEM, VMEM, VMEM],
-        (where, points, centroids),
+        [HERE, VMEM, VMEM],
+        (points, centroids),
         "stats",
         scratch=[pltpu.VMEM((local // lines, LANES), jnp.float32)],
         flops=4 * rows * local * width,
@@ -184,14 +191,14 @@
     out_ref[size : size + 8, :] = jnp.broadcast_to(turned, (8, width))
 
 
-def lead_kernel(cores, order, half, where_ref, twice_ref, norm_ref, acc_ref, cnt_ref, *refs):
+def lead_kernel(cores, order, half, here, twice_ref, norm_ref, acc_ref, cnt_ref, *refs):
     out_acc_ref, out_cnt_ref = refs[-2:]
     near, (d0_ref, d1_ref) = refs[: 2 * cores], refs[2 * cores : 2 * cores + 2]
     size = out_acc_ref.shape[0]
-    place = ahead(order, lax.div(where_ref[0], 4), len(order) // 2)
+    place = ahead(order, lax.div(here[0], 4), len(order) // 2)
     at = pl.ds(pl.multiple_of(place * size, size), size)
     out_acc_ref[...], out_cnt_ref[...] = add_rows(
-        near_rows(cores, half, where_ref[1], near, d0_ref, d1_ref),
+        near_rows(cores, half, here[1], near, d0_ref, d1_ref),
         half,
         twice_ref[at, :],
         norm_ref[at, :],
@@ -200,30 +207,30 @@
     )
 
 
-def block_sums(cores, order, half, steps, where_ref, twice_ref, norm_ref, acc_ref, cnt_ref, lse_ref, near, far, out_ref):
+def block_sums(cores, order, half, steps, here, twice_ref, norm_ref, acc_ref, cnt_ref, lse_ref, near, far, out_ref):
     size = out_ref.shape[0] - 8
-    place = ahead(order, lax.div(where_ref[0], 4), steps)
+    place = ahead(order, lax.div(here[0], 4), steps)
     at = pl.ds(pl.multiple_of(place * size, size), size)
     twice, norm = twice_ref[at, :], norm_ref[at, :]
     acc, cnt = add_rows(
-        near_rows(cores, half, where_ref[1], near, far[0], far[cores]),
+        near_rows(cores, half, here[1], near, far[0], far[cores]),
         half,
         twice,
         norm,
         acc_ref[at, :],
         cnt_ref[at, :],
     )
-    acc, cnt = add_rows(far_rows(cores, half, where_ref[1], far, lse_ref), half, twice, norm, acc, cnt)
+    acc, cnt = add_rows(far_rows(cores, half, here[1], far, lse_ref), half, twice, norm, acc, cnt)
     store_sums(out_ref, acc, cnt)
 
 
-def first_kernel(cores, order, half, where_ref, twice_ref, norm_ref, lse_ref, lead_acc_ref, lead_cnt_ref, *refs):
+def first_kernel(cores, order, half, here, twice_ref, norm_ref, lse_ref, lead_acc_ref, lead_cnt_ref, *refs):
     far, out_ref = refs[: 2 * cores], refs[2 * cores]
     size = lead_acc_ref.shape[0]
-    place = ahead(order, lax.div(where_ref[0], 4), len(order) // 2)
+    place = ahead(order, lax.div(here[0], 4), len(order) // 2)
     at = pl.ds(pl.multiple_of(place * size, size), size)
     acc, cnt = add_rows(
-        far_rows(cores, half, where_ref[1], far, lse_ref),
+        far_rows(cores, half, here[1], far, lse_ref),
         half,
         twice_ref[at, :],
         norm_ref[at, :],
@@ -233,11 +240,11 @@
     store_sums(out_ref, acc, cnt)
 
 
-def rest_kernel(cores, order, half, steps, where_ref, twice_ref, norm_ref, acc_ref, cnt_ref, lse_ref, *refs):
+def rest_kernel(cores, order, half, steps, here, twice_ref, norm_ref, acc_ref, cnt_ref, lse_ref, *refs):
     near, far = refs[: 2 * cores], refs[2 * cores : 4 * cores]
     for s, out_ref in zip(steps, refs[4 * cores :]):
         block_sums(
-            cores, order, half, s, where_ref, twice_ref, norm_ref, acc_ref, cnt_ref, lse_ref, near, far, out_ref
+            cores, order, half, s, here, twice_ref, norm_ref, acc_ref, cnt_ref, lse_ref, near, far, out_ref
         )
 
 
@@ -253,9 +260,9 @@
     out_ref[...] = a_ref[...] + b_ref[...]
 
 
-def finish_kernel(where_ref, twice_ref, mine_ref, first_ref, second_ref, out_ref):
+def finish_kernel(here, twice_ref, mine_ref, first_ref, second_ref, out_ref):
     size, width = out_ref.shape[0] - 8, out_ref.shape[1]
-    start = pl.multiple_of(lax.div(where_ref[0], 4) * size, size)
+    start = pl.multiple_of(lax.div(here[0], 4) * size, size)
     c = 0.5 * twice_ref[pl.ds(start, size), :].astype(jnp.float32)
     total = mine_ref[...] + first_ref[...] + second_ref[...]
     counts = total[size:, :]
@@ -268,14 +275,14 @@
     out_ref[size:, :] = jnp.concatenate([spread] * (width // LANES), axis=1)
 
 
-def place_kernel(names, order, later, where_ref, *refs):
+def place_kernel(names, order, later, here, *refs):
     count, lines = len(names), len(order)
     block_refs = refs[:count]
     new_ref, counts_out_ref, counts_ref, sems = refs[-4:]
     size = block_refs[0].shape[0] - 8
-    plane, line = lax.rem(where_ref[0], 4), lax.div(where_ref[0], 4)
+    plane, line = lax.rem(here[0], 4), lax.div(here[0], 4)
     each = size // LANES
-    odd = lax.rem(where_ref[1], 2)
+    odd = lax.rem(here[1], 2)
     bits = (0, 1 + odd, 2 - odd, 3)
     places = [ahead(order, line, steps) * 4 + (plane ^ bits[way]) for way, steps in names]
     copies = []
@@ -304,7 +311,6 @@
     share = local_cent // 4
     size = share // lines
     order = tuple(range(0, lines, 2)) + tuple(range(1, lines, 2))[::-1]
-    where = jnp.stack([lax.axis_index("dp"), lax.axis_index("cent")]).astype(jnp.int32)
 
     def exchange(x, kind):
         pairs = [
@@ -324,10 +330,10 @@
     def with_siblings(pieces):
         return [a if rc == 0 else flip_core(a, rc) for a in pieces for rc in range(cores)]
 
-    mine = call(open_kernel, f32(2 * half, width), [SMEM, VMEM], (where, points), "open")
+    mine = call(open_kernel, f32(2 * half, width), [HERE, VMEM], (points,), "open")
     by_a, by_b = exchange(mine, 0), exchange(mine, 1)
 
-    pair, twice, norm = stats(where, points, centroids, lines)
+    pair, twice, norm = stats(points, centroids, lines)
     pairs = [pair] + [flip_core(pair, rc) for rc in range(1, cores)]
     tail = max(8, 2 * cores)
     lse, log_evidence, pack_a, pack_b = call(
@@ -356,12 +362,12 @@
     lead = call(
         functools.partial(lead_kernel, cores, order, half),
         (f32(size, width), f32(size, lanes)),
-        [SMEM] + [VMEM] * (6 + 2 * cores),
-        (where, twice, norm, acc, cnt, *near, d0, d1),
+        [HERE] + [VMEM] * (6 + 2 * cores),
+        (twice, norm, acc, cnt, *near, d0, d1),
         "lead",
         flops=4 * size * width * 2 * rows,
     )
-    given = (where, twice, norm, acc, cnt, lse_d)
+    given = (twice, norm, acc, cnt, lse_d)
     far = with_siblings((d0, d1))
     rows_given = (*near, *far)
     block_sum = f32(size + 8, width)
@@ -371,8 +377,8 @@
     first = call(
         functools.partial(first_kernel, cores, order, half),
         block_sum,
-        [SMEM] + [VMEM] * (5 + 2 * cores),
-        (where, twice, norm, lse_d, *lead, *far),
+        [HERE] + [VMEM] * (5 + 2 * cores),
+        (twice, norm, lse_d, *lead, *far),
         "first",
         flops=4 * size * width * 2 * rows,
     )
@@ -381,7 +387,7 @@
         made = call(
             functools.partial(rest_kernel, cores, order, half, steps),
             [block_sum] * len(steps),
-            [SMEM] + [VMEM] * (5 + 4 * cores),
+            [HERE] + [VMEM] * (5 + 4 * cores),
             (*given, *rows_given),
             "rest",
             flops=4 * size * width * 3 * rows * len(steps),
@@ -401,8 +407,8 @@
     done = call(
         finish_kernel,
         block_sum,
-        [SMEM] + [VMEM] * 4,
-        (where, twice, sums[0], from_behind, from_ahead),
+        [HERE] + [VMEM] * 4,
+        (twice, sums[0], from_behind, from_ahead),
         "finish",
     )
 
@@ -432,13 +438,13 @@
     groups = ([k for k in got if k not in middle + late], middle, late)
     new = counts = None
     for later, names in enumerate(groups):
-        args = [where] + [got[k] for k in names]
+        args = [got[k] for k in names]
         if later:
             args += [counts, new]
         new, counts = call(
             functools.partial(place_kernel, names, order, later),
             (f32(local_cent, width), f32(local_cent // LANES, LANES)),
-            [SMEM] + [VMEM] * len(names) + ([VMEM, ANY] if later else []),
+            [HERE] + [VMEM] * len(names) + ([VMEM, ANY] if later else []),
             args,
             ("place_early", "place_middle", "place_late")[later],
             out_specs=(ANY, ANY),

time: 95.2 us -> 93.1 us (0.978)
  Pallas kernels: 21.3 us -> 15.8 us
  waiting for transfers between devices: 37.5 us -> 41.4 us
    pallas_call x13, Pallas kernels: 21.3 us -> 15.8 us  [call(): pl.pallas_call(kernel, out_shape=out_shape, in_specs=in_specs, out_specs=...]
    ppermute x15, waiting for transfers between devices: 15.1 us -> 17.1 us  [exchange(): return lax.ppermute(x, ('dp', 'cent'), pairs)]
    ppermute x7, waiting for transfers between devices: 20.3 us -> 21.6 us  [ring(): lax.ppermute(x, 'dp', [(4 * a + i, 4 * b + i) for a, b in pairs for i in...]
  transfers between devices with their start and end apart: 28 -> 28, of which waited for: 14 -> 17; matrix products, arithmetic and copies ran while one was open for 0% -> 0% of each run, Pallas kernels for 18% -> 14%
where the time goes in v18:
time: 93.1 us; the launch traced here: 92.9 us
  waiting for transfers between devices  41.4 us (44%)
  starting transfers between devices  32.2 us (35%)
  Pallas kernels  15.8 us (17%)
  local copies, waits for them, and re-layouts  2.63 us (3%)
    ppermute x7, waiting for transfers between devices, ring(): lax.ppermute(x, 'dp', [(4 * a + i, 4 * b + i) for a, b in pairs for i in...  21.6 us
    ppermute x15, starting transfers between devices, exchange(): return lax.ppermute(x, ('dp', 'cent'), pairs)  17.4 us
    ppermute x15, waiting for transfers between devices, exchange(): return lax.ppermute(x, ('dp', 'cent'), pairs)  17.1 us
    pallas_call x13, Pallas kernels, call(): pl.pallas_call(kernel, out_shape=out_shape, in_specs=in_specs, out_specs=...  15.8 us
    ppermute x7, starting transfers between devices, ring(): lax.ppermute(x, 'dp', [(4 * a + i, 4 * b + i) for a, b in pairs for i in...  12.8 us
    unnamed x6, local copies, waits for them, and re-layouts  2.63 us
  transfers between devices with their start and end apart: 28, of which 17 were waited for; matrix products, arithmetic and copies ran while one was open for 0% of the time, Pallas kernels for 14%

profile of v18, /device:TPU:0, one launch (start us, length us, event | category | flops | bytes accessed | tf_op | source)
XLA Modules:
  0.0 92.9 jit_solution(17062056150955512485)
XLA Ops:
  0.6 1.0 %copy-done = bf16[1024,256]{1,0:T(8,128)(2,1)S(1)} copy-done((bf16[1024,256]{1,0:T(8,128)(2,1)S(1)}, bf16[1024,256]{1,0:T(8,128)(2,1)}, u32[]{:S(2)}) %copy-start) | copy-done | bytes 524312
  1.7 3.0 %collective-permute-start.1 = (f32[512,256]{1,0:T(8,128)S(1)}, f32[512,256]{1,0:T(8,128)S(1)}, u32[]{:S(2)}, u32[]{:S(2)}) collective-permute-start(f32[512,256]{1,0:T(8,128)S(1)} %open.1), channel_id=1, source_target_pairs={{0,4},{1,3},{2,6},{3,1},{4,0},{5,7},{6,2},{7,5},{8,12},{9,11},{10,... | collective-permute-start | bytes 1572872 | tf_op jit(solution)/shard_map/ppermute | solution.py:321
  4.8 1.5 %collective-permute-start = (f32[512,256]{1,0:T(8,128)S(1)}, f32[512,256]{1,0:T(8,128)S(1)}, u32[]{:S(2)}, u32[]{:S(2)}) collective-permute-start(f32[512,256]{1,0:T(8,128)S(1)} %open.1), channel_id=1, source_target_pairs={{0,2},{1,5},{2,0},{3,7},{4,6},{5,1},{6,4},{7,3},{8,10},{9,13},{10,... | collective-permute-start | bytes 1572872 | tf_op jit(solution)/shard_map/ppermute | solution.py:321
  6.3 1.6 %copy-done.2 = bf16[4096,256]{1,0:T(8,128)(2,1)S(1)} copy-done((bf16[4096,256]{1,0:T(8,128)(2,1)S(1)}, bf16[4096,256]{1,0:T(8,128)(2,1)}, u32[]{:S(2)}) %copy-start.2) | copy-done | bytes 2097176
  7.8 5.3 %stats.1 = (f32[2,1024]{1,0:T(2,128)S(1)}, bf16[1024,256]{1,0:T(8,128)(2,1)S(1)}, f32[1024,128]{1,0:T(8,128)S(1)}) custom-call(bf16[1024,256]{1,0:T(8,128)(2,1)S(1)} %copy-done, bf16[4096,256]{1,0:T(8,128)(2,1)S(1)} %copy-done.2), custom_call_target="tpu_custom_call" | custom-call | flops 4294967296 | bytes 2621440 | tf_op jit(solution)/shard_map/stats/pallas_call | solution.py:34
  13.2 1.2 %collective-permute-done.2.refs_1_ = f32[2,1024]{1,0:T(2,128)S(1)} collective-permute-done((f32[2,1024]{1,0:T(2,128)S(1)}, f32[2,1024]{1,0:T(2,128)S(1)}, u32[]{:S(2)}, u32[]{:S(2)}) %collective-permute-start.2) | collective-permute-done | bytes 8224 | tf_op jit(solution)/shard_map/ppermute | solution.py:324
  14.4 2.6 %collective-permute-done.1.b_ref.refs_7_.refs_6_ = f32[512,256]{1,0:T(8,128)S(1)} collective-permute-done((f32[512,256]{1,0:T(8,128)S(1)}, f32[512,256]{1,0:T(8,128)S(1)}, u32[]{:S(2)}, u32[]{:S(2)}) %collective-permute-start.1) | collective-permute-done | bytes 524320 | tf_op jit(solution)/shard_map/ppermute | solution.py:321
  17.0 0.6 lse.1
  18.2 2.5 %collective-permute-start.5 = (f32[264,256]{1,0:T(8,128)S(1)}, f32[264,256]{1,0:T(8,128)S(1)}, u32[]{:S(2)}, u32[]{:S(2)}) collective-permute-start(f32[264,256]{1,0:T(8,128)S(1)} %get-tuple-element.59), channel_id=1, source_target_pairs={{0,4},{1,3},{2,6},{3,1},{4,0},{5,7},{6,2},{7,5},{8,12},{9,11},{10,... | collective-permute-start | bytes 811016 | tf_op jit(solution)/shard_map/ppermute | solution.py:321
  20.6 0.7 collective-permute-start.6
  21.3 1.4 %own.1 = (f32[1024,256]{1,0:T(8,128)S(1)}, f32[1024,128]{1,0:T(8,128)S(1)}) custom-call(bf16[1024,256]{1,0:T(8,128)(2,1)S(1)} %copy-done.1, bf16[1024,256]{1,0:T(8,128)(2,1)S(1)} %get-tuple-element.46.twice_ref.refs_0_, f32[1024,128]{1,0:T(8,128)S(1)} %get-tuple-element.47.norm_ref.refs_1_, f32[4,256]{1,0:T(4,128)S(1)} %get-tuple-element.63.lse_ref), custom_call_target="tpu_custom_call" | custom-call | flops 1073741824 | bytes 1576960 | tf_op jit(solution)/shard_map/own/pallas_call | solution.py:34
  22.7 0.8 collective-permute-start.7
  23.6 4.1 %collective-permute-done.5.refs_9_.refs_8_.refs_5_ = f32[264,256]{1,0:T(8,128)S(1)} collective-permute-done((f32[264,256]{1,0:T(8,128)S(1)}, f32[264,256]{1,0:T(8,128)S(1)}, u32[]{:S(2)}, u32[]{:S(2)}) %collective-permute-start.5) | collective-permute-done | bytes 270368 | tf_op jit(solution)/shard_map/ppermute | solution.py:321
  27.7 0.9 collective-permute-done.7.refs_4_.refs_2_
  29.2 0.9 lead.1
  31.2 2.6 %collective-permute-start.10 = (f32[264,256]{1,0:T(8,128)S(1)}, f32[264,256]{1,0:T(8,128)S(1)}, u32[]{:S(2)}, u32[]{:S(2)}) collective-permute-start(f32[264,256]{1,0:T(8,128)S(1)} %first.1), channel_id=1, source_target_pairs={{0,16},{2,18},{4,20},{6,22},{16,24},{18,26},{20,28},{22,30},{24,8}... | collective-permute-start | bytes 811016 | tf_op jit(solution)/shard_map/ppermute | solution.py:328
  33.8 1.2 %rest.3 = f32[264,256]{1,0:T(8,128)S(1)} custom-call(bf16[1024,256]{1,0:T(8,128)(2,1)S(1)} %get-tuple-element.46.twice_ref.refs_0_, f32[1024,128]{1,0:T(8,128)S(1)} %get-tuple-element.47.norm_ref.refs_1_, f32[1024,256]{1,0:T(8,128)S(1)} %get-tuple-element.64.refs_2_, f32[1024,128]{1,0:T(8,128)S(1)} %get-tuple-element.65.refs_3_, ...), custom_call_target="tpu_custom_call" | custom-call | flops 805306368 | bytes 5804032 | tf_op jit(solution)/shard_map/rest/pallas_call | solution.py:34
  35.2 2.1 %rest.2 = (f32[264,256]{1,0:T(8,128)S(1)}, f32[264,256]{1,0:T(8,128)S(1)}) custom-call(bf16[1024,256]{1,0:T(8,128)(2,1)S(1)} %get-tuple-element.46.twice_ref.refs_0_, f32[1024,128]{1,0:T(8,128)S(1)} %get-tuple-element.47.norm_ref.refs_1_, f32[1024,256]{1,0:T(8,128)S(1)} %get-tuple-element.64.refs_2_, f32[1024,128]{1,0:T(8,128)S(1)} %get-tuple-element.65.refs_3_, ...), custom_call_target="tpu_custom_call" | custom-call | flops 1610612736 | bytes 5804032 | tf_op jit(solution)/shard_map/rest/pallas_call | solution.py:34
  37.3 3.4 %collective-permute-done.10.b_ref = f32[264,256]{1,0:T(8,128)S(1)} collective-permute-done((f32[264,256]{1,0:T(8,128)S(1)}, f32[264,256]{1,0:T(8,128)S(1)}, u32[]{:S(2)}, u32[]{:S(2)}) %collective-permute-start.10) | collective-permute-done | bytes 270368 | tf_op jit(solution)/shard_map/ppermute | solution.py:328
  40.7 3.4 %collective-permute-start.11 = (f32[264,256]{1,0:T(8,128)S(1)}, f32[264,256]{1,0:T(8,128)S(1)}, u32[]{:S(2)}, u32[]{:S(2)}) collective-permute-start(f32[264,256]{1,0:T(8,128)S(1)} %add.1), channel_id=1, source_target_pairs={{0,16},{2,18},{4,20},{6,22},{16,24},{18,26},{20,28},{22,30},{24,8}... | collective-permute-start | bytes 811016 | tf_op jit(solution)/shard_map/ppermute | solution.py:328
  44.2 4.1 %collective-permute-done.12.refs_3_ = f32[264,256]{1,0:T(8,128)S(1)} collective-permute-done((f32[264,256]{1,0:T(8,128)S(1)}, f32[264,256]{1,0:T(8,128)S(1)}, u32[]{:S(2)}, u32[]{:S(2)}) %collective-permute-start.12) | collective-permute-done | bytes 270368 | tf_op jit(solution)/shard_map/ppermute | solution.py:328
  48.3 4.9 %collective-permute-done.11.refs_2_ = f32[264,256]{1,0:T(8,128)S(1)} collective-permute-done((f32[264,256]{1,0:T(8,128)S(1)}, f32[264,256]{1,0:T(8,128)S(1)}, u32[]{:S(2)}, u32[]{:S(2)}) %collective-permute-start.11) | collective-permute-done | bytes 270368 | tf_op jit(solution)/shard_map/ppermute | solution.py:328
  53.5 1.7 %collective-permute-start.13 = (f32[264,256]{1,0:T(8,128)S(1)}, f32[264,256]{1,0:T(8,128)S(1)}, u32[]{:S(2)}, u32[]{:S(2)}) collective-permute-start(f32[264,256]{1,0:T(8,128)S(1)} %finish.1.refs_0_), channel_id=1, source_target_pairs={{0,16},{2,18},{4,20},{6,22},{16,24},{18,26},{20,28},{22,30},{24,8}... | collective-permute-start | bytes 811016 | tf_op jit(solution)/shard_map/ppermute | solution.py:328
  55.2 0.9 collective-permute-start.16
  56.1 1.0 %collective-permute-start.18 = (f32[264,256]{1,0:T(8,128)S(1)}, f32[264,256]{1,0:T(8,128)S(1)}, u32[]{:S(2)}, u32[]{:S(2)}) collective-permute-start(f32[264,256]{1,0:T(8,128)S(1)} %finish.1.refs_0_), channel_id=1, source_target_pairs={{0,2},{1,5},{2,0},{3,7},{4,6},{5,1},{6,4},{7,3},{8,10},{9,13},{10,... | collective-permute-start | bytes 811016 | tf_op jit(solution)/shard_map/ppermute | solution.py:321
  57.1 4.9 %collective-permute-done.13.refs_4_ = f32[264,256]{1,0:T(8,128)S(1)} collective-permute-done((f32[264,256]{1,0:T(8,128)S(1)}, f32[264,256]{1,0:T(8,128)S(1)}, u32[]{:S(2)}, u32[]{:S(2)}) %collective-permute-start.13) | collective-permute-done | bytes 270368 | tf_op jit(solution)/shard_map/ppermute | solution.py:328
  62.0 1.8 %collective-permute-start.14 = (f32[264,256]{1,0:T(8,128)S(1)}, f32[264,256]{1,0:T(8,128)S(1)}, u32[]{:S(2)}, u32[]{:S(2)}) collective-permute-start(f32[264,256]{1,0:T(8,128)S(1)} %collective-permute-done.13.refs_4_), channel_id=1, source_target_pairs={{0,16},{2,18},{4,20},{6,22},{16,24},{18,26},{20,28},{22,30},{24,8}... | collective-permute-start | bytes 811016 | tf_op jit(solution)/shard_map/ppermute | solution.py:328
  63.8 0.9 collective-permute-start.17
  64.7 1.0 %collective-permute-start.26 = (f32[264,256]{1,0:T(8,128)S(1)}, f32[264,256]{1,0:T(8,128)S(1)}, u32[]{:S(2)}, u32[]{:S(2)}) collective-permute-start(f32[264,256]{1,0:T(8,128)S(1)} %collective-permute-done.13.refs_4_), channel_id=1, source_target_pairs={{0,2},{1,5},{2,0},{3,7},{4,6},{5,1},{6,4},{7,3},{8,10},{9,13},{10,... | collective-permute-start | bytes 811016 | tf_op jit(solution)/shard_map/ppermute | solution.py:321
  65.7 0.7 collective-permute-start.19
  66.4 3.1 %collective-permute-done.14.refs_8_ = f32[264,256]{1,0:T(8,128)S(1)} collective-permute-done((f32[264,256]{1,0:T(8,128)S(1)}, f32[264,256]{1,0:T(8,128)S(1)}, u32[]{:S(2)}, u32[]{:S(2)}) %collective-permute-start.14) | collective-permute-done | bytes 270368 | tf_op jit(solution)/shard_map/ppermute | solution.py:328
  69.5 2.0 %collective-permute-start.15 = (f32[264,256]{1,0:T(8,128)S(1)}, f32[264,256]{1,0:T(8,128)S(1)}, u32[]{:S(2)}, u32[]{:S(2)}) collective-permute-start(f32[264,256]{1,0:T(8,128)S(1)} %finish.1.refs_0_), channel_id=1, source_target_pairs={{0,8},{2,10},{4,12},{6,14},{16,0},{18,2},{20,4},{22,6},{24,16},{26... | collective-permute-start | bytes 811016 | tf_op jit(solution)/shard_map/ppermute | solution.py:328
  71.5 0.6 collective-permute-start.22
  72.1 1.8 %collective-permute-done.26.refs_5_ = f32[264,256]{1,0:T(8,128)S(1)} collective-permute-done((f32[264,256]{1,0:T(8,128)S(1)}, f32[264,256]{1,0:T(8,128)S(1)}, u32[]{:S(2)}, u32[]{:S(2)}) %collective-permute-start.26) | collective-permute-done | bytes 270368 | tf_op jit(solution)/shard_map/ppermute | solution.py:321
  73.9 0.6 collective-permute-start.27
  74.5 1.4 %collective-permute-start.23 = (f32[264,256]{1,0:T(8,128)S(1)}, f32[264,256]{1,0:T(8,128)S(1)}, u32[]{:S(2)}, u32[]{:S(2)}) collective-permute-start(f32[264,256]{1,0:T(8,128)S(1)} %collective-permute-done.14.refs_8_), channel_id=1, source_target_pairs={{0,4},{1,3},{2,6},{3,1},{4,0},{5,7},{6,2},{7,5},{8,12},{9,11},{10,... | collective-permute-start | bytes 811016 | tf_op jit(solution)/shard_map/ppermute | solution.py:321
  75.9 1.2 %collective-permute-done.15.refs_9_ = f32[264,256]{1,0:T(8,128)S(1)} collective-permute-done((f32[264,256]{1,0:T(8,128)S(1)}, f32[264,256]{1,0:T(8,128)S(1)}, u32[]{:S(2)}, u32[]{:S(2)}) %collective-permute-start.15) | collective-permute-done | bytes 270368 | tf_op jit(solution)/shard_map/ppermute | solution.py:328
  77.1 1.1 %collective-permute-start.25 = (f32[264,256]{1,0:T(8,128)S(1)}, f32[264,256]{1,0:T(8,128)S(1)}, u32[]{:S(2)}, u32[]{:S(2)}) collective-permute-start(f32[264,256]{1,0:T(8,128)S(1)} %collective-permute-done.19.refs_3_), channel_id=1, source_target_pairs={{0,8},{2,10},{4,12},{6,14},{16,0},{18,2},{20,4},{22,6},{24,16},{26... | collective-permute-start | bytes 811016 | tf_op jit(solution)/shard_map/ppermute | solution.py:328
  78.1 2.8 %collective-permute-done.22.refs_0_ = f32[264,256]{1,0:T(8,128)S(1)} collective-permute-done((f32[264,256]{1,0:T(8,128)S(1)}, f32[264,256]{1,0:T(8,128)S(1)}, u32[]{:S(2)}, u32[]{:S(2)}) %collective-permute-start.22) | collective-permute-done | bytes 270368 | tf_op jit(solution)/shard_map/ppermute | solution.py:321
  80.9 0.9 collective-permute-start.24
  81.8 1.1 %collective-permute-start.21 = (f32[264,256]{1,0:T(8,128)S(1)}, f32[264,256]{1,0:T(8,128)S(1)}, u32[]{:S(2)}, u32[]{:S(2)}) collective-permute-start(f32[264,256]{1,0:T(8,128)S(1)} %collective-permute-done.15.refs_9_), channel_id=1, source_target_pairs={{0,4},{1,3},{2,6},{3,1},{4,0},{5,7},{6,2},{7,5},{8,12},{9,11},{10,... | collective-permute-start | bytes 811016 | tf_op jit(solution)/shard_map/ppermute | solution.py:321
  83.0 0.6 collective-permute-start.20
  83.5 1.6 %place_early.1 = (f32[4096,256]{1,0:T(8,128)}, f32[32,128]{1,0:T(8,128)S(1)}) custom-call(f32[264,256]{1,0:T(8,128)S(1)} %finish.1.refs_0_, f32[264,256]{1,0:T(8,128)S(1)} %collective-permute-done.18.refs_1_, f32[264,256]{1,0:T(8,128)S(1)} %collective-permute-done.16.refs_2_, f32[264,256]{1,0:T(8,128)S(1)} %collective-permute-done.19.refs_3_, ...), custom_call_target="tpu_custom_call" | custom-call | bytes 2703360 | tf_op jit(solution)/shard_map/place_early/pallas_call | solution.py:34
  85.1 0.7 collective-permute-done.23.refs_1_
  85.8 3.2 %collective-permute-done.24.refs_2_ = f32[264,256]{1,0:T(8,128)S(1)} collective-permute-done((f32[264,256]{1,0:T(8,128)S(1)}, f32[264,256]{1,0:T(8,128)S(1)}, u32[]{:S(2)}, u32[]{:S(2)}) %collective-permute-start.24) | collective-permute-done | bytes 270368 | tf_op jit(solution)/shard_map/ppermute | solution.py:321
  89.0 1.0 %place_middle.1 = (f32[4096,256]{1,0:T(8,128)}, f32[32,128]{1,0:T(8,128)S(1)}) custom-call(f32[264,256]{1,0:T(8,128)S(1)} %collective-permute-done.22.refs_0_, f32[264,256]{1,0:T(8,128)S(1)} %collective-permute-done.23.refs_1_, f32[264,256]{1,0:T(8,128)S(1)} %collective-permute-done.24.refs_2_, ...), custom_call_target="tpu_custom_call", output_to_operand_aliasing={{0}: (5, {})} | custom-call | bytes 5292032 | tf_op jit(solution)/shard_map/place_middle/pallas_call | solution.py:34
  90.0 1.9 %collective-permute-done.21.refs_1_ = f32[264,256]{1,0:T(8,128)S(1)} collective-permute-done((f32[264,256]{1,0:T(8,128)S(1)}, f32[264,256]{1,0:T(8,128)S(1)}, u32[]{:S(2)}, u32[]{:S(2)}) %collective-permute-start.21) | collective-permute-done | bytes 270368 | tf_op jit(solution)/shard_map/ppermute | solution.py:321
  91.9 0.8 place_late.1
  (27 shorter events, 2.8 us)
Async XLA Ops:
  0.6 1.0 %copy-start = (bf16[1024,256]{1,0:T(8,128)(2,1)S(1)}, bf16[1024,256]{1,0:T(8,128)(2,1)}, u32[]{:S(2)}) copy-start(bf16[1024,256]{1,0:T(8,128)(2,1)} %points_ref.1) | copy-start | bytes 1572868
  1.7 19.6 %copy-start.1 = (bf16[1024,256]{1,0:T(8,128)(2,1)S(1)}, bf16[1024,256]{1,0:T(8,128)(2,1)}, u32[]{:S(2)}) copy-start(bf16[1024,256]{1,0:T(8,128)(2,1)} %points_ref.1) | copy-start | bytes 1572868
  1.7 15.3 %collective-permute-start.1 = (f32[512,256]{1,0:T(8,128)S(1)}, f32[512,256]{1,0:T(8,128)S(1)}, u32[]{:S(2)}, u32[]{:S(2)}) collective-permute-start(f32[512,256]{1,0:T(8,128)S(1)} %open.1), channel_id=1, source_target_pairs={{0,4},{1,3},{2,6},{3,1},{4,0},{5,7},{6,2},{7,5},{8,12},{9,11},{10,... | collective-permute-start | bytes 1572872 | tf_op jit(solution)/shard_map/ppermute | solution.py:321
  4.8 12.3 %collective-permute-start = (f32[512,256]{1,0:T(8,128)S(1)}, f32[512,256]{1,0:T(8,128)S(1)}, u32[]{:S(2)}, u32[]{:S(2)}) collective-permute-start(f32[512,256]{1,0:T(8,128)S(1)} %open.1), channel_id=1, source_target_pairs={{0,2},{1,5},{2,0},{3,7},{4,6},{5,1},{6,4},{7,3},{8,10},{9,13},{10,... | collective-permute-start | bytes 1572872 | tf_op jit(solution)/shard_map/ppermute | solution.py:321
  6.2 1.6 %copy-start.2 = (bf16[4096,256]{1,0:T(8,128)(2,1)S(1)}, bf16[4096,256]{1,0:T(8,128)(2,1)}, u32[]{:S(2)}) copy-start(bf16[4096,256]{1,0:T(8,128)(2,1)} %refs_1_.1) | copy-start | bytes 6291460
  13.2 1.2 %collective-permute-start.2 = (f32[2,1024]{1,0:T(2,128)S(1)}, f32[2,1024]{1,0:T(2,128)S(1)}, u32[]{:S(2)}, u32[]{:S(2)}) collective-permute-start(f32[2,1024]{1,0:T(2,128)S(1)} %get-tuple-element.48.refs_0_), channel_id=1, source_target_pairs={{0,1},{1,0},{2,3},{3,2},{4,5},{5,4},{6,7},{7,6},{8,9},{9,8},{10,11... | collective-permute-start | bytes 24584 | tf_op jit(solution)/shard_map/ppermute | solution.py:324
  17.7 5.1 %collective-permute-start.3 = (f32[512,256]{1,0:T(8,128)S(1)}, f32[512,256]{1,0:T(8,128)S(1)}, u32[]{:S(2)}, u32[]{:S(2)}) collective-permute-start(f32[512,256]{1,0:T(8,128)S(1)} %collective-permute-done.a_ref.refs_5_.refs_4_), channel_id=1, source_target_pairs={{0,1},{1,0},{2,3},{3,2},{4,5},{5,4},{6,7},{7,6},{8,9},{9,8},{10,11... | collective-permute-start | bytes 1572872 | tf_op jit(solution)/shard_map/ppermute | solution.py:324
  18.0 4.7 %collective-permute-start.4 = (f32[512,256]{1,0:T(8,128)S(1)}, f32[512,256]{1,0:T(8,128)S(1)}, u32[]{:S(2)}, u32[]{:S(2)}) collective-permute-start(f32[512,256]{1,0:T(8,128)S(1)} %collective-permute-done.1.b_ref.refs_7_.refs_6_), channel_id=1, source_target_pairs={{0,1},{1,0},{2,3},{3,2},{4,5},{5,4},{6,7},{7,6},{8,9},{9,8},{10,11... | collective-permute-start | bytes 1572872 | tf_op jit(solution)/shard_map/ppermute | solution.py:324
  18.2 9.6 %collective-permute-start.5 = (f32[264,256]{1,0:T(8,128)S(1)}, f32[264,256]{1,0:T(8,128)S(1)}, u32[]{:S(2)}, u32[]{:S(2)}) collective-permute-start(f32[264,256]{1,0:T(8,128)S(1)} %get-tuple-element.59), channel_id=1, source_target_pairs={{0,4},{1,3},{2,6},{3,1},{4,0},{5,7},{6,2},{7,5},{8,12},{9,11},{10,... | collective-permute-start | bytes 811016 | tf_op jit(solution)/shard_map/ppermute | solution.py:321
  20.6 7.1 %collective-permute-start.6 = (f32[264,256]{1,0:T(8,128)S(1)}, f32[264,256]{1,0:T(8,128)S(1)}, u32[]{:S(2)}, u32[]{:S(2)}) collective-permute-start(f32[264,256]{1,0:T(8,128)S(1)} %get-tuple-element.60), channel_id=1, source_target_pairs={{0,2},{1,5},{2,0},{3,7},{4,6},{5,1},{6,4},{7,3},{8,10},{9,13},{10,... | collective-permute-start | bytes 811016 | tf_op jit(solution)/shard_map/ppermute | solution.py:321
  22.7 5.9 %collective-permute-start.7 = (f32[4,256]{1,0:T(4,128)S(1)}, f32[4,256]{1,0:T(4,128)S(1)}, u32[]{:S(2)}, u32[]{:S(2)}) collective-permute-start(f32[4,256]{1,0:T(4,128)S(1)} %get-tuple-element.63.lse_ref), channel_id=1, source_target_pairs={{0,6},{2,4},{4,2},{6,0},{8,14},{10,12},{12,10},{14,8},{16,22},{18,... | collective-permute-start | bytes 12296 | tf_op jit(solution)/shard_map/ppermute | solution.py:360
  28.6 1.5 %collective-permute-start.8 = (f32[264,256]{1,0:T(8,128)S(1)}, f32[264,256]{1,0:T(8,128)S(1)}, u32[]{:S(2)}, u32[]{:S(2)}) collective-permute-start(f32[264,256]{1,0:T(8,128)S(1)} %collective-permute-done.5.refs_9_.refs_8_.refs_5_), channel_id=1, source_target_pairs={{0,1},{1,0},{2,3},{3,2},{4,5},{5,4},{6,7},{7,6},{8,9},{9,8},{10,11... | collective-permute-start | bytes 811016 | tf_op jit(solution)/shard_map/ppermute | solution.py:324
  28.7 1.9 %collective-permute-start.9 = (f32[264,256]{1,0:T(8,128)S(1)}, f32[264,256]{1,0:T(8,128)S(1)}, u32[]{:S(2)}, u32[]{:S(2)}) collective-permute-start(f32[264,256]{1,0:T(8,128)S(1)} %collective-permute-done.6.refs_11_.refs_9_.refs_7_), channel_id=1, source_target_pairs={{0,1},{1,0},{2,3},{3,2},{4,5},{5,4},{6,7},{7,6},{8,9},{9,8},{10,11... | collective-permute-start | bytes 811016 | tf_op jit(solution)/shard_map/ppermute | solution.py:324
  31.2 9.5 %collective-permute-start.10 = (f32[264,256]{1,0:T(8,128)S(1)}, f32[264,256]{1,0:T(8,128)S(1)}, u32[]{:S(2)}, u32[]{:S(2)}) collective-permute-start(f32[264,256]{1,0:T(8,128)S(1)} %first.1), channel_id=1, source_target_pairs={{0,16},{2,18},{4,20},{6,22},{16,24},{18,26},{20,28},{22,30},{24,8}... | collective-permute-start | bytes 811016 | tf_op jit(solution)/shard_map/ppermute | solution.py:328
  35.0 13.3 %collective-permute-start.12 = (f32[264,256]{1,0:T(8,128)S(1)}, f32[264,256]{1,0:T(8,128)S(1)}, u32[]{:S(2)}, u32[]{:S(2)}) collective-permute-start(f32[264,256]{1,0:T(8,128)S(1)} %rest.3), channel_id=1, source_target_pairs={{0,8},{2,10},{4,12},{6,14},{16,0},{18,2},{20,4},{22,6},{24,16},{26... | collective-permute-start | bytes 811016 | tf_op jit(solution)/shard_map/ppermute | solution.py:328
  40.7 12.5 %collective-permute-start.11 = (f32[264,256]{1,0:T(8,128)S(1)}, f32[264,256]{1,0:T(8,128)S(1)}, u32[]{:S(2)}, u32[]{:S(2)}) collective-permute-start(f32[264,256]{1,0:T(8,128)S(1)} %add.1), channel_id=1, source_target_pairs={{0,16},{2,18},{4,20},{6,22},{16,24},{18,26},{20,28},{22,30},{24,8}... | collective-permute-start | bytes 811016 | tf_op jit(solution)/shard_map/ppermute | solution.py:328
  53.5 8.5 %collective-permute-start.13 = (f32[264,256]{1,0:T(8,128)S(1)}, f32[264,256]{1,0:T(8,128)S(1)}, u32[]{:S(2)}, u32[]{:S(2)}) collective-permute-start(f32[264,256]{1,0:T(8,128)S(1)} %finish.1.refs_0_), channel_id=1, source_target_pairs={{0,16},{2,18},{4,20},{6,22},{16,24},{18,26},{20,28},{22,30},{24,8}... | collective-permute-start | bytes 811016 | tf_op jit(solution)/shard_map/ppermute | solution.py:328
  55.2 8.6 %collective-permute-start.16 = (f32[264,256]{1,0:T(8,128)S(1)}, f32[264,256]{1,0:T(8,128)S(1)}, u32[]{:S(2)}, u32[]{:S(2)}) collective-permute-start(f32[264,256]{1,0:T(8,128)S(1)} %finish.1.refs_0_), channel_id=1, source_target_pairs={{0,4},{1,3},{2,6},{3,1},{4,0},{5,7},{6,2},{7,5},{8,12},{9,11},{10,... | collective-permute-start | bytes 811016 | tf_op jit(solution)/shard_map/ppermute | solution.py:321
  56.1 9.6 %collective-permute-start.18 = (f32[264,256]{1,0:T(8,128)S(1)}, f32[264,256]{1,0:T(8,128)S(1)}, u32[]{:S(2)}, u32[]{:S(2)}) collective-permute-start(f32[264,256]{1,0:T(8,128)S(1)} %finish.1.refs_0_), channel_id=1, source_target_pairs={{0,2},{1,5},{2,0},{3,7},{4,6},{5,1},{6,4},{7,3},{8,10},{9,13},{10,... | collective-permute-start | bytes 811016 | tf_op jit(solution)/shard_map/ppermute | solution.py:321
  62.0 7.6 %collective-permute-start.14 = (f32[264,256]{1,0:T(8,128)S(1)}, f32[264,256]{1,0:T(8,128)S(1)}, u32[]{:S(2)}, u32[]{:S(2)}) collective-permute-start(f32[264,256]{1,0:T(8,128)S(1)} %collective-permute-done.13.refs_4_), channel_id=1, source_target_pairs={{0,16},{2,18},{4,20},{6,22},{16,24},{18,26},{20,28},{22,30},{24,8}... | collective-permute-start | bytes 811016 | tf_op jit(solution)/shard_map/ppermute | solution.py:328
  63.8 7.7 %collective-permute-start.17 = (f32[264,256]{1,0:T(8,128)S(1)}, f32[264,256]{1,0:T(8,128)S(1)}, u32[]{:S(2)}, u32[]{:S(2)}) collective-permute-start(f32[264,256]{1,0:T(8,128)S(1)} %collective-permute-done.13.refs_4_), channel_id=1, source_target_pairs={{0,4},{1,3},{2,6},{3,1},{4,0},{5,7},{6,2},{7,5},{8,12},{9,11},{10,... | collective-permute-start | bytes 811016 | tf_op jit(solution)/shard_map/ppermute | solution.py:321
  64.7 9.2 %collective-permute-start.26 = (f32[264,256]{1,0:T(8,128)S(1)}, f32[264,256]{1,0:T(8,128)S(1)}, u32[]{:S(2)}, u32[]{:S(2)}) collective-permute-start(f32[264,256]{1,0:T(8,128)S(1)} %collective-permute-done.13.refs_4_), channel_id=1, source_target_pairs={{0,2},{1,5},{2,0},{3,7},{4,6},{5,1},{6,4},{7,3},{8,10},{9,13},{10,... | collective-permute-start | bytes 811016 | tf_op jit(solution)/shard_map/ppermute | solution.py:321
  65.7 10.2 %collective-permute-start.19 = (f32[264,256]{1,0:T(8,128)S(1)}, f32[264,256]{1,0:T(8,128)S(1)}, u32[]{:S(2)}, u32[]{:S(2)}) collective-permute-start(f32[264,256]{1,0:T(8,128)S(1)} %collective-permute-done.18.refs_1_), channel_id=1, source_target_pairs={{0,4},{1,3},{2,6},{3,1},{4,0},{5,7},{6,2},{7,5},{8,12},{9,11},{10,... | collective-permute-start | bytes 811016 | tf_op jit(solution)/shard_map/ppermute | solution.py:321
  69.5 7.5 %collective-permute-start.15 = (f32[264,256]{1,0:T(8,128)S(1)}, f32[264,256]{1,0:T(8,128)S(1)}, u32[]{:S(2)}, u32[]{:S(2)}) collective-permute-start(f32[264,256]{1,0:T(8,128)S(1)} %finish.1.refs_0_), channel_id=1, source_target_pairs={{0,8},{2,10},{4,12},{6,14},{16,0},{18,2},{20,4},{22,6},{24,16},{26... | collective-permute-start | bytes 811016 | tf_op jit(solution)/shard_map/ppermute | solution.py:328
  71.5 9.4 %collective-permute-start.22 = (f32[264,256]{1,0:T(8,128)S(1)}, f32[264,256]{1,0:T(8,128)S(1)}, u32[]{:S(2)}, u32[]{:S(2)}) collective-permute-start(f32[264,256]{1,0:T(8,128)S(1)} %collective-permute-done.14.refs_8_), channel_id=1, source_target_pairs={{0,2},{1,5},{2,0},{3,7},{4,6},{5,1},{6,4},{7,3},{8,10},{9,13},{10,... | collective-permute-start | bytes 811016 | tf_op jit(solution)/shard_map/ppermute | solution.py:321
  73.9 9.1 %collective-permute-start.27 = (f32[264,256]{1,0:T(8,128)S(1)}, f32[264,256]{1,0:T(8,128)S(1)}, u32[]{:S(2)}, u32[]{:S(2)}) collective-permute-start(f32[264,256]{1,0:T(8,128)S(1)} %collective-permute-done.26.refs_5_), channel_id=1, source_target_pairs={{0,4},{1,3},{2,6},{3,1},{4,0},{5,7},{6,2},{7,5},{8,12},{9,11},{10,... | collective-permute-start | bytes 811016 | tf_op jit(solution)/shard_map/ppermute | solution.py:321
  74.5 11.3 %collective-permute-start.23 = (f32[264,256]{1,0:T(8,128)S(1)}, f32[264,256]{1,0:T(8,128)S(1)}, u32[]{:S(2)}, u32[]{:S(2)}) collective-permute-start(f32[264,256]{1,0:T(8,128)S(1)} %collective-permute-done.14.refs_8_), channel_id=1, source_target_pairs={{0,4},{1,3},{2,6},{3,1},{4,0},{5,7},{6,2},{7,5},{8,12},{9,11},{10,... | collective-permute-start | bytes 811016 | tf_op jit(solution)/shard_map/ppermute | solution.py:321
  77.1 8.7 %collective-permute-start.25 = (f32[264,256]{1,0:T(8,128)S(1)}, f32[264,256]{1,0:T(8,128)S(1)}, u32[]{:S(2)}, u32[]{:S(2)}) collective-permute-start(f32[264,256]{1,0:T(8,128)S(1)} %collective-permute-done.19.refs_3_), channel_id=1, source_target_pairs={{0,8},{2,10},{4,12},{6,14},{16,0},{18,2},{20,4},{22,6},{24,16},{26... | collective-permute-start | bytes 811016 | tf_op jit(solution)/shard_map/ppermute | solution.py:328
  80.9 8.1 %collective-permute-start.24 = (f32[264,256]{1,0:T(8,128)S(1)}, f32[264,256]{1,0:T(8,128)S(1)}, u32[]{:S(2)}, u32[]{:S(2)}) collective-permute-start(f32[264,256]{1,0:T(8,128)S(1)} %collective-permute-done.22.refs_0_), channel_id=1, source_target_pairs={{0,4},{1,3},{2,6},{3,1},{4,0},{5,7},{6,2},{7,5},{8,12},{9,11},{10,... | collective-permute-start | bytes 811016 | tf_op jit(solution)/shard_map/ppermute | solution.py:321
  81.8 10.1 %collective-permute-start.21 = (f32[264,256]{1,0:T(8,128)S(1)}, f32[264,256]{1,0:T(8,128)S(1)}, u32[]{:S(2)}, u32[]{:S(2)}) collective-permute-start(f32[264,256]{1,0:T(8,128)S(1)} %collective-permute-done.15.refs_9_), channel_id=1, source_target_pairs={{0,4},{1,3},{2,6},{3,1},{4,0},{5,7},{6,2},{7,5},{8,12},{9,11},{10,... | collective-permute-start | bytes 811016 | tf_op jit(solution)/shard_map/ppermute | solution.py:321
  83.0 9.0 %collective-permute-start.20 = (f32[264,256]{1,0:T(8,128)S(1)}, f32[264,256]{1,0:T(8,128)S(1)}, u32[]{:S(2)}, u32[]{:S(2)}) collective-permute-start(f32[264,256]{1,0:T(8,128)S(1)} %collective-permute-done.15.refs_9_), channel_id=1, source_target_pairs={{0,2},{1,5},{2,0},{3,7},{4,6},{5,1},{6,4},{7,3},{8,10},{9,13},{10,... | collective-permute-start | bytes 811016 | tf_op jit(solution)/shard_map/ppermute | solution.py:321

commit v19 on v18

--- a/solution.py
+++ b/solution.py
@@ -110,9 +110,9 @@
     )
 
 
-def lse_kernel(cores, every, a_ref, b_ref, *refs):
+def lse_kernel(cores, every, *refs):
     pair_refs = refs[:cores]
-    lse_ref, evidence_ref, pack_a_ref, pack_b_ref = refs[cores:]
+    lse_ref, evidence_ref = refs[cores:]
     half = lse_ref.shape[1]
     top = functools.reduce(jnp.maximum, [p[0:1, :] for p in pair_refs])
     total = functools.reduce(jnp.add, [p[1:2, :] * jnp.exp(p[0:1, :] - top) for p in pair_refs])
@@ -122,10 +122,14 @@
         evidence_ref[k : k + 1, :] = evidence[:, k * LANES : (k + 1) * LANES]
     for i in range(2 * cores):
         lse_ref[i : i + 1, :] = lse[:, i * half : (i + 1) * half]
+
+
+def pack_kernel(lse_ref, a_ref, b_ref, pack_a_ref, pack_b_ref):
+    count, half = lse_ref.shape
     for piece, pack_ref in ((a_ref[0:half, :], pack_a_ref), (b_ref[half:, :], pack_b_ref)):
         pack_ref[0:half, :] = piece
         pack_ref[half:, :] = jnp.zeros_like(pack_ref[half:, :])
-        pack_ref[half : half + 2 * cores, 0:half] = lse_ref[...]
+        pack_ref[half : half + count, 0:half] = lse_ref[...]
 
 
 def weigh(twice, norm, x, lse, lanes):
@@ -335,18 +339,13 @@
 
     pair, twice, norm = stats(points, centroids, lines)
     pairs = [pair] + [flip_core(pair, rc) for rc in range(1, cores)]
-    tail = max(8, 2 * cores)
-    lse, log_evidence, pack_a, pack_b = call(
+    lse, log_evidence = call(
         functools.partial(lse_kernel, cores, local_cent * cores),
-        (f32(2 * cores, half), f32(rows // LANES, LANES), f32(half + tail, width), f32(half + tail, width)),
-        [VMEM] * (2 + cores),
-        (by_a, by_b, *pairs),
+        (f32(2 * cores, half), f32(rows // LANES, LANES)),
+        [VMEM] * cores,
+        pairs,
         "lse",
     )
-    d0, d1 = exchange(pack_a, 1), exchange(pack_b, 0)
-
-    by_a, by_b, lse = lax.optimization_barrier((by_a, by_b, lse))
-    near = with_siblings((by_a, by_b))
     lanes = min(LANES, half)
     acc, cnt = call(
         functools.partial(own_kernel, cores),
@@ -356,8 +355,13 @@
         "own",
         flops=4 * share * width * rows,
     )
-    lse, acc, cnt, near = lax.optimization_barrier((lse, acc, cnt, near))
+    lse, acc, cnt, by_a, by_b = lax.optimization_barrier((lse, acc, cnt, by_a, by_b))
+    piece = f32(half + max(8, 2 * cores), width)
+    pack_a, pack_b = call(pack_kernel, (piece, piece), [VMEM] * 3, (lse, by_a, by_b), "pack")
+    d0, d1 = exchange(pack_a, 1), exchange(pack_b, 0)
     lse_d = lax.ppermute(lse, "dp", [(i, i ^ 3) for i in range(n)])
+    by_a, by_b, _ = lax.optimization_barrier((by_a, by_b, pack_a))
+    near = with_siblings((by_a, by_b))
     near, d0, d1, acc, cnt, lse_d = lax.optimization_barrier((near, d0, d1, acc, cnt, lse_d))
     lead = call(
         functools.partial(lead_kernel, cores, order, half),

time: 93.1 us -> 92.9 us (level)
    ppermute x15, waiting for transfers between devices: 17.1 us -> 10.9 us  [exchange(): return lax.ppermute(x, ('dp', 'cent'), pairs)]
    ppermute x1, waiting for transfers between devices: 0.91 us -> 6.56 us  [body(): lse_d = lax.ppermute(lse, 'dp', [(i, i ^ 3) for i in range(n)])]
    pallas_call x13 -> x14, Pallas kernels: 15.8 us -> 15.8 us  [call(): pl.pallas_call(kernel, out_shape=out_shape, in_specs=in_specs, out_specs=...]
  transfers between devices with their start and end apart: 28 -> 28, of which waited for: 17 -> 16; matrix products, arithmetic and copies ran while one was open for 0% -> 0% of each run, Pallas kernels for 14% -> 15%
where the time goes in v19:
time: 92.9 us; the launch traced here: 92.7 us
  waiting for transfers between devices  41 us (44%)
  starting transfers between devices  32.3 us (35%)
  Pallas kernels  15.8 us (17%)
  local copies, waits for them, and re-layouts  2.63 us (3%)
  between operations  0.93 us (1%)
    ppermute x7, waiting for transfers between devices, ring(): lax.ppermute(x, 'dp', [(4 * a + i, 4 * b + i) for a, b in pairs for i in...  21.8 us
    ppermute x15, starting transfers between devices, exchange(): return lax.ppermute(x, ('dp', 'cent'), pairs)  17.3 us
    pallas_call x14, Pallas kernels, call(): pl.pallas_call(kernel, out_shape=out_shape, in_specs=in_specs, out_specs=...  15.8 us
    ppermute x7, starting transfers between devices, ring(): lax.ppermute(x, 'dp', [(4 * a + i, 4 * b + i) for a, b in pairs for i in...  13 us
    ppermute x15, waiting for transfers between devices, exchange(): return lax.ppermute(x, ('dp', 'cent'), pairs)  10.9 us
    ppermute x1, waiting for transfers between devices, body(): lse_d = lax.ppermute(lse, 'dp', [(i, i ^ 3) for i in range(n)])  6.56 us
    unnamed x6, local copies, waits for them, and re-layouts  2.63 us
  transfers between devices with their start and end apart: 28, of which 16 were waited for; matrix products, arithmetic and copies ran while one was open for 0% of the time, Pallas kernels for 15%

profile of v19, /device:TPU:0, one launch (start us, length us, event | category | flops | bytes accessed | tf_op | source)
XLA Modules:
  0.0 92.7 jit_solution(13417838232558495579)
XLA Ops:
  0.6 1.0 %copy-done = bf16[1024,256]{1,0:T(8,128)(2,1)S(1)} copy-done((bf16[1024,256]{1,0:T(8,128)(2,1)S(1)}, bf16[1024,256]{1,0:T(8,128)(2,1)}, u32[]{:S(2)}) %copy-start) | copy-done | bytes 524312
  1.7 3.0 %collective-permute-start.2 = (f32[512,256]{1,0:T(8,128)S(1)}, f32[512,256]{1,0:T(8,128)S(1)}, u32[]{:S(2)}, u32[]{:S(2)}) collective-permute-start(f32[512,256]{1,0:T(8,128)S(1)} %open.1), channel_id=1, source_target_pairs={{0,4},{1,3},{2,6},{3,1},{4,0},{5,7},{6,2},{7,5},{8,12},{9,11},{10,... | collective-permute-start | bytes 1572872 | tf_op jit(solution)/shard_map/ppermute | solution.py:325
  4.8 1.5 %collective-permute-start.1 = (f32[512,256]{1,0:T(8,128)S(1)}, f32[512,256]{1,0:T(8,128)S(1)}, u32[]{:S(2)}, u32[]{:S(2)}) collective-permute-start(f32[512,256]{1,0:T(8,128)S(1)} %open.1), channel_id=1, source_target_pairs={{0,2},{1,5},{2,0},{3,7},{4,6},{5,1},{6,4},{7,3},{8,10},{9,13},{10,... | collective-permute-start | bytes 1572872 | tf_op jit(solution)/shard_map/ppermute | solution.py:325
  6.3 1.6 %copy-done.2 = bf16[4096,256]{1,0:T(8,128)(2,1)S(1)} copy-done((bf16[4096,256]{1,0:T(8,128)(2,1)S(1)}, bf16[4096,256]{1,0:T(8,128)(2,1)}, u32[]{:S(2)}) %copy-start.2) | copy-done | bytes 2097176
  7.8 5.3 %stats.1 = (f32[2,1024]{1,0:T(2,128)S(1)}, bf16[1024,256]{1,0:T(8,128)(2,1)S(1)}, f32[1024,128]{1,0:T(8,128)S(1)}) custom-call(bf16[1024,256]{1,0:T(8,128)(2,1)S(1)} %copy-done, bf16[4096,256]{1,0:T(8,128)(2,1)S(1)} %copy-done.2), custom_call_target="tpu_custom_call" | custom-call | flops 4294967296 | bytes 2621440 | tf_op jit(solution)/shard_map/stats/pallas_call | solution.py:34
  13.2 1.2 %collective-permute-done.refs_1_ = f32[2,1024]{1,0:T(2,128)S(1)} collective-permute-done((f32[2,1024]{1,0:T(2,128)S(1)}, f32[2,1024]{1,0:T(2,128)S(1)}, u32[]{:S(2)}, u32[]{:S(2)}) %collective-permute-start) | collective-permute-done | bytes 8224 | tf_op jit(solution)/shard_map/ppermute | solution.py:328
  14.4 0.6 lse.1
  15.0 1.4 %own.1 = (f32[1024,256]{1,0:T(8,128)S(1)}, f32[1024,128]{1,0:T(8,128)S(1)}) custom-call(bf16[1024,256]{1,0:T(8,128)(2,1)S(1)} %copy-done.1, bf16[1024,256]{1,0:T(8,128)(2,1)S(1)} %get-tuple-element.43.twice_ref.refs_0_, f32[1024,128]{1,0:T(8,128)S(1)} %get-tuple-element.44.norm_ref.refs_1_, f32[4,256]{1,0:T(4,128)S(1)} %get-tuple-element.51.lse_ref), custom_call_target="tpu_custom_call" | custom-call | flops 1073741824 | bytes 1576960 | tf_op jit(solution)/shard_map/own/pallas_call | solution.py:34
  16.4 0.6 collective-permute-done.2.b_ref.refs_7_.refs_6_
  17.6 1.5 %collective-permute-start.6 = (f32[264,256]{1,0:T(8,128)S(1)}, f32[264,256]{1,0:T(8,128)S(1)}, u32[]{:S(2)}, u32[]{:S(2)}) collective-permute-start(f32[264,256]{1,0:T(8,128)S(1)} %get-tuple-element.55), channel_id=1, source_target_pairs={{0,2},{1,5},{2,0},{3,7},{4,6},{5,1},{6,4},{7,3},{8,10},{9,13},{10,... | collective-permute-start | bytes 811016 | tf_op jit(solution)/shard_map/ppermute | solution.py:325
  19.1 1.7 %collective-permute-start.5 = (f32[264,256]{1,0:T(8,128)S(1)}, f32[264,256]{1,0:T(8,128)S(1)}, u32[]{:S(2)}, u32[]{:S(2)}) collective-permute-start(f32[264,256]{1,0:T(8,128)S(1)} %get-tuple-element.52), channel_id=1, source_target_pairs={{0,4},{1,3},{2,6},{3,1},{4,0},{5,7},{6,2},{7,5},{8,12},{9,11},{10,... | collective-permute-start | bytes 811016 | tf_op jit(solution)/shard_map/ppermute | solution.py:325
  20.8 0.8 collective-permute-start.7
  21.6 6.6 %collective-permute-done.7.refs_4_.refs_2_ = f32[4,256]{1,0:T(4,128)S(1)} collective-permute-done((f32[4,256]{1,0:T(4,128)S(1)}, f32[4,256]{1,0:T(4,128)S(1)}, u32[]{:S(2)}, u32[]{:S(2)}) %collective-permute-start.7) | collective-permute-done | bytes 4128 | tf_op jit(solution)/shard_map/ppermute | solution.py:362
  28.2 0.5 collective-permute-start.9
  28.7 0.9 lead.1
  30.1 0.6 first.1
  30.7 2.9 %collective-permute-start.10 = (f32[264,256]{1,0:T(8,128)S(1)}, f32[264,256]{1,0:T(8,128)S(1)}, u32[]{:S(2)}, u32[]{:S(2)}) collective-permute-start(f32[264,256]{1,0:T(8,128)S(1)} %first.1), channel_id=1, source_target_pairs={{0,16},{2,18},{4,20},{6,22},{16,24},{18,26},{20,28},{22,30},{24,8}... | collective-permute-start | bytes 811016 | tf_op jit(solution)/shard_map/ppermute | solution.py:332
  33.6 1.2 %rest.3 = f32[264,256]{1,0:T(8,128)S(1)} custom-call(bf16[1024,256]{1,0:T(8,128)(2,1)S(1)} %get-tuple-element.43.twice_ref.refs_0_, f32[1024,128]{1,0:T(8,128)S(1)} %get-tuple-element.44.norm_ref.refs_1_, f32[1024,256]{1,0:T(8,128)S(1)} %get-tuple-element.58.refs_2_, f32[1024,128]{1,0:T(8,128)S(1)} %get-tuple-element.59.refs_3_, ...), custom_call_target="tpu_custom_call" | custom-call | flops 805306368 | bytes 5804032 | tf_op jit(solution)/shard_map/rest/pallas_call | solution.py:34
  35.0 2.1 %rest.2 = (f32[264,256]{1,0:T(8,128)S(1)}, f32[264,256]{1,0:T(8,128)S(1)}) custom-call(bf16[1024,256]{1,0:T(8,128)(2,1)S(1)} %get-tuple-element.43.twice_ref.refs_0_, f32[1024,128]{1,0:T(8,128)S(1)} %get-tuple-element.44.norm_ref.refs_1_, f32[1024,256]{1,0:T(8,128)S(1)} %get-tuple-element.58.refs_2_, f32[1024,128]{1,0:T(8,128)S(1)} %get-tuple-element.59.refs_3_, ...), custom_call_target="tpu_custom_call" | custom-call | flops 1610612736 | bytes 5804032 | tf_op jit(solution)/shard_map/rest/pallas_call | solution.py:34
  37.1 3.4 %collective-permute-done.10.b_ref = f32[264,256]{1,0:T(8,128)S(1)} collective-permute-done((f32[264,256]{1,0:T(8,128)S(1)}, f32[264,256]{1,0:T(8,128)S(1)}, u32[]{:S(2)}, u32[]{:S(2)}) %collective-permute-start.10) | collective-permute-done | bytes 270368 | tf_op jit(solution)/shard_map/ppermute | solution.py:332
  40.5 3.4 %collective-permute-start.11 = (f32[264,256]{1,0:T(8,128)S(1)}, f32[264,256]{1,0:T(8,128)S(1)}, u32[]{:S(2)}, u32[]{:S(2)}) collective-permute-start(f32[264,256]{1,0:T(8,128)S(1)} %add.1), channel_id=1, source_target_pairs={{0,16},{2,18},{4,20},{6,22},{16,24},{18,26},{20,28},{22,30},{24,8}... | collective-permute-start | bytes 811016 | tf_op jit(solution)/shard_map/ppermute | solution.py:332
  44.0 4.1 %collective-permute-done.12.refs_3_ = f32[264,256]{1,0:T(8,128)S(1)} collective-permute-done((f32[264,256]{1,0:T(8,128)S(1)}, f32[264,256]{1,0:T(8,128)S(1)}, u32[]{:S(2)}, u32[]{:S(2)}) %collective-permute-start.12) | collective-permute-done | bytes 270368 | tf_op jit(solution)/shard_map/ppermute | solution.py:332
  48.1 4.9 %collective-permute-done.11.refs_2_ = f32[264,256]{1,0:T(8,128)S(1)} collective-permute-done((f32[264,256]{1,0:T(8,128)S(1)}, f32[264,256]{1,0:T(8,128)S(1)}, u32[]{:S(2)}, u32[]{:S(2)}) %collective-permute-start.11) | collective-permute-done | bytes 270368 | tf_op jit(solution)/shard_map/ppermute | solution.py:332
  53.3 1.7 %collective-permute-start.13 = (f32[264,256]{1,0:T(8,128)S(1)}, f32[264,256]{1,0:T(8,128)S(1)}, u32[]{:S(2)}, u32[]{:S(2)}) collective-permute-start(f32[264,256]{1,0:T(8,128)S(1)} %finish.1.refs_0_), channel_id=1, source_target_pairs={{0,16},{2,18},{4,20},{6,22},{16,24},{18,26},{20,28},{22,30},{24,8}... | collective-permute-start | bytes 811016 | tf_op jit(solution)/shard_map/ppermute | solution.py:332
  55.0 0.8 collective-permute-start.16
  55.8 0.7 collective-permute-start.18
  56.5 5.2 %collective-permute-done.13.refs_4_ = f32[264,256]{1,0:T(8,128)S(1)} collective-permute-done((f32[264,256]{1,0:T(8,128)S(1)}, f32[264,256]{1,0:T(8,128)S(1)}, u32[]{:S(2)}, u32[]{:S(2)}) %collective-permute-start.13) | collective-permute-done | bytes 270368 | tf_op jit(solution)/shard_map/ppermute | solution.py:332
  61.8 1.8 %collective-permute-start.14 = (f32[264,256]{1,0:T(8,128)S(1)}, f32[264,256]{1,0:T(8,128)S(1)}, u32[]{:S(2)}, u32[]{:S(2)}) collective-permute-start(f32[264,256]{1,0:T(8,128)S(1)} %collective-permute-done.13.refs_4_), channel_id=1, source_target_pairs={{0,16},{2,18},{4,20},{6,22},{16,24},{18,26},{20,28},{22,30},{24,8}... | collective-permute-start | bytes 811016 | tf_op jit(solution)/shard_map/ppermute | solution.py:332
  63.6 0.8 collective-permute-start.17
  64.4 0.7 collective-permute-start.26
  65.2 1.1 %collective-permute-start.19 = (f32[264,256]{1,0:T(8,128)S(1)}, f32[264,256]{1,0:T(8,128)S(1)}, u32[]{:S(2)}, u32[]{:S(2)}) collective-permute-start(f32[264,256]{1,0:T(8,128)S(1)} %collective-permute-done.18.refs_1_), channel_id=1, source_target_pairs={{0,4},{1,3},{2,6},{3,1},{4,0},{5,7},{6,2},{7,5},{8,12},{9,11},{10,... | collective-permute-start | bytes 811016 | tf_op jit(solution)/shard_map/ppermute | solution.py:325
  66.3 3.1 %collective-permute-done.14.refs_8_ = f32[264,256]{1,0:T(8,128)S(1)} collective-permute-done((f32[264,256]{1,0:T(8,128)S(1)}, f32[264,256]{1,0:T(8,128)S(1)}, u32[]{:S(2)}, u32[]{:S(2)}) %collective-permute-start.14) | collective-permute-done | bytes 270368 | tf_op jit(solution)/shard_map/ppermute | solution.py:332
  69.3 2.0 %collective-permute-start.15 = (f32[264,256]{1,0:T(8,128)S(1)}, f32[264,256]{1,0:T(8,128)S(1)}, u32[]{:S(2)}, u32[]{:S(2)}) collective-permute-start(f32[264,256]{1,0:T(8,128)S(1)} %finish.1.refs_0_), channel_id=1, source_target_pairs={{0,8},{2,10},{4,12},{6,14},{16,0},{18,2},{20,4},{22,6},{24,16},{26... | collective-permute-start | bytes 811016 | tf_op jit(solution)/shard_map/ppermute | solution.py:332
  71.3 0.7 collective-permute-start.22
  71.9 1.8 %collective-permute-done.26.refs_5_ = f32[264,256]{1,0:T(8,128)S(1)} collective-permute-done((f32[264,256]{1,0:T(8,128)S(1)}, f32[264,256]{1,0:T(8,128)S(1)}, u32[]{:S(2)}, u32[]{:S(2)}) %collective-permute-start.26) | collective-permute-done | bytes 270368 | tf_op jit(solution)/shard_map/ppermute | solution.py:325
  74.2 1.5 %collective-permute-start.23 = (f32[264,256]{1,0:T(8,128)S(1)}, f32[264,256]{1,0:T(8,128)S(1)}, u32[]{:S(2)}, u32[]{:S(2)}) collective-permute-start(f32[264,256]{1,0:T(8,128)S(1)} %collective-permute-done.14.refs_8_), channel_id=1, source_target_pairs={{0,4},{1,3},{2,6},{3,1},{4,0},{5,7},{6,2},{7,5},{8,12},{9,11},{10,... | collective-permute-start | bytes 811016 | tf_op jit(solution)/shard_map/ppermute | solution.py:325
  75.7 1.1 %collective-permute-done.15.refs_9_ = f32[264,256]{1,0:T(8,128)S(1)} collective-permute-done((f32[264,256]{1,0:T(8,128)S(1)}, f32[264,256]{1,0:T(8,128)S(1)}, u32[]{:S(2)}, u32[]{:S(2)}) %collective-permute-start.15) | collective-permute-done | bytes 270368 | tf_op jit(solution)/shard_map/ppermute | solution.py:332
  76.9 1.1 %collective-permute-start.25 = (f32[264,256]{1,0:T(8,128)S(1)}, f32[264,256]{1,0:T(8,128)S(1)}, u32[]{:S(2)}, u32[]{:S(2)}) collective-permute-start(f32[264,256]{1,0:T(8,128)S(1)} %collective-permute-done.19.refs_3_), channel_id=1, source_target_pairs={{0,8},{2,10},{4,12},{6,14},{16,0},{18,2},{20,4},{22,6},{24,16},{26... | collective-permute-start | bytes 811016 | tf_op jit(solution)/shard_map/ppermute | solution.py:332
  77.9 2.8 %collective-permute-done.22.refs_0_ = f32[264,256]{1,0:T(8,128)S(1)} collective-permute-done((f32[264,256]{1,0:T(8,128)S(1)}, f32[264,256]{1,0:T(8,128)S(1)}, u32[]{:S(2)}, u32[]{:S(2)}) %collective-permute-start.22) | collective-permute-done | bytes 270368 | tf_op jit(solution)/shard_map/ppermute | solution.py:325
  80.7 0.8 collective-permute-start.24
  81.5 1.2 %collective-permute-start.21 = (f32[264,256]{1,0:T(8,128)S(1)}, f32[264,256]{1,0:T(8,128)S(1)}, u32[]{:S(2)}, u32[]{:S(2)}) collective-permute-start(f32[264,256]{1,0:T(8,128)S(1)} %collective-permute-done.15.refs_9_), channel_id=1, source_target_pairs={{0,4},{1,3},{2,6},{3,1},{4,0},{5,7},{6,2},{7,5},{8,12},{9,11},{10,... | collective-permute-start | bytes 811016 | tf_op jit(solution)/shard_map/ppermute | solution.py:325
  82.7 0.7 collective-permute-start.20
  83.4 1.6 %place_early.1 = (f32[4096,256]{1,0:T(8,128)}, f32[32,128]{1,0:T(8,128)S(1)}) custom-call(f32[264,256]{1,0:T(8,128)S(1)} %finish.1.refs_0_, f32[264,256]{1,0:T(8,128)S(1)} %collective-permute-done.18.refs_1_, f32[264,256]{1,0:T(8,128)S(1)} %collective-permute-done.16.refs_2_, f32[264,256]{1,0:T(8,128)S(1)} %collective-permute-done.19.refs_3_, ...), custom_call_target="tpu_custom_call" | custom-call | bytes 2703360 | tf_op jit(solution)/shard_map/place_early/pallas_call | solution.py:34
  85.0 0.6 collective-permute-done.23.refs_1_
  85.6 3.2 %collective-permute-done.24.refs_2_ = f32[264,256]{1,0:T(8,128)S(1)} collective-permute-done((f32[264,256]{1,0:T(8,128)S(1)}, f32[264,256]{1,0:T(8,128)S(1)}, u32[]{:S(2)}, u32[]{:S(2)}) %collective-permute-start.24) | collective-permute-done | bytes 270368 | tf_op jit(solution)/shard_map/ppermute | solution.py:325
  88.8 1.0 %place_middle.1 = (f32[4096,256]{1,0:T(8,128)}, f32[32,128]{1,0:T(8,128)S(1)}) custom-call(f32[264,256]{1,0:T(8,128)S(1)} %collective-permute-done.22.refs_0_, f32[264,256]{1,0:T(8,128)S(1)} %collective-permute-done.23.refs_1_, f32[264,256]{1,0:T(8,128)S(1)} %collective-permute-done.24.refs_2_, ...), custom_call_target="tpu_custom_call", output_to_operand_aliasing={{0}: (5, {})} | custom-call | bytes 5292032 | tf_op jit(solution)/shard_map/place_middle/pallas_call | solution.py:34
  89.9 1.9 %collective-permute-done.21.refs_1_ = f32[264,256]{1,0:T(8,128)S(1)} collective-permute-done((f32[264,256]{1,0:T(8,128)S(1)}, f32[264,256]{1,0:T(8,128)S(1)}, u32[]{:S(2)}, u32[]{:S(2)}) %collective-permute-start.21) | collective-permute-done | bytes 270368 | tf_op jit(solution)/shard_map/ppermute | solution.py:325
  91.7 0.8 place_late.1
  (28 shorter events, 2.4 us)
Async XLA Ops:
  0.6 1.0 %copy-start = (bf16[1024,256]{1,0:T(8,128)(2,1)S(1)}, bf16[1024,256]{1,0:T(8,128)(2,1)}, u32[]{:S(2)}) copy-start(bf16[1024,256]{1,0:T(8,128)(2,1)} %refs_0_.3) | copy-start | bytes 1572868
  1.7 13.3 %copy-start.1 = (bf16[1024,256]{1,0:T(8,128)(2,1)S(1)}, bf16[1024,256]{1,0:T(8,128)(2,1)}, u32[]{:S(2)}) copy-start(bf16[1024,256]{1,0:T(8,128)(2,1)} %refs_0_.3) | copy-start | bytes 1572868
  1.7 15.3 %collective-permute-start.2 = (f32[512,256]{1,0:T(8,128)S(1)}, f32[512,256]{1,0:T(8,128)S(1)}, u32[]{:S(2)}, u32[]{:S(2)}) collective-permute-start(f32[512,256]{1,0:T(8,128)S(1)} %open.1), channel_id=1, source_target_pairs={{0,4},{1,3},{2,6},{3,1},{4,0},{5,7},{6,2},{7,5},{8,12},{9,11},{10,... | collective-permute-start | bytes 1572872 | tf_op jit(solution)/shard_map/ppermute | solution.py:325
  4.8 12.3 %collective-permute-start.1 = (f32[512,256]{1,0:T(8,128)S(1)}, f32[512,256]{1,0:T(8,128)S(1)}, u32[]{:S(2)}, u32[]{:S(2)}) collective-permute-start(f32[512,256]{1,0:T(8,128)S(1)} %open.1), channel_id=1, source_target_pairs={{0,2},{1,5},{2,0},{3,7},{4,6},{5,1},{6,4},{7,3},{8,10},{9,13},{10,... | collective-permute-start | bytes 1572872 | tf_op jit(solution)/shard_map/ppermute | solution.py:325
  6.2 1.6 %copy-start.2 = (bf16[4096,256]{1,0:T(8,128)(2,1)S(1)}, bf16[4096,256]{1,0:T(8,128)(2,1)}, u32[]{:S(2)}) copy-start(bf16[4096,256]{1,0:T(8,128)(2,1)} %refs_1_.1) | copy-start | bytes 6291460
  13.2 1.2 %collective-permute-start = (f32[2,1024]{1,0:T(2,128)S(1)}, f32[2,1024]{1,0:T(2,128)S(1)}, u32[]{:S(2)}, u32[]{:S(2)}) collective-permute-start(f32[2,1024]{1,0:T(2,128)S(1)} %get-tuple-element.45.refs_0_), channel_id=1, source_target_pairs={{0,1},{1,0},{2,3},{3,2},{4,5},{5,4},{6,7},{7,6},{8,9},{9,8},{10,11... | collective-permute-start | bytes 24584 | tf_op jit(solution)/shard_map/ppermute | solution.py:328
  17.1 11.1 %collective-permute-start.3 = (f32[512,256]{1,0:T(8,128)S(1)}, f32[512,256]{1,0:T(8,128)S(1)}, u32[]{:S(2)}, u32[]{:S(2)}) collective-permute-start(f32[512,256]{1,0:T(8,128)S(1)} %collective-permute-done.1.a_ref.refs_5_.refs_4_), channel_id=1, source_target_pairs={{0,1},{1,0},{2,3},{3,2},{4,5},{5,4},{6,7},{7,6},{8,9},{9,8},{10,11... | collective-permute-start | bytes 1572872 | tf_op jit(solution)/shard_map/ppermute | solution.py:328
  17.5 10.7 %collective-permute-start.4 = (f32[512,256]{1,0:T(8,128)S(1)}, f32[512,256]{1,0:T(8,128)S(1)}, u32[]{:S(2)}, u32[]{:S(2)}) collective-permute-start(f32[512,256]{1,0:T(8,128)S(1)} %collective-permute-done.2.b_ref.refs_7_.refs_6_), channel_id=1, source_target_pairs={{0,1},{1,0},{2,3},{3,2},{4,5},{5,4},{6,7},{7,6},{8,9},{9,8},{10,11... | collective-permute-start | bytes 1572872 | tf_op jit(solution)/shard_map/ppermute | solution.py:328
  17.6 10.5 %collective-permute-start.6 = (f32[264,256]{1,0:T(8,128)S(1)}, f32[264,256]{1,0:T(8,128)S(1)}, u32[]{:S(2)}, u32[]{:S(2)}) collective-permute-start(f32[264,256]{1,0:T(8,128)S(1)} %get-tuple-element.55), channel_id=1, source_target_pairs={{0,2},{1,5},{2,0},{3,7},{4,6},{5,1},{6,4},{7,3},{8,10},{9,13},{10,... | collective-permute-start | bytes 811016 | tf_op jit(solution)/shard_map/ppermute | solution.py:325
  19.1 9.0 %collective-permute-start.5 = (f32[264,256]{1,0:T(8,128)S(1)}, f32[264,256]{1,0:T(8,128)S(1)}, u32[]{:S(2)}, u32[]{:S(2)}) collective-permute-start(f32[264,256]{1,0:T(8,128)S(1)} %get-tuple-element.52), channel_id=1, source_target_pairs={{0,4},{1,3},{2,6},{3,1},{4,0},{5,7},{6,2},{7,5},{8,12},{9,11},{10,... | collective-permute-start | bytes 811016 | tf_op jit(solution)/shard_map/ppermute | solution.py:325
  20.8 7.3 %collective-permute-start.7 = (f32[4,256]{1,0:T(4,128)S(1)}, f32[4,256]{1,0:T(4,128)S(1)}, u32[]{:S(2)}, u32[]{:S(2)}) collective-permute-start(f32[4,256]{1,0:T(4,128)S(1)} %get-tuple-element.51.lse_ref), channel_id=1, source_target_pairs={{0,6},{2,4},{4,2},{6,0},{8,14},{10,12},{12,10},{14,8},{16,22},{18,... | collective-permute-start | bytes 12296 | tf_op jit(solution)/shard_map/ppermute | solution.py:362
  28.1 1.6 %collective-permute-start.8 = (f32[264,256]{1,0:T(8,128)S(1)}, f32[264,256]{1,0:T(8,128)S(1)}, u32[]{:S(2)}, u32[]{:S(2)}) collective-permute-start(f32[264,256]{1,0:T(8,128)S(1)} %collective-permute-done.5.refs_9_.refs_8_.refs_5_), channel_id=1, source_target_pairs={{0,1},{1,0},{2,3},{3,2},{4,5},{5,4},{6,7},{7,6},{8,9},{9,8},{10,11... | collective-permute-start | bytes 811016 | tf_op jit(solution)/shard_map/ppermute | solution.py:328
  28.2 1.9 %collective-permute-start.9 = (f32[264,256]{1,0:T(8,128)S(1)}, f32[264,256]{1,0:T(8,128)S(1)}, u32[]{:S(2)}, u32[]{:S(2)}) collective-permute-start(f32[264,256]{1,0:T(8,128)S(1)} %collective-permute-done.6.refs_11_.refs_9_.refs_7_), channel_id=1, source_target_pairs={{0,1},{1,0},{2,3},{3,2},{4,5},{5,4},{6,7},{7,6},{8,9},{9,8},{10,11... | collective-permute-start | bytes 811016 | tf_op jit(solution)/shard_map/ppermute | solution.py:328
  30.7 9.8 %collective-permute-start.10 = (f32[264,256]{1,0:T(8,128)S(1)}, f32[264,256]{1,0:T(8,128)S(1)}, u32[]{:S(2)}, u32[]{:S(2)}) collective-permute-start(f32[264,256]{1,0:T(8,128)S(1)} %first.1), channel_id=1, source_target_pairs={{0,16},{2,18},{4,20},{6,22},{16,24},{18,26},{20,28},{22,30},{24,8}... | collective-permute-start | bytes 811016 | tf_op jit(solution)/shard_map/ppermute | solution.py:332
  34.8 13.3 %collective-permute-start.12 = (f32[264,256]{1,0:T(8,128)S(1)}, f32[264,256]{1,0:T(8,128)S(1)}, u32[]{:S(2)}, u32[]{:S(2)}) collective-permute-start(f32[264,256]{1,0:T(8,128)S(1)} %rest.3), channel_id=1, source_target_pairs={{0,8},{2,10},{4,12},{6,14},{16,0},{18,2},{20,4},{22,6},{24,16},{26... | collective-permute-start | bytes 811016 | tf_op jit(solution)/shard_map/ppermute | solution.py:332
  40.5 12.5 %collective-permute-start.11 = (f32[264,256]{1,0:T(8,128)S(1)}, f32[264,256]{1,0:T(8,128)S(1)}, u32[]{:S(2)}, u32[]{:S(2)}) collective-permute-start(f32[264,256]{1,0:T(8,128)S(1)} %add.1), channel_id=1, source_target_pairs={{0,16},{2,18},{4,20},{6,22},{16,24},{18,26},{20,28},{22,30},{24,8}... | collective-permute-start | bytes 811016 | tf_op jit(solution)/shard_map/ppermute | solution.py:332
  53.3 8.5 %collective-permute-start.13 = (f32[264,256]{1,0:T(8,128)S(1)}, f32[264,256]{1,0:T(8,128)S(1)}, u32[]{:S(2)}, u32[]{:S(2)}) collective-permute-start(f32[264,256]{1,0:T(8,128)S(1)} %finish.1.refs_0_), channel_id=1, source_target_pairs={{0,16},{2,18},{4,20},{6,22},{16,24},{18,26},{20,28},{22,30},{24,8}... | collective-permute-start | bytes 811016 | tf_op jit(solution)/shard_map/ppermute | solution.py:332
  55.0 8.6 %collective-permute-start.16 = (f32[264,256]{1,0:T(8,128)S(1)}, f32[264,256]{1,0:T(8,128)S(1)}, u32[]{:S(2)}, u32[]{:S(2)}) collective-permute-start(f32[264,256]{1,0:T(8,128)S(1)} %finish.1.refs_0_), channel_id=1, source_target_pairs={{0,4},{1,3},{2,6},{3,1},{4,0},{5,7},{6,2},{7,5},{8,12},{9,11},{10,... | collective-permute-start | bytes 811016 | tf_op jit(solution)/shard_map/ppermute | solution.py:325
  55.8 9.3 %collective-permute-start.18 = (f32[264,256]{1,0:T(8,128)S(1)}, f32[264,256]{1,0:T(8,128)S(1)}, u32[]{:S(2)}, u32[]{:S(2)}) collective-permute-start(f32[264,256]{1,0:T(8,128)S(1)} %finish.1.refs_0_), channel_id=1, source_target_pairs={{0,2},{1,5},{2,0},{3,7},{4,6},{5,1},{6,4},{7,3},{8,10},{9,13},{10,... | collective-permute-start | bytes 811016 | tf_op jit(solution)/shard_map/ppermute | solution.py:325
  61.8 7.6 %collective-permute-start.14 = (f32[264,256]{1,0:T(8,128)S(1)}, f32[264,256]{1,0:T(8,128)S(1)}, u32[]{:S(2)}, u32[]{:S(2)}) collective-permute-start(f32[264,256]{1,0:T(8,128)S(1)} %collective-permute-done.13.refs_4_), channel_id=1, source_target_pairs={{0,16},{2,18},{4,20},{6,22},{16,24},{18,26},{20,28},{22,30},{24,8}... | collective-permute-start | bytes 811016 | tf_op jit(solution)/shard_map/ppermute | solution.py:332
  63.6 7.7 %collective-permute-start.17 = (f32[264,256]{1,0:T(8,128)S(1)}, f32[264,256]{1,0:T(8,128)S(1)}, u32[]{:S(2)}, u32[]{:S(2)}) collective-permute-start(f32[264,256]{1,0:T(8,128)S(1)} %collective-permute-done.13.refs_4_), channel_id=1, source_target_pairs={{0,4},{1,3},{2,6},{3,1},{4,0},{5,7},{6,2},{7,5},{8,12},{9,11},{10,... | collective-permute-start | bytes 811016 | tf_op jit(solution)/shard_map/ppermute | solution.py:325
  64.4 9.3 %collective-permute-start.26 = (f32[264,256]{1,0:T(8,128)S(1)}, f32[264,256]{1,0:T(8,128)S(1)}, u32[]{:S(2)}, u32[]{:S(2)}) collective-permute-start(f32[264,256]{1,0:T(8,128)S(1)} %collective-permute-done.13.refs_4_), channel_id=1, source_target_pairs={{0,2},{1,5},{2,0},{3,7},{4,6},{5,1},{6,4},{7,3},{8,10},{9,13},{10,... | collective-permute-start | bytes 811016 | tf_op jit(solution)/shard_map/ppermute | solution.py:325
  65.2 10.6 %collective-permute-start.19 = (f32[264,256]{1,0:T(8,128)S(1)}, f32[264,256]{1,0:T(8,128)S(1)}, u32[]{:S(2)}, u32[]{:S(2)}) collective-permute-start(f32[264,256]{1,0:T(8,128)S(1)} %collective-permute-done.18.refs_1_), channel_id=1, source_target_pairs={{0,4},{1,3},{2,6},{3,1},{4,0},{5,7},{6,2},{7,5},{8,12},{9,11},{10,... | collective-permute-start | bytes 811016 | tf_op jit(solution)/shard_map/ppermute | solution.py:325
  69.3 7.5 %collective-permute-start.15 = (f32[264,256]{1,0:T(8,128)S(1)}, f32[264,256]{1,0:T(8,128)S(1)}, u32[]{:S(2)}, u32[]{:S(2)}) collective-permute-start(f32[264,256]{1,0:T(8,128)S(1)} %finish.1.refs_0_), channel_id=1, source_target_pairs={{0,8},{2,10},{4,12},{6,14},{16,0},{18,2},{20,4},{22,6},{24,16},{26... | collective-permute-start | bytes 811016 | tf_op jit(solution)/shard_map/ppermute | solution.py:332
  71.3 9.4 %collective-permute-start.22 = (f32[264,256]{1,0:T(8,128)S(1)}, f32[264,256]{1,0:T(8,128)S(1)}, u32[]{:S(2)}, u32[]{:S(2)}) collective-permute-start(f32[264,256]{1,0:T(8,128)S(1)} %collective-permute-done.14.refs_8_), channel_id=1, source_target_pairs={{0,2},{1,5},{2,0},{3,7},{4,6},{5,1},{6,4},{7,3},{8,10},{9,13},{10,... | collective-permute-start | bytes 811016 | tf_op jit(solution)/shard_map/ppermute | solution.py:325
  73.7 9.0 %collective-permute-start.27 = (f32[264,256]{1,0:T(8,128)S(1)}, f32[264,256]{1,0:T(8,128)S(1)}, u32[]{:S(2)}, u32[]{:S(2)}) collective-permute-start(f32[264,256]{1,0:T(8,128)S(1)} %collective-permute-done.26.refs_5_), channel_id=1, source_target_pairs={{0,4},{1,3},{2,6},{3,1},{4,0},{5,7},{6,2},{7,5},{8,12},{9,11},{10,... | collective-permute-start | bytes 811016 | tf_op jit(solution)/shard_map/ppermute | solution.py:325
  74.2 11.4 %collective-permute-start.23 = (f32[264,256]{1,0:T(8,128)S(1)}, f32[264,256]{1,0:T(8,128)S(1)}, u32[]{:S(2)}, u32[]{:S(2)}) collective-permute-start(f32[264,256]{1,0:T(8,128)S(1)} %collective-permute-done.14.refs_8_), channel_id=1, source_target_pairs={{0,4},{1,3},{2,6},{3,1},{4,0},{5,7},{6,2},{7,5},{8,12},{9,11},{10,... | collective-permute-start | bytes 811016 | tf_op jit(solution)/shard_map/ppermute | solution.py:325
  76.9 8.8 %collective-permute-start.25 = (f32[264,256]{1,0:T(8,128)S(1)}, f32[264,256]{1,0:T(8,128)S(1)}, u32[]{:S(2)}, u32[]{:S(2)}) collective-permute-start(f32[264,256]{1,0:T(8,128)S(1)} %collective-permute-done.19.refs_3_), channel_id=1, source_target_pairs={{0,8},{2,10},{4,12},{6,14},{16,0},{18,2},{20,4},{22,6},{24,16},{26... | collective-permute-start | bytes 811016 | tf_op jit(solution)/shard_map/ppermute | solution.py:332
  80.7 8.1 %collective-permute-start.24 = (f32[264,256]{1,0:T(8,128)S(1)}, f32[264,256]{1,0:T(8,128)S(1)}, u32[]{:S(2)}, u32[]{:S(2)}) collective-permute-start(f32[264,256]{1,0:T(8,128)S(1)} %collective-permute-done.22.refs_0_), channel_id=1, source_target_pairs={{0,4},{1,3},{2,6},{3,1},{4,0},{5,7},{6,2},{7,5},{8,12},{9,11},{10,... | collective-permute-start | bytes 811016 | tf_op jit(solution)/shard_map/ppermute | solution.py:325
  81.5 10.2 %collective-permute-start.21 = (f32[264,256]{1,0:T(8,128)S(1)}, f32[264,256]{1,0:T(8,128)S(1)}, u32[]{:S(2)}, u32[]{:S(2)}) collective-permute-start(f32[264,256]{1,0:T(8,128)S(1)} %collective-permute-done.15.refs_9_), channel_id=1, source_target_pairs={{0,4},{1,3},{2,6},{3,1},{4,0},{5,7},{6,2},{7,5},{8,12},{9,11},{10,... | collective-permute-start | bytes 811016 | tf_op jit(solution)/shard_map/ppermute | solution.py:325
  82.7 9.0 %collective-permute-start.20 = (f32[264,256]{1,0:T(8,128)S(1)}, f32[264,256]{1,0:T(8,128)S(1)}, u32[]{:S(2)}, u32[]{:S(2)}) collective-permute-start(f32[264,256]{1,0:T(8,128)S(1)} %collective-permute-done.15.refs_9_), channel_id=1, source_target_pairs={{0,2},{1,5},{2,0},{3,7},{4,6},{5,1},{6,4},{7,3},{8,10},{9,13},{10,... | collective-permute-start | bytes 811016 | tf_op jit(solution)/shard_map/ppermute | solution.py:325

commit v20 on v19

--- a/solution.py
+++ b/solution.py
@@ -435,10 +435,10 @@
             x = lax.optimization_barrier((x, got[0, s]))[0]
         got[0, ahead_of] = ring(x, 1 if ahead_of < 0 else -1)
     before = got[3, steps[-1] - 1] if steps[-1] > 0 else got[3, steps[-1] + 1]
-    before = lax.optimization_barrier((before, got[0, steps[-1]]))[0]
+    before = lax.optimization_barrier((before, got[0, steps[-2]]))[0]
     got[3, steps[-1]] = ring(before, -1 if steps[-1] > 0 else 1)
     late = [(1, steps[-1]), (2, steps[-1])]
-    middle = [(w, steps[-2]) for w in (1, 2, 3)] + [(3, steps[-1])]
+    middle = [(w, steps[-2]) for w in (1, 2, 3)]
     groups = ([k for k in got if k not in middle + late], middle, late)
     new = counts = None
     for later, names in enumerate(groups):

time: 92.9 us -> 93.2 us (level)
    ppermute x15, waiting for transfers between devices: 10.9 us -> 16.1 us  [exchange(): return lax.ppermute(x, ('dp', 'cent'), pairs)]
    ppermute x7, waiting for transfers between devices: 21.8 us -> 16.7 us  [ring(): lax.ppermute(x, 'dp', [(4 * a + i, 4 * b + i) for a, b in pairs for i in...]
  transfers between devices with their start and end apart: 28 -> 28, of which waited for: 16 -> 14; matrix products, arithmetic and copies ran while one was open for 0% -> 0% of each run, Pallas kernels for 15% -> 15%
where the time goes in v20:
time: 93.2 us; the launch traced here: 93 us
  waiting for transfers between devices  41 us (44%)
  starting transfers between devices  32.5 us (35%)
  Pallas kernels  15.8 us (17%)
  local copies, waits for them, and re-layouts  2.63 us (3%)
  between operations  0.94 us (1%)
    ppermute x15, starting transfers between devices, exchange(): return lax.ppermute(x, ('dp', 'cent'), pairs)  18 us
    ppermute x7, waiting for transfers between devices, ring(): lax.ppermute(x, 'dp', [(4 * a + i, 4 * b + i) for a, b in pairs for i in...  16.7 us
    ppermute x15, waiting for transfers between devices, exchange(): return lax.ppermute(x, ('dp', 'cent'), pairs)  16.1 us
    pallas_call x14, Pallas kernels, call(): pl.pallas_call(kernel, out_shape=out_shape, in_specs=in_specs, out_specs=...  15.8 us
    ppermute x7, starting transfers between devices, ring(): lax.ppermute(x, 'dp', [(4 * a + i, 4 * b + i) for a, b in pairs for i in...  12.6 us
    ppermute x1, waiting for transfers between devices, body(): lse_d = lax.ppermute(lse, 'dp', [(i, i ^ 3) for i in range(n)])  6.56 us
    unnamed x6, local copies, waits for them, and re-layouts  2.63 us
  transfers between devices with their start and end apart: 28, of which 14 were waited for; matrix products, arithmetic and copies ran while one was open for 0% of the time, Pallas kernels for 15%

profile of v20, /device:TPU:0, one launch (start us, length us, event | category | flops | bytes accessed | tf_op | source)
XLA Modules:
  0.0 93.0 jit_solution(14932046562509278008)
XLA Ops:
  0.6 1.0 %copy-done = bf16[1024,256]{1,0:T(8,128)(2,1)S(1)} copy-done((bf16[1024,256]{1,0:T(8,128)(2,1)S(1)}, bf16[1024,256]{1,0:T(8,128)(2,1)}, u32[]{:S(2)}) %copy-start) | copy-done | bytes 524312
  1.7 3.0 %collective-permute-start.2 = (f32[512,256]{1,0:T(8,128)S(1)}, f32[512,256]{1,0:T(8,128)S(1)}, u32[]{:S(2)}, u32[]{:S(2)}) collective-permute-start(f32[512,256]{1,0:T(8,128)S(1)} %open.1), channel_id=1, source_target_pairs={{0,4},{1,3},{2,6},{3,1},{4,0},{5,7},{6,2},{7,5},{8,12},{9,11},{10,... | collective-permute-start | bytes 1572872 | tf_op jit(solution)/shard_map/ppermute | solution.py:325
  4.8 1.5 %collective-permute-start.1 = (f32[512,256]{1,0:T(8,128)S(1)}, f32[512,256]{1,0:T(8,128)S(1)}, u32[]{:S(2)}, u32[]{:S(2)}) collective-permute-start(f32[512,256]{1,0:T(8,128)S(1)} %open.1), channel_id=1, source_target_pairs={{0,2},{1,5},{2,0},{3,7},{4,6},{5,1},{6,4},{7,3},{8,10},{9,13},{10,... | collective-permute-start | bytes 1572872 | tf_op jit(solution)/shard_map/ppermute | solution.py:325
  6.3 1.6 %copy-done.2 = bf16[4096,256]{1,0:T(8,128)(2,1)S(1)} copy-done((bf16[4096,256]{1,0:T(8,128)(2,1)S(1)}, bf16[4096,256]{1,0:T(8,128)(2,1)}, u32[]{:S(2)}) %copy-start.2) | copy-done | bytes 2097176
  7.8 5.3 %stats.1 = (f32[2,1024]{1,0:T(2,128)S(1)}, bf16[1024,256]{1,0:T(8,128)(2,1)S(1)}, f32[1024,128]{1,0:T(8,128)S(1)}) custom-call(bf16[1024,256]{1,0:T(8,128)(2,1)S(1)} %copy-done, bf16[4096,256]{1,0:T(8,128)(2,1)S(1)} %copy-done.2), custom_call_target="tpu_custom_call" | custom-call | flops 4294967296 | bytes 2621440 | tf_op jit(solution)/shard_map/stats/pallas_call | solution.py:34
  13.2 1.2 %collective-permute-done.refs_1_ = f32[2,1024]{1,0:T(2,128)S(1)} collective-permute-done((f32[2,1024]{1,0:T(2,128)S(1)}, f32[2,1024]{1,0:T(2,128)S(1)}, u32[]{:S(2)}, u32[]{:S(2)}) %collective-permute-start) | collective-permute-done | bytes 8224 | tf_op jit(solution)/shard_map/ppermute | solution.py:328
  14.4 0.6 lse.1
  15.0 1.4 %own.1 = (f32[1024,256]{1,0:T(8,128)S(1)}, f32[1024,128]{1,0:T(8,128)S(1)}) custom-call(bf16[1024,256]{1,0:T(8,128)(2,1)S(1)} %copy-done.1, bf16[1024,256]{1,0:T(8,128)(2,1)S(1)} %get-tuple-element.43.twice_ref.refs_0_, f32[1024,128]{1,0:T(8,128)S(1)} %get-tuple-element.44.norm_ref.refs_1_, f32[4,256]{1,0:T(4,128)S(1)} %get-tuple-element.51.lse_ref), custom_call_target="tpu_custom_call" | custom-call | flops 1073741824 | bytes 1576960 | tf_op jit(solution)/shard_map/own/pallas_call | solution.py:34
  16.4 0.6 collective-permute-done.2.b_ref.refs_7_.refs_6_
  17.1 0.4 collective-permute-start.3
  17.6 1.5 %collective-permute-start.6 = (f32[264,256]{1,0:T(8,128)S(1)}, f32[264,256]{1,0:T(8,128)S(1)}, u32[]{:S(2)}, u32[]{:S(2)}) collective-permute-start(f32[264,256]{1,0:T(8,128)S(1)} %get-tuple-element.55), channel_id=1, source_target_pairs={{0,2},{1,5},{2,0},{3,7},{4,6},{5,1},{6,4},{7,3},{8,10},{9,13},{10,... | collective-permute-start | bytes 811016 | tf_op jit(solution)/shard_map/ppermute | solution.py:325
  19.1 1.7 %collective-permute-start.5 = (f32[264,256]{1,0:T(8,128)S(1)}, f32[264,256]{1,0:T(8,128)S(1)}, u32[]{:S(2)}, u32[]{:S(2)}) collective-permute-start(f32[264,256]{1,0:T(8,128)S(1)} %get-tuple-element.52), channel_id=1, source_target_pairs={{0,4},{1,3},{2,6},{3,1},{4,0},{5,7},{6,2},{7,5},{8,12},{9,11},{10,... | collective-permute-start | bytes 811016 | tf_op jit(solution)/shard_map/ppermute | solution.py:325
  20.8 0.8 collective-permute-start.7
  21.6 6.6 %collective-permute-done.7.refs_4_.refs_2_ = f32[4,256]{1,0:T(4,128)S(1)} collective-permute-done((f32[4,256]{1,0:T(4,128)S(1)}, f32[4,256]{1,0:T(4,128)S(1)}, u32[]{:S(2)}, u32[]{:S(2)}) %collective-permute-start.7) | collective-permute-done | bytes 4128 | tf_op jit(solution)/shard_map/ppermute | solution.py:362
  28.2 0.5 collective-permute-start.9
  28.7 0.9 lead.1
  30.1 0.6 first.1
  30.7 2.9 %collective-permute-start.10 = (f32[264,256]{1,0:T(8,128)S(1)}, f32[264,256]{1,0:T(8,128)S(1)}, u32[]{:S(2)}, u32[]{:S(2)}) collective-permute-start(f32[264,256]{1,0:T(8,128)S(1)} %first.1), channel_id=1, source_target_pairs={{0,16},{2,18},{4,20},{6,22},{16,24},{18,26},{20,28},{22,30},{24,8}... | collective-permute-start | bytes 811016 | tf_op jit(solution)/shard_map/ppermute | solution.py:332
  33.6 1.2 %rest.3 = f32[264,256]{1,0:T(8,128)S(1)} custom-call(bf16[1024,256]{1,0:T(8,128)(2,1)S(1)} %get-tuple-element.43.twice_ref.refs_0_, f32[1024,128]{1,0:T(8,128)S(1)} %get-tuple-element.44.norm_ref.refs_1_, f32[1024,256]{1,0:T(8,128)S(1)} %get-tuple-element.58.refs_2_, f32[1024,128]{1,0:T(8,128)S(1)} %get-tuple-element.59.refs_3_, ...), custom_call_target="tpu_custom_call" | custom-call | flops 805306368 | bytes 5804032 | tf_op jit(solution)/shard_map/rest/pallas_call | solution.py:34
  35.0 2.1 %rest.2 = (f32[264,256]{1,0:T(8,128)S(1)}, f32[264,256]{1,0:T(8,128)S(1)}) custom-call(bf16[1024,256]{1,0:T(8,128)(2,1)S(1)} %get-tuple-element.43.twice_ref.refs_0_, f32[1024,128]{1,0:T(8,128)S(1)} %get-tuple-element.44.norm_ref.refs_1_, f32[1024,256]{1,0:T(8,128)S(1)} %get-tuple-element.58.refs_2_, f32[1024,128]{1,0:T(8,128)S(1)} %get-tuple-element.59.refs_3_, ...), custom_call_target="tpu_custom_call" | custom-call | flops 1610612736 | bytes 5804032 | tf_op jit(solution)/shard_map/rest/pallas_call | solution.py:34
  37.1 3.4 %collective-permute-done.10.b_ref = f32[264,256]{1,0:T(8,128)S(1)} collective-permute-done((f32[264,256]{1,0:T(8,128)S(1)}, f32[264,256]{1,0:T(8,128)S(1)}, u32[]{:S(2)}, u32[]{:S(2)}) %collective-permute-start.10) | collective-permute-done | bytes 270368 | tf_op jit(solution)/shard_map/ppermute | solution.py:332
  40.5 3.4 %collective-permute-start.11 = (f32[264,256]{1,0:T(8,128)S(1)}, f32[264,256]{1,0:T(8,128)S(1)}, u32[]{:S(2)}, u32[]{:S(2)}) collective-permute-start(f32[264,256]{1,0:T(8,128)S(1)} %add.1), channel_id=1, source_target_pairs={{0,16},{2,18},{4,20},{6,22},{16,24},{18,26},{20,28},{22,30},{24,8}... | collective-permute-start | bytes 811016 | tf_op jit(solution)/shard_map/ppermute | solution.py:332
  44.0 4.1 %collective-permute-done.12.refs_3_ = f32[264,256]{1,0:T(8,128)S(1)} collective-permute-done((f32[264,256]{1,0:T(8,128)S(1)}, f32[264,256]{1,0:T(8,128)S(1)}, u32[]{:S(2)}, u32[]{:S(2)}) %collective-permute-start.12) | collective-permute-done | bytes 270368 | tf_op jit(solution)/shard_map/ppermute | solution.py:332
  48.1 4.9 %collective-permute-done.11.refs_2_ = f32[264,256]{1,0:T(8,128)S(1)} collective-permute-done((f32[264,256]{1,0:T(8,128)S(1)}, f32[264,256]{1,0:T(8,128)S(1)}, u32[]{:S(2)}, u32[]{:S(2)}) %collective-permute-start.11) | collective-permute-done | bytes 270368 | tf_op jit(solution)/shard_map/ppermute | solution.py:332
  53.3 0.9 collective-permute-start.16
  54.2 1.6 %collective-permute-start.13 = (f32[264,256]{1,0:T(8,128)S(1)}, f32[264,256]{1,0:T(8,128)S(1)}, u32[]{:S(2)}, u32[]{:S(2)}) collective-permute-start(f32[264,256]{1,0:T(8,128)S(1)} %finish.1.refs_0_), channel_id=1, source_target_pairs={{0,16},{2,18},{4,20},{6,22},{16,24},{18,26},{20,28},{22,30},{24,8}... | collective-permute-start | bytes 811016 | tf_op jit(solution)/shard_map/ppermute | solution.py:332
  55.8 0.7 collective-permute-start.18
  56.6 6.1 %collective-permute-done.16.refs_2_ = f32[264,256]{1,0:T(8,128)S(1)} collective-permute-done((f32[264,256]{1,0:T(8,128)S(1)}, f32[264,256]{1,0:T(8,128)S(1)}, u32[]{:S(2)}, u32[]{:S(2)}) %collective-permute-start.16) | collective-permute-done | bytes 270368 | tf_op jit(solution)/shard_map/ppermute | solution.py:325
  62.7 0.8 collective-permute-start.17
  63.5 1.4 %collective-permute-start.14 = (f32[264,256]{1,0:T(8,128)S(1)}, f32[264,256]{1,0:T(8,128)S(1)}, u32[]{:S(2)}, u32[]{:S(2)}) collective-permute-start(f32[264,256]{1,0:T(8,128)S(1)} %collective-permute-done.13.refs_4_), channel_id=1, source_target_pairs={{0,16},{2,18},{4,20},{6,22},{16,24},{18,26},{20,28},{22,30},{24,8}... | collective-permute-start | bytes 811016 | tf_op jit(solution)/shard_map/ppermute | solution.py:332
  64.9 1.3 %collective-permute-start.25 = (f32[264,256]{1,0:T(8,128)S(1)}, f32[264,256]{1,0:T(8,128)S(1)}, u32[]{:S(2)}, u32[]{:S(2)}) collective-permute-start(f32[264,256]{1,0:T(8,128)S(1)} %collective-permute-done.13.refs_4_), channel_id=1, source_target_pairs={{0,2},{1,5},{2,0},{3,7},{4,6},{5,1},{6,4},{7,3},{8,10},{9,13},{10,... | collective-permute-start | bytes 811016 | tf_op jit(solution)/shard_map/ppermute | solution.py:325
  66.2 1.2 %collective-permute-start.19 = (f32[264,256]{1,0:T(8,128)S(1)}, f32[264,256]{1,0:T(8,128)S(1)}, u32[]{:S(2)}, u32[]{:S(2)}) collective-permute-start(f32[264,256]{1,0:T(8,128)S(1)} %collective-permute-done.18.refs_1_), channel_id=1, source_target_pairs={{0,4},{1,3},{2,6},{3,1},{4,0},{5,7},{6,2},{7,5},{8,12},{9,11},{10,... | collective-permute-start | bytes 811016 | tf_op jit(solution)/shard_map/ppermute | solution.py:325
  67.4 4.4 %collective-permute-done.17.refs_6_ = f32[264,256]{1,0:T(8,128)S(1)} collective-permute-done((f32[264,256]{1,0:T(8,128)S(1)}, f32[264,256]{1,0:T(8,128)S(1)}, u32[]{:S(2)}, u32[]{:S(2)}) %collective-permute-start.17) | collective-permute-done | bytes 270368 | tf_op jit(solution)/shard_map/ppermute | solution.py:325
  71.7 1.2 %collective-permute-start.15 = (f32[264,256]{1,0:T(8,128)S(1)}, f32[264,256]{1,0:T(8,128)S(1)}, u32[]{:S(2)}, u32[]{:S(2)}) collective-permute-start(f32[264,256]{1,0:T(8,128)S(1)} %finish.1.refs_0_), channel_id=1, source_target_pairs={{0,8},{2,10},{4,12},{6,14},{16,0},{18,2},{20,4},{22,6},{24,16},{26... | collective-permute-start | bytes 811016 | tf_op jit(solution)/shard_map/ppermute | solution.py:332
  73.0 0.7 collective-permute-start.22
  73.6 1.4 %collective-permute-start.26 = (f32[264,256]{1,0:T(8,128)S(1)}, f32[264,256]{1,0:T(8,128)S(1)}, u32[]{:S(2)}, u32[]{:S(2)}) collective-permute-start(f32[264,256]{1,0:T(8,128)S(1)} %collective-permute-done.25.refs_5_), channel_id=1, source_target_pairs={{0,4},{1,3},{2,6},{3,1},{4,0},{5,7},{6,2},{7,5},{8,12},{9,11},{10,... | collective-permute-start | bytes 811016 | tf_op jit(solution)/shard_map/ppermute | solution.py:325
  75.1 0.6 collective-permute-start.23
  75.7 1.8 %collective-permute-start.27 = (f32[264,256]{1,0:T(8,128)S(1)}, f32[264,256]{1,0:T(8,128)S(1)}, u32[]{:S(2)}, u32[]{:S(2)}) collective-permute-start(f32[264,256]{1,0:T(8,128)S(1)} %collective-permute-done.19.refs_3_), channel_id=1, source_target_pairs={{0,8},{2,10},{4,12},{6,14},{16,0},{18,2},{20,4},{22,6},{24,16},{26... | collective-permute-start | bytes 811016 | tf_op jit(solution)/shard_map/ppermute | solution.py:332
  77.4 4.3 %collective-permute-done.15.refs_9_ = f32[264,256]{1,0:T(8,128)S(1)} collective-permute-done((f32[264,256]{1,0:T(8,128)S(1)}, f32[264,256]{1,0:T(8,128)S(1)}, u32[]{:S(2)}, u32[]{:S(2)}) %collective-permute-start.15) | collective-permute-done | bytes 270368 | tf_op jit(solution)/shard_map/ppermute | solution.py:332
  81.7 0.7 collective-permute-done.22.refs_0_
  82.4 0.6 collective-permute-start.24
  83.0 1.5 %collective-permute-start.21 = (f32[264,256]{1,0:T(8,128)S(1)}, f32[264,256]{1,0:T(8,128)S(1)}, u32[]{:S(2)}, u32[]{:S(2)}) collective-permute-start(f32[264,256]{1,0:T(8,128)S(1)} %collective-permute-done.15.refs_9_), channel_id=1, source_target_pairs={{0,4},{1,3},{2,6},{3,1},{4,0},{5,7},{6,2},{7,5},{8,12},{9,11},{10,... | collective-permute-start | bytes 811016 | tf_op jit(solution)/shard_map/ppermute | solution.py:325
  84.4 0.7 collective-permute-start.20
  85.1 1.7 %place_early.1 = (f32[4096,256]{1,0:T(8,128)}, f32[32,128]{1,0:T(8,128)S(1)}) custom-call(f32[264,256]{1,0:T(8,128)S(1)} %finish.1.refs_0_, f32[264,256]{1,0:T(8,128)S(1)} %collective-permute-done.18.refs_1_, f32[264,256]{1,0:T(8,128)S(1)} %collective-permute-done.16.refs_2_, f32[264,256]{1,0:T(8,128)S(1)} %collective-permute-done.19.refs_3_, ...), custom_call_target="tpu_custom_call" | custom-call | bytes 2973696 | tf_op jit(solution)/shard_map/place_early/pallas_call | solution.py:34
  86.8 2.3 %collective-permute-done.24.refs_2_ = f32[264,256]{1,0:T(8,128)S(1)} collective-permute-done((f32[264,256]{1,0:T(8,128)S(1)}, f32[264,256]{1,0:T(8,128)S(1)}, u32[]{:S(2)}, u32[]{:S(2)}) %collective-permute-start.24) | collective-permute-done | bytes 270368 | tf_op jit(solution)/shard_map/ppermute | solution.py:325
  89.1 0.9 place_middle.1
  90.0 2.0 %collective-permute-done.21.refs_1_ = f32[264,256]{1,0:T(8,128)S(1)} collective-permute-done((f32[264,256]{1,0:T(8,128)S(1)}, f32[264,256]{1,0:T(8,128)S(1)}, u32[]{:S(2)}, u32[]{:S(2)}) %collective-permute-start.21) | collective-permute-done | bytes 270368 | tf_op jit(solution)/shard_map/ppermute | solution.py:325
  92.0 0.8 place_late.1
  (28 shorter events, 1.5 us)
Async XLA Ops:
  0.6 1.0 %copy-start = (bf16[1024,256]{1,0:T(8,128)(2,1)S(1)}, bf16[1024,256]{1,0:T(8,128)(2,1)}, u32[]{:S(2)}) copy-start(bf16[1024,256]{1,0:T(8,128)(2,1)} %refs_0_.3) | copy-start | bytes 1572868
  1.7 13.3 %copy-start.1 = (bf16[1024,256]{1,0:T(8,128)(2,1)S(1)}, bf16[1024,256]{1,0:T(8,128)(2,1)}, u32[]{:S(2)}) copy-start(bf16[1024,256]{1,0:T(8,128)(2,1)} %refs_0_.3) | copy-start | bytes 1572868
  1.7 15.3 %collective-permute-start.2 = (f32[512,256]{1,0:T(8,128)S(1)}, f32[512,256]{1,0:T(8,128)S(1)}, u32[]{:S(2)}, u32[]{:S(2)}) collective-permute-start(f32[512,256]{1,0:T(8,128)S(1)} %open.1), channel_id=1, source_target_pairs={{0,4},{1,3},{2,6},{3,1},{4,0},{5,7},{6,2},{7,5},{8,12},{9,11},{10,... | collective-permute-start | bytes 1572872 | tf_op jit(solution)/shard_map/ppermute | solution.py:325
  4.8 12.3 %collective-permute-start.1 = (f32[512,256]{1,0:T(8,128)S(1)}, f32[512,256]{1,0:T(8,128)S(1)}, u32[]{:S(2)}, u32[]{:S(2)}) collective-permute-start(f32[512,256]{1,0:T(8,128)S(1)} %open.1), channel_id=1, source_target_pairs={{0,2},{1,5},{2,0},{3,7},{4,6},{5,1},{6,4},{7,3},{8,10},{9,13},{10,... | collective-permute-start | bytes 1572872 | tf_op jit(solution)/shard_map/ppermute | solution.py:325
  6.2 1.6 %copy-start.2 = (bf16[4096,256]{1,0:T(8,128)(2,1)S(1)}, bf16[4096,256]{1,0:T(8,128)(2,1)}, u32[]{:S(2)}) copy-start(bf16[4096,256]{1,0:T(8,128)(2,1)} %refs_1_.1) | copy-start | bytes 6291460
  13.2 1.2 %collective-permute-start = (f32[2,1024]{1,0:T(2,128)S(1)}, f32[2,1024]{1,0:T(2,128)S(1)}, u32[]{:S(2)}, u32[]{:S(2)}) collective-permute-start(f32[2,1024]{1,0:T(2,128)S(1)} %get-tuple-element.45.refs_0_), channel_id=1, source_target_pairs={{0,1},{1,0},{2,3},{3,2},{4,5},{5,4},{6,7},{7,6},{8,9},{9,8},{10,11... | collective-permute-start | bytes 24584 | tf_op jit(solution)/shard_map/ppermute | solution.py:328
  17.1 11.1 %collective-permute-start.3 = (f32[512,256]{1,0:T(8,128)S(1)}, f32[512,256]{1,0:T(8,128)S(1)}, u32[]{:S(2)}, u32[]{:S(2)}) collective-permute-start(f32[512,256]{1,0:T(8,128)S(1)} %collective-permute-done.1.a_ref.refs_5_.refs_4_), channel_id=1, source_target_pairs={{0,1},{1,0},{2,3},{3,2},{4,5},{5,4},{6,7},{7,6},{8,9},{9,8},{10,11... | collective-permute-start | bytes 1572872 | tf_op jit(solution)/shard_map/ppermute | solution.py:328
  17.5 10.7 %collective-permute-start.4 = (f32[512,256]{1,0:T(8,128)S(1)}, f32[512,256]{1,0:T(8,128)S(1)}, u32[]{:S(2)}, u32[]{:S(2)}) collective-permute-start(f32[512,256]{1,0:T(8,128)S(1)} %collective-permute-done.2.b_ref.refs_7_.refs_6_), channel_id=1, source_target_pairs={{0,1},{1,0},{2,3},{3,2},{4,5},{5,4},{6,7},{7,6},{8,9},{9,8},{10,11... | collective-permute-start | bytes 1572872 | tf_op jit(solution)/shard_map/ppermute | solution.py:328
  17.6 10.5 %collective-permute-start.6 = (f32[264,256]{1,0:T(8,128)S(1)}, f32[264,256]{1,0:T(8,128)S(1)}, u32[]{:S(2)}, u32[]{:S(2)}) collective-permute-start(f32[264,256]{1,0:T(8,128)S(1)} %get-tuple-element.55), channel_id=1, source_target_pairs={{0,2},{1,5},{2,0},{3,7},{4,6},{5,1},{6,4},{7,3},{8,10},{9,13},{10,... | collective-permute-start | bytes 811016 | tf_op jit(solution)/shard_map/ppermute | solution.py:325
  19.1 9.0 %collective-permute-start.5 = (f32[264,256]{1,0:T(8,128)S(1)}, f32[264,256]{1,0:T(8,128)S(1)}, u32[]{:S(2)}, u32[]{:S(2)}) collective-permute-start(f32[264,256]{1,0:T(8,128)S(1)} %get-tuple-element.52), channel_id=1, source_target_pairs={{0,4},{1,3},{2,6},{3,1},{4,0},{5,7},{6,2},{7,5},{8,12},{9,11},{10,... | collective-permute-start | bytes 811016 | tf_op jit(solution)/shard_map/ppermute | solution.py:325
  20.8 7.3 %collective-permute-start.7 = (f32[4,256]{1,0:T(4,128)S(1)}, f32[4,256]{1,0:T(4,128)S(1)}, u32[]{:S(2)}, u32[]{:S(2)}) collective-permute-start(f32[4,256]{1,0:T(4,128)S(1)} %get-tuple-element.51.lse_ref), channel_id=1, source_target_pairs={{0,6},{2,4},{4,2},{6,0},{8,14},{10,12},{12,10},{14,8},{16,22},{18,... | collective-permute-start | bytes 12296 | tf_op jit(solution)/shard_map/ppermute | solution.py:362
  28.1 1.6 %collective-permute-start.8 = (f32[264,256]{1,0:T(8,128)S(1)}, f32[264,256]{1,0:T(8,128)S(1)}, u32[]{:S(2)}, u32[]{:S(2)}) collective-permute-start(f32[264,256]{1,0:T(8,128)S(1)} %collective-permute-done.5.refs_9_.refs_8_.refs_5_), channel_id=1, source_target_pairs={{0,1},{1,0},{2,3},{3,2},{4,5},{5,4},{6,7},{7,6},{8,9},{9,8},{10,11... | collective-permute-start | bytes 811016 | tf_op jit(solution)/shard_map/ppermute | solution.py:328
  28.2 1.9 %collective-permute-start.9 = (f32[264,256]{1,0:T(8,128)S(1)}, f32[264,256]{1,0:T(8,128)S(1)}, u32[]{:S(2)}, u32[]{:S(2)}) collective-permute-start(f32[264,256]{1,0:T(8,128)S(1)} %collective-permute-done.6.refs_11_.refs_9_.refs_7_), channel_id=1, source_target_pairs={{0,1},{1,0},{2,3},{3,2},{4,5},{5,4},{6,7},{7,6},{8,9},{9,8},{10,11... | collective-permute-start | bytes 811016 | tf_op jit(solution)/shard_map/ppermute | solution.py:328
  30.7 9.8 %collective-permute-start.10 = (f32[264,256]{1,0:T(8,128)S(1)}, f32[264,256]{1,0:T(8,128)S(1)}, u32[]{:S(2)}, u32[]{:S(2)}) collective-permute-start(f32[264,256]{1,0:T(8,128)S(1)} %first.1), channel_id=1, source_target_pairs={{0,16},{2,18},{4,20},{6,22},{16,24},{18,26},{20,28},{22,30},{24,8}... | collective-permute-start | bytes 811016 | tf_op jit(solution)/shard_map/ppermute | solution.py:332
  34.8 13.3 %collective-permute-start.12 = (f32[264,256]{1,0:T(8,128)S(1)}, f32[264,256]{1,0:T(8,128)S(1)}, u32[]{:S(2)}, u32[]{:S(2)}) collective-permute-start(f32[264,256]{1,0:T(8,128)S(1)} %rest.3), channel_id=1, source_target_pairs={{0,8},{2,10},{4,12},{6,14},{16,0},{18,2},{20,4},{22,6},{24,16},{26... | collective-permute-start | bytes 811016 | tf_op jit(solution)/shard_map/ppermute | solution.py:332
  40.5 12.5 %collective-permute-start.11 = (f32[264,256]{1,0:T(8,128)S(1)}, f32[264,256]{1,0:T(8,128)S(1)}, u32[]{:S(2)}, u32[]{:S(2)}) collective-permute-start(f32[264,256]{1,0:T(8,128)S(1)} %add.1), channel_id=1, source_target_pairs={{0,16},{2,18},{4,20},{6,22},{16,24},{18,26},{20,28},{22,30},{24,8}... | collective-permute-start | bytes 811016 | tf_op jit(solution)/shard_map/ppermute | solution.py:332
  53.3 9.4 %collective-permute-start.16 = (f32[264,256]{1,0:T(8,128)S(1)}, f32[264,256]{1,0:T(8,128)S(1)}, u32[]{:S(2)}, u32[]{:S(2)}) collective-permute-start(f32[264,256]{1,0:T(8,128)S(1)} %finish.1.refs_0_), channel_id=1, source_target_pairs={{0,4},{1,3},{2,6},{3,1},{4,0},{5,7},{6,2},{7,5},{8,12},{9,11},{10,... | collective-permute-start | bytes 811016 | tf_op jit(solution)/shard_map/ppermute | solution.py:325
  54.2 8.5 %collective-permute-start.13 = (f32[264,256]{1,0:T(8,128)S(1)}, f32[264,256]{1,0:T(8,128)S(1)}, u32[]{:S(2)}, u32[]{:S(2)}) collective-permute-start(f32[264,256]{1,0:T(8,128)S(1)} %finish.1.refs_0_), channel_id=1, source_target_pairs={{0,16},{2,18},{4,20},{6,22},{16,24},{18,26},{20,28},{22,30},{24,8}... | collective-permute-start | bytes 811016 | tf_op jit(solution)/shard_map/ppermute | solution.py:332
  55.8 10.3 %collective-permute-start.18 = (f32[264,256]{1,0:T(8,128)S(1)}, f32[264,256]{1,0:T(8,128)S(1)}, u32[]{:S(2)}, u32[]{:S(2)}) collective-permute-start(f32[264,256]{1,0:T(8,128)S(1)} %finish.1.refs_0_), channel_id=1, source_target_pairs={{0,2},{1,5},{2,0},{3,7},{4,6},{5,1},{6,4},{7,3},{8,10},{9,13},{10,... | collective-permute-start | bytes 811016 | tf_op jit(solution)/shard_map/ppermute | solution.py:325
  62.7 9.1 %collective-permute-start.17 = (f32[264,256]{1,0:T(8,128)S(1)}, f32[264,256]{1,0:T(8,128)S(1)}, u32[]{:S(2)}, u32[]{:S(2)}) collective-permute-start(f32[264,256]{1,0:T(8,128)S(1)} %collective-permute-done.13.refs_4_), channel_id=1, source_target_pairs={{0,4},{1,3},{2,6},{3,1},{4,0},{5,7},{6,2},{7,5},{8,12},{9,11},{10,... | collective-permute-start | bytes 811016 | tf_op jit(solution)/shard_map/ppermute | solution.py:325
  63.5 8.3 %collective-permute-start.14 = (f32[264,256]{1,0:T(8,128)S(1)}, f32[264,256]{1,0:T(8,128)S(1)}, u32[]{:S(2)}, u32[]{:S(2)}) collective-permute-start(f32[264,256]{1,0:T(8,128)S(1)} %collective-permute-done.13.refs_4_), channel_id=1, source_target_pairs={{0,16},{2,18},{4,20},{6,22},{16,24},{18,26},{20,28},{22,30},{24,8}... | collective-permute-start | bytes 811016 | tf_op jit(solution)/shard_map/ppermute | solution.py:332
  64.9 8.8 %collective-permute-start.25 = (f32[264,256]{1,0:T(8,128)S(1)}, f32[264,256]{1,0:T(8,128)S(1)}, u32[]{:S(2)}, u32[]{:S(2)}) collective-permute-start(f32[264,256]{1,0:T(8,128)S(1)} %collective-permute-done.13.refs_4_), channel_id=1, source_target_pairs={{0,2},{1,5},{2,0},{3,7},{4,6},{5,1},{6,4},{7,3},{8,10},{9,13},{10,... | collective-permute-start | bytes 811016 | tf_op jit(solution)/shard_map/ppermute | solution.py:325
  66.2 9.5 %collective-permute-start.19 = (f32[264,256]{1,0:T(8,128)S(1)}, f32[264,256]{1,0:T(8,128)S(1)}, u32[]{:S(2)}, u32[]{:S(2)}) collective-permute-start(f32[264,256]{1,0:T(8,128)S(1)} %collective-permute-done.18.refs_1_), channel_id=1, source_target_pairs={{0,4},{1,3},{2,6},{3,1},{4,0},{5,7},{6,2},{7,5},{8,12},{9,11},{10,... | collective-permute-start | bytes 811016 | tf_op jit(solution)/shard_map/ppermute | solution.py:325
  71.7 9.9 %collective-permute-start.15 = (f32[264,256]{1,0:T(8,128)S(1)}, f32[264,256]{1,0:T(8,128)S(1)}, u32[]{:S(2)}, u32[]{:S(2)}) collective-permute-start(f32[264,256]{1,0:T(8,128)S(1)} %finish.1.refs_0_), channel_id=1, source_target_pairs={{0,8},{2,10},{4,12},{6,14},{16,0},{18,2},{20,4},{22,6},{24,16},{26... | collective-permute-start | bytes 811016 | tf_op jit(solution)/shard_map/ppermute | solution.py:332
  73.0 9.4 %collective-permute-start.22 = (f32[264,256]{1,0:T(8,128)S(1)}, f32[264,256]{1,0:T(8,128)S(1)}, u32[]{:S(2)}, u32[]{:S(2)}) collective-permute-start(f32[264,256]{1,0:T(8,128)S(1)} %collective-permute-done.14.refs_8_), channel_id=1, source_target_pairs={{0,2},{1,5},{2,0},{3,7},{4,6},{5,1},{6,4},{7,3},{8,10},{9,13},{10,... | collective-permute-start | bytes 811016 | tf_op jit(solution)/shard_map/ppermute | solution.py:325
  73.6 10.8 %collective-permute-start.26 = (f32[264,256]{1,0:T(8,128)S(1)}, f32[264,256]{1,0:T(8,128)S(1)}, u32[]{:S(2)}, u32[]{:S(2)}) collective-permute-start(f32[264,256]{1,0:T(8,128)S(1)} %collective-permute-done.25.refs_5_), channel_id=1, source_target_pairs={{0,4},{1,3},{2,6},{3,1},{4,0},{5,7},{6,2},{7,5},{8,12},{9,11},{10,... | collective-permute-start | bytes 811016 | tf_op jit(solution)/shard_map/ppermute | solution.py:325
  75.1 11.7 %collective-permute-start.23 = (f32[264,256]{1,0:T(8,128)S(1)}, f32[264,256]{1,0:T(8,128)S(1)}, u32[]{:S(2)}, u32[]{:S(2)}) collective-permute-start(f32[264,256]{1,0:T(8,128)S(1)} %collective-permute-done.14.refs_8_), channel_id=1, source_target_pairs={{0,4},{1,3},{2,6},{3,1},{4,0},{5,7},{6,2},{7,5},{8,12},{9,11},{10,... | collective-permute-start | bytes 811016 | tf_op jit(solution)/shard_map/ppermute | solution.py:325
  75.7 9.4 %collective-permute-start.27 = (f32[264,256]{1,0:T(8,128)S(1)}, f32[264,256]{1,0:T(8,128)S(1)}, u32[]{:S(2)}, u32[]{:S(2)}) collective-permute-start(f32[264,256]{1,0:T(8,128)S(1)} %collective-permute-done.19.refs_3_), channel_id=1, source_target_pairs={{0,8},{2,10},{4,12},{6,14},{16,0},{18,2},{20,4},{22,6},{24,16},{26... | collective-permute-start | bytes 811016 | tf_op jit(solution)/shard_map/ppermute | solution.py:332
  82.4 6.7 %collective-permute-start.24 = (f32[264,256]{1,0:T(8,128)S(1)}, f32[264,256]{1,0:T(8,128)S(1)}, u32[]{:S(2)}, u32[]{:S(2)}) collective-permute-start(f32[264,256]{1,0:T(8,128)S(1)} %collective-permute-done.22.refs_0_), channel_id=1, source_target_pairs={{0,4},{1,3},{2,6},{3,1},{4,0},{5,7},{6,2},{7,5},{8,12},{9,11},{10,... | collective-permute-start | bytes 811016 | tf_op jit(solution)/shard_map/ppermute | solution.py:325
  83.0 9.1 %collective-permute-start.21 = (f32[264,256]{1,0:T(8,128)S(1)}, f32[264,256]{1,0:T(8,128)S(1)}, u32[]{:S(2)}, u32[]{:S(2)}) collective-permute-start(f32[264,256]{1,0:T(8,128)S(1)} %collective-permute-done.15.refs_9_), channel_id=1, source_target_pairs={{0,4},{1,3},{2,6},{3,1},{4,0},{5,7},{6,2},{7,5},{8,12},{9,11},{10,... | collective-permute-start | bytes 811016 | tf_op jit(solution)/shard_map/ppermute | solution.py:325
  84.4 7.6 %collective-permute-start.20 = (f32[264,256]{1,0:T(8,128)S(1)}, f32[264,256]{1,0:T(8,128)S(1)}, u32[]{:S(2)}, u32[]{:S(2)}) collective-permute-start(f32[264,256]{1,0:T(8,128)S(1)} %collective-permute-done.15.refs_9_), channel_id=1, source_target_pairs={{0,2},{1,5},{2,0},{3,7},{4,6},{5,1},{6,4},{7,3},{8,10},{9,13},{10,... | collective-permute-start | bytes 811016 | tf_op jit(solution)/shard_map/ppermute | solution.py:325
